TPU v7x, 128 devices: a whole 4x4x4 slice. The times are simulated.
128 devices in a mesh: dp: 4 (over y_hi, core), tok: 32 (over y_lo, z, x).
Axes of the slice: x: 4, y: 4 (y_hi: 2, y_lo: 2; y = y_hi * 2 + y_lo), z: 4, core: 2. Of those that a mesh axis runs over, the one named last changes fastest.
Arguments:
- attn_float: bfloat16 [8192, 8192], P(('dp', 'tok')), may hold values from -6 to 6
- attn_quant: bfloat16 [8192, 8192], P(('dp', 'tok')), may hold values from -6 to 6
- proj_weight: bfloat16 [8192, 4096], P('tok'), may hold values from -0.0625 to 0.0625
- weight_codes: int32 [8192, 4096], P('tok'), may hold values from 0 to 15
- group_scales: float32 [64, 4096], P('tok'), may hold values from 0.0012 to 0.005
Outputs:
- float_out: bfloat16 [8192, 4096], P(('dp', 'tok'))
- quant_out: bfloat16 [8192, 4096], P(('dp', 'tok'))
- hessian_cols: float32 [8192, 128], P('tok')
- cross_cols: float32 [8192, 128], P('tok')
All inputs are finite; a program needn't handle non-finite values.
Results may differ from a plain program's by a relative error of at most 0.0049.
Values may be sent and summed in bfloat16 or wider, within the bound.
No kernel may reach another device: no remote copies, remote signals or barrier semaphores. Data moves between devices by JAX's collectives and lax.ppermute only.
A program may use at most 320 MiB of HBM per device.

v0:
```python
import jax
import jax.numpy as jnp
from jax import lax
from jax.sharding import PartitionSpec as P

BLOCK = 128


def shards(attn_float, attn_quant, proj_weight, weight_codes, group_scales):
    tok_rows, d_in = attn_float.shape
    features, d_out = proj_weight.shape
    n_data = lax.axis_size("dp")
    n_tokens = lax.axis_size("tok")
    inverse = 1.0 / (tok_rows * n_data * n_tokens)
    shift = (attn_float.astype(jnp.float32) - attn_quant.astype(jnp.float32)).astype(jnp.bfloat16)
    block_part = jnp.concatenate([attn_quant[:, :BLOCK], shift[:, :BLOCK]], axis=1)
    cols_float, cols_quant = (
        lax.all_to_all(attn_float, "tok", split_axis=1, concat_axis=0, tiled=True),
        lax.all_to_all(attn_quant, "tok", split_axis=1, concat_axis=0, tiled=True),
    )
    group_block = lax.all_gather(block_part, "tok", axis=0, tiled=True)
    local = (
        lax.dot_general(
            cols_quant, group_block, (((0,), (0,)), ((), ())), preferred_element_type=jnp.float32
        )
        * inverse
    )
    summed = lax.psum(local, "dp")
    hessian_cols = summed[:, :BLOCK]
    cross_cols = summed[:, BLOCK:]
    groups = group_scales.shape[0]
    values = (weight_codes - 8).astype(jnp.float32).reshape(groups, features // groups, d_out)
    quant_weight = (values * group_scales[:, None, :]).reshape(features, d_out).astype(jnp.bfloat16)
    first = jnp.dot(cols_float, proj_weight, preferred_element_type=jnp.float32)
    second = jnp.dot(cols_quant, quant_weight, preferred_element_type=jnp.float32)
    both = lax.psum_scatter(
        jnp.concatenate([first, second], axis=1), "tok", scatter_dimension=0, tiled=True
    )
    float_out = both[:, :d_out].astype(jnp.bfloat16)
    quant_out = both[:, d_out:].astype(jnp.bfloat16)
    return (float_out, quant_out, hessian_cols, cross_cols)


def solution(mesh):
    placed = (
        P(("dp", "tok"), None),
        P(("dp", "tok"), None),
        P("tok", None),
        P("tok", None),
        P("tok", None),
    )
    return jax.shard_map(
        shards,
        mesh=mesh,
        in_specs=placed,
        out_specs=(P(("dp", "tok"), None), P(("dp", "tok"), None), P("tok", None), P("tok", None)),
        check_vma=False,
    )
```

profile of v0, /device:TPU:0, one launch (start us, length us, event | category | flops | bytes accessed | tf_op | source)
XLA Modules:
  0.0 944.5 jit_solution(16452220647272625883)
XLA Ops:
  7.2 0.0 copy-start
  7.2 0.0 copy-start.2
  7.2 2.5 copy.30
  9.7 9.3 all-to-all-start.1
  18.9 0.0 all-gather.2.cloned.1.call-start
  19.0 0.7 slice.22
  19.7 0.7 subtract_convert_fusion
  20.4 0.6 pad_maximum_fusion.1
  21.1 0.0 all-gather.2.cloned.1.call-update
  21.1 2.4 copy.31
  23.4 0.0 copy-done.2
  23.4 4.1 fusion
  27.5 8.5 all-to-all-done.1
  36.0 4.7 all-to-all-start
  40.7 0.0 all-reduce.2.cloned.1.call-start
  40.7 14.8 %convolution_bitcast_fusion = f32[2048,4096]{1,0:T(8,128)} fusion(bf16[2048,256]{1,0:T(8,128)(2,1)S(1)} %bitcast.28, bf16[256,4096]{1,0:T(8,128)(2,1)} %fusion), kind=kOutput, calls=%fused_computation.1 | convolution fusion | flops 4294967296 | bytes 36700160 | tf_op jit(solution)/shard_map/dot_general | solution.py:35
  55.6 2.0 all-to-all-done
  57.6 14.4 %fusion.4 = f32[2048,4096]{1,0:T(8,128)} fusion(bf16[2048,256]{1,0:T(8,128)(2,1)} %bitcast.1, bf16[256,4096]{1,0:T(8,128)(2,1)S(1)} %copy-done), kind=kOutput, calls=%fused_computation.12 | convolution fusion | flops 4294967296 | bytes 36700160 | tf_op jit(solution)/shard_map/dot_general | solution.py:34
  71.9 104.3 %all-gather.2.cloned.1.call-done = bf16[2048,256]{1,0:T(8,128)(2,1)} async-done(((bf16[64,256]{1,0:T(8,128)(2,1)}), bf16[2048,256]{1,0:T(8,128)(2,1)}) %all-gather.2.cloned.1.call-update) | async-done | bytes 1048592 | tf_op jit(solution)/shard_map/all_gather | solution.py:21
  176.2 2.4 fusion.1
  178.6 0.0 all-reduce.2.cloned.1.call-update
  178.6 0.0 reduce-scatter.2.cloned.1.call-start
  178.7 43.3 %pad_maximum_fusion = f32[2048,8192]{1,0:T(8,128)} fusion(f32[2048,4096]{1,0:T(8,128)} %convolution_bitcast_fusion, f32[2048,4096]{1,0:T(8,128)} %fusion.4), kind=kLoop, calls=%fused_computation | loop fusion | flops 16777216 | bytes 134217728 | tf_op jit(solution)/shard_map/concatenate | solution.py:37
  222.0 0.0 reduce-scatter.2.cloned.1.call-update
  222.1 0.0 copy-start.1
  222.1 0.0 all-reduce.2.cloned.1.call-done
  222.1 1.1 fusion.3
  223.2 0.8 copy.24
  224.0 0.8 copy.23
  224.7 710.5 %reduce-scatter.2.cloned.1.call-done = f32[64,8192]{1,0:T(8,128)} async-done(((f32[2048,8192]{1,0:T(8,128)}), f32[64,8192]{1,0:T(8,128)}) %reduce-scatter.2.cloned.1.call-update) | async-done | bytes 2097168 | tf_op jit(solution)/shard_map/reduce_scatter | solution.py:36
  935.2 1.7 convert.4
  936.9 1.0 fusion.2
  (2 shorter events, 0.0 us)
Async XLA Ops:
  7.2 50.4 %copy-start = (bf16[256,4096]{1,0:T(8,128)(2,1)S(1)}, bf16[256,4096]{1,0:T(8,128)(2,1)}, u32[]{:S(2)}) copy-start(bf16[256,4096]{1,0:T(8,128)(2,1)} %param.7) | copy-start | bytes 6291460
  7.2 16.3 %copy-start.2 = (f32[2,4096]{1,0:T(2,128)S(1)}, f32[2,4096]{1,0:T(2,128)}, u32[]{:S(2)}) copy-start(f32[2,4096]{1,0:T(2,128)} %param.9) | copy-start | bytes 98308
  9.7 26.3 %all-to-all-start.1 = ((bf16[64,32,256]{2,0,1:T(8,128)(2,1)}), bf16[64,32,256]{2,0,1:T(8,128)(2,1)S(1)}, u32[]{:S(2)}, u32[]{:S(2)}) async-start(bf16[64,32,256]{2,0,1:T(8,128)(2,1)} %bitcast.30), calls=%async_computation.1 | async-start | bytes 2097152 | tf_op jit(solution)/shard_map/all_to_all | solution.py:19
  18.9 157.3 %all-gather.2.cloned.1.call-start = ((), (), s32[]{:S(2)}) async-start(), calls=%async_computation.4 | async-start | bytes 1081344 | tf_op jit(solution)/shard_map/all_gather | solution.py:21
  36.0 21.5 %all-to-all-start = ((bf16[64,32,256]{2,0,1:T(8,128)(2,1)}), bf16[64,32,256]{2,0,1:T(8,128)(2,1)}, u32[]{:S(2)}, u32[]{:S(2)}) async-start(bf16[64,32,256]{2,0,1:T(8,128)(2,1)} %bitcast.31), calls=%async_computation | async-start | bytes 2097152 | tf_op jit(solution)/shard_map/all_to_all | solution.py:18
  40.7 181.4 %all-reduce.2.cloned.1.call-start = ((), (), s32[]{:S(2)}) async-start(), calls=%async_computation.5 | async-start | bytes 524288 | tf_op jit(solution)/shard_map/psum | solution.py:28
  178.6 756.6 %reduce-scatter.2.cloned.1.call-start = ((), (), s32[]{:S(2)}) async-start(), calls=%async_computation.3 | async-start | bytes 69206016 | tf_op jit(solution)/shard_map/reduce_scatter | solution.py:36
  222.1 715.9 %copy-start.1 = (bf16[256,4096]{1,0:T(8,128)(2,1)S(1)}, bf16[256,4096]{1,0:T(8,128)(2,1)}, u32[]{:S(2)}) copy-start(bf16[256,4096]{1,0:T(8,128)(2,1)} %param.7) | copy-start | bytes 6291460
Sparse Core Ops, SparseCore 0:
  22.0 154.1 all-gather.1
  179.3 40.3 all-reduce.1
  222.3 712.8 reduce-scatter.1
where the time goes:
time: 946 us; the launch traced here: 944 us
  waiting for transfers between devices  825 us (87%)
  other arithmetic  50.5 us (5%)
  matrix products  31.6 us (3%)
  starting transfers between devices  14.1 us (1%)
  between operations  13.8 us (1%)
    reduce_scatter x1, waiting for transfers between devices, shards(): lax.psum_scatter(jnp.concatenate([first, second], axis=1), 'tok', scatter...  710 us
    all_gather x1, waiting for transfers between devices, shards(): group_block = lax.all_gather(block_part, 'tok', axis=0, tiled=True)  104 us
    concatenate x1, other arithmetic, shards(): jnp.concatenate([first, second], axis=1)  43.3 us
  transfers between devices with their start and end apart: 5, of which 4 were waited for; matrix products, arithmetic and copies ran while one was open for 9% of the time, Pallas kernels for 0%

commit v1 on v0

v1 whole, which is shorter than its diff:
```python
import jax
import jax.numpy as jnp
from jax import lax
from jax.experimental import pallas as pl
from jax.experimental.pallas import tpu as pltpu
from jax.sharding import Mesh
from jax.sharding import PartitionSpec as P

BLOCK = 128
FINE = ("yh", "core", "yl", "z", "x")
PLANE = ("yh", "yl", "x")
F32 = jnp.float32
BF16 = jnp.bfloat16


def params():
    return pltpu.CompilerParams(vmem_limit_bytes=40 << 20)


def pack_kernel(z_ref, float_ref, quant_ref, out_ref, block_ref):
    width = out_ref.shape[2] // 8
    z = z_ref[0]
    for kind, ref in enumerate((float_ref, quant_ref)):
        for j in range(4):
            zj = lax.rem(z + j, 4)
            for yl in range(2):
                for x in range(4):
                    start = pl.multiple_of(((yl * 4 + zj) * 4 + x) * width, width)
                    block = ref[:, pl.ds(start, width)]
                    for half in range(2):
                        at = (j * 2 + (yl ^ half)) * width
                        out_ref[kind * 8 + half * 4 + x, :, at : at + width] = block
    quant = quant_ref[:, :BLOCK]
    shift = (float_ref[:, :BLOCK].astype(F32) - quant.astype(F32)).astype(BF16)
    for d in range(16):
        block_ref[d, :, :BLOCK] = quant
        block_ref[d, :, BLOCK:] = shift


def pack(z, attn_float, attn_quant):
    tokens, d_in = attn_float.shape
    whole = pl.BlockSpec(memory_space=pltpu.VMEM)
    return pl.pallas_call(
        pack_kernel,
        out_shape=(
            jax.ShapeDtypeStruct((16, tokens, d_in // 4), BF16),
            jax.ShapeDtypeStruct((16, tokens, 2 * BLOCK), BF16),
        ),
        in_specs=[pl.BlockSpec(memory_space=pltpu.SMEM), whole, whole],
        out_specs=(whole, whole),
        compiler_params=params(),
        name="pack",
    )(z.reshape(1), attn_float, attn_quant)


def finish_kernel(core_ref, first_ref, second_ref, float_ref, quant_ref):
    core = core_ref[0]
    width = first_ref.shape[2]
    for n, ref in enumerate((first_ref, second_ref)):
        quarter = core if n == 0 else 1 - core
        for kind, out in enumerate((float_ref, quant_ref)):
            for half in range(2):
                at = kind * 8 + half * 4
                total = ref[at].astype(F32)
                for x in range(1, 4):
                    total += ref[at + x].astype(F32)
                start = pl.multiple_of((half * 2 + quarter) * width, width)
                out[:, pl.ds(start, width)] = total.astype(BF16)


def finish(core, first, second):
    _, tokens, width = first.shape
    whole = pl.BlockSpec(memory_space=pltpu.VMEM)
    return pl.pallas_call(
        finish_kernel,
        out_shape=(jax.ShapeDtypeStruct((tokens, 4 * width), BF16),) * 2,
        in_specs=[pl.BlockSpec(memory_space=pltpu.SMEM), whole, whole],
        out_specs=(whole, whole),
        compiler_params=params(),
        name="finish",
    )(core.reshape(1), first, second)


def swap(a, axis):
    return lax.ppermute(a, axis, [(0, 1), (1, 0)])


def shards(attn_float, attn_quant, proj_weight, weight_codes, group_scales):
    tokens, d_in = attn_float.shape
    features, d_out = proj_weight.shape
    groups = group_scales.shape[0]
    half, quarter = d_out // 2, d_out // 4
    inverse = 1.0 / (tokens * 128)
    yh, core, yl, z = (lax.axis_index(a) for a in ("yh", "core", "yl", "z"))

    def weight(kind, col):
        plain = lax.dynamic_slice_in_dim(proj_weight, col, quarter, 1)
        codes = lax.dynamic_slice_in_dim(weight_codes, col, quarter, 1)
        scales = lax.dynamic_slice_in_dim(group_scales, col, quarter, 1)
        values = (codes - 8).astype(F32).reshape(groups, features // groups, quarter)
        quant = (values * scales[:, None, :]).reshape(features, quarter).astype(BF16)
        return jnp.where(kind == 0, plain, quant)

    own = weight(yh, yl * half + core * quarter)
    send = weight(yh ^ core, (1 - yl) * half + core * quarter)
    pairs = []
    for a in range(2):
        for c in range(2):
            for b in range(2):
                pairs.append((a * 4 + c * 2 + b, (a ^ c) * 4 + c * 2 + (1 - b)))
    got = lax.ppermute(send, ("yh", "core", "yl"), pairs)

    payload, block_part = pack(z, attn_float, attn_quant)
    block_all = lax.all_to_all(block_part, PLANE, 0, 0, tiled=True)
    block_all = block_all.reshape(16 * tokens, 2 * BLOCK)

    rows = jnp.concatenate([own, got], axis=0)
    parts = [rows] + [
        lax.ppermute(rows, "z", [((i + j) % 4, i) for i in range(4)]) for j in (1, 2, 3)
    ]
    mine = jnp.concatenate(parts, axis=0)
    other = swap(mine, "core")

    acts = lax.all_to_all(payload, PLANE, 0, 0, tiled=True).reshape(16 * tokens, 8 * features)

    def part(w):
        p = jnp.dot(acts, w, preferred_element_type=F32).astype(BF16)
        return lax.all_to_all(p.reshape(16, tokens, quarter), PLANE, 0, 0, tiled=True)

    float_out, quant_out = finish(core, part(mine), part(other))

    def stats(j):
        picked = acts[:, 2 * j * features : (2 * j + 1) * features]
        return lax.dot_general(
            picked, block_all, (((0,), (0,)), ((), ())), preferred_element_type=F32
        )

    total = stats(0)
    for j in (1, 2, 3):
        total = total + lax.ppermute(
            stats(j).astype(BF16), "z", [(i, (i + j) % 4) for i in range(4)]
        ).astype(F32)
    total = jnp.where(yh == 1, total, swap(total, "yh"))
    total = (total + swap(total, "core")) * inverse
    return float_out, quant_out, total[:, :BLOCK], total[:, BLOCK:]


def solution(mesh):
    fine = Mesh(mesh.devices.reshape(2, 2, 2, 4, 4), FINE)
    rows, tok = P(FINE, None), P(("yl", "z", "x"), None)
    return jax.shard_map(
        shards,
        mesh=fine,
        in_specs=(rows, rows, tok, tok, tok),
        out_specs=(rows, rows, tok, tok),
        check_vma=False,
    )
```

time: 946 us -> 167 us (0.18)
  waiting for transfers between devices: 825 us -> 85.2 us
  other arithmetic: 50.5 us -> 3.19 us
  starting transfers between devices: 14.1 us -> 39.1 us
  between operations: 13.8 us -> 0.78 us
    reduce_scatter x1 -> x0, waiting for transfers between devices: 710 us -> none  [shards(): lax.psum_scatter(jnp.concatenate([first, second], axis=1), 'tok', scatter...]
    all_gather x1 -> x0, waiting for transfers between devices: 104 us -> none  [shards(): group_block = lax.all_gather(block_part, 'tok', axis=0, tiled=True)]
    ppermute x0 -> x10, waiting for transfers between devices: none -> 59.4 us  [the longest x3 42.1 us: shards(): lax.ppermute(rows, 'z', [((i + j) % 4, i) for i in range(4)])]
    concatenate x2 -> x1, other arithmetic: 44 us -> 0.07 us  [shards(): rows = jnp.concatenate([own, got], axis=0)]
    ppermute x0 -> x10, starting transfers between devices: none -> 17.1 us  [the longest x3 6.58 us: shards(): lax.ppermute(stats(j).astype(BF16), 'z', [(i, (i + j) % 4) for i in range...]
    all_to_all x2 -> x4, waiting for transfers between devices: 10.5 us -> 25.8 us  [the longest x2 16.8 us: part(): lax.all_to_all(p.reshape(16, tokens, quarter), PLANE, 0, 0, tiled=True)]
    all_to_all x2 -> x4, starting transfers between devices: 13.9 us -> 22 us  [the longest x2 10.9 us: part(): lax.all_to_all(p.reshape(16, tokens, quarter), PLANE, 0, 0, tiled=True)]
    dot_general x3 -> x6, matrix products: 31.6 us -> 24.2 us  [the longest x2 18.6 us: part(): p = jnp.dot(acts, w, preferred_element_type=F32).astype(BF16)]
  transfers between devices with their start and end apart: 5 -> 14, of which waited for: 4 -> 10; matrix products, arithmetic and copies ran while one was open for 9% -> 18% of each run, Pallas kernels for 0% -> 1%
where the time goes in v1:
time: 167 us; the launch traced here: 165 us
  waiting for transfers between devices  85.2 us (51%)
  starting transfers between devices  39.1 us (23%)
  matrix products  24.2 us (14%)
  local copies, waits for them, and re-layouts  8.48 us (5%)
  Pallas kernels  4.2 us (3%)
  other arithmetic  3.19 us (2%)
    ppermute x3, waiting for transfers between devices, shards(): lax.ppermute(rows, 'z', [((i + j) % 4, i) for i in range(4)])  42.1 us
    dot_general x2, matrix products, part(): p = jnp.dot(acts, w, preferred_element_type=F32).astype(BF16)  18.6 us
    all_to_all x2, waiting for transfers between devices, part(): lax.all_to_all(p.reshape(16, tokens, quarter), PLANE, 0, 0, tiled=True)  16.8 us
    ppermute x3, waiting for transfers between devices, swap(): return lax.ppermute(a, axis, [(0, 1), (1, 0)])  13.3 us
    all_to_all x2, starting transfers between devices, part(): lax.all_to_all(p.reshape(16, tokens, quarter), PLANE, 0, 0, tiled=True)  10.9 us
    all_to_all x1, waiting for transfers between devices, shards(): lax.all_to_all(payload, PLANE, 0, 0, tiled=True)  8.25 us
    all_to_all x1, starting transfers between devices, shards(): lax.all_to_all(payload, PLANE, 0, 0, tiled=True)  6.79 us
    ppermute x3, starting transfers between devices, shards(): lax.ppermute(stats(j).astype(BF16), 'z', [(i, (i + j) % 4) for i in range...  6.58 us
  transfers between devices with their start and end apart: 14, of which 10 were waited for; matrix products, arithmetic and copies ran while one was open for 18% of the time, Pallas kernels for 1%

profile of v1, /device:TPU:0, one launch (start us, length us, event | category | flops | bytes accessed | tf_op | source)
XLA Modules:
  0.0 165.1 jit_solution(12330371697818679153)
XLA Ops:
  1.5 3.1 %fusion.3 = (bf16[256,1024]{1,0:T(8,128)(2,1)}, bf16[256,1024]{1,0:T(8,128)(2,1)S(1)}) fusion(s32[256,4096]{1,0:T(8,128)} %param.8, s32[]{:T(128)S(6)} %select_n.36, f32[2,1024]{1,0:T(2,128)S(1)} %get-tuple-element.16, bf16[256,4096]{1,0:T(8,128)(2,1)} %param.7, pred[]{:T(512)S(6)} %eq.10, f32[2,1024]{1,0:T(2,128)S(1)} %get-tuple-element.17, ...), kind=kLoop, calls=%fused_computation.11 | loop fusion | flops 2621440 | bytes 4210698 | tf_op jit(solution)/shard_map/jit(_where)/select_n | solution.py:102
  4.6 1.7 %collective-permute-start = (bf16[256,1024]{1,0:T(8,128)(2,1)}, bf16[256,1024]{1,0:T(8,128)(2,1)S(1)}, u32[]{:S(2)}, u32[]{:S(2)}) collective-permute-start(bf16[256,1024]{1,0:T(8,128)(2,1)} %get-tuple-element.12), channel_id=1, source_target_pairs={{0,16},{16,0},{32,112},{48,96},{64,80},{80,64},{96,48},{112,32},{1... | collective-permute-start | bytes 1572872 | tf_op jit(solution)/shard_map/ppermute | solution.py:111
  6.2 1.2 pack.1
  7.4 2.0 %copy-done = bf16[16,64,2048]{2,1,0:T(8,128)(2,1)} copy-done((bf16[16,64,2048]{2,1,0:T(8,128)(2,1)}, bf16[16,64,2048]{2,1,0:T(8,128)(2,1)S(1)}, u32[]{:S(2)}) %copy-start) | copy-done | bytes 4194328
  9.5 6.8 %all-to-all-start = ((bf16[16,64,2048]{2,1,0:T(8,128)(2,1)}), bf16[16,64,2048]{2,1,0:T(8,128)(2,1)}, u32[]{:S(2)}, u32[]{:S(2)}) async-start(bf16[16,64,2048]{2,1,0:T(8,128)(2,1)} %copy-done), calls=%async_computation | async-start | bytes 8388608 | tf_op jit(solution)/shard_map/all_to_all | solution.py:124
  16.3 4.1 %collective-permute-start.1 = (bf16[512,1024]{1,0:T(8,128)(2,1)S(1)}, bf16[512,1024]{1,0:T(8,128)(2,1)S(1)}, u32[]{:S(2)}, u32[]{:S(2)}) collective-permute-start(bf16[512,1024]{1,0:T(8,128)(2,1)S(1)} %pad_maximum_fusion), channel_id=1, source_target_pairs={{4,0},{8,4},{12,8},{0,12},{5,1},{9,5},{13,9},{1,13},{6,2},{10,6},{... | collective-permute-start | bytes 3145736 | tf_op jit(solution)/shard_map/ppermute | solution.py:119
  20.5 1.3 collective-permute-start.3
  23.4 40.8 %collective-permute-done.1 = bf16[512,1024]{1,0:T(8,128)(2,1)S(1)} collective-permute-done((bf16[512,1024]{1,0:T(8,128)(2,1)S(1)}, bf16[512,1024]{1,0:T(8,128)(2,1)S(1)}, u32[]{:S(2)}, u32[]{:S(2)}) %collective-permute-start.1) | collective-permute-done | bytes 1048608 | tf_op jit(solution)/shard_map/ppermute | solution.py:119
  64.3 1.1 constant_dynamic-update-slice_fusion.2
  65.3 1.1 constant_dynamic-update-slice_fusion.1
  66.4 1.3 collective-permute-done.3
  67.7 1.0 constant_dynamic-update-slice_fusion
  68.7 8.3 %all-to-all-done = bf16[16,64,2048]{2,1,0:T(8,128)(2,1)} async-done(((bf16[16,64,2048]{2,1,0:T(8,128)(2,1)}), bf16[16,64,2048]{2,1,0:T(8,128)(2,1)}, u32[]{:S(2)}, u32[]{:S(2)}) %all-to-all-start) | async-done | bytes 4194336 | tf_op jit(solution)/shard_map/all_to_all | solution.py:124
  77.0 4.4 %all-to-all-start.3 = ((bf16[16,64,256]{2,1,0:T(8,128)(2,1)}), bf16[16,64,256]{2,1,0:T(8,128)(2,1)S(1)}, u32[]{:S(2)}, u32[]{:S(2)}) async-start(bf16[16,64,256]{2,1,0:T(8,128)(2,1)} %get-tuple-element.11), calls=%async_computation.3 | async-start | bytes 1048576 | tf_op jit(solution)/shard_map/all_to_all | solution.py:114
  81.3 9.3 %convolution_convert_fusion.1 = bf16[1024,1024]{1,0:T(8,128)(2,1)} fusion(bf16[1024,2048]{1,0:T(8,128)(2,1)} %bitcast.2, bf16[2048,1024]{1,0:T(8,128)(2,1)} %constant_dynamic-update-slice_fusion), kind=kOutput, calls=%fused_computation.1 | convolution fusion | flops 4296015872 | bytes 10485760 | tf_op jit(solution)/shard_map/dot_general | solution.py:127
  91.5 6.4 %all-to-all-start.1 = ((bf16[16,64,1024]{2,1,0:T(8,128)(2,1)}), bf16[16,64,1024]{2,1,0:T(8,128)(2,1)S(1)}, u32[]{:S(2)}, u32[]{:S(2)}) async-start(bf16[16,64,1024]{2,1,0:T(8,128)(2,1)} %bitcast.27), calls=%async_computation.1 | async-start | bytes 4194304 | tf_op jit(solution)/shard_map/all_to_all | solution.py:128
  97.9 1.4 convolution_convert_fusion.4
  99.3 9.3 %convolution_convert_fusion = bf16[1024,1024]{1,0:T(8,128)(2,1)} fusion(bf16[1024,2048]{1,0:T(8,128)(2,1)} %bitcast.2, bf16[2048,1024]{1,0:T(8,128)(2,1)} %collective-permute-done.4), kind=kOutput, calls=%fused_computation | convolution fusion | flops 4296015872 | bytes 10485760 | tf_op jit(solution)/shard_map/dot_general | solution.py:127
  108.6 16.8 %all-to-all-done.1.first_ref = bf16[16,64,1024]{2,1,0:T(8,128)(2,1)S(1)} async-done(((bf16[16,64,1024]{2,1,0:T(8,128)(2,1)}), bf16[16,64,1024]{2,1,0:T(8,128)(2,1)S(1)}, u32[]{:S(2)}, u32[]{:S(2)}) %all-to-all-start.1) | async-done | bytes 2097184 | tf_op jit(solution)/shard_map/all_to_all | solution.py:128
  125.4 4.4 %all-to-all-start.2 = ((bf16[16,64,1024]{2,1,0:T(8,128)(2,1)}), bf16[16,64,1024]{2,1,0:T(8,128)(2,1)}, u32[]{:S(2)}, u32[]{:S(2)}) async-start(bf16[16,64,1024]{2,1,0:T(8,128)(2,1)} %bitcast.26), calls=%async_computation.2 | async-start | bytes 4194304 | tf_op jit(solution)/shard_map/all_to_all | solution.py:128
  129.8 1.4 convolution_convert_fusion.3
  131.2 1.4 convolution_convert_fusion.2
  132.6 2.0 %collective-permute-start.5 = (bf16[256,256]{1,0:T(8,128)(2,1)S(1)}, bf16[256,256]{1,0:T(8,128)(2,1)S(1)}, u32[]{:S(2)}, u32[]{:S(2)}) collective-permute-start(bf16[256,256]{1,0:T(8,128)(2,1)S(1)} %convolution_convert_fusion.4), channel_id=1, source_target_pairs={{0,4},{4,8},{8,12},{12,0},{1,5},{5,9},{9,13},{13,1},{2,6},{6,10},{... | collective-permute-start | bytes 393224 | tf_op jit(solution)/shard_map/ppermute | solution.py:140
  134.6 3.6 %collective-permute-start.6 = (bf16[256,256]{1,0:T(8,128)(2,1)S(1)}, bf16[256,256]{1,0:T(8,128)(2,1)S(1)}, u32[]{:S(2)}, u32[]{:S(2)}) collective-permute-start(bf16[256,256]{1,0:T(8,128)(2,1)S(1)} %convolution_convert_fusion.3), channel_id=1, source_target_pairs={{0,8},{4,12},{8,0},{12,4},{1,9},{5,13},{9,1},{13,5},{2,10},{6,14},... | collective-permute-start | bytes 393224 | tf_op jit(solution)/shard_map/ppermute | solution.py:140
  138.2 1.0 collective-permute-start.7
  139.2 1.2 collective-permute-done.5
  140.4 2.2 %collective-permute-done.6 = bf16[256,256]{1,0:T(8,128)(2,1)S(1)} collective-permute-done((bf16[256,256]{1,0:T(8,128)(2,1)S(1)}, bf16[256,256]{1,0:T(8,128)(2,1)S(1)}, u32[]{:S(2)}, u32[]{:S(2)}) %collective-permute-start.6) | collective-permute-done | bytes 131104 | tf_op jit(solution)/shard_map/ppermute | solution.py:140
  143.2 1.4 convert_add_fusion
  144.6 3.4 %collective-permute-start.8 = (f32[256,256]{1,0:T(8,128)S(1)}, f32[256,256]{1,0:T(8,128)S(1)}, u32[]{:S(2)}, u32[]{:S(2)}) collective-permute-start(f32[256,256]{1,0:T(8,128)S(1)} %convert_add_fusion), channel_id=1, source_target_pairs={{0,64},{64,0},{1,65},{65,1},{2,66},{66,2},{3,67},{67,3},{4,68},{68... | collective-permute-start | bytes 786440 | tf_op jit(solution)/shard_map/ppermute | solution.py:85
  147.9 11.8 %collective-permute-done.8 = f32[256,256]{1,0:T(8,128)S(1)} collective-permute-done((f32[256,256]{1,0:T(8,128)S(1)}, f32[256,256]{1,0:T(8,128)S(1)}, u32[]{:S(2)}, u32[]{:S(2)}) %collective-permute-start.8) | collective-permute-done | bytes 262176 | tf_op jit(solution)/shard_map/ppermute | solution.py:85
  159.8 1.5 collective-permute-done.9
  162.1 3.0 %finish.1 = (bf16[64,4096]{1,0:T(8,128)(2,1)}, bf16[64,4096]{1,0:T(8,128)(2,1)}) custom-call(s32[1]{0:T(128)} %bitcast.core_ref, bf16[16,64,1024]{2,1,0:T(8,128)(2,1)S(1)} %all-to-all-done.1.first_ref, bf16[16,64,1024]{2,1,0:T(8,128)(2,1)} %all-to-all-done.2.second_ref), custom_call_target="tpu_custom_call" | custom-call | tf_op jit(solution)/shard_map/finish/pallas_call | solution.py:74
  (21 shorter events, 5.0 us)
Async XLA Ops:
  0.6 5.6 %copy-start.1 = (bf16[64,8192]{1,0:T(8,128)(2,1)S(1)}, bf16[64,8192]{1,0:T(8,128)(2,1)}, u32[]{:S(2)}) copy-start(bf16[64,8192]{1,0:T(8,128)(2,1)} %float_ref.1) | copy-start | bytes 3145732
  0.6 5.6 %copy-start.2 = (bf16[64,8192]{1,0:T(8,128)(2,1)S(1)}, bf16[64,8192]{1,0:T(8,128)(2,1)}, u32[]{:S(2)}) copy-start(bf16[64,8192]{1,0:T(8,128)(2,1)} %quant_ref.1) | copy-start | bytes 3145732
  4.6 11.7 %collective-permute-start = (bf16[256,1024]{1,0:T(8,128)(2,1)}, bf16[256,1024]{1,0:T(8,128)(2,1)S(1)}, u32[]{:S(2)}, u32[]{:S(2)}) collective-permute-start(bf16[256,1024]{1,0:T(8,128)(2,1)} %get-tuple-element.12), channel_id=1, source_target_pairs={{0,16},{16,0},{32,112},{48,96},{64,80},{80,64},{96,48},{112,32},{1... | collective-permute-start | bytes 1572872 | tf_op jit(solution)/shard_map/ppermute | solution.py:111
  7.4 2.0 %copy-start = (bf16[16,64,2048]{2,1,0:T(8,128)(2,1)}, bf16[16,64,2048]{2,1,0:T(8,128)(2,1)S(1)}, u32[]{:S(2)}) copy-start(bf16[16,64,2048]{2,1,0:T(8,128)(2,1)S(1)} %get-tuple-element.8) | copy-start | bytes 12582916
  9.5 67.5 %all-to-all-start = ((bf16[16,64,2048]{2,1,0:T(8,128)(2,1)}), bf16[16,64,2048]{2,1,0:T(8,128)(2,1)}, u32[]{:S(2)}, u32[]{:S(2)}) async-start(bf16[16,64,2048]{2,1,0:T(8,128)(2,1)} %copy-done), calls=%async_computation | async-start | bytes 8388608 | tf_op jit(solution)/shard_map/all_to_all | solution.py:124
  16.3 47.9 %collective-permute-start.1 = (bf16[512,1024]{1,0:T(8,128)(2,1)S(1)}, bf16[512,1024]{1,0:T(8,128)(2,1)S(1)}, u32[]{:S(2)}, u32[]{:S(2)}) collective-permute-start(bf16[512,1024]{1,0:T(8,128)(2,1)S(1)} %pad_maximum_fusion), channel_id=1, source_target_pairs={{4,0},{8,4},{12,8},{0,12},{5,1},{9,5},{13,9},{1,13},{6,2},{10,6},{... | collective-permute-start | bytes 3145736 | tf_op jit(solution)/shard_map/ppermute | solution.py:119
  20.5 44.9 %collective-permute-start.2 = (bf16[512,1024]{1,0:T(8,128)(2,1)S(1)}, bf16[512,1024]{1,0:T(8,128)(2,1)S(1)}, u32[]{:S(2)}, u32[]{:S(2)}) collective-permute-start(bf16[512,1024]{1,0:T(8,128)(2,1)S(1)} %pad_maximum_fusion), channel_id=1, source_target_pairs={{8,0},{12,4},{0,8},{4,12},{9,1},{13,5},{1,9},{5,13},{10,2},{14,6},... | collective-permute-start | bytes 3145736 | tf_op jit(solution)/shard_map/ppermute | solution.py:119
  20.5 47.2 %collective-permute-start.3 = (bf16[512,1024]{1,0:T(8,128)(2,1)S(1)}, bf16[512,1024]{1,0:T(8,128)(2,1)S(1)}, u32[]{:S(2)}, u32[]{:S(2)}) collective-permute-start(bf16[512,1024]{1,0:T(8,128)(2,1)S(1)} %pad_maximum_fusion), channel_id=1, source_target_pairs={{12,0},{0,4},{4,8},{8,12},{13,1},{1,5},{5,9},{9,13},{14,2},{2,6},{... | collective-permute-start | bytes 3145736 | tf_op jit(solution)/shard_map/ppermute | solution.py:119
  68.7 30.6 %collective-permute-start.4 = (bf16[2048,1024]{1,0:T(8,128)(2,1)}, bf16[2048,1024]{1,0:T(8,128)(2,1)}, u32[]{:S(2)}, u32[]{:S(2)}) collective-permute-start(bf16[2048,1024]{1,0:T(8,128)(2,1)} %constant_dynamic-update-slice_fusion), channel_id=1, source_target_pairs={{0,32},{32,0},{1,33},{33,1},{2,34},{34,2},{3,35},{35,3},{4,36},{36... | collective-permute-start | bytes 12582920 | tf_op jit(solution)/shard_map/ppermute | solution.py:85
  77.0 14.5 %all-to-all-start.3 = ((bf16[16,64,256]{2,1,0:T(8,128)(2,1)}), bf16[16,64,256]{2,1,0:T(8,128)(2,1)S(1)}, u32[]{:S(2)}, u32[]{:S(2)}) async-start(bf16[16,64,256]{2,1,0:T(8,128)(2,1)} %get-tuple-element.11), calls=%async_computation.3 | async-start | bytes 1048576 | tf_op jit(solution)/shard_map/all_to_all | solution.py:114
  91.5 33.9 %all-to-all-start.1 = ((bf16[16,64,1024]{2,1,0:T(8,128)(2,1)}), bf16[16,64,1024]{2,1,0:T(8,128)(2,1)S(1)}, u32[]{:S(2)}, u32[]{:S(2)}) async-start(bf16[16,64,1024]{2,1,0:T(8,128)(2,1)} %bitcast.27), calls=%async_computation.1 | async-start | bytes 4194304 | tf_op jit(solution)/shard_map/all_to_all | solution.py:128
  125.4 36.7 %all-to-all-start.2 = ((bf16[16,64,1024]{2,1,0:T(8,128)(2,1)}), bf16[16,64,1024]{2,1,0:T(8,128)(2,1)}, u32[]{:S(2)}, u32[]{:S(2)}) async-start(bf16[16,64,1024]{2,1,0:T(8,128)(2,1)} %bitcast.26), calls=%async_computation.2 | async-start | bytes 4194304 | tf_op jit(solution)/shard_map/all_to_all | solution.py:128
  132.6 7.8 %collective-permute-start.5 = (bf16[256,256]{1,0:T(8,128)(2,1)S(1)}, bf16[256,256]{1,0:T(8,128)(2,1)S(1)}, u32[]{:S(2)}, u32[]{:S(2)}) collective-permute-start(bf16[256,256]{1,0:T(8,128)(2,1)S(1)} %convolution_convert_fusion.4), channel_id=1, source_target_pairs={{0,4},{4,8},{8,12},{12,0},{1,5},{5,9},{9,13},{13,1},{2,6},{6,10},{... | collective-permute-start | bytes 393224 | tf_op jit(solution)/shard_map/ppermute | solution.py:140
  134.6 7.9 %collective-permute-start.6 = (bf16[256,256]{1,0:T(8,128)(2,1)S(1)}, bf16[256,256]{1,0:T(8,128)(2,1)S(1)}, u32[]{:S(2)}, u32[]{:S(2)}) collective-permute-start(bf16[256,256]{1,0:T(8,128)(2,1)S(1)} %convolution_convert_fusion.3), channel_id=1, source_target_pairs={{0,8},{4,12},{8,0},{12,4},{1,9},{5,13},{9,1},{13,5},{2,10},{6,14},... | collective-permute-start | bytes 393224 | tf_op jit(solution)/shard_map/ppermute | solution.py:140
  138.2 5.0 %collective-permute-start.7 = (bf16[256,256]{1,0:T(8,128)(2,1)S(1)}, bf16[256,256]{1,0:T(8,128)(2,1)S(1)}, u32[]{:S(2)}, u32[]{:S(2)}) collective-permute-start(bf16[256,256]{1,0:T(8,128)(2,1)S(1)} %convolution_convert_fusion.2), channel_id=1, source_target_pairs={{0,12},{4,0},{8,4},{12,8},{1,13},{5,1},{9,5},{13,9},{2,14},{6,2},{... | collective-permute-start | bytes 393224 | tf_op jit(solution)/shard_map/ppermute | solution.py:140
  144.6 15.2 %collective-permute-start.8 = (f32[256,256]{1,0:T(8,128)S(1)}, f32[256,256]{1,0:T(8,128)S(1)}, u32[]{:S(2)}, u32[]{:S(2)}) collective-permute-start(f32[256,256]{1,0:T(8,128)S(1)} %convert_add_fusion), channel_id=1, source_target_pairs={{0,64},{64,0},{1,65},{65,1},{2,66},{66,2},{3,67},{67,3},{4,68},{68... | collective-permute-start | bytes 786440 | tf_op jit(solution)/shard_map/ppermute | solution.py:85
  159.8 1.6 collective-permute-start.9

commit v2 on v1

v2 whole, which is shorter than its diff:
```python
import jax
import jax.numpy as jnp
from jax import lax
from jax.experimental import pallas as pl
from jax.experimental.pallas import tpu as pltpu
from jax.sharding import Mesh
from jax.sharding import PartitionSpec as P

BLOCK = 128
CHUNKS = 4
FINE = ("yh", "core", "yl", "z", "x")
F32 = jnp.float32
BF16 = jnp.bfloat16
WHOLE = pl.BlockSpec(memory_space=pltpu.VMEM)
SCALAR = pl.BlockSpec(memory_space=pltpu.SMEM)
LEFT = pl.BlockSpec(memory_space=pl.ANY)


def params():
    return pltpu.CompilerParams(vmem_limit_bytes=40 << 20)


def pack_kernel(at_ref, float_ref, quant_ref, out_ref):
    width = float_ref.shape[1] // 32
    yl, z = at_ref[0], at_ref[1]
    quant = quant_ref[:, :BLOCK]
    shift = (float_ref[:, :BLOCK].astype(F32) - quant.astype(F32)).astype(BF16)
    for kind, ref in enumerate((float_ref, quant_ref)):
        for x in range(4):
            for j in range(4):
                for r in range(2):
                    block = ((yl ^ r) * 4 + lax.rem(z + j, 4)) * 4 + x
                    start = pl.multiple_of(block * width, width)
                    at = (j * 2 + r) * width
                    out_ref[kind * 4 + x, :, at : at + width] = ref[:, pl.ds(start, width)]
            out_ref[kind * 4 + x, :, 8 * width : 8 * width + BLOCK] = quant
            out_ref[kind * 4 + x, :, 8 * width + BLOCK :] = shift


def pack(at, attn_float, attn_quant):
    tokens, d_in = attn_float.shape
    return pl.pallas_call(
        pack_kernel,
        out_shape=jax.ShapeDtypeStruct((8, tokens, d_in // 4 + 2 * BLOCK), BF16),
        in_specs=[SCALAR, WHOLE, WHOLE],
        out_specs=WHOLE,
        compiler_params=params(),
        name="pack",
    )(at, attn_float, attn_quant)


def join_kernel(*refs):
    own_ref, got_ref, out_ref = refs[0], refs[1], refs[-1]
    n = own_ref.shape[0]
    out_ref[:n] = own_ref[...]
    out_ref[n:] = got_ref[...]


def join(own, got, after):
    n, m = own.shape
    return pl.pallas_call(
        join_kernel,
        out_shape=jax.ShapeDtypeStruct((2 * n, m), BF16),
        in_specs=[WHOLE, WHOLE] + [LEFT] * len(after),
        out_specs=WHOLE,
        compiler_params=params(),
        name="join",
    )(own, got, *after)


def project_kernel(core_ref, mine_ref, other_ref, *refs):
    *parts, out_ref = refs
    core = core_ref[0]
    rows = out_ref.shape[2]
    for n, acts in enumerate((mine_ref, other_ref)):
        where = core if n == 0 else 1 - core
        for yh in range(2):
            total, at = None, 0
            for part in parts:
                depth = part.shape[0]
                term = jnp.dot(
                    acts[yh * rows : (yh + 1) * rows, at : at + depth],
                    part[...],
                    preferred_element_type=F32,
                )
                total = term if total is None else total + term
                at += depth
            out_ref[yh, where] = total.astype(BF16)


def project(core, mine, other, parts):
    rows, cols = mine.shape[0] // 2, parts[0].shape[1]
    return pl.pallas_call(
        project_kernel,
        out_shape=jax.ShapeDtypeStruct((2, 2, rows, cols), BF16),
        in_specs=[SCALAR] + [WHOLE] * (2 + len(parts)),
        out_specs=WHOLE,
        compiler_params=params(),
        cost_estimate=pl.CostEstimate(
            flops=8 * rows * cols * 2048, bytes_accessed=8 << 20, transcendentals=0
        ),
        name="project",
    )(core.reshape(1), mine, other, *parts)


def finish_kernel(*refs):
    *parts, float_ref, quant_ref = refs
    width = parts[0].shape[2]
    for c, ref in enumerate(parts):
        for kind, out in enumerate((float_ref, quant_ref)):
            for half in range(2):
                at = kind * 8 + half * 4
                total = ref[at].astype(F32)
                for x in range(1, 4):
                    total += ref[at + x].astype(F32)
                start = (half * len(parts) + c) * width
                out[:, start : start + width] = total.astype(BF16)


def finish(parts):
    _, tokens, width = parts[0].shape
    return pl.pallas_call(
        finish_kernel,
        out_shape=(jax.ShapeDtypeStruct((tokens, 2 * len(parts) * width), BF16),) * 2,
        in_specs=[WHOLE] * len(parts),
        out_specs=(WHOLE, WHOLE),
        compiler_params=params(),
        name="finish",
    )(*parts)


def swap(a, axis):
    return lax.ppermute(a, axis, [(0, 1), (1, 0)])


def from_z(a, j):
    return lax.ppermute(a, "z", [((i + j) % 4, i) for i in range(4)])


def shards(attn_float, attn_quant, proj_weight, weight_codes, group_scales):
    tokens, d_in = attn_float.shape
    features, d_out = proj_weight.shape
    groups = group_scales.shape[0]
    half, width = d_out // 2, d_out // 2 // CHUNKS
    inverse = 1.0 / (tokens * 128)
    yh, core, yl, z = (lax.axis_index(a) for a in ("yh", "core", "yl", "z"))

    payload = pack(jnp.stack([yl, z]), attn_float, attn_quant)
    mine = lax.all_to_all(payload, ("yh", "x"), 0, 0, tiled=True)
    mine = mine.reshape(8 * tokens, 8 * features + 2 * BLOCK)
    other = swap(mine, "core")

    def weight(kind, col, n):
        plain = lax.dynamic_slice_in_dim(proj_weight, col, n, 1)
        codes = lax.dynamic_slice_in_dim(weight_codes, col, n, 1)
        scales = lax.dynamic_slice_in_dim(group_scales, col, n, 1)
        values = (codes - 8).astype(F32).reshape(groups, features // groups, n)
        quant = (values * scales[:, None, :]).reshape(features, n).astype(BF16)
        return jnp.where(kind == 0, plain, quant)

    pairs = []
    for a in range(2):
        for c in range(2):
            for b in range(2):
                pairs.append((a * 4 + c * 2 + b, (a ^ c) * 4 + c * 2 + (1 - b)))
    own, got = [], []
    for first, n in ((0, width), (width, half - width)):
        col = core * half + first
        mine_w, send_w = weight(yh, col, n), weight(yh ^ core, col, n)
        got_w = lax.ppermute(send_w, ("yh", "core", "yl"), pairs)
        for at in range(0, n, width):
            own.append(mine_w[:, at : at + width])
            got.append(got_w[:, at : at + width])

    after, results = (), []
    for c in range(CHUNKS):
        rows = join(own[c], got[c], after)
        up, down = from_z(rows, 1), from_z(rows, 3)
        after = (up, down)
        far0 = from_z(up[:features], 1)
        far1 = from_z(down[features:], 3)
        partial = project(core, mine, other, (rows, up, far0, far1, down))
        results.append(
            lax.all_to_all(
                partial.reshape(16, tokens, width), ("yh", "core", "x"), 0, 0, tiled=True
            )
        )
    float_out, quant_out = finish(results)

    def stats(j):
        at = 2 * j * features
        total = 0.0
        for acts in (mine, other):
            picked = jnp.where(
                core == 0, acts[:, at : at + features], acts[:, at + features : at + 2 * features]
            )
            total = total + lax.dot_general(
                picked, acts[:, 8 * features :], (((0,), (0,)), ((), ())), preferred_element_type=F32
            )
        return total

    total = 0.0
    for j in range(4):
        pairs = [
            (c * 8 + b * 4 + i, c * 8 + (b ^ c) * 4 + (i + j) % 4)
            for c in range(2)
            for b in range(2)
            for i in range(4)
        ]
        total = total + lax.ppermute(stats(j).astype(BF16), ("core", "yl", "z"), pairs).astype(F32)
    total = (total + swap(total, "core")) * inverse
    total = jnp.where(yh == 1, total, swap(total, "yh"))
    return float_out, quant_out, total[:, :BLOCK], total[:, BLOCK:]


def solution(mesh):
    fine = Mesh(mesh.devices.reshape(2, 2, 2, 4, 4), FINE)
    rows, tok = P(FINE, None), P(("yl", "z", "x"), None)
    return jax.shard_map(
        shards,
        mesh=fine,
        in_specs=(rows, rows, tok, tok, tok),
        out_specs=(rows, rows, tok, tok),
        check_vma=False,
    )
```

time: 167 us -> 225 us (1.35)
  blocking collectives: 0 us -> 38.1 us
  waiting for transfers between devices: 85.2 us -> 57.8 us
  starting transfers between devices: 39.1 us -> 62.7 us
  Pallas kernels: 4.2 us -> 22.2 us
  matrix products: 24.2 us -> 13.4 us
  local copies, waits for them, and re-layouts: 8.48 us -> 18.9 us
  other arithmetic: 3.19 us -> 8.87 us
    all_to_all x0 -> x1, blocking collectives: none -> 38.1 us  [shards(): mine = lax.all_to_all(payload, ('yh', 'x'), 0, 0, tiled=True)]
    all_to_all x4, waiting for transfers between devices: 25.8 us -> 0.54 us  [shards(): lax.all_to_all(partial.reshape(16, tokens, width), ('yh', 'core', 'x'), 0...]
    pallas_call x2 -> x10, Pallas kernels: 4.2 us -> 22.2 us  [the longest x4 16.9 us: project(): pl.pallas_call(project_kernel, out_shape=jax.ShapeDtypeStruct((2, 2, rows...]
    ppermute x7 -> x22, starting transfers between devices: 13.6 us -> 26.8 us  [the longest x16 19.9 us: from_z(): return lax.ppermute(a, 'z', [((i + j) % 4, i) for i in range(4)])]
    dot_general x6 -> x8, matrix products: 24.2 us -> 13.4 us  [stats(): lax.dot_general(picked, acts[:, 8 * features:], (((0,), (0,)), ((), ())),...]
    slice x0 -> x10, local copies, waits for them, and re-layouts: none -> 9.88 us  [the longest x4 3.62 us: shards(): far1 = from_z(down[features:], 3)]
    ppermute x3, starting transfers between devices: 3.46 us -> 9.92 us  [swap(): return lax.ppermute(a, axis, [(0, 1), (1, 0)])]
    ppermute x7 -> x22, waiting for transfers between devices: 46.1 us -> 40.2 us  [the longest x16 28.6 us: from_z(): return lax.ppermute(a, 'z', [((i + j) % 4, i) for i in range(4)])]
  transfers between devices with their start and end apart: 14 -> 29, of which waited for: 10 -> 10; matrix products, arithmetic and copies ran while one was open for 18% -> 15% of each run, Pallas kernels for 1% -> 8%
where the time goes in v2:
time: 225 us; the launch traced here: 223 us
  starting transfers between devices  62.7 us (28%)
  waiting for transfers between devices  57.8 us (26%)
  blocking collectives  38.1 us (17%)
  Pallas kernels  22.2 us (10%)
  local copies, waits for them, and re-layouts  18.9 us (8%)
  matrix products  13.4 us (6%)
  other arithmetic  8.87 us (4%)
    all_to_all x1, blocking collectives, shards(): mine = lax.all_to_all(payload, ('yh', 'x'), 0, 0, tiled=True)  38.1 us
    ppermute x16, waiting for transfers between devices, from_z(): return lax.ppermute(a, 'z', [((i + j) % 4, i) for i in range(4)])  28.6 us
    all_to_all x4, starting transfers between devices, shards(): lax.all_to_all(partial.reshape(16, tokens, width), ('yh', 'core', 'x'), 0...  26 us
    ppermute x16, starting transfers between devices, from_z(): return lax.ppermute(a, 'z', [((i + j) % 4, i) for i in range(4)])  19.9 us
    ppermute x3, waiting for transfers between devices, swap(): return lax.ppermute(a, axis, [(0, 1), (1, 0)])  17 us
    pallas_call x4, Pallas kernels, project(): pl.pallas_call(project_kernel, out_shape=jax.ShapeDtypeStruct((2, 2, rows...  16.9 us
    dot_general x8, matrix products, stats(): lax.dot_general(picked, acts[:, 8 * features:], (((0,), (0,)), ((), ())),...  13.4 us
    ppermute x2, waiting for transfers between devices, shards(): got_w = lax.ppermute(send_w, ('yh', 'core', 'yl'), pairs)  11.7 us
  transfers between devices with their start and end apart: 29, of which 10 were waited for; matrix products, arithmetic and copies ran while one was open for 15% of the time, Pallas kernels for 8%

profile of v2, /device:TPU:0, one launch (start us, length us, event | category | flops | bytes accessed | tf_op | source)
XLA Modules:
  0.0 222.9 jit_solution(6213798980627262516)
XLA Ops:
  4.0 38.1 %all_to_all.25 = bf16[8,64,2304]{2,1,0:T(8,128)(2,1)S(1)} all-to-all(bf16[8,64,2304]{2,1,0:T(8,128)(2,1)S(1)} %pack.1), channel_id=1, replica_groups=mesh['yh'=2,'core'=2,'yl'=2,'z'=4,'x'=4] {'yh','x'}, dimensions={0} | all-to-all | bytes 4718592 | tf_op jit(solution)/shard_map/all_to_all | solution.py:149
  42.1 3.8 %broadcast_select_fusion = (bf16[256,1536]{1,0:T(8,128)(2,1)}, bf16[256,1536]{1,0:T(8,128)(2,1)S(1)}) fusion(pred[]{:T(512)S(6)} %eq.9, bf16[256,4096]{1,0:T(8,128)(2,1)} %param.7, s32[]{:T(128)S(6)} %select_n.94, f32[2,1536]{1,0:T(2,128)S(1)} %constant_dynamic-slice_fusion, s32[256,4096]{1,0:T(8,128)} %param.8, pred[]{:T(512)S(6)} %eq.8), kind=kLoop, calls=%fused_computation.10 | loop fusion | flops 2359296 | bytes 3944454 | tf_op jit(solution)/shard_map/jit(_where)/select_n | solution.py:159
  49.2 11.6 %collective-permute-done.1.refs_1_ = bf16[256,512]{1,0:T(8,128)(2,1)S(1)} collective-permute-done((bf16[256,512]{1,0:T(8,128)(2,1)S(1)}, bf16[256,512]{1,0:T(8,128)(2,1)S(1)}, u32[]{:S(2)}, u32[]{:S(2)}) %collective-permute-start.1) | collective-permute-done | bytes 262176 | tf_op jit(solution)/shard_map/ppermute | solution.py:170
  60.9 4.1 %collective-permute-start.2 = (bf16[512,512]{1,0:T(8,128)(2,1)S(1)}, bf16[512,512]{1,0:T(8,128)(2,1)S(1)}, u32[]{:S(2)}, u32[]{:S(2)}) collective-permute-start(bf16[512,512]{1,0:T(8,128)(2,1)S(1)} %join.4.refs_0_), channel_id=1, source_target_pairs={{4,0},{8,4},{12,8},{0,12},{5,1},{9,5},{13,9},{1,13},{6,2},{10,6},{... | collective-permute-start | bytes 1572872 | tf_op jit(solution)/shard_map/ppermute | solution.py:137
  65.8 1.9 fusion.34
  67.7 8.4 %collective-permute-done.2.refs_1_.refs_2_ = bf16[512,512]{1,0:T(8,128)(2,1)S(1)} collective-permute-done((bf16[512,512]{1,0:T(8,128)(2,1)S(1)}, bf16[512,512]{1,0:T(8,128)(2,1)S(1)}, u32[]{:S(2)}, u32[]{:S(2)}) %collective-permute-start.2) | collective-permute-done | bytes 524320 | tf_op jit(solution)/shard_map/ppermute | solution.py:137
  76.1 3.4 %collective-permute-done.4.refs_4_.refs_3_ = bf16[512,512]{1,0:T(8,128)(2,1)S(1)} collective-permute-done((bf16[512,512]{1,0:T(8,128)(2,1)S(1)}, bf16[512,512]{1,0:T(8,128)(2,1)S(1)}, u32[]{:S(2)}, u32[]{:S(2)}) %collective-permute-start.4) | collective-permute-done | bytes 524320 | tf_op jit(solution)/shard_map/ppermute | solution.py:137
  79.9 1.7 collective-permute-start.9
  83.9 10.6 %collective-permute-done.7.refs_1_.refs_2_ = bf16[512,512]{1,0:T(8,128)(2,1)S(1)} collective-permute-done((bf16[512,512]{1,0:T(8,128)(2,1)S(1)}, bf16[512,512]{1,0:T(8,128)(2,1)S(1)}, u32[]{:S(2)}, u32[]{:S(2)}) %collective-permute-start.7) | collective-permute-done | bytes 524320 | tf_op jit(solution)/shard_map/ppermute | solution.py:137
  96.9 2.0 collective-permute-start.13
  101.6 4.0 %project.4 = bf16[2,2,256,512]{3,2,1,0:T(8,128)(2,1)S(1)} custom-call(s32[1]{0:T(128)} %bitcast.core_ref, bf16[512,2304]{1,0:T(8,128)(2,1)S(1)} %bitcast.25, bf16[512,2304]{1,0:T(8,128)(2,1)} %collective-permute-done.other_ref, bf16[512,512]{1,0:T(8,128)(2,1)S(1)} %join.4.refs_0_, bf16[512,512]{1,0:T(8,128)(2,1)S(1)} %collective-permute-done.2.refs_1_.refs_2_, ...), custom_call_target="tpu_custom_call" | custom-call | flops 2147483648 | bytes 8388608 | tf_op jit(solution)/shard_map/project/pallas_call | solution.py:93
  106.6 3.7 %all-to-all-start.1 = ((bf16[16,64,512]{2,1,0:T(8,128)(2,1)}), bf16[16,64,512]{2,1,0:T(8,128)(2,1)S(1)}, u32[]{:S(2)}, u32[]{:S(2)}) async-start(bf16[16,64,512]{2,1,0:T(8,128)(2,1)} %bitcast.34), calls=%async_computation.1 | async-start | bytes 2097152 | tf_op jit(solution)/shard_map/all_to_all | solution.py:184
  112.3 2.1 collective-permute-start.10
  120.8 2.4 %collective-permute-start.12 = (bf16[256,512]{1,0:T(8,128)(2,1)}, bf16[256,512]{1,0:T(8,128)(2,1)}, u32[]{:S(2)}, u32[]{:S(2)}) collective-permute-start(bf16[256,512]{1,0:T(8,128)(2,1)} %slice.150), channel_id=1, source_target_pairs={{4,0},{8,4},{12,8},{0,12},{5,1},{9,5},{13,9},{1,13},{6,2},{10,6},{... | collective-permute-start | bytes 786440 | tf_op jit(solution)/shard_map/ppermute | solution.py:137
  126.9 4.0 %project.5 = bf16[2,2,256,512]{3,2,1,0:T(8,128)(2,1)S(1)} custom-call(s32[1]{0:T(128)} %bitcast.core_ref, bf16[512,2304]{1,0:T(8,128)(2,1)S(1)} %bitcast.28, bf16[512,2304]{1,0:T(8,128)(2,1)} %collective-permute-done.other_ref, bf16[512,512]{1,0:T(8,128)(2,1)S(1)} %copy-done.17, bf16[512,512]{1,0:T(8,128)(2,1)S(1)} %copy-done.5, ...), custom_call_target="tpu_custom_call" | custom-call | flops 2147483648 | bytes 8388608 | tf_op jit(solution)/shard_map/project/pallas_call | solution.py:93
  131.8 7.3 %all-to-all-start.2 = ((bf16[16,64,512]{2,1,0:T(8,128)(2,1)}), bf16[16,64,512]{2,1,0:T(8,128)(2,1)S(1)}, u32[]{:S(2)}, u32[]{:S(2)}) async-start(bf16[16,64,512]{2,1,0:T(8,128)(2,1)} %bitcast.35), calls=%async_computation.2 | async-start | bytes 2097152 | tf_op jit(solution)/shard_map/all_to_all | solution.py:184
  139.2 2.3 %fusion.13 = f32[256,256]{1,0:T(8,128)} fusion(bf16[512,2304]{1,0:T(8,128)(2,1)} %bitcast.29, pred[]{:T(512)S(6)} %eq.11), kind=kOutput, calls=%fused_computation.27 | convolution fusion | flops 67239936 | bytes 1048577 | tf_op jit(solution)/shard_map/dot_general | solution.py:197
  141.4 2.1 fusion.16
  143.5 2.1 fusion.4
  145.6 3.2 %collective-permute-start.22 = (bf16[256,256]{1,0:T(8,128)(2,1)}, bf16[256,256]{1,0:T(8,128)(2,1)}, u32[]{:S(2)}, u32[]{:S(2)}) collective-permute-start(bf16[256,256]{1,0:T(8,128)(2,1)} %fusion.4), channel_id=1, source_target_pairs={{0,12},{4,0},{8,4},{12,8},{16,28},{20,16},{24,20},{28,24},{32,60},... | collective-permute-start | bytes 393224 | tf_op jit(solution)/shard_map/ppermute | solution.py:210
  148.8 2.1 fusion.3
  150.9 4.6 %project.6 = bf16[2,2,256,512]{3,2,1,0:T(8,128)(2,1)S(1)} custom-call(s32[1]{0:T(128)} %bitcast.core_ref, bf16[512,2304]{1,0:T(8,128)(2,1)S(1)} %bitcast.31, bf16[512,2304]{1,0:T(8,128)(2,1)} %collective-permute-done.other_ref, bf16[512,512]{1,0:T(8,128)(2,1)} %join.6.refs_0_, bf16[512,512]{1,0:T(8,128)(2,1)} %collective-permute-done.11.refs_1_.refs_2_, ...), custom_call_target="tpu_custom_call" | custom-call | flops 2147483648 | bytes 8388608 | tf_op jit(solution)/shard_map/project/pallas_call | solution.py:93
  157.0 6.8 %all-to-all-start.3 = ((bf16[16,64,512]{2,1,0:T(8,128)(2,1)}), bf16[16,64,512]{2,1,0:T(8,128)(2,1)S(1)}, u32[]{:S(2)}, u32[]{:S(2)}) async-start(bf16[16,64,512]{2,1,0:T(8,128)(2,1)} %bitcast.33), calls=%async_computation.3 | async-start | bytes 2097152 | tf_op jit(solution)/shard_map/all_to_all | solution.py:184
  169.4 2.5 %collective-permute-start.16 = (bf16[256,512]{1,0:T(8,128)(2,1)S(1)}, bf16[256,512]{1,0:T(8,128)(2,1)S(1)}, u32[]{:S(2)}, u32[]{:S(2)}) collective-permute-start(bf16[256,512]{1,0:T(8,128)(2,1)S(1)} %slice.154), channel_id=1, source_target_pairs={{4,0},{8,4},{12,8},{0,12},{5,1},{9,5},{13,9},{1,13},{6,2},{10,6},{... | collective-permute-start | bytes 786440 | tf_op jit(solution)/shard_map/ppermute | solution.py:137
  173.3 1.7 convert_add_fusion
  175.0 6.5 %collective-permute-start.23 = (f32[256,256]{1,0:T(8,128)}, f32[256,256]{1,0:T(8,128)}, u32[]{:S(2)}, u32[]{:S(2)}) collective-permute-start(f32[256,256]{1,0:T(8,128)} %convert_add_fusion), channel_id=1, source_target_pairs={{0,32},{32,0},{1,33},{33,1},{2,34},{34,2},{3,35},{35,3},{4,36},{36... | collective-permute-start | bytes 786440 | tf_op jit(solution)/shard_map/ppermute | solution.py:133
  181.5 1.9 collective-permute-done.18.refs_3_
  183.4 4.4 %project.7 = bf16[2,2,256,512]{3,2,1,0:T(8,128)(2,1)S(1)} custom-call(s32[1]{0:T(128)} %bitcast.core_ref, bf16[512,2304]{1,0:T(8,128)(2,1)S(1)} %bitcast.32, bf16[512,2304]{1,0:T(8,128)(2,1)} %collective-permute-done.other_ref, bf16[512,512]{1,0:T(8,128)(2,1)} %join.7.refs_0_, bf16[512,512]{1,0:T(8,128)(2,1)} %collective-permute-done.15.refs_1_, ...), custom_call_target="tpu_custom_call" | custom-call | flops 2147483648 | bytes 8388608 | tf_op jit(solution)/shard_map/project/pallas_call | solution.py:93
  188.8 8.2 %all-to-all-start.4 = ((bf16[16,64,512]{2,1,0:T(8,128)(2,1)}), bf16[16,64,512]{2,1,0:T(8,128)(2,1)}, u32[]{:S(2)}, u32[]{:S(2)}) async-start(bf16[16,64,512]{2,1,0:T(8,128)(2,1)} %bitcast.36), calls=%async_computation.4 | async-start | bytes 2097152 | tf_op jit(solution)/shard_map/all_to_all | solution.py:184
  198.1 3.5 %collective-permute-start.24 = (f32[256,256]{1,0:T(8,128)S(1)}, f32[256,256]{1,0:T(8,128)}, u32[]{:S(2)}, u32[]{:S(2)}) collective-permute-start(f32[256,256]{1,0:T(8,128)S(1)} %add_multiply_fusion), channel_id=1, source_target_pairs={{0,64},{64,0},{1,65},{65,1},{2,66},{66,2},{3,67},{67,3},{4,68},{68... | collective-permute-start | bytes 786440 | tf_op jit(solution)/shard_map/ppermute | solution.py:133
  201.6 17.0 %collective-permute-done.24 = f32[256,256]{1,0:T(8,128)} collective-permute-done((f32[256,256]{1,0:T(8,128)S(1)}, f32[256,256]{1,0:T(8,128)}, u32[]{:S(2)}, u32[]{:S(2)}) %collective-permute-start.24) | collective-permute-done | bytes 262176 | tf_op jit(solution)/shard_map/ppermute | solution.py:133
  220.3 2.6 %finish.1 = (bf16[64,4096]{1,0:T(8,128)(2,1)}, bf16[64,4096]{1,0:T(8,128)(2,1)}) custom-call(bf16[16,64,512]{2,1,0:T(8,128)(2,1)S(1)} %all-to-all-done.1.refs_0_, bf16[16,64,512]{2,1,0:T(8,128)(2,1)S(1)} %all-to-all-done.2.refs_1_, bf16[16,64,512]{2,1,0:T(8,128)(2,1)S(1)} %all-to-all-done.3.refs_2_, bf16[16,64,512]{2,1,0:T(8,128)(2,1)} %all-to-all-done.4.refs_3_), custom_call_target="tpu_custom_call" | custom-call | tf_op jit(solution)/shard_map/finish/pallas_call | solution.py:122
  (106 shorter events, 41.5 us)
Async XLA Ops:
  0.6 41.5 %copy-start = (f32[2,4096]{1,0:T(2,128)S(1)}, f32[2,4096]{1,0:T(2,128)}, u32[]{:S(2)}) copy-start(f32[2,4096]{1,0:T(2,128)} %param.9) | copy-start | bytes 98308
  42.1 84.8 %copy-start.1 = (bf16[8,64,2304]{2,1,0:T(8,128)(2,1)}, bf16[8,64,2304]{2,1,0:T(8,128)(2,1)S(1)}, u32[]{:S(2)}) copy-start(bf16[8,64,2304]{2,1,0:T(8,128)(2,1)S(1)} %all_to_all.25) | copy-start | bytes 7077892
  42.1 59.5 %collective-permute-start = (bf16[512,2304]{1,0:T(8,128)(2,1)S(1)}, bf16[512,2304]{1,0:T(8,128)(2,1)}, u32[]{:S(2)}, u32[]{:S(2)}) collective-permute-start(bf16[512,2304]{1,0:T(8,128)(2,1)S(1)} %bitcast.24), channel_id=1, source_target_pairs={{0,32},{32,0},{1,33},{33,1},{2,34},{34,2},{3,35},{35,3},{4,36},{36... | collective-permute-start | bytes 7077896 | tf_op jit(solution)/shard_map/ppermute | solution.py:133
  45.9 19.9 %collective-permute-start.6 = (bf16[256,1536]{1,0:T(8,128)(2,1)}, bf16[256,1536]{1,0:T(8,128)(2,1)}, u32[]{:S(2)}, u32[]{:S(2)}) collective-permute-start(bf16[256,1536]{1,0:T(8,128)(2,1)} %get-tuple-element.8), channel_id=1, source_target_pairs={{0,16},{16,0},{32,112},{48,96},{64,80},{80,64},{96,48},{112,32},{1... | collective-permute-start | bytes 2359304 | tf_op jit(solution)/shard_map/ppermute | solution.py:170
  47.8 13.1 %collective-permute-start.1 = (bf16[256,512]{1,0:T(8,128)(2,1)S(1)}, bf16[256,512]{1,0:T(8,128)(2,1)S(1)}, u32[]{:S(2)}, u32[]{:S(2)}) collective-permute-start(bf16[256,512]{1,0:T(8,128)(2,1)S(1)} %get-tuple-element.10), channel_id=1, source_target_pairs={{0,16},{16,0},{32,112},{48,96},{64,80},{80,64},{96,48},{112,32},{1... | collective-permute-start | bytes 786440 | tf_op jit(solution)/shard_map/ppermute | solution.py:170
  60.9 15.2 %collective-permute-start.2 = (bf16[512,512]{1,0:T(8,128)(2,1)S(1)}, bf16[512,512]{1,0:T(8,128)(2,1)S(1)}, u32[]{:S(2)}, u32[]{:S(2)}) collective-permute-start(bf16[512,512]{1,0:T(8,128)(2,1)S(1)} %join.4.refs_0_), channel_id=1, source_target_pairs={{4,0},{8,4},{12,8},{0,12},{5,1},{9,5},{13,9},{1,13},{6,2},{10,6},{... | collective-permute-start | bytes 1572872 | tf_op jit(solution)/shard_map/ppermute | solution.py:137
  65.0 14.5 %collective-permute-start.4 = (bf16[512,512]{1,0:T(8,128)(2,1)S(1)}, bf16[512,512]{1,0:T(8,128)(2,1)S(1)}, u32[]{:S(2)}, u32[]{:S(2)}) collective-permute-start(bf16[512,512]{1,0:T(8,128)(2,1)S(1)} %join.4.refs_0_), channel_id=1, source_target_pairs={{12,0},{0,4},{4,8},{8,12},{13,1},{1,5},{5,9},{9,13},{14,2},{2,6},{... | collective-permute-start | bytes 1572872 | tf_op jit(solution)/shard_map/ppermute | solution.py:137
  79.6 14.9 %collective-permute-start.7 = (bf16[512,512]{1,0:T(8,128)(2,1)S(1)}, bf16[512,512]{1,0:T(8,128)(2,1)S(1)}, u32[]{:S(2)}, u32[]{:S(2)}) collective-permute-start(bf16[512,512]{1,0:T(8,128)(2,1)S(1)} %join.5.refs_0_), channel_id=1, source_target_pairs={{4,0},{8,4},{12,8},{0,12},{5,1},{9,5},{13,9},{1,13},{6,2},{10,6},{... | collective-permute-start | bytes 1572872 | tf_op jit(solution)/shard_map/ppermute | solution.py:137
  79.9 16.1 %collective-permute-start.9 = (bf16[512,512]{1,0:T(8,128)(2,1)S(1)}, bf16[512,512]{1,0:T(8,128)(2,1)S(1)}, u32[]{:S(2)}, u32[]{:S(2)}) collective-permute-start(bf16[512,512]{1,0:T(8,128)(2,1)S(1)} %join.5.refs_0_), channel_id=1, source_target_pairs={{12,0},{0,4},{4,8},{8,12},{13,1},{1,5},{5,9},{9,13},{14,2},{2,6},{... | collective-permute-start | bytes 1572872 | tf_op jit(solution)/shard_map/ppermute | solution.py:137
  81.7 18.4 %collective-permute-start.3 = (bf16[256,512]{1,0:T(8,128)(2,1)S(1)}, bf16[256,512]{1,0:T(8,128)(2,1)S(1)}, u32[]{:S(2)}, u32[]{:S(2)}) collective-permute-start(bf16[256,512]{1,0:T(8,128)(2,1)S(1)} %slice.142), channel_id=1, source_target_pairs={{4,0},{8,4},{12,8},{0,12},{5,1},{9,5},{13,9},{1,13},{6,2},{10,6},{... | collective-permute-start | bytes 786440 | tf_op jit(solution)/shard_map/ppermute | solution.py:137
  83.3 18.3 %collective-permute-start.5 = (bf16[256,512]{1,0:T(8,128)(2,1)S(1)}, bf16[256,512]{1,0:T(8,128)(2,1)S(1)}, u32[]{:S(2)}, u32[]{:S(2)}) collective-permute-start(bf16[256,512]{1,0:T(8,128)(2,1)S(1)} %slice.143), channel_id=1, source_target_pairs={{12,0},{0,4},{4,8},{8,12},{13,1},{1,5},{5,9},{9,13},{14,2},{2,6},{... | collective-permute-start | bytes 786440 | tf_op jit(solution)/shard_map/ppermute | solution.py:137
  96.9 17.5 %collective-permute-start.11 = (bf16[512,512]{1,0:T(8,128)(2,1)}, bf16[512,512]{1,0:T(8,128)(2,1)}, u32[]{:S(2)}, u32[]{:S(2)}) collective-permute-start(bf16[512,512]{1,0:T(8,128)(2,1)} %join.6.refs_0_), channel_id=1, source_target_pairs={{4,0},{8,4},{12,8},{0,12},{5,1},{9,5},{13,9},{1,13},{6,2},{10,6},{... | collective-permute-start | bytes 1572872 | tf_op jit(solution)/shard_map/ppermute | solution.py:137
  96.9 17.5 %collective-permute-start.13 = (bf16[512,512]{1,0:T(8,128)(2,1)}, bf16[512,512]{1,0:T(8,128)(2,1)}, u32[]{:S(2)}, u32[]{:S(2)}) collective-permute-start(bf16[512,512]{1,0:T(8,128)(2,1)} %join.6.refs_0_), channel_id=1, source_target_pairs={{12,0},{0,4},{4,8},{8,12},{13,1},{1,5},{5,9},{9,13},{14,2},{2,6},{... | collective-permute-start | bytes 1572872 | tf_op jit(solution)/shard_map/ppermute | solution.py:137
  106.6 25.3 %all-to-all-start.1 = ((bf16[16,64,512]{2,1,0:T(8,128)(2,1)}), bf16[16,64,512]{2,1,0:T(8,128)(2,1)S(1)}, u32[]{:S(2)}, u32[]{:S(2)}) async-start(bf16[16,64,512]{2,1,0:T(8,128)(2,1)} %bitcast.34), calls=%async_computation.1 | async-start | bytes 2097152 | tf_op jit(solution)/shard_map/all_to_all | solution.py:184
  111.2 15.6 %collective-permute-start.8 = (bf16[256,512]{1,0:T(8,128)(2,1)S(1)}, bf16[256,512]{1,0:T(8,128)(2,1)S(1)}, u32[]{:S(2)}, u32[]{:S(2)}) collective-permute-start(bf16[256,512]{1,0:T(8,128)(2,1)S(1)} %slice.146), channel_id=1, source_target_pairs={{4,0},{8,4},{12,8},{0,12},{5,1},{9,5},{13,9},{1,13},{6,2},{10,6},{... | collective-permute-start | bytes 786440 | tf_op jit(solution)/shard_map/ppermute | solution.py:137
  112.3 14.6 %collective-permute-start.10 = (bf16[256,512]{1,0:T(8,128)(2,1)S(1)}, bf16[256,512]{1,0:T(8,128)(2,1)S(1)}, u32[]{:S(2)}, u32[]{:S(2)}) collective-permute-start(bf16[256,512]{1,0:T(8,128)(2,1)S(1)} %slice.147), channel_id=1, source_target_pairs={{12,0},{0,4},{4,8},{8,12},{13,1},{1,5},{5,9},{9,13},{14,2},{2,6},{... | collective-permute-start | bytes 786440 | tf_op jit(solution)/shard_map/ppermute | solution.py:137
  117.1 50.7 %collective-permute-start.15 = (bf16[512,512]{1,0:T(8,128)(2,1)}, bf16[512,512]{1,0:T(8,128)(2,1)}, u32[]{:S(2)}, u32[]{:S(2)}) collective-permute-start(bf16[512,512]{1,0:T(8,128)(2,1)} %join.7.refs_0_), channel_id=1, source_target_pairs={{4,0},{8,4},{12,8},{0,12},{5,1},{9,5},{13,9},{1,13},{6,2},{10,6},{... | collective-permute-start | bytes 1572872 | tf_op jit(solution)/shard_map/ppermute | solution.py:137
  118.3 51.1 %collective-permute-start.17 = (bf16[512,512]{1,0:T(8,128)(2,1)}, bf16[512,512]{1,0:T(8,128)(2,1)}, u32[]{:S(2)}, u32[]{:S(2)}) collective-permute-start(bf16[512,512]{1,0:T(8,128)(2,1)} %join.7.refs_0_), channel_id=1, source_target_pairs={{12,0},{0,4},{4,8},{8,12},{13,1},{1,5},{5,9},{9,13},{14,2},{2,6},{... | collective-permute-start | bytes 1572872 | tf_op jit(solution)/shard_map/ppermute | solution.py:137
  120.8 30.1 %collective-permute-start.12 = (bf16[256,512]{1,0:T(8,128)(2,1)}, bf16[256,512]{1,0:T(8,128)(2,1)}, u32[]{:S(2)}, u32[]{:S(2)}) collective-permute-start(bf16[256,512]{1,0:T(8,128)(2,1)} %slice.150), channel_id=1, source_target_pairs={{4,0},{8,4},{12,8},{0,12},{5,1},{9,5},{13,9},{1,13},{6,2},{10,6},{... | collective-permute-start | bytes 786440 | tf_op jit(solution)/shard_map/ppermute | solution.py:137
  126.8 24.1 %collective-permute-start.14 = (bf16[256,512]{1,0:T(8,128)(2,1)}, bf16[256,512]{1,0:T(8,128)(2,1)}, u32[]{:S(2)}, u32[]{:S(2)}) collective-permute-start(bf16[256,512]{1,0:T(8,128)(2,1)} %slice.151), channel_id=1, source_target_pairs={{12,0},{0,4},{4,8},{8,12},{13,1},{1,5},{5,9},{9,13},{14,2},{2,6},{... | collective-permute-start | bytes 786440 | tf_op jit(solution)/shard_map/ppermute | solution.py:137
  131.8 25.1 %all-to-all-start.2 = ((bf16[16,64,512]{2,1,0:T(8,128)(2,1)}), bf16[16,64,512]{2,1,0:T(8,128)(2,1)S(1)}, u32[]{:S(2)}, u32[]{:S(2)}) async-start(bf16[16,64,512]{2,1,0:T(8,128)(2,1)} %bitcast.35), calls=%async_computation.2 | async-start | bytes 2097152 | tf_op jit(solution)/shard_map/all_to_all | solution.py:184
  145.6 27.3 %collective-permute-start.22 = (bf16[256,256]{1,0:T(8,128)(2,1)}, bf16[256,256]{1,0:T(8,128)(2,1)}, u32[]{:S(2)}, u32[]{:S(2)}) collective-permute-start(bf16[256,256]{1,0:T(8,128)(2,1)} %fusion.4), channel_id=1, source_target_pairs={{0,12},{4,0},{8,4},{12,8},{16,28},{20,16},{24,20},{28,24},{32,60},... | collective-permute-start | bytes 393224 | tf_op jit(solution)/shard_map/ppermute | solution.py:210
  150.9 22.4 %collective-permute-start.21 = (bf16[256,256]{1,0:T(8,128)(2,1)}, bf16[256,256]{1,0:T(8,128)(2,1)}, u32[]{:S(2)}, u32[]{:S(2)}) collective-permute-start(bf16[256,256]{1,0:T(8,128)(2,1)} %fusion.3), channel_id=1, source_target_pairs={{0,8},{4,12},{8,0},{12,4},{16,24},{20,28},{24,16},{28,20},{32,56},... | collective-permute-start | bytes 393224 | tf_op jit(solution)/shard_map/ppermute | solution.py:210
  157.0 31.8 %all-to-all-start.3 = ((bf16[16,64,512]{2,1,0:T(8,128)(2,1)}), bf16[16,64,512]{2,1,0:T(8,128)(2,1)S(1)}, u32[]{:S(2)}, u32[]{:S(2)}) async-start(bf16[16,64,512]{2,1,0:T(8,128)(2,1)} %bitcast.33), calls=%async_computation.3 | async-start | bytes 2097152 | tf_op jit(solution)/shard_map/all_to_all | solution.py:184
  163.8 19.6 %copy-start.3 = (bf16[8,64,2304]{2,1,0:T(8,128)(2,1)S(1)}, bf16[8,64,2304]{2,1,0:T(8,128)(2,1)}, u32[]{:S(2)}) copy-start(bf16[8,64,2304]{2,1,0:T(8,128)(2,1)} %copy-done.1) | copy-start | bytes 7077892
  165.4 7.9 %collective-permute-start.20 = (bf16[256,256]{1,0:T(8,128)(2,1)S(1)}, bf16[256,256]{1,0:T(8,128)(2,1)S(1)}, u32[]{:S(2)}, u32[]{:S(2)}) collective-permute-start(bf16[256,256]{1,0:T(8,128)(2,1)S(1)} %fusion.2), channel_id=1, source_target_pairs={{0,4},{4,8},{8,12},{12,0},{16,20},{20,24},{24,28},{28,16},{32,52},... | collective-permute-start | bytes 393224 | tf_op jit(solution)/shard_map/ppermute | solution.py:210
  167.8 5.5 %collective-permute-start.19 = (bf16[256,256]{1,0:T(8,128)(2,1)S(1)}, bf16[256,256]{1,0:T(8,128)(2,1)S(1)}, u32[]{:S(2)}, u32[]{:S(2)}) collective-permute-start(bf16[256,256]{1,0:T(8,128)(2,1)S(1)} %fusion.1), channel_id=1, source_target_pairs={{0,0},{4,4},{8,8},{12,12},{16,16},{20,20},{24,24},{28,28},{32,48},... | collective-permute-start | bytes 393224 | tf_op jit(solution)/shard_map/ppermute | solution.py:210
  169.4 12.1 %collective-permute-start.16 = (bf16[256,512]{1,0:T(8,128)(2,1)S(1)}, bf16[256,512]{1,0:T(8,128)(2,1)S(1)}, u32[]{:S(2)}, u32[]{:S(2)}) collective-permute-start(bf16[256,512]{1,0:T(8,128)(2,1)S(1)} %slice.154), channel_id=1, source_target_pairs={{4,0},{8,4},{12,8},{0,12},{5,1},{9,5},{13,9},{1,13},{6,2},{10,6},{... | collective-permute-start | bytes 786440 | tf_op jit(solution)/shard_map/ppermute | solution.py:137
  172.9 10.5 %collective-permute-start.18 = (bf16[256,512]{1,0:T(8,128)(2,1)S(1)}, bf16[256,512]{1,0:T(8,128)(2,1)S(1)}, u32[]{:S(2)}, u32[]{:S(2)}) collective-permute-start(bf16[256,512]{1,0:T(8,128)(2,1)S(1)} %slice.155), channel_id=1, source_target_pairs={{12,0},{0,4},{4,8},{8,12},{13,1},{1,5},{5,9},{9,13},{14,2},{2,6},{... | collective-permute-start | bytes 786440 | tf_op jit(solution)/shard_map/ppermute | solution.py:137
  175.0 22.0 %collective-permute-start.23 = (f32[256,256]{1,0:T(8,128)}, f32[256,256]{1,0:T(8,128)}, u32[]{:S(2)}, u32[]{:S(2)}) collective-permute-start(f32[256,256]{1,0:T(8,128)} %convert_add_fusion), channel_id=1, source_target_pairs={{0,32},{32,0},{1,33},{33,1},{2,34},{34,2},{3,35},{35,3},{4,36},{36... | collective-permute-start | bytes 786440 | tf_op jit(solution)/shard_map/ppermute | solution.py:133
  188.8 31.5 %all-to-all-start.4 = ((bf16[16,64,512]{2,1,0:T(8,128)(2,1)}), bf16[16,64,512]{2,1,0:T(8,128)(2,1)}, u32[]{:S(2)}, u32[]{:S(2)}) async-start(bf16[16,64,512]{2,1,0:T(8,128)(2,1)} %bitcast.36), calls=%async_computation.4 | async-start | bytes 2097152 | tf_op jit(solution)/shard_map/all_to_all | solution.py:184
  198.1 20.5 %collective-permute-start.24 = (f32[256,256]{1,0:T(8,128)S(1)}, f32[256,256]{1,0:T(8,128)}, u32[]{:S(2)}, u32[]{:S(2)}) collective-permute-start(f32[256,256]{1,0:T(8,128)S(1)} %add_multiply_fusion), channel_id=1, source_target_pairs={{0,64},{64,0},{1,65},{65,1},{2,66},{66,2},{3,67},{67,3},{4,68},{68... | collective-permute-start | bytes 786440 | tf_op jit(solution)/shard_map/ppermute | solution.py:133
  (18 other events, 112.3 us)

commit v3 on v2

--- a/solution.py
+++ b/solution.py
@@ -7,7 +7,7 @@
 from jax.sharding import PartitionSpec as P
 
 BLOCK = 128
-CHUNKS = 4
+WIDTHS = (768, 768, 512)
 FINE = ("yh", "core", "yl", "z", "x")
 F32 = jnp.float32
 BF16 = jnp.bfloat16
@@ -17,10 +17,10 @@
 
 
 def params():
-    return pltpu.CompilerParams(vmem_limit_bytes=40 << 20)
-
-
-def pack_kernel(at_ref, float_ref, quant_ref, out_ref):
+    return pltpu.CompilerParams(vmem_limit_bytes=16 << 20)
+
+
+def pack_kernel(at_ref, float_ref, quant_ref, after_ref, out_ref):
     width = float_ref.shape[1] // 32
     yl, z = at_ref[0], at_ref[1]
     quant = quant_ref[:, :BLOCK]
@@ -37,16 +37,16 @@
             out_ref[kind * 4 + x, :, 8 * width + BLOCK :] = shift
 
 
-def pack(at, attn_float, attn_quant):
+def pack(at, attn_float, attn_quant, after):
     tokens, d_in = attn_float.shape
     return pl.pallas_call(
         pack_kernel,
         out_shape=jax.ShapeDtypeStruct((8, tokens, d_in // 4 + 2 * BLOCK), BF16),
-        in_specs=[SCALAR, WHOLE, WHOLE],
+        in_specs=[SCALAR, WHOLE, WHOLE, LEFT],
         out_specs=WHOLE,
         compiler_params=params(),
         name="pack",
-    )(at, attn_float, attn_quant)
+    )(at, attn_float, attn_quant, after)
 
 
 def join_kernel(*refs):
@@ -69,7 +69,7 @@
 
 
 def project_kernel(core_ref, mine_ref, other_ref, *refs):
-    *parts, out_ref = refs
+    parts, out_ref = refs[:5], refs[-1]
     core = core_ref[0]
     rows = out_ref.shape[2]
     for n, acts in enumerate((mine_ref, other_ref)):
@@ -88,40 +88,42 @@
             out_ref[yh, where] = total.astype(BF16)
 
 
-def project(core, mine, other, parts):
+def project(core, mine, other, parts, after):
     rows, cols = mine.shape[0] // 2, parts[0].shape[1]
     return pl.pallas_call(
         project_kernel,
         out_shape=jax.ShapeDtypeStruct((2, 2, rows, cols), BF16),
-        in_specs=[SCALAR] + [WHOLE] * (2 + len(parts)),
+        in_specs=[SCALAR] + [WHOLE] * (2 + len(parts)) + [LEFT] * len(after),
         out_specs=WHOLE,
         compiler_params=params(),
         cost_estimate=pl.CostEstimate(
             flops=8 * rows * cols * 2048, bytes_accessed=8 << 20, transcendentals=0
         ),
         name="project",
-    )(core.reshape(1), mine, other, *parts)
+    )(core.reshape(1), mine, other, *parts, *after)
 
 
 def finish_kernel(*refs):
     *parts, float_ref, quant_ref = refs
-    width = parts[0].shape[2]
-    for c, ref in enumerate(parts):
+    at_half, start = float_ref.shape[1] // 2, 0
+    for ref in parts:
+        width = ref.shape[2]
         for kind, out in enumerate((float_ref, quant_ref)):
             for half in range(2):
                 at = kind * 8 + half * 4
                 total = ref[at].astype(F32)
                 for x in range(1, 4):
                     total += ref[at + x].astype(F32)
-                start = (half * len(parts) + c) * width
-                out[:, start : start + width] = total.astype(BF16)
+                col = half * at_half + start
+                out[:, col : col + width] = total.astype(BF16)
+        start += width
 
 
 def finish(parts):
-    _, tokens, width = parts[0].shape
+    tokens = parts[0].shape[1]
     return pl.pallas_call(
         finish_kernel,
-        out_shape=(jax.ShapeDtypeStruct((tokens, 2 * len(parts) * width), BF16),) * 2,
+        out_shape=(jax.ShapeDtypeStruct((tokens, 2 * sum(WIDTHS)), BF16),) * 2,
         in_specs=[WHOLE] * len(parts),
         out_specs=(WHOLE, WHOLE),
         compiler_params=params(),
@@ -141,14 +143,9 @@
     tokens, d_in = attn_float.shape
     features, d_out = proj_weight.shape
     groups = group_scales.shape[0]
-    half, width = d_out // 2, d_out // 2 // CHUNKS
+    half = d_out // 2
     inverse = 1.0 / (tokens * 128)
     yh, core, yl, z = (lax.axis_index(a) for a in ("yh", "core", "yl", "z"))
-
-    payload = pack(jnp.stack([yl, z]), attn_float, attn_quant)
-    mine = lax.all_to_all(payload, ("yh", "x"), 0, 0, tiled=True)
-    mine = mine.reshape(8 * tokens, 8 * features + 2 * BLOCK)
-    other = swap(mine, "core")
 
     def weight(kind, col, n):
         plain = lax.dynamic_slice_in_dim(proj_weight, col, n, 1)
@@ -163,29 +160,44 @@
         for c in range(2):
             for b in range(2):
                 pairs.append((a * 4 + c * 2 + b, (a ^ c) * 4 + c * 2 + (1 - b)))
-    own, got = [], []
-    for first, n in ((0, width), (width, half - width)):
+
+    def exchange(first, n):
         col = core * half + first
-        mine_w, send_w = weight(yh, col, n), weight(yh ^ core, col, n)
-        got_w = lax.ppermute(send_w, ("yh", "core", "yl"), pairs)
-        for at in range(0, n, width):
-            own.append(mine_w[:, at : at + width])
-            got.append(got_w[:, at : at + width])
-
-    after, results = (), []
-    for c in range(CHUNKS):
-        rows = join(own[c], got[c], after)
-        up, down = from_z(rows, 1), from_z(rows, 3)
-        after = (up, down)
-        far0 = from_z(up[:features], 1)
-        far1 = from_z(down[features:], 3)
-        partial = project(core, mine, other, (rows, up, far0, far1, down))
-        results.append(
-            lax.all_to_all(
-                partial.reshape(16, tokens, width), ("yh", "core", "x"), 0, 0, tiled=True
-            )
+        own, send = weight(yh, col, n), weight(yh ^ core, col, n)
+        return own, lax.ppermute(send, ("yh", "core", "yl"), pairs)
+
+    def near(rows):
+        return from_z(rows, 1), from_z(rows, 3)
+
+    def far(up, down):
+        return from_z(up[:features], 1), from_z(down[features:], 3)
+
+    w0, w1, w2 = WIDTHS
+    rows0 = join(*exchange(0, w0), ())
+    near0 = near(rows0)
+
+    payload = pack(jnp.stack([yl, z]), attn_float, attn_quant, rows0)
+    mine = lax.all_to_all(payload, ("yh", "x"), 0, 0, tiled=True)
+    mine = mine.reshape(8 * tokens, 8 * features + 2 * BLOCK)
+
+    far0 = far(*near0)
+    rows1 = join(*exchange(w0, w1), far0)
+    near1 = near(rows1)
+    mine, *near0 = lax.optimization_barrier((mine, *near0))
+    other = swap(mine, "core")
+    far1 = far(*near1)
+    rows2 = join(*exchange(w0 + w1, w2), far1)
+    near2 = near(rows2)
+    far2 = far(*near2)
+
+    def part(rows, near, far, after):
+        width = rows.shape[1]
+        partial = project(core, mine, other, (rows, near[0], *far, near[1]), after)
+        return lax.all_to_all(
+            partial.reshape(16, tokens, width), ("yh", "core", "x"), 0, 0, tiled=True
         )
-    float_out, quant_out = finish(results)
+
+    result0 = part(rows0, near0, far0, ())
 
     def stats(j):
         at = 2 * j * features
@@ -209,6 +221,10 @@
         ]
         total = total + lax.ppermute(stats(j).astype(BF16), ("core", "yl", "z"), pairs).astype(F32)
     total = (total + swap(total, "core")) * inverse
+
+    result1 = part(rows1, near1, far1, ())
+    result2 = part(rows2, near2, far2, (total,))
+    float_out, quant_out = finish((result0, result1, result2))
     total = jnp.where(yh == 1, total, swap(total, "yh"))
     return float_out, quant_out, total[:, :BLOCK], total[:, BLOCK:]
 

time: 225 us -> 235 us (1.044)
  waiting for transfers between devices: 57.8 us -> 121 us
  blocking collectives: 38.1 us -> 0 us
  starting transfers between devices: 62.7 us -> 54.8 us
  matrix products: 13.4 us -> 6.74 us
  local copies, waits for them, and re-layouts: 18.9 us -> 24.9 us
  other arithmetic: 8.87 us -> 4.88 us
  Pallas kernels: 22.2 us -> 19.6 us
    all_to_all x1 -> x0, blocking collectives: 38.1 us -> none  [shards(): mine = lax.all_to_all(payload, ('yh', 'x'), 0, 0, tiled=True)]
    ppermute x16 -> x12, waiting for transfers between devices: 28.6 us -> 62 us  [from_z(): return lax.ppermute(a, 'z', [((i + j) % 4, i) for i in range(4)])]
    all_to_all x4, waiting for transfers between devices: 0.54 us -> 28.3 us  [the longest x3 21.1 us: part(): lax.all_to_all(partial.reshape(16, tokens, width), ('yh', 'core', 'x'), 0...]
    unnamed x42 -> x48, local copies, waits for them, and re-layouts: 8.31 us -> 18.7 us
    dot_general x8, matrix products: 13.4 us -> 6.74 us  [stats(): lax.dot_general(picked, acts[:, 8 * features:], (((0,), (0,)), ((), ())),...]
    ppermute x3, waiting for transfers between devices: 17 us -> 23.6 us  [swap(): return lax.ppermute(a, axis, [(0, 1), (1, 0)])]
    ppermute x3, starting transfers between devices: 9.92 us -> 3.52 us  [swap(): return lax.ppermute(a, axis, [(0, 1), (1, 0)])]
    slice x10 -> x6, local copies, waits for them, and re-layouts: 9.88 us -> 4.12 us  [far(): return (from_z(up[:features], 1), from_z(down[features:], 3))]
  transfers between devices with their start and end apart: 29 -> 26, of which waited for: 10 -> 15; matrix products, arithmetic and copies ran while one was open for 15% -> 6% of each run, Pallas kernels for 8% -> 5%
where the time goes in v3:
time: 235 us; the launch traced here: 233 us
  waiting for transfers between devices  121 us (51%)
  starting transfers between devices  54.8 us (23%)
  local copies, waits for them, and re-layouts  24.9 us (11%)
  Pallas kernels  19.6 us (8%)
  matrix products  6.74 us (3%)
  other arithmetic  4.88 us (2%)
    ppermute x12, waiting for transfers between devices, from_z(): return lax.ppermute(a, 'z', [((i + j) % 4, i) for i in range(4)])  62 us
    ppermute x3, waiting for transfers between devices, swap(): return lax.ppermute(a, axis, [(0, 1), (1, 0)])  23.6 us
    all_to_all x3, waiting for transfers between devices, part(): lax.all_to_all(partial.reshape(16, tokens, width), ('yh', 'core', 'x'), 0...  21.1 us
    all_to_all x3, starting transfers between devices, part(): lax.all_to_all(partial.reshape(16, tokens, width), ('yh', 'core', 'x'), 0...  18.7 us
    unnamed x48, local copies, waits for them, and re-layouts  18.7 us
    ppermute x12, starting transfers between devices, from_z(): return lax.ppermute(a, 'z', [((i + j) % 4, i) for i in range(4)])  17.3 us
    pallas_call x3, Pallas kernels, project(): pl.pallas_call(project_kernel, out_shape=jax.ShapeDtypeStruct((2, 2, rows...  14.7 us
    all_to_all x1, waiting for transfers between devices, shards(): mine = lax.all_to_all(payload, ('yh', 'x'), 0, 0, tiled=True)  7.17 us
  transfers between devices with their start and end apart: 26, of which 15 were waited for; matrix products, arithmetic and copies ran while one was open for 6% of the time, Pallas kernels for 5%

profile of v3, /device:TPU:0, one launch (start us, length us, event | category | flops | bytes accessed | tf_op | source)
XLA Modules:
  0.0 232.9 jit_solution(4985644869750184245)
XLA Ops:
  1.4 2.7 %broadcast_select_fusion = (bf16[256,768]{1,0:T(8,128)(2,1)}, bf16[256,768]{1,0:T(8,128)(2,1)S(1)}, bf16[256,768]{1,0:T(8,128)(2,1)S(1)}, bf16[256,768]{1,0:T(8,128)(2,1)S(1)}) fusion(pred[]{:T(512)S(6)} %eq.9, bf16[256,4096]{1,0:T(8,128)(2,1)} %param.7, s32[]{:T(128)S(6)} %select_n.109, f32[2,768]{1,0:T(2,128)S(1)} %get-tuple-element.24, ...), kind=kLoop, calls=%fused_computation.14 | loop fusion | flops 2359296 | bytes 3944458 | tf_op jit(solution)/shard_map/jit(_where)/select_n | solution.py:156
  4.1 1.7 collective-permute-start
  5.8 6.0 %collective-permute-done.refs_1_ = bf16[256,768]{1,0:T(8,128)(2,1)S(1)} collective-permute-done((bf16[256,768]{1,0:T(8,128)(2,1)S(1)}, bf16[256,768]{1,0:T(8,128)(2,1)S(1)}, u32[]{:S(2)}, u32[]{:S(2)}) %collective-permute-start) | collective-permute-done | bytes 393248 | tf_op jit(solution)/shard_map/ppermute | solution.py:167
  16.6 7.0 %all-to-all-start = ((bf16[8,64,2304]{2,1,0:T(8,128)(2,1)}), bf16[8,64,2304]{2,1,0:T(8,128)(2,1)S(1)}, u32[]{:S(2)}, u32[]{:S(2)}) async-start(bf16[8,64,2304]{2,1,0:T(8,128)(2,1)} %copy-done), calls=%async_computation | async-start | bytes 4718592 | tf_op jit(solution)/shard_map/all_to_all | solution.py:180
  23.6 4.0 %collective-permute-start.1 = (bf16[512,768]{1,0:T(8,128)(2,1)S(1)}, bf16[512,768]{1,0:T(8,128)(2,1)S(1)}, u32[]{:S(2)}, u32[]{:S(2)}) collective-permute-start(bf16[512,768]{1,0:T(8,128)(2,1)S(1)} %join.3.after_ref.refs_0_), channel_id=1, source_target_pairs={{4,0},{8,4},{12,8},{0,12},{5,1},{9,5},{13,9},{1,13},{6,2},{10,6},{... | collective-permute-start | bytes 2359304 | tf_op jit(solution)/shard_map/ppermute | solution.py:139
  27.7 15.7 %collective-permute-done.1.refs_1_ = bf16[512,768]{1,0:T(8,128)(2,1)S(1)} collective-permute-done((bf16[512,768]{1,0:T(8,128)(2,1)S(1)}, bf16[512,768]{1,0:T(8,128)(2,1)S(1)}, u32[]{:S(2)}, u32[]{:S(2)}) %collective-permute-start.1) | collective-permute-done | bytes 786464 | tf_op jit(solution)/shard_map/ppermute | solution.py:139
  44.3 2.5 %collective-permute-done.2.refs_4_ = bf16[512,768]{1,0:T(8,128)(2,1)} collective-permute-done((bf16[512,768]{1,0:T(8,128)(2,1)S(1)}, bf16[512,768]{1,0:T(8,128)(2,1)}, u32[]{:S(2)}, u32[]{:S(2)}) %collective-permute-start.2) | collective-permute-done | bytes 786464 | tf_op jit(solution)/shard_map/ppermute | solution.py:139
  46.8 7.2 %all-to-all-done = bf16[8,64,2304]{2,1,0:T(8,128)(2,1)S(1)} async-done(((bf16[8,64,2304]{2,1,0:T(8,128)(2,1)}), bf16[8,64,2304]{2,1,0:T(8,128)(2,1)S(1)}, u32[]{:S(2)}, u32[]{:S(2)}) %all-to-all-start) | async-done | bytes 2359328 | tf_op jit(solution)/shard_map/all_to_all | solution.py:180
  54.0 1.6 collective-permute-start.6
  56.6 4.1 %collective-permute-start.4 = (bf16[256,768]{1,0:T(8,128)(2,1)S(1)}, bf16[256,768]{1,0:T(8,128)(2,1)S(1)}, u32[]{:S(2)}, u32[]{:S(2)}) collective-permute-start(bf16[256,768]{1,0:T(8,128)(2,1)S(1)} %slice.110), channel_id=1, source_target_pairs={{4,0},{8,4},{12,8},{0,12},{5,1},{9,5},{13,9},{1,13},{6,2},{10,6},{... | collective-permute-start | bytes 1179656 | tf_op jit(solution)/shard_map/ppermute | solution.py:139
  62.0 7.2 %collective-permute-done.4.refs_2_ = bf16[256,768]{1,0:T(8,128)(2,1)S(1)} collective-permute-done((bf16[256,768]{1,0:T(8,128)(2,1)S(1)}, bf16[256,768]{1,0:T(8,128)(2,1)S(1)}, u32[]{:S(2)}, u32[]{:S(2)}) %collective-permute-start.4) | collective-permute-done | bytes 393248 | tf_op jit(solution)/shard_map/ppermute | solution.py:139
  69.2 4.5 %collective-permute-done.5.refs_3_ = bf16[256,768]{1,0:T(8,128)(2,1)S(1)} collective-permute-done((bf16[256,768]{1,0:T(8,128)(2,1)S(1)}, bf16[256,768]{1,0:T(8,128)(2,1)S(1)}, u32[]{:S(2)}, u32[]{:S(2)}) %collective-permute-start.5) | collective-permute-done | bytes 393248 | tf_op jit(solution)/shard_map/ppermute | solution.py:139
  76.6 1.9 broadcast_select_fusion.4
  79.1 13.1 %collective-permute-done.7.refs_1_ = bf16[512,768]{1,0:T(8,128)(2,1)} collective-permute-done((bf16[512,768]{1,0:T(8,128)(2,1)S(1)}, bf16[512,768]{1,0:T(8,128)(2,1)}, u32[]{:S(2)}, u32[]{:S(2)}) %collective-permute-start.7) | collective-permute-done | bytes 786464 | tf_op jit(solution)/shard_map/ppermute | solution.py:139
  93.2 1.6 collective-permute-start.8
  98.1 2.8 %collective-permute-start.19 = (bf16[256,256]{1,0:T(8,128)(2,1)S(1)}, bf16[256,256]{1,0:T(8,128)(2,1)S(1)}, u32[]{:S(2)}, u32[]{:S(2)}) collective-permute-start(bf16[256,256]{1,0:T(8,128)(2,1)S(1)} %fusion.3), channel_id=1, source_target_pairs={{0,12},{4,0},{8,4},{12,8},{16,28},{20,16},{24,20},{28,24},{32,60},... | collective-permute-start | bytes 393224 | tf_op jit(solution)/shard_map/ppermute | solution.py:222
  108.8 2.4 %collective-permute-start.12 = (bf16[512,512]{1,0:T(8,128)(2,1)S(1)}, bf16[512,512]{1,0:T(8,128)(2,1)S(1)}, u32[]{:S(2)}, u32[]{:S(2)}) collective-permute-start(bf16[512,512]{1,0:T(8,128)(2,1)S(1)} %join.5.refs_0_), channel_id=1, source_target_pairs={{4,0},{8,4},{12,8},{0,12},{5,1},{9,5},{13,9},{1,13},{6,2},{10,6},{... | collective-permute-start | bytes 1572872 | tf_op jit(solution)/shard_map/ppermute | solution.py:139
  112.5 11.1 %collective-permute-done.12.refs_1_ = bf16[512,512]{1,0:T(8,128)(2,1)S(1)} collective-permute-done((bf16[512,512]{1,0:T(8,128)(2,1)S(1)}, bf16[512,512]{1,0:T(8,128)(2,1)S(1)}, u32[]{:S(2)}, u32[]{:S(2)}) %collective-permute-start.12) | collective-permute-done | bytes 524320 | tf_op jit(solution)/shard_map/ppermute | solution.py:139
  123.7 2.5 %collective-permute-start.13 = (bf16[256,512]{1,0:T(8,128)(2,1)S(1)}, bf16[256,512]{1,0:T(8,128)(2,1)S(1)}, u32[]{:S(2)}, u32[]{:S(2)}) collective-permute-start(bf16[256,512]{1,0:T(8,128)(2,1)S(1)} %slice.114), channel_id=1, source_target_pairs={{4,0},{8,4},{12,8},{0,12},{5,1},{9,5},{13,9},{1,13},{6,2},{10,6},{... | collective-permute-start | bytes 786440 | tf_op jit(solution)/shard_map/ppermute | solution.py:139
  126.4 5.1 %collective-permute-done.13.refs_2_ = bf16[256,512]{1,0:T(8,128)(2,1)S(1)} collective-permute-done((bf16[256,512]{1,0:T(8,128)(2,1)S(1)}, bf16[256,512]{1,0:T(8,128)(2,1)S(1)}, u32[]{:S(2)}, u32[]{:S(2)}) %collective-permute-start.13) | collective-permute-done | bytes 262176 | tf_op jit(solution)/shard_map/ppermute | solution.py:139
  131.4 2.9 %collective-permute-done.15.refs_3_ = bf16[256,512]{1,0:T(8,128)(2,1)S(1)} collective-permute-done((bf16[256,512]{1,0:T(8,128)(2,1)S(1)}, bf16[256,512]{1,0:T(8,128)(2,1)S(1)}, u32[]{:S(2)}, u32[]{:S(2)}) %collective-permute-start.15) | collective-permute-done | bytes 262176 | tf_op jit(solution)/shard_map/ppermute | solution.py:139
  134.3 4.0 %project.5 = bf16[2,2,256,512]{3,2,1,0:T(8,128)(2,1)S(1)} custom-call(s32[1]{0:T(128)} %bitcast.core_ref, bf16[512,2304]{1,0:T(8,128)(2,1)S(1)} %bitcast.36, bf16[512,2304]{1,0:T(8,128)(2,1)} %collective-permute-done.3.other_ref, bf16[512,512]{1,0:T(8,128)(2,1)S(1)} %join.5.refs_0_, bf16[512,512]{1,0:T(8,128)(2,1)S(1)} %collective-permute-done.12.refs_1_, ...), custom_call_target="tpu_custom_call" | custom-call | flops 2147483648 | bytes 8388608 | tf_op jit(solution)/shard_map/project/pallas_call | solution.py:93
  139.3 10.6 %all-to-all-start.3 = ((bf16[16,64,512]{2,1,0:T(8,128)(2,1)}), bf16[16,64,512]{2,1,0:T(8,128)(2,1)S(1)}, u32[]{:S(2)}, u32[]{:S(2)}) async-start(bf16[16,64,512]{2,1,0:T(8,128)(2,1)} %bitcast.39), calls=%async_computation.3 | async-start | bytes 2097152 | tf_op jit(solution)/shard_map/all_to_all | solution.py:196
  154.2 5.2 %project.3 = bf16[2,2,256,768]{3,2,1,0:T(8,128)(2,1)S(1)} custom-call(s32[1]{0:T(128)} %bitcast.core_ref, bf16[512,2304]{1,0:T(8,128)(2,1)S(1)} %bitcast.37, bf16[512,2304]{1,0:T(8,128)(2,1)} %collective-permute-done.3.other_ref, bf16[512,768]{1,0:T(8,128)(2,1)S(1)} %copy-done.5, bf16[512,768]{1,0:T(8,128)(2,1)S(1)} %copy-done.23, ...), custom_call_target="tpu_custom_call" | custom-call | flops 3221225472 | bytes 8388608 | tf_op jit(solution)/shard_map/project/pallas_call | solution.py:93
  160.6 7.1 %all-to-all-done.3.refs_2_ = bf16[16,64,512]{2,1,0:T(8,128)(2,1)S(1)} async-done(((bf16[16,64,512]{2,1,0:T(8,128)(2,1)}), bf16[16,64,512]{2,1,0:T(8,128)(2,1)S(1)}, u32[]{:S(2)}, u32[]{:S(2)}) %all-to-all-start.3) | async-done | bytes 1048608 | tf_op jit(solution)/shard_map/all_to_all | solution.py:196
  167.8 4.4 %all-to-all-start.1 = ((bf16[16,64,768]{2,1,0:T(8,128)(2,1)}), bf16[16,64,768]{2,1,0:T(8,128)(2,1)}, u32[]{:S(2)}, u32[]{:S(2)}) async-start(bf16[16,64,768]{2,1,0:T(8,128)(2,1)} %bitcast.41), calls=%async_computation.1 | async-start | bytes 3145728 | tf_op jit(solution)/shard_map/all_to_all | solution.py:196
  175.3 5.5 %project.4 = bf16[2,2,256,768]{3,2,1,0:T(8,128)(2,1)S(1)} custom-call(s32[1]{0:T(128)} %bitcast.core_ref, bf16[512,2304]{1,0:T(8,128)(2,1)S(1)} %bitcast.38, bf16[512,2304]{1,0:T(8,128)(2,1)} %collective-permute-done.3.other_ref, bf16[512,768]{1,0:T(8,128)(2,1)S(1)} %copy-done.13, bf16[512,768]{1,0:T(8,128)(2,1)} %collective-permute-done.7.refs_1_, ...), custom_call_target="tpu_custom_call" | custom-call | flops 3221225472 | bytes 8388608 | tf_op jit(solution)/shard_map/project/pallas_call | solution.py:93
  182.0 14.0 %all-to-all-done.1.refs_0_ = bf16[16,64,768]{2,1,0:T(8,128)(2,1)} async-done(((bf16[16,64,768]{2,1,0:T(8,128)(2,1)}), bf16[16,64,768]{2,1,0:T(8,128)(2,1)}, u32[]{:S(2)}, u32[]{:S(2)}) %all-to-all-start.1) | async-done | bytes 1572896 | tf_op jit(solution)/shard_map/all_to_all | solution.py:196
  196.0 3.7 %all-to-all-start.2 = ((bf16[16,64,768]{2,1,0:T(8,128)(2,1)}), bf16[16,64,768]{2,1,0:T(8,128)(2,1)S(1)}, u32[]{:S(2)}, u32[]{:S(2)}) async-start(bf16[16,64,768]{2,1,0:T(8,128)(2,1)} %bitcast.40), calls=%async_computation.2 | async-start | bytes 3145728 | tf_op jit(solution)/shard_map/all_to_all | solution.py:196
  199.7 3.4 %collective-permute-start.21 = (f32[256,256]{1,0:T(8,128)S(1)}, f32[256,256]{1,0:T(8,128)S(1)}, u32[]{:S(2)}, u32[]{:S(2)}) collective-permute-start(f32[256,256]{1,0:T(8,128)S(1)} %copy-done.7), channel_id=1, source_target_pairs={{0,64},{64,0},{1,65},{65,1},{2,66},{66,2},{3,67},{67,3},{4,68},{68... | collective-permute-start | bytes 786440 | tf_op jit(solution)/shard_map/ppermute | solution.py:135
  203.1 23.6 %collective-permute-done.21 = f32[256,256]{1,0:T(8,128)S(1)} collective-permute-done((f32[256,256]{1,0:T(8,128)S(1)}, f32[256,256]{1,0:T(8,128)S(1)}, u32[]{:S(2)}, u32[]{:S(2)}) %collective-permute-start.21) | collective-permute-done | bytes 262176 | tf_op jit(solution)/shard_map/ppermute | solution.py:135
  230.1 2.8 %finish.1 = (bf16[64,4096]{1,0:T(8,128)(2,1)}, bf16[64,4096]{1,0:T(8,128)(2,1)}) custom-call(bf16[16,64,768]{2,1,0:T(8,128)(2,1)} %all-to-all-done.1.refs_0_, bf16[16,64,768]{2,1,0:T(8,128)(2,1)S(1)} %copy-done.2, bf16[16,64,512]{2,1,0:T(8,128)(2,1)S(1)} %all-to-all-done.3.refs_2_), custom_call_target="tpu_custom_call" | custom-call | tf_op jit(solution)/shard_map/finish/pallas_call | solution.py:124
  (99 shorter events, 39.8 us)
Async XLA Ops:
  4.1 7.8 %collective-permute-start = (bf16[256,768]{1,0:T(8,128)(2,1)S(1)}, bf16[256,768]{1,0:T(8,128)(2,1)S(1)}, u32[]{:S(2)}, u32[]{:S(2)}) collective-permute-start(bf16[256,768]{1,0:T(8,128)(2,1)S(1)} %get-tuple-element.21), channel_id=1, source_target_pairs={{0,16},{16,0},{32,112},{48,96},{64,80},{80,64},{96,48},{112,32},{1... | collective-permute-start | bytes 1179656 | tf_op jit(solution)/shard_map/ppermute | solution.py:167
  14.4 13.3 %copy-start.4 = (bf16[512,768]{1,0:T(8,128)(2,1)}, bf16[512,768]{1,0:T(8,128)(2,1)S(1)}, u32[]{:S(2)}) copy-start(bf16[512,768]{1,0:T(8,128)(2,1)S(1)} %join.3.after_ref.refs_0_) | copy-start | bytes 2359300
  16.6 37.4 %all-to-all-start = ((bf16[8,64,2304]{2,1,0:T(8,128)(2,1)}), bf16[8,64,2304]{2,1,0:T(8,128)(2,1)S(1)}, u32[]{:S(2)}, u32[]{:S(2)}) async-start(bf16[8,64,2304]{2,1,0:T(8,128)(2,1)} %copy-done), calls=%async_computation | async-start | bytes 4718592 | tf_op jit(solution)/shard_map/all_to_all | solution.py:180
  23.6 19.7 %collective-permute-start.1 = (bf16[512,768]{1,0:T(8,128)(2,1)S(1)}, bf16[512,768]{1,0:T(8,128)(2,1)S(1)}, u32[]{:S(2)}, u32[]{:S(2)}) collective-permute-start(bf16[512,768]{1,0:T(8,128)(2,1)S(1)} %join.3.after_ref.refs_0_), channel_id=1, source_target_pairs={{4,0},{8,4},{12,8},{0,12},{5,1},{9,5},{13,9},{1,13},{6,2},{10,6},{... | collective-permute-start | bytes 2359304 | tf_op jit(solution)/shard_map/ppermute | solution.py:139
  27.7 19.2 %collective-permute-start.2 = (bf16[512,768]{1,0:T(8,128)(2,1)S(1)}, bf16[512,768]{1,0:T(8,128)(2,1)}, u32[]{:S(2)}, u32[]{:S(2)}) collective-permute-start(bf16[512,768]{1,0:T(8,128)(2,1)S(1)} %join.3.after_ref.refs_0_), channel_id=1, source_target_pairs={{12,0},{0,4},{4,8},{8,12},{13,1},{1,5},{5,9},{9,13},{14,2},{2,6},{... | collective-permute-start | bytes 2359304 | tf_op jit(solution)/shard_map/ppermute | solution.py:139
  54.0 42.4 %collective-permute-start.3 = (bf16[512,2304]{1,0:T(8,128)(2,1)S(1)}, bf16[512,2304]{1,0:T(8,128)(2,1)}, u32[]{:S(2)}, u32[]{:S(2)}) collective-permute-start(bf16[512,2304]{1,0:T(8,128)(2,1)S(1)} %bitcast.31), channel_id=1, source_target_pairs={{0,32},{32,0},{1,33},{33,1},{2,34},{34,2},{3,35},{35,3},{4,36},{36... | collective-permute-start | bytes 7077896 | tf_op jit(solution)/shard_map/ppermute | solution.py:135
  54.0 8.0 %collective-permute-start.6 = (bf16[256,768]{1,0:T(8,128)(2,1)}, bf16[256,768]{1,0:T(8,128)(2,1)S(1)}, u32[]{:S(2)}, u32[]{:S(2)}) collective-permute-start(bf16[256,768]{1,0:T(8,128)(2,1)} %get-tuple-element.14), channel_id=1, source_target_pairs={{0,16},{16,0},{32,112},{48,96},{64,80},{80,64},{96,48},{112,32},{1... | collective-permute-start | bytes 1179656 | tf_op jit(solution)/shard_map/ppermute | solution.py:167
  56.6 12.6 %collective-permute-start.4 = (bf16[256,768]{1,0:T(8,128)(2,1)S(1)}, bf16[256,768]{1,0:T(8,128)(2,1)S(1)}, u32[]{:S(2)}, u32[]{:S(2)}) collective-permute-start(bf16[256,768]{1,0:T(8,128)(2,1)S(1)} %slice.110), channel_id=1, source_target_pairs={{4,0},{8,4},{12,8},{0,12},{5,1},{9,5},{13,9},{1,13},{6,2},{10,6},{... | collective-permute-start | bytes 1179656 | tf_op jit(solution)/shard_map/ppermute | solution.py:139
  61.8 12.0 %collective-permute-start.5 = (bf16[256,768]{1,0:T(8,128)(2,1)S(1)}, bf16[256,768]{1,0:T(8,128)(2,1)S(1)}, u32[]{:S(2)}, u32[]{:S(2)}) collective-permute-start(bf16[256,768]{1,0:T(8,128)(2,1)S(1)} %slice.111), channel_id=1, source_target_pairs={{12,0},{0,4},{4,8},{8,12},{13,1},{1,5},{5,9},{9,13},{14,2},{2,6},{... | collective-permute-start | bytes 1179656 | tf_op jit(solution)/shard_map/ppermute | solution.py:139
  73.8 24.3 %copy-start.12 = (bf16[512,768]{1,0:T(8,128)(2,1)}, bf16[512,768]{1,0:T(8,128)(2,1)S(1)}, u32[]{:S(2)}) copy-start(bf16[512,768]{1,0:T(8,128)(2,1)S(1)} %join.4.refs_0_) | copy-start | bytes 2359300
  73.8 18.4 %collective-permute-start.7 = (bf16[512,768]{1,0:T(8,128)(2,1)S(1)}, bf16[512,768]{1,0:T(8,128)(2,1)}, u32[]{:S(2)}, u32[]{:S(2)}) collective-permute-start(bf16[512,768]{1,0:T(8,128)(2,1)S(1)} %join.4.refs_0_), channel_id=1, source_target_pairs={{4,0},{8,4},{12,8},{0,12},{5,1},{9,5},{13,9},{1,13},{6,2},{10,6},{... | collective-permute-start | bytes 2359304 | tf_op jit(solution)/shard_map/ppermute | solution.py:139
  74.5 20.3 %collective-permute-start.9 = (bf16[512,768]{1,0:T(8,128)(2,1)S(1)}, bf16[512,768]{1,0:T(8,128)(2,1)}, u32[]{:S(2)}, u32[]{:S(2)}) collective-permute-start(bf16[512,768]{1,0:T(8,128)(2,1)S(1)} %join.4.refs_0_), channel_id=1, source_target_pairs={{12,0},{0,4},{4,8},{8,12},{13,1},{1,5},{5,9},{9,13},{14,2},{2,6},{... | collective-permute-start | bytes 2359304 | tf_op jit(solution)/shard_map/ppermute | solution.py:139
  78.5 27.5 %collective-permute-start.11 = (bf16[256,512]{1,0:T(8,128)(2,1)}, bf16[256,512]{1,0:T(8,128)(2,1)}, u32[]{:S(2)}, u32[]{:S(2)}) collective-permute-start(bf16[256,512]{1,0:T(8,128)(2,1)} %get-tuple-element.18), channel_id=1, source_target_pairs={{0,16},{16,0},{32,112},{48,96},{64,80},{80,64},{96,48},{112,32},{1... | collective-permute-start | bytes 786440 | tf_op jit(solution)/shard_map/ppermute | solution.py:167
  93.2 13.8 %collective-permute-start.8 = (bf16[256,768]{1,0:T(8,128)(2,1)S(1)}, bf16[256,768]{1,0:T(8,128)(2,1)S(1)}, u32[]{:S(2)}, u32[]{:S(2)}) collective-permute-start(bf16[256,768]{1,0:T(8,128)(2,1)S(1)} %slice.112), channel_id=1, source_target_pairs={{4,0},{8,4},{12,8},{0,12},{5,1},{9,5},{13,9},{1,13},{6,2},{10,6},{... | collective-permute-start | bytes 1179656 | tf_op jit(solution)/shard_map/ppermute | solution.py:139
  95.8 11.9 %collective-permute-start.10 = (bf16[256,768]{1,0:T(8,128)(2,1)S(1)}, bf16[256,768]{1,0:T(8,128)(2,1)S(1)}, u32[]{:S(2)}, u32[]{:S(2)}) collective-permute-start(bf16[256,768]{1,0:T(8,128)(2,1)S(1)} %slice.113), channel_id=1, source_target_pairs={{12,0},{0,4},{4,8},{8,12},{13,1},{1,5},{5,9},{9,13},{14,2},{2,6},{... | collective-permute-start | bytes 1179656 | tf_op jit(solution)/shard_map/ppermute | solution.py:139
  98.1 13.2 %collective-permute-start.19 = (bf16[256,256]{1,0:T(8,128)(2,1)S(1)}, bf16[256,256]{1,0:T(8,128)(2,1)S(1)}, u32[]{:S(2)}, u32[]{:S(2)}) collective-permute-start(bf16[256,256]{1,0:T(8,128)(2,1)S(1)} %fusion.3), channel_id=1, source_target_pairs={{0,12},{4,0},{8,4},{12,8},{16,28},{20,16},{24,20},{28,24},{32,60},... | collective-permute-start | bytes 393224 | tf_op jit(solution)/shard_map/ppermute | solution.py:222
  102.6 9.0 %collective-permute-start.18 = (bf16[256,256]{1,0:T(8,128)(2,1)S(1)}, bf16[256,256]{1,0:T(8,128)(2,1)S(1)}, u32[]{:S(2)}, u32[]{:S(2)}) collective-permute-start(bf16[256,256]{1,0:T(8,128)(2,1)S(1)} %fusion.2), channel_id=1, source_target_pairs={{0,8},{4,12},{8,0},{12,4},{16,24},{20,28},{24,16},{28,20},{32,56},... | collective-permute-start | bytes 393224 | tf_op jit(solution)/shard_map/ppermute | solution.py:222
  106.1 6.2 %collective-permute-start.17 = (bf16[256,256]{1,0:T(8,128)(2,1)S(1)}, bf16[256,256]{1,0:T(8,128)(2,1)S(1)}, u32[]{:S(2)}, u32[]{:S(2)}) collective-permute-start(bf16[256,256]{1,0:T(8,128)(2,1)S(1)} %fusion.1), channel_id=1, source_target_pairs={{0,4},{4,8},{8,12},{12,0},{16,20},{20,24},{24,28},{28,16},{32,52},... | collective-permute-start | bytes 393224 | tf_op jit(solution)/shard_map/ppermute | solution.py:222
  107.0 27.3 %copy-start.18 = (bf16[256,768]{1,0:T(8,128)(2,1)}, bf16[256,768]{1,0:T(8,128)(2,1)S(1)}, u32[]{:S(2)}) copy-start(bf16[256,768]{1,0:T(8,128)(2,1)S(1)} %collective-permute-done.8.refs_2_) | copy-start | bytes 1179652
  107.0 5.3 %collective-permute-start.16 = (bf16[256,256]{1,0:T(8,128)(2,1)S(1)}, bf16[256,256]{1,0:T(8,128)(2,1)S(1)}, u32[]{:S(2)}, u32[]{:S(2)}) collective-permute-start(bf16[256,256]{1,0:T(8,128)(2,1)S(1)} %fusion), channel_id=1, source_target_pairs={{0,0},{4,4},{8,8},{12,12},{16,16},{20,20},{24,24},{28,28},{32,48},... | collective-permute-start | bytes 393224 | tf_op jit(solution)/shard_map/ppermute | solution.py:222
  107.7 18.6 %copy-start.20 = (bf16[256,768]{1,0:T(8,128)(2,1)}, bf16[256,768]{1,0:T(8,128)(2,1)S(1)}, u32[]{:S(2)}) copy-start(bf16[256,768]{1,0:T(8,128)(2,1)S(1)} %collective-permute-done.10.refs_3_) | copy-start | bytes 1179652
  108.8 14.8 %collective-permute-start.12 = (bf16[512,512]{1,0:T(8,128)(2,1)S(1)}, bf16[512,512]{1,0:T(8,128)(2,1)S(1)}, u32[]{:S(2)}, u32[]{:S(2)}) collective-permute-start(bf16[512,512]{1,0:T(8,128)(2,1)S(1)} %join.5.refs_0_), channel_id=1, source_target_pairs={{4,0},{8,4},{12,8},{0,12},{5,1},{9,5},{13,9},{1,13},{6,2},{10,6},{... | collective-permute-start | bytes 1572872 | tf_op jit(solution)/shard_map/ppermute | solution.py:139
  111.3 14.9 %collective-permute-start.14 = (bf16[512,512]{1,0:T(8,128)(2,1)S(1)}, bf16[512,512]{1,0:T(8,128)(2,1)S(1)}, u32[]{:S(2)}, u32[]{:S(2)}) collective-permute-start(bf16[512,512]{1,0:T(8,128)(2,1)S(1)} %join.5.refs_0_), channel_id=1, source_target_pairs={{12,0},{0,4},{4,8},{8,12},{13,1},{1,5},{5,9},{9,13},{14,2},{2,6},{... | collective-permute-start | bytes 1572872 | tf_op jit(solution)/shard_map/ppermute | solution.py:139
  112.4 13.9 %collective-permute-start.20 = (f32[256,256]{1,0:T(8,128)S(1)}, f32[256,256]{1,0:T(8,128)S(1)}, u32[]{:S(2)}, u32[]{:S(2)}) collective-permute-start(f32[256,256]{1,0:T(8,128)S(1)} %convert_add_fusion), channel_id=1, source_target_pairs={{0,32},{32,0},{1,33},{33,1},{2,34},{34,2},{3,35},{35,3},{4,36},{36... | collective-permute-start | bytes 786440 | tf_op jit(solution)/shard_map/ppermute | solution.py:135
  123.7 7.8 %collective-permute-start.13 = (bf16[256,512]{1,0:T(8,128)(2,1)S(1)}, bf16[256,512]{1,0:T(8,128)(2,1)S(1)}, u32[]{:S(2)}, u32[]{:S(2)}) collective-permute-start(bf16[256,512]{1,0:T(8,128)(2,1)S(1)} %slice.114), channel_id=1, source_target_pairs={{4,0},{8,4},{12,8},{0,12},{5,1},{9,5},{13,9},{1,13},{6,2},{10,6},{... | collective-permute-start | bytes 786440 | tf_op jit(solution)/shard_map/ppermute | solution.py:139
  126.2 8.1 %collective-permute-start.15 = (bf16[256,512]{1,0:T(8,128)(2,1)S(1)}, bf16[256,512]{1,0:T(8,128)(2,1)S(1)}, u32[]{:S(2)}, u32[]{:S(2)}) collective-permute-start(bf16[256,512]{1,0:T(8,128)(2,1)S(1)} %slice.115), channel_id=1, source_target_pairs={{12,0},{0,4},{4,8},{8,12},{13,1},{1,5},{5,9},{9,13},{14,2},{2,6},{... | collective-permute-start | bytes 786440 | tf_op jit(solution)/shard_map/ppermute | solution.py:139
  126.3 11.9 %copy-start.6 = (f32[256,256]{1,0:T(8,128)}, f32[256,256]{1,0:T(8,128)S(1)}, u32[]{:S(2)}) copy-start(f32[256,256]{1,0:T(8,128)S(1)} %add_multiply_fusion.refs_5_) | copy-start | bytes 786436
  139.3 28.5 %all-to-all-start.3 = ((bf16[16,64,512]{2,1,0:T(8,128)(2,1)}), bf16[16,64,512]{2,1,0:T(8,128)(2,1)S(1)}, u32[]{:S(2)}, u32[]{:S(2)}) async-start(bf16[16,64,512]{2,1,0:T(8,128)(2,1)} %bitcast.39), calls=%async_computation.3 | async-start | bytes 2097152 | tf_op jit(solution)/shard_map/all_to_all | solution.py:196
  167.8 28.2 %all-to-all-start.1 = ((bf16[16,64,768]{2,1,0:T(8,128)(2,1)}), bf16[16,64,768]{2,1,0:T(8,128)(2,1)}, u32[]{:S(2)}, u32[]{:S(2)}) async-start(bf16[16,64,768]{2,1,0:T(8,128)(2,1)} %bitcast.41), calls=%async_computation.1 | async-start | bytes 3145728 | tf_op jit(solution)/shard_map/all_to_all | solution.py:196
  182.0 17.7 %copy-start.7 = (f32[256,256]{1,0:T(8,128)S(1)}, f32[256,256]{1,0:T(8,128)}, u32[]{:S(2)}) copy-start(f32[256,256]{1,0:T(8,128)} %copy-done.6) | copy-start | bytes 786436
  196.0 31.5 %all-to-all-start.2 = ((bf16[16,64,768]{2,1,0:T(8,128)(2,1)}), bf16[16,64,768]{2,1,0:T(8,128)(2,1)S(1)}, u32[]{:S(2)}, u32[]{:S(2)}) async-start(bf16[16,64,768]{2,1,0:T(8,128)(2,1)} %bitcast.40), calls=%async_computation.2 | async-start | bytes 3145728 | tf_op jit(solution)/shard_map/all_to_all | solution.py:196
  199.7 27.0 %collective-permute-start.21 = (f32[256,256]{1,0:T(8,128)S(1)}, f32[256,256]{1,0:T(8,128)S(1)}, u32[]{:S(2)}, u32[]{:S(2)}) collective-permute-start(f32[256,256]{1,0:T(8,128)S(1)} %copy-done.7), channel_id=1, source_target_pairs={{0,64},{64,0},{1,65},{65,1},{2,66},{66,2},{3,67},{67,3},{4,68},{68... | collective-permute-start | bytes 786440 | tf_op jit(solution)/shard_map/ppermute | solution.py:135
  (18 other events, 23.4 us)

commit v4 on v3

--- a/solution.py
+++ b/solution.py
@@ -20,11 +20,16 @@
     return pltpu.CompilerParams(vmem_limit_bytes=16 << 20)
 
 
-def pack_kernel(at_ref, float_ref, quant_ref, after_ref, out_ref):
+def pack_kernel(at_ref, float_ref, quant_ref, after_ref, out_ref, head_ref, sems, head_sem):
     width = float_ref.shape[1] // 32
     yl, z = at_ref[0], at_ref[1]
-    quant = quant_ref[:, :BLOCK]
-    shift = (float_ref[:, :BLOCK].astype(F32) - quant.astype(F32)).astype(BF16)
+    heads = [
+        pltpu.make_async_copy(ref.at[:, pl.ds(0, BLOCK)], head_ref.at[kind], head_sem.at[kind])
+        for kind, ref in enumerate((float_ref, quant_ref))
+    ]
+    for copy in heads:
+        copy.start()
+    copies = []
     for kind, ref in enumerate((float_ref, quant_ref)):
         for x in range(4):
             for j in range(4):
@@ -32,9 +37,24 @@
                     block = ((yl ^ r) * 4 + lax.rem(z + j, 4)) * 4 + x
                     start = pl.multiple_of(block * width, width)
                     at = (j * 2 + r) * width
-                    out_ref[kind * 4 + x, :, at : at + width] = ref[:, pl.ds(start, width)]
-            out_ref[kind * 4 + x, :, 8 * width : 8 * width + BLOCK] = quant
-            out_ref[kind * 4 + x, :, 8 * width + BLOCK :] = shift
+                    copies.append(
+                        pltpu.make_async_copy(
+                            ref.at[:, pl.ds(start, width)],
+                            out_ref.at[kind * 4 + x, :, pl.ds(at, width)],
+                            sems.at[len(copies)],
+                        )
+                    )
+    for copy in copies:
+        copy.start()
+    for copy in heads:
+        copy.wait()
+    quant = head_ref[1]
+    shift = (head_ref[0].astype(F32) - quant.astype(F32)).astype(BF16)
+    for d in range(8):
+        out_ref[d, :, 8 * width : 8 * width + BLOCK] = quant
+        out_ref[d, :, 8 * width + BLOCK :] = shift
+    for copy in copies:
+        copy.wait()
 
 
 def pack(at, attn_float, attn_quant, after):
@@ -42,11 +62,46 @@
     return pl.pallas_call(
         pack_kernel,
         out_shape=jax.ShapeDtypeStruct((8, tokens, d_in // 4 + 2 * BLOCK), BF16),
-        in_specs=[SCALAR, WHOLE, WHOLE, LEFT],
+        in_specs=[SCALAR, LEFT, LEFT, LEFT],
         out_specs=WHOLE,
+        scratch_shapes=[
+            pltpu.VMEM((2, tokens, BLOCK), BF16),
+            pltpu.SemaphoreType.DMA((64,)),
+            pltpu.SemaphoreType.DMA((2,)),
+        ],
         compiler_params=params(),
         name="pack",
     )(at, attn_float, attn_quant, after)
+
+
+def stats_kernel(core_ref, mine_ref, other_ref, after_ref, *outs):
+    core = core_ref[0]
+    width = outs[0].shape[0]
+    tail = 8 * width
+    for j, out in enumerate(outs):
+        start = pl.multiple_of((2 * j + core) * width, width)
+        total = None
+        for acts in (mine_ref, other_ref):
+            term = lax.dot_general(
+                acts[:, pl.ds(start, width)],
+                acts[:, tail:],
+                (((0,), (0,)), ((), ())),
+                preferred_element_type=F32,
+            )
+            total = term if total is None else total + term
+        out[...] = total.astype(BF16)
+
+
+def stats(core, mine, other, after):
+    width = 2 * BLOCK
+    return pl.pallas_call(
+        stats_kernel,
+        out_shape=(jax.ShapeDtypeStruct((width, width), BF16),) * 4,
+        in_specs=[SCALAR, WHOLE, WHOLE, LEFT],
+        out_specs=(WHOLE,) * 4,
+        compiler_params=params(),
+        name="stats",
+    )(core.reshape(1), mine, other, after)
 
 
 def join_kernel(*refs):
@@ -172,6 +227,12 @@
     def far(up, down):
         return from_z(up[:features], 1), from_z(down[features:], 3)
 
+    def output(partial):
+        width = partial.shape[-1]
+        return lax.all_to_all(
+            partial.reshape(16, tokens, width), ("yh", "core", "x"), 0, 0, tiled=True
+        )
+
     w0, w1, w2 = WIDTHS
     rows0 = join(*exchange(0, w0), ())
     near0 = near(rows0)
@@ -181,51 +242,46 @@
     mine = mine.reshape(8 * tokens, 8 * features + 2 * BLOCK)
 
     far0 = far(*near0)
-    rows1 = join(*exchange(w0, w1), far0)
+    rows1 = join(*exchange(w0, w1), near0)
+    mine, rows1 = lax.optimization_barrier((mine, rows1))
     near1 = near(rows1)
-    mine, *near0 = lax.optimization_barrier((mine, *near0))
     other = swap(mine, "core")
+    partial0 = project(core, mine, other, (rows0, near0[0], *far0, near0[1]), ())
+    result0 = output(partial0)
+
+    near1 = lax.optimization_barrier((*near1, partial0))[:2]
     far1 = far(*near1)
-    rows2 = join(*exchange(w0 + w1, w2), far1)
-    near2 = near(rows2)
-    far2 = far(*near2)
-
-    def part(rows, near, far, after):
-        width = rows.shape[1]
-        partial = project(core, mine, other, (rows, near[0], *far, near[1]), after)
-        return lax.all_to_all(
-            partial.reshape(16, tokens, width), ("yh", "core", "x"), 0, 0, tiled=True
-        )
-
-    result0 = part(rows0, near0, far0, ())
-
-    def stats(j):
-        at = 2 * j * features
-        total = 0.0
-        for acts in (mine, other):
-            picked = jnp.where(
-                core == 0, acts[:, at : at + features], acts[:, at + features : at + 2 * features]
-            )
-            total = total + lax.dot_general(
-                picked, acts[:, 8 * features :], (((0,), (0,)), ((), ())), preferred_element_type=F32
-            )
-        return total
 
     total = 0.0
-    for j in range(4):
-        pairs = [
+    for j, block in enumerate(stats(core, mine, other, partial0)):
+        homes = [
             (c * 8 + b * 4 + i, c * 8 + (b ^ c) * 4 + (i + j) % 4)
             for c in range(2)
             for b in range(2)
             for i in range(4)
         ]
-        total = total + lax.ppermute(stats(j).astype(BF16), ("core", "yl", "z"), pairs).astype(F32)
+        total = total + lax.ppermute(block, ("core", "yl", "z"), homes).astype(F32)
+
+    rows2 = join(*exchange(w0 + w1, w2), far1)
+    near2 = near(rows2)
+    partial1 = project(
+        core, mine, other, (rows1, near1[0], *far1, near1[1]), (rows2, total)
+    )
+    result1 = output(partial1)
     total = (total + swap(total, "core")) * inverse
-
-    result1 = part(rows1, near1, far1, ())
-    result2 = part(rows2, near2, far2, (total,))
+    near2 = lax.optimization_barrier((*near2, partial1))[:2]
+    far2 = far(*near2)
+
+    piece = lax.dynamic_slice_in_dim(total, core * BLOCK, BLOCK, 0)
+    piece = swap(piece, "yh")
+    partial2 = project(core, mine, other, (rows2, near2[0], *far2, near2[1]), (total,))
+    result2 = output(partial2)
+    again = swap(piece, "core")
+    moved = jnp.where(
+        core == 0, jnp.concatenate([piece, again]), jnp.concatenate([again, piece])
+    )
+    total = jnp.where(yh == 1, total, moved)
     float_out, quant_out = finish((result0, result1, result2))
-    total = jnp.where(yh == 1, total, swap(total, "yh"))
     return float_out, quant_out, total[:, :BLOCK], total[:, BLOCK:]
 
 

time: 235 us -> 210 us (0.89)
  waiting for transfers between devices: 121 us -> 93.5 us
  matrix products: 6.74 us -> 0 us
  local copies, waits for them, and re-layouts: 24.9 us -> 31.5 us
  starting transfers between devices: 54.8 us -> 58.6 us
    ppermute x12, waiting for transfers between devices: 62 us -> 32 us  [from_z(): return lax.ppermute(a, 'z', [((i + j) % 4, i) for i in range(4)])]
    ppermute x3, waiting for transfers between devices: 6.2 us -> 32.2 us  [exchange(): return (own, lax.ppermute(send, ('yh', 'core', 'yl'), pairs))]
    all_to_all x3, waiting for transfers between devices: 21.1 us -> 0.01 us  [output(): lax.all_to_all(partial.reshape(16, tokens, width), ('yh', 'core', 'x'), 0...]
    ppermute x4, waiting for transfers between devices: 0.72 us -> 12.9 us  [shards(): total = total + lax.ppermute(block, ('core', 'yl', 'z'), homes).astype(F32)]
    all_to_all x1, waiting for transfers between devices: 7.17 us -> 0.01 us  [shards(): mine = lax.all_to_all(payload, ('yh', 'x'), 0, 0, tiled=True)]
    ppermute x3 -> x4, waiting for transfers between devices: 23.6 us -> 16.5 us  [swap(): return lax.ppermute(a, axis, [(0, 1), (1, 0)])]
    dot_general x8 -> x0, matrix products: 6.74 us -> none  [stats(): lax.dot_general(picked, acts[:, 8 * features:], (((0,), (0,)), ((), ())),...]
    unnamed x48 -> x46, local copies, waits for them, and re-layouts: 18.7 us -> 23.6 us
  transfers between devices with their start and end apart: 26 -> 27, of which waited for: 15 -> 11; matrix products, arithmetic and copies ran while one was open for 6% -> 5% of each run, Pallas kernels for 5% -> 6%
where the time goes in v4:
time: 210 us; the launch traced here: 207 us
  waiting for transfers between devices  93.5 us (45%)
  starting transfers between devices  58.6 us (28%)
  local copies, waits for them, and re-layouts  31.5 us (15%)
  Pallas kernels  17.5 us (8%)
  other arithmetic  5.28 us (3%)
    ppermute x3, waiting for transfers between devices, exchange(): return (own, lax.ppermute(send, ('yh', 'core', 'yl'), pairs))  32.2 us
    ppermute x12, waiting for transfers between devices, from_z(): return lax.ppermute(a, 'z', [((i + j) % 4, i) for i in range(4)])  32 us
    unnamed x46, local copies, waits for them, and re-layouts  23.6 us
    ppermute x12, starting transfers between devices, from_z(): return lax.ppermute(a, 'z', [((i + j) % 4, i) for i in range(4)])  21.9 us
    all_to_all x3, starting transfers between devices, output(): lax.all_to_all(partial.reshape(16, tokens, width), ('yh', 'core', 'x'), 0...  20 us
    ppermute x4, waiting for transfers between devices, swap(): return lax.ppermute(a, axis, [(0, 1), (1, 0)])  16.5 us
    ppermute x4, waiting for transfers between devices, shards(): total = total + lax.ppermute(block, ('core', 'yl', 'z'), homes).astype(F32)  12.9 us
    pallas_call x3, Pallas kernels, project(): pl.pallas_call(project_kernel, out_shape=jax.ShapeDtypeStruct((2, 2, rows...  11.5 us
  transfers between devices with their start and end apart: 27, of which 11 were waited for; matrix products, arithmetic and copies ran while one was open for 5% of the time, Pallas kernels for 6%

profile of v4, /device:TPU:0, one launch (start us, length us, event | category | flops | bytes accessed | tf_op | source)
XLA Modules:
  0.0 207.4 jit_solution(12241439782499486530)
XLA Ops:
  1.4 2.7 %broadcast_select_fusion = (bf16[256,768]{1,0:T(8,128)(2,1)}, bf16[256,768]{1,0:T(8,128)(2,1)S(1)}, bf16[256,768]{1,0:T(8,128)(2,1)S(1)}, bf16[256,768]{1,0:T(8,128)(2,1)S(1)}) fusion(pred[]{:T(512)S(6)} %eq.17, bf16[256,4096]{1,0:T(8,128)(2,1)} %param.7, s32[]{:T(128)S(6)} %select_n.82, f32[2,768]{1,0:T(2,128)S(1)} %get-tuple-element.38, ...), kind=kLoop, calls=%fused_computation.6 | loop fusion | flops 2359296 | bytes 3944458 | tf_op jit(solution)/shard_map/jit(_where)/select_n | solution.py:211
  4.1 1.7 collective-permute-start
  5.8 6.0 %collective-permute-done.refs_1_ = bf16[256,768]{1,0:T(8,128)(2,1)S(1)} collective-permute-done((bf16[256,768]{1,0:T(8,128)(2,1)S(1)}, bf16[256,768]{1,0:T(8,128)(2,1)S(1)}, u32[]{:S(2)}, u32[]{:S(2)}) %collective-permute-start) | collective-permute-done | bytes 393248 | tf_op jit(solution)/shard_map/ppermute | solution.py:222
  14.4 1.8 pack.1
  17.6 7.0 %all-to-all-start = ((bf16[8,64,2304]{2,1,0:T(8,128)(2,1)}), bf16[8,64,2304]{2,1,0:T(8,128)(2,1)S(1)}, u32[]{:S(2)}, u32[]{:S(2)}) async-start(bf16[8,64,2304]{2,1,0:T(8,128)(2,1)} %copy-done.4), calls=%async_computation | async-start | bytes 4718592 | tf_op jit(solution)/shard_map/all_to_all | solution.py:241
  24.6 4.0 %collective-permute-start.2 = (bf16[512,768]{1,0:T(8,128)(2,1)S(1)}, bf16[512,768]{1,0:T(8,128)(2,1)S(1)}, u32[]{:S(2)}, u32[]{:S(2)}) collective-permute-start(bf16[512,768]{1,0:T(8,128)(2,1)S(1)} %join.3.after_ref.refs_0_), channel_id=1, source_target_pairs={{4,0},{8,4},{12,8},{0,12},{5,1},{9,5},{13,9},{1,13},{6,2},{10,6},{... | collective-permute-start | bytes 2359304 | tf_op jit(solution)/shard_map/ppermute | solution.py:194
  29.3 26.1 %collective-permute-done.1.refs_1_ = bf16[256,768]{1,0:T(8,128)(2,1)S(1)} collective-permute-done((bf16[256,768]{1,0:T(8,128)(2,1)}, bf16[256,768]{1,0:T(8,128)(2,1)S(1)}, u32[]{:S(2)}, u32[]{:S(2)}) %collective-permute-start.1) | collective-permute-done | bytes 393248 | tf_op jit(solution)/shard_map/ppermute | solution.py:222
  60.7 4.1 %collective-permute-start.5 = (bf16[256,768]{1,0:T(8,128)(2,1)S(1)}, bf16[256,768]{1,0:T(8,128)(2,1)S(1)}, u32[]{:S(2)}, u32[]{:S(2)}) collective-permute-start(bf16[256,768]{1,0:T(8,128)(2,1)S(1)} %slice.32), channel_id=1, source_target_pairs={{4,0},{8,4},{12,8},{0,12},{5,1},{9,5},{13,9},{1,13},{6,2},{10,6},{... | collective-permute-start | bytes 1179656 | tf_op jit(solution)/shard_map/ppermute | solution.py:194
  65.9 3.2 %collective-permute-start.7 = (bf16[512,768]{1,0:T(8,128)(2,1)}, bf16[512,768]{1,0:T(8,128)(2,1)}, u32[]{:S(2)}, u32[]{:S(2)}) collective-permute-start(bf16[512,768]{1,0:T(8,128)(2,1)} %copy-done.14), channel_id=1, source_target_pairs={{4,0},{8,4},{12,8},{0,12},{5,1},{9,5},{13,9},{1,13},{6,2},{10,6},{... | collective-permute-start | bytes 2359304 | tf_op jit(solution)/shard_map/ppermute | solution.py:194
  69.1 5.2 %collective-permute-done.5.refs_2_ = bf16[256,768]{1,0:T(8,128)(2,1)S(1)} collective-permute-done((bf16[256,768]{1,0:T(8,128)(2,1)S(1)}, bf16[256,768]{1,0:T(8,128)(2,1)S(1)}, u32[]{:S(2)}, u32[]{:S(2)}) %collective-permute-start.5) | collective-permute-done | bytes 393248 | tf_op jit(solution)/shard_map/ppermute | solution.py:194
  74.3 4.8 %collective-permute-done.6.refs_3_ = bf16[256,768]{1,0:T(8,128)(2,1)S(1)} collective-permute-done((bf16[256,768]{1,0:T(8,128)(2,1)S(1)}, bf16[256,768]{1,0:T(8,128)(2,1)S(1)}, u32[]{:S(2)}, u32[]{:S(2)}) %collective-permute-start.6) | collective-permute-done | bytes 393248 | tf_op jit(solution)/shard_map/ppermute | solution.py:194
  79.1 1.7 copy-done.8
  81.9 3.4 %project.3.after_ref = bf16[2,2,256,768]{3,2,1,0:T(8,128)(2,1)S(1)} custom-call(s32[1]{0:T(128)} %bitcast.core_ref, bf16[512,2304]{1,0:T(8,128)(2,1)S(1)} %bitcast.32, bf16[512,2304]{1,0:T(8,128)(2,1)S(1)} %collective-permute-done.4.other_ref, bf16[512,768]{1,0:T(8,128)(2,1)S(1)} %join.3.after_ref.refs_0_, bf16[512,768]{1,0:T(8,128)(2,1)S(1)} %copy-done.8, ...), custom_call_target="tpu_custom_call" | custom-call | flops 3221225472 | bytes 8388608 | tf_op jit(solution)/shard_map/project/pallas_call | solution.py:148
  86.5 6.2 %all-to-all-start.1 = ((bf16[16,64,768]{2,1,0:T(8,128)(2,1)}), bf16[16,64,768]{2,1,0:T(8,128)(2,1)}, u32[]{:S(2)}, u32[]{:S(2)}) async-start(bf16[16,64,768]{2,1,0:T(8,128)(2,1)} %bitcast.36), calls=%async_computation.1 | async-start | bytes 3145728 | tf_op jit(solution)/shard_map/all_to_all | solution.py:232
  92.7 1.7 copy-done.1
  96.7 1.8 slice.26
  99.2 3.9 %collective-permute-start.9 = (bf16[256,768]{1,0:T(8,128)(2,1)}, bf16[256,768]{1,0:T(8,128)(2,1)S(1)}, u32[]{:S(2)}, u32[]{:S(2)}) collective-permute-start(bf16[256,768]{1,0:T(8,128)(2,1)} %slice.26), channel_id=1, source_target_pairs={{4,0},{8,4},{12,8},{0,12},{5,1},{9,5},{13,9},{1,13},{6,2},{10,6},{... | collective-permute-start | bytes 1179656 | tf_op jit(solution)/shard_map/ppermute | solution.py:194
  103.1 1.8 slice.27
  109.2 12.9 %collective-permute-done.13 = bf16[256,256]{1,0:T(8,128)(2,1)} collective-permute-done((bf16[256,256]{1,0:T(8,128)(2,1)S(1)}, bf16[256,256]{1,0:T(8,128)(2,1)}, u32[]{:S(2)}, u32[]{:S(2)}) %collective-permute-start.13) | collective-permute-done | bytes 131104 | tf_op jit(solution)/shard_map/ppermute | solution.py:263
  129.9 4.8 %project.4 = bf16[2,2,256,768]{3,2,1,0:T(8,128)(2,1)S(1)} custom-call(s32[1]{0:T(128)} %bitcast.core_ref, bf16[512,2304]{1,0:T(8,128)(2,1)S(1)} %bitcast.34, bf16[512,2304]{1,0:T(8,128)(2,1)S(1)} %copy-done.2, bf16[512,768]{1,0:T(8,128)(2,1)S(1)} %copy-done.15, bf16[512,768]{1,0:T(8,128)(2,1)} %collective-permute-done.7.refs_1_, ...), custom_call_target="tpu_custom_call" | custom-call | flops 3221225472 | bytes 8388608 | tf_op jit(solution)/shard_map/project/pallas_call | solution.py:148
  135.9 7.0 %all-to-all-start.2 = ((bf16[16,64,768]{2,1,0:T(8,128)(2,1)}), bf16[16,64,768]{2,1,0:T(8,128)(2,1)}, u32[]{:S(2)}, u32[]{:S(2)}) async-start(bf16[16,64,768]{2,1,0:T(8,128)(2,1)} %bitcast.37), calls=%async_computation.2 | async-start | bytes 3145728 | tf_op jit(solution)/shard_map/all_to_all | solution.py:232
  142.9 4.4 %collective-permute-start.16 = (bf16[512,512]{1,0:T(8,128)(2,1)S(1)}, bf16[512,512]{1,0:T(8,128)(2,1)S(1)}, u32[]{:S(2)}, u32[]{:S(2)}) collective-permute-start(bf16[512,512]{1,0:T(8,128)(2,1)S(1)} %join.5.refs_5_.refs_0_), channel_id=1, source_target_pairs={{4,0},{8,4},{12,8},{0,12},{5,1},{9,5},{13,9},{1,13},{6,2},{10,6},{... | collective-permute-start | bytes 1572872 | tf_op jit(solution)/shard_map/ppermute | solution.py:194
  147.3 11.6 %collective-permute-done.16.refs_1_ = bf16[512,512]{1,0:T(8,128)(2,1)S(1)} collective-permute-done((bf16[512,512]{1,0:T(8,128)(2,1)S(1)}, bf16[512,512]{1,0:T(8,128)(2,1)S(1)}, u32[]{:S(2)}, u32[]{:S(2)}) %collective-permute-start.16) | collective-permute-done | bytes 524320 | tf_op jit(solution)/shard_map/ppermute | solution.py:194
  158.9 3.4 %collective-permute-done.17.refs_4_ = bf16[512,512]{1,0:T(8,128)(2,1)S(1)} collective-permute-done((bf16[512,512]{1,0:T(8,128)(2,1)S(1)}, bf16[512,512]{1,0:T(8,128)(2,1)S(1)}, u32[]{:S(2)}, u32[]{:S(2)}) %collective-permute-start.17) | collective-permute-done | bytes 524320 | tf_op jit(solution)/shard_map/ppermute | solution.py:194
  162.7 1.8 collective-permute-start.19
  164.6 5.3 %collective-permute-done.18.refs_2_ = bf16[256,512]{1,0:T(8,128)(2,1)S(1)} collective-permute-done((bf16[256,512]{1,0:T(8,128)(2,1)S(1)}, bf16[256,512]{1,0:T(8,128)(2,1)S(1)}, u32[]{:S(2)}, u32[]{:S(2)}) %collective-permute-start.18) | collective-permute-done | bytes 262176 | tf_op jit(solution)/shard_map/ppermute | solution.py:194
  171.5 1.7 copy-done.3
  173.2 3.3 %project.5 = bf16[2,2,256,512]{3,2,1,0:T(8,128)(2,1)} custom-call(s32[1]{0:T(128)} %bitcast.core_ref, bf16[512,2304]{1,0:T(8,128)(2,1)S(1)} %bitcast.35, bf16[512,2304]{1,0:T(8,128)(2,1)S(1)} %copy-done.3, bf16[512,512]{1,0:T(8,128)(2,1)S(1)} %join.5.refs_5_.refs_0_, bf16[512,512]{1,0:T(8,128)(2,1)S(1)} %collective-permute-done.16.refs_1_, ...), custom_call_target="tpu_custom_call" | custom-call | flops 2147483648 | bytes 8388608 | tf_op jit(solution)/shard_map/project/pallas_call | solution.py:148
  176.5 6.8 %all-to-all-start.3 = ((bf16[16,64,512]{2,1,0:T(8,128)(2,1)}), bf16[16,64,512]{2,1,0:T(8,128)(2,1)S(1)}, u32[]{:S(2)}, u32[]{:S(2)}) async-start(bf16[16,64,512]{2,1,0:T(8,128)(2,1)} %bitcast.9), calls=%async_computation.3 | async-start | bytes 2097152 | tf_op jit(solution)/shard_map/all_to_all | solution.py:232
  183.4 3.5 %collective-permute-start.21 = (f32[128,256]{1,0:T(8,128)S(1)}, f32[128,256]{1,0:T(8,128)S(1)}, u32[]{:S(2)}, u32[]{:S(2)}) collective-permute-start(f32[128,256]{1,0:T(8,128)S(1)} %constant_dynamic-slice_fusion), channel_id=1, source_target_pairs={{0,64},{64,0},{1,65},{65,1},{2,66},{66,2},{3,67},{67,3},{4,68},{68... | collective-permute-start | bytes 393224 | tf_op jit(solution)/shard_map/ppermute | solution.py:190
  186.9 15.2 %collective-permute-done.21 = f32[128,256]{1,0:T(8,128)S(1)} collective-permute-done((f32[128,256]{1,0:T(8,128)S(1)}, f32[128,256]{1,0:T(8,128)S(1)}, u32[]{:S(2)}, u32[]{:S(2)}) %collective-permute-start.21) | collective-permute-done | bytes 131104 | tf_op jit(solution)/shard_map/ppermute | solution.py:190
  204.1 3.3 %finish.1 = (bf16[64,4096]{1,0:T(8,128)(2,1)}, bf16[64,4096]{1,0:T(8,128)(2,1)}) custom-call(bf16[16,64,768]{2,1,0:T(8,128)(2,1)} %all-to-all-done.1.refs_0_, bf16[16,64,768]{2,1,0:T(8,128)(2,1)} %all-to-all-done.2.refs_1_, bf16[16,64,512]{2,1,0:T(8,128)(2,1)S(1)} %all-to-all-done.3.refs_2_), custom_call_target="tpu_custom_call" | custom-call | tf_op jit(solution)/shard_map/finish/pallas_call | solution.py:179
  (93 shorter events, 34.5 us)
Async XLA Ops:
  4.1 7.8 %collective-permute-start = (bf16[256,768]{1,0:T(8,128)(2,1)S(1)}, bf16[256,768]{1,0:T(8,128)(2,1)S(1)}, u32[]{:S(2)}, u32[]{:S(2)}) collective-permute-start(bf16[256,768]{1,0:T(8,128)(2,1)S(1)} %get-tuple-element.35), channel_id=1, source_target_pairs={{0,16},{16,0},{32,112},{48,96},{64,80},{80,64},{96,48},{112,32},{1... | collective-permute-start | bytes 1179656 | tf_op jit(solution)/shard_map/ppermute | solution.py:222
  17.6 40.6 %all-to-all-start = ((bf16[8,64,2304]{2,1,0:T(8,128)(2,1)}), bf16[8,64,2304]{2,1,0:T(8,128)(2,1)S(1)}, u32[]{:S(2)}, u32[]{:S(2)}) async-start(bf16[8,64,2304]{2,1,0:T(8,128)(2,1)} %copy-done.4), calls=%async_computation | async-start | bytes 4718592 | tf_op jit(solution)/shard_map/all_to_all | solution.py:241
  24.6 30.8 %collective-permute-start.2 = (bf16[512,768]{1,0:T(8,128)(2,1)S(1)}, bf16[512,768]{1,0:T(8,128)(2,1)S(1)}, u32[]{:S(2)}, u32[]{:S(2)}) collective-permute-start(bf16[512,768]{1,0:T(8,128)(2,1)S(1)} %join.3.after_ref.refs_0_), channel_id=1, source_target_pairs={{4,0},{8,4},{12,8},{0,12},{5,1},{9,5},{13,9},{1,13},{6,2},{10,6},{... | collective-permute-start | bytes 2359304 | tf_op jit(solution)/shard_map/ppermute | solution.py:194
  28.6 26.8 %collective-permute-start.3 = (bf16[512,768]{1,0:T(8,128)(2,1)S(1)}, bf16[512,768]{1,0:T(8,128)(2,1)S(1)}, u32[]{:S(2)}, u32[]{:S(2)}) collective-permute-start(bf16[512,768]{1,0:T(8,128)(2,1)S(1)} %join.3.after_ref.refs_0_), channel_id=1, source_target_pairs={{12,0},{0,4},{4,8},{8,12},{13,1},{1,5},{5,9},{9,13},{14,2},{2,6},{... | collective-permute-start | bytes 2359304 | tf_op jit(solution)/shard_map/ppermute | solution.py:194
  28.6 26.8 %collective-permute-start.1 = (bf16[256,768]{1,0:T(8,128)(2,1)}, bf16[256,768]{1,0:T(8,128)(2,1)S(1)}, u32[]{:S(2)}, u32[]{:S(2)}) collective-permute-start(bf16[256,768]{1,0:T(8,128)(2,1)} %get-tuple-element.28), channel_id=1, source_target_pairs={{0,16},{16,0},{32,112},{48,96},{64,80},{80,64},{96,48},{112,32},{1... | collective-permute-start | bytes 1179656 | tf_op jit(solution)/shard_map/ppermute | solution.py:222
  58.2 20.9 %collective-permute-start.4 = (bf16[512,2304]{1,0:T(8,128)(2,1)S(1)}, bf16[512,2304]{1,0:T(8,128)(2,1)S(1)}, u32[]{:S(2)}, u32[]{:S(2)}) collective-permute-start(bf16[512,2304]{1,0:T(8,128)(2,1)S(1)} %bitcast.31), channel_id=1, source_target_pairs={{0,32},{32,0},{1,33},{33,1},{2,34},{34,2},{3,35},{35,3},{4,36},{36... | collective-permute-start | bytes 7077896 | tf_op jit(solution)/shard_map/ppermute | solution.py:190
  60.7 13.6 %collective-permute-start.5 = (bf16[256,768]{1,0:T(8,128)(2,1)S(1)}, bf16[256,768]{1,0:T(8,128)(2,1)S(1)}, u32[]{:S(2)}, u32[]{:S(2)}) collective-permute-start(bf16[256,768]{1,0:T(8,128)(2,1)S(1)} %slice.32), channel_id=1, source_target_pairs={{4,0},{8,4},{12,8},{0,12},{5,1},{9,5},{13,9},{1,13},{6,2},{10,6},{... | collective-permute-start | bytes 1179656 | tf_op jit(solution)/shard_map/ppermute | solution.py:194
  65.8 13.3 %collective-permute-start.6 = (bf16[256,768]{1,0:T(8,128)(2,1)S(1)}, bf16[256,768]{1,0:T(8,128)(2,1)S(1)}, u32[]{:S(2)}, u32[]{:S(2)}) collective-permute-start(bf16[256,768]{1,0:T(8,128)(2,1)S(1)} %slice.33), channel_id=1, source_target_pairs={{12,0},{0,4},{4,8},{8,12},{13,1},{1,5},{5,9},{9,13},{14,2},{2,6},{... | collective-permute-start | bytes 1179656 | tf_op jit(solution)/shard_map/ppermute | solution.py:194
  65.9 30.7 %collective-permute-start.7 = (bf16[512,768]{1,0:T(8,128)(2,1)}, bf16[512,768]{1,0:T(8,128)(2,1)}, u32[]{:S(2)}, u32[]{:S(2)}) collective-permute-start(bf16[512,768]{1,0:T(8,128)(2,1)} %copy-done.14), channel_id=1, source_target_pairs={{4,0},{8,4},{12,8},{0,12},{5,1},{9,5},{13,9},{1,13},{6,2},{10,6},{... | collective-permute-start | bytes 2359304 | tf_op jit(solution)/shard_map/ppermute | solution.py:194
  69.1 27.5 %collective-permute-start.8 = (bf16[512,768]{1,0:T(8,128)(2,1)}, bf16[512,768]{1,0:T(8,128)(2,1)}, u32[]{:S(2)}, u32[]{:S(2)}) collective-permute-start(bf16[512,768]{1,0:T(8,128)(2,1)} %copy-done.14), channel_id=1, source_target_pairs={{12,0},{0,4},{4,8},{8,12},{13,1},{1,5},{5,9},{9,13},{14,2},{2,6},{... | collective-permute-start | bytes 2359304 | tf_op jit(solution)/shard_map/ppermute | solution.py:194
  79.1 6.2 %copy-start = (bf16[512,2304]{1,0:T(8,128)(2,1)}, bf16[512,2304]{1,0:T(8,128)(2,1)S(1)}, u32[]{:S(2)}) copy-start(bf16[512,2304]{1,0:T(8,128)(2,1)S(1)} %collective-permute-done.4.other_ref) | copy-start | bytes 7077892
  79.1 1.7 copy-start.8
  86.5 49.3 %all-to-all-start.1 = ((bf16[16,64,768]{2,1,0:T(8,128)(2,1)}), bf16[16,64,768]{2,1,0:T(8,128)(2,1)}, u32[]{:S(2)}, u32[]{:S(2)}) async-start(bf16[16,64,768]{2,1,0:T(8,128)(2,1)} %bitcast.36), calls=%async_computation.1 | async-start | bytes 3145728 | tf_op jit(solution)/shard_map/all_to_all | solution.py:232
  92.7 1.7 copy-start.1
  96.6 8.3 %collective-permute-start.15 = (bf16[256,256]{1,0:T(8,128)(2,1)S(1)}, bf16[256,256]{1,0:T(8,128)(2,1)S(1)}, u32[]{:S(2)}, u32[]{:S(2)}) collective-permute-start(bf16[256,256]{1,0:T(8,128)(2,1)S(1)} %get-tuple-element.23), channel_id=1, source_target_pairs={{0,12},{4,0},{8,4},{12,8},{16,28},{20,16},{24,20},{28,24},{32,60},... | collective-permute-start | bytes 393224 | tf_op jit(solution)/shard_map/ppermute | solution.py:263
  98.4 10.5 %collective-permute-start.14 = (bf16[256,256]{1,0:T(8,128)(2,1)S(1)}, bf16[256,256]{1,0:T(8,128)(2,1)}, u32[]{:S(2)}, u32[]{:S(2)}) collective-permute-start(bf16[256,256]{1,0:T(8,128)(2,1)S(1)} %get-tuple-element.22), channel_id=1, source_target_pairs={{0,8},{4,12},{8,0},{12,4},{16,24},{20,28},{24,16},{28,20},{32,56},... | collective-permute-start | bytes 393224 | tf_op jit(solution)/shard_map/ppermute | solution.py:263
  99.2 24.0 %collective-permute-start.9 = (bf16[256,768]{1,0:T(8,128)(2,1)}, bf16[256,768]{1,0:T(8,128)(2,1)S(1)}, u32[]{:S(2)}, u32[]{:S(2)}) collective-permute-start(bf16[256,768]{1,0:T(8,128)(2,1)} %slice.26), channel_id=1, source_target_pairs={{4,0},{8,4},{12,8},{0,12},{5,1},{9,5},{13,9},{1,13},{6,2},{10,6},{... | collective-permute-start | bytes 1179656 | tf_op jit(solution)/shard_map/ppermute | solution.py:194
  104.9 19.1 %collective-permute-start.10 = (bf16[256,768]{1,0:T(8,128)(2,1)}, bf16[256,768]{1,0:T(8,128)(2,1)S(1)}, u32[]{:S(2)}, u32[]{:S(2)}) collective-permute-start(bf16[256,768]{1,0:T(8,128)(2,1)} %slice.27), channel_id=1, source_target_pairs={{12,0},{0,4},{4,8},{8,12},{13,1},{1,5},{5,9},{9,13},{14,2},{2,6},{... | collective-permute-start | bytes 1179656 | tf_op jit(solution)/shard_map/ppermute | solution.py:194
  104.9 17.2 %collective-permute-start.13 = (bf16[256,256]{1,0:T(8,128)(2,1)S(1)}, bf16[256,256]{1,0:T(8,128)(2,1)}, u32[]{:S(2)}, u32[]{:S(2)}) collective-permute-start(bf16[256,256]{1,0:T(8,128)(2,1)S(1)} %get-tuple-element.21), channel_id=1, source_target_pairs={{0,4},{4,8},{8,12},{12,0},{16,20},{20,24},{24,28},{28,16},{32,52},... | collective-permute-start | bytes 393224 | tf_op jit(solution)/shard_map/ppermute | solution.py:263
  105.5 16.5 %collective-permute-start.12 = (bf16[256,256]{1,0:T(8,128)(2,1)S(1)}, bf16[256,256]{1,0:T(8,128)(2,1)}, u32[]{:S(2)}, u32[]{:S(2)}) collective-permute-start(bf16[256,256]{1,0:T(8,128)(2,1)S(1)} %get-tuple-element.20), channel_id=1, source_target_pairs={{0,0},{4,4},{8,8},{12,12},{16,16},{20,20},{24,24},{28,28},{32,48},... | collective-permute-start | bytes 393224 | tf_op jit(solution)/shard_map/ppermute | solution.py:263
  106.8 19.9 %copy-start.2 = (bf16[512,2304]{1,0:T(8,128)(2,1)S(1)}, bf16[512,2304]{1,0:T(8,128)(2,1)}, u32[]{:S(2)}) copy-start(bf16[512,2304]{1,0:T(8,128)(2,1)} %copy-done) | copy-start | bytes 7077892
  108.9 14.3 %collective-permute-start.11 = (bf16[256,512]{1,0:T(8,128)(2,1)S(1)}, bf16[256,512]{1,0:T(8,128)(2,1)S(1)}, u32[]{:S(2)}, u32[]{:S(2)}) collective-permute-start(bf16[256,512]{1,0:T(8,128)(2,1)S(1)} %get-tuple-element.32), channel_id=1, source_target_pairs={{0,16},{16,0},{32,112},{48,96},{64,80},{80,64},{96,48},{112,32},{1... | collective-permute-start | bytes 786440 | tf_op jit(solution)/shard_map/ppermute | solution.py:222
  135.9 40.7 %all-to-all-start.2 = ((bf16[16,64,768]{2,1,0:T(8,128)(2,1)}), bf16[16,64,768]{2,1,0:T(8,128)(2,1)}, u32[]{:S(2)}, u32[]{:S(2)}) async-start(bf16[16,64,768]{2,1,0:T(8,128)(2,1)} %bitcast.37), calls=%async_computation.2 | async-start | bytes 3145728 | tf_op jit(solution)/shard_map/all_to_all | solution.py:232
  142.9 16.0 %collective-permute-start.16 = (bf16[512,512]{1,0:T(8,128)(2,1)S(1)}, bf16[512,512]{1,0:T(8,128)(2,1)S(1)}, u32[]{:S(2)}, u32[]{:S(2)}) collective-permute-start(bf16[512,512]{1,0:T(8,128)(2,1)S(1)} %join.5.refs_5_.refs_0_), channel_id=1, source_target_pairs={{4,0},{8,4},{12,8},{0,12},{5,1},{9,5},{13,9},{1,13},{6,2},{10,6},{... | collective-permute-start | bytes 1572872 | tf_op jit(solution)/shard_map/ppermute | solution.py:194
  147.3 15.1 %collective-permute-start.17 = (bf16[512,512]{1,0:T(8,128)(2,1)S(1)}, bf16[512,512]{1,0:T(8,128)(2,1)S(1)}, u32[]{:S(2)}, u32[]{:S(2)}) collective-permute-start(bf16[512,512]{1,0:T(8,128)(2,1)S(1)} %join.5.refs_5_.refs_0_), channel_id=1, source_target_pairs={{12,0},{0,4},{4,8},{8,12},{13,1},{1,5},{5,9},{9,13},{14,2},{2,6},{... | collective-permute-start | bytes 1572872 | tf_op jit(solution)/shard_map/ppermute | solution.py:194
  147.3 17.3 %collective-permute-start.20 = (f32[256,256]{1,0:T(8,128)S(1)}, f32[256,256]{1,0:T(8,128)S(1)}, u32[]{:S(2)}, u32[]{:S(2)}) collective-permute-start(f32[256,256]{1,0:T(8,128)S(1)} %convert_add_fusion.refs_6_), channel_id=1, source_target_pairs={{0,32},{32,0},{1,33},{33,1},{2,34},{34,2},{3,35},{35,3},{4,36},{36... | collective-permute-start | bytes 786440 | tf_op jit(solution)/shard_map/ppermute | solution.py:190
  162.3 7.6 %collective-permute-start.18 = (bf16[256,512]{1,0:T(8,128)(2,1)S(1)}, bf16[256,512]{1,0:T(8,128)(2,1)S(1)}, u32[]{:S(2)}, u32[]{:S(2)}) collective-permute-start(bf16[256,512]{1,0:T(8,128)(2,1)S(1)} %slice.28), channel_id=1, source_target_pairs={{4,0},{8,4},{12,8},{0,12},{5,1},{9,5},{13,9},{1,13},{6,2},{10,6},{... | collective-permute-start | bytes 786440 | tf_op jit(solution)/shard_map/ppermute | solution.py:194
  162.7 8.8 %collective-permute-start.19 = (bf16[256,512]{1,0:T(8,128)(2,1)S(1)}, bf16[256,512]{1,0:T(8,128)(2,1)S(1)}, u32[]{:S(2)}, u32[]{:S(2)}) collective-permute-start(bf16[256,512]{1,0:T(8,128)(2,1)S(1)} %slice.29), channel_id=1, source_target_pairs={{12,0},{0,4},{4,8},{8,12},{13,1},{1,5},{5,9},{9,13},{14,2},{2,6},{... | collective-permute-start | bytes 786440 | tf_op jit(solution)/shard_map/ppermute | solution.py:194
  171.5 1.7 copy-start.3
  176.5 27.6 %all-to-all-start.3 = ((bf16[16,64,512]{2,1,0:T(8,128)(2,1)}), bf16[16,64,512]{2,1,0:T(8,128)(2,1)S(1)}, u32[]{:S(2)}, u32[]{:S(2)}) async-start(bf16[16,64,512]{2,1,0:T(8,128)(2,1)} %bitcast.9), calls=%async_computation.3 | async-start | bytes 2097152 | tf_op jit(solution)/shard_map/all_to_all | solution.py:232
  183.4 18.6 %collective-permute-start.21 = (f32[128,256]{1,0:T(8,128)S(1)}, f32[128,256]{1,0:T(8,128)S(1)}, u32[]{:S(2)}, u32[]{:S(2)}) collective-permute-start(f32[128,256]{1,0:T(8,128)S(1)} %constant_dynamic-slice_fusion), channel_id=1, source_target_pairs={{0,64},{64,0},{1,65},{65,1},{2,66},{66,2},{3,67},{67,3},{4,68},{68... | collective-permute-start | bytes 393224 | tf_op jit(solution)/shard_map/ppermute | solution.py:190
  202.0 1.3 collective-permute-start.22
  (18 other events, 18.7 us)

commit v5 on v1

--- a/solution.py
+++ b/solution.py
@@ -13,11 +13,15 @@
 BF16 = jnp.bfloat16
 
 
+WHOLE = pl.BlockSpec(memory_space=pltpu.VMEM)
+SCALAR = pl.BlockSpec(memory_space=pltpu.SMEM)
+
+
 def params():
-    return pltpu.CompilerParams(vmem_limit_bytes=40 << 20)
-
-
-def pack_kernel(z_ref, float_ref, quant_ref, out_ref, block_ref):
+    return pltpu.CompilerParams(vmem_limit_bytes=16 << 20)
+
+
+def pack_kernel(z_ref, float_ref, quant_ref, out_ref):
     width = out_ref.shape[2] // 8
     z = z_ref[0]
     for kind, ref in enumerate((float_ref, quant_ref)):
@@ -30,24 +34,15 @@
                     for half in range(2):
                         at = (j * 2 + (yl ^ half)) * width
                         out_ref[kind * 8 + half * 4 + x, :, at : at + width] = block
-    quant = quant_ref[:, :BLOCK]
-    shift = (float_ref[:, :BLOCK].astype(F32) - quant.astype(F32)).astype(BF16)
-    for d in range(16):
-        block_ref[d, :, :BLOCK] = quant
-        block_ref[d, :, BLOCK:] = shift
 
 
 def pack(z, attn_float, attn_quant):
     tokens, d_in = attn_float.shape
-    whole = pl.BlockSpec(memory_space=pltpu.VMEM)
     return pl.pallas_call(
         pack_kernel,
-        out_shape=(
-            jax.ShapeDtypeStruct((16, tokens, d_in // 4), BF16),
-            jax.ShapeDtypeStruct((16, tokens, 2 * BLOCK), BF16),
-        ),
-        in_specs=[pl.BlockSpec(memory_space=pltpu.SMEM), whole, whole],
-        out_specs=(whole, whole),
+        out_shape=jax.ShapeDtypeStruct((16, tokens, d_in // 4), BF16),
+        in_specs=[SCALAR, WHOLE, WHOLE],
+        out_specs=WHOLE,
         compiler_params=params(),
         name="pack",
     )(z.reshape(1), attn_float, attn_quant)
@@ -70,19 +65,56 @@
 
 def finish(core, first, second):
     _, tokens, width = first.shape
-    whole = pl.BlockSpec(memory_space=pltpu.VMEM)
     return pl.pallas_call(
         finish_kernel,
         out_shape=(jax.ShapeDtypeStruct((tokens, 4 * width), BF16),) * 2,
-        in_specs=[pl.BlockSpec(memory_space=pltpu.SMEM), whole, whole],
-        out_specs=(whole, whole),
+        in_specs=[SCALAR, WHOLE, WHOLE],
+        out_specs=(WHOLE, WHOLE),
         compiler_params=params(),
         name="finish",
     )(core.reshape(1), first, second)
 
 
+def stats_kernel(at_ref, acts_ref, *refs):
+    pieces, outs, block_ref = refs[:4], refs[4:8], refs[8]
+    y, x = at_ref[0], at_ref[1]
+    tokens = pieces[0].shape[0] // 4
+    for dy, piece in enumerate(pieces):
+        for dx in range(4):
+            start = (lax.rem(y + dy, 4) * 4 + lax.rem(x + dx, 4)) * tokens
+            block_ref[pl.ds(pl.multiple_of(start, tokens), tokens)] = piece[
+                dx * tokens : (dx + 1) * tokens
+            ]
+    width = outs[0].shape[0]
+    for j, out in enumerate(outs):
+        out[...] = lax.dot_general(
+            acts_ref[:, 2 * j * width : (2 * j + 1) * width],
+            block_ref[...],
+            (((0,), (0,)), ((), ())),
+            preferred_element_type=F32,
+        ).astype(out.dtype)
+
+
+def stats(at, acts, pieces):
+    width = 2 * BLOCK
+    return pl.pallas_call(
+        stats_kernel,
+        out_shape=(jax.ShapeDtypeStruct((width, width), F32),)
+        + (jax.ShapeDtypeStruct((width, width), BF16),) * 3,
+        in_specs=[SCALAR] + [WHOLE] * 5,
+        out_specs=(WHOLE,) * 4,
+        scratch_shapes=[pltpu.VMEM((acts.shape[0], width), BF16)],
+        compiler_params=params(),
+        name="stats",
+    )(at, acts, *pieces)
+
+
 def swap(a, axis):
     return lax.ppermute(a, axis, [(0, 1), (1, 0)])
+
+
+def ahead(a, axis, j):
+    return lax.ppermute(a, axis, [((i + j) % 4, i) for i in range(4)])
 
 
 def shards(attn_float, attn_quant, proj_weight, weight_codes, group_scales):
@@ -110,38 +142,49 @@
                 pairs.append((a * 4 + c * 2 + b, (a ^ c) * 4 + c * 2 + (1 - b)))
     got = lax.ppermute(send, ("yh", "core", "yl"), pairs)
 
-    payload, block_part = pack(z, attn_float, attn_quant)
-    block_all = lax.all_to_all(block_part, PLANE, 0, 0, tiled=True)
-    block_all = block_all.reshape(16 * tokens, 2 * BLOCK)
-
+    payload = pack(z, attn_float, attn_quant)
     rows = jnp.concatenate([own, got], axis=0)
-    parts = [rows] + [
-        lax.ppermute(rows, "z", [((i + j) % 4, i) for i in range(4)]) for j in (1, 2, 3)
-    ]
+    parts = [rows] + [ahead(rows, "z", j) for j in (1, 2, 3)]
     mine = jnp.concatenate(parts, axis=0)
     other = swap(mine, "core")
 
+    quant = attn_quant[:, :BLOCK]
+    shift = (attn_float[:, :BLOCK].astype(F32) - quant.astype(F32)).astype(BF16)
+    block = jnp.concatenate([quant, shift], axis=1)
+    block, payload = lax.optimization_barrier((block, payload))
     acts = lax.all_to_all(payload, PLANE, 0, 0, tiled=True).reshape(16 * tokens, 8 * features)
 
+    line = jnp.concatenate([block] + [ahead(block, "x", j) for j in (1, 2, 3)], axis=0)
+    pieces = [line] + [ahead(line, ("yh", "yl"), j) for j in (1, 2, 3)]
+    acts, mine, *pieces = lax.optimization_barrier((acts, mine, *pieces))
+
     def part(w):
-        p = jnp.dot(acts, w, preferred_element_type=F32).astype(BF16)
+        return jnp.dot(acts, w, preferred_element_type=F32).astype(BF16)
+
+    def output(p):
         return lax.all_to_all(p.reshape(16, tokens, quarter), PLANE, 0, 0, tiled=True)
 
-    float_out, quant_out = finish(core, part(mine), part(other))
-
-    def stats(j):
-        picked = acts[:, 2 * j * features : (2 * j + 1) * features]
-        return lax.dot_general(
-            picked, block_all, (((0,), (0,)), ((), ())), preferred_element_type=F32
-        )
-
-    total = stats(0)
+    first = part(mine)
+    result1 = output(first)
+
+    acts1, first = lax.optimization_barrier((acts, first))
+    blocks = stats(jnp.stack([yh * 2 + yl, lax.axis_index("x")]), acts1, pieces)
+    total = blocks[0]
     for j in (1, 2, 3):
-        total = total + lax.ppermute(
-            stats(j).astype(BF16), "z", [(i, (i + j) % 4) for i in range(4)]
-        ).astype(F32)
-    total = jnp.where(yh == 1, total, swap(total, "yh"))
+        total = total + ahead(blocks[j], "z", 4 - j).astype(F32)
+    other, total = lax.optimization_barrier((other, total))
+    second = part(other)
     total = (total + swap(total, "core")) * inverse
+    second, total = lax.optimization_barrier((second, total))
+    result2 = output(second)
+
+    piece = swap(lax.dynamic_slice_in_dim(total, core * BLOCK, BLOCK, 0), "yh")
+    again = swap(piece, "core")
+    moved = jnp.where(
+        core == 0, jnp.concatenate([piece, again]), jnp.concatenate([again, piece])
+    )
+    total = jnp.where(yh == 1, total, moved)
+    float_out, quant_out = finish(core, result1, result2)
     return float_out, quant_out, total[:, :BLOCK], total[:, BLOCK:]
 
 

time: 167 us -> 184 us (1.10)
  waiting for transfers between devices: 85.2 us -> 105 us
  matrix products: 24.2 us -> 18.7 us
  Pallas kernels: 4.2 us -> 6.29 us
    ppermute x6 -> x12, waiting for transfers between devices: 46.1 us -> 63 us  [ahead(): return lax.ppermute(a, axis, [((i + j) % 4, i) for i in range(4)])]
    ppermute x3 -> x4, waiting for transfers between devices: 13.3 us -> 24.3 us  [swap(): return lax.ppermute(a, axis, [(0, 1), (1, 0)])]
    all_to_all x1, waiting for transfers between devices: 8.25 us -> 0.01 us  [shards(): lax.all_to_all(payload, PLANE, 0, 0, tiled=True)]
    ppermute x1, waiting for transfers between devices: 0.01 us -> 7.5 us  [shards(): got = lax.ppermute(send, ('yh', 'core', 'yl'), pairs)]
    all_to_all x3 -> x2, waiting for transfers between devices: 17.6 us -> 10.1 us  [output(): lax.all_to_all(p.reshape(16, tokens, quarter), PLANE, 0, 0, tiled=True)]
    all_to_all x3 -> x2, starting transfers between devices: 15.2 us -> 8.16 us  [output(): lax.all_to_all(p.reshape(16, tokens, quarter), PLANE, 0, 0, tiled=True)]
    ppermute x6 -> x12, starting transfers between devices: 11.9 us -> 17.9 us  [ahead(): return lax.ppermute(a, axis, [((i + j) % 4, i) for i in range(4)])]
    dot_general x6 -> x2, matrix products: 24.2 us -> 18.7 us  [part(): return jnp.dot(acts, w, preferred_element_type=F32).astype(BF16)]
  transfers between devices with their start and end apart: 14 -> 20, of which waited for: 10 -> 15; matrix products, arithmetic and copies ran while one was open for 18% -> 14% of each run, Pallas kernels for 1% -> 2%
where the time goes in v5:
time: 184 us; the launch traced here: 183 us
  waiting for transfers between devices  105 us (57%)
  starting transfers between devices  38.5 us (21%)
  matrix products  18.7 us (10%)
  local copies, waits for them, and re-layouts  9.72 us (5%)
  Pallas kernels  6.29 us (3%)
  other arithmetic  3.58 us (2%)
    ppermute x12, waiting for transfers between devices, ahead(): return lax.ppermute(a, axis, [((i + j) % 4, i) for i in range(4)])  63 us
    ppermute x4, waiting for transfers between devices, swap(): return lax.ppermute(a, axis, [(0, 1), (1, 0)])  24.3 us
    dot_general x2, matrix products, part(): return jnp.dot(acts, w, preferred_element_type=F32).astype(BF16)  18.7 us
    ppermute x12, starting transfers between devices, ahead(): return lax.ppermute(a, axis, [((i + j) % 4, i) for i in range(4)])  17.9 us
    all_to_all x2, waiting for transfers between devices, output(): lax.all_to_all(p.reshape(16, tokens, quarter), PLANE, 0, 0, tiled=True)  10.1 us
    all_to_all x2, starting transfers between devices, output(): lax.all_to_all(p.reshape(16, tokens, quarter), PLANE, 0, 0, tiled=True)  8.16 us
    ppermute x1, waiting for transfers between devices, shards(): got = lax.ppermute(send, ('yh', 'core', 'yl'), pairs)  7.5 us
    all_to_all x1, starting transfers between devices, shards(): lax.all_to_all(payload, PLANE, 0, 0, tiled=True)  7.09 us
  transfers between devices with their start and end apart: 20, of which 15 were waited for; matrix products, arithmetic and copies ran while one was open for 14% of the time, Pallas kernels for 2%

profile of v5, /device:TPU:0, one launch (start us, length us, event | category | flops | bytes accessed | tf_op | source)
XLA Modules:
  0.0 182.5 jit_solution(16366752922371462365)
XLA Ops:
  1.5 2.3 %fusion.3 = (bf16[256,1024]{1,0:T(8,128)(2,1)S(1)}, bf16[256,1024]{1,0:T(8,128)(2,1)S(1)}) fusion(s32[256,4096]{1,0:T(8,128)} %param.8, s32[]{:T(128)S(6)} %select_n.45, f32[2,1024]{1,0:T(2,128)S(1)} %get-tuple-element.46, bf16[256,4096]{1,0:T(8,128)(2,1)} %param.7, pred[]{:T(512)S(6)} %eq.13, f32[2,1024]{1,0:T(2,128)S(1)} %get-tuple-element.47, ...), kind=kLoop, calls=%fused_computation.8 | loop fusion | flops 2621440 | bytes 4210698 | tf_op jit(solution)/shard_map/jit(_where)/select_n | solution.py:134
  3.8 1.7 collective-permute-start
  5.6 7.5 %collective-permute-done = bf16[256,1024]{1,0:T(8,128)(2,1)S(1)} collective-permute-done((bf16[256,1024]{1,0:T(8,128)(2,1)S(1)}, bf16[256,1024]{1,0:T(8,128)(2,1)S(1)}, u32[]{:S(2)}, u32[]{:S(2)}) %collective-permute-start) | collective-permute-done | bytes 524320 | tf_op jit(solution)/shard_map/ppermute | solution.py:143
  13.1 1.1 pad_maximum_fusion
  14.2 4.1 %collective-permute-start.1 = (bf16[512,1024]{1,0:T(8,128)(2,1)}, bf16[512,1024]{1,0:T(8,128)(2,1)}, u32[]{:S(2)}, u32[]{:S(2)}) collective-permute-start(bf16[512,1024]{1,0:T(8,128)(2,1)} %pad_maximum_fusion), channel_id=1, source_target_pairs={{4,0},{8,4},{12,8},{0,12},{5,1},{9,5},{13,9},{1,13},{6,2},{10,6},{... | collective-permute-start | bytes 3145736 | tf_op jit(solution)/shard_map/ppermute | solution.py:117
  18.6 2.0 %copy-done = bf16[16,64,2048]{2,1,0:T(8,128)(2,1)} copy-done((bf16[16,64,2048]{2,1,0:T(8,128)(2,1)}, bf16[16,64,2048]{2,1,0:T(8,128)(2,1)S(1)}, u32[]{:S(2)}) %copy-start) | copy-done | bytes 4194328
  20.6 7.1 %all-to-all-start = ((bf16[16,64,2048]{2,1,0:T(8,128)(2,1)}), bf16[16,64,2048]{2,1,0:T(8,128)(2,1)}, u32[]{:S(2)}, u32[]{:S(2)}) async-start(bf16[16,64,2048]{2,1,0:T(8,128)(2,1)} %copy-done), calls=%async_computation | async-start | bytes 8388608 | tf_op jit(solution)/shard_map/all_to_all | solution.py:155
  27.8 1.2 collective-permute-start.3
  30.7 32.9 %collective-permute-done.1 = bf16[512,1024]{1,0:T(8,128)(2,1)} collective-permute-done((bf16[512,1024]{1,0:T(8,128)(2,1)}, bf16[512,1024]{1,0:T(8,128)(2,1)}, u32[]{:S(2)}, u32[]{:S(2)}) %collective-permute-start.1) | collective-permute-done | bytes 1048608 | tf_op jit(solution)/shard_map/ppermute | solution.py:117
  63.6 2.3 %constant_dynamic-update-slice_fusion.2 = bf16[2048,1024]{1,0:T(8,128)(2,1)} fusion(bf16[2048,1024]{1,0:T(8,128)(2,1)} %constant_dynamic-update-slice_fusion.3, bf16[512,1024]{1,0:T(8,128)(2,1)} %collective-permute-done.1), kind=kLoop, calls=%fused_computation.17 | loop fusion | bytes 2097152
  67.0 9.0 %collective-permute-done.3 = bf16[512,1024]{1,0:T(8,128)(2,1)S(1)} collective-permute-done((bf16[512,1024]{1,0:T(8,128)(2,1)}, bf16[512,1024]{1,0:T(8,128)(2,1)S(1)}, u32[]{:S(2)}, u32[]{:S(2)}) %collective-permute-start.3) | collective-permute-done | bytes 1048608 | tf_op jit(solution)/shard_map/ppermute | solution.py:117
  77.0 2.7 %collective-permute-start.4 = (bf16[64,256]{1,0:T(8,128)(2,1)S(1)}, bf16[64,256]{1,0:T(8,128)(2,1)S(1)}, u32[]{:S(2)}, u32[]{:S(2)}) collective-permute-start(bf16[64,256]{1,0:T(8,128)(2,1)S(1)} %pad_maximum_fusion.1), channel_id=1, source_target_pairs={{1,0},{2,1},{3,2},{0,3},{5,4},{6,5},{7,6},{4,7},{9,8},{10,9},{11,1... | collective-permute-start | bytes 98312 | tf_op jit(solution)/shard_map/ppermute | solution.py:117
  81.5 7.6 %collective-permute-done.4 = bf16[64,256]{1,0:T(8,128)(2,1)S(1)} collective-permute-done((bf16[64,256]{1,0:T(8,128)(2,1)S(1)}, bf16[64,256]{1,0:T(8,128)(2,1)S(1)}, u32[]{:S(2)}, u32[]{:S(2)}) %collective-permute-start.4) | collective-permute-done | bytes 32800 | tf_op jit(solution)/shard_map/ppermute | solution.py:117
  89.6 1.9 %collective-permute-start.7 = (bf16[256,256]{1,0:T(8,128)(2,1)S(1)}, bf16[256,256]{1,0:T(8,128)(2,1)S(1)}, u32[]{:S(2)}, u32[]{:S(2)}) collective-permute-start(bf16[256,256]{1,0:T(8,128)(2,1)S(1)} %constant_dynamic-update-slice_fusion.5.refs_0_), channel_id=1, source_target_pairs={{16,0},{64,16},{80,64},{0,80},{17,1},{65,17},{81,65},{1,81},{18,2}... | collective-permute-start | bytes 393224 | tf_op jit(solution)/shard_map/ppermute | solution.py:117
  91.5 1.4 collective-permute-start.8
  93.0 1.3 collective-permute-start.9
  94.3 3.2 %collective-permute-done.7.refs_1_ = bf16[256,256]{1,0:T(8,128)(2,1)S(1)} collective-permute-done((bf16[256,256]{1,0:T(8,128)(2,1)S(1)}, bf16[256,256]{1,0:T(8,128)(2,1)S(1)}, u32[]{:S(2)}, u32[]{:S(2)}) %collective-permute-start.7) | collective-permute-done | bytes 131104 | tf_op jit(solution)/shard_map/ppermute | solution.py:117
  97.4 2.0 %collective-permute-done.8.refs_2_ = bf16[256,256]{1,0:T(8,128)(2,1)S(1)} collective-permute-done((bf16[256,256]{1,0:T(8,128)(2,1)S(1)}, bf16[256,256]{1,0:T(8,128)(2,1)S(1)}, u32[]{:S(2)}, u32[]{:S(2)}) %collective-permute-start.8) | collective-permute-done | bytes 131104 | tf_op jit(solution)/shard_map/ppermute | solution.py:117
  99.4 1.5 collective-permute-done.9.refs_3_
  100.9 9.3 %convolution_convert_fusion.1 = bf16[1024,1024]{1,0:T(8,128)(2,1)} fusion(bf16[1024,2048]{1,0:T(8,128)(2,1)} %bitcast.2.acts_ref, bf16[2048,1024]{1,0:T(8,128)(2,1)} %constant_dynamic-update-slice_fusion), kind=kOutput, calls=%fused_computation.1 | convolution fusion | flops 4296015872 | bytes 10485760 | tf_op jit(solution)/shard_map/dot_general | solution.py:162
  110.2 3.7 %all-to-all-start.1 = ((bf16[16,64,1024]{2,1,0:T(8,128)(2,1)}), bf16[16,64,1024]{2,1,0:T(8,128)(2,1)S(1)}, u32[]{:S(2)}, u32[]{:S(2)}) async-start(bf16[16,64,1024]{2,1,0:T(8,128)(2,1)} %bitcast.23), calls=%async_computation.1 | async-start | bytes 4194304 | tf_op jit(solution)/shard_map/all_to_all | solution.py:165
  114.0 3.0 %stats.1 = (f32[256,256]{1,0:T(8,128)S(1)}, bf16[256,256]{1,0:T(8,128)(2,1)S(1)}, bf16[256,256]{1,0:T(8,128)(2,1)S(1)}, bf16[256,256]{1,0:T(8,128)(2,1)S(1)}) custom-call(s32[2]{0:T(128)S(1)} %pad_add_fusion.at_ref, bf16[1024,2048]{1,0:T(8,128)(2,1)} %bitcast.2.acts_ref, bf16[256,256]{1,0:T(8,128)(2,1)S(1)} %constant_dynamic-update-slice_fusion.5.refs_0_, ...), custom_call_target="tpu_custom_call" | custom-call | tf_op jit(solution)/shard_map/stats/pallas_call | solution.py:100
  117.1 2.0 %collective-permute-start.12 = (bf16[256,256]{1,0:T(8,128)(2,1)S(1)}, bf16[256,256]{1,0:T(8,128)(2,1)S(1)}, u32[]{:S(2)}, u32[]{:S(2)}) collective-permute-start(bf16[256,256]{1,0:T(8,128)(2,1)S(1)} %get-tuple-element.34), channel_id=1, source_target_pairs={{8,0},{12,4},{0,8},{4,12},{9,1},{13,5},{1,9},{5,13},{10,2},{14,6},... | collective-permute-start | bytes 393224 | tf_op jit(solution)/shard_map/ppermute | solution.py:117
  119.2 1.3 collective-permute-start.13
  120.4 5.7 %collective-permute-done.11 = bf16[256,256]{1,0:T(8,128)(2,1)S(1)} collective-permute-done((bf16[256,256]{1,0:T(8,128)(2,1)S(1)}, bf16[256,256]{1,0:T(8,128)(2,1)S(1)}, u32[]{:S(2)}, u32[]{:S(2)}) %collective-permute-start.11) | collective-permute-done | bytes 131104 | tf_op jit(solution)/shard_map/ppermute | solution.py:117
  127.1 9.3 %convolution_convert_fusion = bf16[1024,1024]{1,0:T(8,128)(2,1)} fusion(bf16[1024,2048]{1,0:T(8,128)(2,1)} %bitcast.2.acts_ref, bf16[2048,1024]{1,0:T(8,128)(2,1)} %collective-permute-done.10), kind=kOutput, calls=%fused_computation | convolution fusion | flops 4296015872 | bytes 10485760 | tf_op jit(solution)/shard_map/dot_general | solution.py:162
  136.5 9.2 %all-to-all-done.1.first_ref = bf16[16,64,1024]{2,1,0:T(8,128)(2,1)S(1)} async-done(((bf16[16,64,1024]{2,1,0:T(8,128)(2,1)}), bf16[16,64,1024]{2,1,0:T(8,128)(2,1)S(1)}, u32[]{:S(2)}, u32[]{:S(2)}) %all-to-all-start.1) | async-done | bytes 2097184 | tf_op jit(solution)/shard_map/all_to_all | solution.py:165
  145.6 4.4 %all-to-all-start.2 = ((bf16[16,64,1024]{2,1,0:T(8,128)(2,1)}), bf16[16,64,1024]{2,1,0:T(8,128)(2,1)}, u32[]{:S(2)}, u32[]{:S(2)}) async-start(bf16[16,64,1024]{2,1,0:T(8,128)(2,1)} %bitcast.24), calls=%async_computation.2 | async-start | bytes 4194304 | tf_op jit(solution)/shard_map/all_to_all | solution.py:165
  150.1 3.4 %collective-permute-start.15 = (f32[128,256]{1,0:T(8,128)S(1)}, f32[128,256]{1,0:T(8,128)S(1)}, u32[]{:S(2)}, u32[]{:S(2)}) collective-permute-start(f32[128,256]{1,0:T(8,128)S(1)} %constant_dynamic-slice_fusion), channel_id=1, source_target_pairs={{0,64},{64,0},{1,65},{65,1},{2,66},{66,2},{3,67},{67,3},{4,68},{68... | collective-permute-start | bytes 393224 | tf_op jit(solution)/shard_map/ppermute | solution.py:113
  153.5 23.0 %collective-permute-done.15 = f32[128,256]{1,0:T(8,128)S(1)} collective-permute-done((f32[128,256]{1,0:T(8,128)S(1)}, f32[128,256]{1,0:T(8,128)S(1)}, u32[]{:S(2)}, u32[]{:S(2)}) %collective-permute-start.15) | collective-permute-done | bytes 131104 | tf_op jit(solution)/shard_map/ppermute | solution.py:113
  176.4 1.3 collective-permute-done.16
  179.5 3.0 %finish.1 = (bf16[64,4096]{1,0:T(8,128)(2,1)}, bf16[64,4096]{1,0:T(8,128)(2,1)}) custom-call(s32[1]{0:T(128)} %bitcast.core_ref, bf16[16,64,1024]{2,1,0:T(8,128)(2,1)S(1)} %all-to-all-done.1.first_ref, bf16[16,64,1024]{2,1,0:T(8,128)(2,1)} %all-to-all-done.2.second_ref), custom_call_target="tpu_custom_call" | custom-call | tf_op jit(solution)/shard_map/finish/pallas_call | solution.py:68
  (41 shorter events, 10.2 us)
Async XLA Ops:
  0.6 4.9 %copy-start.1 = (bf16[64,8192]{1,0:T(8,128)(2,1)S(1)}, bf16[64,8192]{1,0:T(8,128)(2,1)}, u32[]{:S(2)}) copy-start(bf16[64,8192]{1,0:T(8,128)(2,1)} %quant_ref.1) | copy-start | bytes 3145732
  0.6 17.6 %slice-start = ((bf16[64,8192]{1,0:T(8,128)(2,1)}), bf16[64,128]{1,0:T(8,128)(2,1)S(1)}, s32[]{:S(2)}) async-start(bf16[64,8192]{1,0:T(8,128)(2,1)} %quant_ref.1), calls=%async_computation.3 | async-start | bytes 32768 | tf_op jit(solution)/shard_map/slice | solution.py:151
  0.7 4.9 %copy-start.2 = (bf16[64,8192]{1,0:T(8,128)(2,1)S(1)}, bf16[64,8192]{1,0:T(8,128)(2,1)}, u32[]{:S(2)}) copy-start(bf16[64,8192]{1,0:T(8,128)(2,1)} %float_ref.1) | copy-start | bytes 3145732
  3.8 9.3 %collective-permute-start = (bf16[256,1024]{1,0:T(8,128)(2,1)S(1)}, bf16[256,1024]{1,0:T(8,128)(2,1)S(1)}, u32[]{:S(2)}, u32[]{:S(2)}) collective-permute-start(bf16[256,1024]{1,0:T(8,128)(2,1)S(1)} %get-tuple-element.42), channel_id=1, source_target_pairs={{0,16},{16,0},{32,112},{48,96},{64,80},{80,64},{96,48},{112,32},{1... | collective-permute-start | bytes 1572872 | tf_op jit(solution)/shard_map/ppermute | solution.py:143
  14.2 49.4 %collective-permute-start.1 = (bf16[512,1024]{1,0:T(8,128)(2,1)}, bf16[512,1024]{1,0:T(8,128)(2,1)}, u32[]{:S(2)}, u32[]{:S(2)}) collective-permute-start(bf16[512,1024]{1,0:T(8,128)(2,1)} %pad_maximum_fusion), channel_id=1, source_target_pairs={{4,0},{8,4},{12,8},{0,12},{5,1},{9,5},{13,9},{1,13},{6,2},{10,6},{... | collective-permute-start | bytes 3145736 | tf_op jit(solution)/shard_map/ppermute | solution.py:117
  18.6 2.0 %copy-start = (bf16[16,64,2048]{2,1,0:T(8,128)(2,1)}, bf16[16,64,2048]{2,1,0:T(8,128)(2,1)S(1)}, u32[]{:S(2)}) copy-start(bf16[16,64,2048]{2,1,0:T(8,128)(2,1)S(1)} %pack.1) | copy-start | bytes 12582916
  20.6 80.3 %all-to-all-start = ((bf16[16,64,2048]{2,1,0:T(8,128)(2,1)}), bf16[16,64,2048]{2,1,0:T(8,128)(2,1)}, u32[]{:S(2)}, u32[]{:S(2)}) async-start(bf16[16,64,2048]{2,1,0:T(8,128)(2,1)} %copy-done), calls=%async_computation | async-start | bytes 8388608 | tf_op jit(solution)/shard_map/all_to_all | solution.py:155
  27.7 38.2 %collective-permute-start.2 = (bf16[512,1024]{1,0:T(8,128)(2,1)}, bf16[512,1024]{1,0:T(8,128)(2,1)S(1)}, u32[]{:S(2)}, u32[]{:S(2)}) collective-permute-start(bf16[512,1024]{1,0:T(8,128)(2,1)} %pad_maximum_fusion), channel_id=1, source_target_pairs={{8,0},{12,4},{0,8},{4,12},{9,1},{13,5},{1,9},{5,13},{10,2},{14,6},... | collective-permute-start | bytes 3145736 | tf_op jit(solution)/shard_map/ppermute | solution.py:117
  27.8 48.2 %collective-permute-start.3 = (bf16[512,1024]{1,0:T(8,128)(2,1)}, bf16[512,1024]{1,0:T(8,128)(2,1)S(1)}, u32[]{:S(2)}, u32[]{:S(2)}) collective-permute-start(bf16[512,1024]{1,0:T(8,128)(2,1)} %pad_maximum_fusion), channel_id=1, source_target_pairs={{12,0},{0,4},{4,8},{8,12},{13,1},{1,5},{5,9},{9,13},{14,2},{2,6},{... | collective-permute-start | bytes 3145736 | tf_op jit(solution)/shard_map/ppermute | solution.py:117
  77.0 49.8 %collective-permute-start.10 = (bf16[2048,1024]{1,0:T(8,128)(2,1)}, bf16[2048,1024]{1,0:T(8,128)(2,1)}, u32[]{:S(2)}, u32[]{:S(2)}) collective-permute-start(bf16[2048,1024]{1,0:T(8,128)(2,1)} %constant_dynamic-update-slice_fusion), channel_id=1, source_target_pairs={{0,32},{32,0},{1,33},{33,1},{2,34},{34,2},{3,35},{35,3},{4,36},{36... | collective-permute-start | bytes 12582920 | tf_op jit(solution)/shard_map/ppermute | solution.py:113
  77.0 12.1 %collective-permute-start.4 = (bf16[64,256]{1,0:T(8,128)(2,1)S(1)}, bf16[64,256]{1,0:T(8,128)(2,1)S(1)}, u32[]{:S(2)}, u32[]{:S(2)}) collective-permute-start(bf16[64,256]{1,0:T(8,128)(2,1)S(1)} %pad_maximum_fusion.1), channel_id=1, source_target_pairs={{1,0},{2,1},{3,2},{0,3},{5,4},{6,5},{7,6},{4,7},{9,8},{10,9},{11,1... | collective-permute-start | bytes 98312 | tf_op jit(solution)/shard_map/ppermute | solution.py:117
  79.8 9.7 %collective-permute-start.5 = (bf16[64,256]{1,0:T(8,128)(2,1)S(1)}, bf16[64,256]{1,0:T(8,128)(2,1)S(1)}, u32[]{:S(2)}, u32[]{:S(2)}) collective-permute-start(bf16[64,256]{1,0:T(8,128)(2,1)S(1)} %pad_maximum_fusion.1), channel_id=1, source_target_pairs={{2,0},{3,1},{0,2},{1,3},{6,4},{7,5},{4,6},{5,7},{10,8},{11,9},{8,1... | collective-permute-start | bytes 98312 | tf_op jit(solution)/shard_map/ppermute | solution.py:117
  80.6 9.0 %collective-permute-start.6 = (bf16[64,256]{1,0:T(8,128)(2,1)S(1)}, bf16[64,256]{1,0:T(8,128)(2,1)S(1)}, u32[]{:S(2)}, u32[]{:S(2)}) collective-permute-start(bf16[64,256]{1,0:T(8,128)(2,1)S(1)} %pad_maximum_fusion.1), channel_id=1, source_target_pairs={{3,0},{0,1},{1,2},{2,3},{7,4},{4,5},{5,6},{6,7},{11,8},{8,9},{9,10... | collective-permute-start | bytes 98312 | tf_op jit(solution)/shard_map/ppermute | solution.py:117
  89.6 7.8 %collective-permute-start.7 = (bf16[256,256]{1,0:T(8,128)(2,1)S(1)}, bf16[256,256]{1,0:T(8,128)(2,1)S(1)}, u32[]{:S(2)}, u32[]{:S(2)}) collective-permute-start(bf16[256,256]{1,0:T(8,128)(2,1)S(1)} %constant_dynamic-update-slice_fusion.5.refs_0_), channel_id=1, source_target_pairs={{16,0},{64,16},{80,64},{0,80},{17,1},{65,17},{81,65},{1,81},{18,2}... | collective-permute-start | bytes 393224 | tf_op jit(solution)/shard_map/ppermute | solution.py:117
  91.5 7.9 %collective-permute-start.8 = (bf16[256,256]{1,0:T(8,128)(2,1)S(1)}, bf16[256,256]{1,0:T(8,128)(2,1)S(1)}, u32[]{:S(2)}, u32[]{:S(2)}) collective-permute-start(bf16[256,256]{1,0:T(8,128)(2,1)S(1)} %constant_dynamic-update-slice_fusion.5.refs_0_), channel_id=1, source_target_pairs={{64,0},{80,16},{0,64},{16,80},{65,1},{81,17},{1,65},{17,81},{66,2}... | collective-permute-start | bytes 393224 | tf_op jit(solution)/shard_map/ppermute | solution.py:117
  93.0 8.0 %collective-permute-start.9 = (bf16[256,256]{1,0:T(8,128)(2,1)S(1)}, bf16[256,256]{1,0:T(8,128)(2,1)S(1)}, u32[]{:S(2)}, u32[]{:S(2)}) collective-permute-start(bf16[256,256]{1,0:T(8,128)(2,1)S(1)} %constant_dynamic-update-slice_fusion.5.refs_0_), channel_id=1, source_target_pairs={{80,0},{0,16},{16,64},{64,80},{81,1},{1,17},{17,65},{65,81},{82,2}... | collective-permute-start | bytes 393224 | tf_op jit(solution)/shard_map/ppermute | solution.py:117
  110.2 35.4 %all-to-all-start.1 = ((bf16[16,64,1024]{2,1,0:T(8,128)(2,1)}), bf16[16,64,1024]{2,1,0:T(8,128)(2,1)S(1)}, u32[]{:S(2)}, u32[]{:S(2)}) async-start(bf16[16,64,1024]{2,1,0:T(8,128)(2,1)} %bitcast.23), calls=%async_computation.1 | async-start | bytes 4194304 | tf_op jit(solution)/shard_map/all_to_all | solution.py:165
  117.0 9.1 %collective-permute-start.11 = (bf16[256,256]{1,0:T(8,128)(2,1)S(1)}, bf16[256,256]{1,0:T(8,128)(2,1)S(1)}, u32[]{:S(2)}, u32[]{:S(2)}) collective-permute-start(bf16[256,256]{1,0:T(8,128)(2,1)S(1)} %get-tuple-element.33), channel_id=1, source_target_pairs={{12,0},{0,4},{4,8},{8,12},{13,1},{1,5},{5,9},{9,13},{14,2},{2,6},{... | collective-permute-start | bytes 393224 | tf_op jit(solution)/shard_map/ppermute | solution.py:117
  117.1 9.0 %collective-permute-start.12 = (bf16[256,256]{1,0:T(8,128)(2,1)S(1)}, bf16[256,256]{1,0:T(8,128)(2,1)S(1)}, u32[]{:S(2)}, u32[]{:S(2)}) collective-permute-start(bf16[256,256]{1,0:T(8,128)(2,1)S(1)} %get-tuple-element.34), channel_id=1, source_target_pairs={{8,0},{12,4},{0,8},{4,12},{9,1},{13,5},{1,9},{5,13},{10,2},{14,6},... | collective-permute-start | bytes 393224 | tf_op jit(solution)/shard_map/ppermute | solution.py:117
  119.2 7.6 %collective-permute-start.13 = (bf16[256,256]{1,0:T(8,128)(2,1)S(1)}, bf16[256,256]{1,0:T(8,128)(2,1)S(1)}, u32[]{:S(2)}, u32[]{:S(2)}) collective-permute-start(bf16[256,256]{1,0:T(8,128)(2,1)S(1)} %get-tuple-element.35), channel_id=1, source_target_pairs={{4,0},{8,4},{12,8},{0,12},{5,1},{9,5},{13,9},{1,13},{6,2},{10,6},{... | collective-permute-start | bytes 393224 | tf_op jit(solution)/shard_map/ppermute | solution.py:117
  126.8 9.6 %collective-permute-start.14 = (f32[256,256]{1,0:T(8,128)S(1)}, f32[256,256]{1,0:T(8,128)S(1)}, u32[]{:S(2)}, u32[]{:S(2)}) collective-permute-start(f32[256,256]{1,0:T(8,128)S(1)} %convert_add_fusion), channel_id=1, source_target_pairs={{0,32},{32,0},{1,33},{33,1},{2,34},{34,2},{3,35},{35,3},{4,36},{36... | collective-permute-start | bytes 786440 | tf_op jit(solution)/shard_map/ppermute | solution.py:113
  145.6 33.9 %all-to-all-start.2 = ((bf16[16,64,1024]{2,1,0:T(8,128)(2,1)}), bf16[16,64,1024]{2,1,0:T(8,128)(2,1)}, u32[]{:S(2)}, u32[]{:S(2)}) async-start(bf16[16,64,1024]{2,1,0:T(8,128)(2,1)} %bitcast.24), calls=%async_computation.2 | async-start | bytes 4194304 | tf_op jit(solution)/shard_map/all_to_all | solution.py:165
  150.1 26.4 %collective-permute-start.15 = (f32[128,256]{1,0:T(8,128)S(1)}, f32[128,256]{1,0:T(8,128)S(1)}, u32[]{:S(2)}, u32[]{:S(2)}) collective-permute-start(f32[128,256]{1,0:T(8,128)S(1)} %constant_dynamic-slice_fusion), channel_id=1, source_target_pairs={{0,64},{64,0},{1,65},{65,1},{2,66},{66,2},{3,67},{67,3},{4,68},{68... | collective-permute-start | bytes 393224 | tf_op jit(solution)/shard_map/ppermute | solution.py:113
  176.4 1.3 collective-permute-start.16

commit v6 on v5

--- a/solution.py
+++ b/solution.py
@@ -75,16 +75,7 @@
     )(core.reshape(1), first, second)
 
 
-def stats_kernel(at_ref, acts_ref, *refs):
-    pieces, outs, block_ref = refs[:4], refs[4:8], refs[8]
-    y, x = at_ref[0], at_ref[1]
-    tokens = pieces[0].shape[0] // 4
-    for dy, piece in enumerate(pieces):
-        for dx in range(4):
-            start = (lax.rem(y + dy, 4) * 4 + lax.rem(x + dx, 4)) * tokens
-            block_ref[pl.ds(pl.multiple_of(start, tokens), tokens)] = piece[
-                dx * tokens : (dx + 1) * tokens
-            ]
+def stats_kernel(acts_ref, block_ref, *outs):
     width = outs[0].shape[0]
     for j, out in enumerate(outs):
         out[...] = lax.dot_general(
@@ -95,18 +86,17 @@
         ).astype(out.dtype)
 
 
-def stats(at, acts, pieces):
+def stats(acts, block):
     width = 2 * BLOCK
     return pl.pallas_call(
         stats_kernel,
         out_shape=(jax.ShapeDtypeStruct((width, width), F32),)
         + (jax.ShapeDtypeStruct((width, width), BF16),) * 3,
-        in_specs=[SCALAR] + [WHOLE] * 5,
+        in_specs=[WHOLE] * 2,
         out_specs=(WHOLE,) * 4,
-        scratch_shapes=[pltpu.VMEM((acts.shape[0], width), BF16)],
         compiler_params=params(),
         name="stats",
-    )(at, acts, *pieces)
+    )(acts, block)
 
 
 def swap(a, axis):
@@ -142,21 +132,18 @@
                 pairs.append((a * 4 + c * 2 + b, (a ^ c) * 4 + c * 2 + (1 - b)))
     got = lax.ppermute(send, ("yh", "core", "yl"), pairs)
 
+    quant = attn_quant[:, :BLOCK]
+    shift = (attn_float[:, :BLOCK].astype(F32) - quant.astype(F32)).astype(BF16)
+    block = jnp.concatenate([quant, shift], axis=1)
+    block = lax.all_gather(block, PLANE, axis=0, tiled=True)
+
     payload = pack(z, attn_float, attn_quant)
     rows = jnp.concatenate([own, got], axis=0)
     parts = [rows] + [ahead(rows, "z", j) for j in (1, 2, 3)]
     mine = jnp.concatenate(parts, axis=0)
     other = swap(mine, "core")
 
-    quant = attn_quant[:, :BLOCK]
-    shift = (attn_float[:, :BLOCK].astype(F32) - quant.astype(F32)).astype(BF16)
-    block = jnp.concatenate([quant, shift], axis=1)
-    block, payload = lax.optimization_barrier((block, payload))
     acts = lax.all_to_all(payload, PLANE, 0, 0, tiled=True).reshape(16 * tokens, 8 * features)
-
-    line = jnp.concatenate([block] + [ahead(block, "x", j) for j in (1, 2, 3)], axis=0)
-    pieces = [line] + [ahead(line, ("yh", "yl"), j) for j in (1, 2, 3)]
-    acts, mine, *pieces = lax.optimization_barrier((acts, mine, *pieces))
 
     def part(w):
         return jnp.dot(acts, w, preferred_element_type=F32).astype(BF16)
@@ -168,14 +155,12 @@
     result1 = output(first)
 
     acts1, first = lax.optimization_barrier((acts, first))
-    blocks = stats(jnp.stack([yh * 2 + yl, lax.axis_index("x")]), acts1, pieces)
+    blocks = stats(acts1, block)
     total = blocks[0]
     for j in (1, 2, 3):
         total = total + ahead(blocks[j], "z", 4 - j).astype(F32)
-    other, total = lax.optimization_barrier((other, total))
-    second = part(other)
     total = (total + swap(total, "core")) * inverse
-    second, total = lax.optimization_barrier((second, total))
+    second, total = lax.optimization_barrier((part(other), total))
     result2 = output(second)
 
     piece = swap(lax.dynamic_slice_in_dim(total, core * BLOCK, BLOCK, 0), "yh")

time: 184 us -> 197 us (1.071)
  blocking collectives: 0 us -> 41.2 us
  waiting for transfers between devices: 105 us -> 84.5 us
  starting transfers between devices: 38.5 us -> 33.4 us
    all_gather x0 -> x1, blocking collectives: none -> 41.2 us  [shards(): block = lax.all_gather(block, PLANE, axis=0, tiled=True)]
    ppermute x12 -> x6, waiting for transfers between devices: 63 us -> 46.1 us  [ahead(): return lax.ppermute(a, axis, [((i + j) % 4, i) for i in range(4)])]
    all_to_all x1, waiting for transfers between devices: 0.01 us -> 8.21 us  [shards(): lax.all_to_all(payload, PLANE, 0, 0, tiled=True)]
    ppermute x1, waiting for transfers between devices: 7.5 us -> 0.01 us  [shards(): got = lax.ppermute(send, ('yh', 'core', 'yl'), pairs)]
    ppermute x12 -> x6, starting transfers between devices: 17.9 us -> 11.9 us  [ahead(): return lax.ppermute(a, axis, [((i + j) % 4, i) for i in range(4)])]
    all_to_all x2, waiting for transfers between devices: 10.1 us -> 4.29 us  [output(): lax.all_to_all(p.reshape(16, tokens, quarter), PLANE, 0, 0, tiled=True)]
    unnamed x13 -> x10, local copies, waits for them, and re-layouts: 7.07 us -> 5.87 us
  transfers between devices with their start and end apart: 20 -> 14, of which waited for: 15 -> 10; matrix products, arithmetic and copies ran while one was open for 14% -> 12% of each run, Pallas kernels for 2% -> 2%
where the time goes in v6:
time: 197 us
  waiting for transfers between devices  84.5 us (43%)
  blocking collectives  41.2 us (21%)
  starting transfers between devices  33.4 us (17%)
  matrix products  18.7 us (9%)
  local copies, waits for them, and re-layouts  8.51 us (4%)
  Pallas kernels  6.26 us (3%)
  other arithmetic  3.28 us (2%)
    ppermute x6, waiting for transfers between devices, ahead(): return lax.ppermute(a, axis, [((i + j) % 4, i) for i in range(4)])  46.1 us
    all_gather x1, blocking collectives, shards(): block = lax.all_gather(block, PLANE, axis=0, tiled=True)  41.2 us
    ppermute x4, waiting for transfers between devices, swap(): return lax.ppermute(a, axis, [(0, 1), (1, 0)])  25.9 us
    dot_general x2, matrix products, part(): return jnp.dot(acts, w, preferred_element_type=F32).astype(BF16)  18.7 us
    ppermute x6, starting transfers between devices, ahead(): return lax.ppermute(a, axis, [((i + j) % 4, i) for i in range(4)])  11.9 us
    all_to_all x2, starting transfers between devices, output(): lax.all_to_all(p.reshape(16, tokens, quarter), PLANE, 0, 0, tiled=True)  9.46 us
    all_to_all x1, waiting for transfers between devices, shards(): lax.all_to_all(payload, PLANE, 0, 0, tiled=True)  8.21 us
    all_to_all x1, starting transfers between devices, shards(): lax.all_to_all(payload, PLANE, 0, 0, tiled=True)  6.79 us
  transfers between devices with their start and end apart: 14, of which 10 were waited for; matrix products, arithmetic and copies ran while one was open for 12% of the time, Pallas kernels for 2%

profile of v6, /device:TPU:0, one launch (start us, length us, event | category | flops | bytes accessed | tf_op | source)
XLA Modules:
  0.0 196.6 jit_solution(2656003354077643916)
XLA Ops:
  0.7 0.9 constant_dynamic-slice_fusion
  1.5 3.1 %fusion.3 = (bf16[256,1024]{1,0:T(8,128)(2,1)}, bf16[256,1024]{1,0:T(8,128)(2,1)S(1)}) fusion(s32[256,4096]{1,0:T(8,128)} %param.8, s32[]{:T(128)S(6)} %select_n.45, f32[2,1024]{1,0:T(2,128)S(1)} %get-tuple-element.26, bf16[256,4096]{1,0:T(8,128)(2,1)} %param.7, pred[]{:T(512)S(6)} %eq.13, f32[2,1024]{1,0:T(2,128)S(1)} %get-tuple-element.27, ...), kind=kLoop, calls=%fused_computation.8 | loop fusion | flops 2621440 | bytes 4210698 | tf_op jit(solution)/shard_map/jit(_where)/select_n | solution.py:124
  4.6 1.7 collective-permute-start
  6.6 2.0 %copy-done = bf16[16,64,2048]{2,1,0:T(8,128)(2,1)} copy-done((bf16[16,64,2048]{2,1,0:T(8,128)(2,1)}, bf16[16,64,2048]{2,1,0:T(8,128)(2,1)S(1)}, u32[]{:S(2)}) %copy-start) | copy-done | bytes 4194328
  8.6 6.8 %all-to-all-start = ((bf16[16,64,2048]{2,1,0:T(8,128)(2,1)}), bf16[16,64,2048]{2,1,0:T(8,128)(2,1)}, u32[]{:S(2)}, u32[]{:S(2)}) async-start(bf16[16,64,2048]{2,1,0:T(8,128)(2,1)} %copy-done), calls=%async_computation | async-start | bytes 8388608 | tf_op jit(solution)/shard_map/all_to_all | solution.py:146
  15.5 4.1 %collective-permute-start.1 = (bf16[512,1024]{1,0:T(8,128)(2,1)S(1)}, bf16[512,1024]{1,0:T(8,128)(2,1)S(1)}, u32[]{:S(2)}, u32[]{:S(2)}) collective-permute-start(bf16[512,1024]{1,0:T(8,128)(2,1)S(1)} %pad_maximum_fusion), channel_id=1, source_target_pairs={{4,0},{8,4},{12,8},{0,12},{5,1},{9,5},{13,9},{1,13},{6,2},{10,6},{... | collective-permute-start | bytes 3145736 | tf_op jit(solution)/shard_map/ppermute | solution.py:107
  19.6 1.3 collective-permute-start.3
  20.8 0.9 constant_dynamic-update-slice_fusion.4
  21.7 0.8 constant_dynamic-update-slice_fusion.3
  22.6 40.8 %collective-permute-done.1 = bf16[512,1024]{1,0:T(8,128)(2,1)S(1)} collective-permute-done((bf16[512,1024]{1,0:T(8,128)(2,1)S(1)}, bf16[512,1024]{1,0:T(8,128)(2,1)S(1)}, u32[]{:S(2)}, u32[]{:S(2)}) %collective-permute-start.1) | collective-permute-done | bytes 1048608 | tf_op jit(solution)/shard_map/ppermute | solution.py:107
  63.4 1.0 constant_dynamic-update-slice_fusion.2
  64.4 1.1 constant_dynamic-update-slice_fusion.1
  65.5 1.3 collective-permute-done.3
  66.8 1.0 constant_dynamic-update-slice_fusion
  67.9 8.2 %all-to-all-done = bf16[16,64,2048]{2,1,0:T(8,128)(2,1)} async-done(((bf16[16,64,2048]{2,1,0:T(8,128)(2,1)}), bf16[16,64,2048]{2,1,0:T(8,128)(2,1)}, u32[]{:S(2)}, u32[]{:S(2)}) %all-to-all-start) | async-done | bytes 4194336 | tf_op jit(solution)/shard_map/all_to_all | solution.py:146
  76.1 9.3 %convolution_convert_fusion.1 = bf16[1024,1024]{1,0:T(8,128)(2,1)} fusion(bf16[1024,2048]{1,0:T(8,128)(2,1)} %bitcast.2.acts_ref, bf16[2048,1024]{1,0:T(8,128)(2,1)} %constant_dynamic-update-slice_fusion), kind=kOutput, calls=%fused_computation.1 | convolution fusion | flops 4296015872 | bytes 10485760 | tf_op jit(solution)/shard_map/dot_general | solution.py:149
  85.4 4.4 %all-to-all-start.1 = ((bf16[16,64,1024]{2,1,0:T(8,128)(2,1)}), bf16[16,64,1024]{2,1,0:T(8,128)(2,1)S(1)}, u32[]{:S(2)}, u32[]{:S(2)}) async-start(bf16[16,64,1024]{2,1,0:T(8,128)(2,1)} %bitcast.21), calls=%async_computation.1 | async-start | bytes 4194304 | tf_op jit(solution)/shard_map/all_to_all | solution.py:152
  89.8 41.2 %all_gather.3.block_ref = bf16[1024,256]{1,0:T(8,128)(2,1)S(1)} all-gather(bf16[64,256]{1,0:T(8,128)(2,1)S(1)} %pad_maximum_fusion.1), channel_id=1, replica_groups=mesh['yh'=2,'core'=2,'yl'=2,'z'=4,'x'=4] {'yh','yl','x'}, dimensions={0}, use_global_device_ids=true | all-gather | bytes 557056 | tf_op jit(solution)/shard_map/all_gather | solution.py:138
  131.0 3.0 %stats.1 = (f32[256,256]{1,0:T(8,128)S(1)}, bf16[256,256]{1,0:T(8,128)(2,1)S(1)}, bf16[256,256]{1,0:T(8,128)(2,1)S(1)}, bf16[256,256]{1,0:T(8,128)(2,1)S(1)}) custom-call(bf16[1024,2048]{1,0:T(8,128)(2,1)} %bitcast.2.acts_ref, bf16[1024,256]{1,0:T(8,128)(2,1)S(1)} %all_gather.3.block_ref), custom_call_target="tpu_custom_call" | custom-call | tf_op jit(solution)/shard_map/stats/pallas_call | solution.py:91
  134.0 2.0 %collective-permute-start.5 = (bf16[256,256]{1,0:T(8,128)(2,1)S(1)}, bf16[256,256]{1,0:T(8,128)(2,1)S(1)}, u32[]{:S(2)}, u32[]{:S(2)}) collective-permute-start(bf16[256,256]{1,0:T(8,128)(2,1)S(1)} %get-tuple-element.15), channel_id=1, source_target_pairs={{12,0},{0,4},{4,8},{8,12},{13,1},{1,5},{5,9},{9,13},{14,2},{2,6},{... | collective-permute-start | bytes 393224 | tf_op jit(solution)/shard_map/ppermute | solution.py:107
  136.0 3.6 %collective-permute-start.6 = (bf16[256,256]{1,0:T(8,128)(2,1)S(1)}, bf16[256,256]{1,0:T(8,128)(2,1)S(1)}, u32[]{:S(2)}, u32[]{:S(2)}) collective-permute-start(bf16[256,256]{1,0:T(8,128)(2,1)S(1)} %get-tuple-element.16), channel_id=1, source_target_pairs={{8,0},{12,4},{0,8},{4,12},{9,1},{13,5},{1,9},{5,13},{10,2},{14,6},... | collective-permute-start | bytes 393224 | tf_op jit(solution)/shard_map/ppermute | solution.py:107
  139.6 1.0 collective-permute-start.7
  141.0 2.9 %collective-permute-done.6 = bf16[256,256]{1,0:T(8,128)(2,1)S(1)} collective-permute-done((bf16[256,256]{1,0:T(8,128)(2,1)S(1)}, bf16[256,256]{1,0:T(8,128)(2,1)S(1)}, u32[]{:S(2)}, u32[]{:S(2)}) %collective-permute-start.6) | collective-permute-done | bytes 131104 | tf_op jit(solution)/shard_map/ppermute | solution.py:107
  144.7 1.5 collective-permute-done.8
  146.3 9.4 %convolution_convert_fusion = bf16[1024,1024]{1,0:T(8,128)(2,1)} fusion(bf16[1024,2048]{1,0:T(8,128)(2,1)} %bitcast.2.acts_ref, bf16[2048,1024]{1,0:T(8,128)(2,1)} %collective-permute-done.4), kind=kOutput, calls=%fused_computation | convolution fusion | flops 4296015872 | bytes 10485760 | tf_op jit(solution)/shard_map/dot_general | solution.py:149
  155.6 5.1 %all-to-all-start.2 = ((bf16[16,64,1024]{2,1,0:T(8,128)(2,1)}), bf16[16,64,1024]{2,1,0:T(8,128)(2,1)}, u32[]{:S(2)}, u32[]{:S(2)}) async-start(bf16[16,64,1024]{2,1,0:T(8,128)(2,1)} %bitcast.22), calls=%async_computation.2 | async-start | bytes 4194304 | tf_op jit(solution)/shard_map/all_to_all | solution.py:152
  160.7 3.4 %collective-permute-start.9 = (f32[128,256]{1,0:T(8,128)S(1)}, f32[128,256]{1,0:T(8,128)S(1)}, u32[]{:S(2)}, u32[]{:S(2)}) collective-permute-start(f32[128,256]{1,0:T(8,128)S(1)} %constant_dynamic-slice_fusion.1), channel_id=1, source_target_pairs={{0,64},{64,0},{1,65},{65,1},{2,66},{66,2},{3,67},{67,3},{4,68},{68... | collective-permute-start | bytes 393224 | tf_op jit(solution)/shard_map/ppermute | solution.py:103
  164.2 23.1 %collective-permute-done.9 = f32[128,256]{1,0:T(8,128)S(1)} collective-permute-done((f32[128,256]{1,0:T(8,128)S(1)}, f32[128,256]{1,0:T(8,128)S(1)}, u32[]{:S(2)}, u32[]{:S(2)}) %collective-permute-start.9) | collective-permute-done | bytes 131104 | tf_op jit(solution)/shard_map/ppermute | solution.py:103
  187.2 1.3 collective-permute-done.10
  188.6 0.7 fusion.5
  189.3 4.3 %all-to-all-done.2.second_ref = bf16[16,64,1024]{2,1,0:T(8,128)(2,1)} async-done(((bf16[16,64,1024]{2,1,0:T(8,128)(2,1)}), bf16[16,64,1024]{2,1,0:T(8,128)(2,1)}, u32[]{:S(2)}, u32[]{:S(2)}) %all-to-all-start.2) | async-done | bytes 2097184 | tf_op jit(solution)/shard_map/all_to_all | solution.py:152
  193.6 3.0 %finish.1 = (bf16[64,4096]{1,0:T(8,128)(2,1)}, bf16[64,4096]{1,0:T(8,128)(2,1)}) custom-call(s32[1]{0:T(128)} %bitcast.core_ref, bf16[16,64,1024]{2,1,0:T(8,128)(2,1)S(1)} %all-to-all-done.1.first_ref, bf16[16,64,1024]{2,1,0:T(8,128)(2,1)} %all-to-all-done.2.second_ref), custom_call_target="tpu_custom_call" | custom-call | tf_op jit(solution)/shard_map/finish/pallas_call | solution.py:68
  (25 shorter events, 1.8 us)
Async XLA Ops:
  0.6 5.6 %copy-start.2 = (bf16[64,8192]{1,0:T(8,128)(2,1)S(1)}, bf16[64,8192]{1,0:T(8,128)(2,1)}, u32[]{:S(2)}) copy-start(bf16[64,8192]{1,0:T(8,128)(2,1)} %float_ref.1) | copy-start | bytes 3145732
  0.6 5.6 %copy-start.1 = (bf16[64,8192]{1,0:T(8,128)(2,1)S(1)}, bf16[64,8192]{1,0:T(8,128)(2,1)}, u32[]{:S(2)}) copy-start(bf16[64,8192]{1,0:T(8,128)(2,1)} %quant_ref.1) | copy-start | bytes 3145732
  4.6 10.8 %collective-permute-start = (bf16[256,1024]{1,0:T(8,128)(2,1)}, bf16[256,1024]{1,0:T(8,128)(2,1)S(1)}, u32[]{:S(2)}, u32[]{:S(2)}) collective-permute-start(bf16[256,1024]{1,0:T(8,128)(2,1)} %get-tuple-element.22), channel_id=1, source_target_pairs={{0,16},{16,0},{32,112},{48,96},{64,80},{80,64},{96,48},{112,32},{1... | collective-permute-start | bytes 1572872 | tf_op jit(solution)/shard_map/ppermute | solution.py:133
  6.6 2.0 %copy-start = (bf16[16,64,2048]{2,1,0:T(8,128)(2,1)}, bf16[16,64,2048]{2,1,0:T(8,128)(2,1)S(1)}, u32[]{:S(2)}) copy-start(bf16[16,64,2048]{2,1,0:T(8,128)(2,1)S(1)} %pack.1) | copy-start | bytes 12582916
  8.6 67.5 %all-to-all-start = ((bf16[16,64,2048]{2,1,0:T(8,128)(2,1)}), bf16[16,64,2048]{2,1,0:T(8,128)(2,1)}, u32[]{:S(2)}, u32[]{:S(2)}) async-start(bf16[16,64,2048]{2,1,0:T(8,128)(2,1)} %copy-done), calls=%async_computation | async-start | bytes 8388608 | tf_op jit(solution)/shard_map/all_to_all | solution.py:146
  15.5 52.4 %slice-start = ((bf16[64,8192]{1,0:T(8,128)(2,1)}), bf16[64,128]{1,0:T(8,128)(2,1)S(1)}, s32[]{:S(2)}) async-start(bf16[64,8192]{1,0:T(8,128)(2,1)} %quant_ref.1), calls=%async_computation.3 | async-start | bytes 32768 | tf_op jit(solution)/shard_map/slice | solution.py:135
  15.5 47.9 %collective-permute-start.1 = (bf16[512,1024]{1,0:T(8,128)(2,1)S(1)}, bf16[512,1024]{1,0:T(8,128)(2,1)S(1)}, u32[]{:S(2)}, u32[]{:S(2)}) collective-permute-start(bf16[512,1024]{1,0:T(8,128)(2,1)S(1)} %pad_maximum_fusion), channel_id=1, source_target_pairs={{4,0},{8,4},{12,8},{0,12},{5,1},{9,5},{13,9},{1,13},{6,2},{10,6},{... | collective-permute-start | bytes 3145736 | tf_op jit(solution)/shard_map/ppermute | solution.py:107
  19.6 44.8 %collective-permute-start.2 = (bf16[512,1024]{1,0:T(8,128)(2,1)S(1)}, bf16[512,1024]{1,0:T(8,128)(2,1)S(1)}, u32[]{:S(2)}, u32[]{:S(2)}) collective-permute-start(bf16[512,1024]{1,0:T(8,128)(2,1)S(1)} %pad_maximum_fusion), channel_id=1, source_target_pairs={{8,0},{12,4},{0,8},{4,12},{9,1},{13,5},{1,9},{5,13},{10,2},{14,6},... | collective-permute-start | bytes 3145736 | tf_op jit(solution)/shard_map/ppermute | solution.py:107
  19.6 47.2 %collective-permute-start.3 = (bf16[512,1024]{1,0:T(8,128)(2,1)S(1)}, bf16[512,1024]{1,0:T(8,128)(2,1)S(1)}, u32[]{:S(2)}, u32[]{:S(2)}) collective-permute-start(bf16[512,1024]{1,0:T(8,128)(2,1)S(1)} %pad_maximum_fusion), channel_id=1, source_target_pairs={{12,0},{0,4},{4,8},{8,12},{13,1},{1,5},{5,9},{9,13},{14,2},{2,6},{... | collective-permute-start | bytes 3145736 | tf_op jit(solution)/shard_map/ppermute | solution.py:107
  67.8 78.4 %collective-permute-start.4 = (bf16[2048,1024]{1,0:T(8,128)(2,1)}, bf16[2048,1024]{1,0:T(8,128)(2,1)}, u32[]{:S(2)}, u32[]{:S(2)}) collective-permute-start(bf16[2048,1024]{1,0:T(8,128)(2,1)} %constant_dynamic-update-slice_fusion), channel_id=1, source_target_pairs={{0,32},{32,0},{1,33},{33,1},{2,34},{34,2},{3,35},{35,3},{4,36},{36... | collective-permute-start | bytes 12582920 | tf_op jit(solution)/shard_map/ppermute | solution.py:103
  85.4 70.2 %all-to-all-start.1 = ((bf16[16,64,1024]{2,1,0:T(8,128)(2,1)}), bf16[16,64,1024]{2,1,0:T(8,128)(2,1)S(1)}, u32[]{:S(2)}, u32[]{:S(2)}) async-start(bf16[16,64,1024]{2,1,0:T(8,128)(2,1)} %bitcast.21), calls=%async_computation.1 | async-start | bytes 4194304 | tf_op jit(solution)/shard_map/all_to_all | solution.py:152
  134.0 7.1 %collective-permute-start.5 = (bf16[256,256]{1,0:T(8,128)(2,1)S(1)}, bf16[256,256]{1,0:T(8,128)(2,1)S(1)}, u32[]{:S(2)}, u32[]{:S(2)}) collective-permute-start(bf16[256,256]{1,0:T(8,128)(2,1)S(1)} %get-tuple-element.15), channel_id=1, source_target_pairs={{12,0},{0,4},{4,8},{8,12},{13,1},{1,5},{5,9},{9,13},{14,2},{2,6},{... | collective-permute-start | bytes 393224 | tf_op jit(solution)/shard_map/ppermute | solution.py:107
  136.0 7.9 %collective-permute-start.6 = (bf16[256,256]{1,0:T(8,128)(2,1)S(1)}, bf16[256,256]{1,0:T(8,128)(2,1)S(1)}, u32[]{:S(2)}, u32[]{:S(2)}) collective-permute-start(bf16[256,256]{1,0:T(8,128)(2,1)S(1)} %get-tuple-element.16), channel_id=1, source_target_pairs={{8,0},{12,4},{0,8},{4,12},{9,1},{13,5},{1,9},{5,13},{10,2},{14,6},... | collective-permute-start | bytes 393224 | tf_op jit(solution)/shard_map/ppermute | solution.py:107
  139.6 5.0 %collective-permute-start.7 = (bf16[256,256]{1,0:T(8,128)(2,1)S(1)}, bf16[256,256]{1,0:T(8,128)(2,1)S(1)}, u32[]{:S(2)}, u32[]{:S(2)}) collective-permute-start(bf16[256,256]{1,0:T(8,128)(2,1)S(1)} %get-tuple-element.17), channel_id=1, source_target_pairs={{4,0},{8,4},{12,8},{0,12},{5,1},{9,5},{13,9},{1,13},{6,2},{10,6},{... | collective-permute-start | bytes 393224 | tf_op jit(solution)/shard_map/ppermute | solution.py:107
  144.6 1.6 collective-permute-start.8
  155.6 38.0 %all-to-all-start.2 = ((bf16[16,64,1024]{2,1,0:T(8,128)(2,1)}), bf16[16,64,1024]{2,1,0:T(8,128)(2,1)}, u32[]{:S(2)}, u32[]{:S(2)}) async-start(bf16[16,64,1024]{2,1,0:T(8,128)(2,1)} %bitcast.22), calls=%async_computation.2 | async-start | bytes 4194304 | tf_op jit(solution)/shard_map/all_to_all | solution.py:152
  160.7 26.5 %collective-permute-start.9 = (f32[128,256]{1,0:T(8,128)S(1)}, f32[128,256]{1,0:T(8,128)S(1)}, u32[]{:S(2)}, u32[]{:S(2)}) collective-permute-start(f32[128,256]{1,0:T(8,128)S(1)} %constant_dynamic-slice_fusion.1), channel_id=1, source_target_pairs={{0,64},{64,0},{1,65},{65,1},{2,66},{66,2},{3,67},{67,3},{4,68},{68... | collective-permute-start | bytes 393224 | tf_op jit(solution)/shard_map/ppermute | solution.py:103
  187.2 1.3 collective-permute-start.10

commit v7 on v6

--- a/solution.py
+++ b/solution.py
@@ -22,8 +22,10 @@
 
 
 def pack_kernel(z_ref, float_ref, quant_ref, out_ref):
-    width = out_ref.shape[2] // 8
+    width = float_ref.shape[1] // 32
     z = z_ref[0]
+    quant = quant_ref[:, :BLOCK]
+    shift = (float_ref[:, :BLOCK].astype(F32) - quant.astype(F32)).astype(BF16)
     for kind, ref in enumerate((float_ref, quant_ref)):
         for j in range(4):
             zj = lax.rem(z + j, 4)
@@ -34,13 +36,16 @@
                     for half in range(2):
                         at = (j * 2 + (yl ^ half)) * width
                         out_ref[kind * 8 + half * 4 + x, :, at : at + width] = block
+    for d in range(16):
+        out_ref[d, :, 8 * width : 8 * width + BLOCK] = quant
+        out_ref[d, :, 8 * width + BLOCK :] = shift
 
 
 def pack(z, attn_float, attn_quant):
     tokens, d_in = attn_float.shape
     return pl.pallas_call(
         pack_kernel,
-        out_shape=jax.ShapeDtypeStruct((16, tokens, d_in // 4), BF16),
+        out_shape=jax.ShapeDtypeStruct((16, tokens, d_in // 4 + 2 * BLOCK), BF16),
         in_specs=[SCALAR, WHOLE, WHOLE],
         out_specs=WHOLE,
         compiler_params=params(),
@@ -75,28 +80,28 @@
     )(core.reshape(1), first, second)
 
 
-def stats_kernel(acts_ref, block_ref, *outs):
+def stats_kernel(acts_ref, *outs):
     width = outs[0].shape[0]
     for j, out in enumerate(outs):
         out[...] = lax.dot_general(
             acts_ref[:, 2 * j * width : (2 * j + 1) * width],
-            block_ref[...],
+            acts_ref[:, 8 * width :],
             (((0,), (0,)), ((), ())),
             preferred_element_type=F32,
         ).astype(out.dtype)
 
 
-def stats(acts, block):
+def stats(acts):
     width = 2 * BLOCK
     return pl.pallas_call(
         stats_kernel,
         out_shape=(jax.ShapeDtypeStruct((width, width), F32),)
         + (jax.ShapeDtypeStruct((width, width), BF16),) * 3,
-        in_specs=[WHOLE] * 2,
+        in_specs=[WHOLE],
         out_specs=(WHOLE,) * 4,
         compiler_params=params(),
         name="stats",
-    )(acts, block)
+    )(acts)
 
 
 def swap(a, axis):
@@ -132,21 +137,17 @@
                 pairs.append((a * 4 + c * 2 + b, (a ^ c) * 4 + c * 2 + (1 - b)))
     got = lax.ppermute(send, ("yh", "core", "yl"), pairs)
 
-    quant = attn_quant[:, :BLOCK]
-    shift = (attn_float[:, :BLOCK].astype(F32) - quant.astype(F32)).astype(BF16)
-    block = jnp.concatenate([quant, shift], axis=1)
-    block = lax.all_gather(block, PLANE, axis=0, tiled=True)
-
     payload = pack(z, attn_float, attn_quant)
     rows = jnp.concatenate([own, got], axis=0)
     parts = [rows] + [ahead(rows, "z", j) for j in (1, 2, 3)]
     mine = jnp.concatenate(parts, axis=0)
     other = swap(mine, "core")
 
-    acts = lax.all_to_all(payload, PLANE, 0, 0, tiled=True).reshape(16 * tokens, 8 * features)
+    acts = lax.all_to_all(payload, PLANE, 0, 0, tiled=True)
+    acts = acts.reshape(16 * tokens, 8 * features + 2 * BLOCK)
 
     def part(w):
-        return jnp.dot(acts, w, preferred_element_type=F32).astype(BF16)
+        return jnp.dot(acts[:, : 8 * features], w, preferred_element_type=F32).astype(BF16)
 
     def output(p):
         return lax.all_to_all(p.reshape(16, tokens, quarter), PLANE, 0, 0, tiled=True)
@@ -155,15 +156,14 @@
     result1 = output(first)
 
     acts1, first = lax.optimization_barrier((acts, first))
-    blocks = stats(acts1, block)
+    blocks = stats(acts1)
     total = blocks[0]
     for j in (1, 2, 3):
         total = total + ahead(blocks[j], "z", 4 - j).astype(F32)
     total = (total + swap(total, "core")) * inverse
-    second, total = lax.optimization_barrier((part(other), total))
+    piece = swap(lax.dynamic_slice_in_dim(total, core * BLOCK, BLOCK, 0), "yh")
+    second, piece = lax.optimization_barrier((part(other), piece))
     result2 = output(second)
-
-    piece = swap(lax.dynamic_slice_in_dim(total, core * BLOCK, BLOCK, 0), "yh")
     again = swap(piece, "core")
     moved = jnp.where(
         core == 0, jnp.concatenate([piece, again]), jnp.concatenate([again, piece])

time: 197 us -> 217 us (1.10)
  waiting for transfers between devices: 84.5 us -> 143 us
  blocking collectives: 41.2 us -> 0 us
  starting transfers between devices: 33.4 us -> 35.6 us
    ppermute x1, waiting for transfers between devices: 0.01 us -> 54.5 us  [shards(): got = lax.ppermute(send, ('yh', 'core', 'yl'), pairs)]
    all_gather x1 -> x0, blocking collectives: 41.2 us -> none  [shards(): block = lax.all_gather(block, PLANE, axis=0, tiled=True)]
    all_to_all x2, waiting for transfers between devices: 4.29 us -> 33.5 us  [output(): lax.all_to_all(p.reshape(16, tokens, quarter), PLANE, 0, 0, tiled=True)]
    ppermute x4, waiting for transfers between devices: 25.9 us -> 14.7 us  [swap(): return lax.ppermute(a, axis, [(0, 1), (1, 0)])]
    all_to_all x1, waiting for transfers between devices: 8.21 us -> 0.01 us  [shards(): acts = lax.all_to_all(payload, PLANE, 0, 0, tiled=True)]
    ppermute x6, waiting for transfers between devices: 46.1 us -> 40.3 us  [ahead(): return lax.ppermute(a, axis, [((i + j) % 4, i) for i in range(4)])]
    all_to_all x2, starting transfers between devices: 9.46 us -> 13.3 us  [output(): lax.all_to_all(p.reshape(16, tokens, quarter), PLANE, 0, 0, tiled=True)]
    ppermute x6, starting transfers between devices: 11.9 us -> 9.31 us  [ahead(): return lax.ppermute(a, axis, [((i + j) % 4, i) for i in range(4)])]
  transfers between devices with their start and end apart: 14 -> 14, of which waited for: 10 -> 8; matrix products, arithmetic and copies ran while one was open for 12% -> 12% of each run, Pallas kernels for 2% -> 1%
where the time goes in v7:
time: 217 us
  waiting for transfers between devices  143 us (66%)
  starting transfers between devices  35.6 us (16%)
  matrix products  18.6 us (9%)
  local copies, waits for them, and re-layouts  10.3 us (5%)
  Pallas kernels  6.46 us (3%)
    ppermute x1, waiting for transfers between devices, shards(): got = lax.ppermute(send, ('yh', 'core', 'yl'), pairs)  54.5 us
    ppermute x6, waiting for transfers between devices, ahead(): return lax.ppermute(a, axis, [((i + j) % 4, i) for i in range(4)])  40.3 us
    all_to_all x2, waiting for transfers between devices, output(): lax.all_to_all(p.reshape(16, tokens, quarter), PLANE, 0, 0, tiled=True)  33.5 us
    dot_general x2, matrix products, part(): jnp.dot(acts[:, :8 * features], w, preferred_element_type=F32).astype(BF16)  18.6 us
    ppermute x4, waiting for transfers between devices, swap(): return lax.ppermute(a, axis, [(0, 1), (1, 0)])  14.7 us
    all_to_all x2, starting transfers between devices, output(): lax.all_to_all(p.reshape(16, tokens, quarter), PLANE, 0, 0, tiled=True)  13.3 us
    ppermute x6, starting transfers between devices, ahead(): return lax.ppermute(a, axis, [((i + j) % 4, i) for i in range(4)])  9.31 us
    unnamed x14, local copies, waits for them, and re-layouts  8.45 us
  transfers between devices with their start and end apart: 14, of which 8 were waited for; matrix products, arithmetic and copies ran while one was open for 12% of the time, Pallas kernels for 1%

profile of v7, /device:TPU:0, one launch (start us, length us, event | category | flops | bytes accessed | tf_op | source)
XLA Modules:
  0.0 216.8 jit_solution(6752952538409502342)
XLA Ops:
  0.6 1.2 copy-done.1
  1.9 1.2 copy-done.2
  3.1 0.4 pack.1
  3.5 2.2 %copy-done = bf16[16,64,2304]{2,1,0:T(8,128)(2,1)} copy-done((bf16[16,64,2304]{2,1,0:T(8,128)(2,1)}, bf16[16,64,2304]{2,1,0:T(8,128)(2,1)S(1)}, u32[]{:S(2)}) %copy-start) | copy-done | bytes 4718616
  5.7 7.3 %all-to-all-start = ((bf16[16,64,2304]{2,1,0:T(8,128)(2,1)}), bf16[16,64,2304]{2,1,0:T(8,128)(2,1)}, u32[]{:S(2)}, u32[]{:S(2)}) async-start(bf16[16,64,2304]{2,1,0:T(8,128)(2,1)} %copy-done), calls=%async_computation | async-start | bytes 9437184 | tf_op jit(solution)/shard_map/all_to_all | solution.py:146
  13.0 2.0 fusion.13
  15.0 1.9 collective-permute-start
  16.9 54.5 %collective-permute-done = bf16[256,1024]{1,0:T(8,128)(2,1)S(1)} collective-permute-done((bf16[256,1024]{1,0:T(8,128)(2,1)S(1)}, bf16[256,1024]{1,0:T(8,128)(2,1)S(1)}, u32[]{:S(2)}, u32[]{:S(2)}) %collective-permute-start) | collective-permute-done | bytes 524320 | tf_op jit(solution)/shard_map/ppermute | solution.py:138
  71.5 4.1 %collective-permute-start.1 = (bf16[512,1024]{1,0:T(8,128)(2,1)S(1)}, bf16[512,1024]{1,0:T(8,128)(2,1)S(1)}, u32[]{:S(2)}, u32[]{:S(2)}) collective-permute-start(bf16[512,1024]{1,0:T(8,128)(2,1)S(1)} %pad_maximum_fusion), channel_id=1, source_target_pairs={{4,0},{8,4},{12,8},{0,12},{5,1},{9,5},{13,9},{1,13},{6,2},{10,6},{... | collective-permute-start | bytes 3145736 | tf_op jit(solution)/shard_map/ppermute | solution.py:112
  75.6 1.3 collective-permute-start.3
  76.8 0.8 constant_dynamic-update-slice_fusion.4
  77.7 0.8 constant_dynamic-update-slice_fusion.3
  78.5 39.0 %collective-permute-done.1 = bf16[512,1024]{1,0:T(8,128)(2,1)S(1)} collective-permute-done((bf16[512,1024]{1,0:T(8,128)(2,1)S(1)}, bf16[512,1024]{1,0:T(8,128)(2,1)S(1)}, u32[]{:S(2)}, u32[]{:S(2)}) %collective-permute-start.1) | collective-permute-done | bytes 1048608 | tf_op jit(solution)/shard_map/ppermute | solution.py:112
  117.5 1.1 constant_dynamic-update-slice_fusion.2
  118.6 1.0 constant_dynamic-update-slice_fusion.1
  119.6 1.3 collective-permute-done.3
  120.9 1.1 constant_dynamic-update-slice_fusion
  122.0 9.3 %fusion.4 = bf16[1024,1024]{1,0:T(8,128)(2,1)} fusion(bf16[2048,1024]{1,0:T(8,128)(2,1)} %constant_dynamic-update-slice_fusion, bf16[1024,2304]{1,0:T(8,128)(2,1)} %bitcast.2.acts_ref), kind=kOutput, calls=%fused_computation.4 | convolution fusion | flops 4296015872 | bytes 10485760 | tf_op jit(solution)/shard_map/dot_general | solution.py:150
  131.3 3.1 %stats.1 = (f32[256,256]{1,0:T(8,128)S(1)}, bf16[256,256]{1,0:T(8,128)(2,1)S(1)}, bf16[256,256]{1,0:T(8,128)(2,1)S(1)}, bf16[256,256]{1,0:T(8,128)(2,1)S(1)}) custom-call(bf16[1024,2304]{1,0:T(8,128)(2,1)} %bitcast.2.acts_ref), custom_call_target="tpu_custom_call" | custom-call | tf_op jit(solution)/shard_map/stats/pallas_call | solution.py:96
  134.5 3.9 %collective-permute-start.6 = (bf16[256,256]{1,0:T(8,128)(2,1)S(1)}, bf16[256,256]{1,0:T(8,128)(2,1)S(1)}, u32[]{:S(2)}, u32[]{:S(2)}) collective-permute-start(bf16[256,256]{1,0:T(8,128)(2,1)S(1)} %get-tuple-element.16), channel_id=1, source_target_pairs={{8,0},{12,4},{0,8},{4,12},{9,1},{13,5},{1,9},{5,13},{10,2},{14,6},... | collective-permute-start | bytes 393224 | tf_op jit(solution)/shard_map/ppermute | solution.py:112
  138.3 8.9 %all-to-all-start.1 = ((bf16[16,64,1024]{2,1,0:T(8,128)(2,1)}), bf16[16,64,1024]{2,1,0:T(8,128)(2,1)S(1)}, u32[]{:S(2)}, u32[]{:S(2)}) async-start(bf16[16,64,1024]{2,1,0:T(8,128)(2,1)} %bitcast.19), calls=%async_computation.1 | async-start | bytes 4194304 | tf_op jit(solution)/shard_map/all_to_all | solution.py:153
  147.4 1.5 collective-permute-done.8
  149.0 3.5 %collective-permute-start.9 = (f32[128,256]{1,0:T(8,128)S(1)}, f32[128,256]{1,0:T(8,128)S(1)}, u32[]{:S(2)}, u32[]{:S(2)}) collective-permute-start(f32[128,256]{1,0:T(8,128)S(1)} %constant_dynamic-slice_fusion.2), channel_id=1, source_target_pairs={{0,64},{64,0},{1,65},{65,1},{2,66},{66,2},{3,67},{67,3},{4,68},{68... | collective-permute-start | bytes 393224 | tf_op jit(solution)/shard_map/ppermute | solution.py:108
  152.5 9.3 %fusion.7 = bf16[1024,1024]{1,0:T(8,128)(2,1)} fusion(bf16[2048,1024]{1,0:T(8,128)(2,1)} %collective-permute-done.4, bf16[1024,2304]{1,0:T(8,128)(2,1)} %bitcast.2.acts_ref), kind=kOutput, calls=%fused_computation.5 | convolution fusion | flops 4296015872 | bytes 10485760 | tf_op jit(solution)/shard_map/dot_general | solution.py:150
  161.9 11.9 %collective-permute-done.9 = f32[128,256]{1,0:T(8,128)S(1)} collective-permute-done((f32[128,256]{1,0:T(8,128)S(1)}, f32[128,256]{1,0:T(8,128)S(1)}, u32[]{:S(2)}, u32[]{:S(2)}) %collective-permute-start.9) | collective-permute-done | bytes 131104 | tf_op jit(solution)/shard_map/ppermute | solution.py:108
  173.7 5.6 %all-to-all-done.1.first_ref = bf16[16,64,1024]{2,1,0:T(8,128)(2,1)S(1)} async-done(((bf16[16,64,1024]{2,1,0:T(8,128)(2,1)}), bf16[16,64,1024]{2,1,0:T(8,128)(2,1)S(1)}, u32[]{:S(2)}, u32[]{:S(2)}) %all-to-all-start.1) | async-done | bytes 2097184 | tf_op jit(solution)/shard_map/all_to_all | solution.py:153
  179.4 4.4 %all-to-all-start.2 = ((bf16[16,64,1024]{2,1,0:T(8,128)(2,1)}), bf16[16,64,1024]{2,1,0:T(8,128)(2,1)}, u32[]{:S(2)}, u32[]{:S(2)}) async-start(bf16[16,64,1024]{2,1,0:T(8,128)(2,1)} %bitcast.20), calls=%async_computation.2 | async-start | bytes 4194304 | tf_op jit(solution)/shard_map/all_to_all | solution.py:153
  183.8 0.1 collective-permute-start.10
  183.9 1.3 collective-permute-done.10
  185.3 0.7 fusion.15
  186.0 27.8 %all-to-all-done.2.second_ref = bf16[16,64,1024]{2,1,0:T(8,128)(2,1)} async-done(((bf16[16,64,1024]{2,1,0:T(8,128)(2,1)}), bf16[16,64,1024]{2,1,0:T(8,128)(2,1)}, u32[]{:S(2)}, u32[]{:S(2)}) %all-to-all-start.2) | async-done | bytes 2097184 | tf_op jit(solution)/shard_map/all_to_all | solution.py:153
  213.8 3.0 %finish.1 = (bf16[64,4096]{1,0:T(8,128)(2,1)}, bf16[64,4096]{1,0:T(8,128)(2,1)}) custom-call(s32[1]{0:T(128)} %bitcast.core_ref, bf16[16,64,1024]{2,1,0:T(8,128)(2,1)S(1)} %all-to-all-done.1.first_ref, bf16[16,64,1024]{2,1,0:T(8,128)(2,1)} %all-to-all-done.2.second_ref), custom_call_target="tpu_custom_call" | custom-call | tf_op jit(solution)/shard_map/finish/pallas_call | solution.py:73
  (24 shorter events, 0.4 us)
Async XLA Ops:
  0.6 1.2 copy-start.1
  1.9 1.2 copy-start.2
  3.5 2.2 %copy-start = (bf16[16,64,2304]{2,1,0:T(8,128)(2,1)}, bf16[16,64,2304]{2,1,0:T(8,128)(2,1)S(1)}, u32[]{:S(2)}) copy-start(bf16[16,64,2304]{2,1,0:T(8,128)(2,1)S(1)} %pack.1) | copy-start | bytes 14155780
  5.7 7.3 %copy-start.4 = (f32[2,4096]{1,0:T(2,128)S(1)}, f32[2,4096]{1,0:T(2,128)}, u32[]{:S(2)}) copy-start(f32[2,4096]{1,0:T(2,128)} %param.9) | copy-start | bytes 98308
  5.7 7.4 %copy-start.3 = (bf16[256,4096]{1,0:T(8,128)(2,1)S(1)}, bf16[256,4096]{1,0:T(8,128)(2,1)}, u32[]{:S(2)}) copy-start(bf16[256,4096]{1,0:T(8,128)(2,1)} %param.7) | copy-start | bytes 6291460
  5.7 116.3 %all-to-all-start = ((bf16[16,64,2304]{2,1,0:T(8,128)(2,1)}), bf16[16,64,2304]{2,1,0:T(8,128)(2,1)}, u32[]{:S(2)}, u32[]{:S(2)}) async-start(bf16[16,64,2304]{2,1,0:T(8,128)(2,1)} %copy-done), calls=%async_computation | async-start | bytes 9437184 | tf_op jit(solution)/shard_map/all_to_all | solution.py:146
  15.0 56.4 %collective-permute-start = (bf16[256,1024]{1,0:T(8,128)(2,1)S(1)}, bf16[256,1024]{1,0:T(8,128)(2,1)S(1)}, u32[]{:S(2)}, u32[]{:S(2)}) collective-permute-start(bf16[256,1024]{1,0:T(8,128)(2,1)S(1)} %get-tuple-element.22), channel_id=1, source_target_pairs={{0,16},{16,0},{32,112},{48,96},{64,80},{80,64},{96,48},{112,32},{1... | collective-permute-start | bytes 1572872 | tf_op jit(solution)/shard_map/ppermute | solution.py:138
  71.5 46.0 %collective-permute-start.1 = (bf16[512,1024]{1,0:T(8,128)(2,1)S(1)}, bf16[512,1024]{1,0:T(8,128)(2,1)S(1)}, u32[]{:S(2)}, u32[]{:S(2)}) collective-permute-start(bf16[512,1024]{1,0:T(8,128)(2,1)S(1)} %pad_maximum_fusion), channel_id=1, source_target_pairs={{4,0},{8,4},{12,8},{0,12},{5,1},{9,5},{13,9},{1,13},{6,2},{10,6},{... | collective-permute-start | bytes 3145736 | tf_op jit(solution)/shard_map/ppermute | solution.py:112
  75.6 43.0 %collective-permute-start.2 = (bf16[512,1024]{1,0:T(8,128)(2,1)S(1)}, bf16[512,1024]{1,0:T(8,128)(2,1)S(1)}, u32[]{:S(2)}, u32[]{:S(2)}) collective-permute-start(bf16[512,1024]{1,0:T(8,128)(2,1)S(1)} %pad_maximum_fusion), channel_id=1, source_target_pairs={{8,0},{12,4},{0,8},{4,12},{9,1},{13,5},{1,9},{5,13},{10,2},{14,6},... | collective-permute-start | bytes 3145736 | tf_op jit(solution)/shard_map/ppermute | solution.py:112
  75.6 45.3 %collective-permute-start.3 = (bf16[512,1024]{1,0:T(8,128)(2,1)S(1)}, bf16[512,1024]{1,0:T(8,128)(2,1)S(1)}, u32[]{:S(2)}, u32[]{:S(2)}) collective-permute-start(bf16[512,1024]{1,0:T(8,128)(2,1)S(1)} %pad_maximum_fusion), channel_id=1, source_target_pairs={{12,0},{0,4},{4,8},{8,12},{13,1},{1,5},{5,9},{9,13},{14,2},{2,6},{... | collective-permute-start | bytes 3145736 | tf_op jit(solution)/shard_map/ppermute | solution.py:112
  122.0 30.6 %collective-permute-start.4 = (bf16[2048,1024]{1,0:T(8,128)(2,1)}, bf16[2048,1024]{1,0:T(8,128)(2,1)}, u32[]{:S(2)}, u32[]{:S(2)}) collective-permute-start(bf16[2048,1024]{1,0:T(8,128)(2,1)} %constant_dynamic-update-slice_fusion), channel_id=1, source_target_pairs={{0,32},{32,0},{1,33},{33,1},{2,34},{34,2},{3,35},{35,3},{4,36},{36... | collective-permute-start | bytes 12582920 | tf_op jit(solution)/shard_map/ppermute | solution.py:108
  134.4 12.9 %collective-permute-start.5 = (bf16[256,256]{1,0:T(8,128)(2,1)S(1)}, bf16[256,256]{1,0:T(8,128)(2,1)S(1)}, u32[]{:S(2)}, u32[]{:S(2)}) collective-permute-start(bf16[256,256]{1,0:T(8,128)(2,1)S(1)} %get-tuple-element.15), channel_id=1, source_target_pairs={{12,0},{0,4},{4,8},{8,12},{13,1},{1,5},{5,9},{9,13},{14,2},{2,6},{... | collective-permute-start | bytes 393224 | tf_op jit(solution)/shard_map/ppermute | solution.py:112
  134.5 12.8 %collective-permute-start.6 = (bf16[256,256]{1,0:T(8,128)(2,1)S(1)}, bf16[256,256]{1,0:T(8,128)(2,1)S(1)}, u32[]{:S(2)}, u32[]{:S(2)}) collective-permute-start(bf16[256,256]{1,0:T(8,128)(2,1)S(1)} %get-tuple-element.16), channel_id=1, source_target_pairs={{8,0},{12,4},{0,8},{4,12},{9,1},{13,5},{1,9},{5,13},{10,2},{14,6},... | collective-permute-start | bytes 393224 | tf_op jit(solution)/shard_map/ppermute | solution.py:112
  138.3 8.9 %collective-permute-start.7 = (bf16[256,256]{1,0:T(8,128)(2,1)S(1)}, bf16[256,256]{1,0:T(8,128)(2,1)S(1)}, u32[]{:S(2)}, u32[]{:S(2)}) collective-permute-start(bf16[256,256]{1,0:T(8,128)(2,1)S(1)} %get-tuple-element.17), channel_id=1, source_target_pairs={{4,0},{8,4},{12,8},{0,12},{5,1},{9,5},{13,9},{1,13},{6,2},{10,6},{... | collective-permute-start | bytes 393224 | tf_op jit(solution)/shard_map/ppermute | solution.py:112
  138.3 41.0 %all-to-all-start.1 = ((bf16[16,64,1024]{2,1,0:T(8,128)(2,1)}), bf16[16,64,1024]{2,1,0:T(8,128)(2,1)S(1)}, u32[]{:S(2)}, u32[]{:S(2)}) async-start(bf16[16,64,1024]{2,1,0:T(8,128)(2,1)} %bitcast.19), calls=%async_computation.1 | async-start | bytes 4194304 | tf_op jit(solution)/shard_map/all_to_all | solution.py:153
  147.3 1.6 collective-permute-start.8
  149.0 24.7 %collective-permute-start.9 = (f32[128,256]{1,0:T(8,128)S(1)}, f32[128,256]{1,0:T(8,128)S(1)}, u32[]{:S(2)}, u32[]{:S(2)}) collective-permute-start(f32[128,256]{1,0:T(8,128)S(1)} %constant_dynamic-slice_fusion.2), channel_id=1, source_target_pairs={{0,64},{64,0},{1,65},{65,1},{2,66},{66,2},{3,67},{67,3},{4,68},{68... | collective-permute-start | bytes 393224 | tf_op jit(solution)/shard_map/ppermute | solution.py:108
  179.4 34.5 %all-to-all-start.2 = ((bf16[16,64,1024]{2,1,0:T(8,128)(2,1)}), bf16[16,64,1024]{2,1,0:T(8,128)(2,1)}, u32[]{:S(2)}, u32[]{:S(2)}) async-start(bf16[16,64,1024]{2,1,0:T(8,128)(2,1)} %bitcast.20), calls=%async_computation.2 | async-start | bytes 4194304 | tf_op jit(solution)/shard_map/all_to_all | solution.py:153
  183.8 1.4 collective-permute-start.10

commit v8 on v7

v8 whole, which is shorter than its diff:
```python
import jax
import jax.numpy as jnp
from jax import lax
from jax.experimental import pallas as pl
from jax.experimental.pallas import tpu as pltpu
from jax.sharding import Mesh
from jax.sharding import PartitionSpec as P

BLOCK = 128
SPLIT = (48, 16)
FINE = ("yh", "core", "yl", "z", "x")
PLANE = ("yh", "yl", "x")
F32 = jnp.float32
BF16 = jnp.bfloat16


WHOLE = pl.BlockSpec(memory_space=pltpu.VMEM)
LEFT = pl.BlockSpec(memory_space=pl.ANY)
SCALAR = pl.BlockSpec(memory_space=pltpu.SMEM)


def params():
    return pltpu.CompilerParams(vmem_limit_bytes=16 << 20)


def pack_kernel(z_ref, float_ref, quant_ref, after_ref, *outs):
    width = float_ref.shape[1] // 32
    z = z_ref[0]
    row = 0
    for out_ref in outs:
        rows = slice(row, row + out_ref.shape[1])
        row = rows.stop
        quant = quant_ref[rows, :BLOCK]
        shift = (float_ref[rows, :BLOCK].astype(F32) - quant.astype(F32)).astype(BF16)
        for kind, ref in enumerate((float_ref, quant_ref)):
            for j in range(4):
                zj = lax.rem(z + j, 4)
                for yl in range(2):
                    for x in range(4):
                        start = pl.multiple_of(((yl * 4 + zj) * 4 + x) * width, width)
                        block = ref[rows, pl.ds(start, width)]
                        for half in range(2):
                            at = ((yl ^ half) * 4 + j) * width
                            out_ref[kind * 8 + half * 4 + x, :, at : at + width] = block
        for d in range(16):
            out_ref[d, :, 8 * width : 8 * width + BLOCK] = quant
            out_ref[d, :, 8 * width + BLOCK :] = shift


def pack(z, attn_float, attn_quant, after):
    d_in = attn_float.shape[1]
    return pl.pallas_call(
        pack_kernel,
        out_shape=tuple(
            jax.ShapeDtypeStruct((16, n, d_in // 4 + 2 * BLOCK), BF16) for n in SPLIT
        ),
        in_specs=[SCALAR, WHOLE, WHOLE, LEFT],
        out_specs=(WHOLE,) * len(SPLIT),
        compiler_params=params(),
        name="pack",
    )(z.reshape(1), attn_float, attn_quant, after)


def join_kernel(*refs):
    *parts, out_ref = refs
    row = 0
    for part in parts:
        out_ref[row : row + part.shape[0]] = part[...]
        row += part.shape[0]


def join(parts):
    rows, cols = parts[0].shape
    return pl.pallas_call(
        join_kernel,
        out_shape=jax.ShapeDtypeStruct((len(parts) * rows, cols), BF16),
        in_specs=[WHOLE] * len(parts),
        out_specs=WHOLE,
        compiler_params=params(),
        name="join",
    )(*parts)


def project_kernel(acts_ref, *refs):
    *weights, out_ref = refs
    tile = 256
    depth, width = weights[0].shape
    for q in range(2):
        for row in range(0, out_ref.shape[0], tile):
            rows = slice(row, row + tile)
            total = jnp.dot(
                acts_ref[rows, :depth], weights[2 * q][...], preferred_element_type=F32
            ) + jnp.dot(
                acts_ref[rows, depth : 2 * depth],
                weights[2 * q + 1][...],
                preferred_element_type=F32,
            )
            out_ref[rows, q * width : (q + 1) * width] = total.astype(BF16)


def project(acts, weights):
    rows, (depth, width) = acts.shape[0], weights[0].shape
    return pl.pallas_call(
        project_kernel,
        out_shape=jax.ShapeDtypeStruct((rows, 2 * width), BF16),
        in_specs=[WHOLE] * 5,
        out_specs=WHOLE,
        compiler_params=params(),
        cost_estimate=pl.CostEstimate(
            flops=16 * rows * depth * width, bytes_accessed=16 << 20, transcendentals=0
        ),
        name="project",
    )(acts, *weights)


def stats_kernel(*refs):
    acts, outs = refs[: len(SPLIT)], refs[len(SPLIT) + 1 :]
    width = outs[0].shape[0]
    for j, out in enumerate(outs):
        total = None
        for ref in acts:
            term = lax.dot_general(
                ref[:, j * width : (j + 1) * width],
                ref[:, 8 * width :],
                (((0,), (0,)), ((), ())),
                preferred_element_type=F32,
            )
            total = term if total is None else total + term
        out[...] = total.astype(out.dtype)


def stats(acts, after):
    width = 2 * BLOCK
    return pl.pallas_call(
        stats_kernel,
        out_shape=(jax.ShapeDtypeStruct((width, width), F32),)
        + (jax.ShapeDtypeStruct((width, width), BF16),) * 3,
        in_specs=[WHOLE] * len(acts) + [LEFT],
        out_specs=(WHOLE,) * 4,
        compiler_params=params(),
        name="stats",
    )(*acts, after)


def finish_kernel(core_ref, *refs):
    *parts, float_ref, quant_ref = refs
    core = core_ref[0]
    row = 0
    for ref in parts:
        rows, width = slice(row, row + ref.shape[1]), ref.shape[2] // 2
        row = rows.stop
        for q in range(2):
            quarter = core if q == 0 else 1 - core
            for kind, out in enumerate((float_ref, quant_ref)):
                for half in range(2):
                    at = kind * 8 + half * 4
                    cols = slice(q * width, (q + 1) * width)
                    total = ref[at, :, cols].astype(F32)
                    for x in range(1, 4):
                        total += ref[at + x, :, cols].astype(F32)
                    start = pl.multiple_of((half * 2 + quarter) * width, width)
                    out[rows, pl.ds(start, width)] = total.astype(BF16)


def finish(core, parts):
    tokens = sum(p.shape[1] for p in parts)
    return pl.pallas_call(
        finish_kernel,
        out_shape=(jax.ShapeDtypeStruct((tokens, 2 * parts[0].shape[2]), BF16),) * 2,
        in_specs=[SCALAR] + [WHOLE] * len(parts),
        out_specs=(WHOLE, WHOLE),
        compiler_params=params(),
        name="finish",
    )(core.reshape(1), *parts)


def swap(a, axis):
    return lax.ppermute(a, axis, [(0, 1), (1, 0)])


def ahead(a, axis, j):
    return lax.ppermute(a, axis, [((i + j) % 4, i) for i in range(4)])


def shards(attn_float, attn_quant, proj_weight, weight_codes, group_scales):
    tokens, d_in = attn_float.shape
    features, d_out = proj_weight.shape
    groups = group_scales.shape[0]
    half, quarter = d_out // 2, d_out // 4
    inverse = 1.0 / (tokens * 128)
    yh, core, yl, z = (lax.axis_index(a) for a in ("yh", "core", "yl", "z"))

    def weight(kind, col):
        plain = lax.dynamic_slice_in_dim(proj_weight, col, quarter, 1)
        codes = lax.dynamic_slice_in_dim(weight_codes, col, quarter, 1)
        scales = lax.dynamic_slice_in_dim(group_scales, col, quarter, 1)
        values = (codes - 8).astype(F32).reshape(groups, features // groups, quarter)
        quant = (values * scales[:, None, :]).reshape(features, quarter).astype(BF16)
        return jnp.where(kind == 0, plain, quant)

    own = weight(yh, yl * half + core * quarter)
    send = weight(yh ^ core, (1 - yl) * half + core * quarter)
    pairs = []
    for a in range(2):
        for c in range(2):
            for b in range(2):
                pairs.append((a * 4 + c * 2 + b, (a ^ c) * 4 + c * 2 + (1 - b)))
    got = lax.ppermute(send, ("yh", "core", "yl"), pairs)

    payload1, payload2 = pack(z, attn_float, attn_quant, send)

    def gather(rows):
        parts = join([rows] + [ahead(rows, "z", j) for j in (1, 2, 3)])
        return parts, swap(parts, "core")

    mine_own, other_own = gather(own)
    mine_got, other_got = gather(got)
    weights = (mine_own, mine_got, other_own, other_got)

    def exchange(p):
        return lax.all_to_all(p, PLANE, 0, 0, tiled=True)

    acts1 = exchange(payload1).reshape(16 * SPLIT[0], -1)
    payload2, acts1 = lax.optimization_barrier((payload2, acts1))
    acts2 = exchange(payload2).reshape(16 * SPLIT[1], -1)

    partial1 = project(acts1, weights)
    partial1, acts2 = lax.optimization_barrier((partial1, acts2))
    result1 = exchange(partial1.reshape(16, SPLIT[0], half))
    partial2 = project(acts2, weights)

    blocks = stats((acts1, acts2), partial2)
    total = blocks[0]
    for j in (1, 2, 3):
        total = total + ahead(blocks[j], "z", 4 - j).astype(F32)
    total = (total + swap(total, "core")) * inverse

    piece = swap(lax.dynamic_slice_in_dim(total, core * BLOCK, BLOCK, 0), "yh")
    partial2, piece, result1 = lax.optimization_barrier((partial2, piece, result1))
    result2 = exchange(partial2.reshape(16, SPLIT[1], half))
    again = swap(piece, "core")
    moved = jnp.where(
        core == 0, jnp.concatenate([piece, again]), jnp.concatenate([again, piece])
    )
    total = jnp.where(yh == 1, total, moved)
    float_out, quant_out = finish(core, (result1, result2))
    return float_out, quant_out, total[:, :BLOCK], total[:, BLOCK:]


def solution(mesh):
    fine = Mesh(mesh.devices.reshape(2, 2, 2, 4, 4), FINE)
    rows, tok = P(FINE, None), P(("yl", "z", "x"), None)
    return jax.shard_map(
        shards,
        mesh=fine,
        in_specs=(rows, rows, tok, tok, tok),
        out_specs=(rows, rows, tok, tok),
        check_vma=False,
    )
```

time: 217 us -> 194 us (0.89)
  waiting for transfers between devices: 143 us -> 109 us
  Pallas kernels: 6.46 us -> 25.4 us
  matrix products: 18.6 us -> 0 us
  starting transfers between devices: 35.6 us -> 47.1 us
  local copies, waits for them, and re-layouts: 10.3 us -> 7.44 us
    pallas_call x2 -> x6, Pallas kernels: 3.37 us -> 23 us  [the longest x2 16.2 us: project(): pl.pallas_call(project_kernel, out_shape=jax.ShapeDtypeStruct((rows, 2 *...]
    dot_general x2 -> x0, matrix products: 18.6 us -> none  [part(): jnp.dot(acts[:, :8 * features], w, preferred_element_type=F32).astype(BF16)]
    ppermute x6 -> x9, waiting for transfers between devices: 40.3 us -> 22 us  [ahead(): return lax.ppermute(a, axis, [((i + j) % 4, i) for i in range(4)])]
    ppermute x1, waiting for transfers between devices: 54.5 us -> 37.4 us  [shards(): got = lax.ppermute(send, ('yh', 'core', 'yl'), pairs)]
    ppermute x6 -> x9, starting transfers between devices: 9.31 us -> 18.1 us  [ahead(): return lax.ppermute(a, axis, [((i + j) % 4, i) for i in range(4)])]
    all_to_all x3 -> x4, starting transfers between devices: 20.6 us -> 23.8 us  [exchange(): return lax.all_to_all(p, PLANE, 0, 0, tiled=True)]
    unnamed x14 -> x16, local copies, waits for them, and re-layouts: 8.45 us -> 5.98 us
    ppermute x4 -> x5, waiting for transfers between devices: 14.7 us -> 16 us  [swap(): return lax.ppermute(a, axis, [(0, 1), (1, 0)])]
  transfers between devices with their start and end apart: 14 -> 19, of which waited for: 8 -> 12; matrix products, arithmetic and copies ran while one was open for 12% -> 0% of each run, Pallas kernels for 1% -> 11%
where the time goes in v8:
time: 194 us; the launch traced here: 193 us
  waiting for transfers between devices  109 us (56%)
  starting transfers between devices  47.1 us (24%)
  Pallas kernels  25.4 us (13%)
  local copies, waits for them, and re-layouts  7.44 us (4%)
  other arithmetic  3.33 us (2%)
    ppermute x1, waiting for transfers between devices, shards(): got = lax.ppermute(send, ('yh', 'core', 'yl'), pairs)  37.4 us
    all_to_all x4, waiting for transfers between devices, exchange(): return lax.all_to_all(p, PLANE, 0, 0, tiled=True)  33.9 us
    all_to_all x4, starting transfers between devices, exchange(): return lax.all_to_all(p, PLANE, 0, 0, tiled=True)  23.8 us
    ppermute x9, waiting for transfers between devices, ahead(): return lax.ppermute(a, axis, [((i + j) % 4, i) for i in range(4)])  22 us
    ppermute x9, starting transfers between devices, ahead(): return lax.ppermute(a, axis, [((i + j) % 4, i) for i in range(4)])  18.1 us
    pallas_call x2, Pallas kernels, project(): pl.pallas_call(project_kernel, out_shape=jax.ShapeDtypeStruct((rows, 2 *...  16.2 us
    ppermute x5, waiting for transfers between devices, swap(): return lax.ppermute(a, axis, [(0, 1), (1, 0)])  16 us
    unnamed x16, local copies, waits for them, and re-layouts  5.98 us
  transfers between devices with their start and end apart: 19, of which 12 were waited for; matrix products, arithmetic and copies ran while one was open for 0% of the time, Pallas kernels for 11%

profile of v8, /device:TPU:0, one launch (start us, length us, event | category | flops | bytes accessed | tf_op | source)
XLA Modules:
  0.0 193.4 jit_solution(14787525266952895241)
XLA Ops:
  1.4 3.2 %fusion.3 = (bf16[256,1024]{1,0:T(8,128)(2,1)}, bf16[256,1024]{1,0:T(8,128)(2,1)S(1)}) fusion(s32[256,4096]{1,0:T(8,128)} %param.8, s32[]{:T(128)S(6)} %select_n.45, f32[2,1024]{1,0:T(2,128)S(1)} %get-tuple-element.38, bf16[256,4096]{1,0:T(8,128)(2,1)} %param.7, pred[]{:T(512)S(6)} %eq.13, f32[2,1024]{1,0:T(2,128)S(1)} %get-tuple-element.39, ...), kind=kLoop, calls=%fused_computation.5 | loop fusion | flops 2621440 | bytes 4210698 | tf_op jit(solution)/shard_map/jit(_where)/select_n | solution.py:199
  5.4 1.8 copy-done.1
  8.2 7.1 %all-to-all-start = ((bf16[16,48,2304]{2,1,0:T(8,128)(2,1)}), bf16[16,48,2304]{2,1,0:T(8,128)(2,1)S(1)}, u32[]{:S(2)}, u32[]{:S(2)}) async-start(bf16[16,48,2304]{2,1,0:T(8,128)(2,1)} %copy-done.1), calls=%async_computation | async-start | bytes 7077888 | tf_op jit(solution)/shard_map/all_to_all | solution.py:221
  15.3 1.9 collective-permute-start.3
  17.2 1.9 collective-permute-start.2
  19.2 3.6 %collective-permute-start.1 = (bf16[256,1024]{1,0:T(8,128)(2,1)}, bf16[256,1024]{1,0:T(8,128)(2,1)S(1)}, u32[]{:S(2)}, u32[]{:S(2)}) collective-permute-start(bf16[256,1024]{1,0:T(8,128)(2,1)} %get-tuple-element.34.refs_0_), channel_id=1, source_target_pairs={{8,0},{12,4},{0,8},{4,12},{9,1},{13,5},{1,9},{5,13},{10,2},{14,6},... | collective-permute-start | bytes 1572872 | tf_op jit(solution)/shard_map/ppermute | solution.py:182
  23.7 37.4 %collective-permute-done.3.refs_0_ = bf16[256,1024]{1,0:T(8,128)(2,1)S(1)} collective-permute-done((bf16[256,1024]{1,0:T(8,128)(2,1)}, bf16[256,1024]{1,0:T(8,128)(2,1)S(1)}, u32[]{:S(2)}, u32[]{:S(2)}) %collective-permute-start.3) | collective-permute-done | bytes 524320 | tf_op jit(solution)/shard_map/ppermute | solution.py:208
  61.1 1.9 collective-permute-start.6
  63.1 3.6 %collective-permute-start.5 = (bf16[256,1024]{1,0:T(8,128)(2,1)S(1)}, bf16[256,1024]{1,0:T(8,128)(2,1)S(1)}, u32[]{:S(2)}, u32[]{:S(2)}) collective-permute-start(bf16[256,1024]{1,0:T(8,128)(2,1)S(1)} %collective-permute-done.3.refs_0_), channel_id=1, source_target_pairs={{8,0},{12,4},{0,8},{4,12},{9,1},{13,5},{1,9},{5,13},{10,2},{14,6},... | collective-permute-start | bytes 1572872 | tf_op jit(solution)/shard_map/ppermute | solution.py:182
  68.7 1.5 join.2.refs_0_
  70.2 6.9 %collective-permute-done.6.refs_3_ = bf16[256,1024]{1,0:T(8,128)(2,1)S(1)} collective-permute-done((bf16[256,1024]{1,0:T(8,128)(2,1)S(1)}, bf16[256,1024]{1,0:T(8,128)(2,1)S(1)}, u32[]{:S(2)}, u32[]{:S(2)}) %collective-permute-start.6) | collective-permute-done | bytes 524320 | tf_op jit(solution)/shard_map/ppermute | solution.py:182
  77.1 10.6 %collective-permute-done.5.refs_2_ = bf16[256,1024]{1,0:T(8,128)(2,1)S(1)} collective-permute-done((bf16[256,1024]{1,0:T(8,128)(2,1)S(1)}, bf16[256,1024]{1,0:T(8,128)(2,1)S(1)}, u32[]{:S(2)}, u32[]{:S(2)}) %collective-permute-start.5) | collective-permute-done | bytes 524320 | tf_op jit(solution)/shard_map/ppermute | solution.py:182
  87.7 1.5 join.3.refs_1_
  89.2 7.9 %all-to-all-start.1 = ((bf16[16,16,2304]{2,1,0:T(8,128)(2,1)}), bf16[16,16,2304]{2,1,0:T(8,128)(2,1)}, u32[]{:S(2)}, u32[]{:S(2)}) async-start(bf16[16,16,2304]{2,1,0:T(8,128)(2,1)} %copy-done.5), calls=%async_computation.1 | async-start | bytes 2359296 | tf_op jit(solution)/shard_map/all_to_all | solution.py:221
  97.2 10.1 %project.2 = bf16[768,2048]{1,0:T(8,128)(2,1)S(1)} custom-call(bf16[768,2304]{1,0:T(8,128)(2,1)S(1)} %bitcast.18, bf16[1024,1024]{1,0:T(8,128)(2,1)} %join.2.refs_0_, bf16[1024,1024]{1,0:T(8,128)(2,1)} %join.3.refs_1_, bf16[1024,1024]{1,0:T(8,128)(2,1)} %collective-permute-done.7.refs_2_, bf16[1024,1024]{1,0:T(8,128)(2,1)} %collective-permute-done.8.refs_3_), custom_call_target="tpu_custom_call" | custom-call | flops 12884901888 | bytes 16777216 | tf_op jit(solution)/shard_map/project/pallas_call | solution.py:103
  107.3 1.7 copy-done.2
  109.0 8.9 %all-to-all-done.1 = bf16[16,16,2304]{2,1,0:T(8,128)(2,1)} async-done(((bf16[16,16,2304]{2,1,0:T(8,128)(2,1)}), bf16[16,16,2304]{2,1,0:T(8,128)(2,1)}, u32[]{:S(2)}, u32[]{:S(2)}) %all-to-all-start.1) | async-done | bytes 1179680 | tf_op jit(solution)/shard_map/all_to_all | solution.py:221
  118.0 4.5 %all-to-all-start.2 = ((bf16[16,48,2048]{2,1,0:T(8,128)(2,1)}), bf16[16,48,2048]{2,1,0:T(8,128)(2,1)}, u32[]{:S(2)}, u32[]{:S(2)}) async-start(bf16[16,48,2048]{2,1,0:T(8,128)(2,1)} %bitcast.21), calls=%async_computation.2 | async-start | bytes 6291456 | tf_op jit(solution)/shard_map/all_to_all | solution.py:221
  122.4 6.1 %project.3.refs_2_ = bf16[256,2048]{1,0:T(8,128)(2,1)S(1)} custom-call(bf16[256,2304]{1,0:T(8,128)(2,1)} %bitcast.5.acts_ref.refs_1_, bf16[1024,1024]{1,0:T(8,128)(2,1)} %join.2.refs_0_, bf16[1024,1024]{1,0:T(8,128)(2,1)} %join.3.refs_1_, bf16[1024,1024]{1,0:T(8,128)(2,1)} %collective-permute-done.7.refs_2_, bf16[1024,1024]{1,0:T(8,128)(2,1)} %collective-permute-done.8.refs_3_), custom_call_target="tpu_custom_call" | custom-call | flops 4294967296 | bytes 16777216 | tf_op jit(solution)/shard_map/project/pallas_call | solution.py:103
  128.6 2.4 %stats.1 = (f32[256,256]{1,0:T(8,128)S(1)}, bf16[256,256]{1,0:T(8,128)(2,1)S(1)}, bf16[256,256]{1,0:T(8,128)(2,1)S(1)}, bf16[256,256]{1,0:T(8,128)(2,1)S(1)}) custom-call(bf16[768,2304]{1,0:T(8,128)(2,1)S(1)} %bitcast.19, bf16[256,2304]{1,0:T(8,128)(2,1)} %bitcast.5.acts_ref.refs_1_, bf16[256,2048]{1,0:T(8,128)(2,1)S(1)} %project.3.refs_2_), custom_call_target="tpu_custom_call" | custom-call | tf_op jit(solution)/shard_map/stats/pallas_call | solution.py:134
  131.0 1.4 collective-permute-start.9
  132.4 2.4 %collective-permute-start.10 = (bf16[256,256]{1,0:T(8,128)(2,1)S(1)}, bf16[256,256]{1,0:T(8,128)(2,1)S(1)}, u32[]{:S(2)}, u32[]{:S(2)}) collective-permute-start(bf16[256,256]{1,0:T(8,128)(2,1)S(1)} %get-tuple-element.26), channel_id=1, source_target_pairs={{8,0},{12,4},{0,8},{4,12},{9,1},{13,5},{1,9},{5,13},{10,2},{14,6},... | collective-permute-start | bytes 393224 | tf_op jit(solution)/shard_map/ppermute | solution.py:182
  134.8 1.4 collective-permute-start.11
  136.1 2.7 %collective-permute-done.9 = bf16[256,256]{1,0:T(8,128)(2,1)S(1)} collective-permute-done((bf16[256,256]{1,0:T(8,128)(2,1)S(1)}, bf16[256,256]{1,0:T(8,128)(2,1)S(1)}, u32[]{:S(2)}, u32[]{:S(2)}) %collective-permute-start.9) | collective-permute-done | bytes 131104 | tf_op jit(solution)/shard_map/ppermute | solution.py:182
  138.9 1.5 collective-permute-done.10
  140.8 1.5 collective-permute-done.12
  142.4 3.1 %collective-permute-start.13 = (f32[128,256]{1,0:T(8,128)S(1)}, f32[128,256]{1,0:T(8,128)S(1)}, u32[]{:S(2)}, u32[]{:S(2)}) collective-permute-start(f32[128,256]{1,0:T(8,128)S(1)} %constant_dynamic-slice_fusion.2), channel_id=1, source_target_pairs={{0,64},{64,0},{1,65},{65,1},{2,66},{66,2},{3,67},{67,3},{4,68},{68... | collective-permute-start | bytes 393224 | tf_op jit(solution)/shard_map/ppermute | solution.py:178
  145.5 13.1 %collective-permute-done.13 = f32[128,256]{1,0:T(8,128)S(1)} collective-permute-done((f32[128,256]{1,0:T(8,128)S(1)}, f32[128,256]{1,0:T(8,128)S(1)}, u32[]{:S(2)}, u32[]{:S(2)}) %collective-permute-start.13) | collective-permute-done | bytes 131104 | tf_op jit(solution)/shard_map/ppermute | solution.py:178
  158.6 10.9 %all-to-all-done.2.refs_0_ = bf16[16,48,2048]{2,1,0:T(8,128)(2,1)} async-done(((bf16[16,48,2048]{2,1,0:T(8,128)(2,1)}), bf16[16,48,2048]{2,1,0:T(8,128)(2,1)}, u32[]{:S(2)}, u32[]{:S(2)}) %all-to-all-start.2) | async-done | bytes 3145760 | tf_op jit(solution)/shard_map/all_to_all | solution.py:221
  169.5 4.3 %all-to-all-start.3 = ((bf16[16,16,2048]{2,1,0:T(8,128)(2,1)}), bf16[16,16,2048]{2,1,0:T(8,128)(2,1)S(1)}, u32[]{:S(2)}, u32[]{:S(2)}) async-start(bf16[16,16,2048]{2,1,0:T(8,128)(2,1)} %bitcast.20), calls=%async_computation.3 | async-start | bytes 2097152 | tf_op jit(solution)/shard_map/all_to_all | solution.py:221
  176.0 14.1 %all-to-all-done.3.refs_1_ = bf16[16,16,2048]{2,1,0:T(8,128)(2,1)S(1)} async-done(((bf16[16,16,2048]{2,1,0:T(8,128)(2,1)}), bf16[16,16,2048]{2,1,0:T(8,128)(2,1)S(1)}, u32[]{:S(2)}, u32[]{:S(2)}) %all-to-all-start.3) | async-done | bytes 1048608 | tf_op jit(solution)/shard_map/all_to_all | solution.py:221
  190.0 3.3 %finish.1 = (bf16[64,4096]{1,0:T(8,128)(2,1)}, bf16[64,4096]{1,0:T(8,128)(2,1)}) custom-call(s32[1]{0:T(128)} %bitcast.core_ref, bf16[16,48,2048]{2,1,0:T(8,128)(2,1)} %all-to-all-done.2.refs_0_, bf16[16,16,2048]{2,1,0:T(8,128)(2,1)S(1)} %all-to-all-done.3.refs_1_), custom_call_target="tpu_custom_call" | custom-call | tf_op jit(solution)/shard_map/finish/pallas_call | solution.py:167
  (36 shorter events, 8.3 us)
Async XLA Ops:
  1.4 3.2 %copy-start.6 = (bf16[64,8192]{1,0:T(8,128)(2,1)S(1)}, bf16[64,8192]{1,0:T(8,128)(2,1)}, u32[]{:S(2)}) copy-start(bf16[64,8192]{1,0:T(8,128)(2,1)} %float_ref.1) | copy-start | bytes 3145732
  1.4 3.2 %copy-start.7 = (bf16[64,8192]{1,0:T(8,128)(2,1)S(1)}, bf16[64,8192]{1,0:T(8,128)(2,1)}, u32[]{:S(2)}) copy-start(bf16[64,8192]{1,0:T(8,128)(2,1)} %quant_ref.1) | copy-start | bytes 3145732
  4.6 0.8 copy-start.3
  5.4 1.8 copy-start.1
  7.1 1.0 copy-start.5
  8.2 81.0 %all-to-all-start = ((bf16[16,48,2304]{2,1,0:T(8,128)(2,1)}), bf16[16,48,2304]{2,1,0:T(8,128)(2,1)S(1)}, u32[]{:S(2)}, u32[]{:S(2)}) async-start(bf16[16,48,2304]{2,1,0:T(8,128)(2,1)} %copy-done.1), calls=%async_computation | async-start | bytes 7077888 | tf_op jit(solution)/shard_map/all_to_all | solution.py:221
  15.3 45.8 %collective-permute-start.3 = (bf16[256,1024]{1,0:T(8,128)(2,1)}, bf16[256,1024]{1,0:T(8,128)(2,1)S(1)}, u32[]{:S(2)}, u32[]{:S(2)}) collective-permute-start(bf16[256,1024]{1,0:T(8,128)(2,1)} %copy-done.3), channel_id=1, source_target_pairs={{0,16},{16,0},{32,112},{48,96},{64,80},{80,64},{96,48},{112,32},{1... | collective-permute-start | bytes 1572872 | tf_op jit(solution)/shard_map/ppermute | solution.py:208
  17.2 49.4 %collective-permute-start.2 = (bf16[256,1024]{1,0:T(8,128)(2,1)}, bf16[256,1024]{1,0:T(8,128)(2,1)S(1)}, u32[]{:S(2)}, u32[]{:S(2)}) collective-permute-start(bf16[256,1024]{1,0:T(8,128)(2,1)} %get-tuple-element.34.refs_0_), channel_id=1, source_target_pairs={{12,0},{0,4},{4,8},{8,12},{13,1},{1,5},{5,9},{9,13},{14,2},{2,6},{... | collective-permute-start | bytes 1572872 | tf_op jit(solution)/shard_map/ppermute | solution.py:182
  19.2 48.5 %collective-permute-start.1 = (bf16[256,1024]{1,0:T(8,128)(2,1)}, bf16[256,1024]{1,0:T(8,128)(2,1)S(1)}, u32[]{:S(2)}, u32[]{:S(2)}) collective-permute-start(bf16[256,1024]{1,0:T(8,128)(2,1)} %get-tuple-element.34.refs_0_), channel_id=1, source_target_pairs={{8,0},{12,4},{0,8},{4,12},{9,1},{13,5},{1,9},{5,13},{10,2},{14,6},... | collective-permute-start | bytes 1572872 | tf_op jit(solution)/shard_map/ppermute | solution.py:182
  22.7 44.9 %collective-permute-start = (bf16[256,1024]{1,0:T(8,128)(2,1)}, bf16[256,1024]{1,0:T(8,128)(2,1)S(1)}, u32[]{:S(2)}, u32[]{:S(2)}) collective-permute-start(bf16[256,1024]{1,0:T(8,128)(2,1)} %get-tuple-element.34.refs_0_), channel_id=1, source_target_pairs={{4,0},{8,4},{12,8},{0,12},{5,1},{9,5},{13,9},{1,13},{6,2},{10,6},{... | collective-permute-start | bytes 1572872 | tf_op jit(solution)/shard_map/ppermute | solution.py:182
  61.1 16.0 %collective-permute-start.6 = (bf16[256,1024]{1,0:T(8,128)(2,1)S(1)}, bf16[256,1024]{1,0:T(8,128)(2,1)S(1)}, u32[]{:S(2)}, u32[]{:S(2)}) collective-permute-start(bf16[256,1024]{1,0:T(8,128)(2,1)S(1)} %collective-permute-done.3.refs_0_), channel_id=1, source_target_pairs={{12,0},{0,4},{4,8},{8,12},{13,1},{1,5},{5,9},{9,13},{14,2},{2,6},{... | collective-permute-start | bytes 1572872 | tf_op jit(solution)/shard_map/ppermute | solution.py:182
  63.1 24.6 %collective-permute-start.5 = (bf16[256,1024]{1,0:T(8,128)(2,1)S(1)}, bf16[256,1024]{1,0:T(8,128)(2,1)S(1)}, u32[]{:S(2)}, u32[]{:S(2)}) collective-permute-start(bf16[256,1024]{1,0:T(8,128)(2,1)S(1)} %collective-permute-done.3.refs_0_), channel_id=1, source_target_pairs={{8,0},{12,4},{0,8},{4,12},{9,1},{13,5},{1,9},{5,13},{10,2},{14,6},... | collective-permute-start | bytes 1572872 | tf_op jit(solution)/shard_map/ppermute | solution.py:182
  66.7 21.1 %collective-permute-start.4 = (bf16[256,1024]{1,0:T(8,128)(2,1)S(1)}, bf16[256,1024]{1,0:T(8,128)(2,1)S(1)}, u32[]{:S(2)}, u32[]{:S(2)}) collective-permute-start(bf16[256,1024]{1,0:T(8,128)(2,1)S(1)} %collective-permute-done.3.refs_0_), channel_id=1, source_target_pairs={{4,0},{8,4},{12,8},{0,12},{5,1},{9,5},{13,9},{1,13},{6,2},{10,6},{... | collective-permute-start | bytes 1572872 | tf_op jit(solution)/shard_map/ppermute | solution.py:182
  67.7 1.0 copy-start.4
  70.2 26.9 %collective-permute-start.7 = (bf16[1024,1024]{1,0:T(8,128)(2,1)}, bf16[1024,1024]{1,0:T(8,128)(2,1)}, u32[]{:S(2)}, u32[]{:S(2)}) collective-permute-start(bf16[1024,1024]{1,0:T(8,128)(2,1)} %join.2.refs_0_), channel_id=1, source_target_pairs={{0,32},{32,0},{1,33},{33,1},{2,34},{34,2},{3,35},{35,3},{4,36},{36... | collective-permute-start | bytes 6291464 | tf_op jit(solution)/shard_map/ppermute | solution.py:178
  89.2 8.0 %collective-permute-start.8 = (bf16[1024,1024]{1,0:T(8,128)(2,1)}, bf16[1024,1024]{1,0:T(8,128)(2,1)}, u32[]{:S(2)}, u32[]{:S(2)}) collective-permute-start(bf16[1024,1024]{1,0:T(8,128)(2,1)} %join.3.refs_1_), channel_id=1, source_target_pairs={{0,32},{32,0},{1,33},{33,1},{2,34},{34,2},{3,35},{35,3},{4,36},{36... | collective-permute-start | bytes 6291464 | tf_op jit(solution)/shard_map/ppermute | solution.py:178
  89.2 28.7 %all-to-all-start.1 = ((bf16[16,16,2304]{2,1,0:T(8,128)(2,1)}), bf16[16,16,2304]{2,1,0:T(8,128)(2,1)}, u32[]{:S(2)}, u32[]{:S(2)}) async-start(bf16[16,16,2304]{2,1,0:T(8,128)(2,1)} %copy-done.5), calls=%async_computation.1 | async-start | bytes 2359296 | tf_op jit(solution)/shard_map/all_to_all | solution.py:221
  107.3 1.7 copy-start.2
  118.0 51.5 %all-to-all-start.2 = ((bf16[16,48,2048]{2,1,0:T(8,128)(2,1)}), bf16[16,48,2048]{2,1,0:T(8,128)(2,1)}, u32[]{:S(2)}, u32[]{:S(2)}) async-start(bf16[16,48,2048]{2,1,0:T(8,128)(2,1)} %bitcast.21), calls=%async_computation.2 | async-start | bytes 6291456 | tf_op jit(solution)/shard_map/all_to_all | solution.py:221
  128.6 2.4 %copy-start = (bf16[256,2048]{1,0:T(8,128)(2,1)}, bf16[256,2048]{1,0:T(8,128)(2,1)S(1)}, u32[]{:S(2)}) copy-start(bf16[256,2048]{1,0:T(8,128)(2,1)S(1)} %project.3.refs_2_) | copy-start | bytes 3145732
  131.0 7.8 %collective-permute-start.9 = (bf16[256,256]{1,0:T(8,128)(2,1)S(1)}, bf16[256,256]{1,0:T(8,128)(2,1)S(1)}, u32[]{:S(2)}, u32[]{:S(2)}) collective-permute-start(bf16[256,256]{1,0:T(8,128)(2,1)S(1)} %get-tuple-element.25), channel_id=1, source_target_pairs={{12,0},{0,4},{4,8},{8,12},{13,1},{1,5},{5,9},{9,13},{14,2},{2,6},{... | collective-permute-start | bytes 393224 | tf_op jit(solution)/shard_map/ppermute | solution.py:182
  132.4 7.9 %collective-permute-start.10 = (bf16[256,256]{1,0:T(8,128)(2,1)S(1)}, bf16[256,256]{1,0:T(8,128)(2,1)S(1)}, u32[]{:S(2)}, u32[]{:S(2)}) collective-permute-start(bf16[256,256]{1,0:T(8,128)(2,1)S(1)} %get-tuple-element.26), channel_id=1, source_target_pairs={{8,0},{12,4},{0,8},{4,12},{9,1},{13,5},{1,9},{5,13},{10,2},{14,6},... | collective-permute-start | bytes 393224 | tf_op jit(solution)/shard_map/ppermute | solution.py:182
  134.8 5.9 %collective-permute-start.11 = (bf16[256,256]{1,0:T(8,128)(2,1)S(1)}, bf16[256,256]{1,0:T(8,128)(2,1)S(1)}, u32[]{:S(2)}, u32[]{:S(2)}) collective-permute-start(bf16[256,256]{1,0:T(8,128)(2,1)S(1)} %get-tuple-element.27), channel_id=1, source_target_pairs={{4,0},{8,4},{12,8},{0,12},{5,1},{9,5},{13,9},{1,13},{6,2},{10,6},{... | collective-permute-start | bytes 393224 | tf_op jit(solution)/shard_map/ppermute | solution.py:182
  140.7 1.6 collective-permute-start.12
  142.4 16.2 %collective-permute-start.13 = (f32[128,256]{1,0:T(8,128)S(1)}, f32[128,256]{1,0:T(8,128)S(1)}, u32[]{:S(2)}, u32[]{:S(2)}) collective-permute-start(f32[128,256]{1,0:T(8,128)S(1)} %constant_dynamic-slice_fusion.2), channel_id=1, source_target_pairs={{0,64},{64,0},{1,65},{65,1},{2,66},{66,2},{3,67},{67,3},{4,68},{68... | collective-permute-start | bytes 393224 | tf_op jit(solution)/shard_map/ppermute | solution.py:178
  169.5 20.5 %all-to-all-start.3 = ((bf16[16,16,2048]{2,1,0:T(8,128)(2,1)}), bf16[16,16,2048]{2,1,0:T(8,128)(2,1)S(1)}, u32[]{:S(2)}, u32[]{:S(2)}) async-start(bf16[16,16,2048]{2,1,0:T(8,128)(2,1)} %bitcast.20), calls=%async_computation.3 | async-start | bytes 2097152 | tf_op jit(solution)/shard_map/all_to_all | solution.py:221
  173.8 1.4 collective-permute-start.14

commit v9 on v7

v9 whole, which is shorter than its diff:
```python
import functools

import jax
import jax.numpy as jnp
from jax import lax
from jax.experimental import pallas as pl
from jax.experimental.pallas import tpu as pltpu
from jax.sharding import Mesh
from jax.sharding import PartitionSpec as P

BLOCK = 128
GROUPS = (
    ((0, 1), (0, 3), (1, 0), (3, 0)),
    ((1, 1), (3, 3), (1, 3), (3, 1)),
    ((1, 2), (3, 2), (2, 1), (2, 3)),
    ((0, 2), (2, 0), (2, 2), (0, 0)),
)
FINE = ("yh", "core", "yl", "z", "x")
PLANE = ("yh", "yl", "x")
F32 = jnp.float32
BF16 = jnp.bfloat16


WHOLE = pl.BlockSpec(memory_space=pltpu.VMEM)
LEFT = pl.BlockSpec(memory_space=pl.ANY)
SCALAR = pl.BlockSpec(memory_space=pltpu.SMEM)


def params():
    return pltpu.CompilerParams(vmem_limit_bytes=16 << 20)


def pack_kernel(z_ref, float_ref, quant_ref, after_ref, out_ref):
    width = float_ref.shape[1] // 32
    z = z_ref[0]
    quant = quant_ref[:, :BLOCK]
    shift = (float_ref[:, :BLOCK].astype(F32) - quant.astype(F32)).astype(BF16)
    for kind, ref in enumerate((float_ref, quant_ref)):
        for j in range(4):
            zj = lax.rem(z + j, 4)
            for yl in range(2):
                for x in range(4):
                    start = pl.multiple_of(((yl * 4 + zj) * 4 + x) * width, width)
                    block = ref[:, pl.ds(start, width)]
                    for half in range(2):
                        at = ((yl ^ half) * 4 + j) * width
                        out_ref[kind * 8 + half * 4 + x, :, at : at + width] = block
    for d in range(16):
        out_ref[d, :, 8 * width : 8 * width + BLOCK] = quant
        out_ref[d, :, 8 * width + BLOCK :] = shift


def pack(z, attn_float, attn_quant, after):
    tokens, d_in = attn_float.shape
    return pl.pallas_call(
        pack_kernel,
        out_shape=jax.ShapeDtypeStruct((16, tokens, d_in // 4 + 2 * BLOCK), BF16),
        in_specs=[SCALAR, WHOLE, WHOLE, LEFT],
        out_specs=WHOLE,
        compiler_params=params(),
        name="pack",
    )(z.reshape(1), attn_float, attn_quant, after)


def join_kernel(*refs):
    *parts, out_ref = refs
    row = 0
    for part in parts:
        out_ref[row : row + part.shape[0]] = part[...]
        row += part.shape[0]


def join(parts):
    rows, cols = parts[0].shape
    return pl.pallas_call(
        join_kernel,
        out_shape=jax.ShapeDtypeStruct((len(parts) * rows, cols), BF16),
        in_specs=[WHOLE] * len(parts),
        out_specs=WHOLE,
        compiler_params=params(),
        name="join",
    )(*parts)


def project_kernel(group, at_ref, acts_ref, *refs):
    weights, outs, rows_ref, part_ref = refs[:4], refs[-6:-2], refs[-2], refs[-1]
    y, x = at_ref[0], at_ref[1]
    depth, width = weights[0].shape
    tokens = outs[0].shape[0]
    for n, (dy, dx) in enumerate(group):
        start = (lax.rem(y + dy, 4) * 4 + lax.rem(x + dx, 4)) * tokens
        rows_ref[n * tokens : (n + 1) * tokens] = acts_ref[
            pl.ds(pl.multiple_of(start, tokens), tokens), : 2 * depth
        ]
    for q in range(2):
        cols = slice(q * width, (q + 1) * width)
        total = jnp.dot(
            rows_ref[:, :depth], weights[2 * q][...], preferred_element_type=F32
        ) + jnp.dot(rows_ref[:, depth:], weights[2 * q + 1][...], preferred_element_type=F32)
        part_ref[...] = total.astype(BF16)
        for n, out in enumerate(outs):
            out[:, cols] = part_ref[n * tokens : (n + 1) * tokens]


def project(group, at, acts, weights, after):
    depth, width = weights[0].shape
    tokens = acts.shape[0] // 16
    return pl.pallas_call(
        functools.partial(project_kernel, group),
        out_shape=(jax.ShapeDtypeStruct((tokens, 2 * width), BF16),) * 4,
        in_specs=[SCALAR] + [WHOLE] * 5 + [LEFT] * len(after),
        out_specs=(WHOLE,) * 4,
        scratch_shapes=[
            pltpu.VMEM((4 * tokens, 2 * depth), BF16),
            pltpu.VMEM((4 * tokens, width), BF16),
        ],
        compiler_params=params(),
        cost_estimate=pl.CostEstimate(
            flops=32 * tokens * depth * width, bytes_accessed=10 << 20, transcendentals=0
        ),
        name="project",
    )(at, acts, *weights, *after)


def stats_kernel(acts_ref, after_ref, *outs):
    width = outs[0].shape[0]
    for j, out in enumerate(outs):
        out[...] = lax.dot_general(
            acts_ref[:, j * width : (j + 1) * width],
            acts_ref[:, 8 * width :],
            (((0,), (0,)), ((), ())),
            preferred_element_type=F32,
        ).astype(out.dtype)


def stats(acts, after):
    width = 2 * BLOCK
    return pl.pallas_call(
        stats_kernel,
        out_shape=(jax.ShapeDtypeStruct((width, width), F32),)
        + (jax.ShapeDtypeStruct((width, width), BF16),) * 3,
        in_specs=[WHOLE, LEFT],
        out_specs=(WHOLE,) * 4,
        compiler_params=params(),
        name="stats",
    )(acts, after)


def finish_kernel(at_ref, *refs):
    parts, outs = refs[:16], refs[16:]
    y, core = at_ref[0], at_ref[1]
    width = parts[0].shape[1] // 2
    for dy in range(4):
        source = lax.rem(y + 4 - dy, 4)
        for q in range(2):
            cols = slice(q * width, (q + 1) * width)
            quarter = core if q == 0 else 1 - core
            start = pl.multiple_of(((source & 1) * 2 + quarter) * width, width)
            total = parts[4 * dy][:, cols].astype(F32)
            for dx in range(1, 4):
                total += parts[4 * dy + dx][:, cols].astype(F32)
            total = total.astype(BF16)
            for kind, out in enumerate(outs):

                @pl.when((source >> 1) == kind)
                def _(out=out, start=start, total=total):
                    out[:, pl.ds(start, width)] = total


def finish(at, parts):
    tokens, width = parts[0].shape
    return pl.pallas_call(
        finish_kernel,
        out_shape=(jax.ShapeDtypeStruct((tokens, 2 * width), BF16),) * 2,
        in_specs=[SCALAR] + [WHOLE] * 16,
        out_specs=(WHOLE, WHOLE),
        compiler_params=params(),
        name="finish",
    )(at, *parts)


def swap(a, axis):
    return lax.ppermute(a, axis, [(0, 1), (1, 0)])


def ahead(a, axis, j):
    return lax.ppermute(a, axis, [((i + j) % 4, i) for i in range(4)])


def shards(attn_float, attn_quant, proj_weight, weight_codes, group_scales):
    tokens, d_in = attn_float.shape
    features, d_out = proj_weight.shape
    groups = group_scales.shape[0]
    half, quarter = d_out // 2, d_out // 4
    inverse = 1.0 / (tokens * 128)
    yh, core, yl, z = (lax.axis_index(a) for a in ("yh", "core", "yl", "z"))

    def weight(kind, col):
        plain = lax.dynamic_slice_in_dim(proj_weight, col, quarter, 1)
        codes = lax.dynamic_slice_in_dim(weight_codes, col, quarter, 1)
        scales = lax.dynamic_slice_in_dim(group_scales, col, quarter, 1)
        values = (codes - 8).astype(F32).reshape(groups, features // groups, quarter)
        quant = (values * scales[:, None, :]).reshape(features, quarter).astype(BF16)
        return jnp.where(kind == 0, plain, quant)

    send = weight(yh ^ core, (1 - yl) * half + core * quarter)
    pairs = []
    for a in range(2):
        for c in range(2):
            for b in range(2):
                pairs.append((a * 4 + c * 2 + b, (a ^ c) * 4 + c * 2 + (1 - b)))
    got = lax.ppermute(send, ("yh", "core", "yl"), pairs)
    col, send = lax.optimization_barrier((yl * half + core * quarter, send))
    own = weight(yh, col)

    payload = pack(z, attn_float, attn_quant, send)
    payload, got = lax.optimization_barrier((payload, got))

    def gather(rows):
        parts = join([rows] + [ahead(rows, "z", j) for j in (1, 2, 3)])
        return parts, swap(parts, "core")

    mine_own, other_own = gather(own)
    mine_got, other_got = gather(got)
    weights = (mine_own, mine_got, other_own, other_got)

    acts = lax.all_to_all(payload, PLANE, 0, 0, tiled=True).reshape(16 * tokens, -1)

    y, x = yh * 2 + yl, lax.axis_index("x")
    arrived, after = {}, [(), ()]
    for n, group in enumerate(GROUPS):
        partials = project(group, jnp.stack([y, x]), acts, weights, after[n])
        if n == 1:
            blocks = stats(acts, partials[0])
        for (dy, dx), partial in zip(group, partials):
            if (dy, dx) != (0, 0):
                to = [
                    (i * 4 + j, (i + dy) % 4 * 4 + (j + dx) % 4)
                    for i in range(4)
                    for j in range(4)
                ]
                partial = lax.ppermute(partial, PLANE, to)
            arrived[dy, dx] = partial
        after.append((arrived[group[0]], arrived[group[1]]))
    results = [arrived[dy, dx] for dy in range(4) for dx in range(4)]
    float_out, quant_out = finish(jnp.stack([y, core]), results)

    total = blocks[0]
    for j in (1, 2, 3):
        total = total + ahead(blocks[j], "z", 4 - j).astype(F32)
    total = (total + swap(total, "core")) * inverse

    piece = swap(lax.dynamic_slice_in_dim(total, core * BLOCK, BLOCK, 0), "yh")
    again = swap(piece, "core")
    moved = jnp.where(
        core == 0, jnp.concatenate([piece, again]), jnp.concatenate([again, piece])
    )
    total = jnp.where(yh == 1, total, moved)
    return float_out, quant_out, total[:, :BLOCK], total[:, BLOCK:]


def solution(mesh):
    fine = Mesh(mesh.devices.reshape(2, 2, 2, 4, 4), FINE)
    rows, tok = P(FINE, None), P(("yl", "z", "x"), None)
    return jax.shard_map(
        shards,
        mesh=fine,
        in_specs=(rows, rows, tok, tok, tok),
        out_specs=(rows, rows, tok, tok),
        check_vma=False,
    )
```

time: 217 us -> 194 us (0.89)
  waiting for transfers between devices: 143 us -> 87.3 us
  Pallas kernels: 6.46 us -> 34.9 us
  starting transfers between devices: 35.6 us -> 54.4 us
  matrix products: 18.6 us -> 0 us
  other arithmetic: 2.16 us -> 4.88 us
    ppermute x1, waiting for transfers between devices: 54.5 us -> 4.96 us  [shards(): got = lax.ppermute(send, ('yh', 'core', 'yl'), pairs)]
    ppermute x0 -> x15, starting transfers between devices: none -> 29.1 us  [shards(): partial = lax.ppermute(partial, PLANE, to)]
    pallas_call x1 -> x7, Pallas kernels: 3 us -> 31.4 us  [the longest x4 27.6 us: project(): pl.pallas_call(functools.partial(project_kernel, group), out_shape=(jax.S...]
    all_to_all x3 -> x1, waiting for transfers between devices: 33.5 us -> 10.6 us  [shards(): lax.all_to_all(payload, PLANE, 0, 0, tiled=True).reshape(16 * tokens, -1)]
    ppermute x0 -> x15, waiting for transfers between devices: none -> 19.7 us  [shards(): partial = lax.ppermute(partial, PLANE, to)]
    dot_general x2 -> x0, matrix products: 18.6 us -> none  [part(): jnp.dot(acts[:, :8 * features], w, preferred_element_type=F32).astype(BF16)]
    all_to_all x3 -> x1, starting transfers between devices: 20.6 us -> 7.16 us  [shards(): lax.all_to_all(payload, PLANE, 0, 0, tiled=True).reshape(16 * tokens, -1)]
    ppermute x6 -> x9, starting transfers between devices: 9.31 us -> 15 us  [ahead(): return lax.ppermute(a, axis, [((i + j) % 4, i) for i in range(4)])]
  transfers between devices with their start and end apart: 14 -> 31, of which waited for: 8 -> 10; matrix products, arithmetic and copies ran while one was open for 12% -> 1% of each run, Pallas kernels for 1% -> 15%
where the time goes in v9:
time: 194 us; the launch traced here: 192 us
  waiting for transfers between devices  87.3 us (45%)
  starting transfers between devices  54.4 us (28%)
  Pallas kernels  34.9 us (18%)
  local copies, waits for them, and re-layouts  9.62 us (5%)
  other arithmetic  4.88 us (3%)
    ppermute x9, waiting for transfers between devices, ahead(): return lax.ppermute(a, axis, [((i + j) % 4, i) for i in range(4)])  42.1 us
    ppermute x15, starting transfers between devices, shards(): partial = lax.ppermute(partial, PLANE, to)  29.1 us
    pallas_call x4, Pallas kernels, project(): pl.pallas_call(functools.partial(project_kernel, group), out_shape=(jax.S...  27.6 us
    ppermute x15, waiting for transfers between devices, shards(): partial = lax.ppermute(partial, PLANE, to)  19.7 us
    ppermute x9, starting transfers between devices, ahead(): return lax.ppermute(a, axis, [((i + j) % 4, i) for i in range(4)])  15 us
    all_to_all x1, waiting for transfers between devices, shards(): lax.all_to_all(payload, PLANE, 0, 0, tiled=True).reshape(16 * tokens, -1)  10.6 us
    ppermute x5, waiting for transfers between devices, swap(): return lax.ppermute(a, axis, [(0, 1), (1, 0)])  9.96 us
    unnamed x24, local copies, waits for them, and re-layouts  8.8 us
  transfers between devices with their start and end apart: 31, of which 10 were waited for; matrix products, arithmetic and copies ran while one was open for 1% of the time, Pallas kernels for 15%

profile of v9, /device:TPU:0, one launch (start us, length us, event | category | flops | bytes accessed | tf_op | source)
XLA Modules:
  0.0 192.0 jit_solution(14648835313386700679)
XLA Ops:
  3.0 1.7 collective-permute-start
  5.1 2.2 %copy-done.1 = bf16[16,64,2304]{2,1,0:T(8,128)(2,1)} copy-done((bf16[16,64,2304]{2,1,0:T(8,128)(2,1)}, bf16[16,64,2304]{2,1,0:T(8,128)(2,1)S(1)}, u32[]{:S(2)}) %copy-start.1) | copy-done | bytes 4718616
  7.3 5.0 %collective-permute-done.refs_0_ = bf16[256,1024]{1,0:T(8,128)(2,1)S(1)} collective-permute-done((bf16[256,1024]{1,0:T(8,128)(2,1)S(1)}, bf16[256,1024]{1,0:T(8,128)(2,1)S(1)}, u32[]{:S(2)}, u32[]{:S(2)}) %collective-permute-start) | collective-permute-done | bytes 524320 | tf_op jit(solution)/shard_map/ppermute | solution.py:212
  12.2 7.2 %all-to-all-start = ((bf16[16,64,2304]{2,1,0:T(8,128)(2,1)}), bf16[16,64,2304]{2,1,0:T(8,128)(2,1)}, u32[]{:S(2)}, u32[]{:S(2)}) async-start(bf16[16,64,2304]{2,1,0:T(8,128)(2,1)} %copy-done.1), calls=%async_computation | async-start | bytes 9437184 | tf_op jit(solution)/shard_map/all_to_all | solution.py:227
  19.5 1.9 %fusion.3.refs_0_ = bf16[256,1024]{1,0:T(8,128)(2,1)S(1)} fusion(s32[256,4096]{1,0:T(8,128)} %param.8, s32[]{:T(128)S(6)} %select_n.45, f32[2,1024]{1,0:T(2,128)S(1)} %constant_dynamic-slice_fusion.1, bf16[256,4096]{1,0:T(8,128)(2,1)} %param.7, pred[]{:T(512)S(6)} %eq.13), kind=kLoop, calls=%fused_computation.5 | loop fusion | flops 1310720 | bytes 2105349 | tf_op jit(solution)/shard_map/jit(_where)/select_n | solution.py:204
  21.4 4.1 %collective-permute-start.1 = (bf16[256,1024]{1,0:T(8,128)(2,1)S(1)}, bf16[256,1024]{1,0:T(8,128)(2,1)S(1)}, u32[]{:S(2)}, u32[]{:S(2)}) collective-permute-start(bf16[256,1024]{1,0:T(8,128)(2,1)S(1)} %fusion.3.refs_0_), channel_id=1, source_target_pairs={{4,0},{8,4},{12,8},{0,12},{5,1},{9,5},{13,9},{1,13},{6,2},{10,6},{... | collective-permute-start | bytes 1572872 | tf_op jit(solution)/shard_map/ppermute | solution.py:187
  26.8 2.0 %collective-permute-start.4 = (bf16[256,1024]{1,0:T(8,128)(2,1)S(1)}, bf16[256,1024]{1,0:T(8,128)(2,1)S(1)}, u32[]{:S(2)}, u32[]{:S(2)}) collective-permute-start(bf16[256,1024]{1,0:T(8,128)(2,1)S(1)} %collective-permute-done.refs_0_), channel_id=1, source_target_pairs={{4,0},{8,4},{12,8},{0,12},{5,1},{9,5},{13,9},{1,13},{6,2},{10,6},{... | collective-permute-start | bytes 1572872 | tf_op jit(solution)/shard_map/ppermute | solution.py:187
  28.8 2.3 %collective-permute-start.5 = (bf16[256,1024]{1,0:T(8,128)(2,1)S(1)}, bf16[256,1024]{1,0:T(8,128)(2,1)S(1)}, u32[]{:S(2)}, u32[]{:S(2)}) collective-permute-start(bf16[256,1024]{1,0:T(8,128)(2,1)S(1)} %collective-permute-done.refs_0_), channel_id=1, source_target_pairs={{8,0},{12,4},{0,8},{4,12},{9,1},{13,5},{1,9},{5,13},{10,2},{14,6},... | collective-permute-start | bytes 1572872 | tf_op jit(solution)/shard_map/ppermute | solution.py:187
  31.1 18.1 %collective-permute-done.1.refs_1_ = bf16[256,1024]{1,0:T(8,128)(2,1)S(1)} collective-permute-done((bf16[256,1024]{1,0:T(8,128)(2,1)S(1)}, bf16[256,1024]{1,0:T(8,128)(2,1)S(1)}, u32[]{:S(2)}, u32[]{:S(2)}) %collective-permute-start.1) | collective-permute-done | bytes 524320 | tf_op jit(solution)/shard_map/ppermute | solution.py:187
  49.2 11.7 %collective-permute-done.3.refs_3_ = bf16[256,1024]{1,0:T(8,128)(2,1)S(1)} collective-permute-done((bf16[256,1024]{1,0:T(8,128)(2,1)S(1)}, bf16[256,1024]{1,0:T(8,128)(2,1)S(1)}, u32[]{:S(2)}, u32[]{:S(2)}) %collective-permute-start.3) | collective-permute-done | bytes 524320 | tf_op jit(solution)/shard_map/ppermute | solution.py:187
  61.1 8.9 %collective-permute-done.4.refs_1_ = bf16[256,1024]{1,0:T(8,128)(2,1)S(1)} collective-permute-done((bf16[256,1024]{1,0:T(8,128)(2,1)S(1)}, bf16[256,1024]{1,0:T(8,128)(2,1)S(1)}, u32[]{:S(2)}, u32[]{:S(2)}) %collective-permute-start.4) | collective-permute-done | bytes 524320 | tf_op jit(solution)/shard_map/ppermute | solution.py:187
  70.0 3.4 %collective-permute-done.6.refs_3_ = bf16[256,1024]{1,0:T(8,128)(2,1)S(1)} collective-permute-done((bf16[256,1024]{1,0:T(8,128)(2,1)S(1)}, bf16[256,1024]{1,0:T(8,128)(2,1)S(1)}, u32[]{:S(2)}, u32[]{:S(2)}) %collective-permute-start.6) | collective-permute-done | bytes 524320 | tf_op jit(solution)/shard_map/ppermute | solution.py:187
  75.0 4.4 %collective-permute-done.8.refs_3_ = bf16[1024,1024]{1,0:T(8,128)(2,1)} collective-permute-done((bf16[1024,1024]{1,0:T(8,128)(2,1)}, bf16[1024,1024]{1,0:T(8,128)(2,1)}, u32[]{:S(2)}, u32[]{:S(2)}) %collective-permute-start.8) | collective-permute-done | bytes 2097184 | tf_op jit(solution)/shard_map/ppermute | solution.py:183
  79.4 10.6 %all-to-all-done = bf16[16,64,2304]{2,1,0:T(8,128)(2,1)} async-done(((bf16[16,64,2304]{2,1,0:T(8,128)(2,1)}), bf16[16,64,2304]{2,1,0:T(8,128)(2,1)}, u32[]{:S(2)}, u32[]{:S(2)}) %all-to-all-start) | async-done | bytes 4718624 | tf_op jit(solution)/shard_map/all_to_all | solution.py:227
  90.0 6.5 %project.4 = (bf16[64,2048]{1,0:T(8,128)(2,1)S(1)}, bf16[64,2048]{1,0:T(8,128)(2,1)S(1)}, bf16[64,2048]{1,0:T(8,128)(2,1)S(1)}, bf16[64,2048]{1,0:T(8,128)(2,1)S(1)}) custom-call(s32[2]{0:T(128)S(1)} %pad_add_fusion.1.at_ref, bf16[1024,2304]{1,0:T(8,128)(2,1)} %bitcast.5.acts_ref, bf16[1024,1024]{1,0:T(8,128)(2,1)S(1)} %join.2.refs_0_, ...), custom_call_target="tpu_custom_call" | custom-call | flops 2147483648 | bytes 10485760 | tf_op jit(solution)/shard_map/project/pallas_call | solution.py:108
  96.6 3.1 %stats.1 = (f32[256,256]{1,0:T(8,128)S(1)}, bf16[256,256]{1,0:T(8,128)(2,1)S(1)}, bf16[256,256]{1,0:T(8,128)(2,1)S(1)}, bf16[256,256]{1,0:T(8,128)(2,1)S(1)}) custom-call(bf16[1024,2304]{1,0:T(8,128)(2,1)} %bitcast.5.acts_ref, bf16[64,2048]{1,0:T(8,128)(2,1)S(1)} %get-tuple-element.34.after_ref), custom_call_target="tpu_custom_call" | custom-call | tf_op jit(solution)/shard_map/stats/pallas_call | solution.py:138
  99.7 5.4 %collective-permute-start.10 = (bf16[64,2048]{1,0:T(8,128)(2,1)S(1)}, bf16[64,2048]{1,0:T(8,128)(2,1)S(1)}, u32[]{:S(2)}, u32[]{:S(2)}) collective-permute-start(bf16[64,2048]{1,0:T(8,128)(2,1)S(1)} %get-tuple-element.35), channel_id=1, source_target_pairs={{0,83},{1,80},{2,81},{3,82},{16,3},{17,0},{18,1},{19,2},{64,19},{6... | collective-permute-start | bytes 786440 | tf_op jit(solution)/shard_map/ppermute | solution.py:242
  105.1 4.0 %collective-permute-start.26 = (bf16[256,256]{1,0:T(8,128)(2,1)S(1)}, bf16[256,256]{1,0:T(8,128)(2,1)S(1)}, u32[]{:S(2)}, u32[]{:S(2)}) collective-permute-start(bf16[256,256]{1,0:T(8,128)(2,1)S(1)} %get-tuple-element.55), channel_id=1, source_target_pairs={{4,0},{8,4},{12,8},{0,12},{5,1},{9,5},{13,9},{1,13},{6,2},{10,6},{... | collective-permute-start | bytes 393224 | tf_op jit(solution)/shard_map/ppermute | solution.py:187
  110.4 6.5 %project.6 = (bf16[64,2048]{1,0:T(8,128)(2,1)S(1)}, bf16[64,2048]{1,0:T(8,128)(2,1)S(1)}, bf16[64,2048]{1,0:T(8,128)(2,1)S(1)}, bf16[64,2048]{1,0:T(8,128)(2,1)S(1)}) custom-call(s32[2]{0:T(128)S(1)} %pad_add_fusion.1.at_ref, bf16[1024,2304]{1,0:T(8,128)(2,1)} %bitcast.5.acts_ref, bf16[1024,1024]{1,0:T(8,128)(2,1)S(1)} %join.2.refs_0_, ...), custom_call_target="tpu_custom_call" | custom-call | flops 2147483648 | bytes 10485760 | tf_op jit(solution)/shard_map/project/pallas_call | solution.py:108
  117.0 3.2 %collective-permute-start.13 = (bf16[64,2048]{1,0:T(8,128)(2,1)S(1)}, bf16[64,2048]{1,0:T(8,128)(2,1)S(1)}, u32[]{:S(2)}, u32[]{:S(2)}) collective-permute-start(bf16[64,2048]{1,0:T(8,128)(2,1)S(1)} %get-tuple-element.39), channel_id=1, source_target_pairs={{0,3},{1,0},{2,1},{3,2},{16,19},{17,16},{18,17},{19,18},{64,67},{6... | collective-permute-start | bytes 786440 | tf_op jit(solution)/shard_map/ppermute | solution.py:242
  120.6 7.2 %project.5 = (bf16[64,2048]{1,0:T(8,128)(2,1)S(1)}, bf16[64,2048]{1,0:T(8,128)(2,1)S(1)}, bf16[64,2048]{1,0:T(8,128)(2,1)}, bf16[64,2048]{1,0:T(8,128)(2,1)S(1)}) custom-call(s32[2]{0:T(128)S(1)} %pad_add_fusion.1.at_ref, bf16[1024,2304]{1,0:T(8,128)(2,1)} %bitcast.5.acts_ref, bf16[1024,1024]{1,0:T(8,128)(2,1)S(1)} %join.2.refs_0_, ...), custom_call_target="tpu_custom_call" | custom-call | flops 2147483648 | bytes 10485760 | tf_op jit(solution)/shard_map/project/pallas_call | solution.py:108
  127.8 3.2 %collective-permute-start.21 = (bf16[64,2048]{1,0:T(8,128)(2,1)S(1)}, bf16[64,2048]{1,0:T(8,128)(2,1)S(1)}, u32[]{:S(2)}, u32[]{:S(2)}) collective-permute-start(bf16[64,2048]{1,0:T(8,128)(2,1)S(1)} %get-tuple-element.47), channel_id=1, source_target_pairs={{0,80},{1,81},{2,82},{3,83},{16,0},{17,1},{18,2},{19,3},{64,16},{6... | collective-permute-start | bytes 786440 | tf_op jit(solution)/shard_map/ppermute | solution.py:242
  131.1 2.6 %collective-permute-start.22 = (bf16[64,2048]{1,0:T(8,128)(2,1)S(1)}, bf16[64,2048]{1,0:T(8,128)(2,1)S(1)}, u32[]{:S(2)}, u32[]{:S(2)}) collective-permute-start(bf16[64,2048]{1,0:T(8,128)(2,1)S(1)} %get-tuple-element.48), channel_id=1, source_target_pairs={{0,81},{1,82},{2,83},{3,80},{16,1},{17,2},{18,3},{19,0},{64,17},{6... | collective-permute-start | bytes 786440 | tf_op jit(solution)/shard_map/ppermute | solution.py:242
  133.7 7.4 %project.7 = (bf16[64,2048]{1,0:T(8,128)(2,1)S(1)}, bf16[64,2048]{1,0:T(8,128)(2,1)}, bf16[64,2048]{1,0:T(8,128)(2,1)}, bf16[64,2048]{1,0:T(8,128)(2,1)}) custom-call(s32[2]{0:T(128)S(1)} %pad_add_fusion.1.at_ref, bf16[1024,2304]{1,0:T(8,128)(2,1)} %bitcast.5.acts_ref, bf16[1024,1024]{1,0:T(8,128)(2,1)S(1)} %join.2.refs_0_, bf16[1024,1024]{1,0:T(8,128)(2,1)} %join.3.refs_1_, ...), custom_call_target="tpu_custom_call" | custom-call | flops 2147483648 | bytes 10485760 | tf_op jit(solution)/shard_map/project/pallas_call | solution.py:108
  141.9 2.9 %collective-permute-start.15 = (bf16[64,2048]{1,0:T(8,128)(2,1)S(1)}, bf16[64,2048]{1,0:T(8,128)(2,1)S(1)}, u32[]{:S(2)}, u32[]{:S(2)}) collective-permute-start(bf16[64,2048]{1,0:T(8,128)(2,1)S(1)} %get-tuple-element.41), channel_id=1, source_target_pairs={{0,18},{1,19},{2,16},{3,17},{16,66},{17,67},{18,64},{19,65},{64,82... | collective-permute-start | bytes 786440 | tf_op jit(solution)/shard_map/ppermute | solution.py:242
  148.9 4.2 %collective-permute-start.19 = (bf16[64,2048]{1,0:T(8,128)(2,1)}, bf16[64,2048]{1,0:T(8,128)(2,1)S(1)}, u32[]{:S(2)}, u32[]{:S(2)}) collective-permute-start(bf16[64,2048]{1,0:T(8,128)(2,1)} %get-tuple-element.45), channel_id=1, source_target_pairs={{0,66},{1,67},{2,64},{3,65},{16,82},{17,83},{18,80},{19,81},{64,2}... | collective-permute-start | bytes 786440 | tf_op jit(solution)/shard_map/ppermute | solution.py:242
  153.1 1.9 collective-permute-start.20
  154.9 2.9 %collective-permute-done.15.refs_6_ = bf16[64,2048]{1,0:T(8,128)(2,1)S(1)} collective-permute-done((bf16[64,2048]{1,0:T(8,128)(2,1)S(1)}, bf16[64,2048]{1,0:T(8,128)(2,1)S(1)}, u32[]{:S(2)}, u32[]{:S(2)}) %collective-permute-start.15) | collective-permute-done | bytes 262176 | tf_op jit(solution)/shard_map/ppermute | solution.py:242
  157.8 2.8 %collective-permute-start.23 = (bf16[64,2048]{1,0:T(8,128)(2,1)}, bf16[64,2048]{1,0:T(8,128)(2,1)S(1)}, u32[]{:S(2)}, u32[]{:S(2)}) collective-permute-start(bf16[64,2048]{1,0:T(8,128)(2,1)} %get-tuple-element.49), channel_id=1, source_target_pairs={{0,82},{1,83},{2,80},{3,81},{16,2},{17,3},{18,0},{19,1},{64,18},{6... | collective-permute-start | bytes 786440 | tf_op jit(solution)/shard_map/ppermute | solution.py:242
  160.6 16.8 %collective-permute-done.17.refs_8_ = bf16[64,2048]{1,0:T(8,128)(2,1)S(1)} collective-permute-done((bf16[64,2048]{1,0:T(8,128)(2,1)S(1)}, bf16[64,2048]{1,0:T(8,128)(2,1)S(1)}, u32[]{:S(2)}, u32[]{:S(2)}) %collective-permute-start.17) | collective-permute-done | bytes 262176 | tf_op jit(solution)/shard_map/ppermute | solution.py:242
  178.4 5.5 %collective-permute-done.28 = f32[128,256]{1,0:T(8,128)} collective-permute-done((f32[128,256]{1,0:T(8,128)S(1)}, f32[128,256]{1,0:T(8,128)}, u32[]{:S(2)}, u32[]{:S(2)}) %collective-permute-start.28) | collective-permute-done | bytes 131104 | tf_op jit(solution)/shard_map/ppermute | solution.py:183
  187.8 2.2 %finish.1 = (bf16[64,4096]{1,0:T(8,128)(2,1)}, bf16[64,4096]{1,0:T(8,128)(2,1)}) custom-call(s32[2]{0:T(128)S(1)} %pad_add_fusion.at_ref, bf16[64,2048]{1,0:T(8,128)(2,1)S(1)} %copy-done.7, bf16[64,2048]{1,0:T(8,128)(2,1)S(1)} %collective-permute-done.11.refs_4_.refs_1_, bf16[64,2048]{1,0:T(8,128)(2,1)S(1)} %collective-permute-done.12.refs_2_, ...), custom_call_target="tpu_custom_call" | custom-call | tf_op jit(solution)/shard_map/finish/pallas_call | solution.py:172
  (74 shorter events, 19.1 us)
Async XLA Ops:
  3.0 9.3 %collective-permute-start = (bf16[256,1024]{1,0:T(8,128)(2,1)S(1)}, bf16[256,1024]{1,0:T(8,128)(2,1)S(1)}, u32[]{:S(2)}, u32[]{:S(2)}) collective-permute-start(bf16[256,1024]{1,0:T(8,128)(2,1)S(1)} %fusion.2.after_ref), channel_id=1, source_target_pairs={{0,16},{16,0},{32,112},{48,96},{64,80},{80,64},{96,48},{112,32},{1... | collective-permute-start | bytes 1572872 | tf_op jit(solution)/shard_map/ppermute | solution.py:212
  12.2 77.7 %all-to-all-start = ((bf16[16,64,2304]{2,1,0:T(8,128)(2,1)}), bf16[16,64,2304]{2,1,0:T(8,128)(2,1)}, u32[]{:S(2)}, u32[]{:S(2)}) async-start(bf16[16,64,2304]{2,1,0:T(8,128)(2,1)} %copy-done.1), calls=%async_computation | async-start | bytes 9437184 | tf_op jit(solution)/shard_map/all_to_all | solution.py:227
  21.4 27.7 %collective-permute-start.1 = (bf16[256,1024]{1,0:T(8,128)(2,1)S(1)}, bf16[256,1024]{1,0:T(8,128)(2,1)S(1)}, u32[]{:S(2)}, u32[]{:S(2)}) collective-permute-start(bf16[256,1024]{1,0:T(8,128)(2,1)S(1)} %fusion.3.refs_0_), channel_id=1, source_target_pairs={{4,0},{8,4},{12,8},{0,12},{5,1},{9,5},{13,9},{1,13},{6,2},{10,6},{... | collective-permute-start | bytes 1572872 | tf_op jit(solution)/shard_map/ppermute | solution.py:187
  25.5 23.6 %collective-permute-start.2 = (bf16[256,1024]{1,0:T(8,128)(2,1)S(1)}, bf16[256,1024]{1,0:T(8,128)(2,1)S(1)}, u32[]{:S(2)}, u32[]{:S(2)}) collective-permute-start(bf16[256,1024]{1,0:T(8,128)(2,1)S(1)} %fusion.3.refs_0_), channel_id=1, source_target_pairs={{8,0},{12,4},{0,8},{4,12},{9,1},{13,5},{1,9},{5,13},{10,2},{14,6},... | collective-permute-start | bytes 1572872 | tf_op jit(solution)/shard_map/ppermute | solution.py:187
  25.5 35.3 %collective-permute-start.3 = (bf16[256,1024]{1,0:T(8,128)(2,1)S(1)}, bf16[256,1024]{1,0:T(8,128)(2,1)S(1)}, u32[]{:S(2)}, u32[]{:S(2)}) collective-permute-start(bf16[256,1024]{1,0:T(8,128)(2,1)S(1)} %fusion.3.refs_0_), channel_id=1, source_target_pairs={{12,0},{0,4},{4,8},{8,12},{13,1},{1,5},{5,9},{9,13},{14,2},{2,6},{... | collective-permute-start | bytes 1572872 | tf_op jit(solution)/shard_map/ppermute | solution.py:187
  26.8 43.2 %collective-permute-start.4 = (bf16[256,1024]{1,0:T(8,128)(2,1)S(1)}, bf16[256,1024]{1,0:T(8,128)(2,1)S(1)}, u32[]{:S(2)}, u32[]{:S(2)}) collective-permute-start(bf16[256,1024]{1,0:T(8,128)(2,1)S(1)} %collective-permute-done.refs_0_), channel_id=1, source_target_pairs={{4,0},{8,4},{12,8},{0,12},{5,1},{9,5},{13,9},{1,13},{6,2},{10,6},{... | collective-permute-start | bytes 1572872 | tf_op jit(solution)/shard_map/ppermute | solution.py:187
  28.8 41.3 %collective-permute-start.5 = (bf16[256,1024]{1,0:T(8,128)(2,1)S(1)}, bf16[256,1024]{1,0:T(8,128)(2,1)S(1)}, u32[]{:S(2)}, u32[]{:S(2)}) collective-permute-start(bf16[256,1024]{1,0:T(8,128)(2,1)S(1)} %collective-permute-done.refs_0_), channel_id=1, source_target_pairs={{8,0},{12,4},{0,8},{4,12},{9,1},{13,5},{1,9},{5,13},{10,2},{14,6},... | collective-permute-start | bytes 1572872 | tf_op jit(solution)/shard_map/ppermute | solution.py:187
  49.1 24.3 %collective-permute-start.6 = (bf16[256,1024]{1,0:T(8,128)(2,1)S(1)}, bf16[256,1024]{1,0:T(8,128)(2,1)S(1)}, u32[]{:S(2)}, u32[]{:S(2)}) collective-permute-start(bf16[256,1024]{1,0:T(8,128)(2,1)S(1)} %collective-permute-done.refs_0_), channel_id=1, source_target_pairs={{12,0},{0,4},{4,8},{8,12},{13,1},{1,5},{5,9},{9,13},{14,2},{2,6},{... | collective-permute-start | bytes 1572872 | tf_op jit(solution)/shard_map/ppermute | solution.py:187
  61.0 13.9 %collective-permute-start.7 = (bf16[1024,1024]{1,0:T(8,128)(2,1)S(1)}, bf16[1024,1024]{1,0:T(8,128)(2,1)}, u32[]{:S(2)}, u32[]{:S(2)}) collective-permute-start(bf16[1024,1024]{1,0:T(8,128)(2,1)S(1)} %join.2.refs_0_), channel_id=1, source_target_pairs={{0,32},{32,0},{1,33},{33,1},{2,34},{34,2},{3,35},{35,3},{4,36},{36... | collective-permute-start | bytes 6291464 | tf_op jit(solution)/shard_map/ppermute | solution.py:183
  74.9 4.5 %collective-permute-start.8 = (bf16[1024,1024]{1,0:T(8,128)(2,1)}, bf16[1024,1024]{1,0:T(8,128)(2,1)}, u32[]{:S(2)}, u32[]{:S(2)}) collective-permute-start(bf16[1024,1024]{1,0:T(8,128)(2,1)} %join.3.refs_1_), channel_id=1, source_target_pairs={{0,32},{32,0},{1,33},{33,1},{2,34},{34,2},{3,35},{35,3},{4,36},{36... | collective-permute-start | bytes 6291464 | tf_op jit(solution)/shard_map/ppermute | solution.py:183
  96.5 23.8 %collective-permute-start.9 = (bf16[64,2048]{1,0:T(8,128)(2,1)S(1)}, bf16[64,2048]{1,0:T(8,128)(2,1)S(1)}, u32[]{:S(2)}, u32[]{:S(2)}) collective-permute-start(bf16[64,2048]{1,0:T(8,128)(2,1)S(1)} %get-tuple-element.34.after_ref), channel_id=1, source_target_pairs={{0,17},{1,18},{2,19},{3,16},{16,65},{17,66},{18,67},{19,64},{64,81... | collective-permute-start | bytes 786440 | tf_op jit(solution)/shard_map/ppermute | solution.py:242
  99.7 20.7 %collective-permute-start.10 = (bf16[64,2048]{1,0:T(8,128)(2,1)S(1)}, bf16[64,2048]{1,0:T(8,128)(2,1)S(1)}, u32[]{:S(2)}, u32[]{:S(2)}) collective-permute-start(bf16[64,2048]{1,0:T(8,128)(2,1)S(1)} %get-tuple-element.35), channel_id=1, source_target_pairs={{0,83},{1,80},{2,81},{3,82},{16,3},{17,0},{18,1},{19,2},{64,19},{6... | collective-permute-start | bytes 786440 | tf_op jit(solution)/shard_map/ppermute | solution.py:242
  105.1 11.8 %collective-permute-start.26 = (bf16[256,256]{1,0:T(8,128)(2,1)S(1)}, bf16[256,256]{1,0:T(8,128)(2,1)S(1)}, u32[]{:S(2)}, u32[]{:S(2)}) collective-permute-start(bf16[256,256]{1,0:T(8,128)(2,1)S(1)} %get-tuple-element.55), channel_id=1, source_target_pairs={{4,0},{8,4},{12,8},{0,12},{5,1},{9,5},{13,9},{1,13},{6,2},{10,6},{... | collective-permute-start | bytes 393224 | tf_op jit(solution)/shard_map/ppermute | solution.py:187
  109.1 7.9 %collective-permute-start.25 = (bf16[256,256]{1,0:T(8,128)(2,1)S(1)}, bf16[256,256]{1,0:T(8,128)(2,1)S(1)}, u32[]{:S(2)}, u32[]{:S(2)}) collective-permute-start(bf16[256,256]{1,0:T(8,128)(2,1)S(1)} %get-tuple-element.54), channel_id=1, source_target_pairs={{8,0},{12,4},{0,8},{4,12},{9,1},{13,5},{1,9},{5,13},{10,2},{14,6},... | collective-permute-start | bytes 393224 | tf_op jit(solution)/shard_map/ppermute | solution.py:187
  109.1 11.1 %collective-permute-start.24 = (bf16[256,256]{1,0:T(8,128)(2,1)S(1)}, bf16[256,256]{1,0:T(8,128)(2,1)S(1)}, u32[]{:S(2)}, u32[]{:S(2)}) collective-permute-start(bf16[256,256]{1,0:T(8,128)(2,1)S(1)} %get-tuple-element.53), channel_id=1, source_target_pairs={{12,0},{0,4},{4,8},{8,12},{13,1},{1,5},{5,9},{9,13},{14,2},{2,6},{... | collective-permute-start | bytes 393224 | tf_op jit(solution)/shard_map/ppermute | solution.py:187
  116.9 11.0 %collective-permute-start.11 = (bf16[64,2048]{1,0:T(8,128)(2,1)S(1)}, bf16[64,2048]{1,0:T(8,128)(2,1)S(1)}, u32[]{:S(2)}, u32[]{:S(2)}) collective-permute-start(bf16[64,2048]{1,0:T(8,128)(2,1)S(1)} %get-tuple-element.37), channel_id=1, source_target_pairs={{0,1},{1,2},{2,3},{3,0},{16,17},{17,18},{18,19},{19,16},{64,65},{6... | collective-permute-start | bytes 786440 | tf_op jit(solution)/shard_map/ppermute | solution.py:242
  117.0 14.1 %collective-permute-start.13 = (bf16[64,2048]{1,0:T(8,128)(2,1)S(1)}, bf16[64,2048]{1,0:T(8,128)(2,1)S(1)}, u32[]{:S(2)}, u32[]{:S(2)}) collective-permute-start(bf16[64,2048]{1,0:T(8,128)(2,1)S(1)} %get-tuple-element.39), channel_id=1, source_target_pairs={{0,3},{1,0},{2,1},{3,2},{16,19},{17,16},{18,17},{19,18},{64,67},{6... | collective-permute-start | bytes 786440 | tf_op jit(solution)/shard_map/ppermute | solution.py:242
  120.2 20.9 %collective-permute-start.14 = (bf16[64,2048]{1,0:T(8,128)(2,1)S(1)}, bf16[64,2048]{1,0:T(8,128)(2,1)S(1)}, u32[]{:S(2)}, u32[]{:S(2)}) collective-permute-start(bf16[64,2048]{1,0:T(8,128)(2,1)S(1)} %get-tuple-element.40), channel_id=1, source_target_pairs={{0,16},{1,17},{2,18},{3,19},{16,64},{17,65},{18,66},{19,67},{64,80... | collective-permute-start | bytes 786440 | tf_op jit(solution)/shard_map/ppermute | solution.py:242
  120.3 20.9 %collective-permute-start.16 = (bf16[64,2048]{1,0:T(8,128)(2,1)S(1)}, bf16[64,2048]{1,0:T(8,128)(2,1)S(1)}, u32[]{:S(2)}, u32[]{:S(2)}) collective-permute-start(bf16[64,2048]{1,0:T(8,128)(2,1)S(1)} %get-tuple-element.42), channel_id=1, source_target_pairs={{0,19},{1,16},{2,17},{3,18},{16,67},{17,64},{18,65},{19,66},{64,83... | collective-permute-start | bytes 786440 | tf_op jit(solution)/shard_map/ppermute | solution.py:242
  120.4 24.5 %collective-permute-start.27 = (f32[256,256]{1,0:T(8,128)S(1)}, f32[256,256]{1,0:T(8,128)S(1)}, u32[]{:S(2)}, u32[]{:S(2)}) collective-permute-start(f32[256,256]{1,0:T(8,128)S(1)} %convert_add_fusion), channel_id=1, source_target_pairs={{0,32},{32,0},{1,33},{33,1},{2,34},{34,2},{3,35},{35,3},{4,36},{36... | collective-permute-start | bytes 786440 | tf_op jit(solution)/shard_map/ppermute | solution.py:183
  127.8 13.3 %copy-start.6 = (bf16[64,2048]{1,0:T(8,128)(2,1)}, bf16[64,2048]{1,0:T(8,128)(2,1)S(1)}, u32[]{:S(2)}) copy-start(bf16[64,2048]{1,0:T(8,128)(2,1)S(1)} %get-tuple-element.36.refs_0_) | copy-start | bytes 786436
  127.8 18.6 %collective-permute-start.21 = (bf16[64,2048]{1,0:T(8,128)(2,1)S(1)}, bf16[64,2048]{1,0:T(8,128)(2,1)S(1)}, u32[]{:S(2)}, u32[]{:S(2)}) collective-permute-start(bf16[64,2048]{1,0:T(8,128)(2,1)S(1)} %get-tuple-element.47), channel_id=1, source_target_pairs={{0,80},{1,81},{2,82},{3,83},{16,0},{17,1},{18,2},{19,3},{64,16},{6... | collective-permute-start | bytes 786440 | tf_op jit(solution)/shard_map/ppermute | solution.py:242
  131.1 17.1 %collective-permute-start.22 = (bf16[64,2048]{1,0:T(8,128)(2,1)S(1)}, bf16[64,2048]{1,0:T(8,128)(2,1)S(1)}, u32[]{:S(2)}, u32[]{:S(2)}) collective-permute-start(bf16[64,2048]{1,0:T(8,128)(2,1)S(1)} %get-tuple-element.48), channel_id=1, source_target_pairs={{0,81},{1,82},{2,83},{3,80},{16,1},{17,2},{18,3},{19,0},{64,17},{6... | collective-permute-start | bytes 786440 | tf_op jit(solution)/shard_map/ppermute | solution.py:242
  141.1 11.9 %collective-permute-start.12 = (bf16[64,2048]{1,0:T(8,128)(2,1)S(1)}, bf16[64,2048]{1,0:T(8,128)(2,1)S(1)}, u32[]{:S(2)}, u32[]{:S(2)}) collective-permute-start(bf16[64,2048]{1,0:T(8,128)(2,1)S(1)} %get-tuple-element.38), channel_id=1, source_target_pairs={{0,2},{1,3},{2,0},{3,1},{16,18},{17,19},{18,16},{19,17},{64,66},{6... | collective-permute-start | bytes 786440 | tf_op jit(solution)/shard_map/ppermute | solution.py:242
  141.9 15.9 %collective-permute-start.15 = (bf16[64,2048]{1,0:T(8,128)(2,1)S(1)}, bf16[64,2048]{1,0:T(8,128)(2,1)S(1)}, u32[]{:S(2)}, u32[]{:S(2)}) collective-permute-start(bf16[64,2048]{1,0:T(8,128)(2,1)S(1)} %get-tuple-element.41), channel_id=1, source_target_pairs={{0,18},{1,19},{2,16},{3,17},{16,66},{17,67},{18,64},{19,65},{64,82... | collective-permute-start | bytes 786440 | tf_op jit(solution)/shard_map/ppermute | solution.py:242
  144.9 32.5 %collective-permute-start.17 = (bf16[64,2048]{1,0:T(8,128)(2,1)S(1)}, bf16[64,2048]{1,0:T(8,128)(2,1)S(1)}, u32[]{:S(2)}, u32[]{:S(2)}) collective-permute-start(bf16[64,2048]{1,0:T(8,128)(2,1)S(1)} %get-tuple-element.43), channel_id=1, source_target_pairs={{0,64},{1,65},{2,66},{3,67},{16,80},{17,81},{18,82},{19,83},{64,0}... | collective-permute-start | bytes 786440 | tf_op jit(solution)/shard_map/ppermute | solution.py:242
  147.2 36.8 %collective-permute-start.18 = (bf16[64,2048]{1,0:T(8,128)(2,1)}, bf16[64,2048]{1,0:T(8,128)(2,1)S(1)}, u32[]{:S(2)}, u32[]{:S(2)}) collective-permute-start(bf16[64,2048]{1,0:T(8,128)(2,1)} %get-tuple-element.44), channel_id=1, source_target_pairs={{0,65},{1,66},{2,67},{3,64},{16,81},{17,82},{18,83},{19,80},{64,1}... | collective-permute-start | bytes 786440 | tf_op jit(solution)/shard_map/ppermute | solution.py:242
  148.9 35.1 %collective-permute-start.19 = (bf16[64,2048]{1,0:T(8,128)(2,1)}, bf16[64,2048]{1,0:T(8,128)(2,1)S(1)}, u32[]{:S(2)}, u32[]{:S(2)}) collective-permute-start(bf16[64,2048]{1,0:T(8,128)(2,1)} %get-tuple-element.45), channel_id=1, source_target_pairs={{0,66},{1,67},{2,64},{3,65},{16,82},{17,83},{18,80},{19,81},{64,2}... | collective-permute-start | bytes 786440 | tf_op jit(solution)/shard_map/ppermute | solution.py:242
  153.1 31.0 %collective-permute-start.20 = (bf16[64,2048]{1,0:T(8,128)(2,1)}, bf16[64,2048]{1,0:T(8,128)(2,1)S(1)}, u32[]{:S(2)}, u32[]{:S(2)}) collective-permute-start(bf16[64,2048]{1,0:T(8,128)(2,1)} %get-tuple-element.46), channel_id=1, source_target_pairs={{0,67},{1,64},{2,65},{3,66},{16,83},{17,80},{18,81},{19,82},{64,3}... | collective-permute-start | bytes 786440 | tf_op jit(solution)/shard_map/ppermute | solution.py:242
  157.8 26.2 %collective-permute-start.23 = (bf16[64,2048]{1,0:T(8,128)(2,1)}, bf16[64,2048]{1,0:T(8,128)(2,1)S(1)}, u32[]{:S(2)}, u32[]{:S(2)}) collective-permute-start(bf16[64,2048]{1,0:T(8,128)(2,1)} %get-tuple-element.49), channel_id=1, source_target_pairs={{0,82},{1,83},{2,80},{3,81},{16,2},{17,3},{18,0},{19,1},{64,18},{6... | collective-permute-start | bytes 786440 | tf_op jit(solution)/shard_map/ppermute | solution.py:242
  177.4 6.6 %collective-permute-start.28 = (f32[128,256]{1,0:T(8,128)S(1)}, f32[128,256]{1,0:T(8,128)}, u32[]{:S(2)}, u32[]{:S(2)}) collective-permute-start(f32[128,256]{1,0:T(8,128)S(1)} %constant_dynamic-slice_fusion), channel_id=1, source_target_pairs={{0,64},{64,0},{1,65},{65,1},{2,66},{66,2},{3,67},{67,3},{4,68},{68... | collective-permute-start | bytes 393224 | tf_op jit(solution)/shard_map/ppermute | solution.py:183
  183.9 6.1 %collective-permute-start.29 = (f32[128,256]{1,0:T(8,128)}, f32[128,256]{1,0:T(8,128)}, u32[]{:S(2)}, u32[]{:S(2)}) collective-permute-start(f32[128,256]{1,0:T(8,128)} %collective-permute-done.28), channel_id=1, source_target_pairs={{0,32},{32,0},{1,33},{33,1},{2,34},{34,2},{3,35},{35,3},{4,36},{36... | collective-permute-start | bytes 393224 | tf_op jit(solution)/shard_map/ppermute | solution.py:183
  (11 other events, 17.0 us)

commit v10 on v5

--- a/solution.py
+++ b/solution.py
@@ -133,7 +133,12 @@
         quant = (values * scales[:, None, :]).reshape(features, quarter).astype(BF16)
         return jnp.where(kind == 0, plain, quant)
 
-    own = weight(yh, yl * half + core * quarter)
+    quant = attn_quant[:, :BLOCK]
+    shift = (attn_float[:, :BLOCK].astype(F32) - quant.astype(F32)).astype(BF16)
+    block = jnp.concatenate([quant, shift], axis=1)
+    line = jnp.concatenate([block] + [ahead(block, "x", j) for j in (1, 2, 3)], axis=0)
+    pieces = [line] + [ahead(line, ("yh", "yl"), j) for j in (1, 2, 3)]
+
     send = weight(yh ^ core, (1 - yl) * half + core * quarter)
     pairs = []
     for a in range(2):
@@ -141,22 +146,18 @@
             for b in range(2):
                 pairs.append((a * 4 + c * 2 + b, (a ^ c) * 4 + c * 2 + (1 - b)))
     got = lax.ppermute(send, ("yh", "core", "yl"), pairs)
+    col, send = lax.optimization_barrier((yl * half + core * quarter, send))
+    own = weight(yh, col)
 
     payload = pack(z, attn_float, attn_quant)
+    payload, got, *pieces = lax.optimization_barrier((payload, got, *pieces))
+
+    acts = lax.all_to_all(payload, PLANE, 0, 0, tiled=True).reshape(16 * tokens, 8 * features)
+
     rows = jnp.concatenate([own, got], axis=0)
     parts = [rows] + [ahead(rows, "z", j) for j in (1, 2, 3)]
     mine = jnp.concatenate(parts, axis=0)
     other = swap(mine, "core")
-
-    quant = attn_quant[:, :BLOCK]
-    shift = (attn_float[:, :BLOCK].astype(F32) - quant.astype(F32)).astype(BF16)
-    block = jnp.concatenate([quant, shift], axis=1)
-    block, payload = lax.optimization_barrier((block, payload))
-    acts = lax.all_to_all(payload, PLANE, 0, 0, tiled=True).reshape(16 * tokens, 8 * features)
-
-    line = jnp.concatenate([block] + [ahead(block, "x", j) for j in (1, 2, 3)], axis=0)
-    pieces = [line] + [ahead(line, ("yh", "yl"), j) for j in (1, 2, 3)]
-    acts, mine, *pieces = lax.optimization_barrier((acts, mine, *pieces))
 
     def part(w):
         return jnp.dot(acts, w, preferred_element_type=F32).astype(BF16)
@@ -164,19 +165,16 @@
     def output(p):
         return lax.all_to_all(p.reshape(16, tokens, quarter), PLANE, 0, 0, tiled=True)
 
-    first = part(mine)
-    result1 = output(first)
+    result1 = output(part(mine))
+    second = part(other)
 
-    acts1, first = lax.optimization_barrier((acts, first))
+    acts1, second = lax.optimization_barrier((acts, second))
     blocks = stats(jnp.stack([yh * 2 + yl, lax.axis_index("x")]), acts1, pieces)
+    result2 = output(second)
     total = blocks[0]
     for j in (1, 2, 3):
         total = total + ahead(blocks[j], "z", 4 - j).astype(F32)
-    other, total = lax.optimization_barrier((other, total))
-    second = part(other)
     total = (total + swap(total, "core")) * inverse
-    second, total = lax.optimization_barrier((second, total))
-    result2 = output(second)
 
     piece = swap(lax.dynamic_slice_in_dim(total, core * BLOCK, BLOCK, 0), "yh")
     again = swap(piece, "core")

time: 184 us -> 169 us (0.918)
  waiting for transfers between devices: 105 us -> 88.9 us
    ppermute x4, waiting for transfers between devices: 24.3 us -> 11.3 us  [swap(): return lax.ppermute(a, axis, [(0, 1), (1, 0)])]
    all_to_all x2, waiting for transfers between devices: 10.1 us -> 21.1 us  [output(): lax.all_to_all(p.reshape(16, tokens, quarter), PLANE, 0, 0, tiled=True)]
    ppermute x12, waiting for transfers between devices: 63 us -> 52 us  [ahead(): return lax.ppermute(a, axis, [((i + j) % 4, i) for i in range(4)])]
    ppermute x1, waiting for transfers between devices: 7.5 us -> 0.01 us  [shards(): got = lax.ppermute(send, ('yh', 'core', 'yl'), pairs)]
    all_to_all x1, waiting for transfers between devices: 0.01 us -> 4.36 us  [shards(): lax.all_to_all(payload, PLANE, 0, 0, tiled=True)]
    unnamed x0 -> x1, other arithmetic: none -> 2.79 us
    all_to_all x1, starting transfers between devices: 7.09 us -> 4.55 us  [shards(): lax.all_to_all(payload, PLANE, 0, 0, tiled=True)]
    unnamed x13 -> x11, local copies, waits for them, and re-layouts: 7.07 us -> 8.16 us
  transfers between devices with their start and end apart: 20 -> 20, of which waited for: 15 -> 14; matrix products, arithmetic and copies ran while one was open for 14% -> 17% of each run, Pallas kernels for 2% -> 2%
where the time goes in v10:
time: 169 us; the launch traced here: 168 us
  waiting for transfers between devices  88.9 us (53%)
  starting transfers between devices  37.2 us (22%)
  matrix products  18.7 us (11%)
  local copies, waits for them, and re-layouts  10.8 us (6%)
  Pallas kernels  6.28 us (4%)
  other arithmetic  5.39 us (3%)
    ppermute x12, waiting for transfers between devices, ahead(): return lax.ppermute(a, axis, [((i + j) % 4, i) for i in range(4)])  52 us
    all_to_all x2, waiting for transfers between devices, output(): lax.all_to_all(p.reshape(16, tokens, quarter), PLANE, 0, 0, tiled=True)  21.1 us
    ppermute x12, starting transfers between devices, ahead(): return lax.ppermute(a, axis, [((i + j) % 4, i) for i in range(4)])  18.8 us
    dot_general x2, matrix products, part(): return jnp.dot(acts, w, preferred_element_type=F32).astype(BF16)  18.7 us
    ppermute x4, waiting for transfers between devices, swap(): return lax.ppermute(a, axis, [(0, 1), (1, 0)])  11.3 us
    all_to_all x2, starting transfers between devices, output(): lax.all_to_all(p.reshape(16, tokens, quarter), PLANE, 0, 0, tiled=True)  8.83 us
    unnamed x11, local copies, waits for them, and re-layouts  8.16 us
    all_to_all x1, starting transfers between devices, shards(): lax.all_to_all(payload, PLANE, 0, 0, tiled=True)  4.55 us
  transfers between devices with their start and end apart: 20, of which 14 were waited for; matrix products, arithmetic and copies ran while one was open for 17% of the time, Pallas kernels for 2%

profile of v10, /device:TPU:0, one launch (start us, length us, event | category | flops | bytes accessed | tf_op | source)
XLA Modules:
  0.0 168.0 jit_solution(2727262412237593292)
XLA Ops:
  1.4 1.6 fusion.2
  3.0 1.7 %collective-permute-start = (bf16[256,1024]{1,0:T(8,128)(2,1)S(1)}, bf16[256,1024]{1,0:T(8,128)(2,1)S(1)}, u32[]{:S(2)}, u32[]{:S(2)}) collective-permute-start(bf16[256,1024]{1,0:T(8,128)(2,1)S(1)} %fusion.2), channel_id=1, source_target_pairs={{0,16},{16,0},{32,112},{48,96},{64,80},{80,64},{96,48},{112,32},{1... | collective-permute-start | bytes 1572872 | tf_op jit(solution)/shard_map/ppermute | solution.py:148
  6.2 1.6 collective-permute-start.3
  7.7 2.7 %collective-permute-start.2 = (bf16[64,256]{1,0:T(8,128)(2,1)S(1)}, bf16[64,256]{1,0:T(8,128)(2,1)S(1)}, u32[]{:S(2)}, u32[]{:S(2)}) collective-permute-start(bf16[64,256]{1,0:T(8,128)(2,1)S(1)} %pad_maximum_fusion.2), channel_id=1, source_target_pairs={{2,0},{3,1},{0,2},{1,3},{6,4},{7,5},{4,6},{5,7},{10,8},{11,9},{8,1... | collective-permute-start | bytes 98312 | tf_op jit(solution)/shard_map/ppermute | solution.py:117
  10.5 1.4 collective-permute-start.1
  11.9 1.5 collective-permute-done.2
  14.4 2.2 %collective-permute-start.4 = (bf16[256,256]{1,0:T(8,128)(2,1)S(1)}, bf16[256,256]{1,0:T(8,128)(2,1)S(1)}, u32[]{:S(2)}, u32[]{:S(2)}) collective-permute-start(bf16[256,256]{1,0:T(8,128)(2,1)S(1)} %pad_maximum_fusion.1.refs_0_), channel_id=1, source_target_pairs={{16,0},{64,16},{80,64},{0,80},{17,1},{65,17},{81,65},{1,81},{18,2}... | collective-permute-start | bytes 393224 | tf_op jit(solution)/shard_map/ppermute | solution.py:117
  17.5 1.3 collective-permute-start.6
  18.8 1.2 copy-done.2
  21.5 2.0 %copy-done.1 = bf16[16,64,2048]{2,1,0:T(8,128)(2,1)} copy-done((bf16[16,64,2048]{2,1,0:T(8,128)(2,1)}, bf16[16,64,2048]{2,1,0:T(8,128)(2,1)S(1)}, u32[]{:S(2)}) %copy-start.1) | copy-done | bytes 4194328
  24.5 4.5 %all-to-all-start = ((bf16[16,64,2048]{2,1,0:T(8,128)(2,1)}), bf16[16,64,2048]{2,1,0:T(8,128)(2,1)}, u32[]{:S(2)}, u32[]{:S(2)}) async-start(bf16[16,64,2048]{2,1,0:T(8,128)(2,1)} %copy-done.1), calls=%async_computation | async-start | bytes 8388608 | tf_op jit(solution)/shard_map/all_to_all | solution.py:155
  29.2 2.8 %constant_dynamic-update-slice_fusion.4 = (bf16[2048,1024]{1,0:T(8,128)(2,1)}, bf16[256,1024]{1,0:T(8,128)(2,1)S(1)}) fusion(f32[2,1024]{1,0:T(2,128)S(1)} %constant_dynamic-slice_fusion.1, s32[256,4096]{1,0:T(8,128)} %param.8, s32[]{:T(128)S(6)} %select_n.45, bf16[256,4096]{1,0:T(8,128)(2,1)} %param.7, pred[]{:T(512)S(6)} %eq.13), kind=kLoop, calls=%fused_computation.20 | loop fusion | flops 1310719 | bytes 2629637
  32.0 4.1 %collective-permute-start.7 = (bf16[512,1024]{1,0:T(8,128)(2,1)S(1)}, bf16[512,1024]{1,0:T(8,128)(2,1)S(1)}, u32[]{:S(2)}, u32[]{:S(2)}) collective-permute-start(bf16[512,1024]{1,0:T(8,128)(2,1)S(1)} %pad_maximum_fusion), channel_id=1, source_target_pairs={{4,0},{8,4},{12,8},{0,12},{5,1},{9,5},{13,9},{1,13},{6,2},{10,6},{... | collective-permute-start | bytes 3145736 | tf_op jit(solution)/shard_map/ppermute | solution.py:117
  36.1 1.3 collective-permute-start.9
  38.2 41.0 %collective-permute-done.7 = bf16[512,1024]{1,0:T(8,128)(2,1)S(1)} collective-permute-done((bf16[512,1024]{1,0:T(8,128)(2,1)S(1)}, bf16[512,1024]{1,0:T(8,128)(2,1)S(1)}, u32[]{:S(2)}, u32[]{:S(2)}) %collective-permute-start.7) | collective-permute-done | bytes 1048608 | tf_op jit(solution)/shard_map/ppermute | solution.py:117
  81.4 1.3 collective-permute-done.9
  83.7 4.4 %all-to-all-done = bf16[16,64,2048]{2,1,0:T(8,128)(2,1)} async-done(((bf16[16,64,2048]{2,1,0:T(8,128)(2,1)}), bf16[16,64,2048]{2,1,0:T(8,128)(2,1)}, u32[]{:S(2)}, u32[]{:S(2)}) %all-to-all-start) | async-done | bytes 4194336 | tf_op jit(solution)/shard_map/all_to_all | solution.py:155
  88.1 9.3 %convolution_convert_fusion.1 = bf16[1024,1024]{1,0:T(8,128)(2,1)} fusion(bf16[1024,2048]{1,0:T(8,128)(2,1)} %bitcast.3.acts_ref, bf16[2048,1024]{1,0:T(8,128)(2,1)} %constant_dynamic-update-slice_fusion), kind=kOutput, calls=%fused_computation.1 | convolution fusion | flops 4296015872 | bytes 10485760 | tf_op jit(solution)/shard_map/dot_general | solution.py:163
  97.4 4.2 %all-to-all-start.1 = ((bf16[16,64,1024]{2,1,0:T(8,128)(2,1)}), bf16[16,64,1024]{2,1,0:T(8,128)(2,1)S(1)}, u32[]{:S(2)}, u32[]{:S(2)}) async-start(bf16[16,64,1024]{2,1,0:T(8,128)(2,1)} %bitcast.24), calls=%async_computation.1 | async-start | bytes 4194304 | tf_op jit(solution)/shard_map/all_to_all | solution.py:166
  101.7 9.3 %convolution_convert_fusion = bf16[1024,1024]{1,0:T(8,128)(2,1)} fusion(bf16[1024,2048]{1,0:T(8,128)(2,1)} %bitcast.3.acts_ref, bf16[2048,1024]{1,0:T(8,128)(2,1)} %collective-permute-done.10), kind=kOutput, calls=%fused_computation | convolution fusion | flops 4296015872 | bytes 10485760 | tf_op jit(solution)/shard_map/dot_general | solution.py:163
  111.0 20.3 %all-to-all-done.1.first_ref = bf16[16,64,1024]{2,1,0:T(8,128)(2,1)S(1)} async-done(((bf16[16,64,1024]{2,1,0:T(8,128)(2,1)}), bf16[16,64,1024]{2,1,0:T(8,128)(2,1)S(1)}, u32[]{:S(2)}, u32[]{:S(2)}) %all-to-all-start.1) | async-done | bytes 2097184 | tf_op jit(solution)/shard_map/all_to_all | solution.py:166
  131.3 4.6 %all-to-all-start.2 = ((bf16[16,64,1024]{2,1,0:T(8,128)(2,1)}), bf16[16,64,1024]{2,1,0:T(8,128)(2,1)}, u32[]{:S(2)}, u32[]{:S(2)}) async-start(bf16[16,64,1024]{2,1,0:T(8,128)(2,1)} %bitcast.23), calls=%async_computation.2 | async-start | bytes 4194304 | tf_op jit(solution)/shard_map/all_to_all | solution.py:166
  136.0 3.0 %stats.1 = (f32[256,256]{1,0:T(8,128)S(1)}, bf16[256,256]{1,0:T(8,128)(2,1)S(1)}, bf16[256,256]{1,0:T(8,128)(2,1)S(1)}, bf16[256,256]{1,0:T(8,128)(2,1)S(1)}) custom-call(s32[2]{0:T(128)S(1)} %pad_add_fusion.at_ref, bf16[1024,2048]{1,0:T(8,128)(2,1)} %bitcast.3.acts_ref, bf16[256,256]{1,0:T(8,128)(2,1)S(1)} %pad_maximum_fusion.1.refs_0_, ...), custom_call_target="tpu_custom_call" | custom-call | tf_op jit(solution)/shard_map/stats/pallas_call | solution.py:100
  139.0 1.9 %collective-permute-start.13 = (bf16[256,256]{1,0:T(8,128)(2,1)S(1)}, bf16[256,256]{1,0:T(8,128)(2,1)S(1)}, u32[]{:S(2)}, u32[]{:S(2)}) collective-permute-start(bf16[256,256]{1,0:T(8,128)(2,1)S(1)} %get-tuple-element.33), channel_id=1, source_target_pairs={{4,0},{8,4},{12,8},{0,12},{5,1},{9,5},{13,9},{1,13},{6,2},{10,6},{... | collective-permute-start | bytes 393224 | tf_op jit(solution)/shard_map/ppermute | solution.py:117
  141.0 1.3 collective-permute-start.11
  142.3 2.5 %collective-permute-done.13 = bf16[256,256]{1,0:T(8,128)(2,1)S(1)} collective-permute-done((bf16[256,256]{1,0:T(8,128)(2,1)S(1)}, bf16[256,256]{1,0:T(8,128)(2,1)S(1)}, u32[]{:S(2)}, u32[]{:S(2)}) %collective-permute-start.13) | collective-permute-done | bytes 131104 | tf_op jit(solution)/shard_map/ppermute | solution.py:117
  144.9 2.7 %collective-permute-done.12 = bf16[256,256]{1,0:T(8,128)(2,1)S(1)} collective-permute-done((bf16[256,256]{1,0:T(8,128)(2,1)S(1)}, bf16[256,256]{1,0:T(8,128)(2,1)S(1)}, u32[]{:S(2)}, u32[]{:S(2)}) %collective-permute-start.12) | collective-permute-done | bytes 131104 | tf_op jit(solution)/shard_map/ppermute | solution.py:117
  148.8 1.5 collective-permute-done.14
  150.4 3.2 %collective-permute-start.15 = (f32[128,256]{1,0:T(8,128)S(1)}, f32[128,256]{1,0:T(8,128)S(1)}, u32[]{:S(2)}, u32[]{:S(2)}) collective-permute-start(f32[128,256]{1,0:T(8,128)S(1)} %constant_dynamic-slice_fusion), channel_id=1, source_target_pairs={{0,64},{64,0},{1,65},{65,1},{2,66},{66,2},{3,67},{67,3},{4,68},{68... | collective-permute-start | bytes 393224 | tf_op jit(solution)/shard_map/ppermute | solution.py:113
  153.6 8.5 %collective-permute-done.15 = f32[128,256]{1,0:T(8,128)S(1)} collective-permute-done((f32[128,256]{1,0:T(8,128)S(1)}, f32[128,256]{1,0:T(8,128)S(1)}, u32[]{:S(2)}, u32[]{:S(2)}) %collective-permute-start.15) | collective-permute-done | bytes 131104 | tf_op jit(solution)/shard_map/ppermute | solution.py:113
  162.0 1.3 collective-permute-done.16
  165.0 3.0 %finish.1 = (bf16[64,4096]{1,0:T(8,128)(2,1)}, bf16[64,4096]{1,0:T(8,128)(2,1)}) custom-call(s32[1]{0:T(128)} %bitcast.core_ref, bf16[16,64,1024]{2,1,0:T(8,128)(2,1)S(1)} %all-to-all-done.1.first_ref, bf16[16,64,1024]{2,1,0:T(8,128)(2,1)} %all-to-all-done.2.second_ref), custom_call_target="tpu_custom_call" | custom-call | tf_op jit(solution)/shard_map/finish/pallas_call | solution.py:68
  (40 shorter events, 13.8 us)
Async XLA Ops:
  0.6 0.8 copy-start
  3.0 21.6 %collective-permute-start = (bf16[256,1024]{1,0:T(8,128)(2,1)S(1)}, bf16[256,1024]{1,0:T(8,128)(2,1)S(1)}, u32[]{:S(2)}, u32[]{:S(2)}) collective-permute-start(bf16[256,1024]{1,0:T(8,128)(2,1)S(1)} %fusion.2), channel_id=1, source_target_pairs={{0,16},{16,0},{32,112},{48,96},{64,80},{80,64},{96,48},{112,32},{1... | collective-permute-start | bytes 1572872 | tf_op jit(solution)/shard_map/ppermute | solution.py:148
  6.2 5.7 %collective-permute-start.3 = (bf16[64,256]{1,0:T(8,128)(2,1)S(1)}, bf16[64,256]{1,0:T(8,128)(2,1)S(1)}, u32[]{:S(2)}, u32[]{:S(2)}) collective-permute-start(bf16[64,256]{1,0:T(8,128)(2,1)S(1)} %pad_maximum_fusion.2), channel_id=1, source_target_pairs={{3,0},{0,1},{1,2},{2,3},{7,4},{4,5},{5,6},{6,7},{11,8},{8,9},{9,10... | collective-permute-start | bytes 98312 | tf_op jit(solution)/shard_map/ppermute | solution.py:117
  7.7 5.7 %collective-permute-start.2 = (bf16[64,256]{1,0:T(8,128)(2,1)S(1)}, bf16[64,256]{1,0:T(8,128)(2,1)S(1)}, u32[]{:S(2)}, u32[]{:S(2)}) collective-permute-start(bf16[64,256]{1,0:T(8,128)(2,1)S(1)} %pad_maximum_fusion.2), channel_id=1, source_target_pairs={{2,0},{3,1},{0,2},{1,3},{6,4},{7,5},{4,6},{5,7},{10,8},{11,9},{8,1... | collective-permute-start | bytes 98312 | tf_op jit(solution)/shard_map/ppermute | solution.py:117
  10.5 3.9 %collective-permute-start.1 = (bf16[64,256]{1,0:T(8,128)(2,1)S(1)}, bf16[64,256]{1,0:T(8,128)(2,1)S(1)}, u32[]{:S(2)}, u32[]{:S(2)}) collective-permute-start(bf16[64,256]{1,0:T(8,128)(2,1)S(1)} %pad_maximum_fusion.2), channel_id=1, source_target_pairs={{1,0},{2,1},{3,2},{0,3},{5,4},{6,5},{7,6},{4,7},{9,8},{10,9},{11,1... | collective-permute-start | bytes 98312 | tf_op jit(solution)/shard_map/ppermute | solution.py:117
  14.4 9.2 %collective-permute-start.4 = (bf16[256,256]{1,0:T(8,128)(2,1)S(1)}, bf16[256,256]{1,0:T(8,128)(2,1)S(1)}, u32[]{:S(2)}, u32[]{:S(2)}) collective-permute-start(bf16[256,256]{1,0:T(8,128)(2,1)S(1)} %pad_maximum_fusion.1.refs_0_), channel_id=1, source_target_pairs={{16,0},{64,16},{80,64},{0,80},{17,1},{65,17},{81,65},{1,81},{18,2}... | collective-permute-start | bytes 393224 | tf_op jit(solution)/shard_map/ppermute | solution.py:117
  16.6 6.9 %collective-permute-start.5 = (bf16[256,256]{1,0:T(8,128)(2,1)S(1)}, bf16[256,256]{1,0:T(8,128)(2,1)S(1)}, u32[]{:S(2)}, u32[]{:S(2)}) collective-permute-start(bf16[256,256]{1,0:T(8,128)(2,1)S(1)} %pad_maximum_fusion.1.refs_0_), channel_id=1, source_target_pairs={{64,0},{80,16},{0,64},{16,80},{65,1},{81,17},{1,65},{17,81},{66,2}... | collective-permute-start | bytes 393224 | tf_op jit(solution)/shard_map/ppermute | solution.py:117
  17.5 7.1 %collective-permute-start.6 = (bf16[256,256]{1,0:T(8,128)(2,1)S(1)}, bf16[256,256]{1,0:T(8,128)(2,1)S(1)}, u32[]{:S(2)}, u32[]{:S(2)}) collective-permute-start(bf16[256,256]{1,0:T(8,128)(2,1)S(1)} %pad_maximum_fusion.1.refs_0_), channel_id=1, source_target_pairs={{80,0},{0,16},{16,64},{64,80},{81,1},{1,17},{17,65},{65,81},{82,2}... | collective-permute-start | bytes 393224 | tf_op jit(solution)/shard_map/ppermute | solution.py:117
  18.8 1.2 copy-start.2
  20.0 1.2 copy-start.3
  21.5 2.0 %copy-start.1 = (bf16[16,64,2048]{2,1,0:T(8,128)(2,1)}, bf16[16,64,2048]{2,1,0:T(8,128)(2,1)S(1)}, u32[]{:S(2)}) copy-start(bf16[16,64,2048]{2,1,0:T(8,128)(2,1)S(1)} %pack.1) | copy-start | bytes 12582916
  24.5 63.6 %all-to-all-start = ((bf16[16,64,2048]{2,1,0:T(8,128)(2,1)}), bf16[16,64,2048]{2,1,0:T(8,128)(2,1)}, u32[]{:S(2)}, u32[]{:S(2)}) async-start(bf16[16,64,2048]{2,1,0:T(8,128)(2,1)} %copy-done.1), calls=%async_computation | async-start | bytes 8388608 | tf_op jit(solution)/shard_map/all_to_all | solution.py:155
  32.0 47.2 %collective-permute-start.7 = (bf16[512,1024]{1,0:T(8,128)(2,1)S(1)}, bf16[512,1024]{1,0:T(8,128)(2,1)S(1)}, u32[]{:S(2)}, u32[]{:S(2)}) collective-permute-start(bf16[512,1024]{1,0:T(8,128)(2,1)S(1)} %pad_maximum_fusion), channel_id=1, source_target_pairs={{4,0},{8,4},{12,8},{0,12},{5,1},{9,5},{13,9},{1,13},{6,2},{10,6},{... | collective-permute-start | bytes 3145736 | tf_op jit(solution)/shard_map/ppermute | solution.py:117
  36.1 44.2 %collective-permute-start.8 = (bf16[512,1024]{1,0:T(8,128)(2,1)S(1)}, bf16[512,1024]{1,0:T(8,128)(2,1)S(1)}, u32[]{:S(2)}, u32[]{:S(2)}) collective-permute-start(bf16[512,1024]{1,0:T(8,128)(2,1)S(1)} %pad_maximum_fusion), channel_id=1, source_target_pairs={{8,0},{12,4},{0,8},{4,12},{9,1},{13,5},{1,9},{5,13},{10,2},{14,6},... | collective-permute-start | bytes 3145736 | tf_op jit(solution)/shard_map/ppermute | solution.py:117
  36.1 46.5 %collective-permute-start.9 = (bf16[512,1024]{1,0:T(8,128)(2,1)S(1)}, bf16[512,1024]{1,0:T(8,128)(2,1)S(1)}, u32[]{:S(2)}, u32[]{:S(2)}) collective-permute-start(bf16[512,1024]{1,0:T(8,128)(2,1)S(1)} %pad_maximum_fusion), channel_id=1, source_target_pairs={{12,0},{0,4},{4,8},{8,12},{13,1},{1,5},{5,9},{9,13},{14,2},{2,6},{... | collective-permute-start | bytes 3145736 | tf_op jit(solution)/shard_map/ppermute | solution.py:117
  83.7 17.9 %collective-permute-start.10 = (bf16[2048,1024]{1,0:T(8,128)(2,1)}, bf16[2048,1024]{1,0:T(8,128)(2,1)}, u32[]{:S(2)}, u32[]{:S(2)}) collective-permute-start(bf16[2048,1024]{1,0:T(8,128)(2,1)} %constant_dynamic-update-slice_fusion), channel_id=1, source_target_pairs={{0,32},{32,0},{1,33},{33,1},{2,34},{34,2},{3,35},{35,3},{4,36},{36... | collective-permute-start | bytes 12582920 | tf_op jit(solution)/shard_map/ppermute | solution.py:113
  97.4 33.8 %all-to-all-start.1 = ((bf16[16,64,1024]{2,1,0:T(8,128)(2,1)}), bf16[16,64,1024]{2,1,0:T(8,128)(2,1)S(1)}, u32[]{:S(2)}, u32[]{:S(2)}) async-start(bf16[16,64,1024]{2,1,0:T(8,128)(2,1)} %bitcast.24), calls=%async_computation.1 | async-start | bytes 4194304 | tf_op jit(solution)/shard_map/all_to_all | solution.py:166
  131.3 33.7 %all-to-all-start.2 = ((bf16[16,64,1024]{2,1,0:T(8,128)(2,1)}), bf16[16,64,1024]{2,1,0:T(8,128)(2,1)}, u32[]{:S(2)}, u32[]{:S(2)}) async-start(bf16[16,64,1024]{2,1,0:T(8,128)(2,1)} %bitcast.23), calls=%async_computation.2 | async-start | bytes 4194304 | tf_op jit(solution)/shard_map/all_to_all | solution.py:166
  139.0 5.9 %collective-permute-start.13 = (bf16[256,256]{1,0:T(8,128)(2,1)S(1)}, bf16[256,256]{1,0:T(8,128)(2,1)S(1)}, u32[]{:S(2)}, u32[]{:S(2)}) collective-permute-start(bf16[256,256]{1,0:T(8,128)(2,1)S(1)} %get-tuple-element.33), channel_id=1, source_target_pairs={{4,0},{8,4},{12,8},{0,12},{5,1},{9,5},{13,9},{1,13},{6,2},{10,6},{... | collective-permute-start | bytes 393224 | tf_op jit(solution)/shard_map/ppermute | solution.py:117
  140.9 6.6 %collective-permute-start.12 = (bf16[256,256]{1,0:T(8,128)(2,1)S(1)}, bf16[256,256]{1,0:T(8,128)(2,1)S(1)}, u32[]{:S(2)}, u32[]{:S(2)}) collective-permute-start(bf16[256,256]{1,0:T(8,128)(2,1)S(1)} %get-tuple-element.32), channel_id=1, source_target_pairs={{8,0},{12,4},{0,8},{4,12},{9,1},{13,5},{1,9},{5,13},{10,2},{14,6},... | collective-permute-start | bytes 393224 | tf_op jit(solution)/shard_map/ppermute | solution.py:117
  141.0 7.6 %collective-permute-start.11 = (bf16[256,256]{1,0:T(8,128)(2,1)S(1)}, bf16[256,256]{1,0:T(8,128)(2,1)S(1)}, u32[]{:S(2)}, u32[]{:S(2)}) collective-permute-start(bf16[256,256]{1,0:T(8,128)(2,1)S(1)} %get-tuple-element.31), channel_id=1, source_target_pairs={{12,0},{0,4},{4,8},{8,12},{13,1},{1,5},{5,9},{9,13},{14,2},{2,6},{... | collective-permute-start | bytes 393224 | tf_op jit(solution)/shard_map/ppermute | solution.py:117
  148.7 1.6 collective-permute-start.14
  150.4 11.7 %collective-permute-start.15 = (f32[128,256]{1,0:T(8,128)S(1)}, f32[128,256]{1,0:T(8,128)S(1)}, u32[]{:S(2)}, u32[]{:S(2)}) collective-permute-start(f32[128,256]{1,0:T(8,128)S(1)} %constant_dynamic-slice_fusion), channel_id=1, source_target_pairs={{0,64},{64,0},{1,65},{65,1},{2,66},{66,2},{3,67},{67,3},{4,68},{68... | collective-permute-start | bytes 393224 | tf_op jit(solution)/shard_map/ppermute | solution.py:113
  162.0 1.3 collective-permute-start.16

commit v11 on v5

--- a/solution.py
+++ b/solution.py
@@ -1,3 +1,5 @@
+import functools
+
 import jax
 import jax.numpy as jnp
 from jax import lax
@@ -7,6 +9,7 @@
 from jax.sharding import PartitionSpec as P
 
 BLOCK = 128
+FIRST = 512
 FINE = ("yh", "core", "yl", "z", "x")
 PLANE = ("yh", "yl", "x")
 F32 = jnp.float32
@@ -48,26 +51,79 @@
     )(z.reshape(1), attn_float, attn_quant)
 
 
+def join_kernel(*refs):
+    *parts, out_ref = refs
+    row = 0
+    for part in parts:
+        out_ref[row : row + part.shape[0]] = part[...]
+        row += part.shape[0]
+
+
+def join(parts):
+    cols = parts[0].shape[1]
+    return pl.pallas_call(
+        join_kernel,
+        out_shape=jax.ShapeDtypeStruct((sum(p.shape[0] for p in parts), cols), BF16),
+        in_specs=[WHOLE] * len(parts),
+        out_specs=WHOLE,
+        compiler_params=params(),
+        name="join",
+    )(*parts)
+
+
+def project_kernel(first, acts_ref, *refs):
+    *weights, out_ref = refs
+    at = 0
+    for n, ref in enumerate(weights):
+        for col in range(first if n == 0 else 0, ref.shape[1], FIRST):
+            for row in range(0, acts_ref.shape[0], 256):
+                out_ref[row : row + 256, at : at + FIRST] = jnp.dot(
+                    acts_ref[row : row + 256, :],
+                    ref[:, col : col + FIRST],
+                    preferred_element_type=F32,
+                ).astype(BF16)
+            at += FIRST
+
+
+def project(acts, weights, first):
+    rows, depth = acts.shape
+    cols = sum(w.shape[1] for w in weights) - first
+    return pl.pallas_call(
+        functools.partial(project_kernel, first),
+        out_shape=jax.ShapeDtypeStruct((rows, cols), BF16),
+        in_specs=[WHOLE] * (1 + len(weights)),
+        out_specs=WHOLE,
+        compiler_params=params(),
+        cost_estimate=pl.CostEstimate(
+            flops=2 * rows * depth * cols, bytes_accessed=14 << 20, transcendentals=0
+        ),
+        name="project",
+    )(acts, *weights)
+
+
 def finish_kernel(core_ref, first_ref, second_ref, float_ref, quant_ref):
     core = core_ref[0]
-    width = first_ref.shape[2]
-    for n, ref in enumerate((first_ref, second_ref)):
-        quarter = core if n == 0 else 1 - core
+    quarter = float_ref.shape[1] // 4
+    pieces = [(first_ref, 0, FIRST, core, 0), (second_ref, 0, quarter - FIRST, core, FIRST)]
+    pieces.append((second_ref, quarter - FIRST, quarter, 1 - core, 0))
+    for ref, col, width, place, shift in pieces:
         for kind, out in enumerate((float_ref, quant_ref)):
             for half in range(2):
                 at = kind * 8 + half * 4
-                total = ref[at].astype(F32)
+                cols = slice(col, col + width)
+                total = ref[at, :, cols].astype(F32)
                 for x in range(1, 4):
-                    total += ref[at + x].astype(F32)
-                start = pl.multiple_of((half * 2 + quarter) * width, width)
+                    total += ref[at + x, :, cols].astype(F32)
+                start = pl.multiple_of((half * 2 + place) * quarter + shift, FIRST)
                 out[:, pl.ds(start, width)] = total.astype(BF16)
 
 
 def finish(core, first, second):
-    _, tokens, width = first.shape
+    tokens = first.shape[1]
+    cols = 2 * (first.shape[2] + second.shape[2])
     return pl.pallas_call(
         finish_kernel,
-        out_shape=(jax.ShapeDtypeStruct((tokens, 4 * width), BF16),) * 2,
+        out_shape=(jax.ShapeDtypeStruct((tokens, cols), BF16),) * 2,
         in_specs=[SCALAR, WHOLE, WHOLE],
         out_specs=(WHOLE, WHOLE),
         compiler_params=params(),
@@ -133,7 +189,6 @@
         quant = (values * scales[:, None, :]).reshape(features, quarter).astype(BF16)
         return jnp.where(kind == 0, plain, quant)
 
-    own = weight(yh, yl * half + core * quarter)
     send = weight(yh ^ core, (1 - yl) * half + core * quarter)
     pairs = []
     for a in range(2):
@@ -141,42 +196,40 @@
             for b in range(2):
                 pairs.append((a * 4 + c * 2 + b, (a ^ c) * 4 + c * 2 + (1 - b)))
     got = lax.ppermute(send, ("yh", "core", "yl"), pairs)
+    col, send = lax.optimization_barrier((yl * half + core * quarter, send))
+    own = weight(yh, col)
 
     payload = pack(z, attn_float, attn_quant)
-    rows = jnp.concatenate([own, got], axis=0)
-    parts = [rows] + [ahead(rows, "z", j) for j in (1, 2, 3)]
-    mine = jnp.concatenate(parts, axis=0)
+    payload, got = lax.optimization_barrier((payload, got))
+
+    acts = lax.all_to_all(payload, PLANE, 0, 0, tiled=True).reshape(16 * tokens, 8 * features)
+
+    rows = join((own, got))
+    mine = join([rows] + [ahead(rows, "z", j) for j in (1, 2, 3)])
     other = swap(mine, "core")
 
     quant = attn_quant[:, :BLOCK]
     shift = (attn_float[:, :BLOCK].astype(F32) - quant.astype(F32)).astype(BF16)
     block = jnp.concatenate([quant, shift], axis=1)
-    block, payload = lax.optimization_barrier((block, payload))
-    acts = lax.all_to_all(payload, PLANE, 0, 0, tiled=True).reshape(16 * tokens, 8 * features)
-
+    block, mine = lax.optimization_barrier((block, mine))
     line = jnp.concatenate([block] + [ahead(block, "x", j) for j in (1, 2, 3)], axis=0)
+
+    def output(p):
+        return lax.all_to_all(p.reshape(16, tokens, -1), PLANE, 0, 0, tiled=True)
+
+    first = jnp.dot(acts, mine[:, :FIRST], preferred_element_type=F32).astype(BF16)
+    line, first = lax.optimization_barrier((line, first))
+    result1 = output(first)
     pieces = [line] + [ahead(line, ("yh", "yl"), j) for j in (1, 2, 3)]
-    acts, mine, *pieces = lax.optimization_barrier((acts, mine, *pieces))
-
-    def part(w):
-        return jnp.dot(acts, w, preferred_element_type=F32).astype(BF16)
-
-    def output(p):
-        return lax.all_to_all(p.reshape(16, tokens, quarter), PLANE, 0, 0, tiled=True)
-
-    first = part(mine)
-    result1 = output(first)
-
-    acts1, first = lax.optimization_barrier((acts, first))
-    blocks = stats(jnp.stack([yh * 2 + yl, lax.axis_index("x")]), acts1, pieces)
+    second = project(acts, (mine, other), FIRST)
+    second, result1, *pieces = lax.optimization_barrier((second, result1, *pieces))
+    result2 = output(second)
+
+    blocks = stats(jnp.stack([yh * 2 + yl, lax.axis_index("x")]), acts, pieces)
     total = blocks[0]
     for j in (1, 2, 3):
         total = total + ahead(blocks[j], "z", 4 - j).astype(F32)
-    other, total = lax.optimization_barrier((other, total))
-    second = part(other)
     total = (total + swap(total, "core")) * inverse
-    second, total = lax.optimization_barrier((second, total))
-    result2 = output(second)
 
     piece = swap(lax.dynamic_slice_in_dim(total, core * BLOCK, BLOCK, 0), "yh")
     again = swap(piece, "core")

time: 184 us -> 172 us (0.935)
  waiting for transfers between devices: 105 us -> 79 us
  Pallas kernels: 6.29 us -> 20.2 us
  matrix products: 18.7 us -> 6.28 us
  starting transfers between devices: 38.5 us -> 43.6 us
  local copies, waits for them, and re-layouts: 9.72 us -> 13.1 us
  other arithmetic: 3.58 us -> 5.87 us
    pallas_call x1 -> x4, Pallas kernels: 3 us -> 16.9 us  [the longest x1 11.3 us: project(): pl.pallas_call(functools.partial(project_kernel, first), out_shape=jax.Sh...]
    dot_general x2 -> x1, matrix products: 18.7 us -> 6.28 us  [shards(): jnp.dot(acts, mine[:, :FIRST], preferred_element_type=F32).astype(BF16)]
    ppermute x4, waiting for transfers between devices: 24.3 us -> 15.7 us  [swap(): return lax.ppermute(a, axis, [(0, 1), (1, 0)])]
    all_to_all x2, waiting for transfers between devices: 10.1 us -> 2.27 us  [output(): return lax.all_to_all(p.reshape(16, tokens, -1), PLANE, 0, 0, tiled=True)]
    ppermute x12, waiting for transfers between devices: 63 us -> 57.7 us  [ahead(): return lax.ppermute(a, axis, [((i + j) % 4, i) for i in range(4)])]
    unnamed x13 -> x28, local copies, waits for them, and re-layouts: 7.07 us -> 12.3 us
    ppermute x1, waiting for transfers between devices: 7.5 us -> 3.13 us  [shards(): got = lax.ppermute(send, ('yh', 'core', 'yl'), pairs)]
    ppermute x12, starting transfers between devices: 17.9 us -> 20.9 us  [ahead(): return lax.ppermute(a, axis, [((i + j) % 4, i) for i in range(4)])]
  transfers between devices with their start and end apart: 20 -> 20, of which waited for: 15 -> 14; matrix products, arithmetic and copies ran while one was open for 14% -> 7% of each run, Pallas kernels for 2% -> 11%
where the time goes in v11:
time: 172 us; the launch traced here: 169 us
  waiting for transfers between devices  79 us (46%)
  starting transfers between devices  43.6 us (25%)
  Pallas kernels  20.2 us (12%)
  local copies, waits for them, and re-layouts  13.1 us (8%)
  matrix products  6.28 us (4%)
  other arithmetic  5.87 us (3%)
    ppermute x12, waiting for transfers between devices, ahead(): return lax.ppermute(a, axis, [((i + j) % 4, i) for i in range(4)])  57.7 us
    ppermute x12, starting transfers between devices, ahead(): return lax.ppermute(a, axis, [((i + j) % 4, i) for i in range(4)])  20.9 us
    ppermute x4, waiting for transfers between devices, swap(): return lax.ppermute(a, axis, [(0, 1), (1, 0)])  15.7 us
    unnamed x28, local copies, waits for them, and re-layouts  12.3 us
    pallas_call x1, Pallas kernels, project(): pl.pallas_call(functools.partial(project_kernel, first), out_shape=jax.Sh...  11.3 us
    all_to_all x2, starting transfers between devices, output(): return lax.all_to_all(p.reshape(16, tokens, -1), PLANE, 0, 0, tiled=True)  10.3 us
    all_to_all x1, starting transfers between devices, shards(): lax.all_to_all(payload, PLANE, 0, 0, tiled=True)  7.09 us
    dot_general x1, matrix products, shards(): jnp.dot(acts, mine[:, :FIRST], preferred_element_type=F32).astype(BF16)  6.28 us
  transfers between devices with their start and end apart: 20, of which 14 were waited for; matrix products, arithmetic and copies ran while one was open for 7% of the time, Pallas kernels for 11%

profile of v11, /device:TPU:0, one launch (start us, length us, event | category | flops | bytes accessed | tf_op | source)
XLA Modules:
  0.0 169.0 jit_solution(10804613020616065450)
XLA Ops:
  1.4 1.6 fusion.7
  3.0 1.7 %collective-permute-start = (bf16[256,1024]{1,0:T(8,128)(2,1)S(1)}, bf16[256,1024]{1,0:T(8,128)(2,1)S(1)}, u32[]{:S(2)}, u32[]{:S(2)}) collective-permute-start(bf16[256,1024]{1,0:T(8,128)(2,1)S(1)} %fusion.7), channel_id=1, source_target_pairs={{0,16},{16,0},{32,112},{48,96},{64,80},{80,64},{96,48},{112,32},{1... | collective-permute-start | bytes 1572872 | tf_op jit(solution)/shard_map/ppermute | solution.py:198
  4.8 1.9 %fusion.8.refs_0_ = bf16[256,1024]{1,0:T(8,128)(2,1)S(1)} fusion(s32[256,4096]{1,0:T(8,128)} %param.8, s32[]{:T(128)S(6)} %select_n.45, f32[2,1024]{1,0:T(2,128)S(1)} %constant_dynamic-slice_fusion.1, bf16[256,4096]{1,0:T(8,128)(2,1)} %param.7, pred[]{:T(512)S(6)} %eq.13), kind=kLoop, calls=%fused_computation.8 | loop fusion | flops 1310720 | bytes 2105349 | tf_op jit(solution)/shard_map/jit(_where)/select_n | solution.py:190
  7.1 2.0 %copy-done.1 = bf16[16,64,2048]{2,1,0:T(8,128)(2,1)} copy-done((bf16[16,64,2048]{2,1,0:T(8,128)(2,1)}, bf16[16,64,2048]{2,1,0:T(8,128)(2,1)S(1)}, u32[]{:S(2)}) %copy-start.1) | copy-done | bytes 4194328
  9.1 3.1 %collective-permute-done.refs_1_ = bf16[256,1024]{1,0:T(8,128)(2,1)S(1)} collective-permute-done((bf16[256,1024]{1,0:T(8,128)(2,1)S(1)}, bf16[256,1024]{1,0:T(8,128)(2,1)S(1)}, u32[]{:S(2)}, u32[]{:S(2)}) %collective-permute-start) | collective-permute-done | bytes 524320 | tf_op jit(solution)/shard_map/ppermute | solution.py:198
  14.1 4.2 %collective-permute-start.1 = (bf16[512,1024]{1,0:T(8,128)(2,1)S(1)}, bf16[512,1024]{1,0:T(8,128)(2,1)}, u32[]{:S(2)}, u32[]{:S(2)}) collective-permute-start(bf16[512,1024]{1,0:T(8,128)(2,1)S(1)} %join.2.refs_0_), channel_id=1, source_target_pairs={{4,0},{8,4},{12,8},{0,12},{5,1},{9,5},{13,9},{1,13},{6,2},{10,6},{... | collective-permute-start | bytes 3145736 | tf_op jit(solution)/shard_map/ppermute | solution.py:173
  18.3 1.3 collective-permute-start.3
  19.6 7.1 %all-to-all-start = ((bf16[16,64,2048]{2,1,0:T(8,128)(2,1)}), bf16[16,64,2048]{2,1,0:T(8,128)(2,1)}, u32[]{:S(2)}, u32[]{:S(2)}) async-start(bf16[16,64,2048]{2,1,0:T(8,128)(2,1)} %copy-done.1), calls=%async_computation | async-start | bytes 8388608 | tf_op jit(solution)/shard_map/all_to_all | solution.py:205
  26.7 36.6 %collective-permute-done.1.refs_1_ = bf16[512,1024]{1,0:T(8,128)(2,1)} collective-permute-done((bf16[512,1024]{1,0:T(8,128)(2,1)S(1)}, bf16[512,1024]{1,0:T(8,128)(2,1)}, u32[]{:S(2)}, u32[]{:S(2)}) %collective-permute-start.1) | collective-permute-done | bytes 1048608 | tf_op jit(solution)/shard_map/ppermute | solution.py:173
  63.3 3.5 %collective-permute-done.3.refs_3_ = bf16[512,1024]{1,0:T(8,128)(2,1)} collective-permute-done((bf16[512,1024]{1,0:T(8,128)(2,1)S(1)}, bf16[512,1024]{1,0:T(8,128)(2,1)}, u32[]{:S(2)}, u32[]{:S(2)}) %collective-permute-start.3) | collective-permute-done | bytes 1048608 | tf_op jit(solution)/shard_map/ppermute | solution.py:173
  66.9 4.1 %join.3.refs_0_ = bf16[2048,1024]{1,0:T(8,128)(2,1)} custom-call(bf16[512,1024]{1,0:T(8,128)(2,1)S(1)} %join.2.refs_0_, bf16[512,1024]{1,0:T(8,128)(2,1)} %collective-permute-done.1.refs_1_, bf16[512,1024]{1,0:T(8,128)(2,1)} %collective-permute-done.2.refs_2_, bf16[512,1024]{1,0:T(8,128)(2,1)} %collective-permute-done.3.refs_3_), custom_call_target="tpu_custom_call" | custom-call | tf_op jit(solution)/shard_map/join/pallas_call | solution.py:64
  71.0 1.6 collective-permute-start.7
  72.6 2.7 %collective-permute-start.6 = (bf16[64,256]{1,0:T(8,128)(2,1)S(1)}, bf16[64,256]{1,0:T(8,128)(2,1)S(1)}, u32[]{:S(2)}, u32[]{:S(2)}) collective-permute-start(bf16[64,256]{1,0:T(8,128)(2,1)S(1)} %pad_maximum_fusion.1), channel_id=1, source_target_pairs={{2,0},{3,1},{0,2},{1,3},{6,4},{7,5},{4,6},{5,7},{10,8},{11,9},{8,1... | collective-permute-start | bytes 98312 | tf_op jit(solution)/shard_map/ppermute | solution.py:173
  75.3 1.4 collective-permute-start.5
  76.8 4.5 %collective-permute-done.7 = bf16[64,256]{1,0:T(8,128)(2,1)S(1)} collective-permute-done((bf16[64,256]{1,0:T(8,128)(2,1)S(1)}, bf16[64,256]{1,0:T(8,128)(2,1)S(1)}, u32[]{:S(2)}, u32[]{:S(2)}) %collective-permute-start.7) | collective-permute-done | bytes 32800 | tf_op jit(solution)/shard_map/ppermute | solution.py:173
  81.2 6.4 %collective-permute-done.6 = bf16[64,256]{1,0:T(8,128)(2,1)S(1)} collective-permute-done((bf16[64,256]{1,0:T(8,128)(2,1)S(1)}, bf16[64,256]{1,0:T(8,128)(2,1)S(1)}, u32[]{:S(2)}, u32[]{:S(2)}) %collective-permute-start.6) | collective-permute-done | bytes 32800 | tf_op jit(solution)/shard_map/ppermute | solution.py:173
  87.9 6.3 %fusion.2 = bf16[1024,512]{1,0:T(8,128)(2,1)} fusion(bf16[1024,2048]{1,0:T(8,128)(2,1)} %bitcast.3.acts_ref, bf16[2048,1024]{1,0:T(8,128)(2,1)} %join.3.refs_0_), kind=kOutput, calls=%fused_computation.2 | convolution fusion | flops 2148007936 | bytes 7340032 | tf_op jit(solution)/shard_map/dot_general | solution.py:220
  94.2 4.6 %all-to-all-start.1 = ((bf16[16,64,512]{2,1,0:T(8,128)(2,1)}), bf16[16,64,512]{2,1,0:T(8,128)(2,1)S(1)}, u32[]{:S(2)}, u32[]{:S(2)}) async-start(bf16[16,64,512]{2,1,0:T(8,128)(2,1)} %bitcast.5), calls=%async_computation.1 | async-start | bytes 2097152 | tf_op jit(solution)/shard_map/all_to_all | solution.py:218
  98.8 3.1 %collective-permute-start.8 = (bf16[256,256]{1,0:T(8,128)(2,1)S(1)}, bf16[256,256]{1,0:T(8,128)(2,1)S(1)}, u32[]{:S(2)}, u32[]{:S(2)}) collective-permute-start(bf16[256,256]{1,0:T(8,128)(2,1)S(1)} %pad_maximum_fusion.refs_0_), channel_id=1, source_target_pairs={{16,0},{64,16},{80,64},{0,80},{17,1},{65,17},{81,65},{1,81},{18,2}... | collective-permute-start | bytes 393224 | tf_op jit(solution)/shard_map/ppermute | solution.py:173
  103.6 11.3 %project.1 = bf16[1024,1536]{1,0:T(8,128)(2,1)S(1)} custom-call(bf16[1024,2048]{1,0:T(8,128)(2,1)} %bitcast.3.acts_ref, bf16[2048,1024]{1,0:T(8,128)(2,1)} %join.3.refs_0_, bf16[2048,1024]{1,0:T(8,128)(2,1)} %collective-permute-done.4.refs_1_), custom_call_target="tpu_custom_call" | custom-call | flops 6442450944 | bytes 14680064 | tf_op jit(solution)/shard_map/project/pallas_call | solution.py:91
  115.0 1.6 copy-done.4
  119.4 5.7 %all-to-all-start.2 = ((bf16[16,64,1536]{2,1,0:T(8,128)(2,1)}), bf16[16,64,1536]{2,1,0:T(8,128)(2,1)S(1)}, u32[]{:S(2)}, u32[]{:S(2)}) async-start(bf16[16,64,1536]{2,1,0:T(8,128)(2,1)} %bitcast.20), calls=%async_computation.2 | async-start | bytes 6291456 | tf_op jit(solution)/shard_map/all_to_all | solution.py:218
  127.1 3.0 %stats.1 = (f32[256,256]{1,0:T(8,128)S(1)}, bf16[256,256]{1,0:T(8,128)(2,1)S(1)}, bf16[256,256]{1,0:T(8,128)(2,1)S(1)}, bf16[256,256]{1,0:T(8,128)(2,1)S(1)}) custom-call(s32[2]{0:T(128)S(1)} %pad_add_fusion.at_ref, bf16[1024,2048]{1,0:T(8,128)(2,1)} %bitcast.3.acts_ref, bf16[256,256]{1,0:T(8,128)(2,1)S(1)} %pad_maximum_fusion.refs_0_, ...), custom_call_target="tpu_custom_call" | custom-call | tf_op jit(solution)/shard_map/stats/pallas_call | solution.py:156
  130.1 3.2 %collective-permute-start.13 = (bf16[256,256]{1,0:T(8,128)(2,1)S(1)}, bf16[256,256]{1,0:T(8,128)(2,1)S(1)}, u32[]{:S(2)}, u32[]{:S(2)}) collective-permute-start(bf16[256,256]{1,0:T(8,128)(2,1)S(1)} %get-tuple-element.41), channel_id=1, source_target_pairs={{4,0},{8,4},{12,8},{0,12},{5,1},{9,5},{13,9},{1,13},{6,2},{10,6},{... | collective-permute-start | bytes 393224 | tf_op jit(solution)/shard_map/ppermute | solution.py:173
  135.8 4.0 %collective-permute-done.12 = bf16[256,256]{1,0:T(8,128)(2,1)S(1)} collective-permute-done((bf16[256,256]{1,0:T(8,128)(2,1)S(1)}, bf16[256,256]{1,0:T(8,128)(2,1)S(1)}, u32[]{:S(2)}, u32[]{:S(2)}) %collective-permute-start.12) | collective-permute-done | bytes 131104 | tf_op jit(solution)/shard_map/ppermute | solution.py:173
  139.7 1.4 collective-permute-done.11
  144.0 3.5 %collective-permute-start.15 = (f32[128,256]{1,0:T(8,128)S(1)}, f32[128,256]{1,0:T(8,128)}, u32[]{:S(2)}, u32[]{:S(2)}) collective-permute-start(f32[128,256]{1,0:T(8,128)S(1)} %constant_dynamic-slice_fusion), channel_id=1, source_target_pairs={{0,64},{64,0},{1,65},{65,1},{2,66},{66,2},{3,67},{67,3},{4,68},{68... | collective-permute-start | bytes 393224 | tf_op jit(solution)/shard_map/ppermute | solution.py:169
  147.5 13.0 %collective-permute-done.15 = f32[128,256]{1,0:T(8,128)} collective-permute-done((f32[128,256]{1,0:T(8,128)S(1)}, f32[128,256]{1,0:T(8,128)}, u32[]{:S(2)}, u32[]{:S(2)}) %collective-permute-start.15) | collective-permute-done | bytes 131104 | tf_op jit(solution)/shard_map/ppermute | solution.py:169
  160.5 1.7 collective-permute-done.16
  164.1 2.3 %all-to-all-done.2.second_ref = bf16[16,64,1536]{2,1,0:T(8,128)(2,1)S(1)} async-done(((bf16[16,64,1536]{2,1,0:T(8,128)(2,1)}), bf16[16,64,1536]{2,1,0:T(8,128)(2,1)S(1)}, u32[]{:S(2)}, u32[]{:S(2)}) %all-to-all-start.2) | async-done | bytes 3145760 | tf_op jit(solution)/shard_map/all_to_all | solution.py:218
  166.4 1.2 copy-done.3
  167.6 1.4 finish.1
  (58 shorter events, 17.0 us)
Async XLA Ops:
  0.6 0.8 copy-start
  0.6 6.1 %copy-start.6 = (bf16[64,8192]{1,0:T(8,128)(2,1)S(1)}, bf16[64,8192]{1,0:T(8,128)(2,1)}, u32[]{:S(2)}) copy-start(bf16[64,8192]{1,0:T(8,128)(2,1)} %float_ref.1) | copy-start | bytes 3145732
  0.7 6.1 %copy-start.5 = (bf16[64,8192]{1,0:T(8,128)(2,1)S(1)}, bf16[64,8192]{1,0:T(8,128)(2,1)}, u32[]{:S(2)}) copy-start(bf16[64,8192]{1,0:T(8,128)(2,1)} %quant_ref.1) | copy-start | bytes 3145732
  3.0 9.3 %collective-permute-start = (bf16[256,1024]{1,0:T(8,128)(2,1)S(1)}, bf16[256,1024]{1,0:T(8,128)(2,1)S(1)}, u32[]{:S(2)}, u32[]{:S(2)}) collective-permute-start(bf16[256,1024]{1,0:T(8,128)(2,1)S(1)} %fusion.7), channel_id=1, source_target_pairs={{0,16},{16,0},{32,112},{48,96},{64,80},{80,64},{96,48},{112,32},{1... | collective-permute-start | bytes 1572872 | tf_op jit(solution)/shard_map/ppermute | solution.py:198
  7.0 2.0 %copy-start.1 = (bf16[16,64,2048]{2,1,0:T(8,128)(2,1)}, bf16[16,64,2048]{2,1,0:T(8,128)(2,1)S(1)}, u32[]{:S(2)}) copy-start(bf16[16,64,2048]{2,1,0:T(8,128)(2,1)S(1)} %pack.1) | copy-start | bytes 12582916
  12.2 0.8 copy-start.7
  13.0 1.0 copy-start.8
  14.1 49.2 %collective-permute-start.1 = (bf16[512,1024]{1,0:T(8,128)(2,1)S(1)}, bf16[512,1024]{1,0:T(8,128)(2,1)}, u32[]{:S(2)}, u32[]{:S(2)}) collective-permute-start(bf16[512,1024]{1,0:T(8,128)(2,1)S(1)} %join.2.refs_0_), channel_id=1, source_target_pairs={{4,0},{8,4},{12,8},{0,12},{5,1},{9,5},{13,9},{1,13},{6,2},{10,6},{... | collective-permute-start | bytes 3145736 | tf_op jit(solution)/shard_map/ppermute | solution.py:173
  18.3 45.0 %collective-permute-start.2 = (bf16[512,1024]{1,0:T(8,128)(2,1)S(1)}, bf16[512,1024]{1,0:T(8,128)(2,1)}, u32[]{:S(2)}, u32[]{:S(2)}) collective-permute-start(bf16[512,1024]{1,0:T(8,128)(2,1)S(1)} %join.2.refs_0_), channel_id=1, source_target_pairs={{8,0},{12,4},{0,8},{4,12},{9,1},{13,5},{1,9},{5,13},{10,2},{14,6},... | collective-permute-start | bytes 3145736 | tf_op jit(solution)/shard_map/ppermute | solution.py:173
  18.3 48.5 %collective-permute-start.3 = (bf16[512,1024]{1,0:T(8,128)(2,1)S(1)}, bf16[512,1024]{1,0:T(8,128)(2,1)}, u32[]{:S(2)}, u32[]{:S(2)}) collective-permute-start(bf16[512,1024]{1,0:T(8,128)(2,1)S(1)} %join.2.refs_0_), channel_id=1, source_target_pairs={{12,0},{0,4},{4,8},{8,12},{13,1},{1,5},{5,9},{9,13},{14,2},{2,6},{... | collective-permute-start | bytes 3145736 | tf_op jit(solution)/shard_map/ppermute | solution.py:173
  19.6 68.3 %all-to-all-start = ((bf16[16,64,2048]{2,1,0:T(8,128)(2,1)}), bf16[16,64,2048]{2,1,0:T(8,128)(2,1)}, u32[]{:S(2)}, u32[]{:S(2)}) async-start(bf16[16,64,2048]{2,1,0:T(8,128)(2,1)} %copy-done.1), calls=%async_computation | async-start | bytes 8388608 | tf_op jit(solution)/shard_map/all_to_all | solution.py:205
  26.7 44.3 %slice-start = ((bf16[64,8192]{1,0:T(8,128)(2,1)}), bf16[64,128]{1,0:T(8,128)(2,1)S(1)}, s32[]{:S(2)}) async-start(bf16[64,8192]{1,0:T(8,128)(2,1)} %quant_ref.1), calls=%async_computation.3 | async-start | bytes 32768 | tf_op jit(solution)/shard_map/slice | solution.py:211
  71.0 32.6 %collective-permute-start.4 = (bf16[2048,1024]{1,0:T(8,128)(2,1)}, bf16[2048,1024]{1,0:T(8,128)(2,1)}, u32[]{:S(2)}, u32[]{:S(2)}) collective-permute-start(bf16[2048,1024]{1,0:T(8,128)(2,1)} %join.3.refs_0_), channel_id=1, source_target_pairs={{0,32},{32,0},{1,33},{33,1},{2,34},{34,2},{3,35},{35,3},{4,36},{36... | collective-permute-start | bytes 12582920 | tf_op jit(solution)/shard_map/ppermute | solution.py:169
  71.0 10.2 %collective-permute-start.7 = (bf16[64,256]{1,0:T(8,128)(2,1)S(1)}, bf16[64,256]{1,0:T(8,128)(2,1)S(1)}, u32[]{:S(2)}, u32[]{:S(2)}) collective-permute-start(bf16[64,256]{1,0:T(8,128)(2,1)S(1)} %pad_maximum_fusion.1), channel_id=1, source_target_pairs={{3,0},{0,1},{1,2},{2,3},{7,4},{4,5},{5,6},{6,7},{11,8},{8,9},{9,10... | collective-permute-start | bytes 98312 | tf_op jit(solution)/shard_map/ppermute | solution.py:173
  72.6 15.1 %collective-permute-start.6 = (bf16[64,256]{1,0:T(8,128)(2,1)S(1)}, bf16[64,256]{1,0:T(8,128)(2,1)S(1)}, u32[]{:S(2)}, u32[]{:S(2)}) collective-permute-start(bf16[64,256]{1,0:T(8,128)(2,1)S(1)} %pad_maximum_fusion.1), channel_id=1, source_target_pairs={{2,0},{3,1},{0,2},{1,3},{6,4},{7,5},{4,6},{5,7},{10,8},{11,9},{8,1... | collective-permute-start | bytes 98312 | tf_op jit(solution)/shard_map/ppermute | solution.py:173
  75.3 12.3 %collective-permute-start.5 = (bf16[64,256]{1,0:T(8,128)(2,1)S(1)}, bf16[64,256]{1,0:T(8,128)(2,1)S(1)}, u32[]{:S(2)}, u32[]{:S(2)}) collective-permute-start(bf16[64,256]{1,0:T(8,128)(2,1)S(1)} %pad_maximum_fusion.1), channel_id=1, source_target_pairs={{1,0},{2,1},{3,2},{0,3},{5,4},{6,5},{7,6},{4,7},{9,8},{10,9},{11,1... | collective-permute-start | bytes 98312 | tf_op jit(solution)/shard_map/ppermute | solution.py:173
  94.2 24.1 %all-to-all-start.1 = ((bf16[16,64,512]{2,1,0:T(8,128)(2,1)}), bf16[16,64,512]{2,1,0:T(8,128)(2,1)S(1)}, u32[]{:S(2)}, u32[]{:S(2)}) async-start(bf16[16,64,512]{2,1,0:T(8,128)(2,1)} %bitcast.5), calls=%async_computation.1 | async-start | bytes 2097152 | tf_op jit(solution)/shard_map/all_to_all | solution.py:218
  98.8 17.8 %collective-permute-start.8 = (bf16[256,256]{1,0:T(8,128)(2,1)S(1)}, bf16[256,256]{1,0:T(8,128)(2,1)S(1)}, u32[]{:S(2)}, u32[]{:S(2)}) collective-permute-start(bf16[256,256]{1,0:T(8,128)(2,1)S(1)} %pad_maximum_fusion.refs_0_), channel_id=1, source_target_pairs={{16,0},{64,16},{80,64},{0,80},{17,1},{65,17},{81,65},{1,81},{18,2}... | collective-permute-start | bytes 393224 | tf_op jit(solution)/shard_map/ppermute | solution.py:173
  101.9 14.7 %collective-permute-start.9 = (bf16[256,256]{1,0:T(8,128)(2,1)S(1)}, bf16[256,256]{1,0:T(8,128)(2,1)S(1)}, u32[]{:S(2)}, u32[]{:S(2)}) collective-permute-start(bf16[256,256]{1,0:T(8,128)(2,1)S(1)} %pad_maximum_fusion.refs_0_), channel_id=1, source_target_pairs={{64,0},{80,16},{0,64},{16,80},{65,1},{81,17},{1,65},{17,81},{66,2}... | collective-permute-start | bytes 393224 | tf_op jit(solution)/shard_map/ppermute | solution.py:173
  102.8 14.9 %collective-permute-start.10 = (bf16[256,256]{1,0:T(8,128)(2,1)S(1)}, bf16[256,256]{1,0:T(8,128)(2,1)S(1)}, u32[]{:S(2)}, u32[]{:S(2)}) collective-permute-start(bf16[256,256]{1,0:T(8,128)(2,1)S(1)} %pad_maximum_fusion.refs_0_), channel_id=1, source_target_pairs={{80,0},{0,16},{16,64},{64,80},{81,1},{1,17},{17,65},{65,81},{82,2}... | collective-permute-start | bytes 393224 | tf_op jit(solution)/shard_map/ppermute | solution.py:173
  114.9 1.6 copy-start.4
  118.3 1.1 copy-start.2
  119.4 46.9 %all-to-all-start.2 = ((bf16[16,64,1536]{2,1,0:T(8,128)(2,1)}), bf16[16,64,1536]{2,1,0:T(8,128)(2,1)S(1)}, u32[]{:S(2)}, u32[]{:S(2)}) async-start(bf16[16,64,1536]{2,1,0:T(8,128)(2,1)} %bitcast.20), calls=%async_computation.2 | async-start | bytes 6291456 | tf_op jit(solution)/shard_map/all_to_all | solution.py:218
  125.3 0.9 copy-start.10
  126.2 0.9 copy-start.12
  130.1 5.7 %collective-permute-start.13 = (bf16[256,256]{1,0:T(8,128)(2,1)S(1)}, bf16[256,256]{1,0:T(8,128)(2,1)S(1)}, u32[]{:S(2)}, u32[]{:S(2)}) collective-permute-start(bf16[256,256]{1,0:T(8,128)(2,1)S(1)} %get-tuple-element.41), channel_id=1, source_target_pairs={{4,0},{8,4},{12,8},{0,12},{5,1},{9,5},{13,9},{1,13},{6,2},{10,6},{... | collective-permute-start | bytes 393224 | tf_op jit(solution)/shard_map/ppermute | solution.py:173
  133.2 6.5 %collective-permute-start.12 = (bf16[256,256]{1,0:T(8,128)(2,1)S(1)}, bf16[256,256]{1,0:T(8,128)(2,1)S(1)}, u32[]{:S(2)}, u32[]{:S(2)}) collective-permute-start(bf16[256,256]{1,0:T(8,128)(2,1)S(1)} %get-tuple-element.40), channel_id=1, source_target_pairs={{8,0},{12,4},{0,8},{4,12},{9,1},{13,5},{1,9},{5,13},{10,2},{14,6},... | collective-permute-start | bytes 393224 | tf_op jit(solution)/shard_map/ppermute | solution.py:173
  134.4 6.7 %collective-permute-start.11 = (bf16[256,256]{1,0:T(8,128)(2,1)S(1)}, bf16[256,256]{1,0:T(8,128)(2,1)S(1)}, u32[]{:S(2)}, u32[]{:S(2)}) collective-permute-start(bf16[256,256]{1,0:T(8,128)(2,1)S(1)} %get-tuple-element.39), channel_id=1, source_target_pairs={{12,0},{0,4},{4,8},{8,12},{13,1},{1,5},{5,9},{9,13},{14,2},{2,6},{... | collective-permute-start | bytes 393224 | tf_op jit(solution)/shard_map/ppermute | solution.py:173
  141.2 1.7 %collective-permute-start.14 = (f32[256,256]{1,0:T(8,128)S(1)}, f32[256,256]{1,0:T(8,128)}, u32[]{:S(2)}, u32[]{:S(2)}) collective-permute-start(f32[256,256]{1,0:T(8,128)S(1)} %convert_add_fusion), channel_id=1, source_target_pairs={{0,32},{32,0},{1,33},{33,1},{2,34},{34,2},{3,35},{35,3},{4,36},{36... | collective-permute-start | bytes 786440 | tf_op jit(solution)/shard_map/ppermute | solution.py:169
  144.0 16.5 %collective-permute-start.15 = (f32[128,256]{1,0:T(8,128)S(1)}, f32[128,256]{1,0:T(8,128)}, u32[]{:S(2)}, u32[]{:S(2)}) collective-permute-start(f32[128,256]{1,0:T(8,128)S(1)} %constant_dynamic-slice_fusion), channel_id=1, source_target_pairs={{0,64},{64,0},{1,65},{65,1},{2,66},{66,2},{3,67},{67,3},{4,68},{68... | collective-permute-start | bytes 393224 | tf_op jit(solution)/shard_map/ppermute | solution.py:169
  160.5 1.7 %collective-permute-start.16 = (f32[128,256]{1,0:T(8,128)}, f32[128,256]{1,0:T(8,128)}, u32[]{:S(2)}, u32[]{:S(2)}) collective-permute-start(f32[128,256]{1,0:T(8,128)} %collective-permute-done.15), channel_id=1, source_target_pairs={{0,32},{32,0},{1,33},{33,1},{2,34},{34,2},{3,35},{35,3},{4,36},{36... | collective-permute-start | bytes 393224 | tf_op jit(solution)/shard_map/ppermute | solution.py:169
  166.4 1.2 copy-start.3
  (3 other events, 2.0 us)

commit v12 on v10

--- a/solution.py
+++ b/solution.py
@@ -14,6 +14,7 @@
 
 
 WHOLE = pl.BlockSpec(memory_space=pltpu.VMEM)
+LEFT = pl.BlockSpec(memory_space=pl.ANY)
 SCALAR = pl.BlockSpec(memory_space=pltpu.SMEM)
 
 
@@ -48,35 +49,76 @@
     )(z.reshape(1), attn_float, attn_quant)
 
 
-def finish_kernel(core_ref, first_ref, second_ref, float_ref, quant_ref):
-    core = core_ref[0]
-    width = first_ref.shape[2]
-    for n, ref in enumerate((first_ref, second_ref)):
-        quarter = core if n == 0 else 1 - core
-        for kind, out in enumerate((float_ref, quant_ref)):
+def project_kernel(acts_ref, *refs):
+    *weights, out_ref = refs
+    depth, width = weights[0].shape
+    tile = 512
+    for q in range(2):
+        for col in range(0, width, tile):
+            for row in range(0, acts_ref.shape[0], 256):
+                rows, total = slice(row, row + 256), None
+                for j in range(4):
+                    term = jnp.dot(
+                        acts_ref[rows, j * depth : (j + 1) * depth],
+                        weights[4 * q + j][:, col : col + tile],
+                        preferred_element_type=F32,
+                    )
+                    total = term if total is None else total + term
+                at = q * width + col
+                out_ref[rows, at : at + tile] = total.astype(BF16)
+
+
+def project(acts, weights):
+    rows, depth = acts.shape
+    cols = 2 * weights[0].shape[1]
+    return pl.pallas_call(
+        project_kernel,
+        out_shape=jax.ShapeDtypeStruct((rows, cols), BF16),
+        in_specs=[WHOLE] * (1 + len(weights)),
+        out_specs=WHOLE,
+        compiler_params=params(),
+        cost_estimate=pl.CostEstimate(
+            flops=2 * rows * depth * cols, bytes_accessed=16 << 20, transcendentals=0
+        ),
+        name="project",
+    )(acts, *weights)
+
+
+def finish_kernel(at_ref, parts_ref, total_ref, moved_ref, *outs):
+    core, yh = at_ref[0], at_ref[1]
+    width = parts_ref.shape[2] // 2
+    for q in range(2):
+        quarter = core if q == 0 else 1 - core
+        for kind, out in enumerate(outs[:2]):
             for half in range(2):
                 at = kind * 8 + half * 4
-                total = ref[at].astype(F32)
+                cols = slice(q * width, (q + 1) * width)
+                total = parts_ref[at, :, cols].astype(F32)
                 for x in range(1, 4):
-                    total += ref[at + x].astype(F32)
+                    total += parts_ref[at + x, :, cols].astype(F32)
                 start = pl.multiple_of((half * 2 + quarter) * width, width)
                 out[:, pl.ds(start, width)] = total.astype(BF16)
-
-
-def finish(core, first, second):
-    _, tokens, width = first.shape
+    total = jnp.where(yh == 1, total_ref[...], moved_ref[...])
+    outs[2][...] = total[:, :BLOCK]
+    outs[3][...] = total[:, BLOCK:]
+
+
+def finish(at, parts, total, moved):
+    tokens, cols = parts.shape[1:]
+    rows = total.shape[0]
     return pl.pallas_call(
         finish_kernel,
-        out_shape=(jax.ShapeDtypeStruct((tokens, 4 * width), BF16),) * 2,
-        in_specs=[SCALAR, WHOLE, WHOLE],
-        out_specs=(WHOLE, WHOLE),
+        out_shape=(jax.ShapeDtypeStruct((tokens, 2 * cols), BF16),) * 2
+        + (jax.ShapeDtypeStruct((rows, BLOCK), F32),) * 2,
+        in_specs=[SCALAR] + [WHOLE] * 3,
+        out_specs=(WHOLE,) * 4,
         compiler_params=params(),
         name="finish",
-    )(core.reshape(1), first, second)
+    )(at, parts, total, moved)
 
 
 def stats_kernel(at_ref, acts_ref, *refs):
-    pieces, outs, block_ref = refs[:4], refs[4:8], refs[8]
+    pieces, outs, block_ref = refs[:4], refs[5:9], refs[9]
     y, x = at_ref[0], at_ref[1]
     tokens = pieces[0].shape[0] // 4
     for dy, piece in enumerate(pieces):
@@ -95,18 +137,18 @@
         ).astype(out.dtype)
 
 
-def stats(at, acts, pieces):
+def stats(at, acts, pieces, after):
     width = 2 * BLOCK
     return pl.pallas_call(
         stats_kernel,
         out_shape=(jax.ShapeDtypeStruct((width, width), F32),)
         + (jax.ShapeDtypeStruct((width, width), BF16),) * 3,
-        in_specs=[SCALAR] + [WHOLE] * 5,
+        in_specs=[SCALAR] + [WHOLE] * 5 + [LEFT],
         out_specs=(WHOLE,) * 4,
         scratch_shapes=[pltpu.VMEM((acts.shape[0], width), BF16)],
         compiler_params=params(),
         name="stats",
-    )(at, acts, *pieces)
+    )(at, acts, *pieces, after)
 
 
 def swap(a, axis):
@@ -132,12 +174,6 @@
         values = (codes - 8).astype(F32).reshape(groups, features // groups, quarter)
         quant = (values * scales[:, None, :]).reshape(features, quarter).astype(BF16)
         return jnp.where(kind == 0, plain, quant)
-
-    quant = attn_quant[:, :BLOCK]
-    shift = (attn_float[:, :BLOCK].astype(F32) - quant.astype(F32)).astype(BF16)
-    block = jnp.concatenate([quant, shift], axis=1)
-    line = jnp.concatenate([block] + [ahead(block, "x", j) for j in (1, 2, 3)], axis=0)
-    pieces = [line] + [ahead(line, ("yh", "yl"), j) for j in (1, 2, 3)]
 
     send = weight(yh ^ core, (1 - yl) * half + core * quarter)
     pairs = []
@@ -150,40 +186,32 @@
     own = weight(yh, col)
 
     payload = pack(z, attn_float, attn_quant)
-    payload, got, *pieces = lax.optimization_barrier((payload, got, *pieces))
+    payload, got = lax.optimization_barrier((payload, got))
 
     acts = lax.all_to_all(payload, PLANE, 0, 0, tiled=True).reshape(16 * tokens, 8 * features)
 
     rows = jnp.concatenate([own, got], axis=0)
     parts = [rows] + [ahead(rows, "z", j) for j in (1, 2, 3)]
-    mine = jnp.concatenate(parts, axis=0)
-    other = swap(mine, "core")
-
-    def part(w):
-        return jnp.dot(acts, w, preferred_element_type=F32).astype(BF16)
-
-    def output(p):
-        return lax.all_to_all(p.reshape(16, tokens, quarter), PLANE, 0, 0, tiled=True)
-
-    result1 = output(part(mine))
-    second = part(other)
-
-    acts1, second = lax.optimization_barrier((acts, second))
-    blocks = stats(jnp.stack([yh * 2 + yl, lax.axis_index("x")]), acts1, pieces)
-    result2 = output(second)
+    weights = parts + [swap(p, "core") for p in parts]
+
+    quant = attn_quant[:, :BLOCK]
+    shift = (attn_float[:, :BLOCK].astype(F32) - quant.astype(F32)).astype(BF16)
+    block = jnp.concatenate([quant, shift], axis=1)
+    block, *parts = lax.optimization_barrier((block, *parts))
+    line = jnp.concatenate([block] + [ahead(block, "x", j) for j in (1, 2, 3)], axis=0)
+    line, acts = lax.optimization_barrier((line, acts))
+    pieces = [line] + [ahead(line, ("yh", "yl"), j) for j in (1, 2, 3)]
+
+    partial = project(acts, weights)
+    partial, *pieces = lax.optimization_barrier((partial, *pieces))
+    result = lax.all_to_all(partial.reshape(16, tokens, half), PLANE, 0, 0, tiled=True)
+
+    blocks = stats(jnp.stack([yh * 2 + yl, lax.axis_index("x")]), acts, pieces, partial)
     total = blocks[0]
     for j in (1, 2, 3):
         total = total + ahead(blocks[j], "z", 4 - j).astype(F32)
     total = (total + swap(total, "core")) * inverse
-
-    piece = swap(lax.dynamic_slice_in_dim(total, core * BLOCK, BLOCK, 0), "yh")
-    again = swap(piece, "core")
-    moved = jnp.where(
-        core == 0, jnp.concatenate([piece, again]), jnp.concatenate([again, piece])
-    )
-    total = jnp.where(yh == 1, total, moved)
-    float_out, quant_out = finish(core, result1, result2)
-    return float_out, quant_out, total[:, :BLOCK], total[:, BLOCK:]
+    return finish(jnp.stack([core, yh]), result, total, swap(total, "yh"))
 
 
 def solution(mesh):

time: 169 us -> 174 us (1.030)
  matrix products: 18.7 us -> 0 us
  Pallas kernels: 6.28 us -> 19.7 us
  waiting for transfers between devices: 88.9 us -> 102 us
    dot_general x2 -> x0, matrix products: 18.7 us -> none  [part(): return jnp.dot(acts, w, preferred_element_type=F32).astype(BF16)]
    ppermute x4 -> x6, waiting for transfers between devices: 11.3 us -> 28 us  [swap(): return lax.ppermute(a, axis, [(0, 1), (1, 0)])]
    all_to_all x2 -> x1, waiting for transfers between devices: 21.1 us -> 6.47 us  [shards(): lax.all_to_all(partial.reshape(16, tokens, half), PLANE, 0, 0, tiled=True)]
    pallas_call x1 -> x2, Pallas kernels: 3 us -> 16.5 us  [the longest x1 12.8 us: project(): pl.pallas_call(project_kernel, out_shape=jax.ShapeDtypeStruct((rows, cols...]
    ppermute x12, waiting for transfers between devices: 52 us -> 64.3 us  [ahead(): return lax.ppermute(a, axis, [((i + j) % 4, i) for i in range(4)])]
    all_to_all x1, waiting for transfers between devices: 4.36 us -> 0.01 us  [shards(): lax.all_to_all(payload, PLANE, 0, 0, tiled=True)]
    all_to_all x2 -> x1, starting transfers between devices: 8.83 us -> 4.56 us  [shards(): lax.all_to_all(partial.reshape(16, tokens, half), PLANE, 0, 0, tiled=True)]
    unnamed x1 -> x0, other arithmetic: 2.79 us -> none
  transfers between devices with their start and end apart: 20 -> 21, of which waited for: 14 -> 13; matrix products, arithmetic and copies ran while one was open for 17% -> 2% of each run, Pallas kernels for 2% -> 9%
where the time goes in v12:
time: 174 us; the launch traced here: 173 us
  waiting for transfers between devices  102 us (59%)
  starting transfers between devices  37.1 us (21%)
  Pallas kernels  19.7 us (11%)
  local copies, waits for them, and re-layouts  9.47 us (5%)
  other arithmetic  4.63 us (3%)
    ppermute x12, waiting for transfers between devices, ahead(): return lax.ppermute(a, axis, [((i + j) % 4, i) for i in range(4)])  64.3 us
    ppermute x6, waiting for transfers between devices, swap(): return lax.ppermute(a, axis, [(0, 1), (1, 0)])  28 us
    ppermute x12, starting transfers between devices, ahead(): return lax.ppermute(a, axis, [((i + j) % 4, i) for i in range(4)])  20.2 us
    pallas_call x1, Pallas kernels, project(): pl.pallas_call(project_kernel, out_shape=jax.ShapeDtypeStruct((rows, cols...  12.8 us
    unnamed x14, local copies, waits for them, and re-layouts  9.39 us
    all_to_all x1, starting transfers between devices, shards(): lax.all_to_all(payload, PLANE, 0, 0, tiled=True)  7.17 us
    all_to_all x1, waiting for transfers between devices, shards(): lax.all_to_all(partial.reshape(16, tokens, half), PLANE, 0, 0, tiled=True)  6.47 us
    all_to_all x1, starting transfers between devices, shards(): lax.all_to_all(partial.reshape(16, tokens, half), PLANE, 0, 0, tiled=True)  4.56 us
  transfers between devices with their start and end apart: 21, of which 13 were waited for; matrix products, arithmetic and copies ran while one was open for 2% of the time, Pallas kernels for 9%

profile of v12, /device:TPU:0, one launch (start us, length us, event | category | flops | bytes accessed | tf_op | source)
XLA Modules:
  0.0 173.3 jit_solution(11736511222831842841)
XLA Ops:
  1.4 1.6 fusion.2
  3.0 1.7 %collective-permute-start = (bf16[256,1024]{1,0:T(8,128)(2,1)S(1)}, bf16[256,1024]{1,0:T(8,128)(2,1)S(1)}, u32[]{:S(2)}, u32[]{:S(2)}) collective-permute-start(bf16[256,1024]{1,0:T(8,128)(2,1)S(1)} %fusion.2), channel_id=1, source_target_pairs={{0,16},{16,0},{32,112},{48,96},{64,80},{80,64},{96,48},{112,32},{1... | collective-permute-start | bytes 1572872 | tf_op jit(solution)/shard_map/ppermute | solution.py:184
  7.5 2.0 %copy-done.1 = bf16[16,64,2048]{2,1,0:T(8,128)(2,1)} copy-done((bf16[16,64,2048]{2,1,0:T(8,128)(2,1)}, bf16[16,64,2048]{2,1,0:T(8,128)(2,1)S(1)}, u32[]{:S(2)}) %copy-start.1) | copy-done | bytes 4194328
  9.5 2.8 %collective-permute-done = bf16[256,1024]{1,0:T(8,128)(2,1)S(1)} collective-permute-done((bf16[256,1024]{1,0:T(8,128)(2,1)S(1)}, bf16[256,1024]{1,0:T(8,128)(2,1)S(1)}, u32[]{:S(2)}, u32[]{:S(2)}) %collective-permute-start) | collective-permute-done | bytes 524320 | tf_op jit(solution)/shard_map/ppermute | solution.py:184
  12.2 7.2 %all-to-all-start = ((bf16[16,64,2048]{2,1,0:T(8,128)(2,1)}), bf16[16,64,2048]{2,1,0:T(8,128)(2,1)}, u32[]{:S(2)}, u32[]{:S(2)}) async-start(bf16[16,64,2048]{2,1,0:T(8,128)(2,1)} %copy-done.1), calls=%async_computation | async-start | bytes 8388608 | tf_op jit(solution)/shard_map/all_to_all | solution.py:191
  19.5 2.0 %fusion.3 = bf16[256,1024]{1,0:T(8,128)(2,1)S(1)} fusion(s32[256,4096]{1,0:T(8,128)} %param.8, s32[]{:T(128)S(6)} %select_n.28, f32[2,1024]{1,0:T(2,128)S(1)} %constant_dynamic-slice_fusion, bf16[256,4096]{1,0:T(8,128)(2,1)} %param.7, pred[]{:T(512)S(6)} %eq.6), kind=kLoop, calls=%fused_computation.6 | loop fusion | flops 1310720 | bytes 2105349 | tf_op jit(solution)/shard_map/jit(_where)/select_n | solution.py:176
  21.6 2.0 %collective-permute-start.3 = (bf16[512,1024]{1,0:T(8,128)(2,1)S(1)}, bf16[512,1024]{1,0:T(8,128)(2,1)S(1)}, u32[]{:S(2)}, u32[]{:S(2)}) collective-permute-start(bf16[512,1024]{1,0:T(8,128)(2,1)S(1)} %pad_maximum_fusion.refs_0_), channel_id=1, source_target_pairs={{12,0},{0,4},{4,8},{8,12},{13,1},{1,5},{5,9},{9,13},{14,2},{2,6},{... | collective-permute-start | bytes 3145736 | tf_op jit(solution)/shard_map/ppermute | solution.py:159
  23.6 2.2 %collective-permute-start.1 = (bf16[512,1024]{1,0:T(8,128)(2,1)S(1)}, bf16[512,1024]{1,0:T(8,128)(2,1)}, u32[]{:S(2)}, u32[]{:S(2)}) collective-permute-start(bf16[512,1024]{1,0:T(8,128)(2,1)S(1)} %pad_maximum_fusion.refs_0_), channel_id=1, source_target_pairs={{4,0},{8,4},{12,8},{0,12},{5,1},{9,5},{13,9},{1,13},{6,2},{10,6},{... | collective-permute-start | bytes 3145736 | tf_op jit(solution)/shard_map/ppermute | solution.py:159
  25.8 1.8 %collective-permute-start.2 = (bf16[512,1024]{1,0:T(8,128)(2,1)S(1)}, bf16[512,1024]{1,0:T(8,128)(2,1)}, u32[]{:S(2)}, u32[]{:S(2)}) collective-permute-start(bf16[512,1024]{1,0:T(8,128)(2,1)S(1)} %pad_maximum_fusion.refs_0_), channel_id=1, source_target_pairs={{8,0},{12,4},{0,8},{4,12},{9,1},{13,5},{1,9},{5,13},{10,2},{14,6},... | collective-permute-start | bytes 3145736 | tf_op jit(solution)/shard_map/ppermute | solution.py:159
  27.6 21.3 %collective-permute-done.3.refs_3_ = bf16[512,1024]{1,0:T(8,128)(2,1)S(1)} collective-permute-done((bf16[512,1024]{1,0:T(8,128)(2,1)S(1)}, bf16[512,1024]{1,0:T(8,128)(2,1)S(1)}, u32[]{:S(2)}, u32[]{:S(2)}) %collective-permute-start.3) | collective-permute-done | bytes 1048608 | tf_op jit(solution)/shard_map/ppermute | solution.py:159
  48.9 21.4 %collective-permute-done.1.refs_1_ = bf16[512,1024]{1,0:T(8,128)(2,1)} collective-permute-done((bf16[512,1024]{1,0:T(8,128)(2,1)S(1)}, bf16[512,1024]{1,0:T(8,128)(2,1)}, u32[]{:S(2)}, u32[]{:S(2)}) %collective-permute-start.1) | collective-permute-done | bytes 1048608 | tf_op jit(solution)/shard_map/ppermute | solution.py:159
  70.3 1.9 %collective-permute-done.2.refs_2_ = bf16[512,1024]{1,0:T(8,128)(2,1)} collective-permute-done((bf16[512,1024]{1,0:T(8,128)(2,1)S(1)}, bf16[512,1024]{1,0:T(8,128)(2,1)}, u32[]{:S(2)}, u32[]{:S(2)}) %collective-permute-start.2) | collective-permute-done | bytes 1048608 | tf_op jit(solution)/shard_map/ppermute | solution.py:159
  73.0 2.9 %collective-permute-start.4 = (bf16[64,256]{1,0:T(8,128)(2,1)S(1)}, bf16[64,256]{1,0:T(8,128)(2,1)S(1)}, u32[]{:S(2)}, u32[]{:S(2)}) collective-permute-start(bf16[64,256]{1,0:T(8,128)(2,1)S(1)} %pad_maximum_fusion.2), channel_id=1, source_target_pairs={{1,0},{2,1},{3,2},{0,3},{5,4},{6,5},{7,6},{4,7},{9,8},{10,9},{11,1... | collective-permute-start | bytes 98312 | tf_op jit(solution)/shard_map/ppermute | solution.py:159
  75.8 5.1 %collective-permute-done.4 = bf16[64,256]{1,0:T(8,128)(2,1)S(1)} collective-permute-done((bf16[64,256]{1,0:T(8,128)(2,1)S(1)}, bf16[64,256]{1,0:T(8,128)(2,1)S(1)}, u32[]{:S(2)}, u32[]{:S(2)}) %collective-permute-start.4) | collective-permute-done | bytes 32800 | tf_op jit(solution)/shard_map/ppermute | solution.py:159
  81.0 5.4 %collective-permute-done.5 = bf16[64,256]{1,0:T(8,128)(2,1)S(1)} collective-permute-done((bf16[64,256]{1,0:T(8,128)(2,1)S(1)}, bf16[64,256]{1,0:T(8,128)(2,1)S(1)}, u32[]{:S(2)}, u32[]{:S(2)}) %collective-permute-start.5) | collective-permute-done | bytes 32800 | tf_op jit(solution)/shard_map/ppermute | solution.py:159
  86.4 5.1 %collective-permute-done.6 = bf16[64,256]{1,0:T(8,128)(2,1)S(1)} collective-permute-done((bf16[64,256]{1,0:T(8,128)(2,1)S(1)}, bf16[64,256]{1,0:T(8,128)(2,1)S(1)}, u32[]{:S(2)}, u32[]{:S(2)}) %collective-permute-start.6) | collective-permute-done | bytes 32800 | tf_op jit(solution)/shard_map/ppermute | solution.py:159
  91.6 1.8 %collective-permute-start.11 = (bf16[256,256]{1,0:T(8,128)(2,1)S(1)}, bf16[256,256]{1,0:T(8,128)(2,1)S(1)}, u32[]{:S(2)}, u32[]{:S(2)}) collective-permute-start(bf16[256,256]{1,0:T(8,128)(2,1)S(1)} %pad_maximum_fusion.1.refs_0_), channel_id=1, source_target_pairs={{16,0},{64,16},{80,64},{0,80},{17,1},{65,17},{81,65},{1,81},{18,2}... | collective-permute-start | bytes 393224 | tf_op jit(solution)/shard_map/ppermute | solution.py:159
  93.3 1.3 collective-permute-start.12
  94.6 1.3 collective-permute-start.13
  96.0 12.8 %project.1.refs_4_ = bf16[1024,2048]{1,0:T(8,128)(2,1)S(1)} custom-call(bf16[1024,2048]{1,0:T(8,128)(2,1)} %bitcast.5.acts_ref, bf16[512,1024]{1,0:T(8,128)(2,1)S(1)} %pad_maximum_fusion.refs_0_, bf16[512,1024]{1,0:T(8,128)(2,1)} %collective-permute-done.1.refs_1_, bf16[512,1024]{1,0:T(8,128)(2,1)} %collective-permute-done.2.refs_2_, ...), custom_call_target="tpu_custom_call" | custom-call | flops 8589934592 | bytes 16777216 | tf_op jit(solution)/shard_map/project/pallas_call | solution.py:74
  108.8 2.0 %copy-done.2 = bf16[1024,2048]{1,0:T(8,128)(2,1)} copy-done((bf16[1024,2048]{1,0:T(8,128)(2,1)}, bf16[1024,2048]{1,0:T(8,128)(2,1)S(1)}, u32[]{:S(2)}) %copy-start.2) | copy-done | bytes 4194328
  110.8 4.6 %all-to-all-start.1 = ((bf16[16,64,2048]{2,1,0:T(8,128)(2,1)}), bf16[16,64,2048]{2,1,0:T(8,128)(2,1)}, u32[]{:S(2)}, u32[]{:S(2)}) async-start(bf16[16,64,2048]{2,1,0:T(8,128)(2,1)} %bitcast.19), calls=%async_computation.1 | async-start | bytes 8388608 | tf_op jit(solution)/shard_map/all_to_all | solution.py:207
  115.4 2.2 %copy-done.3 = bf16[1024,2048]{1,0:T(8,128)(2,1)S(1)} copy-done((bf16[1024,2048]{1,0:T(8,128)(2,1)S(1)}, bf16[1024,2048]{1,0:T(8,128)(2,1)}, u32[]{:S(2)}) %copy-start.3) | copy-done | bytes 4194328
  117.6 3.0 %stats.1 = (f32[256,256]{1,0:T(8,128)S(1)}, bf16[256,256]{1,0:T(8,128)(2,1)S(1)}, bf16[256,256]{1,0:T(8,128)(2,1)S(1)}, bf16[256,256]{1,0:T(8,128)(2,1)S(1)}) custom-call(s32[2]{0:T(128)S(1)} %pad_add_fusion.1.at_ref, bf16[1024,2048]{1,0:T(8,128)(2,1)} %bitcast.5.acts_ref, bf16[256,256]{1,0:T(8,128)(2,1)S(1)} %pad_maximum_fusion.1.refs_0_, ...), custom_call_target="tpu_custom_call" | custom-call | tf_op jit(solution)/shard_map/stats/pallas_call | solution.py:142
  120.6 2.0 %collective-permute-start.14 = (bf16[256,256]{1,0:T(8,128)(2,1)S(1)}, bf16[256,256]{1,0:T(8,128)(2,1)S(1)}, u32[]{:S(2)}, u32[]{:S(2)}) collective-permute-start(bf16[256,256]{1,0:T(8,128)(2,1)S(1)} %get-tuple-element.31), channel_id=1, source_target_pairs={{12,0},{0,4},{4,8},{8,12},{13,1},{1,5},{5,9},{9,13},{14,2},{2,6},{... | collective-permute-start | bytes 393224 | tf_op jit(solution)/shard_map/ppermute | solution.py:159
  122.6 3.9 %collective-permute-start.15 = (bf16[256,256]{1,0:T(8,128)(2,1)S(1)}, bf16[256,256]{1,0:T(8,128)(2,1)S(1)}, u32[]{:S(2)}, u32[]{:S(2)}) collective-permute-start(bf16[256,256]{1,0:T(8,128)(2,1)S(1)} %get-tuple-element.32), channel_id=1, source_target_pairs={{8,0},{12,4},{0,8},{4,12},{9,1},{13,5},{1,9},{5,13},{10,2},{14,6},... | collective-permute-start | bytes 393224 | tf_op jit(solution)/shard_map/ppermute | solution.py:159
  128.1 2.9 %collective-permute-done.15 = bf16[256,256]{1,0:T(8,128)(2,1)S(1)} collective-permute-done((bf16[256,256]{1,0:T(8,128)(2,1)S(1)}, bf16[256,256]{1,0:T(8,128)(2,1)S(1)}, u32[]{:S(2)}, u32[]{:S(2)}) %collective-permute-start.15) | collective-permute-done | bytes 131104 | tf_op jit(solution)/shard_map/ppermute | solution.py:159
  131.7 1.5 collective-permute-done.17
  133.3 3.4 %collective-permute-start.18 = (f32[256,256]{1,0:T(8,128)S(1)}, f32[256,256]{1,0:T(8,128)S(1)}, u32[]{:S(2)}, u32[]{:S(2)}) collective-permute-start(f32[256,256]{1,0:T(8,128)S(1)} %add_multiply_fusion.total_ref), channel_id=1, source_target_pairs={{0,64},{64,0},{1,65},{65,1},{2,66},{66,2},{3,67},{67,3},{4,68},{68... | collective-permute-start | bytes 786440 | tf_op jit(solution)/shard_map/ppermute | solution.py:155
  136.7 26.5 %collective-permute-done.18.moved_ref = f32[256,256]{1,0:T(8,128)S(1)} collective-permute-done((f32[256,256]{1,0:T(8,128)S(1)}, f32[256,256]{1,0:T(8,128)S(1)}, u32[]{:S(2)}, u32[]{:S(2)}) %collective-permute-start.18) | collective-permute-done | bytes 262176 | tf_op jit(solution)/shard_map/ppermute | solution.py:155
  163.2 6.5 %all-to-all-done.1.parts_ref = bf16[16,64,2048]{2,1,0:T(8,128)(2,1)} async-done(((bf16[16,64,2048]{2,1,0:T(8,128)(2,1)}), bf16[16,64,2048]{2,1,0:T(8,128)(2,1)}, u32[]{:S(2)}, u32[]{:S(2)}) %all-to-all-start.1) | async-done | bytes 4194336 | tf_op jit(solution)/shard_map/all_to_all | solution.py:207
  169.6 3.7 %finish.1 = (bf16[64,4096]{1,0:T(8,128)(2,1)}, bf16[64,4096]{1,0:T(8,128)(2,1)}, f32[256,128]{1,0:T(8,128)}, f32[256,128]{1,0:T(8,128)}) custom-call(s32[2]{0:T(128)S(1)} %pad_add_fusion.at_ref, bf16[16,64,2048]{2,1,0:T(8,128)(2,1)} %all-to-all-done.1.parts_ref, f32[256,256]{1,0:T(8,128)S(1)} %add_multiply_fusion.total_ref, ...), custom_call_target="tpu_custom_call" | custom-call | tf_op jit(solution)/shard_map/finish/pallas_call | solution.py:109
  (42 shorter events, 6.9 us)
Async XLA Ops:
  0.6 0.8 copy-start
  3.0 9.3 %collective-permute-start = (bf16[256,1024]{1,0:T(8,128)(2,1)S(1)}, bf16[256,1024]{1,0:T(8,128)(2,1)S(1)}, u32[]{:S(2)}, u32[]{:S(2)}) collective-permute-start(bf16[256,1024]{1,0:T(8,128)(2,1)S(1)} %fusion.2), channel_id=1, source_target_pairs={{0,16},{16,0},{32,112},{48,96},{64,80},{80,64},{96,48},{112,32},{1... | collective-permute-start | bytes 1572872 | tf_op jit(solution)/shard_map/ppermute | solution.py:184
  4.7 1.2 copy-start.4
  5.9 1.2 copy-start.6
  7.4 2.0 %copy-start.1 = (bf16[16,64,2048]{2,1,0:T(8,128)(2,1)}, bf16[16,64,2048]{2,1,0:T(8,128)(2,1)S(1)}, u32[]{:S(2)}) copy-start(bf16[16,64,2048]{2,1,0:T(8,128)(2,1)S(1)} %pack.1) | copy-start | bytes 12582916
  12.2 79.3 %all-to-all-start = ((bf16[16,64,2048]{2,1,0:T(8,128)(2,1)}), bf16[16,64,2048]{2,1,0:T(8,128)(2,1)}, u32[]{:S(2)}, u32[]{:S(2)}) async-start(bf16[16,64,2048]{2,1,0:T(8,128)(2,1)} %copy-done.1), calls=%async_computation | async-start | bytes 8388608 | tf_op jit(solution)/shard_map/all_to_all | solution.py:191
  19.4 52.8 %copy-start.5 = (bf16[64,8192]{1,0:T(8,128)(2,1)S(1)}, bf16[64,8192]{1,0:T(8,128)(2,1)}, u32[]{:S(2)}) copy-start(bf16[64,8192]{1,0:T(8,128)(2,1)} %quant_ref.1) | copy-start | bytes 3145732
  19.4 53.5 %slice-start = ((bf16[64,8192]{1,0:T(8,128)(2,1)}), bf16[64,128]{1,0:T(8,128)(2,1)S(1)}, s32[]{:S(2)}) async-start(bf16[64,8192]{1,0:T(8,128)(2,1)} %quant_ref.1), calls=%async_computation.2 | async-start | bytes 32768 | tf_op jit(solution)/shard_map/slice | solution.py:197
  21.6 27.3 %collective-permute-start.3 = (bf16[512,1024]{1,0:T(8,128)(2,1)S(1)}, bf16[512,1024]{1,0:T(8,128)(2,1)S(1)}, u32[]{:S(2)}, u32[]{:S(2)}) collective-permute-start(bf16[512,1024]{1,0:T(8,128)(2,1)S(1)} %pad_maximum_fusion.refs_0_), channel_id=1, source_target_pairs={{12,0},{0,4},{4,8},{8,12},{13,1},{1,5},{5,9},{9,13},{14,2},{2,6},{... | collective-permute-start | bytes 3145736 | tf_op jit(solution)/shard_map/ppermute | solution.py:159
  23.6 46.7 %collective-permute-start.1 = (bf16[512,1024]{1,0:T(8,128)(2,1)S(1)}, bf16[512,1024]{1,0:T(8,128)(2,1)}, u32[]{:S(2)}, u32[]{:S(2)}) collective-permute-start(bf16[512,1024]{1,0:T(8,128)(2,1)S(1)} %pad_maximum_fusion.refs_0_), channel_id=1, source_target_pairs={{4,0},{8,4},{12,8},{0,12},{5,1},{9,5},{13,9},{1,13},{6,2},{10,6},{... | collective-permute-start | bytes 3145736 | tf_op jit(solution)/shard_map/ppermute | solution.py:159
  25.8 46.4 %collective-permute-start.2 = (bf16[512,1024]{1,0:T(8,128)(2,1)S(1)}, bf16[512,1024]{1,0:T(8,128)(2,1)}, u32[]{:S(2)}, u32[]{:S(2)}) collective-permute-start(bf16[512,1024]{1,0:T(8,128)(2,1)S(1)} %pad_maximum_fusion.refs_0_), channel_id=1, source_target_pairs={{8,0},{12,4},{0,8},{4,12},{9,1},{13,5},{1,9},{5,13},{10,2},{14,6},... | collective-permute-start | bytes 3145736 | tf_op jit(solution)/shard_map/ppermute | solution.py:159
  27.6 65.8 %collective-permute-start.7 = (bf16[512,1024]{1,0:T(8,128)(2,1)S(1)}, bf16[512,1024]{1,0:T(8,128)(2,1)}, u32[]{:S(2)}, u32[]{:S(2)}) collective-permute-start(bf16[512,1024]{1,0:T(8,128)(2,1)S(1)} %pad_maximum_fusion.refs_0_), channel_id=1, source_target_pairs={{0,32},{32,0},{1,33},{33,1},{2,34},{34,2},{3,35},{35,3},{4,36},{36... | collective-permute-start | bytes 3145736 | tf_op jit(solution)/shard_map/ppermute | solution.py:155
  48.9 45.8 %collective-permute-start.10 = (bf16[512,1024]{1,0:T(8,128)(2,1)S(1)}, bf16[512,1024]{1,0:T(8,128)(2,1)}, u32[]{:S(2)}, u32[]{:S(2)}) collective-permute-start(bf16[512,1024]{1,0:T(8,128)(2,1)S(1)} %collective-permute-done.3.refs_3_), channel_id=1, source_target_pairs={{0,32},{32,0},{1,33},{33,1},{2,34},{34,2},{3,35},{35,3},{4,36},{36... | collective-permute-start | bytes 3145736 | tf_op jit(solution)/shard_map/ppermute | solution.py:155
  70.3 25.7 %collective-permute-start.8 = (bf16[512,1024]{1,0:T(8,128)(2,1)}, bf16[512,1024]{1,0:T(8,128)(2,1)}, u32[]{:S(2)}, u32[]{:S(2)}) collective-permute-start(bf16[512,1024]{1,0:T(8,128)(2,1)} %collective-permute-done.1.refs_1_), channel_id=1, source_target_pairs={{0,32},{32,0},{1,33},{33,1},{2,34},{34,2},{3,35},{35,3},{4,36},{36... | collective-permute-start | bytes 3145736 | tf_op jit(solution)/shard_map/ppermute | solution.py:155
  72.2 23.7 %collective-permute-start.9 = (bf16[512,1024]{1,0:T(8,128)(2,1)}, bf16[512,1024]{1,0:T(8,128)(2,1)}, u32[]{:S(2)}, u32[]{:S(2)}) collective-permute-start(bf16[512,1024]{1,0:T(8,128)(2,1)} %collective-permute-done.2.refs_2_), channel_id=1, source_target_pairs={{0,32},{32,0},{1,33},{33,1},{2,34},{34,2},{3,35},{35,3},{4,36},{36... | collective-permute-start | bytes 3145736 | tf_op jit(solution)/shard_map/ppermute | solution.py:155
  73.0 8.0 %collective-permute-start.4 = (bf16[64,256]{1,0:T(8,128)(2,1)S(1)}, bf16[64,256]{1,0:T(8,128)(2,1)S(1)}, u32[]{:S(2)}, u32[]{:S(2)}) collective-permute-start(bf16[64,256]{1,0:T(8,128)(2,1)S(1)} %pad_maximum_fusion.2), channel_id=1, source_target_pairs={{1,0},{2,1},{3,2},{0,3},{5,4},{6,5},{7,6},{4,7},{9,8},{10,9},{11,1... | collective-permute-start | bytes 98312 | tf_op jit(solution)/shard_map/ppermute | solution.py:159
  81.0 5.4 %collective-permute-start.5 = (bf16[64,256]{1,0:T(8,128)(2,1)S(1)}, bf16[64,256]{1,0:T(8,128)(2,1)S(1)}, u32[]{:S(2)}, u32[]{:S(2)}) collective-permute-start(bf16[64,256]{1,0:T(8,128)(2,1)S(1)} %pad_maximum_fusion.2), channel_id=1, source_target_pairs={{2,0},{3,1},{0,2},{1,3},{6,4},{7,5},{4,6},{5,7},{10,8},{11,9},{8,1... | collective-permute-start | bytes 98312 | tf_op jit(solution)/shard_map/ppermute | solution.py:159
  86.4 5.1 %collective-permute-start.6 = (bf16[64,256]{1,0:T(8,128)(2,1)S(1)}, bf16[64,256]{1,0:T(8,128)(2,1)S(1)}, u32[]{:S(2)}, u32[]{:S(2)}) collective-permute-start(bf16[64,256]{1,0:T(8,128)(2,1)S(1)} %pad_maximum_fusion.2), channel_id=1, source_target_pairs={{3,0},{0,1},{1,2},{2,3},{7,4},{4,5},{5,6},{6,7},{11,8},{8,9},{9,10... | collective-permute-start | bytes 98312 | tf_op jit(solution)/shard_map/ppermute | solution.py:159
  91.6 19.2 %collective-permute-start.11 = (bf16[256,256]{1,0:T(8,128)(2,1)S(1)}, bf16[256,256]{1,0:T(8,128)(2,1)S(1)}, u32[]{:S(2)}, u32[]{:S(2)}) collective-permute-start(bf16[256,256]{1,0:T(8,128)(2,1)S(1)} %pad_maximum_fusion.1.refs_0_), channel_id=1, source_target_pairs={{16,0},{64,16},{80,64},{0,80},{17,1},{65,17},{81,65},{1,81},{18,2}... | collective-permute-start | bytes 393224 | tf_op jit(solution)/shard_map/ppermute | solution.py:159
  93.3 17.4 %collective-permute-start.12 = (bf16[256,256]{1,0:T(8,128)(2,1)S(1)}, bf16[256,256]{1,0:T(8,128)(2,1)S(1)}, u32[]{:S(2)}, u32[]{:S(2)}) collective-permute-start(bf16[256,256]{1,0:T(8,128)(2,1)S(1)} %pad_maximum_fusion.1.refs_0_), channel_id=1, source_target_pairs={{64,0},{80,16},{0,64},{16,80},{65,1},{81,17},{1,65},{17,81},{66,2}... | collective-permute-start | bytes 393224 | tf_op jit(solution)/shard_map/ppermute | solution.py:159
  94.6 16.1 %collective-permute-start.13 = (bf16[256,256]{1,0:T(8,128)(2,1)S(1)}, bf16[256,256]{1,0:T(8,128)(2,1)S(1)}, u32[]{:S(2)}, u32[]{:S(2)}) collective-permute-start(bf16[256,256]{1,0:T(8,128)(2,1)S(1)} %pad_maximum_fusion.1.refs_0_), channel_id=1, source_target_pairs={{80,0},{0,16},{16,64},{64,80},{81,1},{1,17},{17,65},{65,81},{82,2}... | collective-permute-start | bytes 393224 | tf_op jit(solution)/shard_map/ppermute | solution.py:159
  108.8 2.0 %copy-start.2 = (bf16[1024,2048]{1,0:T(8,128)(2,1)}, bf16[1024,2048]{1,0:T(8,128)(2,1)S(1)}, u32[]{:S(2)}) copy-start(bf16[1024,2048]{1,0:T(8,128)(2,1)S(1)} %project.1.refs_4_) | copy-start | bytes 12582916
  110.8 58.9 %all-to-all-start.1 = ((bf16[16,64,2048]{2,1,0:T(8,128)(2,1)}), bf16[16,64,2048]{2,1,0:T(8,128)(2,1)}, u32[]{:S(2)}, u32[]{:S(2)}) async-start(bf16[16,64,2048]{2,1,0:T(8,128)(2,1)} %bitcast.19), calls=%async_computation.1 | async-start | bytes 8388608 | tf_op jit(solution)/shard_map/all_to_all | solution.py:207
  115.4 2.2 %copy-start.3 = (bf16[1024,2048]{1,0:T(8,128)(2,1)S(1)}, bf16[1024,2048]{1,0:T(8,128)(2,1)}, u32[]{:S(2)}) copy-start(bf16[1024,2048]{1,0:T(8,128)(2,1)} %copy-done.2) | copy-start | bytes 12582916
  120.6 7.4 %collective-permute-start.14 = (bf16[256,256]{1,0:T(8,128)(2,1)S(1)}, bf16[256,256]{1,0:T(8,128)(2,1)S(1)}, u32[]{:S(2)}, u32[]{:S(2)}) collective-permute-start(bf16[256,256]{1,0:T(8,128)(2,1)S(1)} %get-tuple-element.31), channel_id=1, source_target_pairs={{12,0},{0,4},{4,8},{8,12},{13,1},{1,5},{5,9},{9,13},{14,2},{2,6},{... | collective-permute-start | bytes 393224 | tf_op jit(solution)/shard_map/ppermute | solution.py:159
  122.6 8.3 %collective-permute-start.15 = (bf16[256,256]{1,0:T(8,128)(2,1)S(1)}, bf16[256,256]{1,0:T(8,128)(2,1)S(1)}, u32[]{:S(2)}, u32[]{:S(2)}) collective-permute-start(bf16[256,256]{1,0:T(8,128)(2,1)S(1)} %get-tuple-element.32), channel_id=1, source_target_pairs={{8,0},{12,4},{0,8},{4,12},{9,1},{13,5},{1,9},{5,13},{10,2},{14,6},... | collective-permute-start | bytes 393224 | tf_op jit(solution)/shard_map/ppermute | solution.py:159
  126.6 5.0 %collective-permute-start.16 = (bf16[256,256]{1,0:T(8,128)(2,1)S(1)}, bf16[256,256]{1,0:T(8,128)(2,1)S(1)}, u32[]{:S(2)}, u32[]{:S(2)}) collective-permute-start(bf16[256,256]{1,0:T(8,128)(2,1)S(1)} %get-tuple-element.33), channel_id=1, source_target_pairs={{4,0},{8,4},{12,8},{0,12},{5,1},{9,5},{13,9},{1,13},{6,2},{10,6},{... | collective-permute-start | bytes 393224 | tf_op jit(solution)/shard_map/ppermute | solution.py:159
  131.6 1.6 collective-permute-start.17
  133.3 29.9 %collective-permute-start.18 = (f32[256,256]{1,0:T(8,128)S(1)}, f32[256,256]{1,0:T(8,128)S(1)}, u32[]{:S(2)}, u32[]{:S(2)}) collective-permute-start(f32[256,256]{1,0:T(8,128)S(1)} %add_multiply_fusion.total_ref), channel_id=1, source_target_pairs={{0,64},{64,0},{1,65},{65,1},{2,66},{66,2},{3,67},{67,3},{4,68},{68... | collective-permute-start | bytes 786440 | tf_op jit(solution)/shard_map/ppermute | solution.py:155

commit v13 on v12

--- a/solution.py
+++ b/solution.py
@@ -22,41 +22,56 @@
     return pltpu.CompilerParams(vmem_limit_bytes=16 << 20)
 
 
-def pack_kernel(z_ref, float_ref, quant_ref, out_ref):
-    width = out_ref.shape[2] // 8
+def pack_kernel(z_ref, float_ref, quant_ref, after_ref, out_ref, sem):
+    width = float_ref.shape[1] // 32
     z = z_ref[0]
+    copies = []
     for kind, ref in enumerate((float_ref, quant_ref)):
         for j in range(4):
             zj = lax.rem(z + j, 4)
             for yl in range(2):
                 for x in range(4):
                     start = pl.multiple_of(((yl * 4 + zj) * 4 + x) * width, width)
-                    block = ref[:, pl.ds(start, width)]
                     for half in range(2):
                         at = (j * 2 + (yl ^ half)) * width
-                        out_ref[kind * 8 + half * 4 + x, :, at : at + width] = block
-
-
-def pack(z, attn_float, attn_quant):
+                        copies.append(
+                            pltpu.make_async_copy(
+                                ref.at[:, pl.ds(start, width)],
+                                out_ref.at[kind * 8 + half * 4 + x, :, pl.ds(at, width)],
+                                sem.at[len(copies)],
+                            )
+                        )
+    for copy in copies:
+        copy.start()
+    for copy in copies:
+        copy.wait()
+
+
+def pack(z, attn_float, attn_quant, after):
     tokens, d_in = attn_float.shape
     return pl.pallas_call(
         pack_kernel,
         out_shape=jax.ShapeDtypeStruct((16, tokens, d_in // 4), BF16),
-        in_specs=[SCALAR, WHOLE, WHOLE],
-        out_specs=WHOLE,
+        in_specs=[SCALAR, LEFT, LEFT, LEFT],
+        out_specs=LEFT,
+        scratch_shapes=[pltpu.SemaphoreType.DMA((128,))],
         compiler_params=params(),
         name="pack",
-    )(z.reshape(1), attn_float, attn_quant)
+    )(z.reshape(1), attn_float, attn_quant, after)
 
 
 def project_kernel(acts_ref, *refs):
-    *weights, out_ref = refs
+    weights, out_ref, buffer, sems = refs[:-3], refs[-3], refs[-2], refs[-1]
     depth, width = weights[0].shape
-    tile = 512
-    for q in range(2):
-        for col in range(0, width, tile):
-            for row in range(0, acts_ref.shape[0], 256):
-                rows, total = slice(row, row + 256), None
+    tile, step = 512, buffer.shape[1]
+    copies = []
+    for n in range(acts_ref.shape[0] // step):
+        if n >= 2:
+            copies[n - 2].wait()
+        rows = slice(n * step, (n + 1) * step)
+        for q in range(2):
+            for col in range(0, width, tile):
+                total = None
                 for j in range(4):
                     term = jnp.dot(
                         acts_ref[rows, j * depth : (j + 1) * depth],
@@ -65,7 +80,15 @@
                     )
                     total = term if total is None else total + term
                 at = q * width + col
-                out_ref[rows, at : at + tile] = total.astype(BF16)
+                buffer[n % 2, :, at : at + tile] = total.astype(BF16)
+        copies.append(
+            pltpu.make_async_copy(
+                buffer.at[n % 2], out_ref.at[pl.ds(n * step, step)], sems.at[n % 2]
+            )
+        )
+        copies[n].start()
+    for copy in copies[-2:]:
+        copy.wait()
 
 
 def project(acts, weights):
@@ -75,7 +98,11 @@
         project_kernel,
         out_shape=jax.ShapeDtypeStruct((rows, cols), BF16),
         in_specs=[WHOLE] * (1 + len(weights)),
-        out_specs=WHOLE,
+        out_specs=LEFT,
+        scratch_shapes=[
+            pltpu.VMEM((2, 256, cols), BF16),
+            pltpu.SemaphoreType.DMA((2,)),
+        ],
         compiler_params=params(),
         cost_estimate=pl.CostEstimate(
             flops=2 * rows * depth * cols, bytes_accessed=16 << 20, transcendentals=0
@@ -175,7 +202,16 @@
         quant = (values * scales[:, None, :]).reshape(features, quarter).astype(BF16)
         return jnp.where(kind == 0, plain, quant)
 
-    send = weight(yh ^ core, (1 - yl) * half + core * quarter)
+    quant = attn_quant[:, :BLOCK]
+    shift = (attn_float[:, :BLOCK].astype(F32) - quant.astype(F32)).astype(BF16)
+    block = jnp.concatenate([quant, shift], axis=1)
+    col = (1 - yl) * half + core * quarter
+    block, col = lax.optimization_barrier((block, col))
+    line = jnp.concatenate([block] + [ahead(block, "x", j) for j in (1, 2, 3)], axis=0)
+
+    send = weight(yh ^ core, col)
+    line, send = lax.optimization_barrier((line, send))
+    pieces = [line] + [ahead(line, ("yh", "yl"), j) for j in (1, 2, 3)]
     pairs = []
     for a in range(2):
         for c in range(2):
@@ -185,8 +221,8 @@
     col, send = lax.optimization_barrier((yl * half + core * quarter, send))
     own = weight(yh, col)
 
-    payload = pack(z, attn_float, attn_quant)
-    payload, got = lax.optimization_barrier((payload, got))
+    payload = pack(z, attn_float, attn_quant, send)
+    payload, got, *pieces = lax.optimization_barrier((payload, got, *pieces))
 
     acts = lax.all_to_all(payload, PLANE, 0, 0, tiled=True).reshape(16 * tokens, 8 * features)
 
@@ -194,16 +230,7 @@
     parts = [rows] + [ahead(rows, "z", j) for j in (1, 2, 3)]
     weights = parts + [swap(p, "core") for p in parts]
 
-    quant = attn_quant[:, :BLOCK]
-    shift = (attn_float[:, :BLOCK].astype(F32) - quant.astype(F32)).astype(BF16)
-    block = jnp.concatenate([quant, shift], axis=1)
-    block, *parts = lax.optimization_barrier((block, *parts))
-    line = jnp.concatenate([block] + [ahead(block, "x", j) for j in (1, 2, 3)], axis=0)
-    line, acts = lax.optimization_barrier((line, acts))
-    pieces = [line] + [ahead(line, ("yh", "yl"), j) for j in (1, 2, 3)]
-
     partial = project(acts, weights)
-    partial, *pieces = lax.optimization_barrier((partial, *pieces))
     result = lax.all_to_all(partial.reshape(16, tokens, half), PLANE, 0, 0, tiled=True)
 
     blocks = stats(jnp.stack([yh * 2 + yl, lax.axis_index("x")]), acts, pieces, partial)

time: 174 us -> 186 us (1.069)
  local copies, waits for them, and re-layouts: 9.47 us -> 22.8 us
  waiting for transfers between devices: 102 us -> 95.2 us
  starting transfers between devices: 37.1 us -> 40.3 us
    ppermute x12, waiting for transfers between devices: 64.3 us -> 48.8 us  [ahead(): return lax.ppermute(a, axis, [((i + j) % 4, i) for i in range(4)])]
    unnamed x14 -> x36, local copies, waits for them, and re-layouts: 9.39 us -> 21.9 us
    all_to_all x1, waiting for transfers between devices: 6.47 us -> 13.7 us  [shards(): lax.all_to_all(partial.reshape(16, tokens, half), PLANE, 0, 0, tiled=True)]
    ppermute x12, starting transfers between devices: 20.2 us -> 24.4 us  [ahead(): return lax.ppermute(a, axis, [((i + j) % 4, i) for i in range(4)])]
    ppermute x1, waiting for transfers between devices: 2.76 us -> 0.01 us  [shards(): got = lax.ppermute(send, ('yh', 'core', 'yl'), pairs)]
    ppermute x6, waiting for transfers between devices: 28 us -> 30.4 us  [swap(): return lax.ppermute(a, axis, [(0, 1), (1, 0)])]
    all_to_all x1, waiting for transfers between devices: 0.01 us -> 2.29 us  [shards(): lax.all_to_all(payload, PLANE, 0, 0, tiled=True)]
    pallas_call x1, Pallas kernels: 0.29 us -> 2.26 us  [pack(): pl.pallas_call(pack_kernel, out_shape=jax.ShapeDtypeStruct((16, tokens, d...]
  transfers between devices with their start and end apart: 21 -> 21, of which waited for: 13 -> 11; matrix products, arithmetic and copies ran while one was open for 2% -> 2% of each run, Pallas kernels for 9% -> 3%
where the time goes in v13:
time: 186 us; the launch traced here: 185 us
  waiting for transfers between devices  95.2 us (51%)
  starting transfers between devices  40.3 us (22%)
  local copies, waits for them, and re-layouts  22.8 us (12%)
  Pallas kernels  20.8 us (11%)
  other arithmetic  4.95 us (3%)
    ppermute x12, waiting for transfers between devices, ahead(): return lax.ppermute(a, axis, [((i + j) % 4, i) for i in range(4)])  48.8 us
    ppermute x6, waiting for transfers between devices, swap(): return lax.ppermute(a, axis, [(0, 1), (1, 0)])  30.4 us
    ppermute x12, starting transfers between devices, ahead(): return lax.ppermute(a, axis, [((i + j) % 4, i) for i in range(4)])  24.4 us
    unnamed x36, local copies, waits for them, and re-layouts  21.9 us
    all_to_all x1, waiting for transfers between devices, shards(): lax.all_to_all(partial.reshape(16, tokens, half), PLANE, 0, 0, tiled=True)  13.7 us
    pallas_call x1, Pallas kernels, project(): pl.pallas_call(project_kernel, out_shape=jax.ShapeDtypeStruct((rows, cols...  11.8 us
    all_to_all x1, starting transfers between devices, shards(): lax.all_to_all(payload, PLANE, 0, 0, tiled=True)  5.64 us
    all_to_all x1, starting transfers between devices, shards(): lax.all_to_all(partial.reshape(16, tokens, half), PLANE, 0, 0, tiled=True)  4.64 us
  transfers between devices with their start and end apart: 21, of which 11 were waited for; matrix products, arithmetic and copies ran while one was open for 2% of the time, Pallas kernels for 3%

profile of v13, /device:TPU:0, one launch (start us, length us, event | category | flops | bytes accessed | tf_op | source)
XLA Modules:
  0.0 184.9 jit_solution(5455153322468096635)
XLA Ops:
  2.1 1.6 collective-permute-start.2
  3.8 2.7 %collective-permute-start.1 = (bf16[64,256]{1,0:T(8,128)(2,1)S(1)}, bf16[64,256]{1,0:T(8,128)(2,1)S(1)}, u32[]{:S(2)}, u32[]{:S(2)}) collective-permute-start(bf16[64,256]{1,0:T(8,128)(2,1)S(1)} %pad_maximum_fusion.2), channel_id=1, source_target_pairs={{2,0},{3,1},{0,2},{1,3},{6,4},{7,5},{4,6},{5,7},{10,8},{11,9},{8,1... | collective-permute-start | bytes 98312 | tf_op jit(solution)/shard_map/ppermute | solution.py:186
  6.5 1.4 collective-permute-start
  8.0 1.9 %fusion.2.after_ref = bf16[256,1024]{1,0:T(8,128)(2,1)S(1)} fusion(s32[256,4096]{1,0:T(8,128)} %param.8, s32[]{:T(128)S(6)} %select_n.25, f32[2,1024]{1,0:T(2,128)S(1)} %constant_dynamic-slice_fusion.1, bf16[256,4096]{1,0:T(8,128)(2,1)} %param.7, pred[]{:T(512)S(6)} %eq.6), kind=kLoop, calls=%fused_computation.5 | loop fusion | flops 1310720 | bytes 2105349 | tf_op jit(solution)/shard_map/jit(_where)/select_n | solution.py:203
  10.4 1.7 collective-permute-start.3
  12.5 3.2 %collective-permute-start.5 = (bf16[256,256]{1,0:T(8,128)(2,1)S(1)}, bf16[256,256]{1,0:T(8,128)(2,1)S(1)}, u32[]{:S(2)}, u32[]{:S(2)}) collective-permute-start(bf16[256,256]{1,0:T(8,128)(2,1)S(1)} %pad_maximum_fusion.1.refs_0_), channel_id=1, source_target_pairs={{64,0},{80,16},{0,64},{16,80},{65,1},{81,17},{1,65},{17,81},{66,2}... | collective-permute-start | bytes 393224 | tf_op jit(solution)/shard_map/ppermute | solution.py:186
  15.7 1.9 %collective-permute-start.4 = (bf16[256,256]{1,0:T(8,128)(2,1)S(1)}, bf16[256,256]{1,0:T(8,128)(2,1)S(1)}, u32[]{:S(2)}, u32[]{:S(2)}) collective-permute-start(bf16[256,256]{1,0:T(8,128)(2,1)S(1)} %pad_maximum_fusion.1.refs_0_), channel_id=1, source_target_pairs={{16,0},{64,16},{80,64},{0,80},{17,1},{65,17},{81,65},{1,81},{18,2}... | collective-permute-start | bytes 393224 | tf_op jit(solution)/shard_map/ppermute | solution.py:186
  20.1 2.3 %pack.1 = bf16[16,64,2048]{2,1,0:T(8,128)(2,1)S(1)} custom-call(s32[1]{0:T(128)} %bitcast.2.z_ref, bf16[64,8192]{1,0:T(8,128)(2,1)S(1)} %copy-done.5, bf16[64,8192]{1,0:T(8,128)(2,1)S(1)} %copy-done.4, bf16[256,1024]{1,0:T(8,128)(2,1)S(1)} %fusion.2.after_ref), custom_call_target="tpu_custom_call" | custom-call | tf_op jit(solution)/shard_map/pack/pallas_call | solution.py:52
  22.4 2.0 %copy-done.3 = bf16[16,64,2048]{2,1,0:T(8,128)(2,1)} copy-done((bf16[16,64,2048]{2,1,0:T(8,128)(2,1)}, bf16[16,64,2048]{2,1,0:T(8,128)(2,1)S(1)}, u32[]{:S(2)}) %copy-start.3) | copy-done | bytes 4194328
  24.4 1.4 collective-permute-done.5.refs_2_
  25.8 5.6 %all-to-all-start = ((bf16[16,64,2048]{2,1,0:T(8,128)(2,1)}), bf16[16,64,2048]{2,1,0:T(8,128)(2,1)}, u32[]{:S(2)}, u32[]{:S(2)}) async-start(bf16[16,64,2048]{2,1,0:T(8,128)(2,1)} %copy-done.3), calls=%async_computation | async-start | bytes 8388608 | tf_op jit(solution)/shard_map/all_to_all | solution.py:227
  31.5 1.9 %fusion.3 = bf16[256,1024]{1,0:T(8,128)(2,1)S(1)} fusion(s32[256,4096]{1,0:T(8,128)} %param.8, s32[]{:T(128)S(6)} %select_n.28, f32[2,1024]{1,0:T(2,128)S(1)} %constant_dynamic-slice_fusion, bf16[256,4096]{1,0:T(8,128)(2,1)} %param.7, pred[]{:T(512)S(6)} %eq.7), kind=kLoop, calls=%fused_computation.6 | loop fusion | flops 1310720 | bytes 2105349 | tf_op jit(solution)/shard_map/jit(_where)/select_n | solution.py:203
  33.5 2.0 %collective-permute-start.9 = (bf16[512,1024]{1,0:T(8,128)(2,1)S(1)}, bf16[512,1024]{1,0:T(8,128)(2,1)S(1)}, u32[]{:S(2)}, u32[]{:S(2)}) collective-permute-start(bf16[512,1024]{1,0:T(8,128)(2,1)S(1)} %pad_maximum_fusion.refs_0_), channel_id=1, source_target_pairs={{12,0},{0,4},{4,8},{8,12},{13,1},{1,5},{5,9},{9,13},{14,2},{2,6},{... | collective-permute-start | bytes 3145736 | tf_op jit(solution)/shard_map/ppermute | solution.py:186
  35.5 3.6 %collective-permute-start.8 = (bf16[512,1024]{1,0:T(8,128)(2,1)S(1)}, bf16[512,1024]{1,0:T(8,128)(2,1)S(1)}, u32[]{:S(2)}, u32[]{:S(2)}) collective-permute-start(bf16[512,1024]{1,0:T(8,128)(2,1)S(1)} %pad_maximum_fusion.refs_0_), channel_id=1, source_target_pairs={{8,0},{12,4},{0,8},{4,12},{9,1},{13,5},{1,9},{5,13},{10,2},{14,6},... | collective-permute-start | bytes 3145736 | tf_op jit(solution)/shard_map/ppermute | solution.py:186
  40.1 20.7 %collective-permute-done.9.refs_3_ = bf16[512,1024]{1,0:T(8,128)(2,1)S(1)} collective-permute-done((bf16[512,1024]{1,0:T(8,128)(2,1)S(1)}, bf16[512,1024]{1,0:T(8,128)(2,1)S(1)}, u32[]{:S(2)}, u32[]{:S(2)}) %collective-permute-start.9) | collective-permute-done | bytes 1048608 | tf_op jit(solution)/shard_map/ppermute | solution.py:186
  60.8 22.4 %collective-permute-done.8.refs_2_ = bf16[512,1024]{1,0:T(8,128)(2,1)S(1)} collective-permute-done((bf16[512,1024]{1,0:T(8,128)(2,1)S(1)}, bf16[512,1024]{1,0:T(8,128)(2,1)S(1)}, u32[]{:S(2)}, u32[]{:S(2)}) %collective-permute-start.8) | collective-permute-done | bytes 1048608 | tf_op jit(solution)/shard_map/ppermute | solution.py:186
  89.6 2.3 %all-to-all-done = bf16[16,64,2048]{2,1,0:T(8,128)(2,1)} async-done(((bf16[16,64,2048]{2,1,0:T(8,128)(2,1)}), bf16[16,64,2048]{2,1,0:T(8,128)(2,1)}, u32[]{:S(2)}, u32[]{:S(2)}) %all-to-all-start) | async-done | bytes 4194336 | tf_op jit(solution)/shard_map/all_to_all | solution.py:227
  91.9 1.2 copy-done.7
  99.2 11.8 %project.1.refs_4_ = bf16[1024,2048]{1,0:T(8,128)(2,1)S(1)} custom-call(bf16[1024,2048]{1,0:T(8,128)(2,1)} %bitcast.4.acts_ref, bf16[512,1024]{1,0:T(8,128)(2,1)S(1)} %pad_maximum_fusion.refs_0_, bf16[512,1024]{1,0:T(8,128)(2,1)S(1)} %copy-done.9, bf16[512,1024]{1,0:T(8,128)(2,1)S(1)} %copy-done.7, bf16[512,1024]{1,0:T(8,128)(2,1)S(1)} %collective-permute-done.9.refs_3_, ...), custom_call_target="tpu_custom_call" | custom-call | flops 8589934592 | bytes 16777216 | tf_op jit(solution)/shard_map/project/pallas_call | solution.py:97
  111.1 2.0 %copy-done.1 = bf16[1024,2048]{1,0:T(8,128)(2,1)} copy-done((bf16[1024,2048]{1,0:T(8,128)(2,1)}, bf16[1024,2048]{1,0:T(8,128)(2,1)S(1)}, u32[]{:S(2)}) %copy-start.1) | copy-done | bytes 4194328
  113.1 4.6 %all-to-all-start.1 = ((bf16[16,64,2048]{2,1,0:T(8,128)(2,1)}), bf16[16,64,2048]{2,1,0:T(8,128)(2,1)}, u32[]{:S(2)}, u32[]{:S(2)}) async-start(bf16[16,64,2048]{2,1,0:T(8,128)(2,1)} %bitcast.19), calls=%async_computation.1 | async-start | bytes 8388608 | tf_op jit(solution)/shard_map/all_to_all | solution.py:234
  117.8 2.2 %copy-done.2 = bf16[1024,2048]{1,0:T(8,128)(2,1)S(1)} copy-done((bf16[1024,2048]{1,0:T(8,128)(2,1)S(1)}, bf16[1024,2048]{1,0:T(8,128)(2,1)}, u32[]{:S(2)}) %copy-start.2) | copy-done | bytes 4194328
  120.0 3.0 %stats.1 = (f32[256,256]{1,0:T(8,128)S(1)}, bf16[256,256]{1,0:T(8,128)(2,1)S(1)}, bf16[256,256]{1,0:T(8,128)(2,1)S(1)}, bf16[256,256]{1,0:T(8,128)(2,1)S(1)}) custom-call(s32[2]{0:T(128)S(1)} %pad_add_fusion.1.at_ref, bf16[1024,2048]{1,0:T(8,128)(2,1)} %bitcast.4.acts_ref, bf16[256,256]{1,0:T(8,128)(2,1)S(1)} %pad_maximum_fusion.1.refs_0_, ...), custom_call_target="tpu_custom_call" | custom-call | tf_op jit(solution)/shard_map/stats/pallas_call | solution.py:169
  123.0 1.9 %collective-permute-start.14 = (bf16[256,256]{1,0:T(8,128)(2,1)S(1)}, bf16[256,256]{1,0:T(8,128)(2,1)S(1)}, u32[]{:S(2)}, u32[]{:S(2)}) collective-permute-start(bf16[256,256]{1,0:T(8,128)(2,1)S(1)} %get-tuple-element.33), channel_id=1, source_target_pairs={{12,0},{0,4},{4,8},{8,12},{13,1},{1,5},{5,9},{9,13},{14,2},{2,6},{... | collective-permute-start | bytes 393224 | tf_op jit(solution)/shard_map/ppermute | solution.py:186
  124.9 3.6 %collective-permute-start.15 = (bf16[256,256]{1,0:T(8,128)(2,1)S(1)}, bf16[256,256]{1,0:T(8,128)(2,1)S(1)}, u32[]{:S(2)}, u32[]{:S(2)}) collective-permute-start(bf16[256,256]{1,0:T(8,128)(2,1)S(1)} %get-tuple-element.34), channel_id=1, source_target_pairs={{8,0},{12,4},{0,8},{4,12},{9,1},{13,5},{1,9},{5,13},{10,2},{14,6},... | collective-permute-start | bytes 393224 | tf_op jit(solution)/shard_map/ppermute | solution.py:186
  129.5 1.5 collective-permute-done.14
  131.0 1.9 %collective-permute-done.15 = bf16[256,256]{1,0:T(8,128)(2,1)S(1)} collective-permute-done((bf16[256,256]{1,0:T(8,128)(2,1)S(1)}, bf16[256,256]{1,0:T(8,128)(2,1)S(1)}, u32[]{:S(2)}, u32[]{:S(2)}) %collective-permute-start.15) | collective-permute-done | bytes 131104 | tf_op jit(solution)/shard_map/ppermute | solution.py:186
  133.6 1.5 collective-permute-done.17
  135.2 3.4 %collective-permute-start.18 = (f32[256,256]{1,0:T(8,128)S(1)}, f32[256,256]{1,0:T(8,128)S(1)}, u32[]{:S(2)}, u32[]{:S(2)}) collective-permute-start(f32[256,256]{1,0:T(8,128)S(1)} %add_multiply_fusion.total_ref), channel_id=1, source_target_pairs={{0,64},{64,0},{1,65},{65,1},{2,66},{66,2},{3,67},{67,3},{4,68},{68... | collective-permute-start | bytes 786440 | tf_op jit(solution)/shard_map/ppermute | solution.py:182
  138.6 28.8 %collective-permute-done.18.moved_ref = f32[256,256]{1,0:T(8,128)S(1)} collective-permute-done((f32[256,256]{1,0:T(8,128)S(1)}, f32[256,256]{1,0:T(8,128)S(1)}, u32[]{:S(2)}, u32[]{:S(2)}) %collective-permute-start.18) | collective-permute-done | bytes 262176 | tf_op jit(solution)/shard_map/ppermute | solution.py:182
  167.4 13.7 %all-to-all-done.1.parts_ref = bf16[16,64,2048]{2,1,0:T(8,128)(2,1)} async-done(((bf16[16,64,2048]{2,1,0:T(8,128)(2,1)}), bf16[16,64,2048]{2,1,0:T(8,128)(2,1)}, u32[]{:S(2)}, u32[]{:S(2)}) %all-to-all-start.1) | async-done | bytes 4194336 | tf_op jit(solution)/shard_map/all_to_all | solution.py:234
  181.2 3.7 %finish.1 = (bf16[64,4096]{1,0:T(8,128)(2,1)}, bf16[64,4096]{1,0:T(8,128)(2,1)}, f32[256,128]{1,0:T(8,128)}, f32[256,128]{1,0:T(8,128)}) custom-call(s32[2]{0:T(128)S(1)} %pad_add_fusion.at_ref, bf16[16,64,2048]{2,1,0:T(8,128)(2,1)} %all-to-all-done.1.parts_ref, f32[256,256]{1,0:T(8,128)S(1)} %add_multiply_fusion.total_ref, ...), custom_call_target="tpu_custom_call" | custom-call | tf_op jit(solution)/shard_map/finish/pallas_call | solution.py:136
  (63 shorter events, 20.6 us)
Async XLA Ops:
  0.6 7.3 %copy-start = (f32[2,4096]{1,0:T(2,128)S(1)}, f32[2,4096]{1,0:T(2,128)}, u32[]{:S(2)}) copy-start(f32[2,4096]{1,0:T(2,128)} %param.9) | copy-start | bytes 98308
  2.1 7.8 %collective-permute-start.2 = (bf16[64,256]{1,0:T(8,128)(2,1)S(1)}, bf16[64,256]{1,0:T(8,128)(2,1)S(1)}, u32[]{:S(2)}, u32[]{:S(2)}) collective-permute-start(bf16[64,256]{1,0:T(8,128)(2,1)S(1)} %pad_maximum_fusion.2), channel_id=1, source_target_pairs={{3,0},{0,1},{1,2},{2,3},{7,4},{4,5},{5,6},{6,7},{11,8},{8,9},{9,10... | collective-permute-start | bytes 98312 | tf_op jit(solution)/shard_map/ppermute | solution.py:186
  3.8 6.2 %collective-permute-start.1 = (bf16[64,256]{1,0:T(8,128)(2,1)S(1)}, bf16[64,256]{1,0:T(8,128)(2,1)S(1)}, u32[]{:S(2)}, u32[]{:S(2)}) collective-permute-start(bf16[64,256]{1,0:T(8,128)(2,1)S(1)} %pad_maximum_fusion.2), channel_id=1, source_target_pairs={{2,0},{3,1},{0,2},{1,3},{6,4},{7,5},{4,6},{5,7},{10,8},{11,9},{8,1... | collective-permute-start | bytes 98312 | tf_op jit(solution)/shard_map/ppermute | solution.py:186
  6.5 3.9 %collective-permute-start = (bf16[64,256]{1,0:T(8,128)(2,1)S(1)}, bf16[64,256]{1,0:T(8,128)(2,1)S(1)}, u32[]{:S(2)}, u32[]{:S(2)}) collective-permute-start(bf16[64,256]{1,0:T(8,128)(2,1)S(1)} %pad_maximum_fusion.2), channel_id=1, source_target_pairs={{1,0},{2,1},{3,2},{0,3},{5,4},{6,5},{7,6},{4,7},{9,8},{10,9},{11,1... | collective-permute-start | bytes 98312 | tf_op jit(solution)/shard_map/ppermute | solution.py:186
  10.4 15.3 %collective-permute-start.3 = (bf16[256,1024]{1,0:T(8,128)(2,1)S(1)}, bf16[256,1024]{1,0:T(8,128)(2,1)S(1)}, u32[]{:S(2)}, u32[]{:S(2)}) collective-permute-start(bf16[256,1024]{1,0:T(8,128)(2,1)S(1)} %fusion.2.after_ref), channel_id=1, source_target_pairs={{0,16},{16,0},{32,112},{48,96},{64,80},{80,64},{96,48},{112,32},{1... | collective-permute-start | bytes 1572872 | tf_op jit(solution)/shard_map/ppermute | solution.py:220
  12.1 12.3 %collective-permute-start.6 = (bf16[256,256]{1,0:T(8,128)(2,1)S(1)}, bf16[256,256]{1,0:T(8,128)(2,1)S(1)}, u32[]{:S(2)}, u32[]{:S(2)}) collective-permute-start(bf16[256,256]{1,0:T(8,128)(2,1)S(1)} %pad_maximum_fusion.1.refs_0_), channel_id=1, source_target_pairs={{80,0},{0,16},{16,64},{64,80},{81,1},{1,17},{17,65},{65,81},{82,2}... | collective-permute-start | bytes 393224 | tf_op jit(solution)/shard_map/ppermute | solution.py:186
  12.5 13.2 %collective-permute-start.5 = (bf16[256,256]{1,0:T(8,128)(2,1)S(1)}, bf16[256,256]{1,0:T(8,128)(2,1)S(1)}, u32[]{:S(2)}, u32[]{:S(2)}) collective-permute-start(bf16[256,256]{1,0:T(8,128)(2,1)S(1)} %pad_maximum_fusion.1.refs_0_), channel_id=1, source_target_pairs={{64,0},{80,16},{0,64},{16,80},{65,1},{81,17},{1,65},{17,81},{66,2}... | collective-permute-start | bytes 393224 | tf_op jit(solution)/shard_map/ppermute | solution.py:186
  15.7 10.0 %collective-permute-start.4 = (bf16[256,256]{1,0:T(8,128)(2,1)S(1)}, bf16[256,256]{1,0:T(8,128)(2,1)S(1)}, u32[]{:S(2)}, u32[]{:S(2)}) collective-permute-start(bf16[256,256]{1,0:T(8,128)(2,1)S(1)} %pad_maximum_fusion.1.refs_0_), channel_id=1, source_target_pairs={{16,0},{64,16},{80,64},{0,80},{17,1},{65,17},{81,65},{1,81},{18,2}... | collective-permute-start | bytes 393224 | tf_op jit(solution)/shard_map/ppermute | solution.py:186
  17.6 1.2 copy-start.4
  18.8 1.2 copy-start.5
  22.3 2.0 %copy-start.3 = (bf16[16,64,2048]{2,1,0:T(8,128)(2,1)}, bf16[16,64,2048]{2,1,0:T(8,128)(2,1)S(1)}, u32[]{:S(2)}) copy-start(bf16[16,64,2048]{2,1,0:T(8,128)(2,1)S(1)} %pack.1) | copy-start | bytes 12582916
  25.8 66.1 %all-to-all-start = ((bf16[16,64,2048]{2,1,0:T(8,128)(2,1)}), bf16[16,64,2048]{2,1,0:T(8,128)(2,1)}, u32[]{:S(2)}, u32[]{:S(2)}) async-start(bf16[16,64,2048]{2,1,0:T(8,128)(2,1)} %copy-done.3), calls=%async_computation | async-start | bytes 8388608 | tf_op jit(solution)/shard_map/all_to_all | solution.py:227
  33.5 27.3 %collective-permute-start.9 = (bf16[512,1024]{1,0:T(8,128)(2,1)S(1)}, bf16[512,1024]{1,0:T(8,128)(2,1)S(1)}, u32[]{:S(2)}, u32[]{:S(2)}) collective-permute-start(bf16[512,1024]{1,0:T(8,128)(2,1)S(1)} %pad_maximum_fusion.refs_0_), channel_id=1, source_target_pairs={{12,0},{0,4},{4,8},{8,12},{13,1},{1,5},{5,9},{9,13},{14,2},{2,6},{... | collective-permute-start | bytes 3145736 | tf_op jit(solution)/shard_map/ppermute | solution.py:186
  35.5 47.7 %collective-permute-start.8 = (bf16[512,1024]{1,0:T(8,128)(2,1)S(1)}, bf16[512,1024]{1,0:T(8,128)(2,1)S(1)}, u32[]{:S(2)}, u32[]{:S(2)}) collective-permute-start(bf16[512,1024]{1,0:T(8,128)(2,1)S(1)} %pad_maximum_fusion.refs_0_), channel_id=1, source_target_pairs={{8,0},{12,4},{0,8},{4,12},{9,1},{13,5},{1,9},{5,13},{10,2},{14,6},... | collective-permute-start | bytes 3145736 | tf_op jit(solution)/shard_map/ppermute | solution.py:186
  39.1 45.1 %collective-permute-start.7 = (bf16[512,1024]{1,0:T(8,128)(2,1)S(1)}, bf16[512,1024]{1,0:T(8,128)(2,1)S(1)}, u32[]{:S(2)}, u32[]{:S(2)}) collective-permute-start(bf16[512,1024]{1,0:T(8,128)(2,1)S(1)} %pad_maximum_fusion.refs_0_), channel_id=1, source_target_pairs={{4,0},{8,4},{12,8},{0,12},{5,1},{9,5},{13,9},{1,13},{6,2},{10,6},{... | collective-permute-start | bytes 3145736 | tf_op jit(solution)/shard_map/ppermute | solution.py:186
  40.1 45.6 %collective-permute-start.10 = (bf16[512,1024]{1,0:T(8,128)(2,1)S(1)}, bf16[512,1024]{1,0:T(8,128)(2,1)S(1)}, u32[]{:S(2)}, u32[]{:S(2)}) collective-permute-start(bf16[512,1024]{1,0:T(8,128)(2,1)S(1)} %pad_maximum_fusion.refs_0_), channel_id=1, source_target_pairs={{0,32},{32,0},{1,33},{33,1},{2,34},{34,2},{3,35},{35,3},{4,36},{36... | collective-permute-start | bytes 3145736 | tf_op jit(solution)/shard_map/ppermute | solution.py:182
  60.8 25.8 %collective-permute-start.13 = (bf16[512,1024]{1,0:T(8,128)(2,1)S(1)}, bf16[512,1024]{1,0:T(8,128)(2,1)S(1)}, u32[]{:S(2)}, u32[]{:S(2)}) collective-permute-start(bf16[512,1024]{1,0:T(8,128)(2,1)S(1)} %collective-permute-done.9.refs_3_), channel_id=1, source_target_pairs={{0,32},{32,0},{1,33},{33,1},{2,34},{34,2},{3,35},{35,3},{4,36},{36... | collective-permute-start | bytes 3145736 | tf_op jit(solution)/shard_map/ppermute | solution.py:182
  83.2 4.4 %collective-permute-start.12 = (bf16[512,1024]{1,0:T(8,128)(2,1)S(1)}, bf16[512,1024]{1,0:T(8,128)(2,1)S(1)}, u32[]{:S(2)}, u32[]{:S(2)}) collective-permute-start(bf16[512,1024]{1,0:T(8,128)(2,1)S(1)} %collective-permute-done.8.refs_2_), channel_id=1, source_target_pairs={{0,32},{32,0},{1,33},{33,1},{2,34},{34,2},{3,35},{35,3},{4,36},{36... | collective-permute-start | bytes 3145736 | tf_op jit(solution)/shard_map/ppermute | solution.py:182
  84.2 4.4 %collective-permute-start.11 = (bf16[512,1024]{1,0:T(8,128)(2,1)S(1)}, bf16[512,1024]{1,0:T(8,128)(2,1)S(1)}, u32[]{:S(2)}, u32[]{:S(2)}) collective-permute-start(bf16[512,1024]{1,0:T(8,128)(2,1)S(1)} %collective-permute-done.7.refs_1_), channel_id=1, source_target_pairs={{0,32},{32,0},{1,33},{33,1},{2,34},{34,2},{3,35},{35,3},{4,36},{36... | collective-permute-start | bytes 3145736 | tf_op jit(solution)/shard_map/ppermute | solution.py:182
  91.9 1.2 copy-start.7
  94.3 1.2 copy-start.11
  95.6 1.2 copy-start.13
  96.8 1.2 copy-start.15
  98.0 1.2 copy-start.17
  111.1 2.0 %copy-start.1 = (bf16[1024,2048]{1,0:T(8,128)(2,1)}, bf16[1024,2048]{1,0:T(8,128)(2,1)S(1)}, u32[]{:S(2)}) copy-start(bf16[1024,2048]{1,0:T(8,128)(2,1)S(1)} %project.1.refs_4_) | copy-start | bytes 12582916
  113.1 68.1 %all-to-all-start.1 = ((bf16[16,64,2048]{2,1,0:T(8,128)(2,1)}), bf16[16,64,2048]{2,1,0:T(8,128)(2,1)}, u32[]{:S(2)}, u32[]{:S(2)}) async-start(bf16[16,64,2048]{2,1,0:T(8,128)(2,1)} %bitcast.19), calls=%async_computation.1 | async-start | bytes 8388608 | tf_op jit(solution)/shard_map/all_to_all | solution.py:234
  117.8 2.2 %copy-start.2 = (bf16[1024,2048]{1,0:T(8,128)(2,1)S(1)}, bf16[1024,2048]{1,0:T(8,128)(2,1)}, u32[]{:S(2)}) copy-start(bf16[1024,2048]{1,0:T(8,128)(2,1)} %copy-done.1) | copy-start | bytes 12582916
  123.0 8.0 %collective-permute-start.14 = (bf16[256,256]{1,0:T(8,128)(2,1)S(1)}, bf16[256,256]{1,0:T(8,128)(2,1)S(1)}, u32[]{:S(2)}, u32[]{:S(2)}) collective-permute-start(bf16[256,256]{1,0:T(8,128)(2,1)S(1)} %get-tuple-element.33), channel_id=1, source_target_pairs={{12,0},{0,4},{4,8},{8,12},{13,1},{1,5},{5,9},{9,13},{14,2},{2,6},{... | collective-permute-start | bytes 393224 | tf_op jit(solution)/shard_map/ppermute | solution.py:186
  124.9 7.9 %collective-permute-start.15 = (bf16[256,256]{1,0:T(8,128)(2,1)S(1)}, bf16[256,256]{1,0:T(8,128)(2,1)S(1)}, u32[]{:S(2)}, u32[]{:S(2)}) collective-permute-start(bf16[256,256]{1,0:T(8,128)(2,1)S(1)} %get-tuple-element.34), channel_id=1, source_target_pairs={{8,0},{12,4},{0,8},{4,12},{9,1},{13,5},{1,9},{5,13},{10,2},{14,6},... | collective-permute-start | bytes 393224 | tf_op jit(solution)/shard_map/ppermute | solution.py:186
  128.5 5.0 %collective-permute-start.16 = (bf16[256,256]{1,0:T(8,128)(2,1)S(1)}, bf16[256,256]{1,0:T(8,128)(2,1)S(1)}, u32[]{:S(2)}, u32[]{:S(2)}) collective-permute-start(bf16[256,256]{1,0:T(8,128)(2,1)S(1)} %get-tuple-element.35), channel_id=1, source_target_pairs={{4,0},{8,4},{12,8},{0,12},{5,1},{9,5},{13,9},{1,13},{6,2},{10,6},{... | collective-permute-start | bytes 393224 | tf_op jit(solution)/shard_map/ppermute | solution.py:186
  133.5 1.6 collective-permute-start.17
  135.2 32.3 %collective-permute-start.18 = (f32[256,256]{1,0:T(8,128)S(1)}, f32[256,256]{1,0:T(8,128)S(1)}, u32[]{:S(2)}, u32[]{:S(2)}) collective-permute-start(f32[256,256]{1,0:T(8,128)S(1)} %add_multiply_fusion.total_ref), channel_id=1, source_target_pairs={{0,64},{64,0},{1,65},{65,1},{2,66},{66,2},{3,67},{67,3},{4,68},{68... | collective-permute-start | bytes 786440 | tf_op jit(solution)/shard_map/ppermute | solution.py:182
  (7 other events, 7.1 us)

commit v14 on v12

--- a/solution.py
+++ b/solution.py
@@ -23,7 +23,7 @@
 
 
 def pack_kernel(z_ref, float_ref, quant_ref, out_ref):
-    width = out_ref.shape[2] // 8
+    width = float_ref.shape[1] // 32
     z = z_ref[0]
     for kind, ref in enumerate((float_ref, quant_ref)):
         for j in range(4):
@@ -35,13 +35,17 @@
                     for half in range(2):
                         at = (j * 2 + (yl ^ half)) * width
                         out_ref[kind * 8 + half * 4 + x, :, at : at + width] = block
+    quant = quant_ref[:, :BLOCK]
+    shift = (float_ref[:, :BLOCK].astype(F32) - quant.astype(F32)).astype(BF16)
+    for d in range(16):
+        out_ref[d, :, 8 * width :] = shift if d // 4 % 2 else quant
 
 
 def pack(z, attn_float, attn_quant):
     tokens, d_in = attn_float.shape
     return pl.pallas_call(
         pack_kernel,
-        out_shape=jax.ShapeDtypeStruct((16, tokens, d_in // 4), BF16),
+        out_shape=jax.ShapeDtypeStruct((16, tokens, d_in // 4 + BLOCK), BF16),
         in_specs=[SCALAR, WHOLE, WHOLE],
         out_specs=WHOLE,
         compiler_params=params(),
@@ -69,7 +73,7 @@
 
 
 def project(acts, weights):
-    rows, depth = acts.shape
+    rows, depth = acts.shape[0], 4 * weights[0].shape[0]
     cols = 2 * weights[0].shape[1]
     return pl.pallas_call(
         project_kernel,
@@ -84,8 +88,9 @@
     )(acts, *weights)
 
 
-def finish_kernel(at_ref, parts_ref, total_ref, moved_ref, *outs):
-    core, yh = at_ref[0], at_ref[1]
+def finish_kernel(at_ref, parts_ref, total_ref, *refs):
+    (side_ref, down_ref, cross_ref), outs = refs[:3], refs[3:]
+    core, yh, yl = at_ref[0], at_ref[1], at_ref[2]
     width = parts_ref.shape[2] // 2
     for q in range(2):
         quarter = core if q == 0 else 1 - core
@@ -98,57 +103,49 @@
                     total += parts_ref[at + x, :, cols].astype(F32)
                 start = pl.multiple_of((half * 2 + quarter) * width, width)
                 out[:, pl.ds(start, width)] = total.astype(BF16)
-    total = jnp.where(yh == 1, total_ref[...], moved_ref[...])
-    outs[2][...] = total[:, :BLOCK]
-    outs[3][...] = total[:, BLOCK:]
+    rows = outs[2].shape[0]
+    own = jnp.where(yh == 1, total_ref[:rows], down_ref[...].astype(F32))
+    other = jnp.where(yh == 1, side_ref[...].astype(F32), cross_ref[...].astype(F32))
+    outs[2][...] = jnp.where(yl == 0, own, other)
+    outs[3][...] = jnp.where(yl == 0, other, own)
 
 
 def finish(at, parts, total, moved):
     tokens, cols = parts.shape[1:]
-    rows = total.shape[0]
+    rows = total.shape[0] // 2
     return pl.pallas_call(
         finish_kernel,
         out_shape=(jax.ShapeDtypeStruct((tokens, 2 * cols), BF16),) * 2
         + (jax.ShapeDtypeStruct((rows, BLOCK), F32),) * 2,
-        in_specs=[SCALAR] + [WHOLE] * 3,
+        in_specs=[SCALAR] + [WHOLE] * (2 + len(moved)),
         out_specs=(WHOLE,) * 4,
         compiler_params=params(),
         name="finish",
-    )(at, parts, total, moved)
-
-
-def stats_kernel(at_ref, acts_ref, *refs):
-    pieces, outs, block_ref = refs[:4], refs[5:9], refs[9]
-    y, x = at_ref[0], at_ref[1]
-    tokens = pieces[0].shape[0] // 4
-    for dy, piece in enumerate(pieces):
-        for dx in range(4):
-            start = (lax.rem(y + dy, 4) * 4 + lax.rem(x + dx, 4)) * tokens
-            block_ref[pl.ds(pl.multiple_of(start, tokens), tokens)] = piece[
-                dx * tokens : (dx + 1) * tokens
-            ]
+    )(at, parts, total, *moved)
+
+
+def stats_kernel(acts_ref, after_ref, *outs):
     width = outs[0].shape[0]
     for j, out in enumerate(outs):
         out[...] = lax.dot_general(
-            acts_ref[:, 2 * j * width : (2 * j + 1) * width],
-            block_ref[...],
+            acts_ref[:, j * width : (j + 1) * width],
+            acts_ref[:, 4 * width :],
             (((0,), (0,)), ((), ())),
             preferred_element_type=F32,
         ).astype(out.dtype)
 
 
-def stats(at, acts, pieces, after):
-    width = 2 * BLOCK
+def stats(acts, after):
+    width = (acts.shape[1] - BLOCK) // 4
     return pl.pallas_call(
         stats_kernel,
-        out_shape=(jax.ShapeDtypeStruct((width, width), F32),)
-        + (jax.ShapeDtypeStruct((width, width), BF16),) * 3,
-        in_specs=[SCALAR] + [WHOLE] * 5 + [LEFT],
+        out_shape=(jax.ShapeDtypeStruct((width, BLOCK), F32),)
+        + (jax.ShapeDtypeStruct((width, BLOCK), BF16),) * 3,
+        in_specs=[WHOLE, LEFT],
         out_specs=(WHOLE,) * 4,
-        scratch_shapes=[pltpu.VMEM((acts.shape[0], width), BF16)],
         compiler_params=params(),
         name="stats",
-    )(at, acts, *pieces, after)
+    )(acts, after)
 
 
 def swap(a, axis):
@@ -188,30 +185,27 @@
     payload = pack(z, attn_float, attn_quant)
     payload, got = lax.optimization_barrier((payload, got))
 
-    acts = lax.all_to_all(payload, PLANE, 0, 0, tiled=True).reshape(16 * tokens, 8 * features)
+    acts = lax.all_to_all(payload, PLANE, 0, 0, tiled=True).reshape(16 * tokens, -1)
 
     rows = jnp.concatenate([own, got], axis=0)
     parts = [rows] + [ahead(rows, "z", j) for j in (1, 2, 3)]
     weights = parts + [swap(p, "core") for p in parts]
 
-    quant = attn_quant[:, :BLOCK]
-    shift = (attn_float[:, :BLOCK].astype(F32) - quant.astype(F32)).astype(BF16)
-    block = jnp.concatenate([quant, shift], axis=1)
-    block, *parts = lax.optimization_barrier((block, *parts))
-    line = jnp.concatenate([block] + [ahead(block, "x", j) for j in (1, 2, 3)], axis=0)
-    line, acts = lax.optimization_barrier((line, acts))
-    pieces = [line] + [ahead(line, ("yh", "yl"), j) for j in (1, 2, 3)]
-
     partial = project(acts, weights)
-    partial, *pieces = lax.optimization_barrier((partial, *pieces))
     result = lax.all_to_all(partial.reshape(16, tokens, half), PLANE, 0, 0, tiled=True)
 
-    blocks = stats(jnp.stack([yh * 2 + yl, lax.axis_index("x")]), acts, pieces, partial)
+    blocks = stats(acts, partial)
     total = blocks[0]
     for j in (1, 2, 3):
         total = total + ahead(blocks[j], "z", 4 - j).astype(F32)
     total = (total + swap(total, "core")) * inverse
-    return finish(jnp.stack([core, yh]), result, total, swap(total, "yh"))
+    here, there = total[:features].astype(BF16), total[features:].astype(BF16)
+    moved = (
+        swap(there, "yl"),
+        swap(here, "yh"),
+        lax.ppermute(there, ("yh", "yl"), [(i, 3 - i) for i in range(4)]),
+    )
+    return finish(jnp.stack([core, yh, yl]), result, total, moved)
 
 
 def solution(mesh):

time: 174 us -> 175 us (level)
  local copies, waits for them, and re-layouts: 9.47 us -> 20.7 us
  starting transfers between devices: 37.1 us -> 32.3 us
  waiting for transfers between devices: 102 us -> 97.8 us
    ppermute x12 -> x6, waiting for transfers between devices: 64.3 us -> 47.9 us  [ahead(): return lax.ppermute(a, axis, [((i + j) % 4, i) for i in range(4)])]
    unnamed x14 -> x32, local copies, waits for them, and re-layouts: 9.39 us -> 20.6 us
    all_to_all x1, waiting for transfers between devices: 0.01 us -> 8.69 us  [shards(): lax.all_to_all(payload, PLANE, 0, 0, tiled=True).reshape(16 * tokens, -1)]
    ppermute x12 -> x6, starting transfers between devices: 20.2 us -> 13.3 us  [ahead(): return lax.ppermute(a, axis, [((i + j) % 4, i) for i in range(4)])]
    all_to_all x1, waiting for transfers between devices: 6.47 us -> 12.1 us  [shards(): lax.all_to_all(partial.reshape(16, tokens, half), PLANE, 0, 0, tiled=True)]
    ppermute x0 -> x1, starting transfers between devices: none -> 3.18 us  [shards(): lax.ppermute(there, ('yh', 'yl'), [(i, 3 - i) for i in range(4)])]
    ppermute x6 -> x7, waiting for transfers between devices: 28 us -> 26.4 us  [swap(): return lax.ppermute(a, axis, [(0, 1), (1, 0)])]
  transfers between devices with their start and end apart: 21 -> 17, of which waited for: 13 -> 11; matrix products, arithmetic and copies ran while one was open for 2% -> 1% of each run, Pallas kernels for 9% -> 2%
where the time goes in v14:
time: 175 us; the launch traced here: 174 us
  waiting for transfers between devices  97.8 us (56%)
  starting transfers between devices  32.3 us (18%)
  local copies, waits for them, and re-layouts  20.7 us (12%)
  Pallas kernels  18.6 us (11%)
  other arithmetic  3.74 us (2%)
    ppermute x6, waiting for transfers between devices, ahead(): return lax.ppermute(a, axis, [((i + j) % 4, i) for i in range(4)])  47.9 us
    ppermute x7, waiting for transfers between devices, swap(): return lax.ppermute(a, axis, [(0, 1), (1, 0)])  26.4 us
    unnamed x32, local copies, waits for them, and re-layouts  20.6 us
    ppermute x6, starting transfers between devices, ahead(): return lax.ppermute(a, axis, [((i + j) % 4, i) for i in range(4)])  13.3 us
    all_to_all x1, waiting for transfers between devices, shards(): lax.all_to_all(partial.reshape(16, tokens, half), PLANE, 0, 0, tiled=True)  12.1 us
    pallas_call x1, Pallas kernels, project(): pl.pallas_call(project_kernel, out_shape=jax.ShapeDtypeStruct((rows, cols...  11.1 us
    all_to_all x1, waiting for transfers between devices, shards(): lax.all_to_all(payload, PLANE, 0, 0, tiled=True).reshape(16 * tokens, -1)  8.69 us
    all_to_all x1, starting transfers between devices, shards(): lax.all_to_all(payload, PLANE, 0, 0, tiled=True).reshape(16 * tokens, -1)  7.16 us
  transfers between devices with their start and end apart: 17, of which 11 were waited for; matrix products, arithmetic and copies ran while one was open for 1% of the time, Pallas kernels for 2%

profile of v14, /device:TPU:0, one launch (start us, length us, event | category | flops | bytes accessed | tf_op | source)
XLA Modules:
  0.0 173.9 jit_solution(14244318496164598995)
XLA Ops:
  1.4 1.6 fusion.2
  3.0 1.7 %collective-permute-start = (bf16[256,1024]{1,0:T(8,128)(2,1)S(1)}, bf16[256,1024]{1,0:T(8,128)(2,1)S(1)}, u32[]{:S(2)}, u32[]{:S(2)}) collective-permute-start(bf16[256,1024]{1,0:T(8,128)(2,1)S(1)} %fusion.2), channel_id=1, source_target_pairs={{0,16},{16,0},{32,112},{48,96},{64,80},{80,64},{96,48},{112,32},{1... | collective-permute-start | bytes 1572872 | tf_op jit(solution)/shard_map/ppermute | solution.py:181
  4.7 1.2 copy-done.4
  7.5 2.1 %copy-done.1 = bf16[16,64,2176]{2,1,0:T(8,128)(2,1)} copy-done((bf16[16,64,2176]{2,1,0:T(8,128)(2,1)}, bf16[16,64,2176]{2,1,0:T(8,128)(2,1)S(1)}, u32[]{:S(2)}) %copy-start.1) | copy-done | bytes 4456472
  9.5 2.7 %collective-permute-done = bf16[256,1024]{1,0:T(8,128)(2,1)S(1)} collective-permute-done((bf16[256,1024]{1,0:T(8,128)(2,1)S(1)}, bf16[256,1024]{1,0:T(8,128)(2,1)S(1)}, u32[]{:S(2)}, u32[]{:S(2)}) %collective-permute-start) | collective-permute-done | bytes 524320 | tf_op jit(solution)/shard_map/ppermute | solution.py:181
  12.2 7.2 %all-to-all-start = ((bf16[16,64,2176]{2,1,0:T(8,128)(2,1)}), bf16[16,64,2176]{2,1,0:T(8,128)(2,1)}, u32[]{:S(2)}, u32[]{:S(2)}) async-start(bf16[16,64,2176]{2,1,0:T(8,128)(2,1)} %copy-done.1), calls=%async_computation | async-start | bytes 8912896 | tf_op jit(solution)/shard_map/all_to_all | solution.py:188
  19.5 1.9 %fusion.3 = bf16[256,1024]{1,0:T(8,128)(2,1)S(1)} fusion(s32[256,4096]{1,0:T(8,128)} %param.8, s32[]{:T(128)S(6)} %select_n.28, f32[2,1024]{1,0:T(2,128)S(1)} %constant_dynamic-slice_fusion, bf16[256,4096]{1,0:T(8,128)(2,1)} %param.7, pred[]{:T(512)S(6)} %eq.7), kind=kLoop, calls=%fused_computation.6 | loop fusion | flops 1310720 | bytes 2105349 | tf_op jit(solution)/shard_map/jit(_where)/select_n | solution.py:173
  21.5 2.0 %collective-permute-start.3 = (bf16[512,1024]{1,0:T(8,128)(2,1)S(1)}, bf16[512,1024]{1,0:T(8,128)(2,1)S(1)}, u32[]{:S(2)}, u32[]{:S(2)}) collective-permute-start(bf16[512,1024]{1,0:T(8,128)(2,1)S(1)} %pad_maximum_fusion.refs_0_), channel_id=1, source_target_pairs={{12,0},{0,4},{4,8},{8,12},{13,1},{1,5},{5,9},{9,13},{14,2},{2,6},{... | collective-permute-start | bytes 3145736 | tf_op jit(solution)/shard_map/ppermute | solution.py:156
  23.5 3.6 %collective-permute-start.2 = (bf16[512,1024]{1,0:T(8,128)(2,1)S(1)}, bf16[512,1024]{1,0:T(8,128)(2,1)S(1)}, u32[]{:S(2)}, u32[]{:S(2)}) collective-permute-start(bf16[512,1024]{1,0:T(8,128)(2,1)S(1)} %pad_maximum_fusion.refs_0_), channel_id=1, source_target_pairs={{8,0},{12,4},{0,8},{4,12},{9,1},{13,5},{1,9},{5,13},{10,2},{14,6},... | collective-permute-start | bytes 3145736 | tf_op jit(solution)/shard_map/ppermute | solution.py:156
  28.1 20.7 %collective-permute-done.3.refs_3_ = bf16[512,1024]{1,0:T(8,128)(2,1)S(1)} collective-permute-done((bf16[512,1024]{1,0:T(8,128)(2,1)S(1)}, bf16[512,1024]{1,0:T(8,128)(2,1)S(1)}, u32[]{:S(2)}, u32[]{:S(2)}) %collective-permute-start.3) | collective-permute-done | bytes 1048608 | tf_op jit(solution)/shard_map/ppermute | solution.py:156
  48.8 23.2 %collective-permute-done.2.refs_2_ = bf16[512,1024]{1,0:T(8,128)(2,1)S(1)} collective-permute-done((bf16[512,1024]{1,0:T(8,128)(2,1)S(1)}, bf16[512,1024]{1,0:T(8,128)(2,1)S(1)}, u32[]{:S(2)}, u32[]{:S(2)}) %collective-permute-start.2) | collective-permute-done | bytes 1048608 | tf_op jit(solution)/shard_map/ppermute | solution.py:156
  77.5 8.7 %all-to-all-done = bf16[16,64,2176]{2,1,0:T(8,128)(2,1)} async-done(((bf16[16,64,2176]{2,1,0:T(8,128)(2,1)}), bf16[16,64,2176]{2,1,0:T(8,128)(2,1)}, u32[]{:S(2)}, u32[]{:S(2)}) %all-to-all-start) | async-done | bytes 4456480 | tf_op jit(solution)/shard_map/all_to_all | solution.py:188
  86.2 1.2 copy-done.7
  87.4 1.2 copy-done.9
  88.6 1.2 copy-done.11
  89.9 1.2 copy-done.13
  92.3 11.1 %project.1.after_ref = bf16[1024,2048]{1,0:T(8,128)(2,1)S(1)} custom-call(bf16[1024,2176]{1,0:T(8,128)(2,1)} %bitcast.5.acts_ref, bf16[512,1024]{1,0:T(8,128)(2,1)S(1)} %pad_maximum_fusion.refs_0_, bf16[512,1024]{1,0:T(8,128)(2,1)S(1)} %copy-done.7, bf16[512,1024]{1,0:T(8,128)(2,1)S(1)} %collective-permute-done.2.refs_2_, ...), custom_call_target="tpu_custom_call" | custom-call | flops 8589934592 | bytes 16777216 | tf_op jit(solution)/shard_map/project/pallas_call | solution.py:78
  103.4 2.1 %copy-done.2 = bf16[1024,2048]{1,0:T(8,128)(2,1)} copy-done((bf16[1024,2048]{1,0:T(8,128)(2,1)}, bf16[1024,2048]{1,0:T(8,128)(2,1)S(1)}, u32[]{:S(2)}) %copy-start.2) | copy-done | bytes 4194328
  105.5 4.7 %all-to-all-start.1 = ((bf16[16,64,2048]{2,1,0:T(8,128)(2,1)}), bf16[16,64,2048]{2,1,0:T(8,128)(2,1)}, u32[]{:S(2)}, u32[]{:S(2)}) async-start(bf16[16,64,2048]{2,1,0:T(8,128)(2,1)} %bitcast.18), calls=%async_computation.1 | async-start | bytes 8388608 | tf_op jit(solution)/shard_map/all_to_all | solution.py:195
  110.1 2.2 %copy-done.3 = bf16[1024,2048]{1,0:T(8,128)(2,1)S(1)} copy-done((bf16[1024,2048]{1,0:T(8,128)(2,1)S(1)}, bf16[1024,2048]{1,0:T(8,128)(2,1)}, u32[]{:S(2)}) %copy-start.3) | copy-done | bytes 4194328
  112.3 3.6 %stats.1 = (f32[512,128]{1,0:T(8,128)S(1)}, bf16[512,128]{1,0:T(8,128)(2,1)S(1)}, bf16[512,128]{1,0:T(8,128)(2,1)S(1)}, bf16[512,128]{1,0:T(8,128)(2,1)S(1)}) custom-call(bf16[1024,2176]{1,0:T(8,128)(2,1)} %bitcast.5.acts_ref, bf16[1024,2048]{1,0:T(8,128)(2,1)S(1)} %copy-done.3), custom_call_target="tpu_custom_call" | custom-call | tf_op jit(solution)/shard_map/stats/pallas_call | solution.py:140
  115.9 2.2 %collective-permute-start.8 = (bf16[512,128]{1,0:T(8,128)(2,1)S(1)}, bf16[512,128]{1,0:T(8,128)(2,1)S(1)}, u32[]{:S(2)}, u32[]{:S(2)}) collective-permute-start(bf16[512,128]{1,0:T(8,128)(2,1)S(1)} %get-tuple-element.15), channel_id=1, source_target_pairs={{12,0},{0,4},{4,8},{8,12},{13,1},{1,5},{5,9},{9,13},{14,2},{2,6},{... | collective-permute-start | bytes 393224 | tf_op jit(solution)/shard_map/ppermute | solution.py:156
  118.1 3.6 %collective-permute-start.9 = (bf16[512,128]{1,0:T(8,128)(2,1)S(1)}, bf16[512,128]{1,0:T(8,128)(2,1)S(1)}, u32[]{:S(2)}, u32[]{:S(2)}) collective-permute-start(bf16[512,128]{1,0:T(8,128)(2,1)S(1)} %get-tuple-element.16), channel_id=1, source_target_pairs={{8,0},{12,4},{0,8},{4,12},{9,1},{13,5},{1,9},{5,13},{10,2},{14,6},... | collective-permute-start | bytes 393224 | tf_op jit(solution)/shard_map/ppermute | solution.py:156
  122.7 1.9 %collective-permute-done.8 = bf16[512,128]{1,0:T(8,128)(2,1)S(1)} collective-permute-done((bf16[512,128]{1,0:T(8,128)(2,1)S(1)}, bf16[512,128]{1,0:T(8,128)(2,1)S(1)}, u32[]{:S(2)}, u32[]{:S(2)}) %collective-permute-start.8) | collective-permute-done | bytes 131104 | tf_op jit(solution)/shard_map/ppermute | solution.py:156
  124.5 1.8 %collective-permute-done.9 = bf16[512,128]{1,0:T(8,128)(2,1)S(1)} collective-permute-done((bf16[512,128]{1,0:T(8,128)(2,1)S(1)}, bf16[512,128]{1,0:T(8,128)(2,1)S(1)}, u32[]{:S(2)}, u32[]{:S(2)}) %collective-permute-start.9) | collective-permute-done | bytes 131104 | tf_op jit(solution)/shard_map/ppermute | solution.py:156
  126.8 1.5 collective-permute-done.11
  128.4 3.2 %collective-permute-start.14 = (bf16[256,128]{1,0:T(8,128)(2,1)S(1)}, bf16[256,128]{1,0:T(8,128)(2,1)S(1)}, u32[]{:S(2)}, u32[]{:S(2)}) collective-permute-start(bf16[256,128]{1,0:T(8,128)(2,1)S(1)} %get-tuple-element.21), channel_id=1, source_target_pairs={{0,80},{16,64},{64,16},{80,0},{1,81},{17,65},{65,17},{81,1},{2,82}... | collective-permute-start | bytes 196616 | tf_op jit(solution)/shard_map/ppermute | solution.py:206
  131.8 1.4 collective-permute-start.13
  133.2 22.4 %collective-permute-done.13.refs_1_ = bf16[256,128]{1,0:T(8,128)(2,1)S(1)} collective-permute-done((bf16[256,128]{1,0:T(8,128)(2,1)S(1)}, bf16[256,128]{1,0:T(8,128)(2,1)S(1)}, u32[]{:S(2)}, u32[]{:S(2)}) %collective-permute-start.13) | collective-permute-done | bytes 65568 | tf_op jit(solution)/shard_map/ppermute | solution.py:152
  155.6 2.5 %collective-permute-done.12.refs_0_ = bf16[256,128]{1,0:T(8,128)(2,1)S(1)} collective-permute-done((bf16[256,128]{1,0:T(8,128)(2,1)S(1)}, bf16[256,128]{1,0:T(8,128)(2,1)S(1)}, u32[]{:S(2)}, u32[]{:S(2)}) %collective-permute-start.12) | collective-permute-done | bytes 65568 | tf_op jit(solution)/shard_map/ppermute | solution.py:152
  158.1 12.1 %all-to-all-done.1.parts_ref = bf16[16,64,2048]{2,1,0:T(8,128)(2,1)} async-done(((bf16[16,64,2048]{2,1,0:T(8,128)(2,1)}), bf16[16,64,2048]{2,1,0:T(8,128)(2,1)}, u32[]{:S(2)}, u32[]{:S(2)}) %all-to-all-start.1) | async-done | bytes 4194336 | tf_op jit(solution)/shard_map/all_to_all | solution.py:195
  170.2 3.7 %finish.1 = (bf16[64,4096]{1,0:T(8,128)(2,1)}, bf16[64,4096]{1,0:T(8,128)(2,1)}, f32[256,128]{1,0:T(8,128)}, f32[256,128]{1,0:T(8,128)}) custom-call(s32[3]{0:T(128)S(1)} %pad_add_fusion.at_ref, bf16[16,64,2048]{2,1,0:T(8,128)(2,1)} %all-to-all-done.1.parts_ref, f32[512,128]{1,0:T(8,128)S(1)} %get-tuple-element.19.total_ref, ...), custom_call_target="tpu_custom_call" | custom-call | tf_op jit(solution)/shard_map/finish/pallas_call | solution.py:116
  (47 shorter events, 12.0 us)
Async XLA Ops:
  3.0 9.3 %collective-permute-start = (bf16[256,1024]{1,0:T(8,128)(2,1)S(1)}, bf16[256,1024]{1,0:T(8,128)(2,1)S(1)}, u32[]{:S(2)}, u32[]{:S(2)}) collective-permute-start(bf16[256,1024]{1,0:T(8,128)(2,1)S(1)} %fusion.2), channel_id=1, source_target_pairs={{0,16},{16,0},{32,112},{48,96},{64,80},{80,64},{96,48},{112,32},{1... | collective-permute-start | bytes 1572872 | tf_op jit(solution)/shard_map/ppermute | solution.py:181
  4.7 1.2 copy-start.4
  5.9 1.2 copy-start.5
  7.5 2.1 %copy-start.1 = (bf16[16,64,2176]{2,1,0:T(8,128)(2,1)}, bf16[16,64,2176]{2,1,0:T(8,128)(2,1)S(1)}, u32[]{:S(2)}) copy-start(bf16[16,64,2176]{2,1,0:T(8,128)(2,1)S(1)} %pack.1) | copy-start | bytes 13369348
  12.2 74.0 %all-to-all-start = ((bf16[16,64,2176]{2,1,0:T(8,128)(2,1)}), bf16[16,64,2176]{2,1,0:T(8,128)(2,1)}, u32[]{:S(2)}, u32[]{:S(2)}) async-start(bf16[16,64,2176]{2,1,0:T(8,128)(2,1)} %copy-done.1), calls=%async_computation | async-start | bytes 8912896 | tf_op jit(solution)/shard_map/all_to_all | solution.py:188
  21.5 27.3 %collective-permute-start.3 = (bf16[512,1024]{1,0:T(8,128)(2,1)S(1)}, bf16[512,1024]{1,0:T(8,128)(2,1)S(1)}, u32[]{:S(2)}, u32[]{:S(2)}) collective-permute-start(bf16[512,1024]{1,0:T(8,128)(2,1)S(1)} %pad_maximum_fusion.refs_0_), channel_id=1, source_target_pairs={{12,0},{0,4},{4,8},{8,12},{13,1},{1,5},{5,9},{9,13},{14,2},{2,6},{... | collective-permute-start | bytes 3145736 | tf_op jit(solution)/shard_map/ppermute | solution.py:156
  23.5 48.5 %collective-permute-start.2 = (bf16[512,1024]{1,0:T(8,128)(2,1)S(1)}, bf16[512,1024]{1,0:T(8,128)(2,1)S(1)}, u32[]{:S(2)}, u32[]{:S(2)}) collective-permute-start(bf16[512,1024]{1,0:T(8,128)(2,1)S(1)} %pad_maximum_fusion.refs_0_), channel_id=1, source_target_pairs={{8,0},{12,4},{0,8},{4,12},{9,1},{13,5},{1,9},{5,13},{10,2},{14,6},... | collective-permute-start | bytes 3145736 | tf_op jit(solution)/shard_map/ppermute | solution.py:156
  27.1 45.0 %collective-permute-start.1 = (bf16[512,1024]{1,0:T(8,128)(2,1)S(1)}, bf16[512,1024]{1,0:T(8,128)(2,1)S(1)}, u32[]{:S(2)}, u32[]{:S(2)}) collective-permute-start(bf16[512,1024]{1,0:T(8,128)(2,1)S(1)} %pad_maximum_fusion.refs_0_), channel_id=1, source_target_pairs={{4,0},{8,4},{12,8},{0,12},{5,1},{9,5},{13,9},{1,13},{6,2},{10,6},{... | collective-permute-start | bytes 3145736 | tf_op jit(solution)/shard_map/ppermute | solution.py:156
  28.1 45.4 %collective-permute-start.4 = (bf16[512,1024]{1,0:T(8,128)(2,1)S(1)}, bf16[512,1024]{1,0:T(8,128)(2,1)S(1)}, u32[]{:S(2)}, u32[]{:S(2)}) collective-permute-start(bf16[512,1024]{1,0:T(8,128)(2,1)S(1)} %pad_maximum_fusion.refs_0_), channel_id=1, source_target_pairs={{0,32},{32,0},{1,33},{33,1},{2,34},{34,2},{3,35},{35,3},{4,36},{36... | collective-permute-start | bytes 3145736 | tf_op jit(solution)/shard_map/ppermute | solution.py:152
  48.8 25.7 %collective-permute-start.7 = (bf16[512,1024]{1,0:T(8,128)(2,1)S(1)}, bf16[512,1024]{1,0:T(8,128)(2,1)S(1)}, u32[]{:S(2)}, u32[]{:S(2)}) collective-permute-start(bf16[512,1024]{1,0:T(8,128)(2,1)S(1)} %collective-permute-done.3.refs_3_), channel_id=1, source_target_pairs={{0,32},{32,0},{1,33},{33,1},{2,34},{34,2},{3,35},{35,3},{4,36},{36... | collective-permute-start | bytes 3145736 | tf_op jit(solution)/shard_map/ppermute | solution.py:152
  72.0 3.4 %collective-permute-start.6 = (bf16[512,1024]{1,0:T(8,128)(2,1)S(1)}, bf16[512,1024]{1,0:T(8,128)(2,1)S(1)}, u32[]{:S(2)}, u32[]{:S(2)}) collective-permute-start(bf16[512,1024]{1,0:T(8,128)(2,1)S(1)} %collective-permute-done.2.refs_2_), channel_id=1, source_target_pairs={{0,32},{32,0},{1,33},{33,1},{2,34},{34,2},{3,35},{35,3},{4,36},{36... | collective-permute-start | bytes 3145736 | tf_op jit(solution)/shard_map/ppermute | solution.py:152
  72.0 4.5 %collective-permute-start.5 = (bf16[512,1024]{1,0:T(8,128)(2,1)S(1)}, bf16[512,1024]{1,0:T(8,128)(2,1)S(1)}, u32[]{:S(2)}, u32[]{:S(2)}) collective-permute-start(bf16[512,1024]{1,0:T(8,128)(2,1)S(1)} %collective-permute-done.1.refs_1_), channel_id=1, source_target_pairs={{0,32},{32,0},{1,33},{33,1},{2,34},{34,2},{3,35},{35,3},{4,36},{36... | collective-permute-start | bytes 3145736 | tf_op jit(solution)/shard_map/ppermute | solution.py:152
  72.5 1.0 copy-start.6
  73.5 1.0 copy-start.8
  74.5 1.0 copy-start.10
  75.5 1.0 copy-start.12
  76.5 1.0 copy-start.14
  86.2 1.2 copy-start.7
  87.4 1.2 copy-start.9
  88.6 1.2 copy-start.11
  89.9 1.2 copy-start.13
  91.1 1.2 copy-start.15
  103.4 2.1 %copy-start.2 = (bf16[1024,2048]{1,0:T(8,128)(2,1)}, bf16[1024,2048]{1,0:T(8,128)(2,1)S(1)}, u32[]{:S(2)}) copy-start(bf16[1024,2048]{1,0:T(8,128)(2,1)S(1)} %project.1.after_ref) | copy-start | bytes 12582916
  105.5 64.7 %all-to-all-start.1 = ((bf16[16,64,2048]{2,1,0:T(8,128)(2,1)}), bf16[16,64,2048]{2,1,0:T(8,128)(2,1)}, u32[]{:S(2)}, u32[]{:S(2)}) async-start(bf16[16,64,2048]{2,1,0:T(8,128)(2,1)} %bitcast.18), calls=%async_computation.1 | async-start | bytes 8388608 | tf_op jit(solution)/shard_map/all_to_all | solution.py:195
  110.1 2.2 %copy-start.3 = (bf16[1024,2048]{1,0:T(8,128)(2,1)S(1)}, bf16[1024,2048]{1,0:T(8,128)(2,1)}, u32[]{:S(2)}) copy-start(bf16[1024,2048]{1,0:T(8,128)(2,1)} %copy-done.2) | copy-start | bytes 12582916
  115.9 8.6 %collective-permute-start.8 = (bf16[512,128]{1,0:T(8,128)(2,1)S(1)}, bf16[512,128]{1,0:T(8,128)(2,1)S(1)}, u32[]{:S(2)}, u32[]{:S(2)}) collective-permute-start(bf16[512,128]{1,0:T(8,128)(2,1)S(1)} %get-tuple-element.15), channel_id=1, source_target_pairs={{12,0},{0,4},{4,8},{8,12},{13,1},{1,5},{5,9},{9,13},{14,2},{2,6},{... | collective-permute-start | bytes 393224 | tf_op jit(solution)/shard_map/ppermute | solution.py:156
  118.1 8.3 %collective-permute-start.9 = (bf16[512,128]{1,0:T(8,128)(2,1)S(1)}, bf16[512,128]{1,0:T(8,128)(2,1)S(1)}, u32[]{:S(2)}, u32[]{:S(2)}) collective-permute-start(bf16[512,128]{1,0:T(8,128)(2,1)S(1)} %get-tuple-element.16), channel_id=1, source_target_pairs={{8,0},{12,4},{0,8},{4,12},{9,1},{13,5},{1,9},{5,13},{10,2},{14,6},... | collective-permute-start | bytes 393224 | tf_op jit(solution)/shard_map/ppermute | solution.py:156
  121.7 5.0 %collective-permute-start.10 = (bf16[512,128]{1,0:T(8,128)(2,1)S(1)}, bf16[512,128]{1,0:T(8,128)(2,1)S(1)}, u32[]{:S(2)}, u32[]{:S(2)}) collective-permute-start(bf16[512,128]{1,0:T(8,128)(2,1)S(1)} %get-tuple-element.17), channel_id=1, source_target_pairs={{4,0},{8,4},{12,8},{0,12},{5,1},{9,5},{13,9},{1,13},{6,2},{10,6},{... | collective-permute-start | bytes 393224 | tf_op jit(solution)/shard_map/ppermute | solution.py:156
  126.7 1.6 collective-permute-start.11
  128.4 27.3 %collective-permute-start.14 = (bf16[256,128]{1,0:T(8,128)(2,1)S(1)}, bf16[256,128]{1,0:T(8,128)(2,1)S(1)}, u32[]{:S(2)}, u32[]{:S(2)}) collective-permute-start(bf16[256,128]{1,0:T(8,128)(2,1)S(1)} %get-tuple-element.21), channel_id=1, source_target_pairs={{0,80},{16,64},{64,16},{80,0},{1,81},{17,65},{65,17},{81,1},{2,82}... | collective-permute-start | bytes 196616 | tf_op jit(solution)/shard_map/ppermute | solution.py:206
  131.5 26.6 %collective-permute-start.12 = (bf16[256,128]{1,0:T(8,128)(2,1)S(1)}, bf16[256,128]{1,0:T(8,128)(2,1)S(1)}, u32[]{:S(2)}, u32[]{:S(2)}) collective-permute-start(bf16[256,128]{1,0:T(8,128)(2,1)S(1)} %get-tuple-element.21), channel_id=1, source_target_pairs={{0,16},{16,0},{1,17},{17,1},{2,18},{18,2},{3,19},{19,3},{4,20},{20... | collective-permute-start | bytes 196616 | tf_op jit(solution)/shard_map/ppermute | solution.py:152
  131.8 23.8 %collective-permute-start.13 = (bf16[256,128]{1,0:T(8,128)(2,1)S(1)}, bf16[256,128]{1,0:T(8,128)(2,1)S(1)}, u32[]{:S(2)}, u32[]{:S(2)}) collective-permute-start(bf16[256,128]{1,0:T(8,128)(2,1)S(1)} %get-tuple-element.20), channel_id=1, source_target_pairs={{0,64},{64,0},{1,65},{65,1},{2,66},{66,2},{3,67},{67,3},{4,68},{68... | collective-permute-start | bytes 196616 | tf_op jit(solution)/shard_map/ppermute | solution.py:152
  (1 other events, 0.8 us)

commit v15 on v14

--- a/solution.py
+++ b/solution.py
@@ -57,50 +57,47 @@
     *weights, out_ref = refs
     depth, width = weights[0].shape
     tile = 512
-    for q in range(2):
-        for col in range(0, width, tile):
-            for row in range(0, acts_ref.shape[0], 256):
-                rows, total = slice(row, row + 256), None
-                for j in range(4):
-                    term = jnp.dot(
-                        acts_ref[rows, j * depth : (j + 1) * depth],
-                        weights[4 * q + j][:, col : col + tile],
-                        preferred_element_type=F32,
-                    )
-                    total = term if total is None else total + term
-                at = q * width + col
-                out_ref[rows, at : at + tile] = total.astype(BF16)
+    for col in range(0, width, tile):
+        total = None
+        for j, ref in enumerate(weights):
+            term = jnp.dot(
+                acts_ref[:, j * depth : (j + 1) * depth],
+                ref[:, col : col + tile],
+                preferred_element_type=F32,
+            )
+            total = term if total is None else total + term
+        out_ref[:, col : col + tile] = total.astype(BF16)
 
 
 def project(acts, weights):
-    rows, depth = acts.shape[0], 4 * weights[0].shape[0]
-    cols = 2 * weights[0].shape[1]
+    rows, cols = acts.shape[0], weights[0].shape[1]
+    step = 256
     return pl.pallas_call(
         project_kernel,
         out_shape=jax.ShapeDtypeStruct((rows, cols), BF16),
-        in_specs=[WHOLE] * (1 + len(weights)),
-        out_specs=WHOLE,
+        grid=(rows // step,),
+        in_specs=[pl.BlockSpec((step, acts.shape[1]), lambda i: (i, 0))] + [WHOLE] * len(weights),
+        out_specs=pl.BlockSpec((step, cols), lambda i: (i, 0)),
         compiler_params=params(),
         cost_estimate=pl.CostEstimate(
-            flops=2 * rows * depth * cols, bytes_accessed=16 << 20, transcendentals=0
+            flops=2 * rows * 2048 * cols, bytes_accessed=12 << 20, transcendentals=0
         ),
         name="project",
     )(acts, *weights)
 
 
-def finish_kernel(at_ref, parts_ref, total_ref, *refs):
+def finish_kernel(at_ref, first_ref, second_ref, total_ref, *refs):
     (side_ref, down_ref, cross_ref), outs = refs[:3], refs[3:]
     core, yh, yl = at_ref[0], at_ref[1], at_ref[2]
-    width = parts_ref.shape[2] // 2
-    for q in range(2):
+    width = first_ref.shape[2]
+    for q, ref in enumerate((first_ref, second_ref)):
         quarter = core if q == 0 else 1 - core
         for kind, out in enumerate(outs[:2]):
             for half in range(2):
                 at = kind * 8 + half * 4
-                cols = slice(q * width, (q + 1) * width)
-                total = parts_ref[at, :, cols].astype(F32)
+                total = ref[at].astype(F32)
                 for x in range(1, 4):
-                    total += parts_ref[at + x, :, cols].astype(F32)
+                    total += ref[at + x].astype(F32)
                 start = pl.multiple_of((half * 2 + quarter) * width, width)
                 out[:, pl.ds(start, width)] = total.astype(BF16)
     rows = outs[2].shape[0]
@@ -110,18 +107,18 @@
     outs[3][...] = jnp.where(yl == 0, other, own)
 
 
-def finish(at, parts, total, moved):
-    tokens, cols = parts.shape[1:]
+def finish(at, first, second, total, moved):
+    tokens, cols = first.shape[1:]
     rows = total.shape[0] // 2
     return pl.pallas_call(
         finish_kernel,
-        out_shape=(jax.ShapeDtypeStruct((tokens, 2 * cols), BF16),) * 2
+        out_shape=(jax.ShapeDtypeStruct((tokens, 4 * cols), BF16),) * 2
         + (jax.ShapeDtypeStruct((rows, BLOCK), F32),) * 2,
-        in_specs=[SCALAR] + [WHOLE] * (2 + len(moved)),
+        in_specs=[SCALAR] + [WHOLE] * (3 + len(moved)),
         out_specs=(WHOLE,) * 4,
         compiler_params=params(),
         name="finish",
-    )(at, parts, total, *moved)
+    )(at, first, second, total, *moved)
 
 
 def stats_kernel(acts_ref, after_ref, *outs):
@@ -189,12 +186,16 @@
 
     rows = jnp.concatenate([own, got], axis=0)
     parts = [rows] + [ahead(rows, "z", j) for j in (1, 2, 3)]
-    weights = parts + [swap(p, "core") for p in parts]
-
-    partial = project(acts, weights)
-    result = lax.all_to_all(partial.reshape(16, tokens, half), PLANE, 0, 0, tiled=True)
-
-    blocks = stats(acts, partial)
+    others = [swap(p, "core") for p in parts]
+
+    def output(p):
+        return lax.all_to_all(p.reshape(16, tokens, quarter), PLANE, 0, 0, tiled=True)
+
+    result1 = output(project(acts, parts))
+    second = project(acts, others)
+
+    blocks = stats(acts, second)
+    result2 = output(second)
     total = blocks[0]
     for j in (1, 2, 3):
         total = total + ahead(blocks[j], "z", 4 - j).astype(F32)
@@ -205,7 +206,7 @@
         swap(here, "yh"),
         lax.ppermute(there, ("yh", "yl"), [(i, 3 - i) for i in range(4)]),
     )
-    return finish(jnp.stack([core, yh, yl]), result, total, moved)
+    return finish(jnp.stack([core, yh, yl]), result1, result2, total, moved)
 
 
 def solution(mesh):

time: 175 us -> 169 us (0.966)
  local copies, waits for them, and re-layouts: 20.7 us -> 9.47 us
  starting transfers between devices: 32.3 us -> 34.4 us
  Pallas kernels: 18.6 us -> 20.6 us
    ppermute x7, waiting for transfers between devices: 26.4 us -> 12.9 us  [swap(): return lax.ppermute(a, axis, [(0, 1), (1, 0)])]
    unnamed x32 -> x24, local copies, waits for them, and re-layouts: 20.6 us -> 9.38 us
    all_to_all x1 -> x2, waiting for transfers between devices: 12.1 us -> 17.1 us  [output(): lax.all_to_all(p.reshape(16, tokens, quarter), PLANE, 0, 0, tiled=True)]
    all_to_all x1 -> x2, starting transfers between devices: 4.66 us -> 9.04 us  [output(): lax.all_to_all(p.reshape(16, tokens, quarter), PLANE, 0, 0, tiled=True)]
    ppermute x6, waiting for transfers between devices: 47.9 us -> 52 us  [ahead(): return lax.ppermute(a, axis, [((i + j) % 4, i) for i in range(4)])]
    all_to_all x1, waiting for transfers between devices: 8.69 us -> 11.6 us  [shards(): lax.all_to_all(payload, PLANE, 0, 0, tiled=True).reshape(16 * tokens, -1)]
    ppermute x6, starting transfers between devices: 13.3 us -> 10.7 us  [ahead(): return lax.ppermute(a, axis, [((i + j) % 4, i) for i in range(4)])]
    pallas_call x1 -> x2, Pallas kernels: 11.1 us -> 13.6 us  [project(): pl.pallas_call(project_kernel, out_shape=jax.ShapeDtypeStruct((rows, cols...]
  transfers between devices with their start and end apart: 17 -> 18, of which waited for: 11 -> 16; matrix products, arithmetic and copies ran while one was open for 1% -> 1% of each run, Pallas kernels for 2% -> 7%
where the time goes in v15:
time: 169 us; the launch traced here: 168 us
  waiting for transfers between devices  98.7 us (58%)
  starting transfers between devices  34.4 us (20%)
  Pallas kernels  20.6 us (12%)
  local copies, waits for them, and re-layouts  9.47 us (6%)
  other arithmetic  3.79 us (2%)
    ppermute x6, waiting for transfers between devices, ahead(): return lax.ppermute(a, axis, [((i + j) % 4, i) for i in range(4)])  52 us
    all_to_all x2, waiting for transfers between devices, output(): lax.all_to_all(p.reshape(16, tokens, quarter), PLANE, 0, 0, tiled=True)  17.1 us
    pallas_call x2, Pallas kernels, project(): pl.pallas_call(project_kernel, out_shape=jax.ShapeDtypeStruct((rows, cols...  13.6 us
    ppermute x7, waiting for transfers between devices, swap(): return lax.ppermute(a, axis, [(0, 1), (1, 0)])  12.9 us
    all_to_all x1, waiting for transfers between devices, shards(): lax.all_to_all(payload, PLANE, 0, 0, tiled=True).reshape(16 * tokens, -1)  11.6 us
    ppermute x6, starting transfers between devices, ahead(): return lax.ppermute(a, axis, [((i + j) % 4, i) for i in range(4)])  10.7 us
    unnamed x24, local copies, waits for them, and re-layouts  9.38 us
    all_to_all x2, starting transfers between devices, output(): lax.all_to_all(p.reshape(16, tokens, quarter), PLANE, 0, 0, tiled=True)  9.04 us
  transfers between devices with their start and end apart: 18, of which 16 were waited for; matrix products, arithmetic and copies ran while one was open for 1% of the time, Pallas kernels for 7%

profile of v15, /device:TPU:0, one launch (start us, length us, event | category | flops | bytes accessed | tf_op | source)
XLA Modules:
  0.0 167.8 jit_solution(14904107066771138961)
XLA Ops:
  1.4 1.6 fusion.2
  3.0 1.7 %collective-permute-start = (bf16[256,1024]{1,0:T(8,128)(2,1)S(1)}, bf16[256,1024]{1,0:T(8,128)(2,1)S(1)}, u32[]{:S(2)}, u32[]{:S(2)}) collective-permute-start(bf16[256,1024]{1,0:T(8,128)(2,1)S(1)} %fusion.2), channel_id=1, source_target_pairs={{0,16},{16,0},{32,112},{48,96},{64,80},{80,64},{96,48},{112,32},{1... | collective-permute-start | bytes 1572872 | tf_op jit(solution)/shard_map/ppermute | solution.py:178
  5.0 2.1 %copy-done.1 = bf16[16,64,2176]{2,1,0:T(8,128)(2,1)} copy-done((bf16[16,64,2176]{2,1,0:T(8,128)(2,1)}, bf16[16,64,2176]{2,1,0:T(8,128)(2,1)S(1)}, u32[]{:S(2)}) %copy-start.1) | copy-done | bytes 4456472
  7.1 5.1 %collective-permute-done = bf16[256,1024]{1,0:T(8,128)(2,1)S(1)} collective-permute-done((bf16[256,1024]{1,0:T(8,128)(2,1)S(1)}, bf16[256,1024]{1,0:T(8,128)(2,1)S(1)}, u32[]{:S(2)}, u32[]{:S(2)}) %collective-permute-start) | collective-permute-done | bytes 524320 | tf_op jit(solution)/shard_map/ppermute | solution.py:178
  13.0 7.2 %all-to-all-start = ((bf16[16,64,2176]{2,1,0:T(8,128)(2,1)}), bf16[16,64,2176]{2,1,0:T(8,128)(2,1)}, u32[]{:S(2)}, u32[]{:S(2)}) async-start(bf16[16,64,2176]{2,1,0:T(8,128)(2,1)} %copy-done.1), calls=%async_computation | async-start | bytes 8912896 | tf_op jit(solution)/shard_map/all_to_all | solution.py:185
  20.3 2.0 %fusion.3 = bf16[256,1024]{1,0:T(8,128)(2,1)S(1)} fusion(s32[256,4096]{1,0:T(8,128)} %param.8, s32[]{:T(128)S(6)} %select_n.28, f32[2,1024]{1,0:T(2,128)S(1)} %constant_dynamic-slice_fusion, bf16[256,4096]{1,0:T(8,128)(2,1)} %param.7, pred[]{:T(512)S(6)} %eq.7), kind=kLoop, calls=%fused_computation.6 | loop fusion | flops 1310720 | bytes 2105349 | tf_op jit(solution)/shard_map/jit(_where)/select_n | solution.py:170
  22.4 4.1 %collective-permute-start.1 = (bf16[512,1024]{1,0:T(8,128)(2,1)S(1)}, bf16[512,1024]{1,0:T(8,128)(2,1)S(1)}, u32[]{:S(2)}, u32[]{:S(2)}) collective-permute-start(bf16[512,1024]{1,0:T(8,128)(2,1)S(1)} %pad_maximum_fusion.refs_0_), channel_id=1, source_target_pairs={{4,0},{8,4},{12,8},{0,12},{5,1},{9,5},{13,9},{1,13},{6,2},{10,6},{... | collective-permute-start | bytes 3145736 | tf_op jit(solution)/shard_map/ppermute | solution.py:153
  26.5 1.3 collective-permute-start.3
  27.7 43.2 %collective-permute-done.1.refs_1_ = bf16[512,1024]{1,0:T(8,128)(2,1)S(1)} collective-permute-done((bf16[512,1024]{1,0:T(8,128)(2,1)S(1)}, bf16[512,1024]{1,0:T(8,128)(2,1)S(1)}, u32[]{:S(2)}, u32[]{:S(2)}) %collective-permute-start.1) | collective-permute-done | bytes 1048608 | tf_op jit(solution)/shard_map/ppermute | solution.py:153
  72.0 2.4 %collective-permute-done.3.refs_3_ = bf16[512,1024]{1,0:T(8,128)(2,1)S(1)} collective-permute-done((bf16[512,1024]{1,0:T(8,128)(2,1)S(1)}, bf16[512,1024]{1,0:T(8,128)(2,1)S(1)}, u32[]{:S(2)}, u32[]{:S(2)}) %collective-permute-start.3) | collective-permute-done | bytes 1048608 | tf_op jit(solution)/shard_map/ppermute | solution.py:153
  75.4 11.6 %all-to-all-done = bf16[16,64,2176]{2,1,0:T(8,128)(2,1)} async-done(((bf16[16,64,2176]{2,1,0:T(8,128)(2,1)}), bf16[16,64,2176]{2,1,0:T(8,128)(2,1)}, u32[]{:S(2)}, u32[]{:S(2)}) %all-to-all-start) | async-done | bytes 4456480 | tf_op jit(solution)/shard_map/all_to_all | solution.py:185
  89.4 6.3 %project.2 = bf16[1024,1024]{1,0:T(8,128)(2,1)S(1)} custom-call(bf16[1024,2176]{1,0:T(8,128)(2,1)} %bitcast.5.acts_ref, bf16[512,1024]{1,0:T(8,128)(2,1)S(1)} %pad_maximum_fusion.refs_0_, bf16[512,1024]{1,0:T(8,128)(2,1)S(1)} %collective-permute-done.1.refs_1_, bf16[512,1024]{1,0:T(8,128)(2,1)S(1)} %copy-done.7, bf16[512,1024]{1,0:T(8,128)(2,1)S(1)} %copy-done.9), custom_call_target="tpu_custom_call" | custom-call | flops 4294967296 | bytes 12582912 | tf_op jit(solution)/shard_map/project/pallas_call | solution.py:75
  95.7 1.4 copy-done.2
  97.1 4.6 %all-to-all-start.1 = ((bf16[16,64,1024]{2,1,0:T(8,128)(2,1)}), bf16[16,64,1024]{2,1,0:T(8,128)(2,1)S(1)}, u32[]{:S(2)}, u32[]{:S(2)}) async-start(bf16[16,64,1024]{2,1,0:T(8,128)(2,1)} %bitcast.19), calls=%async_computation.1 | async-start | bytes 4194304 | tf_op jit(solution)/shard_map/all_to_all | solution.py:192
  102.8 2.2 %collective-permute-done.4.refs_0_ = bf16[512,1024]{1,0:T(8,128)(2,1)S(1)} collective-permute-done((bf16[512,1024]{1,0:T(8,128)(2,1)S(1)}, bf16[512,1024]{1,0:T(8,128)(2,1)S(1)}, u32[]{:S(2)}, u32[]{:S(2)}) %collective-permute-start.4) | collective-permute-done | bytes 1048608 | tf_op jit(solution)/shard_map/ppermute | solution.py:149
  106.2 1.5 collective-permute-done.6.refs_2_
  107.7 1.5 collective-permute-done.7.refs_3_
  109.2 7.3 %project.3.after_ref = bf16[1024,1024]{1,0:T(8,128)(2,1)} custom-call(bf16[1024,2176]{1,0:T(8,128)(2,1)} %bitcast.5.acts_ref, bf16[512,1024]{1,0:T(8,128)(2,1)S(1)} %collective-permute-done.4.refs_0_, bf16[512,1024]{1,0:T(8,128)(2,1)S(1)} %collective-permute-done.5.refs_1_, bf16[512,1024]{1,0:T(8,128)(2,1)S(1)} %collective-permute-done.6.refs_2_, ...), custom_call_target="tpu_custom_call" | custom-call | flops 4294967296 | bytes 12582912 | tf_op jit(solution)/shard_map/project/pallas_call | solution.py:75
  116.5 14.4 %all-to-all-done.1.first_ref = bf16[16,64,1024]{2,1,0:T(8,128)(2,1)S(1)} async-done(((bf16[16,64,1024]{2,1,0:T(8,128)(2,1)}), bf16[16,64,1024]{2,1,0:T(8,128)(2,1)S(1)}, u32[]{:S(2)}, u32[]{:S(2)}) %all-to-all-start.1) | async-done | bytes 2097184 | tf_op jit(solution)/shard_map/all_to_all | solution.py:192
  130.9 4.4 %all-to-all-start.2 = ((bf16[16,64,1024]{2,1,0:T(8,128)(2,1)}), bf16[16,64,1024]{2,1,0:T(8,128)(2,1)}, u32[]{:S(2)}, u32[]{:S(2)}) async-start(bf16[16,64,1024]{2,1,0:T(8,128)(2,1)} %bitcast.8), calls=%async_computation.2 | async-start | bytes 4194304 | tf_op jit(solution)/shard_map/all_to_all | solution.py:192
  135.4 3.6 %stats.1 = (f32[512,128]{1,0:T(8,128)S(1)}, bf16[512,128]{1,0:T(8,128)(2,1)S(1)}, bf16[512,128]{1,0:T(8,128)(2,1)S(1)}, bf16[512,128]{1,0:T(8,128)(2,1)S(1)}) custom-call(bf16[1024,2176]{1,0:T(8,128)(2,1)} %bitcast.5.acts_ref, bf16[1024,1024]{1,0:T(8,128)(2,1)} %project.3.after_ref), custom_call_target="tpu_custom_call" | custom-call | tf_op jit(solution)/shard_map/stats/pallas_call | solution.py:137
  138.9 4.1 %collective-permute-start.10 = (bf16[512,128]{1,0:T(8,128)(2,1)S(1)}, bf16[512,128]{1,0:T(8,128)(2,1)S(1)}, u32[]{:S(2)}, u32[]{:S(2)}) collective-permute-start(bf16[512,128]{1,0:T(8,128)(2,1)S(1)} %get-tuple-element.17), channel_id=1, source_target_pairs={{4,0},{8,4},{12,8},{0,12},{5,1},{9,5},{13,9},{1,13},{6,2},{10,6},{... | collective-permute-start | bytes 393224 | tf_op jit(solution)/shard_map/ppermute | solution.py:153
  143.1 1.2 collective-permute-start.8
  144.3 2.9 %collective-permute-done.10 = bf16[512,128]{1,0:T(8,128)(2,1)S(1)} collective-permute-done((bf16[512,128]{1,0:T(8,128)(2,1)S(1)}, bf16[512,128]{1,0:T(8,128)(2,1)S(1)}, u32[]{:S(2)}, u32[]{:S(2)}) %collective-permute-start.10) | collective-permute-done | bytes 131104 | tf_op jit(solution)/shard_map/ppermute | solution.py:153
  147.2 2.4 %collective-permute-done.9 = bf16[512,128]{1,0:T(8,128)(2,1)S(1)} collective-permute-done((bf16[512,128]{1,0:T(8,128)(2,1)S(1)}, bf16[512,128]{1,0:T(8,128)(2,1)S(1)}, u32[]{:S(2)}, u32[]{:S(2)}) %collective-permute-start.9) | collective-permute-done | bytes 131104 | tf_op jit(solution)/shard_map/ppermute | solution.py:153
  150.8 1.5 collective-permute-done.11
  152.4 1.8 %collective-permute-start.12 = (bf16[256,128]{1,0:T(8,128)(2,1)S(1)}, bf16[256,128]{1,0:T(8,128)(2,1)S(1)}, u32[]{:S(2)}, u32[]{:S(2)}) collective-permute-start(bf16[256,128]{1,0:T(8,128)(2,1)S(1)} %get-tuple-element.21), channel_id=1, source_target_pairs={{0,16},{16,0},{1,17},{17,1},{2,18},{18,2},{3,19},{19,3},{4,20},{20... | collective-permute-start | bytes 196616 | tf_op jit(solution)/shard_map/ppermute | solution.py:149
  154.2 2.1 %collective-permute-start.14 = (bf16[256,128]{1,0:T(8,128)(2,1)S(1)}, bf16[256,128]{1,0:T(8,128)(2,1)S(1)}, u32[]{:S(2)}, u32[]{:S(2)}) collective-permute-start(bf16[256,128]{1,0:T(8,128)(2,1)S(1)} %get-tuple-element.21), channel_id=1, source_target_pairs={{0,80},{16,64},{64,16},{80,0},{1,81},{17,65},{65,17},{81,1},{2,82}... | collective-permute-start | bytes 196616 | tf_op jit(solution)/shard_map/ppermute | solution.py:207
  157.0 3.3 %collective-permute-done.12.refs_0_ = bf16[256,128]{1,0:T(8,128)(2,1)S(1)} collective-permute-done((bf16[256,128]{1,0:T(8,128)(2,1)S(1)}, bf16[256,128]{1,0:T(8,128)(2,1)S(1)}, u32[]{:S(2)}, u32[]{:S(2)}) %collective-permute-start.12) | collective-permute-done | bytes 65568 | tf_op jit(solution)/shard_map/ppermute | solution.py:149
  160.3 1.8 %collective-permute-done.13.refs_1_ = bf16[256,128]{1,0:T(8,128)(2,1)S(1)} collective-permute-done((bf16[256,128]{1,0:T(8,128)(2,1)S(1)}, bf16[256,128]{1,0:T(8,128)(2,1)S(1)}, u32[]{:S(2)}, u32[]{:S(2)}) %collective-permute-start.13) | collective-permute-done | bytes 65568 | tf_op jit(solution)/shard_map/ppermute | solution.py:149
  162.1 2.7 %all-to-all-done.2.second_ref = bf16[16,64,1024]{2,1,0:T(8,128)(2,1)} async-done(((bf16[16,64,1024]{2,1,0:T(8,128)(2,1)}), bf16[16,64,1024]{2,1,0:T(8,128)(2,1)}, u32[]{:S(2)}, u32[]{:S(2)}) %all-to-all-start.2) | async-done | bytes 2097184 | tf_op jit(solution)/shard_map/all_to_all | solution.py:192
  164.8 3.1 %finish.1 = (bf16[64,4096]{1,0:T(8,128)(2,1)}, bf16[64,4096]{1,0:T(8,128)(2,1)}, f32[256,128]{1,0:T(8,128)}, f32[256,128]{1,0:T(8,128)}) custom-call(s32[3]{0:T(128)S(1)} %pad_add_fusion.at_ref, bf16[16,64,1024]{2,1,0:T(8,128)(2,1)S(1)} %all-to-all-done.1.first_ref, bf16[16,64,1024]{2,1,0:T(8,128)(2,1)} %all-to-all-done.2.second_ref, ...), custom_call_target="tpu_custom_call" | custom-call | tf_op jit(solution)/shard_map/finish/pallas_call | solution.py:113
  (42 shorter events, 10.6 us)
Async XLA Ops:
  0.6 0.8 copy-start
  0.6 4.1 %copy-start.3 = (bf16[64,8192]{1,0:T(8,128)(2,1)S(1)}, bf16[64,8192]{1,0:T(8,128)(2,1)}, u32[]{:S(2)}) copy-start(bf16[64,8192]{1,0:T(8,128)(2,1)} %float_ref.1) | copy-start | bytes 3145732
  0.7 4.0 %copy-start.4 = (bf16[64,8192]{1,0:T(8,128)(2,1)S(1)}, bf16[64,8192]{1,0:T(8,128)(2,1)}, u32[]{:S(2)}) copy-start(bf16[64,8192]{1,0:T(8,128)(2,1)} %quant_ref.1) | copy-start | bytes 3145732
  3.0 9.3 %collective-permute-start = (bf16[256,1024]{1,0:T(8,128)(2,1)S(1)}, bf16[256,1024]{1,0:T(8,128)(2,1)S(1)}, u32[]{:S(2)}, u32[]{:S(2)}) collective-permute-start(bf16[256,1024]{1,0:T(8,128)(2,1)S(1)} %fusion.2), channel_id=1, source_target_pairs={{0,16},{16,0},{32,112},{48,96},{64,80},{80,64},{96,48},{112,32},{1... | collective-permute-start | bytes 1572872 | tf_op jit(solution)/shard_map/ppermute | solution.py:178
  5.0 2.1 %copy-start.1 = (bf16[16,64,2176]{2,1,0:T(8,128)(2,1)}, bf16[16,64,2176]{2,1,0:T(8,128)(2,1)S(1)}, u32[]{:S(2)}) copy-start(bf16[16,64,2176]{2,1,0:T(8,128)(2,1)S(1)} %pack.1) | copy-start | bytes 13369348
  12.2 0.8 copy-start.10
  13.0 74.0 %all-to-all-start = ((bf16[16,64,2176]{2,1,0:T(8,128)(2,1)}), bf16[16,64,2176]{2,1,0:T(8,128)(2,1)}, u32[]{:S(2)}, u32[]{:S(2)}) async-start(bf16[16,64,2176]{2,1,0:T(8,128)(2,1)} %copy-done.1), calls=%async_computation | async-start | bytes 8912896 | tf_op jit(solution)/shard_map/all_to_all | solution.py:185
  20.2 2.1 %copy-start.11 = (bf16[256,1024]{1,0:T(8,128)(2,1)S(1)}, bf16[256,1024]{1,0:T(8,128)(2,1)}, u32[]{:S(2)}) copy-start(bf16[256,1024]{1,0:T(8,128)(2,1)} %copy-done.10) | copy-start | bytes 1572868
  22.4 48.6 %collective-permute-start.1 = (bf16[512,1024]{1,0:T(8,128)(2,1)S(1)}, bf16[512,1024]{1,0:T(8,128)(2,1)S(1)}, u32[]{:S(2)}, u32[]{:S(2)}) collective-permute-start(bf16[512,1024]{1,0:T(8,128)(2,1)S(1)} %pad_maximum_fusion.refs_0_), channel_id=1, source_target_pairs={{4,0},{8,4},{12,8},{0,12},{5,1},{9,5},{13,9},{1,13},{6,2},{10,6},{... | collective-permute-start | bytes 3145736 | tf_op jit(solution)/shard_map/ppermute | solution.py:153
  26.5 44.5 %collective-permute-start.2 = (bf16[512,1024]{1,0:T(8,128)(2,1)S(1)}, bf16[512,1024]{1,0:T(8,128)(2,1)S(1)}, u32[]{:S(2)}, u32[]{:S(2)}) collective-permute-start(bf16[512,1024]{1,0:T(8,128)(2,1)S(1)} %pad_maximum_fusion.refs_0_), channel_id=1, source_target_pairs={{8,0},{12,4},{0,8},{4,12},{9,1},{13,5},{1,9},{5,13},{10,2},{14,6},... | collective-permute-start | bytes 3145736 | tf_op jit(solution)/shard_map/ppermute | solution.py:153
  26.5 47.9 %collective-permute-start.3 = (bf16[512,1024]{1,0:T(8,128)(2,1)S(1)}, bf16[512,1024]{1,0:T(8,128)(2,1)S(1)}, u32[]{:S(2)}, u32[]{:S(2)}) collective-permute-start(bf16[512,1024]{1,0:T(8,128)(2,1)S(1)} %pad_maximum_fusion.refs_0_), channel_id=1, source_target_pairs={{12,0},{0,4},{4,8},{8,12},{13,1},{1,5},{5,9},{9,13},{14,2},{2,6},{... | collective-permute-start | bytes 3145736 | tf_op jit(solution)/shard_map/ppermute | solution.py:153
  71.0 24.8 %copy-start.5 = (bf16[512,1024]{1,0:T(8,128)(2,1)}, bf16[512,1024]{1,0:T(8,128)(2,1)S(1)}, u32[]{:S(2)}) copy-start(bf16[512,1024]{1,0:T(8,128)(2,1)S(1)} %collective-permute-done.1.refs_1_) | copy-start | bytes 3145732
  71.0 1.0 copy-start.6
  74.4 1.0 copy-start.8
  87.0 1.2 copy-start.7
  88.2 1.2 copy-start.9
  95.7 1.4 copy-start.2
  97.1 33.8 %all-to-all-start.1 = ((bf16[16,64,1024]{2,1,0:T(8,128)(2,1)}), bf16[16,64,1024]{2,1,0:T(8,128)(2,1)S(1)}, u32[]{:S(2)}, u32[]{:S(2)}) async-start(bf16[16,64,1024]{2,1,0:T(8,128)(2,1)} %bitcast.19), calls=%async_computation.1 | async-start | bytes 4194304 | tf_op jit(solution)/shard_map/all_to_all | solution.py:192
  101.7 3.3 %collective-permute-start.4 = (bf16[512,1024]{1,0:T(8,128)(2,1)S(1)}, bf16[512,1024]{1,0:T(8,128)(2,1)S(1)}, u32[]{:S(2)}, u32[]{:S(2)}) collective-permute-start(bf16[512,1024]{1,0:T(8,128)(2,1)S(1)} %pad_maximum_fusion.refs_0_), channel_id=1, source_target_pairs={{0,32},{32,0},{1,33},{33,1},{2,34},{34,2},{3,35},{35,3},{4,36},{36... | collective-permute-start | bytes 3145736 | tf_op jit(solution)/shard_map/ppermute | solution.py:149
  101.8 4.4 %collective-permute-start.5 = (bf16[512,1024]{1,0:T(8,128)(2,1)}, bf16[512,1024]{1,0:T(8,128)(2,1)S(1)}, u32[]{:S(2)}, u32[]{:S(2)}) collective-permute-start(bf16[512,1024]{1,0:T(8,128)(2,1)} %copy-done.5), channel_id=1, source_target_pairs={{0,32},{32,0},{1,33},{33,1},{2,34},{34,2},{3,35},{35,3},{4,36},{36... | collective-permute-start | bytes 3145736 | tf_op jit(solution)/shard_map/ppermute | solution.py:149
  102.3 5.4 %collective-permute-start.6 = (bf16[512,1024]{1,0:T(8,128)(2,1)}, bf16[512,1024]{1,0:T(8,128)(2,1)S(1)}, u32[]{:S(2)}, u32[]{:S(2)}) collective-permute-start(bf16[512,1024]{1,0:T(8,128)(2,1)} %copy-done.6), channel_id=1, source_target_pairs={{0,32},{32,0},{1,33},{33,1},{2,34},{34,2},{3,35},{35,3},{4,36},{36... | collective-permute-start | bytes 3145736 | tf_op jit(solution)/shard_map/ppermute | solution.py:149
  102.4 6.8 %collective-permute-start.7 = (bf16[512,1024]{1,0:T(8,128)(2,1)}, bf16[512,1024]{1,0:T(8,128)(2,1)S(1)}, u32[]{:S(2)}, u32[]{:S(2)}) collective-permute-start(bf16[512,1024]{1,0:T(8,128)(2,1)} %copy-done.8), channel_id=1, source_target_pairs={{0,32},{32,0},{1,33},{33,1},{2,34},{34,2},{3,35},{35,3},{4,36},{36... | collective-permute-start | bytes 3145736 | tf_op jit(solution)/shard_map/ppermute | solution.py:149
  130.9 33.8 %all-to-all-start.2 = ((bf16[16,64,1024]{2,1,0:T(8,128)(2,1)}), bf16[16,64,1024]{2,1,0:T(8,128)(2,1)}, u32[]{:S(2)}, u32[]{:S(2)}) async-start(bf16[16,64,1024]{2,1,0:T(8,128)(2,1)} %bitcast.8), calls=%async_computation.2 | async-start | bytes 4194304 | tf_op jit(solution)/shard_map/all_to_all | solution.py:192
  138.9 8.3 %collective-permute-start.10 = (bf16[512,128]{1,0:T(8,128)(2,1)S(1)}, bf16[512,128]{1,0:T(8,128)(2,1)S(1)}, u32[]{:S(2)}, u32[]{:S(2)}) collective-permute-start(bf16[512,128]{1,0:T(8,128)(2,1)S(1)} %get-tuple-element.17), channel_id=1, source_target_pairs={{4,0},{8,4},{12,8},{0,12},{5,1},{9,5},{13,9},{1,13},{6,2},{10,6},{... | collective-permute-start | bytes 393224 | tf_op jit(solution)/shard_map/ppermute | solution.py:153
  143.1 6.6 %collective-permute-start.9 = (bf16[512,128]{1,0:T(8,128)(2,1)S(1)}, bf16[512,128]{1,0:T(8,128)(2,1)S(1)}, u32[]{:S(2)}, u32[]{:S(2)}) collective-permute-start(bf16[512,128]{1,0:T(8,128)(2,1)S(1)} %get-tuple-element.16), channel_id=1, source_target_pairs={{8,0},{12,4},{0,8},{4,12},{9,1},{13,5},{1,9},{5,13},{10,2},{14,6},... | collective-permute-start | bytes 393224 | tf_op jit(solution)/shard_map/ppermute | solution.py:153
  143.1 7.6 %collective-permute-start.8 = (bf16[512,128]{1,0:T(8,128)(2,1)S(1)}, bf16[512,128]{1,0:T(8,128)(2,1)S(1)}, u32[]{:S(2)}, u32[]{:S(2)}) collective-permute-start(bf16[512,128]{1,0:T(8,128)(2,1)S(1)} %get-tuple-element.15), channel_id=1, source_target_pairs={{12,0},{0,4},{4,8},{8,12},{13,1},{1,5},{5,9},{9,13},{14,2},{2,6},{... | collective-permute-start | bytes 393224 | tf_op jit(solution)/shard_map/ppermute | solution.py:153
  150.7 1.6 collective-permute-start.11
  152.4 8.0 %collective-permute-start.12 = (bf16[256,128]{1,0:T(8,128)(2,1)S(1)}, bf16[256,128]{1,0:T(8,128)(2,1)S(1)}, u32[]{:S(2)}, u32[]{:S(2)}) collective-permute-start(bf16[256,128]{1,0:T(8,128)(2,1)S(1)} %get-tuple-element.21), channel_id=1, source_target_pairs={{0,16},{16,0},{1,17},{17,1},{2,18},{18,2},{3,19},{19,3},{4,20},{20... | collective-permute-start | bytes 196616 | tf_op jit(solution)/shard_map/ppermute | solution.py:149
  154.2 7.9 %collective-permute-start.14 = (bf16[256,128]{1,0:T(8,128)(2,1)S(1)}, bf16[256,128]{1,0:T(8,128)(2,1)S(1)}, u32[]{:S(2)}, u32[]{:S(2)}) collective-permute-start(bf16[256,128]{1,0:T(8,128)(2,1)S(1)} %get-tuple-element.21), channel_id=1, source_target_pairs={{0,80},{16,64},{64,16},{80,0},{1,81},{17,65},{65,17},{81,1},{2,82}... | collective-permute-start | bytes 196616 | tf_op jit(solution)/shard_map/ppermute | solution.py:207
  156.3 5.8 %collective-permute-start.13 = (bf16[256,128]{1,0:T(8,128)(2,1)S(1)}, bf16[256,128]{1,0:T(8,128)(2,1)S(1)}, u32[]{:S(2)}, u32[]{:S(2)}) collective-permute-start(bf16[256,128]{1,0:T(8,128)(2,1)S(1)} %get-tuple-element.20), channel_id=1, source_target_pairs={{0,64},{64,0},{1,65},{65,1},{2,66},{66,2},{3,67},{67,3},{4,68},{68... | collective-permute-start | bytes 196616 | tf_op jit(solution)/shard_map/ppermute | solution.py:149

commit v16 on v15

--- a/solution.py
+++ b/solution.py
@@ -54,7 +54,7 @@
 
 
 def project_kernel(acts_ref, *refs):
-    *weights, out_ref = refs
+    weights, out_ref = refs[:4], refs[-1]
     depth, width = weights[0].shape
     tile = 512
     for col in range(0, width, tile):
@@ -69,21 +69,22 @@
         out_ref[:, col : col + tile] = total.astype(BF16)
 
 
-def project(acts, weights):
+def project(acts, weights, after):
     rows, cols = acts.shape[0], weights[0].shape[1]
     step = 256
     return pl.pallas_call(
         project_kernel,
         out_shape=jax.ShapeDtypeStruct((rows, cols), BF16),
         grid=(rows // step,),
-        in_specs=[pl.BlockSpec((step, acts.shape[1]), lambda i: (i, 0))] + [WHOLE] * len(weights),
+        in_specs=[pl.BlockSpec((step, acts.shape[1]), lambda i: (i, 0))] + [WHOLE] * len(weights)
+        + [LEFT] * len(after),
         out_specs=pl.BlockSpec((step, cols), lambda i: (i, 0)),
         compiler_params=params(),
         cost_estimate=pl.CostEstimate(
             flops=2 * rows * 2048 * cols, bytes_accessed=12 << 20, transcendentals=0
         ),
         name="project",
-    )(acts, *weights)
+    )(acts, *weights, *after)
 
 
 def finish_kernel(at_ref, first_ref, second_ref, total_ref, *refs):
@@ -180,25 +181,26 @@
     own = weight(yh, col)
 
     payload = pack(z, attn_float, attn_quant)
-    payload, got = lax.optimization_barrier((payload, got))
+    rows = jnp.concatenate([own, got], axis=0)
+    payload, rows = lax.optimization_barrier((payload, rows))
+    parts = [rows] + [ahead(rows, "z", j) for j in (1, 2, 3)]
 
     acts = lax.all_to_all(payload, PLANE, 0, 0, tiled=True).reshape(16 * tokens, -1)
-
-    rows = jnp.concatenate([own, got], axis=0)
-    parts = [rows] + [ahead(rows, "z", j) for j in (1, 2, 3)]
-    others = [swap(p, "core") for p in parts]
+    acts, *parts = lax.optimization_barrier((acts, *parts))
 
     def output(p):
         return lax.all_to_all(p.reshape(16, tokens, quarter), PLANE, 0, 0, tiled=True)
 
-    result1 = output(project(acts, parts))
-    second = project(acts, others)
-
-    blocks = stats(acts, second)
-    result2 = output(second)
+    first = project(acts, parts, ())
+    first, *parts = lax.optimization_barrier((first, *parts))
+    result1 = output(first)
+    others = [swap(p, "core") for p in parts]
+
+    blocks = stats(acts, first)
     total = blocks[0]
     for j in (1, 2, 3):
         total = total + ahead(blocks[j], "z", 4 - j).astype(F32)
+    second = project(acts, others, (total,))
     total = (total + swap(total, "core")) * inverse
     here, there = total[:features].astype(BF16), total[features:].astype(BF16)
     moved = (
@@ -206,6 +208,8 @@
         swap(here, "yh"),
         lax.ppermute(there, ("yh", "yl"), [(i, 3 - i) for i in range(4)]),
     )
+    second, total, *moved = lax.optimization_barrier((second, total, *moved))
+    result2 = output(second)
     return finish(jnp.stack([core, yh, yl]), result1, result2, total, moved)
 
 

time: 169 us -> 172 us (1.018)
  starting transfers between devices: 34.4 us -> 39.1 us
  local copies, waits for them, and re-layouts: 9.47 us -> 6.51 us
    all_to_all x2, waiting for transfers between devices: 17.1 us -> 30.3 us  [output(): lax.all_to_all(p.reshape(16, tokens, quarter), PLANE, 0, 0, tiled=True)]
    ppermute x7, waiting for transfers between devices: 12.9 us -> 3.39 us  [swap(): return lax.ppermute(a, axis, [(0, 1), (1, 0)])]
    ppermute x6, waiting for transfers between devices: 52 us -> 47.4 us  [ahead(): return lax.ppermute(a, axis, [((i + j) % 4, i) for i in range(4)])]
    all_to_all x1, waiting for transfers between devices: 11.6 us -> 15.3 us  [shards(): lax.all_to_all(payload, PLANE, 0, 0, tiled=True).reshape(16 * tokens, -1)]
    unnamed x24, local copies, waits for them, and re-layouts: 9.38 us -> 6.42 us
    all_to_all x2, starting transfers between devices: 9.04 us -> 11.6 us  [output(): lax.all_to_all(p.reshape(16, tokens, quarter), PLANE, 0, 0, tiled=True)]
    ppermute x6, starting transfers between devices: 10.7 us -> 13.2 us  [ahead(): return lax.ppermute(a, axis, [((i + j) % 4, i) for i in range(4)])]
    ppermute x1, waiting for transfers between devices: 5.12 us -> 3.18 us  [shards(): got = lax.ppermute(send, ('yh', 'core', 'yl'), pairs)]
  transfers between devices with their start and end apart: 18 -> 18, of which waited for: 16 -> 9; matrix products, arithmetic and copies ran while one was open for 1% -> 1% of each run, Pallas kernels for 7% -> 6%
where the time goes in v16:
time: 172 us
  waiting for transfers between devices  99.5 us (58%)
  starting transfers between devices  39.1 us (23%)
  Pallas kernels  20.7 us (12%)
  local copies, waits for them, and re-layouts  6.51 us (4%)
  other arithmetic  4.96 us (3%)
    ppermute x6, waiting for transfers between devices, ahead(): return lax.ppermute(a, axis, [((i + j) % 4, i) for i in range(4)])  47.4 us
    all_to_all x2, waiting for transfers between devices, output(): lax.all_to_all(p.reshape(16, tokens, quarter), PLANE, 0, 0, tiled=True)  30.3 us
    all_to_all x1, waiting for transfers between devices, shards(): lax.all_to_all(payload, PLANE, 0, 0, tiled=True).reshape(16 * tokens, -1)  15.3 us
    pallas_call x2, Pallas kernels, project(): pl.pallas_call(project_kernel, out_shape=jax.ShapeDtypeStruct((rows, cols...  13.6 us
    ppermute x6, starting transfers between devices, ahead(): return lax.ppermute(a, axis, [((i + j) % 4, i) for i in range(4)])  13.2 us
    all_to_all x2, starting transfers between devices, output(): lax.all_to_all(p.reshape(16, tokens, quarter), PLANE, 0, 0, tiled=True)  11.6 us
    all_to_all x1, starting transfers between devices, shards(): lax.all_to_all(payload, PLANE, 0, 0, tiled=True).reshape(16 * tokens, -1)  7.17 us
    unnamed x24, local copies, waits for them, and re-layouts  6.42 us
  transfers between devices with their start and end apart: 18, of which 9 were waited for; matrix products, arithmetic and copies ran while one was open for 1% of the time, Pallas kernels for 6%

profile of v16, /device:TPU:0, one launch (start us, length us, event | category | flops | bytes accessed | tf_op | source)
XLA Modules:
  0.0 171.6 jit_solution(16100998928144416914)
XLA Ops:
  0.7 0.7 copy-done
  1.4 1.7 fusion.2
  3.1 1.7 %collective-permute-start = (bf16[256,1024]{1,0:T(8,128)(2,1)S(1)}, bf16[256,1024]{1,0:T(8,128)(2,1)}, u32[]{:S(2)}, u32[]{:S(2)}) collective-permute-start(bf16[256,1024]{1,0:T(8,128)(2,1)S(1)} %fusion.2), channel_id=1, source_target_pairs={{0,16},{16,0},{32,112},{48,96},{64,80},{80,64},{96,48},{112,32},{1... | collective-permute-start | bytes 1572872 | tf_op jit(solution)/shard_map/ppermute | solution.py:179
  4.9 1.9 %fusion.3 = bf16[256,1024]{1,0:T(8,128)(2,1)S(1)} fusion(s32[256,4096]{1,0:T(8,128)} %param.8, s32[]{:T(128)S(6)} %select_n.28, f32[2,1024]{1,0:T(2,128)S(1)} %constant_dynamic-slice_fusion, bf16[256,4096]{1,0:T(8,128)(2,1)} %param.7, pred[]{:T(512)S(6)} %eq.6), kind=kLoop, calls=%fused_computation.6 | loop fusion | flops 1310720 | bytes 2105349 | tf_op jit(solution)/shard_map/jit(_where)/select_n | solution.py:171
  7.2 2.1 %copy-done.1 = bf16[16,64,2176]{2,1,0:T(8,128)(2,1)} copy-done((bf16[16,64,2176]{2,1,0:T(8,128)(2,1)}, bf16[16,64,2176]{2,1,0:T(8,128)(2,1)S(1)}, u32[]{:S(2)}) %copy-start.1) | copy-done | bytes 4456472
  9.3 3.2 %collective-permute-done = bf16[256,1024]{1,0:T(8,128)(2,1)} collective-permute-done((bf16[256,1024]{1,0:T(8,128)(2,1)S(1)}, bf16[256,1024]{1,0:T(8,128)(2,1)}, u32[]{:S(2)}, u32[]{:S(2)}) %collective-permute-start) | collective-permute-done | bytes 524320 | tf_op jit(solution)/shard_map/ppermute | solution.py:179
  12.5 1.1 pad_maximum_fusion.refs_0_
  13.6 7.2 %all-to-all-start = ((bf16[16,64,2176]{2,1,0:T(8,128)(2,1)}), bf16[16,64,2176]{2,1,0:T(8,128)(2,1)}, u32[]{:S(2)}, u32[]{:S(2)}) async-start(bf16[16,64,2176]{2,1,0:T(8,128)(2,1)} %copy-done.1), calls=%async_computation | async-start | bytes 8912896 | tf_op jit(solution)/shard_map/all_to_all | solution.py:188
  20.8 2.0 %collective-permute-start.3 = (bf16[512,1024]{1,0:T(8,128)(2,1)S(1)}, bf16[512,1024]{1,0:T(8,128)(2,1)S(1)}, u32[]{:S(2)}, u32[]{:S(2)}) collective-permute-start(bf16[512,1024]{1,0:T(8,128)(2,1)S(1)} %pad_maximum_fusion.refs_0_), channel_id=1, source_target_pairs={{12,0},{0,4},{4,8},{8,12},{13,1},{1,5},{5,9},{9,13},{14,2},{2,6},{... | collective-permute-start | bytes 3145736 | tf_op jit(solution)/shard_map/ppermute | solution.py:154
  22.8 3.6 %collective-permute-start.2 = (bf16[512,1024]{1,0:T(8,128)(2,1)S(1)}, bf16[512,1024]{1,0:T(8,128)(2,1)S(1)}, u32[]{:S(2)}, u32[]{:S(2)}) collective-permute-start(bf16[512,1024]{1,0:T(8,128)(2,1)S(1)} %pad_maximum_fusion.refs_0_), channel_id=1, source_target_pairs={{8,0},{12,4},{0,8},{4,12},{9,1},{13,5},{1,9},{5,13},{10,2},{14,6},... | collective-permute-start | bytes 3145736 | tf_op jit(solution)/shard_map/ppermute | solution.py:154
  26.3 1.0 collective-permute-start.1
  27.4 20.7 %collective-permute-done.3.refs_3_ = bf16[512,1024]{1,0:T(8,128)(2,1)S(1)} collective-permute-done((bf16[512,1024]{1,0:T(8,128)(2,1)S(1)}, bf16[512,1024]{1,0:T(8,128)(2,1)S(1)}, u32[]{:S(2)}, u32[]{:S(2)}) %collective-permute-start.3) | collective-permute-done | bytes 1048608 | tf_op jit(solution)/shard_map/ppermute | solution.py:154
  48.1 23.2 %collective-permute-done.2.refs_2_ = bf16[512,1024]{1,0:T(8,128)(2,1)S(1)} collective-permute-done((bf16[512,1024]{1,0:T(8,128)(2,1)S(1)}, bf16[512,1024]{1,0:T(8,128)(2,1)S(1)}, u32[]{:S(2)}, u32[]{:S(2)}) %collective-permute-start.2) | collective-permute-done | bytes 1048608 | tf_op jit(solution)/shard_map/ppermute | solution.py:154
  71.3 1.0 copy-done.9
  72.3 15.3 %all-to-all-done = bf16[16,64,2176]{2,1,0:T(8,128)(2,1)} async-done(((bf16[16,64,2176]{2,1,0:T(8,128)(2,1)}), bf16[16,64,2176]{2,1,0:T(8,128)(2,1)}, u32[]{:S(2)}, u32[]{:S(2)}) %all-to-all-start) | async-done | bytes 4456480 | tf_op jit(solution)/shard_map/all_to_all | solution.py:188
  87.6 1.2 copy-done.10
  88.8 7.3 %project.2.after_ref = bf16[1024,1024]{1,0:T(8,128)(2,1)} custom-call(bf16[1024,2176]{1,0:T(8,128)(2,1)} %bitcast.6.acts_ref, bf16[512,1024]{1,0:T(8,128)(2,1)S(1)} %pad_maximum_fusion.refs_0_, bf16[512,1024]{1,0:T(8,128)(2,1)S(1)} %copy-done.10, bf16[512,1024]{1,0:T(8,128)(2,1)S(1)} %collective-permute-done.2.refs_2_, ...), custom_call_target="tpu_custom_call" | custom-call | flops 4294967296 | bytes 12582912 | tf_op jit(solution)/shard_map/project/pallas_call | solution.py:75
  96.1 4.6 %all-to-all-start.1 = ((bf16[16,64,1024]{2,1,0:T(8,128)(2,1)}), bf16[16,64,1024]{2,1,0:T(8,128)(2,1)S(1)}, u32[]{:S(2)}, u32[]{:S(2)}) async-start(bf16[16,64,1024]{2,1,0:T(8,128)(2,1)} %bitcast.7), calls=%async_computation.1 | async-start | bytes 4194304 | tf_op jit(solution)/shard_map/all_to_all | solution.py:192
  100.7 3.7 %stats.1 = (f32[512,128]{1,0:T(8,128)S(1)}, bf16[512,128]{1,0:T(8,128)(2,1)S(1)}, bf16[512,128]{1,0:T(8,128)(2,1)S(1)}, bf16[512,128]{1,0:T(8,128)(2,1)S(1)}) custom-call(bf16[1024,2176]{1,0:T(8,128)(2,1)} %bitcast.6.acts_ref, bf16[1024,1024]{1,0:T(8,128)(2,1)} %project.2.after_ref), custom_call_target="tpu_custom_call" | custom-call | tf_op jit(solution)/shard_map/stats/pallas_call | solution.py:138
  104.5 2.0 %collective-permute-start.8 = (bf16[512,128]{1,0:T(8,128)(2,1)S(1)}, bf16[512,128]{1,0:T(8,128)(2,1)S(1)}, u32[]{:S(2)}, u32[]{:S(2)}) collective-permute-start(bf16[512,128]{1,0:T(8,128)(2,1)S(1)} %get-tuple-element.40), channel_id=1, source_target_pairs={{12,0},{0,4},{4,8},{8,12},{13,1},{1,5},{5,9},{9,13},{14,2},{2,6},{... | collective-permute-start | bytes 393224 | tf_op jit(solution)/shard_map/ppermute | solution.py:154
  106.4 3.6 %collective-permute-start.9 = (bf16[512,128]{1,0:T(8,128)(2,1)S(1)}, bf16[512,128]{1,0:T(8,128)(2,1)S(1)}, u32[]{:S(2)}, u32[]{:S(2)}) collective-permute-start(bf16[512,128]{1,0:T(8,128)(2,1)S(1)} %get-tuple-element.41), channel_id=1, source_target_pairs={{8,0},{12,4},{0,8},{4,12},{9,1},{13,5},{1,9},{5,13},{10,2},{14,6},... | collective-permute-start | bytes 393224 | tf_op jit(solution)/shard_map/ppermute | solution.py:154
  110.0 1.0 collective-permute-start.10
  111.5 1.4 collective-permute-done.8
  112.9 1.6 collective-permute-done.9
  115.2 3.4 %collective-permute-done.11 = f32[512,128]{1,0:T(8,128)S(1)} collective-permute-done((f32[512,128]{1,0:T(8,128)S(1)}, f32[512,128]{1,0:T(8,128)S(1)}, u32[]{:S(2)}, u32[]{:S(2)}) %collective-permute-start.11) | collective-permute-done | bytes 262176 | tf_op jit(solution)/shard_map/ppermute | solution.py:150
  118.6 3.2 %collective-permute-start.14 = (bf16[256,128]{1,0:T(8,128)(2,1)S(1)}, bf16[256,128]{1,0:T(8,128)(2,1)S(1)}, u32[]{:S(2)}, u32[]{:S(2)}) collective-permute-start(bf16[256,128]{1,0:T(8,128)(2,1)S(1)} %get-tuple-element.51), channel_id=1, source_target_pairs={{0,80},{16,64},{64,16},{80,0},{1,81},{17,65},{65,17},{81,1},{2,82}... | collective-permute-start | bytes 196616 | tf_op jit(solution)/shard_map/ppermute | solution.py:209
  122.1 1.3 collective-permute-start.13
  123.4 6.3 %project.3 = bf16[1024,1024]{1,0:T(8,128)(2,1)S(1)} custom-call(bf16[1024,2176]{1,0:T(8,128)(2,1)} %bitcast.6.acts_ref, bf16[512,1024]{1,0:T(8,128)(2,1)S(1)} %collective-permute-done.4.refs_0_, bf16[512,1024]{1,0:T(8,128)(2,1)S(1)} %collective-permute-done.5.refs_1_, bf16[512,1024]{1,0:T(8,128)(2,1)S(1)} %collective-permute-done.6.refs_2_, ...), custom_call_target="tpu_custom_call" | custom-call | flops 4294967296 | bytes 12582912 | tf_op jit(solution)/shard_map/project/pallas_call | solution.py:75
  129.8 1.3 copy-done.2
  131.1 7.0 %all-to-all-start.2 = ((bf16[16,64,1024]{2,1,0:T(8,128)(2,1)}), bf16[16,64,1024]{2,1,0:T(8,128)(2,1)}, u32[]{:S(2)}, u32[]{:S(2)}) async-start(bf16[16,64,1024]{2,1,0:T(8,128)(2,1)} %bitcast.19), calls=%async_computation.2 | async-start | bytes 4194304 | tf_op jit(solution)/shard_map/all_to_all | solution.py:192
  138.2 30.3 %all-to-all-done.2.second_ref = bf16[16,64,1024]{2,1,0:T(8,128)(2,1)} async-done(((bf16[16,64,1024]{2,1,0:T(8,128)(2,1)}), bf16[16,64,1024]{2,1,0:T(8,128)(2,1)}, u32[]{:S(2)}, u32[]{:S(2)}) %all-to-all-start.2) | async-done | bytes 2097184 | tf_op jit(solution)/shard_map/all_to_all | solution.py:192
  168.5 3.1 %finish.1 = (bf16[64,4096]{1,0:T(8,128)(2,1)}, bf16[64,4096]{1,0:T(8,128)(2,1)}, f32[256,128]{1,0:T(8,128)}, f32[256,128]{1,0:T(8,128)}) custom-call(s32[3]{0:T(128)S(1)} %pad_add_fusion.at_ref, bf16[16,64,1024]{2,1,0:T(8,128)(2,1)S(1)} %all-to-all-done.1.first_ref, bf16[16,64,1024]{2,1,0:T(8,128)(2,1)} %all-to-all-done.2.second_ref, ...), custom_call_target="tpu_custom_call" | custom-call | tf_op jit(solution)/shard_map/finish/pallas_call | solution.py:114
  (42 shorter events, 2.0 us)
Async XLA Ops:
  0.6 0.8 copy-start
  1.4 5.5 %copy-start.3 = (bf16[64,8192]{1,0:T(8,128)(2,1)S(1)}, bf16[64,8192]{1,0:T(8,128)(2,1)}, u32[]{:S(2)}) copy-start(bf16[64,8192]{1,0:T(8,128)(2,1)} %float_ref.1) | copy-start | bytes 3145732
  1.4 5.5 %copy-start.4 = (bf16[64,8192]{1,0:T(8,128)(2,1)S(1)}, bf16[64,8192]{1,0:T(8,128)(2,1)}, u32[]{:S(2)}) copy-start(bf16[64,8192]{1,0:T(8,128)(2,1)} %quant_ref.1) | copy-start | bytes 3145732
  3.1 9.4 %collective-permute-start = (bf16[256,1024]{1,0:T(8,128)(2,1)S(1)}, bf16[256,1024]{1,0:T(8,128)(2,1)}, u32[]{:S(2)}, u32[]{:S(2)}) collective-permute-start(bf16[256,1024]{1,0:T(8,128)(2,1)S(1)} %fusion.2), channel_id=1, source_target_pairs={{0,16},{16,0},{32,112},{48,96},{64,80},{80,64},{96,48},{112,32},{1... | collective-permute-start | bytes 1572872 | tf_op jit(solution)/shard_map/ppermute | solution.py:179
  7.2 2.1 %copy-start.1 = (bf16[16,64,2176]{2,1,0:T(8,128)(2,1)}, bf16[16,64,2176]{2,1,0:T(8,128)(2,1)S(1)}, u32[]{:S(2)}) copy-start(bf16[16,64,2176]{2,1,0:T(8,128)(2,1)S(1)} %pack.1) | copy-start | bytes 13369348
  13.6 74.0 %all-to-all-start = ((bf16[16,64,2176]{2,1,0:T(8,128)(2,1)}), bf16[16,64,2176]{2,1,0:T(8,128)(2,1)}, u32[]{:S(2)}, u32[]{:S(2)}) async-start(bf16[16,64,2176]{2,1,0:T(8,128)(2,1)} %copy-done.1), calls=%async_computation | async-start | bytes 8912896 | tf_op jit(solution)/shard_map/all_to_all | solution.py:188
  20.8 27.3 %collective-permute-start.3 = (bf16[512,1024]{1,0:T(8,128)(2,1)S(1)}, bf16[512,1024]{1,0:T(8,128)(2,1)S(1)}, u32[]{:S(2)}, u32[]{:S(2)}) collective-permute-start(bf16[512,1024]{1,0:T(8,128)(2,1)S(1)} %pad_maximum_fusion.refs_0_), channel_id=1, source_target_pairs={{12,0},{0,4},{4,8},{8,12},{13,1},{1,5},{5,9},{9,13},{14,2},{2,6},{... | collective-permute-start | bytes 3145736 | tf_op jit(solution)/shard_map/ppermute | solution.py:154
  22.8 48.5 %collective-permute-start.2 = (bf16[512,1024]{1,0:T(8,128)(2,1)S(1)}, bf16[512,1024]{1,0:T(8,128)(2,1)S(1)}, u32[]{:S(2)}, u32[]{:S(2)}) collective-permute-start(bf16[512,1024]{1,0:T(8,128)(2,1)S(1)} %pad_maximum_fusion.refs_0_), channel_id=1, source_target_pairs={{8,0},{12,4},{0,8},{4,12},{9,1},{13,5},{1,9},{5,13},{10,2},{14,6},... | collective-permute-start | bytes 3145736 | tf_op jit(solution)/shard_map/ppermute | solution.py:154
  26.3 44.9 %collective-permute-start.1 = (bf16[512,1024]{1,0:T(8,128)(2,1)S(1)}, bf16[512,1024]{1,0:T(8,128)(2,1)S(1)}, u32[]{:S(2)}, u32[]{:S(2)}) collective-permute-start(bf16[512,1024]{1,0:T(8,128)(2,1)S(1)} %pad_maximum_fusion.refs_0_), channel_id=1, source_target_pairs={{4,0},{8,4},{12,8},{0,12},{5,1},{9,5},{13,9},{1,13},{6,2},{10,6},{... | collective-permute-start | bytes 3145736 | tf_op jit(solution)/shard_map/ppermute | solution.py:154
  48.1 48.0 %copy-start.5 = (bf16[512,1024]{1,0:T(8,128)(2,1)}, bf16[512,1024]{1,0:T(8,128)(2,1)S(1)}, u32[]{:S(2)}) copy-start(bf16[512,1024]{1,0:T(8,128)(2,1)S(1)} %collective-permute-done.3.refs_3_) | copy-start | bytes 3145732
  71.3 24.8 %copy-start.7 = (bf16[512,1024]{1,0:T(8,128)(2,1)}, bf16[512,1024]{1,0:T(8,128)(2,1)S(1)}, u32[]{:S(2)}) copy-start(bf16[512,1024]{1,0:T(8,128)(2,1)S(1)} %collective-permute-done.2.refs_2_) | copy-start | bytes 3145732
  71.3 1.0 copy-start.9
  87.6 1.2 copy-start.10
  96.1 35.0 %all-to-all-start.1 = ((bf16[16,64,1024]{2,1,0:T(8,128)(2,1)}), bf16[16,64,1024]{2,1,0:T(8,128)(2,1)S(1)}, u32[]{:S(2)}, u32[]{:S(2)}) async-start(bf16[16,64,1024]{2,1,0:T(8,128)(2,1)} %bitcast.7), calls=%async_computation.1 | async-start | bytes 4194304 | tf_op jit(solution)/shard_map/all_to_all | solution.py:192
  100.7 10.3 %copy-start.11 = (bf16[512,1024]{1,0:T(8,128)(2,1)S(1)}, bf16[512,1024]{1,0:T(8,128)(2,1)}, u32[]{:S(2)}) copy-start(bf16[512,1024]{1,0:T(8,128)(2,1)} %copy-done.9) | copy-start | bytes 3145732
  100.7 12.2 %copy-start.8 = (bf16[512,1024]{1,0:T(8,128)(2,1)S(1)}, bf16[512,1024]{1,0:T(8,128)(2,1)}, u32[]{:S(2)}) copy-start(bf16[512,1024]{1,0:T(8,128)(2,1)} %copy-done.7) | copy-start | bytes 3145732
  100.7 13.8 %copy-start.6 = (bf16[512,1024]{1,0:T(8,128)(2,1)S(1)}, bf16[512,1024]{1,0:T(8,128)(2,1)}, u32[]{:S(2)}) copy-start(bf16[512,1024]{1,0:T(8,128)(2,1)} %copy-done.5) | copy-start | bytes 3145732
  104.5 8.5 %collective-permute-start.8 = (bf16[512,128]{1,0:T(8,128)(2,1)S(1)}, bf16[512,128]{1,0:T(8,128)(2,1)S(1)}, u32[]{:S(2)}, u32[]{:S(2)}) collective-permute-start(bf16[512,128]{1,0:T(8,128)(2,1)S(1)} %get-tuple-element.40), channel_id=1, source_target_pairs={{12,0},{0,4},{4,8},{8,12},{13,1},{1,5},{5,9},{9,13},{14,2},{2,6},{... | collective-permute-start | bytes 393224 | tf_op jit(solution)/shard_map/ppermute | solution.py:154
  106.4 8.1 %collective-permute-start.9 = (bf16[512,128]{1,0:T(8,128)(2,1)S(1)}, bf16[512,128]{1,0:T(8,128)(2,1)S(1)}, u32[]{:S(2)}, u32[]{:S(2)}) collective-permute-start(bf16[512,128]{1,0:T(8,128)(2,1)S(1)} %get-tuple-element.41), channel_id=1, source_target_pairs={{8,0},{12,4},{0,8},{4,12},{9,1},{13,5},{1,9},{5,13},{10,2},{14,6},... | collective-permute-start | bytes 393224 | tf_op jit(solution)/shard_map/ppermute | solution.py:154
  110.0 5.0 %collective-permute-start.10 = (bf16[512,128]{1,0:T(8,128)(2,1)S(1)}, bf16[512,128]{1,0:T(8,128)(2,1)S(1)}, u32[]{:S(2)}, u32[]{:S(2)}) collective-permute-start(bf16[512,128]{1,0:T(8,128)(2,1)S(1)} %get-tuple-element.42), channel_id=1, source_target_pairs={{4,0},{8,4},{12,8},{0,12},{5,1},{9,5},{13,9},{1,13},{6,2},{10,6},{... | collective-permute-start | bytes 393224 | tf_op jit(solution)/shard_map/ppermute | solution.py:154
  111.0 10.8 %collective-permute-start.4 = (bf16[512,1024]{1,0:T(8,128)(2,1)S(1)}, bf16[512,1024]{1,0:T(8,128)(2,1)S(1)}, u32[]{:S(2)}, u32[]{:S(2)}) collective-permute-start(bf16[512,1024]{1,0:T(8,128)(2,1)S(1)} %pad_maximum_fusion.refs_0_), channel_id=1, source_target_pairs={{0,32},{32,0},{1,33},{33,1},{2,34},{34,2},{3,35},{35,3},{4,36},{36... | collective-permute-start | bytes 3145736 | tf_op jit(solution)/shard_map/ppermute | solution.py:150
  111.0 11.1 %collective-permute-start.5 = (bf16[512,1024]{1,0:T(8,128)(2,1)S(1)}, bf16[512,1024]{1,0:T(8,128)(2,1)S(1)}, u32[]{:S(2)}, u32[]{:S(2)}) collective-permute-start(bf16[512,1024]{1,0:T(8,128)(2,1)S(1)} %copy-done.11), channel_id=1, source_target_pairs={{0,32},{32,0},{1,33},{33,1},{2,34},{34,2},{3,35},{35,3},{4,36},{36... | collective-permute-start | bytes 3145736 | tf_op jit(solution)/shard_map/ppermute | solution.py:150
  112.9 10.5 %collective-permute-start.6 = (bf16[512,1024]{1,0:T(8,128)(2,1)S(1)}, bf16[512,1024]{1,0:T(8,128)(2,1)S(1)}, u32[]{:S(2)}, u32[]{:S(2)}) collective-permute-start(bf16[512,1024]{1,0:T(8,128)(2,1)S(1)} %copy-done.8), channel_id=1, source_target_pairs={{0,32},{32,0},{1,33},{33,1},{2,34},{34,2},{3,35},{35,3},{4,36},{36... | collective-permute-start | bytes 3145736 | tf_op jit(solution)/shard_map/ppermute | solution.py:150
  114.5 8.9 %collective-permute-start.7 = (bf16[512,1024]{1,0:T(8,128)(2,1)S(1)}, bf16[512,1024]{1,0:T(8,128)(2,1)S(1)}, u32[]{:S(2)}, u32[]{:S(2)}) collective-permute-start(bf16[512,1024]{1,0:T(8,128)(2,1)S(1)} %copy-done.6), channel_id=1, source_target_pairs={{0,32},{32,0},{1,33},{33,1},{2,34},{34,2},{3,35},{35,3},{4,36},{36... | collective-permute-start | bytes 3145736 | tf_op jit(solution)/shard_map/ppermute | solution.py:150
  115.1 3.5 %collective-permute-start.11 = (f32[512,128]{1,0:T(8,128)S(1)}, f32[512,128]{1,0:T(8,128)S(1)}, u32[]{:S(2)}, u32[]{:S(2)}) collective-permute-start(f32[512,128]{1,0:T(8,128)S(1)} %convert_add_fusion.refs_4_), channel_id=1, source_target_pairs={{0,32},{32,0},{1,33},{33,1},{2,34},{34,2},{3,35},{35,3},{4,36},{36... | collective-permute-start | bytes 786440 | tf_op jit(solution)/shard_map/ppermute | solution.py:150
  118.6 12.4 %collective-permute-start.14 = (bf16[256,128]{1,0:T(8,128)(2,1)S(1)}, bf16[256,128]{1,0:T(8,128)(2,1)S(1)}, u32[]{:S(2)}, u32[]{:S(2)}) collective-permute-start(bf16[256,128]{1,0:T(8,128)(2,1)S(1)} %get-tuple-element.51), channel_id=1, source_target_pairs={{0,80},{16,64},{64,16},{80,0},{1,81},{17,65},{65,17},{81,1},{2,82}... | collective-permute-start | bytes 196616 | tf_op jit(solution)/shard_map/ppermute | solution.py:209
  121.9 9.2 %collective-permute-start.12 = (bf16[256,128]{1,0:T(8,128)(2,1)S(1)}, bf16[256,128]{1,0:T(8,128)(2,1)S(1)}, u32[]{:S(2)}, u32[]{:S(2)}) collective-permute-start(bf16[256,128]{1,0:T(8,128)(2,1)S(1)} %get-tuple-element.51), channel_id=1, source_target_pairs={{0,16},{16,0},{1,17},{17,1},{2,18},{18,2},{3,19},{19,3},{4,20},{20... | collective-permute-start | bytes 196616 | tf_op jit(solution)/shard_map/ppermute | solution.py:150
  122.1 9.0 %collective-permute-start.13 = (bf16[256,128]{1,0:T(8,128)(2,1)S(1)}, bf16[256,128]{1,0:T(8,128)(2,1)S(1)}, u32[]{:S(2)}, u32[]{:S(2)}) collective-permute-start(bf16[256,128]{1,0:T(8,128)(2,1)S(1)} %get-tuple-element.50), channel_id=1, source_target_pairs={{0,64},{64,0},{1,65},{65,1},{2,66},{66,2},{3,67},{67,3},{4,68},{68... | collective-permute-start | bytes 196616 | tf_op jit(solution)/shard_map/ppermute | solution.py:150
  129.7 1.3 copy-start.2
  131.1 37.4 %all-to-all-start.2 = ((bf16[16,64,1024]{2,1,0:T(8,128)(2,1)}), bf16[16,64,1024]{2,1,0:T(8,128)(2,1)}, u32[]{:S(2)}, u32[]{:S(2)}) async-start(bf16[16,64,1024]{2,1,0:T(8,128)(2,1)} %bitcast.19), calls=%async_computation.2 | async-start | bytes 4194304 | tf_op jit(solution)/shard_map/all_to_all | solution.py:192

commit v17 on v16

--- a/solution.py
+++ b/solution.py
@@ -19,7 +19,7 @@
 
 
 def params():
-    return pltpu.CompilerParams(vmem_limit_bytes=16 << 20)
+    return pltpu.CompilerParams(vmem_limit_bytes=6 << 20)
 
 
 def pack_kernel(z_ref, float_ref, quant_ref, out_ref):
@@ -181,20 +181,18 @@
     own = weight(yh, col)
 
     payload = pack(z, attn_float, attn_quant)
+    payload, got = lax.optimization_barrier((payload, got))
     rows = jnp.concatenate([own, got], axis=0)
-    payload, rows = lax.optimization_barrier((payload, rows))
     parts = [rows] + [ahead(rows, "z", j) for j in (1, 2, 3)]
 
     acts = lax.all_to_all(payload, PLANE, 0, 0, tiled=True).reshape(16 * tokens, -1)
-    acts, *parts = lax.optimization_barrier((acts, *parts))
+    others = [swap(p, "core") for p in parts]
 
     def output(p):
         return lax.all_to_all(p.reshape(16, tokens, quarter), PLANE, 0, 0, tiled=True)
 
     first = project(acts, parts, ())
-    first, *parts = lax.optimization_barrier((first, *parts))
     result1 = output(first)
-    others = [swap(p, "core") for p in parts]
 
     blocks = stats(acts, first)
     total = blocks[0]
@@ -208,9 +206,10 @@
         swap(here, "yh"),
         lax.ppermute(there, ("yh", "yl"), [(i, 3 - i) for i in range(4)]),
     )
-    second, total, *moved = lax.optimization_barrier((second, total, *moved))
+    at = jnp.stack([core, yh, yl])
+    at, second, total, *moved = lax.optimization_barrier((at, second, total, *moved))
     result2 = output(second)
-    return finish(jnp.stack([core, yh, yl]), result1, result2, total, moved)
+    return finish(at, result1, result2, total, moved)
 
 
 def solution(mesh):

time: 172 us -> 168 us (0.977)
  blocking collectives: 0 us -> 34.9 us
  waiting for transfers between devices: 99.5 us -> 68.9 us
  starting transfers between devices: 39.1 us -> 32.1 us
    all_to_all x0 -> x1, blocking collectives: none -> 34.9 us  [output(): lax.all_to_all(p.reshape(16, tokens, quarter), PLANE, 0, 0, tiled=True)]
    all_to_all x2 -> x1, waiting for transfers between devices: 30.3 us -> 0.01 us  [output(): lax.all_to_all(p.reshape(16, tokens, quarter), PLANE, 0, 0, tiled=True)]
    all_to_all x2 -> x1, starting transfers between devices: 11.6 us -> 4.6 us  [output(): lax.all_to_all(p.reshape(16, tokens, quarter), PLANE, 0, 0, tiled=True)]
    ppermute x1, waiting for transfers between devices: 3.18 us -> 5.12 us  [shards(): got = lax.ppermute(send, ('yh', 'core', 'yl'), pairs)]
    unnamed x24 -> x28, local copies, waits for them, and re-layouts: 6.42 us -> 7.15 us
  transfers between devices with their start and end apart: 18 -> 17, of which waited for: 9 -> 8; matrix products, arithmetic and copies ran while one was open for 1% -> 1% of each run, Pallas kernels for 6% -> 6%
where the time goes in v17:
time: 168 us
  waiting for transfers between devices  68.9 us (41%)
  blocking collectives  34.9 us (21%)
  starting transfers between devices  32.1 us (19%)
  Pallas kernels  19.8 us (12%)
  local copies, waits for them, and re-layouts  7.24 us (4%)
  other arithmetic  3.78 us (2%)
    ppermute x6, waiting for transfers between devices, ahead(): return lax.ppermute(a, axis, [((i + j) % 4, i) for i in range(4)])  46.4 us
    all_to_all x1, blocking collectives, output(): lax.all_to_all(p.reshape(16, tokens, quarter), PLANE, 0, 0, tiled=True)  34.9 us
    all_to_all x1, waiting for transfers between devices, shards(): lax.all_to_all(payload, PLANE, 0, 0, tiled=True).reshape(16 * tokens, -1)  14.1 us
    pallas_call x2, Pallas kernels, project(): pl.pallas_call(project_kernel, out_shape=jax.ShapeDtypeStruct((rows, cols...  13.7 us
    ppermute x6, starting transfers between devices, ahead(): return lax.ppermute(a, axis, [((i + j) % 4, i) for i in range(4)])  13.2 us
    all_to_all x1, starting transfers between devices, shards(): lax.all_to_all(payload, PLANE, 0, 0, tiled=True).reshape(16 * tokens, -1)  7.16 us
    unnamed x28, local copies, waits for them, and re-layouts  7.15 us
    ppermute x1, waiting for transfers between devices, shards(): got = lax.ppermute(send, ('yh', 'core', 'yl'), pairs)  5.12 us
  transfers between devices with their start and end apart: 17, of which 8 were waited for; matrix products, arithmetic and copies ran while one was open for 1% of the time, Pallas kernels for 6%

profile of v17, /device:TPU:0, one launch (start us, length us, event | category | flops | bytes accessed | tf_op | source)
XLA Modules:
  0.0 167.5 jit_solution(10325583593240240644)
XLA Ops:
  0.7 0.7 copy-done
  1.4 1.6 fusion.2
  3.0 1.7 %collective-permute-start = (bf16[256,1024]{1,0:T(8,128)(2,1)S(1)}, bf16[256,1024]{1,0:T(8,128)(2,1)S(1)}, u32[]{:S(2)}, u32[]{:S(2)}) collective-permute-start(bf16[256,1024]{1,0:T(8,128)(2,1)S(1)} %fusion.2), channel_id=1, source_target_pairs={{0,16},{16,0},{32,112},{48,96},{64,80},{80,64},{96,48},{112,32},{1... | collective-permute-start | bytes 1572872 | tf_op jit(solution)/shard_map/ppermute | solution.py:179
  5.0 2.1 %copy-done.1 = bf16[16,64,2176]{2,1,0:T(8,128)(2,1)} copy-done((bf16[16,64,2176]{2,1,0:T(8,128)(2,1)}, bf16[16,64,2176]{2,1,0:T(8,128)(2,1)S(1)}, u32[]{:S(2)}) %copy-start.1) | copy-done | bytes 4456472
  7.1 5.1 %collective-permute-done = bf16[256,1024]{1,0:T(8,128)(2,1)S(1)} collective-permute-done((bf16[256,1024]{1,0:T(8,128)(2,1)S(1)}, bf16[256,1024]{1,0:T(8,128)(2,1)S(1)}, u32[]{:S(2)}, u32[]{:S(2)}) %collective-permute-start) | collective-permute-done | bytes 524320 | tf_op jit(solution)/shard_map/ppermute | solution.py:179
  12.2 0.8 copy-done.12
  13.0 7.2 %all-to-all-start = ((bf16[16,64,2176]{2,1,0:T(8,128)(2,1)}), bf16[16,64,2176]{2,1,0:T(8,128)(2,1)}, u32[]{:S(2)}, u32[]{:S(2)}) async-start(bf16[16,64,2176]{2,1,0:T(8,128)(2,1)} %copy-done.1), calls=%async_computation | async-start | bytes 8912896 | tf_op jit(solution)/shard_map/all_to_all | solution.py:188
  20.3 2.0 %fusion.3 = bf16[256,1024]{1,0:T(8,128)(2,1)S(1)} fusion(s32[256,4096]{1,0:T(8,128)} %param.8, s32[]{:T(128)S(6)} %select_n.28, f32[2,1024]{1,0:T(2,128)S(1)} %constant_dynamic-slice_fusion, bf16[256,4096]{1,0:T(8,128)(2,1)} %param.7, pred[]{:T(512)S(6)} %eq.7), kind=kLoop, calls=%fused_computation.6 | loop fusion | flops 1310720 | bytes 2105349 | tf_op jit(solution)/shard_map/jit(_where)/select_n | solution.py:171
  22.4 2.0 %collective-permute-start.6 = (bf16[512,1024]{1,0:T(8,128)(2,1)S(1)}, bf16[512,1024]{1,0:T(8,128)(2,1)S(1)}, u32[]{:S(2)}, u32[]{:S(2)}) collective-permute-start(bf16[512,1024]{1,0:T(8,128)(2,1)S(1)} %pad_maximum_fusion.refs_0_), channel_id=1, source_target_pairs={{12,0},{0,4},{4,8},{8,12},{13,1},{1,5},{5,9},{9,13},{14,2},{2,6},{... | collective-permute-start | bytes 3145736 | tf_op jit(solution)/shard_map/ppermute | solution.py:154
  24.4 3.6 %collective-permute-start.4 = (bf16[512,1024]{1,0:T(8,128)(2,1)S(1)}, bf16[512,1024]{1,0:T(8,128)(2,1)S(1)}, u32[]{:S(2)}, u32[]{:S(2)}) collective-permute-start(bf16[512,1024]{1,0:T(8,128)(2,1)S(1)} %pad_maximum_fusion.refs_0_), channel_id=1, source_target_pairs={{8,0},{12,4},{0,8},{4,12},{9,1},{13,5},{1,9},{5,13},{10,2},{14,6},... | collective-permute-start | bytes 3145736 | tf_op jit(solution)/shard_map/ppermute | solution.py:154
  27.9 1.0 collective-permute-start.2
  28.9 20.7 %collective-permute-done.6.refs_3_ = bf16[512,1024]{1,0:T(8,128)(2,1)S(1)} collective-permute-done((bf16[512,1024]{1,0:T(8,128)(2,1)S(1)}, bf16[512,1024]{1,0:T(8,128)(2,1)S(1)}, u32[]{:S(2)}, u32[]{:S(2)}) %collective-permute-start.6) | collective-permute-done | bytes 1048608 | tf_op jit(solution)/shard_map/ppermute | solution.py:154
  49.7 1.0 copy-done.9
  50.6 22.3 %collective-permute-done.4.refs_2_ = bf16[512,1024]{1,0:T(8,128)(2,1)S(1)} collective-permute-done((bf16[512,1024]{1,0:T(8,128)(2,1)S(1)}, bf16[512,1024]{1,0:T(8,128)(2,1)S(1)}, u32[]{:S(2)}, u32[]{:S(2)}) %collective-permute-start.4) | collective-permute-done | bytes 1048608 | tf_op jit(solution)/shard_map/ppermute | solution.py:154
  72.9 14.1 %all-to-all-done = bf16[16,64,2176]{2,1,0:T(8,128)(2,1)} async-done(((bf16[16,64,2176]{2,1,0:T(8,128)(2,1)}), bf16[16,64,2176]{2,1,0:T(8,128)(2,1)}, u32[]{:S(2)}, u32[]{:S(2)}) %all-to-all-start) | async-done | bytes 4456480 | tf_op jit(solution)/shard_map/all_to_all | solution.py:188
  87.0 1.2 copy-done.10
  88.2 7.3 %project.2.after_ref = bf16[1024,1024]{1,0:T(8,128)(2,1)} custom-call(bf16[1024,2176]{1,0:T(8,128)(2,1)} %bitcast.5.acts_ref, bf16[512,1024]{1,0:T(8,128)(2,1)S(1)} %pad_maximum_fusion.refs_0_, bf16[512,1024]{1,0:T(8,128)(2,1)S(1)} %collective-permute-done.2.refs_1_, bf16[512,1024]{1,0:T(8,128)(2,1)S(1)} %collective-permute-done.4.refs_2_, ...), custom_call_target="tpu_custom_call" | custom-call | flops 4294967296 | bytes 12582912 | tf_op jit(solution)/shard_map/project/pallas_call | solution.py:75
  95.5 4.6 %all-to-all-start.1 = ((bf16[16,64,1024]{2,1,0:T(8,128)(2,1)}), bf16[16,64,1024]{2,1,0:T(8,128)(2,1)S(1)}, u32[]{:S(2)}, u32[]{:S(2)}) async-start(bf16[16,64,1024]{2,1,0:T(8,128)(2,1)} %bitcast.7), calls=%async_computation.1 | async-start | bytes 4194304 | tf_op jit(solution)/shard_map/all_to_all | solution.py:192
  100.1 3.7 %stats.1 = (f32[512,128]{1,0:T(8,128)S(1)}, bf16[512,128]{1,0:T(8,128)(2,1)S(1)}, bf16[512,128]{1,0:T(8,128)(2,1)S(1)}, bf16[512,128]{1,0:T(8,128)(2,1)S(1)}) custom-call(bf16[1024,2176]{1,0:T(8,128)(2,1)} %bitcast.5.acts_ref, bf16[1024,1024]{1,0:T(8,128)(2,1)} %project.2.after_ref), custom_call_target="tpu_custom_call" | custom-call | tf_op jit(solution)/shard_map/stats/pallas_call | solution.py:138
  103.9 2.0 %collective-permute-start.8 = (bf16[512,128]{1,0:T(8,128)(2,1)S(1)}, bf16[512,128]{1,0:T(8,128)(2,1)S(1)}, u32[]{:S(2)}, u32[]{:S(2)}) collective-permute-start(bf16[512,128]{1,0:T(8,128)(2,1)S(1)} %get-tuple-element.21), channel_id=1, source_target_pairs={{12,0},{0,4},{4,8},{8,12},{13,1},{1,5},{5,9},{9,13},{14,2},{2,6},{... | collective-permute-start | bytes 393224 | tf_op jit(solution)/shard_map/ppermute | solution.py:154
  105.8 3.6 %collective-permute-start.9 = (bf16[512,128]{1,0:T(8,128)(2,1)S(1)}, bf16[512,128]{1,0:T(8,128)(2,1)S(1)}, u32[]{:S(2)}, u32[]{:S(2)}) collective-permute-start(bf16[512,128]{1,0:T(8,128)(2,1)S(1)} %get-tuple-element.22), channel_id=1, source_target_pairs={{8,0},{12,4},{0,8},{4,12},{9,1},{13,5},{1,9},{5,13},{10,2},{14,6},... | collective-permute-start | bytes 393224 | tf_op jit(solution)/shard_map/ppermute | solution.py:154
  109.4 1.0 collective-permute-start.10
  110.4 0.5 collective-permute-start.7
  111.0 1.4 collective-permute-done.8
  112.3 1.6 collective-permute-done.9
  114.7 3.3 %collective-permute-done.11 = f32[512,128]{1,0:T(8,128)S(1)} collective-permute-done((f32[512,128]{1,0:T(8,128)S(1)}, f32[512,128]{1,0:T(8,128)S(1)}, u32[]{:S(2)}, u32[]{:S(2)}) %collective-permute-start.11) | collective-permute-done | bytes 262176 | tf_op jit(solution)/shard_map/ppermute | solution.py:150
  118.0 3.2 %collective-permute-start.14 = (bf16[256,128]{1,0:T(8,128)(2,1)S(1)}, bf16[256,128]{1,0:T(8,128)(2,1)S(1)}, u32[]{:S(2)}, u32[]{:S(2)}) collective-permute-start(bf16[256,128]{1,0:T(8,128)(2,1)S(1)} %get-tuple-element.33), channel_id=1, source_target_pairs={{0,80},{16,64},{64,16},{80,0},{1,81},{17,65},{65,17},{81,1},{2,82}... | collective-permute-start | bytes 196616 | tf_op jit(solution)/shard_map/ppermute | solution.py:207
  121.5 1.3 collective-permute-start.13
  122.8 6.4 %project.3 = bf16[1024,1024]{1,0:T(8,128)(2,1)S(1)} custom-call(bf16[1024,2176]{1,0:T(8,128)(2,1)} %bitcast.5.acts_ref, bf16[512,1024]{1,0:T(8,128)(2,1)S(1)} %collective-permute-done.1.refs_0_, bf16[512,1024]{1,0:T(8,128)(2,1)S(1)} %collective-permute-done.3.refs_1_, bf16[512,1024]{1,0:T(8,128)(2,1)S(1)} %collective-permute-done.5.refs_2_, ...), custom_call_target="tpu_custom_call" | custom-call | flops 4294967296 | bytes 12582912 | tf_op jit(solution)/shard_map/project/pallas_call | solution.py:75
  129.3 1.3 copy-done.2
  130.6 34.9 %all_to_all.15.second_ref = bf16[16,64,1024]{2,1,0:T(8,128)(2,1)S(1)} all-to-all(bf16[16,64,1024]{2,1,0:T(8,128)(2,1)} %bitcast.19), channel_id=1, replica_groups=mesh['yh'=2,'core'=2,'yl'=2,'z'=4,'x'=4] {'yh','yl','x'}, dimensions={0} | all-to-all | bytes 4194304 | tf_op jit(solution)/shard_map/all_to_all | solution.py:192
  165.5 2.0 %finish.1 = (bf16[64,4096]{1,0:T(8,128)(2,1)}, bf16[64,4096]{1,0:T(8,128)(2,1)}, f32[256,128]{1,0:T(8,128)}, f32[256,128]{1,0:T(8,128)}) custom-call(s32[3]{0:T(128)S(1)} %pad_add_fusion.at_ref, bf16[16,64,1024]{2,1,0:T(8,128)(2,1)S(1)} %all-to-all-done.1.first_ref, bf16[16,64,1024]{2,1,0:T(8,128)(2,1)S(1)} %all_to_all.15.second_ref, ...), custom_call_target="tpu_custom_call" | custom-call | tf_op jit(solution)/shard_map/finish/pallas_call | solution.py:114
  (45 shorter events, 1.6 us)
Async XLA Ops:
  0.6 0.8 copy-start
  0.6 4.1 %copy-start.4 = (bf16[64,8192]{1,0:T(8,128)(2,1)S(1)}, bf16[64,8192]{1,0:T(8,128)(2,1)}, u32[]{:S(2)}) copy-start(bf16[64,8192]{1,0:T(8,128)(2,1)} %quant_ref.1) | copy-start | bytes 3145732
  0.7 4.0 %copy-start.3 = (bf16[64,8192]{1,0:T(8,128)(2,1)S(1)}, bf16[64,8192]{1,0:T(8,128)(2,1)}, u32[]{:S(2)}) copy-start(bf16[64,8192]{1,0:T(8,128)(2,1)} %float_ref.1) | copy-start | bytes 3145732
  3.0 9.3 %collective-permute-start = (bf16[256,1024]{1,0:T(8,128)(2,1)S(1)}, bf16[256,1024]{1,0:T(8,128)(2,1)S(1)}, u32[]{:S(2)}, u32[]{:S(2)}) collective-permute-start(bf16[256,1024]{1,0:T(8,128)(2,1)S(1)} %fusion.2), channel_id=1, source_target_pairs={{0,16},{16,0},{32,112},{48,96},{64,80},{80,64},{96,48},{112,32},{1... | collective-permute-start | bytes 1572872 | tf_op jit(solution)/shard_map/ppermute | solution.py:179
  5.0 2.1 %copy-start.1 = (bf16[16,64,2176]{2,1,0:T(8,128)(2,1)}, bf16[16,64,2176]{2,1,0:T(8,128)(2,1)S(1)}, u32[]{:S(2)}) copy-start(bf16[16,64,2176]{2,1,0:T(8,128)(2,1)S(1)} %pack.1) | copy-start | bytes 13369348
  12.2 0.8 copy-start.12
  13.0 74.0 %all-to-all-start = ((bf16[16,64,2176]{2,1,0:T(8,128)(2,1)}), bf16[16,64,2176]{2,1,0:T(8,128)(2,1)}, u32[]{:S(2)}, u32[]{:S(2)}) async-start(bf16[16,64,2176]{2,1,0:T(8,128)(2,1)} %copy-done.1), calls=%async_computation | async-start | bytes 8912896 | tf_op jit(solution)/shard_map/all_to_all | solution.py:188
  20.2 2.1 %copy-start.13 = (bf16[256,1024]{1,0:T(8,128)(2,1)S(1)}, bf16[256,1024]{1,0:T(8,128)(2,1)}, u32[]{:S(2)}) copy-start(bf16[256,1024]{1,0:T(8,128)(2,1)} %copy-done.12) | copy-start | bytes 1572868
  22.4 27.3 %collective-permute-start.6 = (bf16[512,1024]{1,0:T(8,128)(2,1)S(1)}, bf16[512,1024]{1,0:T(8,128)(2,1)S(1)}, u32[]{:S(2)}, u32[]{:S(2)}) collective-permute-start(bf16[512,1024]{1,0:T(8,128)(2,1)S(1)} %pad_maximum_fusion.refs_0_), channel_id=1, source_target_pairs={{12,0},{0,4},{4,8},{8,12},{13,1},{1,5},{5,9},{9,13},{14,2},{2,6},{... | collective-permute-start | bytes 3145736 | tf_op jit(solution)/shard_map/ppermute | solution.py:154
  24.4 48.5 %collective-permute-start.4 = (bf16[512,1024]{1,0:T(8,128)(2,1)S(1)}, bf16[512,1024]{1,0:T(8,128)(2,1)S(1)}, u32[]{:S(2)}, u32[]{:S(2)}) collective-permute-start(bf16[512,1024]{1,0:T(8,128)(2,1)S(1)} %pad_maximum_fusion.refs_0_), channel_id=1, source_target_pairs={{8,0},{12,4},{0,8},{4,12},{9,1},{13,5},{1,9},{5,13},{10,2},{14,6},... | collective-permute-start | bytes 3145736 | tf_op jit(solution)/shard_map/ppermute | solution.py:154
  27.9 44.9 %collective-permute-start.2 = (bf16[512,1024]{1,0:T(8,128)(2,1)S(1)}, bf16[512,1024]{1,0:T(8,128)(2,1)S(1)}, u32[]{:S(2)}, u32[]{:S(2)}) collective-permute-start(bf16[512,1024]{1,0:T(8,128)(2,1)S(1)} %pad_maximum_fusion.refs_0_), channel_id=1, source_target_pairs={{4,0},{8,4},{12,8},{0,12},{5,1},{9,5},{13,9},{1,13},{6,2},{10,6},{... | collective-permute-start | bytes 3145736 | tf_op jit(solution)/shard_map/ppermute | solution.py:154
  49.7 1.0 copy-start.9
  72.9 22.6 %copy-start.5 = (bf16[512,1024]{1,0:T(8,128)(2,1)}, bf16[512,1024]{1,0:T(8,128)(2,1)S(1)}, u32[]{:S(2)}) copy-start(bf16[512,1024]{1,0:T(8,128)(2,1)S(1)} %collective-permute-done.4.refs_2_) | copy-start | bytes 3145732
  72.9 22.6 %copy-start.7 = (bf16[512,1024]{1,0:T(8,128)(2,1)}, bf16[512,1024]{1,0:T(8,128)(2,1)S(1)}, u32[]{:S(2)}) copy-start(bf16[512,1024]{1,0:T(8,128)(2,1)S(1)} %collective-permute-done.2.refs_1_) | copy-start | bytes 3145732
  87.0 1.2 copy-start.10
  95.5 35.1 %all-to-all-start.1 = ((bf16[16,64,1024]{2,1,0:T(8,128)(2,1)}), bf16[16,64,1024]{2,1,0:T(8,128)(2,1)S(1)}, u32[]{:S(2)}, u32[]{:S(2)}) async-start(bf16[16,64,1024]{2,1,0:T(8,128)(2,1)} %bitcast.7), calls=%async_computation.1 | async-start | bytes 4194304 | tf_op jit(solution)/shard_map/all_to_all | solution.py:192
  100.1 10.3 %copy-start.11 = (bf16[512,1024]{1,0:T(8,128)(2,1)S(1)}, bf16[512,1024]{1,0:T(8,128)(2,1)}, u32[]{:S(2)}) copy-start(bf16[512,1024]{1,0:T(8,128)(2,1)} %copy-done.9) | copy-start | bytes 3145732
  100.1 12.2 %copy-start.6 = (bf16[512,1024]{1,0:T(8,128)(2,1)S(1)}, bf16[512,1024]{1,0:T(8,128)(2,1)}, u32[]{:S(2)}) copy-start(bf16[512,1024]{1,0:T(8,128)(2,1)} %copy-done.5) | copy-start | bytes 3145732
  100.1 13.8 %copy-start.8 = (bf16[512,1024]{1,0:T(8,128)(2,1)S(1)}, bf16[512,1024]{1,0:T(8,128)(2,1)}, u32[]{:S(2)}) copy-start(bf16[512,1024]{1,0:T(8,128)(2,1)} %copy-done.7) | copy-start | bytes 3145732
  103.9 8.5 %collective-permute-start.8 = (bf16[512,128]{1,0:T(8,128)(2,1)S(1)}, bf16[512,128]{1,0:T(8,128)(2,1)S(1)}, u32[]{:S(2)}, u32[]{:S(2)}) collective-permute-start(bf16[512,128]{1,0:T(8,128)(2,1)S(1)} %get-tuple-element.21), channel_id=1, source_target_pairs={{12,0},{0,4},{4,8},{8,12},{13,1},{1,5},{5,9},{9,13},{14,2},{2,6},{... | collective-permute-start | bytes 393224 | tf_op jit(solution)/shard_map/ppermute | solution.py:154
  105.8 8.1 %collective-permute-start.9 = (bf16[512,128]{1,0:T(8,128)(2,1)S(1)}, bf16[512,128]{1,0:T(8,128)(2,1)S(1)}, u32[]{:S(2)}, u32[]{:S(2)}) collective-permute-start(bf16[512,128]{1,0:T(8,128)(2,1)S(1)} %get-tuple-element.22), channel_id=1, source_target_pairs={{8,0},{12,4},{0,8},{4,12},{9,1},{13,5},{1,9},{5,13},{10,2},{14,6},... | collective-permute-start | bytes 393224 | tf_op jit(solution)/shard_map/ppermute | solution.py:154
  109.4 5.0 %collective-permute-start.10 = (bf16[512,128]{1,0:T(8,128)(2,1)S(1)}, bf16[512,128]{1,0:T(8,128)(2,1)S(1)}, u32[]{:S(2)}, u32[]{:S(2)}) collective-permute-start(bf16[512,128]{1,0:T(8,128)(2,1)S(1)} %get-tuple-element.23), channel_id=1, source_target_pairs={{4,0},{8,4},{12,8},{0,12},{5,1},{9,5},{13,9},{1,13},{6,2},{10,6},{... | collective-permute-start | bytes 393224 | tf_op jit(solution)/shard_map/ppermute | solution.py:154
  110.4 10.8 %collective-permute-start.1 = (bf16[512,1024]{1,0:T(8,128)(2,1)S(1)}, bf16[512,1024]{1,0:T(8,128)(2,1)S(1)}, u32[]{:S(2)}, u32[]{:S(2)}) collective-permute-start(bf16[512,1024]{1,0:T(8,128)(2,1)S(1)} %pad_maximum_fusion.refs_0_), channel_id=1, source_target_pairs={{0,32},{32,0},{1,33},{33,1},{2,34},{34,2},{3,35},{35,3},{4,36},{36... | collective-permute-start | bytes 3145736 | tf_op jit(solution)/shard_map/ppermute | solution.py:150
  110.4 11.1 %collective-permute-start.7 = (bf16[512,1024]{1,0:T(8,128)(2,1)S(1)}, bf16[512,1024]{1,0:T(8,128)(2,1)S(1)}, u32[]{:S(2)}, u32[]{:S(2)}) collective-permute-start(bf16[512,1024]{1,0:T(8,128)(2,1)S(1)} %copy-done.11), channel_id=1, source_target_pairs={{0,32},{32,0},{1,33},{33,1},{2,34},{34,2},{3,35},{35,3},{4,36},{36... | collective-permute-start | bytes 3145736 | tf_op jit(solution)/shard_map/ppermute | solution.py:150
  112.3 10.5 %collective-permute-start.5 = (bf16[512,1024]{1,0:T(8,128)(2,1)S(1)}, bf16[512,1024]{1,0:T(8,128)(2,1)S(1)}, u32[]{:S(2)}, u32[]{:S(2)}) collective-permute-start(bf16[512,1024]{1,0:T(8,128)(2,1)S(1)} %copy-done.6), channel_id=1, source_target_pairs={{0,32},{32,0},{1,33},{33,1},{2,34},{34,2},{3,35},{35,3},{4,36},{36... | collective-permute-start | bytes 3145736 | tf_op jit(solution)/shard_map/ppermute | solution.py:150
  113.9 8.9 %collective-permute-start.3 = (bf16[512,1024]{1,0:T(8,128)(2,1)S(1)}, bf16[512,1024]{1,0:T(8,128)(2,1)S(1)}, u32[]{:S(2)}, u32[]{:S(2)}) collective-permute-start(bf16[512,1024]{1,0:T(8,128)(2,1)S(1)} %copy-done.8), channel_id=1, source_target_pairs={{0,32},{32,0},{1,33},{33,1},{2,34},{34,2},{3,35},{35,3},{4,36},{36... | collective-permute-start | bytes 3145736 | tf_op jit(solution)/shard_map/ppermute | solution.py:150
  114.5 3.5 %collective-permute-start.11 = (f32[512,128]{1,0:T(8,128)S(1)}, f32[512,128]{1,0:T(8,128)S(1)}, u32[]{:S(2)}, u32[]{:S(2)}) collective-permute-start(f32[512,128]{1,0:T(8,128)S(1)} %convert_add_fusion.refs_4_), channel_id=1, source_target_pairs={{0,32},{32,0},{1,33},{33,1},{2,34},{34,2},{3,35},{35,3},{4,36},{36... | collective-permute-start | bytes 786440 | tf_op jit(solution)/shard_map/ppermute | solution.py:150
  118.0 12.6 %collective-permute-start.14 = (bf16[256,128]{1,0:T(8,128)(2,1)S(1)}, bf16[256,128]{1,0:T(8,128)(2,1)S(1)}, u32[]{:S(2)}, u32[]{:S(2)}) collective-permute-start(bf16[256,128]{1,0:T(8,128)(2,1)S(1)} %get-tuple-element.33), channel_id=1, source_target_pairs={{0,80},{16,64},{64,16},{80,0},{1,81},{17,65},{65,17},{81,1},{2,82}... | collective-permute-start | bytes 196616 | tf_op jit(solution)/shard_map/ppermute | solution.py:207
  121.3 9.4 %collective-permute-start.12 = (bf16[256,128]{1,0:T(8,128)(2,1)S(1)}, bf16[256,128]{1,0:T(8,128)(2,1)S(1)}, u32[]{:S(2)}, u32[]{:S(2)}) collective-permute-start(bf16[256,128]{1,0:T(8,128)(2,1)S(1)} %get-tuple-element.33), channel_id=1, source_target_pairs={{0,16},{16,0},{1,17},{17,1},{2,18},{18,2},{3,19},{19,3},{4,20},{20... | collective-permute-start | bytes 196616 | tf_op jit(solution)/shard_map/ppermute | solution.py:150
  121.5 9.1 %collective-permute-start.13 = (bf16[256,128]{1,0:T(8,128)(2,1)S(1)}, bf16[256,128]{1,0:T(8,128)(2,1)S(1)}, u32[]{:S(2)}, u32[]{:S(2)}) collective-permute-start(bf16[256,128]{1,0:T(8,128)(2,1)S(1)} %get-tuple-element.32), channel_id=1, source_target_pairs={{0,64},{64,0},{1,65},{65,1},{2,66},{66,2},{3,67},{67,3},{4,68},{68... | collective-permute-start | bytes 196616 | tf_op jit(solution)/shard_map/ppermute | solution.py:150
  129.3 1.3 copy-start.2

commit v18 on v17

--- a/solution.py
+++ b/solution.py
@@ -191,7 +191,7 @@
     def output(p):
         return lax.all_to_all(p.reshape(16, tokens, quarter), PLANE, 0, 0, tiled=True)
 
-    first = project(acts, parts, ())
+    first = project(acts, parts, others)
     result1 = output(first)
 
     blocks = stats(acts, first)

time: 168 us -> 170 us (1.012)
  local copies, waits for them, and re-layouts: 7.24 us -> 15.5 us
  waiting for transfers between devices: 68.9 us -> 63.6 us
    unnamed x28 -> x42, local copies, waits for them, and re-layouts: 7.15 us -> 15.4 us
    all_to_all x1, waiting for transfers between devices: 14.1 us -> 9.02 us  [shards(): lax.all_to_all(payload, PLANE, 0, 0, tiled=True).reshape(16 * tokens, -1)]
  transfers between devices with their start and end apart: 17 -> 17, of which waited for: 8 -> 11; matrix products, arithmetic and copies ran while one was open for 1% -> 1% of each run, Pallas kernels for 6% -> 6%
where the time goes in v18:
time: 170 us
  waiting for transfers between devices  63.6 us (37%)
  blocking collectives  34.3 us (20%)
  starting transfers between devices  32 us (19%)
  Pallas kernels  19.8 us (12%)
  local copies, waits for them, and re-layouts  15.5 us (9%)
  other arithmetic  3.74 us (2%)
    ppermute x6, waiting for transfers between devices, ahead(): return lax.ppermute(a, axis, [((i + j) % 4, i) for i in range(4)])  46.9 us
    all_to_all x1, blocking collectives, output(): lax.all_to_all(p.reshape(16, tokens, quarter), PLANE, 0, 0, tiled=True)  34.3 us
    unnamed x42, local copies, waits for them, and re-layouts  15.4 us
    pallas_call x2, Pallas kernels, project(): pl.pallas_call(project_kernel, out_shape=jax.ShapeDtypeStruct((rows, cols...  13.7 us
    ppermute x6, starting transfers between devices, ahead(): return lax.ppermute(a, axis, [((i + j) % 4, i) for i in range(4)])  13.2 us
    all_to_all x1, waiting for transfers between devices, shards(): lax.all_to_all(payload, PLANE, 0, 0, tiled=True).reshape(16 * tokens, -1)  9.02 us
    all_to_all x1, starting transfers between devices, shards(): lax.all_to_all(payload, PLANE, 0, 0, tiled=True).reshape(16 * tokens, -1)  7.16 us
    ppermute x1, waiting for transfers between devices, shards(): got = lax.ppermute(send, ('yh', 'core', 'yl'), pairs)  5.1 us
  transfers between devices with their start and end apart: 17, of which 11 were waited for; matrix products, arithmetic and copies ran while one was open for 1% of the time, Pallas kernels for 6%

profile of v18, /device:TPU:0, one launch (start us, length us, event | category | flops | bytes accessed | tf_op | source)
XLA Modules:
  0.0 169.8 jit_solution(5104250174900092178)
XLA Ops:
  1.4 1.6 fusion.2
  3.0 1.7 %collective-permute-start = (bf16[256,1024]{1,0:T(8,128)(2,1)S(1)}, bf16[256,1024]{1,0:T(8,128)(2,1)S(1)}, u32[]{:S(2)}, u32[]{:S(2)}) collective-permute-start(bf16[256,1024]{1,0:T(8,128)(2,1)S(1)} %fusion.2), channel_id=1, source_target_pairs={{0,16},{16,0},{32,112},{48,96},{64,80},{80,64},{96,48},{112,32},{1... | collective-permute-start | bytes 1572872 | tf_op jit(solution)/shard_map/ppermute | solution.py:179
  5.0 2.1 %copy-done.1 = bf16[16,64,2176]{2,1,0:T(8,128)(2,1)} copy-done((bf16[16,64,2176]{2,1,0:T(8,128)(2,1)}, bf16[16,64,2176]{2,1,0:T(8,128)(2,1)S(1)}, u32[]{:S(2)}) %copy-start.1) | copy-done | bytes 4456472
  7.1 5.1 %collective-permute-done = bf16[256,1024]{1,0:T(8,128)(2,1)S(1)} collective-permute-done((bf16[256,1024]{1,0:T(8,128)(2,1)S(1)}, bf16[256,1024]{1,0:T(8,128)(2,1)S(1)}, u32[]{:S(2)}, u32[]{:S(2)}) %collective-permute-start) | collective-permute-done | bytes 524320 | tf_op jit(solution)/shard_map/ppermute | solution.py:179
  12.2 7.2 %all-to-all-start = ((bf16[16,64,2176]{2,1,0:T(8,128)(2,1)}), bf16[16,64,2176]{2,1,0:T(8,128)(2,1)}, u32[]{:S(2)}, u32[]{:S(2)}) async-start(bf16[16,64,2176]{2,1,0:T(8,128)(2,1)} %copy-done.1), calls=%async_computation | async-start | bytes 8912896 | tf_op jit(solution)/shard_map/all_to_all | solution.py:188
  19.5 1.9 %fusion.3 = bf16[256,1024]{1,0:T(8,128)(2,1)S(1)} fusion(s32[256,4096]{1,0:T(8,128)} %param.8, s32[]{:T(128)S(6)} %select_n.28, f32[2,1024]{1,0:T(2,128)S(1)} %constant_dynamic-slice_fusion, bf16[256,4096]{1,0:T(8,128)(2,1)} %param.7, pred[]{:T(512)S(6)} %eq.7), kind=kLoop, calls=%fused_computation.6 | loop fusion | flops 1310720 | bytes 2105349 | tf_op jit(solution)/shard_map/jit(_where)/select_n | solution.py:171
  21.5 2.0 %collective-permute-start.6 = (bf16[512,1024]{1,0:T(8,128)(2,1)S(1)}, bf16[512,1024]{1,0:T(8,128)(2,1)S(1)}, u32[]{:S(2)}, u32[]{:S(2)}) collective-permute-start(bf16[512,1024]{1,0:T(8,128)(2,1)S(1)} %pad_maximum_fusion.refs_0_), channel_id=1, source_target_pairs={{12,0},{0,4},{4,8},{8,12},{13,1},{1,5},{5,9},{9,13},{14,2},{2,6},{... | collective-permute-start | bytes 3145736 | tf_op jit(solution)/shard_map/ppermute | solution.py:154
  23.5 3.6 %collective-permute-start.4 = (bf16[512,1024]{1,0:T(8,128)(2,1)S(1)}, bf16[512,1024]{1,0:T(8,128)(2,1)S(1)}, u32[]{:S(2)}, u32[]{:S(2)}) collective-permute-start(bf16[512,1024]{1,0:T(8,128)(2,1)S(1)} %pad_maximum_fusion.refs_0_), channel_id=1, source_target_pairs={{8,0},{12,4},{0,8},{4,12},{9,1},{13,5},{1,9},{5,13},{10,2},{14,6},... | collective-permute-start | bytes 3145736 | tf_op jit(solution)/shard_map/ppermute | solution.py:154
  28.1 20.7 %collective-permute-done.6.refs_3_ = bf16[512,1024]{1,0:T(8,128)(2,1)S(1)} collective-permute-done((bf16[512,1024]{1,0:T(8,128)(2,1)S(1)}, bf16[512,1024]{1,0:T(8,128)(2,1)S(1)}, u32[]{:S(2)}, u32[]{:S(2)}) %collective-permute-start.6) | collective-permute-done | bytes 1048608 | tf_op jit(solution)/shard_map/ppermute | solution.py:154
  49.8 22.2 %collective-permute-done.4.refs_2_ = bf16[512,1024]{1,0:T(8,128)(2,1)S(1)} collective-permute-done((bf16[512,1024]{1,0:T(8,128)(2,1)S(1)}, bf16[512,1024]{1,0:T(8,128)(2,1)S(1)}, u32[]{:S(2)}, u32[]{:S(2)}) %collective-permute-start.4) | collective-permute-done | bytes 1048608 | tf_op jit(solution)/shard_map/ppermute | solution.py:154
  72.0 1.1 copy-done.17
  74.7 1.0 copy-done.9
  77.2 9.0 %all-to-all-done = bf16[16,64,2176]{2,1,0:T(8,128)(2,1)} async-done(((bf16[16,64,2176]{2,1,0:T(8,128)(2,1)}), bf16[16,64,2176]{2,1,0:T(8,128)(2,1)}, u32[]{:S(2)}, u32[]{:S(2)}) %all-to-all-start) | async-done | bytes 4456480 | tf_op jit(solution)/shard_map/all_to_all | solution.py:188
  86.2 1.2 copy-done.10
  87.4 1.2 copy-done.13
  88.6 1.2 copy-done.16
  89.9 1.2 copy-done.18
  91.1 1.2 copy-done.20
  92.3 7.3 %project.2.after_ref = bf16[1024,1024]{1,0:T(8,128)(2,1)} custom-call(bf16[1024,2176]{1,0:T(8,128)(2,1)} %bitcast.5.acts_ref, bf16[512,1024]{1,0:T(8,128)(2,1)S(1)} %pad_maximum_fusion.refs_0_, bf16[512,1024]{1,0:T(8,128)(2,1)S(1)} %copy-done.20, bf16[512,1024]{1,0:T(8,128)(2,1)S(1)} %copy-done.18, bf16[512,1024]{1,0:T(8,128)(2,1)S(1)} %copy-done.16, ...), custom_call_target="tpu_custom_call" | custom-call | flops 4294967296 | bytes 12582912 | tf_op jit(solution)/shard_map/project/pallas_call | solution.py:75
  99.6 4.6 %all-to-all-start.1 = ((bf16[16,64,1024]{2,1,0:T(8,128)(2,1)}), bf16[16,64,1024]{2,1,0:T(8,128)(2,1)S(1)}, u32[]{:S(2)}, u32[]{:S(2)}) async-start(bf16[16,64,1024]{2,1,0:T(8,128)(2,1)} %bitcast.7), calls=%async_computation.1 | async-start | bytes 4194304 | tf_op jit(solution)/shard_map/all_to_all | solution.py:192
  104.2 3.7 %stats.1 = (f32[512,128]{1,0:T(8,128)S(1)}, bf16[512,128]{1,0:T(8,128)(2,1)S(1)}, bf16[512,128]{1,0:T(8,128)(2,1)S(1)}, bf16[512,128]{1,0:T(8,128)(2,1)S(1)}) custom-call(bf16[1024,2176]{1,0:T(8,128)(2,1)} %bitcast.5.acts_ref, bf16[1024,1024]{1,0:T(8,128)(2,1)} %project.2.after_ref), custom_call_target="tpu_custom_call" | custom-call | tf_op jit(solution)/shard_map/stats/pallas_call | solution.py:138
  108.0 2.0 %collective-permute-start.8 = (bf16[512,128]{1,0:T(8,128)(2,1)S(1)}, bf16[512,128]{1,0:T(8,128)(2,1)S(1)}, u32[]{:S(2)}, u32[]{:S(2)}) collective-permute-start(bf16[512,128]{1,0:T(8,128)(2,1)S(1)} %get-tuple-element.21), channel_id=1, source_target_pairs={{12,0},{0,4},{4,8},{8,12},{13,1},{1,5},{5,9},{9,13},{14,2},{2,6},{... | collective-permute-start | bytes 393224 | tf_op jit(solution)/shard_map/ppermute | solution.py:154
  110.0 3.6 %collective-permute-start.9 = (bf16[512,128]{1,0:T(8,128)(2,1)S(1)}, bf16[512,128]{1,0:T(8,128)(2,1)S(1)}, u32[]{:S(2)}, u32[]{:S(2)}) collective-permute-start(bf16[512,128]{1,0:T(8,128)(2,1)S(1)} %get-tuple-element.22), channel_id=1, source_target_pairs={{8,0},{12,4},{0,8},{4,12},{9,1},{13,5},{1,9},{5,13},{10,2},{14,6},... | collective-permute-start | bytes 393224 | tf_op jit(solution)/shard_map/ppermute | solution.py:154
  114.6 1.9 %collective-permute-done.8 = bf16[512,128]{1,0:T(8,128)(2,1)S(1)} collective-permute-done((bf16[512,128]{1,0:T(8,128)(2,1)S(1)}, bf16[512,128]{1,0:T(8,128)(2,1)S(1)}, u32[]{:S(2)}, u32[]{:S(2)}) %collective-permute-start.8) | collective-permute-done | bytes 131104 | tf_op jit(solution)/shard_map/ppermute | solution.py:154
  116.4 1.6 collective-permute-done.9
  118.7 1.4 collective-permute-done.11
  120.3 3.2 %collective-permute-start.14 = (bf16[256,128]{1,0:T(8,128)(2,1)S(1)}, bf16[256,128]{1,0:T(8,128)(2,1)S(1)}, u32[]{:S(2)}, u32[]{:S(2)}) collective-permute-start(bf16[256,128]{1,0:T(8,128)(2,1)S(1)} %get-tuple-element.33), channel_id=1, source_target_pairs={{0,80},{16,64},{64,16},{80,0},{1,81},{17,65},{65,17},{81,1},{2,82}... | collective-permute-start | bytes 196616 | tf_op jit(solution)/shard_map/ppermute | solution.py:207
  123.7 1.3 collective-permute-start.13
  125.0 6.4 %project.3 = bf16[1024,1024]{1,0:T(8,128)(2,1)S(1)} custom-call(bf16[1024,2176]{1,0:T(8,128)(2,1)} %bitcast.5.acts_ref, bf16[512,1024]{1,0:T(8,128)(2,1)S(1)} %copy-done.6, bf16[512,1024]{1,0:T(8,128)(2,1)S(1)} %copy-done.14, bf16[512,1024]{1,0:T(8,128)(2,1)S(1)} %copy-done.11, bf16[512,1024]{1,0:T(8,128)(2,1)S(1)} %copy-done.8, ...), custom_call_target="tpu_custom_call" | custom-call | flops 4294967296 | bytes 12582912 | tf_op jit(solution)/shard_map/project/pallas_call | solution.py:75
  131.5 1.4 copy-done.2
  133.4 34.3 %all_to_all.15.second_ref = bf16[16,64,1024]{2,1,0:T(8,128)(2,1)S(1)} all-to-all(bf16[16,64,1024]{2,1,0:T(8,128)(2,1)} %bitcast.19), channel_id=1, replica_groups=mesh['yh'=2,'core'=2,'yl'=2,'z'=4,'x'=4] {'yh','yl','x'}, dimensions={0} | all-to-all | bytes 4194304 | tf_op jit(solution)/shard_map/all_to_all | solution.py:192
  167.7 2.0 %finish.1 = (bf16[64,4096]{1,0:T(8,128)(2,1)}, bf16[64,4096]{1,0:T(8,128)(2,1)}, f32[256,128]{1,0:T(8,128)}, f32[256,128]{1,0:T(8,128)}) custom-call(s32[3]{0:T(128)S(1)} %pad_add_fusion.at_ref, bf16[16,64,1024]{2,1,0:T(8,128)(2,1)S(1)} %all-to-all-done.1.first_ref, bf16[16,64,1024]{2,1,0:T(8,128)(2,1)S(1)} %all_to_all.15.second_ref, ...), custom_call_target="tpu_custom_call" | custom-call | tf_op jit(solution)/shard_map/finish/pallas_call | solution.py:114
  (59 shorter events, 8.8 us)
Async XLA Ops:
  0.6 4.1 %copy-start.4 = (bf16[64,8192]{1,0:T(8,128)(2,1)S(1)}, bf16[64,8192]{1,0:T(8,128)(2,1)}, u32[]{:S(2)}) copy-start(bf16[64,8192]{1,0:T(8,128)(2,1)} %quant_ref.1) | copy-start | bytes 3145732
  0.7 4.0 %copy-start.3 = (bf16[64,8192]{1,0:T(8,128)(2,1)S(1)}, bf16[64,8192]{1,0:T(8,128)(2,1)}, u32[]{:S(2)}) copy-start(bf16[64,8192]{1,0:T(8,128)(2,1)} %float_ref.1) | copy-start | bytes 3145732
  3.0 9.3 %collective-permute-start = (bf16[256,1024]{1,0:T(8,128)(2,1)S(1)}, bf16[256,1024]{1,0:T(8,128)(2,1)S(1)}, u32[]{:S(2)}, u32[]{:S(2)}) collective-permute-start(bf16[256,1024]{1,0:T(8,128)(2,1)S(1)} %fusion.2), channel_id=1, source_target_pairs={{0,16},{16,0},{32,112},{48,96},{64,80},{80,64},{96,48},{112,32},{1... | collective-permute-start | bytes 1572872 | tf_op jit(solution)/shard_map/ppermute | solution.py:179
  5.0 2.1 %copy-start.1 = (bf16[16,64,2176]{2,1,0:T(8,128)(2,1)}, bf16[16,64,2176]{2,1,0:T(8,128)(2,1)S(1)}, u32[]{:S(2)}) copy-start(bf16[16,64,2176]{2,1,0:T(8,128)(2,1)S(1)} %pack.1) | copy-start | bytes 13369348
  12.2 74.0 %all-to-all-start = ((bf16[16,64,2176]{2,1,0:T(8,128)(2,1)}), bf16[16,64,2176]{2,1,0:T(8,128)(2,1)}, u32[]{:S(2)}, u32[]{:S(2)}) async-start(bf16[16,64,2176]{2,1,0:T(8,128)(2,1)} %copy-done.1), calls=%async_computation | async-start | bytes 8912896 | tf_op jit(solution)/shard_map/all_to_all | solution.py:188
  21.5 27.3 %collective-permute-start.6 = (bf16[512,1024]{1,0:T(8,128)(2,1)S(1)}, bf16[512,1024]{1,0:T(8,128)(2,1)S(1)}, u32[]{:S(2)}, u32[]{:S(2)}) collective-permute-start(bf16[512,1024]{1,0:T(8,128)(2,1)S(1)} %pad_maximum_fusion.refs_0_), channel_id=1, source_target_pairs={{12,0},{0,4},{4,8},{8,12},{13,1},{1,5},{5,9},{9,13},{14,2},{2,6},{... | collective-permute-start | bytes 3145736 | tf_op jit(solution)/shard_map/ppermute | solution.py:154
  23.5 48.5 %collective-permute-start.4 = (bf16[512,1024]{1,0:T(8,128)(2,1)S(1)}, bf16[512,1024]{1,0:T(8,128)(2,1)S(1)}, u32[]{:S(2)}, u32[]{:S(2)}) collective-permute-start(bf16[512,1024]{1,0:T(8,128)(2,1)S(1)} %pad_maximum_fusion.refs_0_), channel_id=1, source_target_pairs={{8,0},{12,4},{0,8},{4,12},{9,1},{13,5},{1,9},{5,13},{10,2},{14,6},... | collective-permute-start | bytes 3145736 | tf_op jit(solution)/shard_map/ppermute | solution.py:154
  27.1 46.0 %collective-permute-start.2 = (bf16[512,1024]{1,0:T(8,128)(2,1)S(1)}, bf16[512,1024]{1,0:T(8,128)(2,1)S(1)}, u32[]{:S(2)}, u32[]{:S(2)}) collective-permute-start(bf16[512,1024]{1,0:T(8,128)(2,1)S(1)} %pad_maximum_fusion.refs_0_), channel_id=1, source_target_pairs={{4,0},{8,4},{12,8},{0,12},{5,1},{9,5},{13,9},{1,13},{6,2},{10,6},{... | collective-permute-start | bytes 3145736 | tf_op jit(solution)/shard_map/ppermute | solution.py:154
  28.1 46.5 %collective-permute-start.1 = (bf16[512,1024]{1,0:T(8,128)(2,1)S(1)}, bf16[512,1024]{1,0:T(8,128)(2,1)S(1)}, u32[]{:S(2)}, u32[]{:S(2)}) collective-permute-start(bf16[512,1024]{1,0:T(8,128)(2,1)S(1)} %pad_maximum_fusion.refs_0_), channel_id=1, source_target_pairs={{0,32},{32,0},{1,33},{33,1},{2,34},{34,2},{3,35},{35,3},{4,36},{36... | collective-permute-start | bytes 3145736 | tf_op jit(solution)/shard_map/ppermute | solution.py:150
  48.8 25.8 %collective-permute-start.7 = (bf16[512,1024]{1,0:T(8,128)(2,1)S(1)}, bf16[512,1024]{1,0:T(8,128)(2,1)S(1)}, u32[]{:S(2)}, u32[]{:S(2)}) collective-permute-start(bf16[512,1024]{1,0:T(8,128)(2,1)S(1)} %collective-permute-done.6.refs_3_), channel_id=1, source_target_pairs={{0,32},{32,0},{1,33},{33,1},{2,34},{34,2},{3,35},{35,3},{4,36},{36... | collective-permute-start | bytes 3145736 | tf_op jit(solution)/shard_map/ppermute | solution.py:150
  72.0 2.7 %collective-permute-start.5 = (bf16[512,1024]{1,0:T(8,128)(2,1)S(1)}, bf16[512,1024]{1,0:T(8,128)(2,1)S(1)}, u32[]{:S(2)}, u32[]{:S(2)}) collective-permute-start(bf16[512,1024]{1,0:T(8,128)(2,1)S(1)} %collective-permute-done.4.refs_2_), channel_id=1, source_target_pairs={{0,32},{32,0},{1,33},{33,1},{2,34},{34,2},{3,35},{35,3},{4,36},{36... | collective-permute-start | bytes 3145736 | tf_op jit(solution)/shard_map/ppermute | solution.py:150
  73.1 3.1 %collective-permute-start.3 = (bf16[512,1024]{1,0:T(8,128)(2,1)S(1)}, bf16[512,1024]{1,0:T(8,128)(2,1)S(1)}, u32[]{:S(2)}, u32[]{:S(2)}) collective-permute-start(bf16[512,1024]{1,0:T(8,128)(2,1)S(1)} %collective-permute-done.2.refs_1_), channel_id=1, source_target_pairs={{0,32},{32,0},{1,33},{33,1},{2,34},{34,2},{3,35},{35,3},{4,36},{36... | collective-permute-start | bytes 3145736 | tf_op jit(solution)/shard_map/ppermute | solution.py:150
  74.6 25.0 %copy-start.5 = (bf16[512,1024]{1,0:T(8,128)(2,1)}, bf16[512,1024]{1,0:T(8,128)(2,1)S(1)}, u32[]{:S(2)}) copy-start(bf16[512,1024]{1,0:T(8,128)(2,1)S(1)} %collective-permute-done.1.refs_4_.refs_0_) | copy-start | bytes 3145732
  74.6 25.0 %copy-start.7 = (bf16[512,1024]{1,0:T(8,128)(2,1)}, bf16[512,1024]{1,0:T(8,128)(2,1)S(1)}, u32[]{:S(2)}) copy-start(bf16[512,1024]{1,0:T(8,128)(2,1)S(1)} %collective-permute-done.7.refs_7_.refs_3_) | copy-start | bytes 3145732
  86.2 1.2 copy-start.10
  87.4 1.2 copy-start.13
  88.6 1.2 copy-start.16
  89.9 1.2 copy-start.18
  91.1 1.2 copy-start.20
  99.6 33.8 %all-to-all-start.1 = ((bf16[16,64,1024]{2,1,0:T(8,128)(2,1)}), bf16[16,64,1024]{2,1,0:T(8,128)(2,1)S(1)}, u32[]{:S(2)}, u32[]{:S(2)}) async-start(bf16[16,64,1024]{2,1,0:T(8,128)(2,1)} %bitcast.7), calls=%async_computation.1 | async-start | bytes 4194304 | tf_op jit(solution)/shard_map/all_to_all | solution.py:192
  104.2 20.8 %copy-start.11 = (bf16[512,1024]{1,0:T(8,128)(2,1)S(1)}, bf16[512,1024]{1,0:T(8,128)(2,1)}, u32[]{:S(2)}) copy-start(bf16[512,1024]{1,0:T(8,128)(2,1)} %copy-done.9) | copy-start | bytes 3145732
  104.2 20.8 %copy-start.14 = (bf16[512,1024]{1,0:T(8,128)(2,1)S(1)}, bf16[512,1024]{1,0:T(8,128)(2,1)}, u32[]{:S(2)}) copy-start(bf16[512,1024]{1,0:T(8,128)(2,1)} %copy-done.12) | copy-start | bytes 3145732
  108.0 17.1 %copy-start.6 = (bf16[512,1024]{1,0:T(8,128)(2,1)S(1)}, bf16[512,1024]{1,0:T(8,128)(2,1)}, u32[]{:S(2)}) copy-start(bf16[512,1024]{1,0:T(8,128)(2,1)} %copy-done.5) | copy-start | bytes 3145732
  108.0 17.1 %copy-start.8 = (bf16[512,1024]{1,0:T(8,128)(2,1)S(1)}, bf16[512,1024]{1,0:T(8,128)(2,1)}, u32[]{:S(2)}) copy-start(bf16[512,1024]{1,0:T(8,128)(2,1)} %copy-done.7) | copy-start | bytes 3145732
  108.0 8.5 %collective-permute-start.8 = (bf16[512,128]{1,0:T(8,128)(2,1)S(1)}, bf16[512,128]{1,0:T(8,128)(2,1)S(1)}, u32[]{:S(2)}, u32[]{:S(2)}) collective-permute-start(bf16[512,128]{1,0:T(8,128)(2,1)S(1)} %get-tuple-element.21), channel_id=1, source_target_pairs={{12,0},{0,4},{4,8},{8,12},{13,1},{1,5},{5,9},{9,13},{14,2},{2,6},{... | collective-permute-start | bytes 393224 | tf_op jit(solution)/shard_map/ppermute | solution.py:154
  110.0 8.1 %collective-permute-start.9 = (bf16[512,128]{1,0:T(8,128)(2,1)S(1)}, bf16[512,128]{1,0:T(8,128)(2,1)S(1)}, u32[]{:S(2)}, u32[]{:S(2)}) collective-permute-start(bf16[512,128]{1,0:T(8,128)(2,1)S(1)} %get-tuple-element.22), channel_id=1, source_target_pairs={{8,0},{12,4},{0,8},{4,12},{9,1},{13,5},{1,9},{5,13},{10,2},{14,6},... | collective-permute-start | bytes 393224 | tf_op jit(solution)/shard_map/ppermute | solution.py:154
  113.5 5.0 %collective-permute-start.10 = (bf16[512,128]{1,0:T(8,128)(2,1)S(1)}, bf16[512,128]{1,0:T(8,128)(2,1)S(1)}, u32[]{:S(2)}, u32[]{:S(2)}) collective-permute-start(bf16[512,128]{1,0:T(8,128)(2,1)S(1)} %get-tuple-element.23), channel_id=1, source_target_pairs={{4,0},{8,4},{12,8},{0,12},{5,1},{9,5},{13,9},{1,13},{6,2},{10,6},{... | collective-permute-start | bytes 393224 | tf_op jit(solution)/shard_map/ppermute | solution.py:154
  118.6 1.6 collective-permute-start.11
  120.3 12.6 %collective-permute-start.14 = (bf16[256,128]{1,0:T(8,128)(2,1)S(1)}, bf16[256,128]{1,0:T(8,128)(2,1)S(1)}, u32[]{:S(2)}, u32[]{:S(2)}) collective-permute-start(bf16[256,128]{1,0:T(8,128)(2,1)S(1)} %get-tuple-element.33), channel_id=1, source_target_pairs={{0,80},{16,64},{64,16},{80,0},{1,81},{17,65},{65,17},{81,1},{2,82}... | collective-permute-start | bytes 196616 | tf_op jit(solution)/shard_map/ppermute | solution.py:207
  123.5 9.4 %collective-permute-start.12 = (bf16[256,128]{1,0:T(8,128)(2,1)S(1)}, bf16[256,128]{1,0:T(8,128)(2,1)S(1)}, u32[]{:S(2)}, u32[]{:S(2)}) collective-permute-start(bf16[256,128]{1,0:T(8,128)(2,1)S(1)} %get-tuple-element.33), channel_id=1, source_target_pairs={{0,16},{16,0},{1,17},{17,1},{2,18},{18,2},{3,19},{19,3},{4,20},{20... | collective-permute-start | bytes 196616 | tf_op jit(solution)/shard_map/ppermute | solution.py:150
  123.7 9.1 %collective-permute-start.13 = (bf16[256,128]{1,0:T(8,128)(2,1)S(1)}, bf16[256,128]{1,0:T(8,128)(2,1)S(1)}, u32[]{:S(2)}, u32[]{:S(2)}) collective-permute-start(bf16[256,128]{1,0:T(8,128)(2,1)S(1)} %get-tuple-element.32), channel_id=1, source_target_pairs={{0,64},{64,0},{1,65},{65,1},{2,66},{66,2},{3,67},{67,3},{4,68},{68... | collective-permute-start | bytes 196616 | tf_op jit(solution)/shard_map/ppermute | solution.py:150
  131.5 1.4 copy-start.2
  (6 other events, 5.8 us)

commit v19 on v18

--- a/solution.py
+++ b/solution.py
@@ -19,7 +19,7 @@
 
 
 def params():
-    return pltpu.CompilerParams(vmem_limit_bytes=6 << 20)
+    return pltpu.CompilerParams(vmem_limit_bytes=12 << 20)
 
 
 def pack_kernel(z_ref, float_ref, quant_ref, out_ref):
@@ -76,7 +76,10 @@
         project_kernel,
         out_shape=jax.ShapeDtypeStruct((rows, cols), BF16),
         grid=(rows // step,),
-        in_specs=[pl.BlockSpec((step, acts.shape[1]), lambda i: (i, 0))] + [WHOLE] * len(weights)
+        in_specs=[pl.BlockSpec((step, acts.shape[1]), lambda i: (i, 0))]
+        + [
+            pl.BlockSpec(w.shape, lambda i: (0, 0), pipeline_mode=pl.Buffered(1)) for w in weights
+        ]
         + [LEFT] * len(after),
         out_specs=pl.BlockSpec((step, cols), lambda i: (i, 0)),
         compiler_params=params(),
@@ -198,7 +201,7 @@
     total = blocks[0]
     for j in (1, 2, 3):
         total = total + ahead(blocks[j], "z", 4 - j).astype(F32)
-    second = project(acts, others, (total,))
+    second = project(acts, others, (blocks[0],))
     total = (total + swap(total, "core")) * inverse
     here, there = total[:features].astype(BF16), total[features:].astype(BF16)
     moved = (

time: 170 us -> 170 us (level)
  no operation moved by 1% of the time
where the time goes in v19:
time: 170 us
  waiting for transfers between devices  63.6 us (37%)
  blocking collectives  34.3 us (20%)
  starting transfers between devices  32 us (19%)
  Pallas kernels  19.8 us (12%)
  local copies, waits for them, and re-layouts  15.5 us (9%)
  other arithmetic  3.74 us (2%)
    ppermute x6, waiting for transfers between devices, ahead(): return lax.ppermute(a, axis, [((i + j) % 4, i) for i in range(4)])  46.9 us
    all_to_all x1, blocking collectives, output(): lax.all_to_all(p.reshape(16, tokens, quarter), PLANE, 0, 0, tiled=True)  34.3 us
    unnamed x42, local copies, waits for them, and re-layouts  15.4 us
    pallas_call x2, Pallas kernels, project(): pl.pallas_call(project_kernel, out_shape=jax.ShapeDtypeStruct((rows, cols...  13.7 us
    ppermute x6, starting transfers between devices, ahead(): return lax.ppermute(a, axis, [((i + j) % 4, i) for i in range(4)])  13.2 us
    all_to_all x1, waiting for transfers between devices, shards(): lax.all_to_all(payload, PLANE, 0, 0, tiled=True).reshape(16 * tokens, -1)  9.02 us
    all_to_all x1, starting transfers between devices, shards(): lax.all_to_all(payload, PLANE, 0, 0, tiled=True).reshape(16 * tokens, -1)  7.16 us
    ppermute x1, waiting for transfers between devices, shards(): got = lax.ppermute(send, ('yh', 'core', 'yl'), pairs)  5.1 us
  transfers between devices with their start and end apart: 17, of which 11 were waited for; matrix products, arithmetic and copies ran while one was open for 1% of the time, Pallas kernels for 6%

profile of v19, /device:TPU:0, one launch (start us, length us, event | category | flops | bytes accessed | tf_op | source)
XLA Modules:
  0.0 169.8 jit_solution(5639372876452500787)
XLA Ops:
  1.4 1.6 fusion.2
  3.0 1.7 %collective-permute-start = (bf16[256,1024]{1,0:T(8,128)(2,1)S(1)}, bf16[256,1024]{1,0:T(8,128)(2,1)S(1)}, u32[]{:S(2)}, u32[]{:S(2)}) collective-permute-start(bf16[256,1024]{1,0:T(8,128)(2,1)S(1)} %fusion.2), channel_id=1, source_target_pairs={{0,16},{16,0},{32,112},{48,96},{64,80},{80,64},{96,48},{112,32},{1... | collective-permute-start | bytes 1572872 | tf_op jit(solution)/shard_map/ppermute | solution.py:182
  5.0 2.1 %copy-done.1 = bf16[16,64,2176]{2,1,0:T(8,128)(2,1)} copy-done((bf16[16,64,2176]{2,1,0:T(8,128)(2,1)}, bf16[16,64,2176]{2,1,0:T(8,128)(2,1)S(1)}, u32[]{:S(2)}) %copy-start.1) | copy-done | bytes 4456472
  7.1 5.1 %collective-permute-done = bf16[256,1024]{1,0:T(8,128)(2,1)S(1)} collective-permute-done((bf16[256,1024]{1,0:T(8,128)(2,1)S(1)}, bf16[256,1024]{1,0:T(8,128)(2,1)S(1)}, u32[]{:S(2)}, u32[]{:S(2)}) %collective-permute-start) | collective-permute-done | bytes 524320 | tf_op jit(solution)/shard_map/ppermute | solution.py:182
  12.2 7.2 %all-to-all-start = ((bf16[16,64,2176]{2,1,0:T(8,128)(2,1)}), bf16[16,64,2176]{2,1,0:T(8,128)(2,1)}, u32[]{:S(2)}, u32[]{:S(2)}) async-start(bf16[16,64,2176]{2,1,0:T(8,128)(2,1)} %copy-done.1), calls=%async_computation | async-start | bytes 8912896 | tf_op jit(solution)/shard_map/all_to_all | solution.py:191
  19.5 1.9 %fusion.3 = bf16[256,1024]{1,0:T(8,128)(2,1)S(1)} fusion(s32[256,4096]{1,0:T(8,128)} %param.8, s32[]{:T(128)S(6)} %select_n.28, f32[2,1024]{1,0:T(2,128)S(1)} %constant_dynamic-slice_fusion, bf16[256,4096]{1,0:T(8,128)(2,1)} %param.7, pred[]{:T(512)S(6)} %eq.7), kind=kLoop, calls=%fused_computation.6 | loop fusion | flops 1310720 | bytes 2105349 | tf_op jit(solution)/shard_map/jit(_where)/select_n | solution.py:174
  21.5 2.0 %collective-permute-start.6 = (bf16[512,1024]{1,0:T(8,128)(2,1)S(1)}, bf16[512,1024]{1,0:T(8,128)(2,1)S(1)}, u32[]{:S(2)}, u32[]{:S(2)}) collective-permute-start(bf16[512,1024]{1,0:T(8,128)(2,1)S(1)} %pad_maximum_fusion.refs_0_), channel_id=1, source_target_pairs={{12,0},{0,4},{4,8},{8,12},{13,1},{1,5},{5,9},{9,13},{14,2},{2,6},{... | collective-permute-start | bytes 3145736 | tf_op jit(solution)/shard_map/ppermute | solution.py:157
  23.5 3.6 %collective-permute-start.4 = (bf16[512,1024]{1,0:T(8,128)(2,1)S(1)}, bf16[512,1024]{1,0:T(8,128)(2,1)S(1)}, u32[]{:S(2)}, u32[]{:S(2)}) collective-permute-start(bf16[512,1024]{1,0:T(8,128)(2,1)S(1)} %pad_maximum_fusion.refs_0_), channel_id=1, source_target_pairs={{8,0},{12,4},{0,8},{4,12},{9,1},{13,5},{1,9},{5,13},{10,2},{14,6},... | collective-permute-start | bytes 3145736 | tf_op jit(solution)/shard_map/ppermute | solution.py:157
  28.1 20.7 %collective-permute-done.6.refs_3_ = bf16[512,1024]{1,0:T(8,128)(2,1)S(1)} collective-permute-done((bf16[512,1024]{1,0:T(8,128)(2,1)S(1)}, bf16[512,1024]{1,0:T(8,128)(2,1)S(1)}, u32[]{:S(2)}, u32[]{:S(2)}) %collective-permute-start.6) | collective-permute-done | bytes 1048608 | tf_op jit(solution)/shard_map/ppermute | solution.py:157
  49.8 22.2 %collective-permute-done.4.refs_2_ = bf16[512,1024]{1,0:T(8,128)(2,1)S(1)} collective-permute-done((bf16[512,1024]{1,0:T(8,128)(2,1)S(1)}, bf16[512,1024]{1,0:T(8,128)(2,1)S(1)}, u32[]{:S(2)}, u32[]{:S(2)}) %collective-permute-start.4) | collective-permute-done | bytes 1048608 | tf_op jit(solution)/shard_map/ppermute | solution.py:157
  72.0 1.1 copy-done.17
  74.7 1.0 copy-done.9
  77.2 9.0 %all-to-all-done = bf16[16,64,2176]{2,1,0:T(8,128)(2,1)} async-done(((bf16[16,64,2176]{2,1,0:T(8,128)(2,1)}), bf16[16,64,2176]{2,1,0:T(8,128)(2,1)}, u32[]{:S(2)}, u32[]{:S(2)}) %all-to-all-start) | async-done | bytes 4456480 | tf_op jit(solution)/shard_map/all_to_all | solution.py:191
  86.2 1.2 copy-done.10
  87.4 1.2 copy-done.13
  88.6 1.2 copy-done.16
  89.9 1.2 copy-done.18
  91.1 1.2 copy-done.20
  92.3 7.3 %project.2.after_ref = bf16[1024,1024]{1,0:T(8,128)(2,1)} custom-call(bf16[1024,2176]{1,0:T(8,128)(2,1)} %bitcast.5.acts_ref, bf16[512,1024]{1,0:T(8,128)(2,1)S(1)} %pad_maximum_fusion.refs_0_, bf16[512,1024]{1,0:T(8,128)(2,1)S(1)} %copy-done.20, bf16[512,1024]{1,0:T(8,128)(2,1)S(1)} %copy-done.18, bf16[512,1024]{1,0:T(8,128)(2,1)S(1)} %copy-done.16, ...), custom_call_target="tpu_custom_call" | custom-call | flops 4294967296 | bytes 12582912 | tf_op jit(solution)/shard_map/project/pallas_call | solution.py:75
  99.6 4.6 %all-to-all-start.1 = ((bf16[16,64,1024]{2,1,0:T(8,128)(2,1)}), bf16[16,64,1024]{2,1,0:T(8,128)(2,1)S(1)}, u32[]{:S(2)}, u32[]{:S(2)}) async-start(bf16[16,64,1024]{2,1,0:T(8,128)(2,1)} %bitcast.7), calls=%async_computation.1 | async-start | bytes 4194304 | tf_op jit(solution)/shard_map/all_to_all | solution.py:195
  104.2 3.7 %stats.1 = (f32[512,128]{1,0:T(8,128)S(1)}, bf16[512,128]{1,0:T(8,128)(2,1)S(1)}, bf16[512,128]{1,0:T(8,128)(2,1)S(1)}, bf16[512,128]{1,0:T(8,128)(2,1)S(1)}) custom-call(bf16[1024,2176]{1,0:T(8,128)(2,1)} %bitcast.5.acts_ref, bf16[1024,1024]{1,0:T(8,128)(2,1)} %project.2.after_ref), custom_call_target="tpu_custom_call" | custom-call | tf_op jit(solution)/shard_map/stats/pallas_call | solution.py:141
  108.0 2.0 %collective-permute-start.8 = (bf16[512,128]{1,0:T(8,128)(2,1)S(1)}, bf16[512,128]{1,0:T(8,128)(2,1)S(1)}, u32[]{:S(2)}, u32[]{:S(2)}) collective-permute-start(bf16[512,128]{1,0:T(8,128)(2,1)S(1)} %get-tuple-element.21), channel_id=1, source_target_pairs={{12,0},{0,4},{4,8},{8,12},{13,1},{1,5},{5,9},{9,13},{14,2},{2,6},{... | collective-permute-start | bytes 393224 | tf_op jit(solution)/shard_map/ppermute | solution.py:157
  110.0 3.6 %collective-permute-start.9 = (bf16[512,128]{1,0:T(8,128)(2,1)S(1)}, bf16[512,128]{1,0:T(8,128)(2,1)S(1)}, u32[]{:S(2)}, u32[]{:S(2)}) collective-permute-start(bf16[512,128]{1,0:T(8,128)(2,1)S(1)} %get-tuple-element.22), channel_id=1, source_target_pairs={{8,0},{12,4},{0,8},{4,12},{9,1},{13,5},{1,9},{5,13},{10,2},{14,6},... | collective-permute-start | bytes 393224 | tf_op jit(solution)/shard_map/ppermute | solution.py:157
  114.6 1.9 %collective-permute-done.8 = bf16[512,128]{1,0:T(8,128)(2,1)S(1)} collective-permute-done((bf16[512,128]{1,0:T(8,128)(2,1)S(1)}, bf16[512,128]{1,0:T(8,128)(2,1)S(1)}, u32[]{:S(2)}, u32[]{:S(2)}) %collective-permute-start.8) | collective-permute-done | bytes 131104 | tf_op jit(solution)/shard_map/ppermute | solution.py:157
  116.4 1.6 collective-permute-done.9
  118.7 1.4 collective-permute-done.11
  120.3 3.2 %collective-permute-start.14 = (bf16[256,128]{1,0:T(8,128)(2,1)S(1)}, bf16[256,128]{1,0:T(8,128)(2,1)S(1)}, u32[]{:S(2)}, u32[]{:S(2)}) collective-permute-start(bf16[256,128]{1,0:T(8,128)(2,1)S(1)} %get-tuple-element.33), channel_id=1, source_target_pairs={{0,80},{16,64},{64,16},{80,0},{1,81},{17,65},{65,17},{81,1},{2,82}... | collective-permute-start | bytes 196616 | tf_op jit(solution)/shard_map/ppermute | solution.py:210
  123.7 1.3 collective-permute-start.13
  125.0 6.4 %project.3 = bf16[1024,1024]{1,0:T(8,128)(2,1)S(1)} custom-call(bf16[1024,2176]{1,0:T(8,128)(2,1)} %bitcast.5.acts_ref, bf16[512,1024]{1,0:T(8,128)(2,1)S(1)} %copy-done.6, bf16[512,1024]{1,0:T(8,128)(2,1)S(1)} %copy-done.14, bf16[512,1024]{1,0:T(8,128)(2,1)S(1)} %copy-done.11, bf16[512,1024]{1,0:T(8,128)(2,1)S(1)} %copy-done.8, ...), custom_call_target="tpu_custom_call" | custom-call | flops 4294967296 | bytes 12582912 | tf_op jit(solution)/shard_map/project/pallas_call | solution.py:75
  131.5 1.4 copy-done.2
  133.4 34.3 %all_to_all.15.second_ref = bf16[16,64,1024]{2,1,0:T(8,128)(2,1)S(1)} all-to-all(bf16[16,64,1024]{2,1,0:T(8,128)(2,1)} %bitcast.19), channel_id=1, replica_groups=mesh['yh'=2,'core'=2,'yl'=2,'z'=4,'x'=4] {'yh','yl','x'}, dimensions={0} | all-to-all | bytes 4194304 | tf_op jit(solution)/shard_map/all_to_all | solution.py:195
  167.7 2.0 %finish.1 = (bf16[64,4096]{1,0:T(8,128)(2,1)}, bf16[64,4096]{1,0:T(8,128)(2,1)}, f32[256,128]{1,0:T(8,128)}, f32[256,128]{1,0:T(8,128)}) custom-call(s32[3]{0:T(128)S(1)} %pad_add_fusion.at_ref, bf16[16,64,1024]{2,1,0:T(8,128)(2,1)S(1)} %all-to-all-done.1.first_ref, bf16[16,64,1024]{2,1,0:T(8,128)(2,1)S(1)} %all_to_all.15.second_ref, ...), custom_call_target="tpu_custom_call" | custom-call | tf_op jit(solution)/shard_map/finish/pallas_call | solution.py:117
  (59 shorter events, 8.8 us)
Async XLA Ops:
  0.6 4.1 %copy-start.4 = (bf16[64,8192]{1,0:T(8,128)(2,1)S(1)}, bf16[64,8192]{1,0:T(8,128)(2,1)}, u32[]{:S(2)}) copy-start(bf16[64,8192]{1,0:T(8,128)(2,1)} %quant_ref.1) | copy-start | bytes 3145732
  0.7 4.0 %copy-start.3 = (bf16[64,8192]{1,0:T(8,128)(2,1)S(1)}, bf16[64,8192]{1,0:T(8,128)(2,1)}, u32[]{:S(2)}) copy-start(bf16[64,8192]{1,0:T(8,128)(2,1)} %float_ref.1) | copy-start | bytes 3145732
  3.0 9.3 %collective-permute-start = (bf16[256,1024]{1,0:T(8,128)(2,1)S(1)}, bf16[256,1024]{1,0:T(8,128)(2,1)S(1)}, u32[]{:S(2)}, u32[]{:S(2)}) collective-permute-start(bf16[256,1024]{1,0:T(8,128)(2,1)S(1)} %fusion.2), channel_id=1, source_target_pairs={{0,16},{16,0},{32,112},{48,96},{64,80},{80,64},{96,48},{112,32},{1... | collective-permute-start | bytes 1572872 | tf_op jit(solution)/shard_map/ppermute | solution.py:182
  5.0 2.1 %copy-start.1 = (bf16[16,64,2176]{2,1,0:T(8,128)(2,1)}, bf16[16,64,2176]{2,1,0:T(8,128)(2,1)S(1)}, u32[]{:S(2)}) copy-start(bf16[16,64,2176]{2,1,0:T(8,128)(2,1)S(1)} %pack.1) | copy-start | bytes 13369348
  12.2 74.0 %all-to-all-start = ((bf16[16,64,2176]{2,1,0:T(8,128)(2,1)}), bf16[16,64,2176]{2,1,0:T(8,128)(2,1)}, u32[]{:S(2)}, u32[]{:S(2)}) async-start(bf16[16,64,2176]{2,1,0:T(8,128)(2,1)} %copy-done.1), calls=%async_computation | async-start | bytes 8912896 | tf_op jit(solution)/shard_map/all_to_all | solution.py:191
  21.5 27.3 %collective-permute-start.6 = (bf16[512,1024]{1,0:T(8,128)(2,1)S(1)}, bf16[512,1024]{1,0:T(8,128)(2,1)S(1)}, u32[]{:S(2)}, u32[]{:S(2)}) collective-permute-start(bf16[512,1024]{1,0:T(8,128)(2,1)S(1)} %pad_maximum_fusion.refs_0_), channel_id=1, source_target_pairs={{12,0},{0,4},{4,8},{8,12},{13,1},{1,5},{5,9},{9,13},{14,2},{2,6},{... | collective-permute-start | bytes 3145736 | tf_op jit(solution)/shard_map/ppermute | solution.py:157
  23.5 48.5 %collective-permute-start.4 = (bf16[512,1024]{1,0:T(8,128)(2,1)S(1)}, bf16[512,1024]{1,0:T(8,128)(2,1)S(1)}, u32[]{:S(2)}, u32[]{:S(2)}) collective-permute-start(bf16[512,1024]{1,0:T(8,128)(2,1)S(1)} %pad_maximum_fusion.refs_0_), channel_id=1, source_target_pairs={{8,0},{12,4},{0,8},{4,12},{9,1},{13,5},{1,9},{5,13},{10,2},{14,6},... | collective-permute-start | bytes 3145736 | tf_op jit(solution)/shard_map/ppermute | solution.py:157
  27.1 46.0 %collective-permute-start.2 = (bf16[512,1024]{1,0:T(8,128)(2,1)S(1)}, bf16[512,1024]{1,0:T(8,128)(2,1)S(1)}, u32[]{:S(2)}, u32[]{:S(2)}) collective-permute-start(bf16[512,1024]{1,0:T(8,128)(2,1)S(1)} %pad_maximum_fusion.refs_0_), channel_id=1, source_target_pairs={{4,0},{8,4},{12,8},{0,12},{5,1},{9,5},{13,9},{1,13},{6,2},{10,6},{... | collective-permute-start | bytes 3145736 | tf_op jit(solution)/shard_map/ppermute | solution.py:157
  28.1 46.5 %collective-permute-start.1 = (bf16[512,1024]{1,0:T(8,128)(2,1)S(1)}, bf16[512,1024]{1,0:T(8,128)(2,1)S(1)}, u32[]{:S(2)}, u32[]{:S(2)}) collective-permute-start(bf16[512,1024]{1,0:T(8,128)(2,1)S(1)} %pad_maximum_fusion.refs_0_), channel_id=1, source_target_pairs={{0,32},{32,0},{1,33},{33,1},{2,34},{34,2},{3,35},{35,3},{4,36},{36... | collective-permute-start | bytes 3145736 | tf_op jit(solution)/shard_map/ppermute | solution.py:153
  48.8 25.8 %collective-permute-start.7 = (bf16[512,1024]{1,0:T(8,128)(2,1)S(1)}, bf16[512,1024]{1,0:T(8,128)(2,1)S(1)}, u32[]{:S(2)}, u32[]{:S(2)}) collective-permute-start(bf16[512,1024]{1,0:T(8,128)(2,1)S(1)} %collective-permute-done.6.refs_3_), channel_id=1, source_target_pairs={{0,32},{32,0},{1,33},{33,1},{2,34},{34,2},{3,35},{35,3},{4,36},{36... | collective-permute-start | bytes 3145736 | tf_op jit(solution)/shard_map/ppermute | solution.py:153
  72.0 2.7 %collective-permute-start.5 = (bf16[512,1024]{1,0:T(8,128)(2,1)S(1)}, bf16[512,1024]{1,0:T(8,128)(2,1)S(1)}, u32[]{:S(2)}, u32[]{:S(2)}) collective-permute-start(bf16[512,1024]{1,0:T(8,128)(2,1)S(1)} %collective-permute-done.4.refs_2_), channel_id=1, source_target_pairs={{0,32},{32,0},{1,33},{33,1},{2,34},{34,2},{3,35},{35,3},{4,36},{36... | collective-permute-start | bytes 3145736 | tf_op jit(solution)/shard_map/ppermute | solution.py:153
  73.1 3.1 %collective-permute-start.3 = (bf16[512,1024]{1,0:T(8,128)(2,1)S(1)}, bf16[512,1024]{1,0:T(8,128)(2,1)S(1)}, u32[]{:S(2)}, u32[]{:S(2)}) collective-permute-start(bf16[512,1024]{1,0:T(8,128)(2,1)S(1)} %collective-permute-done.2.refs_1_), channel_id=1, source_target_pairs={{0,32},{32,0},{1,33},{33,1},{2,34},{34,2},{3,35},{35,3},{4,36},{36... | collective-permute-start | bytes 3145736 | tf_op jit(solution)/shard_map/ppermute | solution.py:153
  74.6 25.0 %copy-start.5 = (bf16[512,1024]{1,0:T(8,128)(2,1)}, bf16[512,1024]{1,0:T(8,128)(2,1)S(1)}, u32[]{:S(2)}) copy-start(bf16[512,1024]{1,0:T(8,128)(2,1)S(1)} %collective-permute-done.1.refs_4_.refs_0_) | copy-start | bytes 3145732
  74.6 25.0 %copy-start.7 = (bf16[512,1024]{1,0:T(8,128)(2,1)}, bf16[512,1024]{1,0:T(8,128)(2,1)S(1)}, u32[]{:S(2)}) copy-start(bf16[512,1024]{1,0:T(8,128)(2,1)S(1)} %collective-permute-done.7.refs_7_.refs_3_) | copy-start | bytes 3145732
  86.2 1.2 copy-start.10
  87.4 1.2 copy-start.13
  88.6 1.2 copy-start.16
  89.9 1.2 copy-start.18
  91.1 1.2 copy-start.20
  99.6 33.8 %all-to-all-start.1 = ((bf16[16,64,1024]{2,1,0:T(8,128)(2,1)}), bf16[16,64,1024]{2,1,0:T(8,128)(2,1)S(1)}, u32[]{:S(2)}, u32[]{:S(2)}) async-start(bf16[16,64,1024]{2,1,0:T(8,128)(2,1)} %bitcast.7), calls=%async_computation.1 | async-start | bytes 4194304 | tf_op jit(solution)/shard_map/all_to_all | solution.py:195
  104.2 20.8 %copy-start.11 = (bf16[512,1024]{1,0:T(8,128)(2,1)S(1)}, bf16[512,1024]{1,0:T(8,128)(2,1)}, u32[]{:S(2)}) copy-start(bf16[512,1024]{1,0:T(8,128)(2,1)} %copy-done.9) | copy-start | bytes 3145732
  104.2 20.8 %copy-start.14 = (bf16[512,1024]{1,0:T(8,128)(2,1)S(1)}, bf16[512,1024]{1,0:T(8,128)(2,1)}, u32[]{:S(2)}) copy-start(bf16[512,1024]{1,0:T(8,128)(2,1)} %copy-done.12) | copy-start | bytes 3145732
  108.0 17.1 %copy-start.6 = (bf16[512,1024]{1,0:T(8,128)(2,1)S(1)}, bf16[512,1024]{1,0:T(8,128)(2,1)}, u32[]{:S(2)}) copy-start(bf16[512,1024]{1,0:T(8,128)(2,1)} %copy-done.5) | copy-start | bytes 3145732
  108.0 17.1 %copy-start.8 = (bf16[512,1024]{1,0:T(8,128)(2,1)S(1)}, bf16[512,1024]{1,0:T(8,128)(2,1)}, u32[]{:S(2)}) copy-start(bf16[512,1024]{1,0:T(8,128)(2,1)} %copy-done.7) | copy-start | bytes 3145732
  108.0 8.5 %collective-permute-start.8 = (bf16[512,128]{1,0:T(8,128)(2,1)S(1)}, bf16[512,128]{1,0:T(8,128)(2,1)S(1)}, u32[]{:S(2)}, u32[]{:S(2)}) collective-permute-start(bf16[512,128]{1,0:T(8,128)(2,1)S(1)} %get-tuple-element.21), channel_id=1, source_target_pairs={{12,0},{0,4},{4,8},{8,12},{13,1},{1,5},{5,9},{9,13},{14,2},{2,6},{... | collective-permute-start | bytes 393224 | tf_op jit(solution)/shard_map/ppermute | solution.py:157
  110.0 8.1 %collective-permute-start.9 = (bf16[512,128]{1,0:T(8,128)(2,1)S(1)}, bf16[512,128]{1,0:T(8,128)(2,1)S(1)}, u32[]{:S(2)}, u32[]{:S(2)}) collective-permute-start(bf16[512,128]{1,0:T(8,128)(2,1)S(1)} %get-tuple-element.22), channel_id=1, source_target_pairs={{8,0},{12,4},{0,8},{4,12},{9,1},{13,5},{1,9},{5,13},{10,2},{14,6},... | collective-permute-start | bytes 393224 | tf_op jit(solution)/shard_map/ppermute | solution.py:157
  113.5 5.0 %collective-permute-start.10 = (bf16[512,128]{1,0:T(8,128)(2,1)S(1)}, bf16[512,128]{1,0:T(8,128)(2,1)S(1)}, u32[]{:S(2)}, u32[]{:S(2)}) collective-permute-start(bf16[512,128]{1,0:T(8,128)(2,1)S(1)} %get-tuple-element.23), channel_id=1, source_target_pairs={{4,0},{8,4},{12,8},{0,12},{5,1},{9,5},{13,9},{1,13},{6,2},{10,6},{... | collective-permute-start | bytes 393224 | tf_op jit(solution)/shard_map/ppermute | solution.py:157
  118.6 1.6 collective-permute-start.11
  120.3 12.6 %collective-permute-start.14 = (bf16[256,128]{1,0:T(8,128)(2,1)S(1)}, bf16[256,128]{1,0:T(8,128)(2,1)S(1)}, u32[]{:S(2)}, u32[]{:S(2)}) collective-permute-start(bf16[256,128]{1,0:T(8,128)(2,1)S(1)} %get-tuple-element.33), channel_id=1, source_target_pairs={{0,80},{16,64},{64,16},{80,0},{1,81},{17,65},{65,17},{81,1},{2,82}... | collective-permute-start | bytes 196616 | tf_op jit(solution)/shard_map/ppermute | solution.py:210
  123.5 9.4 %collective-permute-start.12 = (bf16[256,128]{1,0:T(8,128)(2,1)S(1)}, bf16[256,128]{1,0:T(8,128)(2,1)S(1)}, u32[]{:S(2)}, u32[]{:S(2)}) collective-permute-start(bf16[256,128]{1,0:T(8,128)(2,1)S(1)} %get-tuple-element.33), channel_id=1, source_target_pairs={{0,16},{16,0},{1,17},{17,1},{2,18},{18,2},{3,19},{19,3},{4,20},{20... | collective-permute-start | bytes 196616 | tf_op jit(solution)/shard_map/ppermute | solution.py:153
  123.7 9.1 %collective-permute-start.13 = (bf16[256,128]{1,0:T(8,128)(2,1)S(1)}, bf16[256,128]{1,0:T(8,128)(2,1)S(1)}, u32[]{:S(2)}, u32[]{:S(2)}) collective-permute-start(bf16[256,128]{1,0:T(8,128)(2,1)S(1)} %get-tuple-element.32), channel_id=1, source_target_pairs={{0,64},{64,0},{1,65},{65,1},{2,66},{66,2},{3,67},{67,3},{4,68},{68... | collective-permute-start | bytes 196616 | tf_op jit(solution)/shard_map/ppermute | solution.py:153
  131.5 1.4 copy-start.2
  (6 other events, 5.8 us)

commit v20 on v18

--- a/solution.py
+++ b/solution.py
@@ -19,7 +19,7 @@
 
 
 def params():
-    return pltpu.CompilerParams(vmem_limit_bytes=6 << 20)
+    return pltpu.CompilerParams(vmem_limit_bytes=16 << 20)
 
 
 def pack_kernel(z_ref, float_ref, quant_ref, out_ref):
@@ -53,38 +53,30 @@
     )(z.reshape(1), attn_float, attn_quant)
 
 
-def project_kernel(acts_ref, *refs):
-    weights, out_ref = refs[:4], refs[-1]
-    depth, width = weights[0].shape
+def project_kernel(acts_ref, weight_ref, out_ref):
+    depth, width = weight_ref.shape
     tile = 512
     for col in range(0, width, tile):
-        total = None
-        for j, ref in enumerate(weights):
-            term = jnp.dot(
-                acts_ref[:, j * depth : (j + 1) * depth],
-                ref[:, col : col + tile],
-                preferred_element_type=F32,
-            )
-            total = term if total is None else total + term
-        out_ref[:, col : col + tile] = total.astype(BF16)
-
-
-def project(acts, weights, after):
-    rows, cols = acts.shape[0], weights[0].shape[1]
+        out_ref[:, col : col + tile] = jnp.dot(
+            acts_ref[:, :depth], weight_ref[:, col : col + tile], preferred_element_type=F32
+        ).astype(BF16)
+
+
+def project(acts, weight):
+    rows, (depth, cols) = acts.shape[0], weight.shape
     step = 256
     return pl.pallas_call(
         project_kernel,
         out_shape=jax.ShapeDtypeStruct((rows, cols), BF16),
         grid=(rows // step,),
-        in_specs=[pl.BlockSpec((step, acts.shape[1]), lambda i: (i, 0))] + [WHOLE] * len(weights)
-        + [LEFT] * len(after),
+        in_specs=[pl.BlockSpec((step, acts.shape[1]), lambda i: (i, 0)), WHOLE],
         out_specs=pl.BlockSpec((step, cols), lambda i: (i, 0)),
         compiler_params=params(),
         cost_estimate=pl.CostEstimate(
-            flops=2 * rows * 2048 * cols, bytes_accessed=12 << 20, transcendentals=0
+            flops=2 * rows * depth * cols, bytes_accessed=12 << 20, transcendentals=0
         ),
         name="project",
-    )(acts, *weights, *after)
+    )(acts, weight)
 
 
 def finish_kernel(at_ref, first_ref, second_ref, total_ref, *refs):
@@ -186,19 +178,20 @@
     parts = [rows] + [ahead(rows, "z", j) for j in (1, 2, 3)]
 
     acts = lax.all_to_all(payload, PLANE, 0, 0, tiled=True).reshape(16 * tokens, -1)
-    others = [swap(p, "core") for p in parts]
+    mine = jnp.concatenate(parts, axis=0)
+    other = swap(mine, "core")
 
     def output(p):
         return lax.all_to_all(p.reshape(16, tokens, quarter), PLANE, 0, 0, tiled=True)
 
-    first = project(acts, parts, others)
+    first = project(acts, mine)
     result1 = output(first)
 
     blocks = stats(acts, first)
     total = blocks[0]
     for j in (1, 2, 3):
         total = total + ahead(blocks[j], "z", 4 - j).astype(F32)
-    second = project(acts, others, (total,))
+    second = project(acts, other)
     total = (total + swap(total, "core")) * inverse
     here, there = total[:features].astype(BF16), total[features:].astype(BF16)
     moved = (

time: 170 us -> 167 us (0.982)
  local copies, waits for them, and re-layouts: 15.5 us -> 10.7 us
  starting transfers between devices: 32 us -> 29 us
  Pallas kernels: 19.8 us -> 22.1 us
    unnamed x42 -> x13, local copies, waits for them, and re-layouts: 15.4 us -> 9.53 us
    ppermute x6, waiting for transfers between devices: 46.9 us -> 50 us  [ahead(): return lax.ppermute(a, axis, [((i + j) % 4, i) for i in range(4)])]
    unnamed x0 -> x1, other arithmetic: none -> 2.71 us
    pallas_call x2, Pallas kernels: 13.7 us -> 16.2 us  [project(): pl.pallas_call(project_kernel, out_shape=jax.ShapeDtypeStruct((rows, cols...]
    ppermute x6, starting transfers between devices: 13.2 us -> 10.7 us  [ahead(): return lax.ppermute(a, axis, [((i + j) % 4, i) for i in range(4)])]
    ppermute x1, waiting for transfers between devices: 5.1 us -> 2.68 us  [shards(): got = lax.ppermute(send, ('yh', 'core', 'yl'), pairs)]
    select_n x2 -> x1, other arithmetic: 3.5 us -> 1.56 us  [weight(): return jnp.where(kind == 0, plain, quant)]
    all_to_all x1, waiting for transfers between devices: 9.02 us -> 10.9 us  [shards(): lax.all_to_all(payload, PLANE, 0, 0, tiled=True).reshape(16 * tokens, -1)]
  transfers between devices with their start and end apart: 17 -> 14, of which waited for: 11 -> 8; matrix products, arithmetic and copies ran while one was open for 1% -> 4% of each run, Pallas kernels for 6% -> 12%
where the time goes in v20:
time: 167 us
  waiting for transfers between devices  65 us (39%)
  blocking collectives  34.7 us (21%)
  starting transfers between devices  29 us (17%)
  Pallas kernels  22.1 us (13%)
  local copies, waits for them, and re-layouts  10.7 us (6%)
  other arithmetic  4.52 us (3%)
    ppermute x6, waiting for transfers between devices, ahead(): return lax.ppermute(a, axis, [((i + j) % 4, i) for i in range(4)])  50 us
    all_to_all x1, blocking collectives, output(): lax.all_to_all(p.reshape(16, tokens, quarter), PLANE, 0, 0, tiled=True)  34.7 us
    pallas_call x2, Pallas kernels, project(): pl.pallas_call(project_kernel, out_shape=jax.ShapeDtypeStruct((rows, cols...  16.2 us
    all_to_all x1, waiting for transfers between devices, shards(): lax.all_to_all(payload, PLANE, 0, 0, tiled=True).reshape(16 * tokens, -1)  10.9 us
    ppermute x6, starting transfers between devices, ahead(): return lax.ppermute(a, axis, [((i + j) % 4, i) for i in range(4)])  10.7 us
    unnamed x13, local copies, waits for them, and re-layouts  9.53 us
    all_to_all x1, starting transfers between devices, shards(): lax.all_to_all(payload, PLANE, 0, 0, tiled=True).reshape(16 * tokens, -1)  7.16 us
    all_to_all x1, starting transfers between devices, output(): lax.all_to_all(p.reshape(16, tokens, quarter), PLANE, 0, 0, tiled=True)  4.6 us
  transfers between devices with their start and end apart: 14, of which 8 were waited for; matrix products, arithmetic and copies ran while one was open for 4% of the time, Pallas kernels for 12%

profile of v20, /device:TPU:0, one launch (start us, length us, event | category | flops | bytes accessed | tf_op | source)
XLA Modules:
  0.0 166.7 jit_solution(8688401010986013700)
XLA Ops:
  1.4 1.6 fusion.2
  3.0 1.7 %collective-permute-start = (bf16[256,1024]{1,0:T(8,128)(2,1)S(1)}, bf16[256,1024]{1,0:T(8,128)(2,1)S(1)}, u32[]{:S(2)}, u32[]{:S(2)}) collective-permute-start(bf16[256,1024]{1,0:T(8,128)(2,1)S(1)} %fusion.2), channel_id=1, source_target_pairs={{0,16},{16,0},{32,112},{48,96},{64,80},{80,64},{96,48},{112,32},{1... | collective-permute-start | bytes 1572872 | tf_op jit(solution)/shard_map/ppermute | solution.py:171
  4.7 1.2 copy-done.3
  5.9 1.2 copy-done.4
  7.5 2.1 %copy-done.1 = bf16[16,64,2176]{2,1,0:T(8,128)(2,1)} copy-done((bf16[16,64,2176]{2,1,0:T(8,128)(2,1)}, bf16[16,64,2176]{2,1,0:T(8,128)(2,1)S(1)}, u32[]{:S(2)}) %copy-start.1) | copy-done | bytes 4456472
  9.5 2.7 %collective-permute-done = bf16[256,1024]{1,0:T(8,128)(2,1)S(1)} collective-permute-done((bf16[256,1024]{1,0:T(8,128)(2,1)S(1)}, bf16[256,1024]{1,0:T(8,128)(2,1)S(1)}, u32[]{:S(2)}, u32[]{:S(2)}) %collective-permute-start) | collective-permute-done | bytes 524320 | tf_op jit(solution)/shard_map/ppermute | solution.py:171
  12.2 7.2 %all-to-all-start = ((bf16[16,64,2176]{2,1,0:T(8,128)(2,1)}), bf16[16,64,2176]{2,1,0:T(8,128)(2,1)}, u32[]{:S(2)}, u32[]{:S(2)}) async-start(bf16[16,64,2176]{2,1,0:T(8,128)(2,1)} %copy-done.1), calls=%async_computation | async-start | bytes 8912896 | tf_op jit(solution)/shard_map/all_to_all | solution.py:180
  19.5 2.7 %constant_dynamic-update-slice_fusion.4 = (bf16[2048,1024]{1,0:T(8,128)(2,1)}, bf16[256,1024]{1,0:T(8,128)(2,1)S(1)}) fusion(f32[2,1024]{1,0:T(2,128)S(1)} %constant_dynamic-slice_fusion, s32[256,4096]{1,0:T(8,128)} %param.8, s32[]{:T(128)S(6)} %select_n.28, bf16[256,4096]{1,0:T(8,128)(2,1)} %param.7, pred[]{:T(512)S(6)} %eq.7), kind=kLoop, calls=%fused_computation.13 | loop fusion | flops 1310719 | bytes 2629637
  22.3 4.1 %collective-permute-start.1 = (bf16[512,1024]{1,0:T(8,128)(2,1)S(1)}, bf16[512,1024]{1,0:T(8,128)(2,1)S(1)}, u32[]{:S(2)}, u32[]{:S(2)}) collective-permute-start(bf16[512,1024]{1,0:T(8,128)(2,1)S(1)} %pad_maximum_fusion), channel_id=1, source_target_pairs={{4,0},{8,4},{12,8},{0,12},{5,1},{9,5},{13,9},{1,13},{6,2},{10,6},{... | collective-permute-start | bytes 3145736 | tf_op jit(solution)/shard_map/ppermute | solution.py:146
  26.4 1.3 collective-permute-start.3
  27.6 0.8 constant_dynamic-update-slice_fusion.3
  28.5 42.4 %collective-permute-done.1 = bf16[512,1024]{1,0:T(8,128)(2,1)S(1)} collective-permute-done((bf16[512,1024]{1,0:T(8,128)(2,1)S(1)}, bf16[512,1024]{1,0:T(8,128)(2,1)S(1)}, u32[]{:S(2)}, u32[]{:S(2)}) %collective-permute-start.1) | collective-permute-done | bytes 1048608 | tf_op jit(solution)/shard_map/ppermute | solution.py:146
  70.9 1.0 constant_dynamic-update-slice_fusion.2
  71.9 1.1 constant_dynamic-update-slice_fusion.1
  73.0 1.3 collective-permute-done.3
  74.3 1.0 constant_dynamic-update-slice_fusion.weight_ref
  75.3 10.9 %all-to-all-done = bf16[16,64,2176]{2,1,0:T(8,128)(2,1)} async-done(((bf16[16,64,2176]{2,1,0:T(8,128)(2,1)}), bf16[16,64,2176]{2,1,0:T(8,128)(2,1)}, u32[]{:S(2)}, u32[]{:S(2)}) %all-to-all-start) | async-done | bytes 4456480 | tf_op jit(solution)/shard_map/all_to_all | solution.py:180
  86.2 8.6 %project.3.after_ref = bf16[1024,1024]{1,0:T(8,128)(2,1)} custom-call(bf16[1024,2176]{1,0:T(8,128)(2,1)} %bitcast.5.acts_ref, bf16[2048,1024]{1,0:T(8,128)(2,1)} %constant_dynamic-update-slice_fusion.weight_ref), custom_call_target="tpu_custom_call" | custom-call | flops 4294967296 | bytes 12582912 | tf_op jit(solution)/shard_map/project/pallas_call | solution.py:68
  94.8 4.6 %all-to-all-start.1 = ((bf16[16,64,1024]{2,1,0:T(8,128)(2,1)}), bf16[16,64,1024]{2,1,0:T(8,128)(2,1)S(1)}, u32[]{:S(2)}, u32[]{:S(2)}) async-start(bf16[16,64,1024]{2,1,0:T(8,128)(2,1)} %bitcast.7), calls=%async_computation.1 | async-start | bytes 4194304 | tf_op jit(solution)/shard_map/all_to_all | solution.py:185
  99.4 3.6 %stats.1 = (f32[512,128]{1,0:T(8,128)S(1)}, bf16[512,128]{1,0:T(8,128)(2,1)S(1)}, bf16[512,128]{1,0:T(8,128)(2,1)S(1)}, bf16[512,128]{1,0:T(8,128)(2,1)S(1)}) custom-call(bf16[1024,2176]{1,0:T(8,128)(2,1)} %bitcast.5.acts_ref, bf16[1024,1024]{1,0:T(8,128)(2,1)} %project.3.after_ref), custom_call_target="tpu_custom_call" | custom-call | tf_op jit(solution)/shard_map/stats/pallas_call | solution.py:130
  103.0 4.1 %collective-permute-start.7 = (bf16[512,128]{1,0:T(8,128)(2,1)S(1)}, bf16[512,128]{1,0:T(8,128)(2,1)S(1)}, u32[]{:S(2)}, u32[]{:S(2)}) collective-permute-start(bf16[512,128]{1,0:T(8,128)(2,1)S(1)} %get-tuple-element.23), channel_id=1, source_target_pairs={{4,0},{8,4},{12,8},{0,12},{5,1},{9,5},{13,9},{1,13},{6,2},{10,6},{... | collective-permute-start | bytes 393224 | tf_op jit(solution)/shard_map/ppermute | solution.py:146
  107.1 1.3 collective-permute-start.5
  108.3 2.9 %collective-permute-done.7 = bf16[512,128]{1,0:T(8,128)(2,1)S(1)} collective-permute-done((bf16[512,128]{1,0:T(8,128)(2,1)S(1)}, bf16[512,128]{1,0:T(8,128)(2,1)S(1)}, u32[]{:S(2)}, u32[]{:S(2)}) %collective-permute-start.7) | collective-permute-done | bytes 131104 | tf_op jit(solution)/shard_map/ppermute | solution.py:146
  111.2 2.4 %collective-permute-done.6 = bf16[512,128]{1,0:T(8,128)(2,1)S(1)} collective-permute-done((bf16[512,128]{1,0:T(8,128)(2,1)S(1)}, bf16[512,128]{1,0:T(8,128)(2,1)S(1)}, u32[]{:S(2)}, u32[]{:S(2)}) %collective-permute-start.6) | collective-permute-done | bytes 131104 | tf_op jit(solution)/shard_map/ppermute | solution.py:146
  113.6 1.0 collective-permute-done.5
  114.9 1.4 collective-permute-done.8
  116.4 2.0 %collective-permute-start.9 = (bf16[256,128]{1,0:T(8,128)(2,1)S(1)}, bf16[256,128]{1,0:T(8,128)(2,1)S(1)}, u32[]{:S(2)}, u32[]{:S(2)}) collective-permute-start(bf16[256,128]{1,0:T(8,128)(2,1)S(1)} %get-tuple-element.33), channel_id=1, source_target_pairs={{0,16},{16,0},{1,17},{17,1},{2,18},{18,2},{3,19},{19,3},{4,20},{20... | collective-permute-start | bytes 196616 | tf_op jit(solution)/shard_map/ppermute | solution.py:142
  118.4 2.1 %collective-permute-start.11 = (bf16[256,128]{1,0:T(8,128)(2,1)S(1)}, bf16[256,128]{1,0:T(8,128)(2,1)S(1)}, u32[]{:S(2)}, u32[]{:S(2)}) collective-permute-start(bf16[256,128]{1,0:T(8,128)(2,1)S(1)} %get-tuple-element.33), channel_id=1, source_target_pairs={{0,80},{16,64},{64,16},{80,0},{1,81},{17,65},{65,17},{81,1},{2,82}... | collective-permute-start | bytes 196616 | tf_op jit(solution)/shard_map/ppermute | solution.py:200
  121.1 7.6 %project.2 = bf16[1024,1024]{1,0:T(8,128)(2,1)S(1)} custom-call(bf16[1024,2176]{1,0:T(8,128)(2,1)} %bitcast.5.acts_ref, bf16[2048,1024]{1,0:T(8,128)(2,1)} %collective-permute-done.4.weight_ref), custom_call_target="tpu_custom_call" | custom-call | flops 4294967296 | bytes 12582912 | tf_op jit(solution)/shard_map/project/pallas_call | solution.py:68
  128.7 1.3 copy-done.2
  130.0 34.7 %all_to_all.15.second_ref = bf16[16,64,1024]{2,1,0:T(8,128)(2,1)S(1)} all-to-all(bf16[16,64,1024]{2,1,0:T(8,128)(2,1)} %bitcast.19), channel_id=1, replica_groups=mesh['yh'=2,'core'=2,'yl'=2,'z'=4,'x'=4] {'yh','yl','x'}, dimensions={0} | all-to-all | bytes 4194304 | tf_op jit(solution)/shard_map/all_to_all | solution.py:185
  164.7 2.0 %finish.1 = (bf16[64,4096]{1,0:T(8,128)(2,1)}, bf16[64,4096]{1,0:T(8,128)(2,1)}, f32[256,128]{1,0:T(8,128)}, f32[256,128]{1,0:T(8,128)}) custom-call(s32[3]{0:T(128)S(1)} %pad_add_fusion.at_ref, bf16[16,64,1024]{2,1,0:T(8,128)(2,1)S(1)} %all-to-all-done.1.first_ref, bf16[16,64,1024]{2,1,0:T(8,128)(2,1)S(1)} %all_to_all.15.second_ref, ...), custom_call_target="tpu_custom_call" | custom-call | tf_op jit(solution)/shard_map/finish/pallas_call | solution.py:106
  (25 shorter events, 2.1 us)
Async XLA Ops:
  0.6 0.8 copy-start
  3.0 9.3 %collective-permute-start = (bf16[256,1024]{1,0:T(8,128)(2,1)S(1)}, bf16[256,1024]{1,0:T(8,128)(2,1)S(1)}, u32[]{:S(2)}, u32[]{:S(2)}) collective-permute-start(bf16[256,1024]{1,0:T(8,128)(2,1)S(1)} %fusion.2), channel_id=1, source_target_pairs={{0,16},{16,0},{32,112},{48,96},{64,80},{80,64},{96,48},{112,32},{1... | collective-permute-start | bytes 1572872 | tf_op jit(solution)/shard_map/ppermute | solution.py:171
  4.7 1.2 copy-start.3
  5.9 1.2 copy-start.4
  7.5 2.1 %copy-start.1 = (bf16[16,64,2176]{2,1,0:T(8,128)(2,1)}, bf16[16,64,2176]{2,1,0:T(8,128)(2,1)S(1)}, u32[]{:S(2)}) copy-start(bf16[16,64,2176]{2,1,0:T(8,128)(2,1)S(1)} %pack.1) | copy-start | bytes 13369348
  12.2 74.0 %all-to-all-start = ((bf16[16,64,2176]{2,1,0:T(8,128)(2,1)}), bf16[16,64,2176]{2,1,0:T(8,128)(2,1)}, u32[]{:S(2)}, u32[]{:S(2)}) async-start(bf16[16,64,2176]{2,1,0:T(8,128)(2,1)} %copy-done.1), calls=%async_computation | async-start | bytes 8912896 | tf_op jit(solution)/shard_map/all_to_all | solution.py:180
  22.3 48.6 %collective-permute-start.1 = (bf16[512,1024]{1,0:T(8,128)(2,1)S(1)}, bf16[512,1024]{1,0:T(8,128)(2,1)S(1)}, u32[]{:S(2)}, u32[]{:S(2)}) collective-permute-start(bf16[512,1024]{1,0:T(8,128)(2,1)S(1)} %pad_maximum_fusion), channel_id=1, source_target_pairs={{4,0},{8,4},{12,8},{0,12},{5,1},{9,5},{13,9},{1,13},{6,2},{10,6},{... | collective-permute-start | bytes 3145736 | tf_op jit(solution)/shard_map/ppermute | solution.py:146
  26.4 45.5 %collective-permute-start.2 = (bf16[512,1024]{1,0:T(8,128)(2,1)S(1)}, bf16[512,1024]{1,0:T(8,128)(2,1)S(1)}, u32[]{:S(2)}, u32[]{:S(2)}) collective-permute-start(bf16[512,1024]{1,0:T(8,128)(2,1)S(1)} %pad_maximum_fusion), channel_id=1, source_target_pairs={{8,0},{12,4},{0,8},{4,12},{9,1},{13,5},{1,9},{5,13},{10,2},{14,6},... | collective-permute-start | bytes 3145736 | tf_op jit(solution)/shard_map/ppermute | solution.py:146
  26.4 47.9 %collective-permute-start.3 = (bf16[512,1024]{1,0:T(8,128)(2,1)S(1)}, bf16[512,1024]{1,0:T(8,128)(2,1)S(1)}, u32[]{:S(2)}, u32[]{:S(2)}) collective-permute-start(bf16[512,1024]{1,0:T(8,128)(2,1)S(1)} %pad_maximum_fusion), channel_id=1, source_target_pairs={{12,0},{0,4},{4,8},{8,12},{13,1},{1,5},{5,9},{9,13},{14,2},{2,6},{... | collective-permute-start | bytes 3145736 | tf_op jit(solution)/shard_map/ppermute | solution.py:146
  75.3 45.7 %collective-permute-start.4 = (bf16[2048,1024]{1,0:T(8,128)(2,1)}, bf16[2048,1024]{1,0:T(8,128)(2,1)}, u32[]{:S(2)}, u32[]{:S(2)}) collective-permute-start(bf16[2048,1024]{1,0:T(8,128)(2,1)} %constant_dynamic-update-slice_fusion.weight_ref), channel_id=1, source_target_pairs={{0,32},{32,0},{1,33},{33,1},{2,34},{34,2},{3,35},{35,3},{4,36},{36... | collective-permute-start | bytes 12582920 | tf_op jit(solution)/shard_map/ppermute | solution.py:142
  94.8 35.2 %all-to-all-start.1 = ((bf16[16,64,1024]{2,1,0:T(8,128)(2,1)}), bf16[16,64,1024]{2,1,0:T(8,128)(2,1)S(1)}, u32[]{:S(2)}, u32[]{:S(2)}) async-start(bf16[16,64,1024]{2,1,0:T(8,128)(2,1)} %bitcast.7), calls=%async_computation.1 | async-start | bytes 4194304 | tf_op jit(solution)/shard_map/all_to_all | solution.py:185
  103.0 8.3 %collective-permute-start.7 = (bf16[512,128]{1,0:T(8,128)(2,1)S(1)}, bf16[512,128]{1,0:T(8,128)(2,1)S(1)}, u32[]{:S(2)}, u32[]{:S(2)}) collective-permute-start(bf16[512,128]{1,0:T(8,128)(2,1)S(1)} %get-tuple-element.23), channel_id=1, source_target_pairs={{4,0},{8,4},{12,8},{0,12},{5,1},{9,5},{13,9},{1,13},{6,2},{10,6},{... | collective-permute-start | bytes 393224 | tf_op jit(solution)/shard_map/ppermute | solution.py:146
  107.1 6.6 %collective-permute-start.6 = (bf16[512,128]{1,0:T(8,128)(2,1)S(1)}, bf16[512,128]{1,0:T(8,128)(2,1)S(1)}, u32[]{:S(2)}, u32[]{:S(2)}) collective-permute-start(bf16[512,128]{1,0:T(8,128)(2,1)S(1)} %get-tuple-element.22), channel_id=1, source_target_pairs={{8,0},{12,4},{0,8},{4,12},{9,1},{13,5},{1,9},{5,13},{10,2},{14,6},... | collective-permute-start | bytes 393224 | tf_op jit(solution)/shard_map/ppermute | solution.py:146
  107.1 7.6 %collective-permute-start.5 = (bf16[512,128]{1,0:T(8,128)(2,1)S(1)}, bf16[512,128]{1,0:T(8,128)(2,1)S(1)}, u32[]{:S(2)}, u32[]{:S(2)}) collective-permute-start(bf16[512,128]{1,0:T(8,128)(2,1)S(1)} %get-tuple-element.21), channel_id=1, source_target_pairs={{12,0},{0,4},{4,8},{8,12},{13,1},{1,5},{5,9},{9,13},{14,2},{2,6},{... | collective-permute-start | bytes 393224 | tf_op jit(solution)/shard_map/ppermute | solution.py:146
  114.7 1.6 collective-permute-start.8
  116.4 13.6 %collective-permute-start.9 = (bf16[256,128]{1,0:T(8,128)(2,1)S(1)}, bf16[256,128]{1,0:T(8,128)(2,1)S(1)}, u32[]{:S(2)}, u32[]{:S(2)}) collective-permute-start(bf16[256,128]{1,0:T(8,128)(2,1)S(1)} %get-tuple-element.33), channel_id=1, source_target_pairs={{0,16},{16,0},{1,17},{17,1},{2,18},{18,2},{3,19},{19,3},{4,20},{20... | collective-permute-start | bytes 196616 | tf_op jit(solution)/shard_map/ppermute | solution.py:142
  118.4 11.6 %collective-permute-start.11 = (bf16[256,128]{1,0:T(8,128)(2,1)S(1)}, bf16[256,128]{1,0:T(8,128)(2,1)S(1)}, u32[]{:S(2)}, u32[]{:S(2)}) collective-permute-start(bf16[256,128]{1,0:T(8,128)(2,1)S(1)} %get-tuple-element.33), channel_id=1, source_target_pairs={{0,80},{16,64},{64,16},{80,0},{1,81},{17,65},{65,17},{81,1},{2,82}... | collective-permute-start | bytes 196616 | tf_op jit(solution)/shard_map/ppermute | solution.py:200
  120.5 9.5 %collective-permute-start.10 = (bf16[256,128]{1,0:T(8,128)(2,1)S(1)}, bf16[256,128]{1,0:T(8,128)(2,1)S(1)}, u32[]{:S(2)}, u32[]{:S(2)}) collective-permute-start(bf16[256,128]{1,0:T(8,128)(2,1)S(1)} %get-tuple-element.32), channel_id=1, source_target_pairs={{0,64},{64,0},{1,65},{65,1},{2,66},{66,2},{3,67},{67,3},{4,68},{68... | collective-permute-start | bytes 196616 | tf_op jit(solution)/shard_map/ppermute | solution.py:142
  128.7 1.3 copy-start.2

commit v21 on v20

--- a/solution.py
+++ b/solution.py
@@ -162,6 +162,7 @@
         quant = (values * scales[:, None, :]).reshape(features, quarter).astype(BF16)
         return jnp.where(kind == 0, plain, quant)
 
+    own = weight(yh, yl * half + core * quarter)
     send = weight(yh ^ core, (1 - yl) * half + core * quarter)
     pairs = []
     for a in range(2):
@@ -169,11 +170,7 @@
             for b in range(2):
                 pairs.append((a * 4 + c * 2 + b, (a ^ c) * 4 + c * 2 + (1 - b)))
     got = lax.ppermute(send, ("yh", "core", "yl"), pairs)
-    col, send = lax.optimization_barrier((yl * half + core * quarter, send))
-    own = weight(yh, col)
-
     payload = pack(z, attn_float, attn_quant)
-    payload, got = lax.optimization_barrier((payload, got))
     rows = jnp.concatenate([own, got], axis=0)
     parts = [rows] + [ahead(rows, "z", j) for j in (1, 2, 3)]
 
@@ -189,9 +186,11 @@
 
     blocks = stats(acts, first)
     total = blocks[0]
-    for j in (1, 2, 3):
-        total = total + ahead(blocks[j], "z", 4 - j).astype(F32)
+    came = [ahead(blocks[j], "z", 4 - j) for j in (1, 2, 3)]
     second = project(acts, other)
+    second, *came = lax.optimization_barrier((second, *came))
+    for block in came:
+        total = total + block.astype(F32)
     total = (total + swap(total, "core")) * inverse
     here, there = total[:features].astype(BF16), total[features:].astype(BF16)
     moved = (

time: 167 us -> 171 us (1.024)
  waiting for transfers between devices: 65 us -> 70.5 us
  blocking collectives: 34.7 us -> 32.6 us
    ppermute x6, waiting for transfers between devices: 50 us -> 32.9 us  [ahead(): return lax.ppermute(a, axis, [((i + j) % 4, i) for i in range(4)])]
    all_to_all x1, waiting for transfers between devices: 10.9 us -> 23 us  [shards(): lax.all_to_all(payload, PLANE, 0, 0, tiled=True).reshape(16 * tokens, -1)]
    ppermute x4, waiting for transfers between devices: 1.45 us -> 6.73 us  [swap(): return lax.ppermute(a, axis, [(0, 1), (1, 0)])]
    ppermute x1, waiting for transfers between devices: 2.68 us -> 7.52 us  [shards(): got = lax.ppermute(send, ('yh', 'core', 'yl'), pairs)]
    unnamed x1 -> x0, other arithmetic: 2.71 us -> none
    all_to_all x1, blocking collectives: 34.7 us -> 32.6 us  [output(): lax.all_to_all(p.reshape(16, tokens, quarter), PLANE, 0, 0, tiled=True)]
    unnamed x13 -> x12, local copies, waits for them, and re-layouts: 9.53 us -> 8.29 us
  transfers between devices with their start and end apart: 14 -> 14, of which waited for: 8 -> 7; matrix products, arithmetic and copies ran while one was open for 4% -> 5% of each run, Pallas kernels for 12% -> 12%
where the time goes in v21:
time: 171 us
  waiting for transfers between devices  70.5 us (41%)
  blocking collectives  32.6 us (19%)
  starting transfers between devices  29.8 us (17%)
  Pallas kernels  22.1 us (13%)
  local copies, waits for them, and re-layouts  11.4 us (7%)
  other arithmetic  3.45 us (2%)
    ppermute x6, waiting for transfers between devices, ahead(): return lax.ppermute(a, axis, [((i + j) % 4, i) for i in range(4)])  32.9 us
    all_to_all x1, blocking collectives, output(): lax.all_to_all(p.reshape(16, tokens, quarter), PLANE, 0, 0, tiled=True)  32.6 us
    all_to_all x1, waiting for transfers between devices, shards(): lax.all_to_all(payload, PLANE, 0, 0, tiled=True).reshape(16 * tokens, -1)  23 us
    pallas_call x2, Pallas kernels, project(): pl.pallas_call(project_kernel, out_shape=jax.ShapeDtypeStruct((rows, cols...  16.2 us
    ppermute x6, starting transfers between devices, ahead(): return lax.ppermute(a, axis, [((i + j) % 4, i) for i in range(4)])  11.6 us
    unnamed x12, local copies, waits for them, and re-layouts  8.29 us
    ppermute x1, waiting for transfers between devices, shards(): got = lax.ppermute(send, ('yh', 'core', 'yl'), pairs)  7.52 us
    all_to_all x1, starting transfers between devices, shards(): lax.all_to_all(payload, PLANE, 0, 0, tiled=True).reshape(16 * tokens, -1)  7.08 us
  transfers between devices with their start and end apart: 14, of which 7 were waited for; matrix products, arithmetic and copies ran while one was open for 5% of the time, Pallas kernels for 12%

profile of v21, /device:TPU:0, one launch (start us, length us, event | category | flops | bytes accessed | tf_op | source)
XLA Modules:
  0.0 170.6 jit_solution(4834736230192898880)
XLA Ops:
  0.7 0.9 constant_dynamic-slice_fusion
  1.5 2.3 %fusion.3 = (bf16[256,1024]{1,0:T(8,128)(2,1)S(1)}, bf16[256,1024]{1,0:T(8,128)(2,1)S(1)}) fusion(s32[256,4096]{1,0:T(8,128)} %param.8, s32[]{:T(128)S(6)} %select_n.28, f32[2,1024]{1,0:T(2,128)S(1)} %get-tuple-element.38, bf16[256,4096]{1,0:T(8,128)(2,1)} %param.7, pred[]{:T(512)S(6)} %eq.7, f32[2,1024]{1,0:T(2,128)S(1)} %get-tuple-element.39, ...), kind=kLoop, calls=%fused_computation.6 | loop fusion | flops 2621440 | bytes 4210698 | tf_op jit(solution)/shard_map/jit(_where)/select_n | solution.py:163
  3.8 1.7 %collective-permute-start = (bf16[256,1024]{1,0:T(8,128)(2,1)S(1)}, bf16[256,1024]{1,0:T(8,128)(2,1)S(1)}, u32[]{:S(2)}, u32[]{:S(2)}) collective-permute-start(bf16[256,1024]{1,0:T(8,128)(2,1)S(1)} %get-tuple-element.34), channel_id=1, source_target_pairs={{0,16},{16,0},{32,112},{48,96},{64,80},{80,64},{96,48},{112,32},{1... | collective-permute-start | bytes 1572872 | tf_op jit(solution)/shard_map/ppermute | solution.py:172
  5.5 7.5 %collective-permute-done = bf16[256,1024]{1,0:T(8,128)(2,1)S(1)} collective-permute-done((bf16[256,1024]{1,0:T(8,128)(2,1)S(1)}, bf16[256,1024]{1,0:T(8,128)(2,1)S(1)}, u32[]{:S(2)}, u32[]{:S(2)}) %collective-permute-start) | collective-permute-done | bytes 524320 | tf_op jit(solution)/shard_map/ppermute | solution.py:172
  13.0 1.0 pad_maximum_fusion
  14.1 4.1 %collective-permute-start.1 = (bf16[512,1024]{1,0:T(8,128)(2,1)}, bf16[512,1024]{1,0:T(8,128)(2,1)}, u32[]{:S(2)}, u32[]{:S(2)}) collective-permute-start(bf16[512,1024]{1,0:T(8,128)(2,1)} %pad_maximum_fusion), channel_id=1, source_target_pairs={{4,0},{8,4},{12,8},{0,12},{5,1},{9,5},{13,9},{1,13},{6,2},{10,6},{... | collective-permute-start | bytes 3145736 | tf_op jit(solution)/shard_map/ppermute | solution.py:146
  18.2 1.3 collective-permute-start.3
  19.5 0.3 pack.1
  19.8 2.1 %copy-done = bf16[16,64,2176]{2,1,0:T(8,128)(2,1)} copy-done((bf16[16,64,2176]{2,1,0:T(8,128)(2,1)}, bf16[16,64,2176]{2,1,0:T(8,128)(2,1)S(1)}, u32[]{:S(2)}) %copy-start) | copy-done | bytes 4456472
  21.9 7.1 %all-to-all-start = ((bf16[16,64,2176]{2,1,0:T(8,128)(2,1)}), bf16[16,64,2176]{2,1,0:T(8,128)(2,1)}, u32[]{:S(2)}, u32[]{:S(2)}) async-start(bf16[16,64,2176]{2,1,0:T(8,128)(2,1)} %copy-done), calls=%async_computation | async-start | bytes 8912896 | tf_op jit(solution)/shard_map/all_to_all | solution.py:177
  28.9 0.8 constant_dynamic-update-slice_fusion.4
  29.8 0.8 constant_dynamic-update-slice_fusion.3
  30.6 32.9 %collective-permute-done.1 = bf16[512,1024]{1,0:T(8,128)(2,1)} collective-permute-done((bf16[512,1024]{1,0:T(8,128)(2,1)}, bf16[512,1024]{1,0:T(8,128)(2,1)}, u32[]{:S(2)}, u32[]{:S(2)}) %collective-permute-start.1) | collective-permute-done | bytes 1048608 | tf_op jit(solution)/shard_map/ppermute | solution.py:146
  63.5 2.3 %constant_dynamic-update-slice_fusion.2 = bf16[2048,1024]{1,0:T(8,128)(2,1)} fusion(bf16[2048,1024]{1,0:T(8,128)(2,1)} %constant_dynamic-update-slice_fusion.3, bf16[512,1024]{1,0:T(8,128)(2,1)} %collective-permute-done.1), kind=kLoop, calls=%fused_computation.11 | loop fusion | bytes 2097152
  65.8 2.3 %constant_dynamic-update-slice_fusion.1 = bf16[2048,1024]{1,0:T(8,128)(2,1)} fusion(bf16[2048,1024]{1,0:T(8,128)(2,1)} %constant_dynamic-update-slice_fusion.2, bf16[512,1024]{1,0:T(8,128)(2,1)} %collective-permute-done.2), kind=kLoop, calls=%fused_computation.10 | loop fusion | bytes 2097152
  68.1 2.3 %constant_dynamic-update-slice_fusion.weight_ref = bf16[2048,1024]{1,0:T(8,128)(2,1)} fusion(bf16[2048,1024]{1,0:T(8,128)(2,1)} %constant_dynamic-update-slice_fusion.1, bf16[512,1024]{1,0:T(8,128)(2,1)} %collective-permute-done.3), kind=kLoop, calls=%fused_computation.9 | loop fusion | bytes 2097152 | tf_op jit(solution)/shard_map/concatenate | solution.py:178
  70.3 23.0 %all-to-all-done = bf16[16,64,2176]{2,1,0:T(8,128)(2,1)} async-done(((bf16[16,64,2176]{2,1,0:T(8,128)(2,1)}), bf16[16,64,2176]{2,1,0:T(8,128)(2,1)}, u32[]{:S(2)}, u32[]{:S(2)}) %all-to-all-start) | async-done | bytes 4456480 | tf_op jit(solution)/shard_map/all_to_all | solution.py:177
  93.3 8.6 %project.3.after_ref = bf16[1024,1024]{1,0:T(8,128)(2,1)} custom-call(bf16[1024,2176]{1,0:T(8,128)(2,1)} %bitcast.4.acts_ref, bf16[2048,1024]{1,0:T(8,128)(2,1)} %constant_dynamic-update-slice_fusion.weight_ref), custom_call_target="tpu_custom_call" | custom-call | flops 4294967296 | bytes 12582912 | tf_op jit(solution)/shard_map/project/pallas_call | solution.py:68
  101.9 4.6 %all-to-all-start.1 = ((bf16[16,64,1024]{2,1,0:T(8,128)(2,1)}), bf16[16,64,1024]{2,1,0:T(8,128)(2,1)S(1)}, u32[]{:S(2)}, u32[]{:S(2)}) async-start(bf16[16,64,1024]{2,1,0:T(8,128)(2,1)} %bitcast.7), calls=%async_computation.1 | async-start | bytes 4194304 | tf_op jit(solution)/shard_map/all_to_all | solution.py:182
  106.5 3.6 %stats.1 = (f32[512,128]{1,0:T(8,128)S(1)}, bf16[512,128]{1,0:T(8,128)(2,1)S(1)}, bf16[512,128]{1,0:T(8,128)(2,1)S(1)}, bf16[512,128]{1,0:T(8,128)(2,1)S(1)}) custom-call(bf16[1024,2176]{1,0:T(8,128)(2,1)} %bitcast.4.acts_ref, bf16[1024,1024]{1,0:T(8,128)(2,1)} %project.3.after_ref), custom_call_target="tpu_custom_call" | custom-call | tf_op jit(solution)/shard_map/stats/pallas_call | solution.py:130
  110.1 2.3 %collective-permute-start.5 = (bf16[512,128]{1,0:T(8,128)(2,1)S(1)}, bf16[512,128]{1,0:T(8,128)(2,1)S(1)}, u32[]{:S(2)}, u32[]{:S(2)}) collective-permute-start(bf16[512,128]{1,0:T(8,128)(2,1)S(1)} %get-tuple-element.18), channel_id=1, source_target_pairs={{12,0},{0,4},{4,8},{8,12},{13,1},{1,5},{5,9},{9,13},{14,2},{2,6},{... | collective-permute-start | bytes 393224 | tf_op jit(solution)/shard_map/ppermute | solution.py:146
  112.4 2.5 %collective-permute-start.6 = (bf16[512,128]{1,0:T(8,128)(2,1)S(1)}, bf16[512,128]{1,0:T(8,128)(2,1)S(1)}, u32[]{:S(2)}, u32[]{:S(2)}) collective-permute-start(bf16[512,128]{1,0:T(8,128)(2,1)S(1)} %get-tuple-element.19), channel_id=1, source_target_pairs={{8,0},{12,4},{0,8},{4,12},{9,1},{13,5},{1,9},{5,13},{10,2},{14,6},... | collective-permute-start | bytes 393224 | tf_op jit(solution)/shard_map/ppermute | solution.py:146
  114.8 1.5 collective-permute-start.7
  116.3 7.6 %project.2 = bf16[1024,1024]{1,0:T(8,128)(2,1)S(1)} custom-call(bf16[1024,2176]{1,0:T(8,128)(2,1)} %bitcast.4.acts_ref, bf16[2048,1024]{1,0:T(8,128)(2,1)} %collective-permute-done.4.weight_ref), custom_call_target="tpu_custom_call" | custom-call | flops 4294967296 | bytes 12582912 | tf_op jit(solution)/shard_map/project/pallas_call | solution.py:68
  124.1 1.5 collective-permute-done.8
  125.7 2.0 %collective-permute-start.9 = (bf16[256,128]{1,0:T(8,128)(2,1)S(1)}, bf16[256,128]{1,0:T(8,128)(2,1)S(1)}, u32[]{:S(2)}, u32[]{:S(2)}) collective-permute-start(bf16[256,128]{1,0:T(8,128)(2,1)S(1)} %get-tuple-element.37), channel_id=1, source_target_pairs={{0,16},{16,0},{1,17},{17,1},{2,18},{18,2},{3,19},{19,3},{4,20},{20... | collective-permute-start | bytes 196616 | tf_op jit(solution)/shard_map/ppermute | solution.py:142
  127.7 2.1 %collective-permute-start.11 = (bf16[256,128]{1,0:T(8,128)(2,1)S(1)}, bf16[256,128]{1,0:T(8,128)(2,1)S(1)}, u32[]{:S(2)}, u32[]{:S(2)}) collective-permute-start(bf16[256,128]{1,0:T(8,128)(2,1)S(1)} %get-tuple-element.37), channel_id=1, source_target_pairs={{0,80},{16,64},{64,16},{80,0},{1,81},{17,65},{65,17},{81,1},{2,82}... | collective-permute-start | bytes 196616 | tf_op jit(solution)/shard_map/ppermute | solution.py:199
  129.7 0.6 collective-permute-start.10
  130.6 5.1 %collective-permute-done.10.refs_1_ = bf16[256,128]{1,0:T(8,128)(2,1)S(1)} collective-permute-done((bf16[256,128]{1,0:T(8,128)(2,1)S(1)}, bf16[256,128]{1,0:T(8,128)(2,1)S(1)}, u32[]{:S(2)}, u32[]{:S(2)}) %collective-permute-start.10) | collective-permute-done | bytes 65568 | tf_op jit(solution)/shard_map/ppermute | solution.py:142
  135.6 0.3 collective-permute-done.11.refs_2_
  136.0 32.6 %all_to_all.15.second_ref = bf16[16,64,1024]{2,1,0:T(8,128)(2,1)S(1)} all-to-all(bf16[16,64,1024]{2,1,0:T(8,128)(2,1)} %bitcast.19), channel_id=1, replica_groups=mesh['yh'=2,'core'=2,'yl'=2,'z'=4,'x'=4] {'yh','yl','x'}, dimensions={0} | all-to-all | bytes 4194304 | tf_op jit(solution)/shard_map/all_to_all | solution.py:182
  168.6 2.0 %finish.1 = (bf16[64,4096]{1,0:T(8,128)(2,1)}, bf16[64,4096]{1,0:T(8,128)(2,1)}, f32[256,128]{1,0:T(8,128)}, f32[256,128]{1,0:T(8,128)}) custom-call(s32[3]{0:T(128)S(1)} %pad_add_fusion.at_ref, bf16[16,64,1024]{2,1,0:T(8,128)(2,1)S(1)} %all-to-all-done.1.first_ref, bf16[16,64,1024]{2,1,0:T(8,128)(2,1)S(1)} %all_to_all.15.second_ref, ...), custom_call_target="tpu_custom_call" | custom-call | tf_op jit(solution)/shard_map/finish/pallas_call | solution.py:106
  (22 shorter events, 0.4 us)
Async XLA Ops:
  0.6 18.8 %copy-start.2 = (bf16[64,8192]{1,0:T(8,128)(2,1)S(1)}, bf16[64,8192]{1,0:T(8,128)(2,1)}, u32[]{:S(2)}) copy-start(bf16[64,8192]{1,0:T(8,128)(2,1)} %float_ref.1) | copy-start | bytes 3145732
  0.6 18.8 %copy-start.3 = (bf16[64,8192]{1,0:T(8,128)(2,1)S(1)}, bf16[64,8192]{1,0:T(8,128)(2,1)}, u32[]{:S(2)}) copy-start(bf16[64,8192]{1,0:T(8,128)(2,1)} %quant_ref.1) | copy-start | bytes 3145732
  3.8 9.3 %collective-permute-start = (bf16[256,1024]{1,0:T(8,128)(2,1)S(1)}, bf16[256,1024]{1,0:T(8,128)(2,1)S(1)}, u32[]{:S(2)}, u32[]{:S(2)}) collective-permute-start(bf16[256,1024]{1,0:T(8,128)(2,1)S(1)} %get-tuple-element.34), channel_id=1, source_target_pairs={{0,16},{16,0},{32,112},{48,96},{64,80},{80,64},{96,48},{112,32},{1... | collective-permute-start | bytes 1572872 | tf_op jit(solution)/shard_map/ppermute | solution.py:172
  14.1 49.4 %collective-permute-start.1 = (bf16[512,1024]{1,0:T(8,128)(2,1)}, bf16[512,1024]{1,0:T(8,128)(2,1)}, u32[]{:S(2)}, u32[]{:S(2)}) collective-permute-start(bf16[512,1024]{1,0:T(8,128)(2,1)} %pad_maximum_fusion), channel_id=1, source_target_pairs={{4,0},{8,4},{12,8},{0,12},{5,1},{9,5},{13,9},{1,13},{6,2},{10,6},{... | collective-permute-start | bytes 3145736 | tf_op jit(solution)/shard_map/ppermute | solution.py:146
  18.2 47.6 %collective-permute-start.2 = (bf16[512,1024]{1,0:T(8,128)(2,1)}, bf16[512,1024]{1,0:T(8,128)(2,1)}, u32[]{:S(2)}, u32[]{:S(2)}) collective-permute-start(bf16[512,1024]{1,0:T(8,128)(2,1)} %pad_maximum_fusion), channel_id=1, source_target_pairs={{8,0},{12,4},{0,8},{4,12},{9,1},{13,5},{1,9},{5,13},{10,2},{14,6},... | collective-permute-start | bytes 3145736 | tf_op jit(solution)/shard_map/ppermute | solution.py:146
  18.2 49.9 %collective-permute-start.3 = (bf16[512,1024]{1,0:T(8,128)(2,1)}, bf16[512,1024]{1,0:T(8,128)(2,1)}, u32[]{:S(2)}, u32[]{:S(2)}) collective-permute-start(bf16[512,1024]{1,0:T(8,128)(2,1)} %pad_maximum_fusion), channel_id=1, source_target_pairs={{12,0},{0,4},{4,8},{8,12},{13,1},{1,5},{5,9},{9,13},{14,2},{2,6},{... | collective-permute-start | bytes 3145736 | tf_op jit(solution)/shard_map/ppermute | solution.py:146
  19.8 2.1 %copy-start = (bf16[16,64,2176]{2,1,0:T(8,128)(2,1)}, bf16[16,64,2176]{2,1,0:T(8,128)(2,1)S(1)}, u32[]{:S(2)}) copy-start(bf16[16,64,2176]{2,1,0:T(8,128)(2,1)S(1)} %pack.1) | copy-start | bytes 13369348
  21.9 71.5 %all-to-all-start = ((bf16[16,64,2176]{2,1,0:T(8,128)(2,1)}), bf16[16,64,2176]{2,1,0:T(8,128)(2,1)}, u32[]{:S(2)}, u32[]{:S(2)}) async-start(bf16[16,64,2176]{2,1,0:T(8,128)(2,1)} %copy-done), calls=%async_computation | async-start | bytes 8912896 | tf_op jit(solution)/shard_map/all_to_all | solution.py:177
  70.3 46.0 %collective-permute-start.4 = (bf16[2048,1024]{1,0:T(8,128)(2,1)}, bf16[2048,1024]{1,0:T(8,128)(2,1)}, u32[]{:S(2)}, u32[]{:S(2)}) collective-permute-start(bf16[2048,1024]{1,0:T(8,128)(2,1)} %constant_dynamic-update-slice_fusion.weight_ref), channel_id=1, source_target_pairs={{0,32},{32,0},{1,33},{33,1},{2,34},{34,2},{3,35},{35,3},{4,36},{36... | collective-permute-start | bytes 12582920 | tf_op jit(solution)/shard_map/ppermute | solution.py:142
  101.9 34.0 %all-to-all-start.1 = ((bf16[16,64,1024]{2,1,0:T(8,128)(2,1)}), bf16[16,64,1024]{2,1,0:T(8,128)(2,1)S(1)}, u32[]{:S(2)}, u32[]{:S(2)}) async-start(bf16[16,64,1024]{2,1,0:T(8,128)(2,1)} %bitcast.7), calls=%async_computation.1 | async-start | bytes 4194304 | tf_op jit(solution)/shard_map/all_to_all | solution.py:182
  110.1 13.8 %collective-permute-start.5 = (bf16[512,128]{1,0:T(8,128)(2,1)S(1)}, bf16[512,128]{1,0:T(8,128)(2,1)S(1)}, u32[]{:S(2)}, u32[]{:S(2)}) collective-permute-start(bf16[512,128]{1,0:T(8,128)(2,1)S(1)} %get-tuple-element.18), channel_id=1, source_target_pairs={{12,0},{0,4},{4,8},{8,12},{13,1},{1,5},{5,9},{9,13},{14,2},{2,6},{... | collective-permute-start | bytes 393224 | tf_op jit(solution)/shard_map/ppermute | solution.py:146
  112.4 11.6 %collective-permute-start.6 = (bf16[512,128]{1,0:T(8,128)(2,1)S(1)}, bf16[512,128]{1,0:T(8,128)(2,1)S(1)}, u32[]{:S(2)}, u32[]{:S(2)}) collective-permute-start(bf16[512,128]{1,0:T(8,128)(2,1)S(1)} %get-tuple-element.19), channel_id=1, source_target_pairs={{8,0},{12,4},{0,8},{4,12},{9,1},{13,5},{1,9},{5,13},{10,2},{14,6},... | collective-permute-start | bytes 393224 | tf_op jit(solution)/shard_map/ppermute | solution.py:146
  114.8 9.1 %collective-permute-start.7 = (bf16[512,128]{1,0:T(8,128)(2,1)S(1)}, bf16[512,128]{1,0:T(8,128)(2,1)S(1)}, u32[]{:S(2)}, u32[]{:S(2)}) collective-permute-start(bf16[512,128]{1,0:T(8,128)(2,1)S(1)} %get-tuple-element.20), channel_id=1, source_target_pairs={{4,0},{8,4},{12,8},{0,12},{5,1},{9,5},{13,9},{1,13},{6,2},{10,6},{... | collective-permute-start | bytes 393224 | tf_op jit(solution)/shard_map/ppermute | solution.py:146
  123.9 12.1 %copy-start.1 = (bf16[1024,1024]{1,0:T(8,128)(2,1)}, bf16[1024,1024]{1,0:T(8,128)(2,1)S(1)}, u32[]{:S(2)}) copy-start(bf16[1024,1024]{1,0:T(8,128)(2,1)S(1)} %project.2) | copy-start | bytes 6291460
  124.0 1.6 collective-permute-start.8
  125.7 4.9 %collective-permute-start.9 = (bf16[256,128]{1,0:T(8,128)(2,1)S(1)}, bf16[256,128]{1,0:T(8,128)(2,1)S(1)}, u32[]{:S(2)}, u32[]{:S(2)}) collective-permute-start(bf16[256,128]{1,0:T(8,128)(2,1)S(1)} %get-tuple-element.37), channel_id=1, source_target_pairs={{0,16},{16,0},{1,17},{17,1},{2,18},{18,2},{3,19},{19,3},{4,20},{20... | collective-permute-start | bytes 196616 | tf_op jit(solution)/shard_map/ppermute | solution.py:142
  127.7 8.3 %collective-permute-start.11 = (bf16[256,128]{1,0:T(8,128)(2,1)S(1)}, bf16[256,128]{1,0:T(8,128)(2,1)S(1)}, u32[]{:S(2)}, u32[]{:S(2)}) collective-permute-start(bf16[256,128]{1,0:T(8,128)(2,1)S(1)} %get-tuple-element.37), channel_id=1, source_target_pairs={{0,80},{16,64},{64,16},{80,0},{1,81},{17,65},{65,17},{81,1},{2,82}... | collective-permute-start | bytes 196616 | tf_op jit(solution)/shard_map/ppermute | solution.py:199
  129.7 5.9 %collective-permute-start.10 = (bf16[256,128]{1,0:T(8,128)(2,1)S(1)}, bf16[256,128]{1,0:T(8,128)(2,1)S(1)}, u32[]{:S(2)}, u32[]{:S(2)}) collective-permute-start(bf16[256,128]{1,0:T(8,128)(2,1)S(1)} %get-tuple-element.36), channel_id=1, source_target_pairs={{0,64},{64,0},{1,65},{65,1},{2,66},{66,2},{3,67},{67,3},{4,68},{68... | collective-permute-start | bytes 196616 | tf_op jit(solution)/shard_map/ppermute | solution.py:142

commit v22 on v21

--- a/solution.py
+++ b/solution.py
@@ -162,7 +162,6 @@
         quant = (values * scales[:, None, :]).reshape(features, quarter).astype(BF16)
         return jnp.where(kind == 0, plain, quant)
 
-    own = weight(yh, yl * half + core * quarter)
     send = weight(yh ^ core, (1 - yl) * half + core * quarter)
     pairs = []
     for a in range(2):
@@ -170,7 +169,11 @@
             for b in range(2):
                 pairs.append((a * 4 + c * 2 + b, (a ^ c) * 4 + c * 2 + (1 - b)))
     got = lax.ppermute(send, ("yh", "core", "yl"), pairs)
+    col, send = lax.optimization_barrier((yl * half + core * quarter, send))
+    own = weight(yh, col)
+
     payload = pack(z, attn_float, attn_quant)
+    payload, got = lax.optimization_barrier((payload, got))
     rows = jnp.concatenate([own, got], axis=0)
     parts = [rows] + [ahead(rows, "z", j) for j in (1, 2, 3)]
 

time: 171 us -> 168 us (0.982)
  waiting for transfers between devices: 70.5 us -> 67.3 us
    ppermute x1, waiting for transfers between devices: 7.52 us -> 2.32 us  [shards(): got = lax.ppermute(send, ('yh', 'core', 'yl'), pairs)]
    ppermute x6, waiting for transfers between devices: 32.9 us -> 35.8 us  [ahead(): return lax.ppermute(a, axis, [((i + j) % 4, i) for i in range(4)])]
    unnamed x0 -> x1, other arithmetic: none -> 2.73 us
    unnamed x12 -> x15, local copies, waits for them, and re-layouts: 8.29 us -> 10.3 us
  transfers between devices with their start and end apart: 14 -> 14, of which waited for: 7 -> 7; matrix products, arithmetic and copies ran while one was open for 5% -> 6% of each run, Pallas kernels for 12% -> 11%
where the time goes in v22:
time: 168 us; the launch traced here: 167 us
  waiting for transfers between devices  67.3 us (40%)
  blocking collectives  32.6 us (19%)
  starting transfers between devices  29.8 us (18%)
  Pallas kernels  20.8 us (12%)
  local copies, waits for them, and re-layouts  11.5 us (7%)
  other arithmetic  4.53 us (3%)
    ppermute x6, waiting for transfers between devices, ahead(): return lax.ppermute(a, axis, [((i + j) % 4, i) for i in range(4)])  35.8 us
    all_to_all x1, blocking collectives, output(): lax.all_to_all(p.reshape(16, tokens, quarter), PLANE, 0, 0, tiled=True)  32.6 us
    all_to_all x1, waiting for transfers between devices, shards(): lax.all_to_all(payload, PLANE, 0, 0, tiled=True).reshape(16 * tokens, -1)  22.1 us
    pallas_call x2, Pallas kernels, project(): pl.pallas_call(project_kernel, out_shape=jax.ShapeDtypeStruct((rows, cols...  14.9 us
    ppermute x6, starting transfers between devices, ahead(): return lax.ppermute(a, axis, [((i + j) % 4, i) for i in range(4)])  11.7 us
    unnamed x15, local copies, waits for them, and re-layouts  10.3 us
    all_to_all x1, starting transfers between devices, shards(): lax.all_to_all(payload, PLANE, 0, 0, tiled=True).reshape(16 * tokens, -1)  7.08 us
    ppermute x4, waiting for transfers between devices, swap(): return lax.ppermute(a, axis, [(0, 1), (1, 0)])  6.74 us
  transfers between devices with their start and end apart: 14, of which 7 were waited for; matrix products, arithmetic and copies ran while one was open for 6% of the time, Pallas kernels for 11%

profile of v22, /device:TPU:0, one launch (start us, length us, event | category | flops | bytes accessed | tf_op | source)
XLA Modules:
  0.0 167.4 jit_solution(5032204785796573137)
XLA Ops:
  0.7 0.7 copy-done
  1.4 1.6 fusion.2
  3.0 1.7 %collective-permute-start = (bf16[256,1024]{1,0:T(8,128)(2,1)S(1)}, bf16[256,1024]{1,0:T(8,128)(2,1)S(1)}, u32[]{:S(2)}, u32[]{:S(2)}) collective-permute-start(bf16[256,1024]{1,0:T(8,128)(2,1)S(1)} %fusion.2), channel_id=1, source_target_pairs={{0,16},{16,0},{32,112},{48,96},{64,80},{80,64},{96,48},{112,32},{1... | collective-permute-start | bytes 1572872 | tf_op jit(solution)/shard_map/ppermute | solution.py:171
  4.8 2.7 %constant_dynamic-update-slice_fusion.4 = (bf16[2048,1024]{1,0:T(8,128)(2,1)}, bf16[256,1024]{1,0:T(8,128)(2,1)S(1)}) fusion(f32[2,1024]{1,0:T(2,128)S(1)} %constant_dynamic-slice_fusion, s32[256,4096]{1,0:T(8,128)} %param.8, s32[]{:T(128)S(6)} %select_n.28, bf16[256,4096]{1,0:T(8,128)(2,1)} %param.7, pred[]{:T(512)S(6)} %eq.7), kind=kLoop, calls=%fused_computation.13 | loop fusion | flops 1310719 | bytes 2629637
  7.5 0.3 pack.1
  7.8 2.1 %copy-done.1 = bf16[16,64,2176]{2,1,0:T(8,128)(2,1)} copy-done((bf16[16,64,2176]{2,1,0:T(8,128)(2,1)}, bf16[16,64,2176]{2,1,0:T(8,128)(2,1)S(1)}, u32[]{:S(2)}) %copy-start.1) | copy-done | bytes 4456472
  9.9 2.3 %collective-permute-done = bf16[256,1024]{1,0:T(8,128)(2,1)S(1)} collective-permute-done((bf16[256,1024]{1,0:T(8,128)(2,1)S(1)}, bf16[256,1024]{1,0:T(8,128)(2,1)S(1)}, u32[]{:S(2)}, u32[]{:S(2)}) %collective-permute-start) | collective-permute-done | bytes 524320 | tf_op jit(solution)/shard_map/ppermute | solution.py:171
  12.3 4.2 %collective-permute-start.1 = (bf16[512,1024]{1,0:T(8,128)(2,1)S(1)}, bf16[512,1024]{1,0:T(8,128)(2,1)}, u32[]{:S(2)}, u32[]{:S(2)}) collective-permute-start(bf16[512,1024]{1,0:T(8,128)(2,1)S(1)} %pad_maximum_fusion), channel_id=1, source_target_pairs={{4,0},{8,4},{12,8},{0,12},{5,1},{9,5},{13,9},{1,13},{6,2},{10,6},{... | collective-permute-start | bytes 3145736 | tf_op jit(solution)/shard_map/ppermute | solution.py:146
  16.5 1.3 collective-permute-start.3
  17.7 7.1 %all-to-all-start = ((bf16[16,64,2176]{2,1,0:T(8,128)(2,1)}), bf16[16,64,2176]{2,1,0:T(8,128)(2,1)}, u32[]{:S(2)}, u32[]{:S(2)}) async-start(bf16[16,64,2176]{2,1,0:T(8,128)(2,1)} %copy-done.1), calls=%async_computation | async-start | bytes 8912896 | tf_op jit(solution)/shard_map/all_to_all | solution.py:180
  24.8 0.8 constant_dynamic-update-slice_fusion.3
  25.7 35.8 %collective-permute-done.1 = bf16[512,1024]{1,0:T(8,128)(2,1)} collective-permute-done((bf16[512,1024]{1,0:T(8,128)(2,1)S(1)}, bf16[512,1024]{1,0:T(8,128)(2,1)}, u32[]{:S(2)}, u32[]{:S(2)}) %collective-permute-start.1) | collective-permute-done | bytes 1048608 | tf_op jit(solution)/shard_map/ppermute | solution.py:146
  61.5 2.3 %constant_dynamic-update-slice_fusion.2 = bf16[2048,1024]{1,0:T(8,128)(2,1)} fusion(bf16[2048,1024]{1,0:T(8,128)(2,1)} %constant_dynamic-update-slice_fusion.3, bf16[512,1024]{1,0:T(8,128)(2,1)} %collective-permute-done.1), kind=kLoop, calls=%fused_computation.11 | loop fusion | bytes 2097152
  63.8 2.3 %constant_dynamic-update-slice_fusion.1 = bf16[2048,1024]{1,0:T(8,128)(2,1)} fusion(bf16[2048,1024]{1,0:T(8,128)(2,1)} %constant_dynamic-update-slice_fusion.2, bf16[512,1024]{1,0:T(8,128)(2,1)} %collective-permute-done.2), kind=kLoop, calls=%fused_computation.10 | loop fusion | bytes 2097152
  66.0 1.1 constant_dynamic-update-slice_fusion.weight_ref
  67.1 22.1 %all-to-all-done = bf16[16,64,2176]{2,1,0:T(8,128)(2,1)} async-done(((bf16[16,64,2176]{2,1,0:T(8,128)(2,1)}), bf16[16,64,2176]{2,1,0:T(8,128)(2,1)}, u32[]{:S(2)}, u32[]{:S(2)}) %all-to-all-start) | async-done | bytes 4456480 | tf_op jit(solution)/shard_map/all_to_all | solution.py:180
  89.2 2.2 %copy-done.5 = bf16[2048,1024]{1,0:T(8,128)(2,1)S(1)} copy-done((bf16[2048,1024]{1,0:T(8,128)(2,1)S(1)}, bf16[2048,1024]{1,0:T(8,128)(2,1)}, u32[]{:S(2)}) %copy-start.5) | copy-done | bytes 4194328
  91.4 7.3 %project.3.after_ref = bf16[1024,1024]{1,0:T(8,128)(2,1)} custom-call(bf16[1024,2176]{1,0:T(8,128)(2,1)} %bitcast.5.acts_ref, bf16[2048,1024]{1,0:T(8,128)(2,1)S(1)} %copy-done.5), custom_call_target="tpu_custom_call" | custom-call | flops 4294967296 | bytes 12582912 | tf_op jit(solution)/shard_map/project/pallas_call | solution.py:68
  98.7 4.6 %all-to-all-start.1 = ((bf16[16,64,1024]{2,1,0:T(8,128)(2,1)}), bf16[16,64,1024]{2,1,0:T(8,128)(2,1)S(1)}, u32[]{:S(2)}, u32[]{:S(2)}) async-start(bf16[16,64,1024]{2,1,0:T(8,128)(2,1)} %bitcast.7), calls=%async_computation.1 | async-start | bytes 4194304 | tf_op jit(solution)/shard_map/all_to_all | solution.py:185
  103.3 3.6 %stats.1 = (f32[512,128]{1,0:T(8,128)S(1)}, bf16[512,128]{1,0:T(8,128)(2,1)S(1)}, bf16[512,128]{1,0:T(8,128)(2,1)S(1)}, bf16[512,128]{1,0:T(8,128)(2,1)S(1)}) custom-call(bf16[1024,2176]{1,0:T(8,128)(2,1)} %bitcast.5.acts_ref, bf16[1024,1024]{1,0:T(8,128)(2,1)} %project.3.after_ref), custom_call_target="tpu_custom_call" | custom-call | tf_op jit(solution)/shard_map/stats/pallas_call | solution.py:130
  106.9 2.3 %collective-permute-start.5 = (bf16[512,128]{1,0:T(8,128)(2,1)S(1)}, bf16[512,128]{1,0:T(8,128)(2,1)S(1)}, u32[]{:S(2)}, u32[]{:S(2)}) collective-permute-start(bf16[512,128]{1,0:T(8,128)(2,1)S(1)} %get-tuple-element.24), channel_id=1, source_target_pairs={{12,0},{0,4},{4,8},{8,12},{13,1},{1,5},{5,9},{9,13},{14,2},{2,6},{... | collective-permute-start | bytes 393224 | tf_op jit(solution)/shard_map/ppermute | solution.py:146
  109.2 2.5 %collective-permute-start.6 = (bf16[512,128]{1,0:T(8,128)(2,1)S(1)}, bf16[512,128]{1,0:T(8,128)(2,1)S(1)}, u32[]{:S(2)}, u32[]{:S(2)}) collective-permute-start(bf16[512,128]{1,0:T(8,128)(2,1)S(1)} %get-tuple-element.25), channel_id=1, source_target_pairs={{8,0},{12,4},{0,8},{4,12},{9,1},{13,5},{1,9},{5,13},{10,2},{14,6},... | collective-permute-start | bytes 393224 | tf_op jit(solution)/shard_map/ppermute | solution.py:146
  111.6 1.5 collective-permute-start.7
  113.1 7.6 %project.2 = bf16[1024,1024]{1,0:T(8,128)(2,1)S(1)} custom-call(bf16[1024,2176]{1,0:T(8,128)(2,1)} %bitcast.5.acts_ref, bf16[2048,1024]{1,0:T(8,128)(2,1)} %collective-permute-done.4.weight_ref), custom_call_target="tpu_custom_call" | custom-call | flops 4294967296 | bytes 12582912 | tf_op jit(solution)/shard_map/project/pallas_call | solution.py:68
  120.9 1.5 collective-permute-done.8
  122.5 2.0 %collective-permute-start.9 = (bf16[256,128]{1,0:T(8,128)(2,1)S(1)}, bf16[256,128]{1,0:T(8,128)(2,1)S(1)}, u32[]{:S(2)}, u32[]{:S(2)}) collective-permute-start(bf16[256,128]{1,0:T(8,128)(2,1)S(1)} %get-tuple-element.41), channel_id=1, source_target_pairs={{0,16},{16,0},{1,17},{17,1},{2,18},{18,2},{3,19},{19,3},{4,20},{20... | collective-permute-start | bytes 196616 | tf_op jit(solution)/shard_map/ppermute | solution.py:142
  124.5 2.1 %collective-permute-start.11 = (bf16[256,128]{1,0:T(8,128)(2,1)S(1)}, bf16[256,128]{1,0:T(8,128)(2,1)S(1)}, u32[]{:S(2)}, u32[]{:S(2)}) collective-permute-start(bf16[256,128]{1,0:T(8,128)(2,1)S(1)} %get-tuple-element.41), channel_id=1, source_target_pairs={{0,80},{16,64},{64,16},{80,0},{1,81},{17,65},{65,17},{81,1},{2,82}... | collective-permute-start | bytes 196616 | tf_op jit(solution)/shard_map/ppermute | solution.py:202
  126.5 0.6 collective-permute-start.10
  127.4 5.1 %collective-permute-done.10.refs_1_ = bf16[256,128]{1,0:T(8,128)(2,1)S(1)} collective-permute-done((bf16[256,128]{1,0:T(8,128)(2,1)S(1)}, bf16[256,128]{1,0:T(8,128)(2,1)S(1)}, u32[]{:S(2)}, u32[]{:S(2)}) %collective-permute-start.10) | collective-permute-done | bytes 65568 | tf_op jit(solution)/shard_map/ppermute | solution.py:142
  132.4 0.3 collective-permute-done.11.refs_2_
  132.8 32.6 %all_to_all.15.second_ref = bf16[16,64,1024]{2,1,0:T(8,128)(2,1)S(1)} all-to-all(bf16[16,64,1024]{2,1,0:T(8,128)(2,1)} %bitcast.19), channel_id=1, replica_groups=mesh['yh'=2,'core'=2,'yl'=2,'z'=4,'x'=4] {'yh','yl','x'}, dimensions={0} | all-to-all | bytes 4194304 | tf_op jit(solution)/shard_map/all_to_all | solution.py:185
  165.4 2.0 %finish.1 = (bf16[64,4096]{1,0:T(8,128)(2,1)}, bf16[64,4096]{1,0:T(8,128)(2,1)}, f32[256,128]{1,0:T(8,128)}, f32[256,128]{1,0:T(8,128)}) custom-call(s32[3]{0:T(128)S(1)} %pad_add_fusion.at_ref, bf16[16,64,1024]{2,1,0:T(8,128)(2,1)S(1)} %all-to-all-done.1.first_ref, bf16[16,64,1024]{2,1,0:T(8,128)(2,1)S(1)} %all_to_all.15.second_ref, ...), custom_call_target="tpu_custom_call" | custom-call | tf_op jit(solution)/shard_map/finish/pallas_call | solution.py:106
  (27 shorter events, 0.6 us)
Async XLA Ops:
  0.6 0.8 copy-start
  0.6 6.9 %copy-start.3 = (bf16[64,8192]{1,0:T(8,128)(2,1)S(1)}, bf16[64,8192]{1,0:T(8,128)(2,1)}, u32[]{:S(2)}) copy-start(bf16[64,8192]{1,0:T(8,128)(2,1)} %float_ref.1) | copy-start | bytes 3145732
  0.7 6.9 %copy-start.4 = (bf16[64,8192]{1,0:T(8,128)(2,1)S(1)}, bf16[64,8192]{1,0:T(8,128)(2,1)}, u32[]{:S(2)}) copy-start(bf16[64,8192]{1,0:T(8,128)(2,1)} %quant_ref.1) | copy-start | bytes 3145732
  3.0 9.3 %collective-permute-start = (bf16[256,1024]{1,0:T(8,128)(2,1)S(1)}, bf16[256,1024]{1,0:T(8,128)(2,1)S(1)}, u32[]{:S(2)}, u32[]{:S(2)}) collective-permute-start(bf16[256,1024]{1,0:T(8,128)(2,1)S(1)} %fusion.2), channel_id=1, source_target_pairs={{0,16},{16,0},{32,112},{48,96},{64,80},{80,64},{96,48},{112,32},{1... | collective-permute-start | bytes 1572872 | tf_op jit(solution)/shard_map/ppermute | solution.py:171
  7.8 2.1 %copy-start.1 = (bf16[16,64,2176]{2,1,0:T(8,128)(2,1)}, bf16[16,64,2176]{2,1,0:T(8,128)(2,1)S(1)}, u32[]{:S(2)}) copy-start(bf16[16,64,2176]{2,1,0:T(8,128)(2,1)S(1)} %pack.1) | copy-start | bytes 13369348
  12.3 49.2 %collective-permute-start.1 = (bf16[512,1024]{1,0:T(8,128)(2,1)S(1)}, bf16[512,1024]{1,0:T(8,128)(2,1)}, u32[]{:S(2)}, u32[]{:S(2)}) collective-permute-start(bf16[512,1024]{1,0:T(8,128)(2,1)S(1)} %pad_maximum_fusion), channel_id=1, source_target_pairs={{4,0},{8,4},{12,8},{0,12},{5,1},{9,5},{13,9},{1,13},{6,2},{10,6},{... | collective-permute-start | bytes 3145736 | tf_op jit(solution)/shard_map/ppermute | solution.py:146
  16.5 47.3 %collective-permute-start.2 = (bf16[512,1024]{1,0:T(8,128)(2,1)S(1)}, bf16[512,1024]{1,0:T(8,128)(2,1)}, u32[]{:S(2)}, u32[]{:S(2)}) collective-permute-start(bf16[512,1024]{1,0:T(8,128)(2,1)S(1)} %pad_maximum_fusion), channel_id=1, source_target_pairs={{8,0},{12,4},{0,8},{4,12},{9,1},{13,5},{1,9},{5,13},{10,2},{14,6},... | collective-permute-start | bytes 3145736 | tf_op jit(solution)/shard_map/ppermute | solution.py:146
  16.5 49.5 %collective-permute-start.3 = (bf16[512,1024]{1,0:T(8,128)(2,1)S(1)}, bf16[512,1024]{1,0:T(8,128)(2,1)S(1)}, u32[]{:S(2)}, u32[]{:S(2)}) collective-permute-start(bf16[512,1024]{1,0:T(8,128)(2,1)S(1)} %pad_maximum_fusion), channel_id=1, source_target_pairs={{12,0},{0,4},{4,8},{8,12},{13,1},{1,5},{5,9},{9,13},{14,2},{2,6},{... | collective-permute-start | bytes 3145736 | tf_op jit(solution)/shard_map/ppermute | solution.py:146
  17.7 71.5 %all-to-all-start = ((bf16[16,64,2176]{2,1,0:T(8,128)(2,1)}), bf16[16,64,2176]{2,1,0:T(8,128)(2,1)}, u32[]{:S(2)}, u32[]{:S(2)}) async-start(bf16[16,64,2176]{2,1,0:T(8,128)(2,1)} %copy-done.1), calls=%async_computation | async-start | bytes 8912896 | tf_op jit(solution)/shard_map/all_to_all | solution.py:180
  67.1 46.0 %collective-permute-start.4 = (bf16[2048,1024]{1,0:T(8,128)(2,1)}, bf16[2048,1024]{1,0:T(8,128)(2,1)}, u32[]{:S(2)}, u32[]{:S(2)}) collective-permute-start(bf16[2048,1024]{1,0:T(8,128)(2,1)} %constant_dynamic-update-slice_fusion.weight_ref), channel_id=1, source_target_pairs={{0,32},{32,0},{1,33},{33,1},{2,34},{34,2},{3,35},{35,3},{4,36},{36... | collective-permute-start | bytes 12582920 | tf_op jit(solution)/shard_map/ppermute | solution.py:142
  89.2 2.2 %copy-start.5 = (bf16[2048,1024]{1,0:T(8,128)(2,1)S(1)}, bf16[2048,1024]{1,0:T(8,128)(2,1)}, u32[]{:S(2)}) copy-start(bf16[2048,1024]{1,0:T(8,128)(2,1)} %constant_dynamic-update-slice_fusion.weight_ref) | copy-start | bytes 12582916
  98.7 34.0 %all-to-all-start.1 = ((bf16[16,64,1024]{2,1,0:T(8,128)(2,1)}), bf16[16,64,1024]{2,1,0:T(8,128)(2,1)S(1)}, u32[]{:S(2)}, u32[]{:S(2)}) async-start(bf16[16,64,1024]{2,1,0:T(8,128)(2,1)} %bitcast.7), calls=%async_computation.1 | async-start | bytes 4194304 | tf_op jit(solution)/shard_map/all_to_all | solution.py:185
  106.9 13.8 %collective-permute-start.5 = (bf16[512,128]{1,0:T(8,128)(2,1)S(1)}, bf16[512,128]{1,0:T(8,128)(2,1)S(1)}, u32[]{:S(2)}, u32[]{:S(2)}) collective-permute-start(bf16[512,128]{1,0:T(8,128)(2,1)S(1)} %get-tuple-element.24), channel_id=1, source_target_pairs={{12,0},{0,4},{4,8},{8,12},{13,1},{1,5},{5,9},{9,13},{14,2},{2,6},{... | collective-permute-start | bytes 393224 | tf_op jit(solution)/shard_map/ppermute | solution.py:146
  109.2 11.5 %collective-permute-start.6 = (bf16[512,128]{1,0:T(8,128)(2,1)S(1)}, bf16[512,128]{1,0:T(8,128)(2,1)S(1)}, u32[]{:S(2)}, u32[]{:S(2)}) collective-permute-start(bf16[512,128]{1,0:T(8,128)(2,1)S(1)} %get-tuple-element.25), channel_id=1, source_target_pairs={{8,0},{12,4},{0,8},{4,12},{9,1},{13,5},{1,9},{5,13},{10,2},{14,6},... | collective-permute-start | bytes 393224 | tf_op jit(solution)/shard_map/ppermute | solution.py:146
  111.6 9.1 %collective-permute-start.7 = (bf16[512,128]{1,0:T(8,128)(2,1)S(1)}, bf16[512,128]{1,0:T(8,128)(2,1)S(1)}, u32[]{:S(2)}, u32[]{:S(2)}) collective-permute-start(bf16[512,128]{1,0:T(8,128)(2,1)S(1)} %get-tuple-element.26), channel_id=1, source_target_pairs={{4,0},{8,4},{12,8},{0,12},{5,1},{9,5},{13,9},{1,13},{6,2},{10,6},{... | collective-permute-start | bytes 393224 | tf_op jit(solution)/shard_map/ppermute | solution.py:146
  120.7 12.1 %copy-start.2 = (bf16[1024,1024]{1,0:T(8,128)(2,1)}, bf16[1024,1024]{1,0:T(8,128)(2,1)S(1)}, u32[]{:S(2)}) copy-start(bf16[1024,1024]{1,0:T(8,128)(2,1)S(1)} %project.2) | copy-start | bytes 6291460
  120.8 1.6 collective-permute-start.8
  122.5 4.9 %collective-permute-start.9 = (bf16[256,128]{1,0:T(8,128)(2,1)S(1)}, bf16[256,128]{1,0:T(8,128)(2,1)S(1)}, u32[]{:S(2)}, u32[]{:S(2)}) collective-permute-start(bf16[256,128]{1,0:T(8,128)(2,1)S(1)} %get-tuple-element.41), channel_id=1, source_target_pairs={{0,16},{16,0},{1,17},{17,1},{2,18},{18,2},{3,19},{19,3},{4,20},{20... | collective-permute-start | bytes 196616 | tf_op jit(solution)/shard_map/ppermute | solution.py:142
  124.5 8.3 %collective-permute-start.11 = (bf16[256,128]{1,0:T(8,128)(2,1)S(1)}, bf16[256,128]{1,0:T(8,128)(2,1)S(1)}, u32[]{:S(2)}, u32[]{:S(2)}) collective-permute-start(bf16[256,128]{1,0:T(8,128)(2,1)S(1)} %get-tuple-element.41), channel_id=1, source_target_pairs={{0,80},{16,64},{64,16},{80,0},{1,81},{17,65},{65,17},{81,1},{2,82}... | collective-permute-start | bytes 196616 | tf_op jit(solution)/shard_map/ppermute | solution.py:202
  126.5 5.9 %collective-permute-start.10 = (bf16[256,128]{1,0:T(8,128)(2,1)S(1)}, bf16[256,128]{1,0:T(8,128)(2,1)S(1)}, u32[]{:S(2)}, u32[]{:S(2)}) collective-permute-start(bf16[256,128]{1,0:T(8,128)(2,1)S(1)} %get-tuple-element.40), channel_id=1, source_target_pairs={{0,64},{64,0},{1,65},{65,1},{2,66},{66,2},{3,67},{67,3},{4,68},{68... | collective-permute-start | bytes 196616 | tf_op jit(solution)/shard_map/ppermute | solution.py:142

commit v23 on v21

--- a/solution.py
+++ b/solution.py
@@ -14,16 +14,16 @@
 
 
 WHOLE = pl.BlockSpec(memory_space=pltpu.VMEM)
+SCALAR = pl.BlockSpec(memory_space=pltpu.SMEM)
 LEFT = pl.BlockSpec(memory_space=pl.ANY)
-SCALAR = pl.BlockSpec(memory_space=pltpu.SMEM)
-
-
-def params():
-    return pltpu.CompilerParams(vmem_limit_bytes=16 << 20)
-
-
-def pack_kernel(z_ref, float_ref, quant_ref, out_ref):
-    width = float_ref.shape[1] // 32
+
+
+def params(mib=16):
+    return pltpu.CompilerParams(vmem_limit_bytes=mib << 20)
+
+
+def pack_kernel(z_ref, float_ref, quant_ref, out_ref, block_ref):
+    width = out_ref.shape[2] // 8
     z = z_ref[0]
     for kind, ref in enumerate((float_ref, quant_ref)):
         for j in range(4):
@@ -38,17 +38,22 @@
     quant = quant_ref[:, :BLOCK]
     shift = (float_ref[:, :BLOCK].astype(F32) - quant.astype(F32)).astype(BF16)
     for d in range(16):
-        out_ref[d, :, 8 * width :] = shift if d // 4 % 2 else quant
+        block_ref[d, :, :BLOCK] = quant
+        block_ref[d, :, BLOCK:] = shift
 
 
 def pack(z, attn_float, attn_quant):
     tokens, d_in = attn_float.shape
+    whole = pl.BlockSpec(memory_space=pltpu.VMEM)
     return pl.pallas_call(
         pack_kernel,
-        out_shape=jax.ShapeDtypeStruct((16, tokens, d_in // 4 + BLOCK), BF16),
-        in_specs=[SCALAR, WHOLE, WHOLE],
-        out_specs=WHOLE,
-        compiler_params=params(),
+        out_shape=(
+            jax.ShapeDtypeStruct((16, tokens, d_in // 4), BF16),
+            jax.ShapeDtypeStruct((16, tokens, 2 * BLOCK), BF16),
+        ),
+        in_specs=[pl.BlockSpec(memory_space=pltpu.SMEM), whole, whole],
+        out_specs=(whole, whole),
+        compiler_params=params(40),
         name="pack",
     )(z.reshape(1), attn_float, attn_quant)
 
@@ -80,8 +85,8 @@
 
 
 def finish_kernel(at_ref, first_ref, second_ref, total_ref, *refs):
-    (side_ref, down_ref, cross_ref), outs = refs[:3], refs[3:]
-    core, yh, yl = at_ref[0], at_ref[1], at_ref[2]
+    moved_ref, outs = refs[0], refs[1:]
+    core, yh = at_ref[0], at_ref[1]
     width = first_ref.shape[2]
     for q, ref in enumerate((first_ref, second_ref)):
         quarter = core if q == 0 else 1 - core
@@ -93,57 +98,51 @@
                     total += ref[at + x].astype(F32)
                 start = pl.multiple_of((half * 2 + quarter) * width, width)
                 out[:, pl.ds(start, width)] = total.astype(BF16)
-    rows = outs[2].shape[0]
-    own = jnp.where(yh == 1, total_ref[:rows], down_ref[...].astype(F32))
-    other = jnp.where(yh == 1, side_ref[...].astype(F32), cross_ref[...].astype(F32))
-    outs[2][...] = jnp.where(yl == 0, own, other)
-    outs[3][...] = jnp.where(yl == 0, other, own)
+    total = jnp.where(yh == 1, total_ref[...], moved_ref[...].astype(F32))
+    outs[2][...] = total[:, :BLOCK]
+    outs[3][...] = total[:, BLOCK:]
 
 
 def finish(at, first, second, total, moved):
     tokens, cols = first.shape[1:]
-    rows = total.shape[0] // 2
+    rows = total.shape[0]
     return pl.pallas_call(
         finish_kernel,
         out_shape=(jax.ShapeDtypeStruct((tokens, 4 * cols), BF16),) * 2
         + (jax.ShapeDtypeStruct((rows, BLOCK), F32),) * 2,
-        in_specs=[SCALAR] + [WHOLE] * (3 + len(moved)),
+        in_specs=[SCALAR] + [WHOLE] * 4,
         out_specs=(WHOLE,) * 4,
         compiler_params=params(),
         name="finish",
-    )(at, first, second, total, *moved)
-
-
-def stats_kernel(acts_ref, after_ref, *outs):
+    )(at, first, second, total, moved)
+
+
+def stats_kernel(acts_ref, block_ref, after_ref, *outs):
     width = outs[0].shape[0]
     for j, out in enumerate(outs):
         out[...] = lax.dot_general(
-            acts_ref[:, j * width : (j + 1) * width],
-            acts_ref[:, 4 * width :],
+            acts_ref[:, 2 * j * width : (2 * j + 1) * width],
+            block_ref[...],
             (((0,), (0,)), ((), ())),
             preferred_element_type=F32,
         ).astype(out.dtype)
 
 
-def stats(acts, after):
-    width = (acts.shape[1] - BLOCK) // 4
+def stats(acts, block, after):
+    width = 2 * BLOCK
     return pl.pallas_call(
         stats_kernel,
-        out_shape=(jax.ShapeDtypeStruct((width, BLOCK), F32),)
-        + (jax.ShapeDtypeStruct((width, BLOCK), BF16),) * 3,
-        in_specs=[WHOLE, LEFT],
+        out_shape=(jax.ShapeDtypeStruct((width, width), F32),)
+        + (jax.ShapeDtypeStruct((width, width), BF16),) * 3,
+        in_specs=[WHOLE, WHOLE, LEFT],
         out_specs=(WHOLE,) * 4,
         compiler_params=params(),
         name="stats",
-    )(acts, after)
+    )(acts, block, after)
 
 
 def swap(a, axis):
     return lax.ppermute(a, axis, [(0, 1), (1, 0)])
-
-
-def ahead(a, axis, j):
-    return lax.ppermute(a, axis, [((i + j) % 4, i) for i in range(4)])
 
 
 def shards(attn_float, attn_quant, proj_weight, weight_codes, group_scales):
@@ -170,36 +169,39 @@
             for b in range(2):
                 pairs.append((a * 4 + c * 2 + b, (a ^ c) * 4 + c * 2 + (1 - b)))
     got = lax.ppermute(send, ("yh", "core", "yl"), pairs)
-    payload = pack(z, attn_float, attn_quant)
+
+    payload, block_part = pack(z, attn_float, attn_quant)
+    block_all = lax.all_to_all(block_part, PLANE, 0, 0, tiled=True)
+    block_all = block_all.reshape(16 * tokens, 2 * BLOCK)
+
     rows = jnp.concatenate([own, got], axis=0)
-    parts = [rows] + [ahead(rows, "z", j) for j in (1, 2, 3)]
-
-    acts = lax.all_to_all(payload, PLANE, 0, 0, tiled=True).reshape(16 * tokens, -1)
+    parts = [rows] + [
+        lax.ppermute(rows, "z", [((i + j) % 4, i) for i in range(4)]) for j in (1, 2, 3)
+    ]
     mine = jnp.concatenate(parts, axis=0)
     other = swap(mine, "core")
 
+    acts = lax.all_to_all(payload, PLANE, 0, 0, tiled=True).reshape(16 * tokens, 8 * features)
+
     def output(p):
         return lax.all_to_all(p.reshape(16, tokens, quarter), PLANE, 0, 0, tiled=True)
 
     first = project(acts, mine)
     result1 = output(first)
 
-    blocks = stats(acts, first)
-    total = blocks[0]
-    came = [ahead(blocks[j], "z", 4 - j) for j in (1, 2, 3)]
+    blocks = stats(acts, block_all, first)
+    came = [
+        lax.ppermute(blocks[j], "z", [(i, (i + j) % 4) for i in range(4)]) for j in (1, 2, 3)
+    ]
     second = project(acts, other)
     second, *came = lax.optimization_barrier((second, *came))
+    total = blocks[0]
     for block in came:
         total = total + block.astype(F32)
     total = (total + swap(total, "core")) * inverse
-    here, there = total[:features].astype(BF16), total[features:].astype(BF16)
-    moved = (
-        swap(there, "yl"),
-        swap(here, "yh"),
-        lax.ppermute(there, ("yh", "yl"), [(i, 3 - i) for i in range(4)]),
-    )
-    at = jnp.stack([core, yh, yl])
-    at, second, total, *moved = lax.optimization_barrier((at, second, total, *moved))
+    moved = swap(total.astype(BF16), "yh")
+    at = jnp.stack([core, yh])
+    at, second, total, moved = lax.optimization_barrier((at, second, total, moved))
     result2 = output(second)
     return finish(at, result1, result2, total, moved)
 

time: 171 us -> 177 us (1.035)
  starting transfers between devices: 29.8 us -> 34.2 us
  local copies, waits for them, and re-layouts: 11.4 us -> 15.7 us
  waiting for transfers between devices: 70.5 us -> 67.6 us
    unnamed x12 -> x16, local copies, waits for them, and re-layouts: 8.29 us -> 12.6 us
    all_to_all x1 -> x2, starting transfers between devices: 7.08 us -> 11.3 us  [the longest x1 7.09 us: shards(): lax.all_to_all(payload, PLANE, 0, 0, tiled=True)]
    ppermute x7 -> x6, starting transfers between devices: 13.7 us -> 11.5 us  [the longest x3 6.16 us: shards(): lax.ppermute(blocks[j], 'z', [(i, (i + j) % 4) for i in range(4)])]
    all_to_all x1 -> x2, waiting for transfers between devices: 23 us -> 21.1 us  [the longest x1 19.9 us: shards(): lax.all_to_all(payload, PLANE, 0, 0, tiled=True)]
    ppermute x7 -> x6, waiting for transfers between devices: 33.3 us -> 32.1 us  [the longest x3 32 us: shards(): lax.ppermute(rows, 'z', [((i + j) % 4, i) for i in range(4)])]
    ppermute x4 -> x3, starting transfers between devices: 2.7 us -> 3.6 us  [swap(): return lax.ppermute(a, axis, [(0, 1), (1, 0)])]
    ppermute x4 -> x3, waiting for transfers between devices: 6.73 us -> 6.87 us  [swap(): return lax.ppermute(a, axis, [(0, 1), (1, 0)])]
  transfers between devices with their start and end apart: 14 -> 13, of which waited for: 7 -> 6; matrix products, arithmetic and copies ran while one was open for 5% -> 5% of each run, Pallas kernels for 12% -> 11%
where the time goes in v23:
time: 177 us
  waiting for transfers between devices  67.6 us (38%)
  starting transfers between devices  34.2 us (19%)
  blocking collectives  33.4 us (19%)
  Pallas kernels  21.3 us (12%)
  local copies, waits for them, and re-layouts  15.7 us (9%)
  other arithmetic  3.56 us (2%)
    all_to_all x1, blocking collectives, output(): lax.all_to_all(p.reshape(16, tokens, quarter), PLANE, 0, 0, tiled=True)  33.4 us
    ppermute x3, waiting for transfers between devices, shards(): lax.ppermute(rows, 'z', [((i + j) % 4, i) for i in range(4)])  32 us
    all_to_all x1, waiting for transfers between devices, shards(): lax.all_to_all(payload, PLANE, 0, 0, tiled=True)  19.9 us
    pallas_call x2, Pallas kernels, project(): pl.pallas_call(project_kernel, out_shape=jax.ShapeDtypeStruct((rows, cols...  15.1 us
    unnamed x16, local copies, waits for them, and re-layouts  12.6 us
    ppermute x1, waiting for transfers between devices, shards(): got = lax.ppermute(send, ('yh', 'core', 'yl'), pairs)  7.52 us
    all_to_all x1, starting transfers between devices, shards(): lax.all_to_all(payload, PLANE, 0, 0, tiled=True)  7.09 us
    ppermute x3, waiting for transfers between devices, swap(): return lax.ppermute(a, axis, [(0, 1), (1, 0)])  6.87 us
  transfers between devices with their start and end apart: 13, of which 6 were waited for; matrix products, arithmetic and copies ran while one was open for 5% of the time, Pallas kernels for 11%

profile of v23, /device:TPU:0, one launch (start us, length us, event | category | flops | bytes accessed | tf_op | source)
XLA Modules:
  0.0 176.6 jit_solution(10487323245693754252)
XLA Ops:
  1.5 2.3 %fusion.3 = (bf16[256,1024]{1,0:T(8,128)(2,1)S(1)}, bf16[256,1024]{1,0:T(8,128)(2,1)S(1)}) fusion(s32[256,4096]{1,0:T(8,128)} %param.8, s32[]{:T(128)S(6)} %select_n.28, f32[2,1024]{1,0:T(2,128)S(1)} %get-tuple-element.36, bf16[256,4096]{1,0:T(8,128)(2,1)} %param.7, pred[]{:T(512)S(6)} %eq.7, f32[2,1024]{1,0:T(2,128)S(1)} %get-tuple-element.37, ...), kind=kLoop, calls=%fused_computation.6 | loop fusion | flops 2621440 | bytes 4210698 | tf_op jit(solution)/shard_map/jit(_where)/select_n | solution.py:162
  3.8 1.7 collective-permute-start
  5.5 7.5 %collective-permute-done = bf16[256,1024]{1,0:T(8,128)(2,1)S(1)} collective-permute-done((bf16[256,1024]{1,0:T(8,128)(2,1)S(1)}, bf16[256,1024]{1,0:T(8,128)(2,1)S(1)}, u32[]{:S(2)}, u32[]{:S(2)}) %collective-permute-start) | collective-permute-done | bytes 524320 | tf_op jit(solution)/shard_map/ppermute | solution.py:171
  13.0 1.1 pad_maximum_fusion
  14.2 4.1 %collective-permute-start.1 = (bf16[512,1024]{1,0:T(8,128)(2,1)}, bf16[512,1024]{1,0:T(8,128)(2,1)}, u32[]{:S(2)}, u32[]{:S(2)}) collective-permute-start(bf16[512,1024]{1,0:T(8,128)(2,1)} %pad_maximum_fusion), channel_id=1, source_target_pairs={{4,0},{8,4},{12,8},{0,12},{5,1},{9,5},{13,9},{1,13},{6,2},{10,6},{... | collective-permute-start | bytes 3145736 | tf_op jit(solution)/shard_map/ppermute | solution.py:179
  18.3 1.3 collective-permute-start.3
  19.6 1.2 pack.1
  20.8 2.0 %copy-done.2 = bf16[16,64,2048]{2,1,0:T(8,128)(2,1)} copy-done((bf16[16,64,2048]{2,1,0:T(8,128)(2,1)}, bf16[16,64,2048]{2,1,0:T(8,128)(2,1)S(1)}, u32[]{:S(2)}) %copy-start.2) | copy-done | bytes 4194328
  22.8 7.1 %all-to-all-start = ((bf16[16,64,2048]{2,1,0:T(8,128)(2,1)}), bf16[16,64,2048]{2,1,0:T(8,128)(2,1)}, u32[]{:S(2)}, u32[]{:S(2)}) async-start(bf16[16,64,2048]{2,1,0:T(8,128)(2,1)} %copy-done.2), calls=%async_computation | async-start | bytes 8388608 | tf_op jit(solution)/shard_map/all_to_all | solution.py:184
  29.9 0.9 constant_dynamic-update-slice_fusion.4
  31.6 32.0 %collective-permute-done.1 = bf16[512,1024]{1,0:T(8,128)(2,1)} collective-permute-done((bf16[512,1024]{1,0:T(8,128)(2,1)}, bf16[512,1024]{1,0:T(8,128)(2,1)}, u32[]{:S(2)}, u32[]{:S(2)}) %collective-permute-start.1) | collective-permute-done | bytes 1048608 | tf_op jit(solution)/shard_map/ppermute | solution.py:179
  63.6 2.3 %constant_dynamic-update-slice_fusion.2 = bf16[2048,1024]{1,0:T(8,128)(2,1)} fusion(bf16[2048,1024]{1,0:T(8,128)(2,1)} %constant_dynamic-update-slice_fusion.3, bf16[512,1024]{1,0:T(8,128)(2,1)} %collective-permute-done.1), kind=kLoop, calls=%fused_computation.11 | loop fusion | bytes 2097152
  65.9 2.3 %constant_dynamic-update-slice_fusion.1 = bf16[2048,1024]{1,0:T(8,128)(2,1)} fusion(bf16[2048,1024]{1,0:T(8,128)(2,1)} %constant_dynamic-update-slice_fusion.2, bf16[512,1024]{1,0:T(8,128)(2,1)} %collective-permute-done.2), kind=kLoop, calls=%fused_computation.10 | loop fusion | bytes 2097152
  68.2 2.3 %constant_dynamic-update-slice_fusion.weight_ref = bf16[2048,1024]{1,0:T(8,128)(2,1)} fusion(bf16[2048,1024]{1,0:T(8,128)(2,1)} %constant_dynamic-update-slice_fusion.1, bf16[512,1024]{1,0:T(8,128)(2,1)} %collective-permute-done.3), kind=kLoop, calls=%fused_computation.9 | loop fusion | bytes 2097152 | tf_op jit(solution)/shard_map/concatenate | solution.py:181
  70.5 19.9 %all-to-all-done = bf16[16,64,2048]{2,1,0:T(8,128)(2,1)} async-done(((bf16[16,64,2048]{2,1,0:T(8,128)(2,1)}), bf16[16,64,2048]{2,1,0:T(8,128)(2,1)}, u32[]{:S(2)}, u32[]{:S(2)}) %all-to-all-start) | async-done | bytes 4194336 | tf_op jit(solution)/shard_map/all_to_all | solution.py:184
  90.4 4.2 %all-to-all-start.1 = ((bf16[16,64,256]{2,1,0:T(8,128)(2,1)}), bf16[16,64,256]{2,1,0:T(8,128)(2,1)S(1)}, u32[]{:S(2)}, u32[]{:S(2)}) async-start(bf16[16,64,256]{2,1,0:T(8,128)(2,1)} %get-tuple-element.19), calls=%async_computation.1 | async-start | bytes 1048576 | tf_op jit(solution)/shard_map/all_to_all | solution.py:174
  94.7 7.6 %project.3.after_ref = bf16[1024,1024]{1,0:T(8,128)(2,1)S(1)} custom-call(bf16[1024,2048]{1,0:T(8,128)(2,1)} %bitcast.3.acts_ref, bf16[2048,1024]{1,0:T(8,128)(2,1)} %constant_dynamic-update-slice_fusion.weight_ref), custom_call_target="tpu_custom_call" | custom-call | flops 4294967296 | bytes 12582912 | tf_op jit(solution)/shard_map/project/pallas_call | solution.py:73
  102.2 1.4 copy-done
  103.6 1.2 all-to-all-done.1
  104.8 6.0 %all-to-all-start.2 = ((bf16[16,64,1024]{2,1,0:T(8,128)(2,1)}), bf16[16,64,1024]{2,1,0:T(8,128)(2,1)S(1)}, u32[]{:S(2)}, u32[]{:S(2)}) async-start(bf16[16,64,1024]{2,1,0:T(8,128)(2,1)} %bitcast.19), calls=%async_computation.2 | async-start | bytes 4194304 | tf_op jit(solution)/shard_map/all_to_all | solution.py:187
  110.8 1.6 copy-done.1
  112.4 3.0 %stats.1 = (f32[256,256]{1,0:T(8,128)S(1)}, bf16[256,256]{1,0:T(8,128)(2,1)S(1)}, bf16[256,256]{1,0:T(8,128)(2,1)S(1)}, bf16[256,256]{1,0:T(8,128)(2,1)S(1)}) custom-call(bf16[1024,2048]{1,0:T(8,128)(2,1)} %bitcast.3.acts_ref, bf16[1024,256]{1,0:T(8,128)(2,1)S(1)} %bitcast.21, bf16[1024,1024]{1,0:T(8,128)(2,1)S(1)} %copy-done.1), custom_call_target="tpu_custom_call" | custom-call | tf_op jit(solution)/shard_map/stats/pallas_call | solution.py:133
  115.4 2.3 %collective-permute-start.5 = (bf16[256,256]{1,0:T(8,128)(2,1)S(1)}, bf16[256,256]{1,0:T(8,128)(2,1)S(1)}, u32[]{:S(2)}, u32[]{:S(2)}) collective-permute-start(bf16[256,256]{1,0:T(8,128)(2,1)S(1)} %get-tuple-element.20), channel_id=1, source_target_pairs={{0,4},{4,8},{8,12},{12,0},{1,5},{5,9},{9,13},{13,1},{2,6},{6,10},{... | collective-permute-start | bytes 393224 | tf_op jit(solution)/shard_map/ppermute | solution.py:194
  117.7 2.4 %collective-permute-start.6 = (bf16[256,256]{1,0:T(8,128)(2,1)S(1)}, bf16[256,256]{1,0:T(8,128)(2,1)S(1)}, u32[]{:S(2)}, u32[]{:S(2)}) collective-permute-start(bf16[256,256]{1,0:T(8,128)(2,1)S(1)} %get-tuple-element.21), channel_id=1, source_target_pairs={{0,8},{4,12},{8,0},{12,4},{1,9},{5,13},{9,1},{13,5},{2,10},{6,14},... | collective-permute-start | bytes 393224 | tf_op jit(solution)/shard_map/ppermute | solution.py:194
  120.1 1.5 collective-permute-start.7
  121.6 7.6 %project.2 = bf16[1024,1024]{1,0:T(8,128)(2,1)S(1)} custom-call(bf16[1024,2048]{1,0:T(8,128)(2,1)} %bitcast.3.acts_ref, bf16[2048,1024]{1,0:T(8,128)(2,1)} %collective-permute-done.4.weight_ref), custom_call_target="tpu_custom_call" | custom-call | flops 4294967296 | bytes 12582912 | tf_op jit(solution)/shard_map/project/pallas_call | solution.py:73
  129.2 1.3 copy-done.3
  130.7 1.5 collective-permute-done.8
  132.2 3.5 %collective-permute-start.9 = (bf16[256,256]{1,0:T(8,128)(2,1)S(1)}, bf16[256,256]{1,0:T(8,128)(2,1)S(1)}, u32[]{:S(2)}, u32[]{:S(2)}) collective-permute-start(bf16[256,256]{1,0:T(8,128)(2,1)S(1)} %get-tuple-element.32), channel_id=1, source_target_pairs={{0,64},{64,0},{1,65},{65,1},{2,66},{66,2},{3,67},{67,3},{4,68},{68... | collective-permute-start | bytes 393224 | tf_op jit(solution)/shard_map/ppermute | solution.py:145
  135.8 5.3 %collective-permute-done.9.refs_0_ = bf16[256,256]{1,0:T(8,128)(2,1)S(1)} collective-permute-done((bf16[256,256]{1,0:T(8,128)(2,1)S(1)}, bf16[256,256]{1,0:T(8,128)(2,1)S(1)}, u32[]{:S(2)}, u32[]{:S(2)}) %collective-permute-start.9) | collective-permute-done | bytes 131104 | tf_op jit(solution)/shard_map/ppermute | solution.py:145
  141.2 33.4 %all_to_all.20.second_ref = bf16[16,64,1024]{2,1,0:T(8,128)(2,1)S(1)} all-to-all(bf16[16,64,1024]{2,1,0:T(8,128)(2,1)} %bitcast.20), channel_id=1, replica_groups=mesh['yh'=2,'core'=2,'yl'=2,'z'=4,'x'=4] {'yh','yl','x'}, dimensions={0} | all-to-all | bytes 4194304 | tf_op jit(solution)/shard_map/all_to_all | solution.py:187
  174.5 2.0 %finish.1 = (bf16[64,4096]{1,0:T(8,128)(2,1)}, bf16[64,4096]{1,0:T(8,128)(2,1)}, f32[256,128]{1,0:T(8,128)}, f32[256,128]{1,0:T(8,128)}) custom-call(s32[2]{0:T(128)S(1)} %pad_add_fusion.at_ref, bf16[16,64,1024]{2,1,0:T(8,128)(2,1)S(1)} %all-to-all-done.2.first_ref, bf16[16,64,1024]{2,1,0:T(8,128)(2,1)S(1)} %all_to_all.20.second_ref, ...), custom_call_target="tpu_custom_call" | custom-call | tf_op jit(solution)/shard_map/finish/pallas_call | solution.py:109
  (23 shorter events, 2.0 us)
Async XLA Ops:
  0.6 18.9 %copy-start.4 = (bf16[64,8192]{1,0:T(8,128)(2,1)S(1)}, bf16[64,8192]{1,0:T(8,128)(2,1)}, u32[]{:S(2)}) copy-start(bf16[64,8192]{1,0:T(8,128)(2,1)} %float_ref.1) | copy-start | bytes 3145732
  0.6 18.9 %copy-start.5 = (bf16[64,8192]{1,0:T(8,128)(2,1)S(1)}, bf16[64,8192]{1,0:T(8,128)(2,1)}, u32[]{:S(2)}) copy-start(bf16[64,8192]{1,0:T(8,128)(2,1)} %quant_ref.1) | copy-start | bytes 3145732
  3.8 9.3 %collective-permute-start = (bf16[256,1024]{1,0:T(8,128)(2,1)S(1)}, bf16[256,1024]{1,0:T(8,128)(2,1)S(1)}, u32[]{:S(2)}, u32[]{:S(2)}) collective-permute-start(bf16[256,1024]{1,0:T(8,128)(2,1)S(1)} %get-tuple-element.34), channel_id=1, source_target_pairs={{0,16},{16,0},{32,112},{48,96},{64,80},{80,64},{96,48},{112,32},{1... | collective-permute-start | bytes 1572872 | tf_op jit(solution)/shard_map/ppermute | solution.py:171
  14.2 49.4 %collective-permute-start.1 = (bf16[512,1024]{1,0:T(8,128)(2,1)}, bf16[512,1024]{1,0:T(8,128)(2,1)}, u32[]{:S(2)}, u32[]{:S(2)}) collective-permute-start(bf16[512,1024]{1,0:T(8,128)(2,1)} %pad_maximum_fusion), channel_id=1, source_target_pairs={{4,0},{8,4},{12,8},{0,12},{5,1},{9,5},{13,9},{1,13},{6,2},{10,6},{... | collective-permute-start | bytes 3145736 | tf_op jit(solution)/shard_map/ppermute | solution.py:179
  18.3 47.6 %collective-permute-start.2 = (bf16[512,1024]{1,0:T(8,128)(2,1)}, bf16[512,1024]{1,0:T(8,128)(2,1)}, u32[]{:S(2)}, u32[]{:S(2)}) collective-permute-start(bf16[512,1024]{1,0:T(8,128)(2,1)} %pad_maximum_fusion), channel_id=1, source_target_pairs={{8,0},{12,4},{0,8},{4,12},{9,1},{13,5},{1,9},{5,13},{10,2},{14,6},... | collective-permute-start | bytes 3145736 | tf_op jit(solution)/shard_map/ppermute | solution.py:179
  18.3 49.9 %collective-permute-start.3 = (bf16[512,1024]{1,0:T(8,128)(2,1)}, bf16[512,1024]{1,0:T(8,128)(2,1)}, u32[]{:S(2)}, u32[]{:S(2)}) collective-permute-start(bf16[512,1024]{1,0:T(8,128)(2,1)} %pad_maximum_fusion), channel_id=1, source_target_pairs={{12,0},{0,4},{4,8},{8,12},{13,1},{1,5},{5,9},{9,13},{14,2},{2,6},{... | collective-permute-start | bytes 3145736 | tf_op jit(solution)/shard_map/ppermute | solution.py:179
  20.8 2.0 %copy-start.2 = (bf16[16,64,2048]{2,1,0:T(8,128)(2,1)}, bf16[16,64,2048]{2,1,0:T(8,128)(2,1)S(1)}, u32[]{:S(2)}) copy-start(bf16[16,64,2048]{2,1,0:T(8,128)(2,1)S(1)} %get-tuple-element.18) | copy-start | bytes 12582916
  22.8 67.6 %all-to-all-start = ((bf16[16,64,2048]{2,1,0:T(8,128)(2,1)}), bf16[16,64,2048]{2,1,0:T(8,128)(2,1)}, u32[]{:S(2)}, u32[]{:S(2)}) async-start(bf16[16,64,2048]{2,1,0:T(8,128)(2,1)} %copy-done.2), calls=%async_computation | async-start | bytes 8388608 | tf_op jit(solution)/shard_map/all_to_all | solution.py:184
  70.5 51.1 %collective-permute-start.4 = (bf16[2048,1024]{1,0:T(8,128)(2,1)}, bf16[2048,1024]{1,0:T(8,128)(2,1)}, u32[]{:S(2)}, u32[]{:S(2)}) collective-permute-start(bf16[2048,1024]{1,0:T(8,128)(2,1)} %constant_dynamic-update-slice_fusion.weight_ref), channel_id=1, source_target_pairs={{0,32},{32,0},{1,33},{33,1},{2,34},{34,2},{3,35},{35,3},{4,36},{36... | collective-permute-start | bytes 12582920 | tf_op jit(solution)/shard_map/ppermute | solution.py:145
  90.4 14.4 %all-to-all-start.1 = ((bf16[16,64,256]{2,1,0:T(8,128)(2,1)}), bf16[16,64,256]{2,1,0:T(8,128)(2,1)S(1)}, u32[]{:S(2)}, u32[]{:S(2)}) async-start(bf16[16,64,256]{2,1,0:T(8,128)(2,1)} %get-tuple-element.19), calls=%async_computation.1 | async-start | bytes 1048576 | tf_op jit(solution)/shard_map/all_to_all | solution.py:174
  102.2 1.4 copy-start
  104.8 36.4 %all-to-all-start.2 = ((bf16[16,64,1024]{2,1,0:T(8,128)(2,1)}), bf16[16,64,1024]{2,1,0:T(8,128)(2,1)S(1)}, u32[]{:S(2)}, u32[]{:S(2)}) async-start(bf16[16,64,1024]{2,1,0:T(8,128)(2,1)} %bitcast.19), calls=%async_computation.2 | async-start | bytes 4194304 | tf_op jit(solution)/shard_map/all_to_all | solution.py:187
  110.8 1.6 copy-start.1
  115.4 15.1 %collective-permute-start.5 = (bf16[256,256]{1,0:T(8,128)(2,1)S(1)}, bf16[256,256]{1,0:T(8,128)(2,1)S(1)}, u32[]{:S(2)}, u32[]{:S(2)}) collective-permute-start(bf16[256,256]{1,0:T(8,128)(2,1)S(1)} %get-tuple-element.20), channel_id=1, source_target_pairs={{0,4},{4,8},{8,12},{12,0},{1,5},{5,9},{9,13},{13,1},{2,6},{6,10},{... | collective-permute-start | bytes 393224 | tf_op jit(solution)/shard_map/ppermute | solution.py:194
  117.7 12.8 %collective-permute-start.6 = (bf16[256,256]{1,0:T(8,128)(2,1)S(1)}, bf16[256,256]{1,0:T(8,128)(2,1)S(1)}, u32[]{:S(2)}, u32[]{:S(2)}) collective-permute-start(bf16[256,256]{1,0:T(8,128)(2,1)S(1)} %get-tuple-element.21), channel_id=1, source_target_pairs={{0,8},{4,12},{8,0},{12,4},{1,9},{5,13},{9,1},{13,5},{2,10},{6,14},... | collective-permute-start | bytes 393224 | tf_op jit(solution)/shard_map/ppermute | solution.py:194
  120.1 10.4 %collective-permute-start.7 = (bf16[256,256]{1,0:T(8,128)(2,1)S(1)}, bf16[256,256]{1,0:T(8,128)(2,1)S(1)}, u32[]{:S(2)}, u32[]{:S(2)}) collective-permute-start(bf16[256,256]{1,0:T(8,128)(2,1)S(1)} %get-tuple-element.22), channel_id=1, source_target_pairs={{0,12},{4,0},{8,4},{12,8},{1,13},{5,1},{9,5},{13,9},{2,14},{6,2},{... | collective-permute-start | bytes 393224 | tf_op jit(solution)/shard_map/ppermute | solution.py:194
  129.2 1.3 copy-start.3
  130.6 1.6 collective-permute-start.8
  132.2 8.9 %collective-permute-start.9 = (bf16[256,256]{1,0:T(8,128)(2,1)S(1)}, bf16[256,256]{1,0:T(8,128)(2,1)S(1)}, u32[]{:S(2)}, u32[]{:S(2)}) collective-permute-start(bf16[256,256]{1,0:T(8,128)(2,1)S(1)} %get-tuple-element.32), channel_id=1, source_target_pairs={{0,64},{64,0},{1,65},{65,1},{2,66},{66,2},{3,67},{67,3},{4,68},{68... | collective-permute-start | bytes 393224 | tf_op jit(solution)/shard_map/ppermute | solution.py:145

commit v24 on v17

--- a/solution.py
+++ b/solution.py
@@ -19,7 +19,7 @@
 
 
 def params():
-    return pltpu.CompilerParams(vmem_limit_bytes=6 << 20)
+    return pltpu.CompilerParams(vmem_limit_bytes=12 << 20)
 
 
 def pack_kernel(z_ref, float_ref, quant_ref, out_ref):
@@ -146,6 +146,21 @@
     )(acts, after)
 
 
+def tick_kernel(acts_ref, out_ref):
+    out_ref[...] = jnp.zeros_like(out_ref)
+
+
+def tick(acts):
+    return pl.pallas_call(
+        tick_kernel,
+        out_shape=jax.ShapeDtypeStruct((8, 128), F32),
+        in_specs=[LEFT],
+        out_specs=WHOLE,
+        compiler_params=params(),
+        name="tick",
+    )(acts)
+
+
 def swap(a, axis):
     return lax.ppermute(a, axis, [(0, 1), (1, 0)])
 
@@ -181,11 +196,13 @@
     own = weight(yh, col)
 
     payload = pack(z, attn_float, attn_quant)
-    payload, got = lax.optimization_barrier((payload, got))
     rows = jnp.concatenate([own, got], axis=0)
+    payload, rows = lax.optimization_barrier((payload, rows))
     parts = [rows] + [ahead(rows, "z", j) for j in (1, 2, 3)]
 
     acts = lax.all_to_all(payload, PLANE, 0, 0, tiled=True).reshape(16 * tokens, -1)
+    there = tick(acts)
+    there, *parts = lax.optimization_barrier((there, *parts))
     others = [swap(p, "core") for p in parts]
 
     def output(p):

time: 168 us -> 168 us (level)
  waiting for transfers between devices: 68.9 us -> 71.1 us
    ppermute x6, waiting for transfers between devices: 46.4 us -> 50.9 us  [ahead(): return lax.ppermute(a, axis, [((i + j) % 4, i) for i in range(4)])]
    ppermute x1, waiting for transfers between devices: 5.12 us -> 3.08 us  [shards(): got = lax.ppermute(send, ('yh', 'core', 'yl'), pairs)]
    ppermute x6, starting transfers between devices: 13.2 us -> 11.3 us  [ahead(): return lax.ppermute(a, axis, [((i + j) % 4, i) for i in range(4)])]
    unnamed x28 -> x24, local copies, waits for them, and re-layouts: 7.15 us -> 6.38 us
  transfers between devices with their start and end apart: 17 -> 17, of which waited for: 8 -> 7; matrix products, arithmetic and copies ran while one was open for 1% -> 1% of each run, Pallas kernels for 6% -> 6%
where the time goes in v24:
time: 168 us; the launch traced here: 167 us
  waiting for transfers between devices  71.1 us (42%)
  blocking collectives  34.6 us (21%)
  starting transfers between devices  30.7 us (18%)
  Pallas kernels  19.8 us (12%)
  local copies, waits for them, and re-layouts  6.47 us (4%)
  other arithmetic  3.89 us (2%)
    ppermute x6, waiting for transfers between devices, ahead(): return lax.ppermute(a, axis, [((i + j) % 4, i) for i in range(4)])  50.9 us
    all_to_all x1, blocking collectives, output(): lax.all_to_all(p.reshape(16, tokens, quarter), PLANE, 0, 0, tiled=True)  34.6 us
    all_to_all x1, waiting for transfers between devices, shards(): lax.all_to_all(payload, PLANE, 0, 0, tiled=True).reshape(16 * tokens, -1)  14.8 us
    pallas_call x2, Pallas kernels, project(): pl.pallas_call(project_kernel, out_shape=jax.ShapeDtypeStruct((rows, cols...  13.7 us
    ppermute x6, starting transfers between devices, ahead(): return lax.ppermute(a, axis, [((i + j) % 4, i) for i in range(4)])  11.3 us
    all_to_all x1, starting transfers between devices, shards(): lax.all_to_all(payload, PLANE, 0, 0, tiled=True).reshape(16 * tokens, -1)  7.17 us
    unnamed x24, local copies, waits for them, and re-layouts  6.38 us
    all_to_all x1, starting transfers between devices, output(): lax.all_to_all(p.reshape(16, tokens, quarter), PLANE, 0, 0, tiled=True)  4.6 us
  transfers between devices with their start and end apart: 17, of which 7 were waited for; matrix products, arithmetic and copies ran while one was open for 1% of the time, Pallas kernels for 6%

profile of v24, /device:TPU:0, one launch (start us, length us, event | category | flops | bytes accessed | tf_op | source)
XLA Modules:
  0.0 167.3 jit_solution(13548014484434464459)
XLA Ops:
  0.7 0.7 copy-done
  1.4 1.7 %fusion.2 = bf16[256,1024]{1,0:T(8,128)(2,1)S(1)} fusion(s32[256,4096]{1,0:T(8,128)} %param.8, s32[]{:T(128)S(6)} %select_n.26, f32[2,1024]{1,0:T(2,128)S(1)} %constant_dynamic-slice_fusion.1, bf16[256,4096]{1,0:T(8,128)(2,1)} %param.7, pred[]{:T(512)S(6)} %eq.7), kind=kLoop, calls=%fused_computation.5 | loop fusion | flops 1310720 | bytes 2105349 | tf_op jit(solution)/shard_map/jit(_where)/select_n | solution.py:186
  3.1 1.7 %collective-permute-start = (bf16[256,1024]{1,0:T(8,128)(2,1)S(1)}, bf16[256,1024]{1,0:T(8,128)(2,1)S(1)}, u32[]{:S(2)}, u32[]{:S(2)}) collective-permute-start(bf16[256,1024]{1,0:T(8,128)(2,1)S(1)} %fusion.2), channel_id=1, source_target_pairs={{0,16},{16,0},{32,112},{48,96},{64,80},{80,64},{96,48},{112,32},{1... | collective-permute-start | bytes 1572872 | tf_op jit(solution)/shard_map/ppermute | solution.py:194
  4.9 1.9 %fusion.3 = bf16[256,1024]{1,0:T(8,128)(2,1)S(1)} fusion(s32[256,4096]{1,0:T(8,128)} %param.8, s32[]{:T(128)S(6)} %select_n.28, f32[2,1024]{1,0:T(2,128)S(1)} %constant_dynamic-slice_fusion, bf16[256,4096]{1,0:T(8,128)(2,1)} %param.7, pred[]{:T(512)S(6)} %eq.6), kind=kLoop, calls=%fused_computation.6 | loop fusion | flops 1310720 | bytes 2105349 | tf_op jit(solution)/shard_map/jit(_where)/select_n | solution.py:186
  6.9 0.3 pack.1
  7.2 2.1 %copy-done.1 = bf16[16,64,2176]{2,1,0:T(8,128)(2,1)} copy-done((bf16[16,64,2176]{2,1,0:T(8,128)(2,1)}, bf16[16,64,2176]{2,1,0:T(8,128)(2,1)S(1)}, u32[]{:S(2)}) %copy-start.1) | copy-done | bytes 4456472
  9.3 3.1 %collective-permute-done = bf16[256,1024]{1,0:T(8,128)(2,1)S(1)} collective-permute-done((bf16[256,1024]{1,0:T(8,128)(2,1)S(1)}, bf16[256,1024]{1,0:T(8,128)(2,1)S(1)}, u32[]{:S(2)}, u32[]{:S(2)}) %collective-permute-start) | collective-permute-done | bytes 524320 | tf_op jit(solution)/shard_map/ppermute | solution.py:194
  12.4 7.2 %all-to-all-start = ((bf16[16,64,2176]{2,1,0:T(8,128)(2,1)}), bf16[16,64,2176]{2,1,0:T(8,128)(2,1)}, u32[]{:S(2)}, u32[]{:S(2)}) async-start(bf16[16,64,2176]{2,1,0:T(8,128)(2,1)} %copy-done.1), calls=%async_computation | async-start | bytes 8912896 | tf_op jit(solution)/shard_map/all_to_all | solution.py:203
  19.6 4.1 %collective-permute-start.1 = (bf16[512,1024]{1,0:T(8,128)(2,1)S(1)}, bf16[512,1024]{1,0:T(8,128)(2,1)S(1)}, u32[]{:S(2)}, u32[]{:S(2)}) collective-permute-start(bf16[512,1024]{1,0:T(8,128)(2,1)S(1)} %pad_maximum_fusion.refs_0_), channel_id=1, source_target_pairs={{4,0},{8,4},{12,8},{0,12},{5,1},{9,5},{13,9},{1,13},{6,2},{10,6},{... | collective-permute-start | bytes 3145736 | tf_op jit(solution)/shard_map/ppermute | solution.py:169
  23.7 1.3 collective-permute-start.3
  25.0 43.2 %collective-permute-done.1.refs_1_ = bf16[512,1024]{1,0:T(8,128)(2,1)S(1)} collective-permute-done((bf16[512,1024]{1,0:T(8,128)(2,1)S(1)}, bf16[512,1024]{1,0:T(8,128)(2,1)S(1)}, u32[]{:S(2)}, u32[]{:S(2)}) %collective-permute-start.1) | collective-permute-done | bytes 1048608 | tf_op jit(solution)/shard_map/ppermute | solution.py:169
  68.2 1.0 copy-done.9
  69.2 2.4 %collective-permute-done.3.refs_3_ = bf16[512,1024]{1,0:T(8,128)(2,1)S(1)} collective-permute-done((bf16[512,1024]{1,0:T(8,128)(2,1)S(1)}, bf16[512,1024]{1,0:T(8,128)(2,1)S(1)}, u32[]{:S(2)}, u32[]{:S(2)}) %collective-permute-start.3) | collective-permute-done | bytes 1048608 | tf_op jit(solution)/shard_map/ppermute | solution.py:169
  71.6 14.8 %all-to-all-done = bf16[16,64,2176]{2,1,0:T(8,128)(2,1)} async-done(((bf16[16,64,2176]{2,1,0:T(8,128)(2,1)}), bf16[16,64,2176]{2,1,0:T(8,128)(2,1)}, u32[]{:S(2)}, u32[]{:S(2)}) %all-to-all-start) | async-done | bytes 4456480 | tf_op jit(solution)/shard_map/all_to_all | solution.py:203
  86.4 1.2 copy-done.10
  87.6 7.3 %project.2.after_ref = bf16[1024,1024]{1,0:T(8,128)(2,1)} custom-call(bf16[1024,2176]{1,0:T(8,128)(2,1)} %bitcast.6.acts_ref, bf16[512,1024]{1,0:T(8,128)(2,1)S(1)} %pad_maximum_fusion.refs_0_, bf16[512,1024]{1,0:T(8,128)(2,1)S(1)} %copy-done.10, bf16[512,1024]{1,0:T(8,128)(2,1)S(1)} %collective-permute-done.2.refs_2_, ...), custom_call_target="tpu_custom_call" | custom-call | flops 4294967296 | bytes 12582912 | tf_op jit(solution)/shard_map/project/pallas_call | solution.py:75
  95.0 4.6 %all-to-all-start.1 = ((bf16[16,64,1024]{2,1,0:T(8,128)(2,1)}), bf16[16,64,1024]{2,1,0:T(8,128)(2,1)S(1)}, u32[]{:S(2)}, u32[]{:S(2)}) async-start(bf16[16,64,1024]{2,1,0:T(8,128)(2,1)} %bitcast.7), calls=%async_computation.1 | async-start | bytes 4194304 | tf_op jit(solution)/shard_map/all_to_all | solution.py:209
  99.6 3.7 %stats.1 = (f32[512,128]{1,0:T(8,128)S(1)}, bf16[512,128]{1,0:T(8,128)(2,1)S(1)}, bf16[512,128]{1,0:T(8,128)(2,1)S(1)}, bf16[512,128]{1,0:T(8,128)(2,1)S(1)}) custom-call(bf16[1024,2176]{1,0:T(8,128)(2,1)} %bitcast.6.acts_ref, bf16[1024,1024]{1,0:T(8,128)(2,1)} %project.2.after_ref), custom_call_target="tpu_custom_call" | custom-call | tf_op jit(solution)/shard_map/stats/pallas_call | solution.py:138
  103.3 4.1 %collective-permute-start.10 = (bf16[512,128]{1,0:T(8,128)(2,1)S(1)}, bf16[512,128]{1,0:T(8,128)(2,1)S(1)}, u32[]{:S(2)}, u32[]{:S(2)}) collective-permute-start(bf16[512,128]{1,0:T(8,128)(2,1)S(1)} %get-tuple-element.31), channel_id=1, source_target_pairs={{4,0},{8,4},{12,8},{0,12},{5,1},{9,5},{13,9},{1,13},{6,2},{10,6},{... | collective-permute-start | bytes 393224 | tf_op jit(solution)/shard_map/ppermute | solution.py:169
  107.4 1.9 %collective-permute-start.9 = (bf16[512,128]{1,0:T(8,128)(2,1)S(1)}, bf16[512,128]{1,0:T(8,128)(2,1)S(1)}, u32[]{:S(2)}, u32[]{:S(2)}) collective-permute-start(bf16[512,128]{1,0:T(8,128)(2,1)S(1)} %get-tuple-element.30), channel_id=1, source_target_pairs={{8,0},{12,4},{0,8},{4,12},{9,1},{13,5},{1,9},{5,13},{10,2},{14,6},... | collective-permute-start | bytes 393224 | tf_op jit(solution)/shard_map/ppermute | solution.py:169
  109.3 0.5 collective-permute-start.5
  109.8 1.5 collective-permute-done.10
  111.3 3.7 %collective-permute-done.8 = bf16[512,128]{1,0:T(8,128)(2,1)S(1)} collective-permute-done((bf16[512,128]{1,0:T(8,128)(2,1)S(1)}, bf16[512,128]{1,0:T(8,128)(2,1)S(1)}, u32[]{:S(2)}, u32[]{:S(2)}) %collective-permute-start.8) | collective-permute-done | bytes 131104 | tf_op jit(solution)/shard_map/ppermute | solution.py:169
  115.1 0.6 collective-permute-start.11
  115.7 2.3 %collective-permute-done.11 = f32[512,128]{1,0:T(8,128)S(1)} collective-permute-done((f32[512,128]{1,0:T(8,128)S(1)}, f32[512,128]{1,0:T(8,128)S(1)}, u32[]{:S(2)}, u32[]{:S(2)}) %collective-permute-start.11) | collective-permute-done | bytes 262176 | tf_op jit(solution)/shard_map/ppermute | solution.py:165
  118.1 2.0 %collective-permute-start.12 = (bf16[256,128]{1,0:T(8,128)(2,1)S(1)}, bf16[256,128]{1,0:T(8,128)(2,1)S(1)}, u32[]{:S(2)}, u32[]{:S(2)}) collective-permute-start(bf16[256,128]{1,0:T(8,128)(2,1)S(1)} %get-tuple-element.41), channel_id=1, source_target_pairs={{0,16},{16,0},{1,17},{17,1},{2,18},{18,2},{3,19},{19,3},{4,20},{20... | collective-permute-start | bytes 196616 | tf_op jit(solution)/shard_map/ppermute | solution.py:165
  120.1 2.1 %collective-permute-start.14 = (bf16[256,128]{1,0:T(8,128)(2,1)S(1)}, bf16[256,128]{1,0:T(8,128)(2,1)S(1)}, u32[]{:S(2)}, u32[]{:S(2)}) collective-permute-start(bf16[256,128]{1,0:T(8,128)(2,1)S(1)} %get-tuple-element.41), channel_id=1, source_target_pairs={{0,80},{16,64},{64,16},{80,0},{1,81},{17,65},{65,17},{81,1},{2,82}... | collective-permute-start | bytes 196616 | tf_op jit(solution)/shard_map/ppermute | solution.py:224
  122.2 0.7 collective-permute-start.13
  122.9 6.4 %project.3 = bf16[1024,1024]{1,0:T(8,128)(2,1)S(1)} custom-call(bf16[1024,2176]{1,0:T(8,128)(2,1)} %bitcast.6.acts_ref, bf16[512,1024]{1,0:T(8,128)(2,1)S(1)} %collective-permute-done.4.refs_0_, bf16[512,1024]{1,0:T(8,128)(2,1)S(1)} %collective-permute-done.5.refs_1_, bf16[512,1024]{1,0:T(8,128)(2,1)S(1)} %collective-permute-done.6.refs_2_, ...), custom_call_target="tpu_custom_call" | custom-call | flops 4294967296 | bytes 12582912 | tf_op jit(solution)/shard_map/project/pallas_call | solution.py:75
  129.3 1.3 copy-done.2
  130.7 34.6 %all_to_all.15.second_ref = bf16[16,64,1024]{2,1,0:T(8,128)(2,1)S(1)} all-to-all(bf16[16,64,1024]{2,1,0:T(8,128)(2,1)} %bitcast.19), channel_id=1, replica_groups=mesh['yh'=2,'core'=2,'yl'=2,'z'=4,'x'=4] {'yh','yl','x'}, dimensions={0} | all-to-all | bytes 4194304 | tf_op jit(solution)/shard_map/all_to_all | solution.py:209
  165.3 2.0 %finish.1 = (bf16[64,4096]{1,0:T(8,128)(2,1)}, bf16[64,4096]{1,0:T(8,128)(2,1)}, f32[256,128]{1,0:T(8,128)}, f32[256,128]{1,0:T(8,128)}) custom-call(s32[3]{0:T(128)S(1)} %pad_add_fusion.at_ref, bf16[16,64,1024]{2,1,0:T(8,128)(2,1)S(1)} %all-to-all-done.1.first_ref, bf16[16,64,1024]{2,1,0:T(8,128)(2,1)S(1)} %all_to_all.15.second_ref, ...), custom_call_target="tpu_custom_call" | custom-call | tf_op jit(solution)/shard_map/finish/pallas_call | solution.py:114
  (41 shorter events, 0.4 us)
Async XLA Ops:
  0.6 0.8 copy-start
  1.4 5.5 %copy-start.3 = (bf16[64,8192]{1,0:T(8,128)(2,1)S(1)}, bf16[64,8192]{1,0:T(8,128)(2,1)}, u32[]{:S(2)}) copy-start(bf16[64,8192]{1,0:T(8,128)(2,1)} %float_ref.1) | copy-start | bytes 3145732
  1.4 5.5 %copy-start.4 = (bf16[64,8192]{1,0:T(8,128)(2,1)S(1)}, bf16[64,8192]{1,0:T(8,128)(2,1)}, u32[]{:S(2)}) copy-start(bf16[64,8192]{1,0:T(8,128)(2,1)} %quant_ref.1) | copy-start | bytes 3145732
  3.1 9.3 %collective-permute-start = (bf16[256,1024]{1,0:T(8,128)(2,1)S(1)}, bf16[256,1024]{1,0:T(8,128)(2,1)S(1)}, u32[]{:S(2)}, u32[]{:S(2)}) collective-permute-start(bf16[256,1024]{1,0:T(8,128)(2,1)S(1)} %fusion.2), channel_id=1, source_target_pairs={{0,16},{16,0},{32,112},{48,96},{64,80},{80,64},{96,48},{112,32},{1... | collective-permute-start | bytes 1572872 | tf_op jit(solution)/shard_map/ppermute | solution.py:194
  7.2 2.1 %copy-start.1 = (bf16[16,64,2176]{2,1,0:T(8,128)(2,1)}, bf16[16,64,2176]{2,1,0:T(8,128)(2,1)S(1)}, u32[]{:S(2)}) copy-start(bf16[16,64,2176]{2,1,0:T(8,128)(2,1)S(1)} %pack.1) | copy-start | bytes 13369348
  12.4 74.0 %all-to-all-start = ((bf16[16,64,2176]{2,1,0:T(8,128)(2,1)}), bf16[16,64,2176]{2,1,0:T(8,128)(2,1)}, u32[]{:S(2)}, u32[]{:S(2)}) async-start(bf16[16,64,2176]{2,1,0:T(8,128)(2,1)} %copy-done.1), calls=%async_computation | async-start | bytes 8912896 | tf_op jit(solution)/shard_map/all_to_all | solution.py:203
  19.6 48.6 %collective-permute-start.1 = (bf16[512,1024]{1,0:T(8,128)(2,1)S(1)}, bf16[512,1024]{1,0:T(8,128)(2,1)S(1)}, u32[]{:S(2)}, u32[]{:S(2)}) collective-permute-start(bf16[512,1024]{1,0:T(8,128)(2,1)S(1)} %pad_maximum_fusion.refs_0_), channel_id=1, source_target_pairs={{4,0},{8,4},{12,8},{0,12},{5,1},{9,5},{13,9},{1,13},{6,2},{10,6},{... | collective-permute-start | bytes 3145736 | tf_op jit(solution)/shard_map/ppermute | solution.py:169
  23.7 45.5 %collective-permute-start.2 = (bf16[512,1024]{1,0:T(8,128)(2,1)S(1)}, bf16[512,1024]{1,0:T(8,128)(2,1)S(1)}, u32[]{:S(2)}, u32[]{:S(2)}) collective-permute-start(bf16[512,1024]{1,0:T(8,128)(2,1)S(1)} %pad_maximum_fusion.refs_0_), channel_id=1, source_target_pairs={{8,0},{12,4},{0,8},{4,12},{9,1},{13,5},{1,9},{5,13},{10,2},{14,6},... | collective-permute-start | bytes 3145736 | tf_op jit(solution)/shard_map/ppermute | solution.py:169
  23.7 47.9 %collective-permute-start.3 = (bf16[512,1024]{1,0:T(8,128)(2,1)S(1)}, bf16[512,1024]{1,0:T(8,128)(2,1)S(1)}, u32[]{:S(2)}, u32[]{:S(2)}) collective-permute-start(bf16[512,1024]{1,0:T(8,128)(2,1)S(1)} %pad_maximum_fusion.refs_0_), channel_id=1, source_target_pairs={{12,0},{0,4},{4,8},{8,12},{13,1},{1,5},{5,9},{9,13},{14,2},{2,6},{... | collective-permute-start | bytes 3145736 | tf_op jit(solution)/shard_map/ppermute | solution.py:169
  68.2 1.0 copy-start.9
  69.2 25.8 %copy-start.5 = (bf16[512,1024]{1,0:T(8,128)(2,1)}, bf16[512,1024]{1,0:T(8,128)(2,1)S(1)}, u32[]{:S(2)}) copy-start(bf16[512,1024]{1,0:T(8,128)(2,1)S(1)} %collective-permute-done.2.refs_2_) | copy-start | bytes 3145732
  71.6 23.3 %copy-start.7 = (bf16[512,1024]{1,0:T(8,128)(2,1)}, bf16[512,1024]{1,0:T(8,128)(2,1)S(1)}, u32[]{:S(2)}) copy-start(bf16[512,1024]{1,0:T(8,128)(2,1)S(1)} %collective-permute-done.3.refs_3_) | copy-start | bytes 3145732
  86.4 1.2 copy-start.10
  95.0 35.7 %all-to-all-start.1 = ((bf16[16,64,1024]{2,1,0:T(8,128)(2,1)}), bf16[16,64,1024]{2,1,0:T(8,128)(2,1)S(1)}, u32[]{:S(2)}, u32[]{:S(2)}) async-start(bf16[16,64,1024]{2,1,0:T(8,128)(2,1)} %bitcast.7), calls=%async_computation.1 | async-start | bytes 4194304 | tf_op jit(solution)/shard_map/all_to_all | solution.py:209
  99.6 9.7 %copy-start.11 = (bf16[512,1024]{1,0:T(8,128)(2,1)S(1)}, bf16[512,1024]{1,0:T(8,128)(2,1)}, u32[]{:S(2)}) copy-start(bf16[512,1024]{1,0:T(8,128)(2,1)} %copy-done.9) | copy-start | bytes 3145732
  99.6 11.8 %copy-start.6 = (bf16[512,1024]{1,0:T(8,128)(2,1)S(1)}, bf16[512,1024]{1,0:T(8,128)(2,1)}, u32[]{:S(2)}) copy-start(bf16[512,1024]{1,0:T(8,128)(2,1)} %copy-done.5) | copy-start | bytes 3145732
  99.6 15.4 %copy-start.8 = (bf16[512,1024]{1,0:T(8,128)(2,1)S(1)}, bf16[512,1024]{1,0:T(8,128)(2,1)}, u32[]{:S(2)}) copy-start(bf16[512,1024]{1,0:T(8,128)(2,1)} %copy-done.7) | copy-start | bytes 3145732
  103.3 8.0 %collective-permute-start.10 = (bf16[512,128]{1,0:T(8,128)(2,1)S(1)}, bf16[512,128]{1,0:T(8,128)(2,1)S(1)}, u32[]{:S(2)}, u32[]{:S(2)}) collective-permute-start(bf16[512,128]{1,0:T(8,128)(2,1)S(1)} %get-tuple-element.31), channel_id=1, source_target_pairs={{4,0},{8,4},{12,8},{0,12},{5,1},{9,5},{13,9},{1,13},{6,2},{10,6},{... | collective-permute-start | bytes 393224 | tf_op jit(solution)/shard_map/ppermute | solution.py:169
  107.4 7.6 %collective-permute-start.8 = (bf16[512,128]{1,0:T(8,128)(2,1)S(1)}, bf16[512,128]{1,0:T(8,128)(2,1)S(1)}, u32[]{:S(2)}, u32[]{:S(2)}) collective-permute-start(bf16[512,128]{1,0:T(8,128)(2,1)S(1)} %get-tuple-element.29), channel_id=1, source_target_pairs={{12,0},{0,4},{4,8},{8,12},{13,1},{1,5},{5,9},{9,13},{14,2},{2,6},{... | collective-permute-start | bytes 393224 | tf_op jit(solution)/shard_map/ppermute | solution.py:169
  107.4 7.6 %collective-permute-start.9 = (bf16[512,128]{1,0:T(8,128)(2,1)S(1)}, bf16[512,128]{1,0:T(8,128)(2,1)S(1)}, u32[]{:S(2)}, u32[]{:S(2)}) collective-permute-start(bf16[512,128]{1,0:T(8,128)(2,1)S(1)} %get-tuple-element.30), channel_id=1, source_target_pairs={{8,0},{12,4},{0,8},{4,12},{9,1},{13,5},{1,9},{5,13},{10,2},{14,6},... | collective-permute-start | bytes 393224 | tf_op jit(solution)/shard_map/ppermute | solution.py:169
  109.3 10.8 %collective-permute-start.4 = (bf16[512,1024]{1,0:T(8,128)(2,1)S(1)}, bf16[512,1024]{1,0:T(8,128)(2,1)S(1)}, u32[]{:S(2)}, u32[]{:S(2)}) collective-permute-start(bf16[512,1024]{1,0:T(8,128)(2,1)S(1)} %pad_maximum_fusion.refs_0_), channel_id=1, source_target_pairs={{0,32},{32,0},{1,33},{33,1},{2,34},{34,2},{3,35},{35,3},{4,36},{36... | collective-permute-start | bytes 3145736 | tf_op jit(solution)/shard_map/ppermute | solution.py:165
  109.3 12.9 %collective-permute-start.5 = (bf16[512,1024]{1,0:T(8,128)(2,1)S(1)}, bf16[512,1024]{1,0:T(8,128)(2,1)S(1)}, u32[]{:S(2)}, u32[]{:S(2)}) collective-permute-start(bf16[512,1024]{1,0:T(8,128)(2,1)S(1)} %copy-done.11), channel_id=1, source_target_pairs={{0,32},{32,0},{1,33},{33,1},{2,34},{34,2},{3,35},{35,3},{4,36},{36... | collective-permute-start | bytes 3145736 | tf_op jit(solution)/shard_map/ppermute | solution.py:165
  111.3 11.5 %collective-permute-start.6 = (bf16[512,1024]{1,0:T(8,128)(2,1)S(1)}, bf16[512,1024]{1,0:T(8,128)(2,1)S(1)}, u32[]{:S(2)}, u32[]{:S(2)}) collective-permute-start(bf16[512,1024]{1,0:T(8,128)(2,1)S(1)} %copy-done.6), channel_id=1, source_target_pairs={{0,32},{32,0},{1,33},{33,1},{2,34},{34,2},{3,35},{35,3},{4,36},{36... | collective-permute-start | bytes 3145736 | tf_op jit(solution)/shard_map/ppermute | solution.py:165
  115.0 7.9 %collective-permute-start.7 = (bf16[512,1024]{1,0:T(8,128)(2,1)S(1)}, bf16[512,1024]{1,0:T(8,128)(2,1)S(1)}, u32[]{:S(2)}, u32[]{:S(2)}) collective-permute-start(bf16[512,1024]{1,0:T(8,128)(2,1)S(1)} %copy-done.8), channel_id=1, source_target_pairs={{0,32},{32,0},{1,33},{33,1},{2,34},{34,2},{3,35},{35,3},{4,36},{36... | collective-permute-start | bytes 3145736 | tf_op jit(solution)/shard_map/ppermute | solution.py:165
  115.1 3.0 %collective-permute-start.11 = (f32[512,128]{1,0:T(8,128)S(1)}, f32[512,128]{1,0:T(8,128)S(1)}, u32[]{:S(2)}, u32[]{:S(2)}) collective-permute-start(f32[512,128]{1,0:T(8,128)S(1)} %convert_add_fusion.refs_4_), channel_id=1, source_target_pairs={{0,32},{32,0},{1,33},{33,1},{2,34},{34,2},{3,35},{35,3},{4,36},{36... | collective-permute-start | bytes 786440 | tf_op jit(solution)/shard_map/ppermute | solution.py:165
  118.1 12.6 %collective-permute-start.12 = (bf16[256,128]{1,0:T(8,128)(2,1)S(1)}, bf16[256,128]{1,0:T(8,128)(2,1)S(1)}, u32[]{:S(2)}, u32[]{:S(2)}) collective-permute-start(bf16[256,128]{1,0:T(8,128)(2,1)S(1)} %get-tuple-element.41), channel_id=1, source_target_pairs={{0,16},{16,0},{1,17},{17,1},{2,18},{18,2},{3,19},{19,3},{4,20},{20... | collective-permute-start | bytes 196616 | tf_op jit(solution)/shard_map/ppermute | solution.py:165
  120.1 10.6 %collective-permute-start.14 = (bf16[256,128]{1,0:T(8,128)(2,1)S(1)}, bf16[256,128]{1,0:T(8,128)(2,1)S(1)}, u32[]{:S(2)}, u32[]{:S(2)}) collective-permute-start(bf16[256,128]{1,0:T(8,128)(2,1)S(1)} %get-tuple-element.41), channel_id=1, source_target_pairs={{0,80},{16,64},{64,16},{80,0},{1,81},{17,65},{65,17},{81,1},{2,82}... | collective-permute-start | bytes 196616 | tf_op jit(solution)/shard_map/ppermute | solution.py:224
  122.2 8.5 %collective-permute-start.13 = (bf16[256,128]{1,0:T(8,128)(2,1)S(1)}, bf16[256,128]{1,0:T(8,128)(2,1)S(1)}, u32[]{:S(2)}, u32[]{:S(2)}) collective-permute-start(bf16[256,128]{1,0:T(8,128)(2,1)S(1)} %get-tuple-element.40), channel_id=1, source_target_pairs={{0,64},{64,0},{1,65},{65,1},{2,66},{66,2},{3,67},{67,3},{4,68},{68... | collective-permute-start | bytes 196616 | tf_op jit(solution)/shard_map/ppermute | solution.py:165
  129.3 1.4 copy-start.2

commit v25 on v24

--- a/solution.py
+++ b/solution.py
@@ -213,9 +213,11 @@
 
     blocks = stats(acts, first)
     total = blocks[0]
-    for j in (1, 2, 3):
-        total = total + ahead(blocks[j], "z", 4 - j).astype(F32)
-    second = project(acts, others, (total,))
+    came = [ahead(blocks[j], "z", 4 - j) for j in (1, 2, 3)]
+    second = project(acts, others, (blocks[0],))
+    second, *came = lax.optimization_barrier((second, *came))
+    for block in came:
+        total = total + block.astype(F32)
     total = (total + swap(total, "core")) * inverse
     here, there = total[:features].astype(BF16), total[features:].astype(BF16)
     moved = (

time: 168 us -> 166 us (0.988)
  local copies, waits for them, and re-layouts: 6.47 us -> 2.91 us
  Pallas kernels: 19.8 us -> 21.8 us
    ppermute x7, waiting for transfers between devices: 2.32 us -> 8.02 us  [swap(): return lax.ppermute(a, axis, [(0, 1), (1, 0)])]
    ppermute x6, waiting for transfers between devices: 50.9 us -> 46.8 us  [ahead(): return lax.ppermute(a, axis, [((i + j) % 4, i) for i in range(4)])]
    unnamed x24 -> x10, local copies, waits for them, and re-layouts: 6.38 us -> 2.82 us
    pallas_call x2, Pallas kernels: 13.7 us -> 15.9 us  [project(): pl.pallas_call(project_kernel, out_shape=jax.ShapeDtypeStruct((rows, cols...]
  transfers between devices with their start and end apart: 17 -> 17, of which waited for: 7 -> 7; matrix products, arithmetic and copies ran while one was open for 1% -> 1% of each run, Pallas kernels for 6% -> 12%
where the time goes in v25:
time: 166 us
  waiting for transfers between devices  71.6 us (43%)
  blocking collectives  33 us (20%)
  starting transfers between devices  30.6 us (18%)
  Pallas kernels  21.8 us (13%)
  other arithmetic  4.93 us (3%)
  local copies, waits for them, and re-layouts  2.91 us (2%)
    ppermute x6, waiting for transfers between devices, ahead(): return lax.ppermute(a, axis, [((i + j) % 4, i) for i in range(4)])  46.8 us
    all_to_all x1, blocking collectives, output(): lax.all_to_all(p.reshape(16, tokens, quarter), PLANE, 0, 0, tiled=True)  33 us
    pallas_call x2, Pallas kernels, project(): pl.pallas_call(project_kernel, out_shape=jax.ShapeDtypeStruct((rows, cols...  15.9 us
    all_to_all x1, waiting for transfers between devices, shards(): lax.all_to_all(payload, PLANE, 0, 0, tiled=True).reshape(16 * tokens, -1)  13.7 us
    ppermute x6, starting transfers between devices, ahead(): return lax.ppermute(a, axis, [((i + j) % 4, i) for i in range(4)])  11.3 us
    ppermute x7, waiting for transfers between devices, swap(): return lax.ppermute(a, axis, [(0, 1), (1, 0)])  8.02 us
    all_to_all x1, starting transfers between devices, shards(): lax.all_to_all(payload, PLANE, 0, 0, tiled=True).reshape(16 * tokens, -1)  7.17 us
    all_to_all x1, starting transfers between devices, output(): lax.all_to_all(p.reshape(16, tokens, quarter), PLANE, 0, 0, tiled=True)  4.6 us
  transfers between devices with their start and end apart: 17, of which 7 were waited for; matrix products, arithmetic and copies ran while one was open for 1% of the time, Pallas kernels for 12%

profile of v25, /device:TPU:0, one launch (start us, length us, event | category | flops | bytes accessed | tf_op | source)
XLA Modules:
  0.0 165.8 jit_solution(6001095906781821999)
XLA Ops:
  0.7 0.7 copy-done
  1.4 1.7 %fusion.2 = bf16[256,1024]{1,0:T(8,128)(2,1)S(1)} fusion(s32[256,4096]{1,0:T(8,128)} %param.8, s32[]{:T(128)S(6)} %select_n.26, f32[2,1024]{1,0:T(2,128)S(1)} %constant_dynamic-slice_fusion.1, bf16[256,4096]{1,0:T(8,128)(2,1)} %param.7, pred[]{:T(512)S(6)} %eq.7), kind=kLoop, calls=%fused_computation.5 | loop fusion | flops 1310720 | bytes 2105349 | tf_op jit(solution)/shard_map/jit(_where)/select_n | solution.py:186
  3.1 1.7 %collective-permute-start = (bf16[256,1024]{1,0:T(8,128)(2,1)S(1)}, bf16[256,1024]{1,0:T(8,128)(2,1)}, u32[]{:S(2)}, u32[]{:S(2)}) collective-permute-start(bf16[256,1024]{1,0:T(8,128)(2,1)S(1)} %fusion.2), channel_id=1, source_target_pairs={{0,16},{16,0},{32,112},{48,96},{64,80},{80,64},{96,48},{112,32},{1... | collective-permute-start | bytes 1572872 | tf_op jit(solution)/shard_map/ppermute | solution.py:194
  4.9 0.1 constant_dynamic-slice_fusion
  4.9 1.9 %fusion.3 = bf16[256,1024]{1,0:T(8,128)(2,1)S(1)} fusion(s32[256,4096]{1,0:T(8,128)} %param.8, s32[]{:T(128)S(6)} %select_n.28, f32[2,1024]{1,0:T(2,128)S(1)} %constant_dynamic-slice_fusion, bf16[256,4096]{1,0:T(8,128)(2,1)} %param.7, pred[]{:T(512)S(6)} %eq.6), kind=kLoop, calls=%fused_computation.6 | loop fusion | flops 1310720 | bytes 2105349 | tf_op jit(solution)/shard_map/jit(_where)/select_n | solution.py:186
  6.9 0.3 pack.1
  7.2 2.1 %copy-done.1 = bf16[16,64,2176]{2,1,0:T(8,128)(2,1)} copy-done((bf16[16,64,2176]{2,1,0:T(8,128)(2,1)}, bf16[16,64,2176]{2,1,0:T(8,128)(2,1)S(1)}, u32[]{:S(2)}) %copy-start.1) | copy-done | bytes 4456472
  9.3 3.2 %collective-permute-done = bf16[256,1024]{1,0:T(8,128)(2,1)} collective-permute-done((bf16[256,1024]{1,0:T(8,128)(2,1)S(1)}, bf16[256,1024]{1,0:T(8,128)(2,1)}, u32[]{:S(2)}, u32[]{:S(2)}) %collective-permute-start) | collective-permute-done | bytes 524320 | tf_op jit(solution)/shard_map/ppermute | solution.py:194
  12.5 1.1 pad_maximum_fusion.refs_0_
  13.6 7.2 %all-to-all-start = ((bf16[16,64,2176]{2,1,0:T(8,128)(2,1)}), bf16[16,64,2176]{2,1,0:T(8,128)(2,1)}, u32[]{:S(2)}, u32[]{:S(2)}) async-start(bf16[16,64,2176]{2,1,0:T(8,128)(2,1)} %copy-done.1), calls=%async_computation | async-start | bytes 8912896 | tf_op jit(solution)/shard_map/all_to_all | solution.py:203
  20.8 4.1 %collective-permute-start.1 = (bf16[512,1024]{1,0:T(8,128)(2,1)S(1)}, bf16[512,1024]{1,0:T(8,128)(2,1)}, u32[]{:S(2)}, u32[]{:S(2)}) collective-permute-start(bf16[512,1024]{1,0:T(8,128)(2,1)S(1)} %pad_maximum_fusion.refs_0_), channel_id=1, source_target_pairs={{4,0},{8,4},{12,8},{0,12},{5,1},{9,5},{13,9},{1,13},{6,2},{10,6},{... | collective-permute-start | bytes 3145736 | tf_op jit(solution)/shard_map/ppermute | solution.py:169
  24.9 1.3 collective-permute-start.3
  26.1 43.2 %collective-permute-done.1.refs_1_ = bf16[512,1024]{1,0:T(8,128)(2,1)} collective-permute-done((bf16[512,1024]{1,0:T(8,128)(2,1)S(1)}, bf16[512,1024]{1,0:T(8,128)(2,1)}, u32[]{:S(2)}, u32[]{:S(2)}) %collective-permute-start.1) | collective-permute-done | bytes 1048608 | tf_op jit(solution)/shard_map/ppermute | solution.py:169
  69.4 3.5 %collective-permute-done.3.refs_3_ = bf16[512,1024]{1,0:T(8,128)(2,1)} collective-permute-done((bf16[512,1024]{1,0:T(8,128)(2,1)S(1)}, bf16[512,1024]{1,0:T(8,128)(2,1)}, u32[]{:S(2)}, u32[]{:S(2)}) %collective-permute-start.3) | collective-permute-done | bytes 1048608 | tf_op jit(solution)/shard_map/ppermute | solution.py:169
  72.9 0.5 collective-permute-start.5
  73.4 0.5 collective-permute-start.7
  73.9 13.7 %all-to-all-done = bf16[16,64,2176]{2,1,0:T(8,128)(2,1)} async-done(((bf16[16,64,2176]{2,1,0:T(8,128)(2,1)}), bf16[16,64,2176]{2,1,0:T(8,128)(2,1)}, u32[]{:S(2)}, u32[]{:S(2)}) %all-to-all-start) | async-done | bytes 4456480 | tf_op jit(solution)/shard_map/all_to_all | solution.py:203
  87.6 8.3 %project.2.after_ref = bf16[1024,1024]{1,0:T(8,128)(2,1)} custom-call(bf16[1024,2176]{1,0:T(8,128)(2,1)} %bitcast.6.acts_ref, bf16[512,1024]{1,0:T(8,128)(2,1)S(1)} %pad_maximum_fusion.refs_0_, bf16[512,1024]{1,0:T(8,128)(2,1)} %collective-permute-done.1.refs_1_, bf16[512,1024]{1,0:T(8,128)(2,1)} %collective-permute-done.2.refs_2_, ...), custom_call_target="tpu_custom_call" | custom-call | flops 4294967296 | bytes 12582912 | tf_op jit(solution)/shard_map/project/pallas_call | solution.py:75
  95.8 4.6 %all-to-all-start.1 = ((bf16[16,64,1024]{2,1,0:T(8,128)(2,1)}), bf16[16,64,1024]{2,1,0:T(8,128)(2,1)S(1)}, u32[]{:S(2)}, u32[]{:S(2)}) async-start(bf16[16,64,1024]{2,1,0:T(8,128)(2,1)} %bitcast.7), calls=%async_computation.1 | async-start | bytes 4194304 | tf_op jit(solution)/shard_map/all_to_all | solution.py:209
  100.5 3.6 %stats.1 = (f32[512,128]{1,0:T(8,128)S(1)}, bf16[512,128]{1,0:T(8,128)(2,1)S(1)}, bf16[512,128]{1,0:T(8,128)(2,1)S(1)}, bf16[512,128]{1,0:T(8,128)(2,1)S(1)}) custom-call(bf16[1024,2176]{1,0:T(8,128)(2,1)} %bitcast.6.acts_ref, bf16[1024,1024]{1,0:T(8,128)(2,1)} %project.2.after_ref), custom_call_target="tpu_custom_call" | custom-call | tf_op jit(solution)/shard_map/stats/pallas_call | solution.py:138
  104.0 4.1 %collective-permute-start.10 = (bf16[512,128]{1,0:T(8,128)(2,1)S(1)}, bf16[512,128]{1,0:T(8,128)(2,1)S(1)}, u32[]{:S(2)}, u32[]{:S(2)}) collective-permute-start(bf16[512,128]{1,0:T(8,128)(2,1)S(1)} %get-tuple-element.35), channel_id=1, source_target_pairs={{4,0},{8,4},{12,8},{0,12},{5,1},{9,5},{13,9},{1,13},{6,2},{10,6},{... | collective-permute-start | bytes 393224 | tf_op jit(solution)/shard_map/ppermute | solution.py:169
  108.1 1.9 %collective-permute-start.9 = (bf16[512,128]{1,0:T(8,128)(2,1)S(1)}, bf16[512,128]{1,0:T(8,128)(2,1)S(1)}, u32[]{:S(2)}, u32[]{:S(2)}) collective-permute-start(bf16[512,128]{1,0:T(8,128)(2,1)S(1)} %get-tuple-element.34), channel_id=1, source_target_pairs={{8,0},{12,4},{0,8},{4,12},{9,1},{13,5},{1,9},{5,13},{10,2},{14,6},... | collective-permute-start | bytes 393224 | tf_op jit(solution)/shard_map/ppermute | solution.py:169
  110.0 7.6 %project.3 = bf16[1024,1024]{1,0:T(8,128)(2,1)S(1)} custom-call(bf16[1024,2176]{1,0:T(8,128)(2,1)} %bitcast.6.acts_ref, bf16[512,1024]{1,0:T(8,128)(2,1)} %collective-permute-done.4.refs_0_, bf16[512,1024]{1,0:T(8,128)(2,1)} %collective-permute-done.5.refs_1_, bf16[512,1024]{1,0:T(8,128)(2,1)} %collective-permute-done.6.refs_2_, ...), custom_call_target="tpu_custom_call" | custom-call | flops 4294967296 | bytes 12582912 | tf_op jit(solution)/shard_map/project/pallas_call | solution.py:75
  117.7 0.1 collective-permute-start.11
  117.8 1.5 collective-permute-done.11
  119.4 2.0 %collective-permute-start.12 = (bf16[256,128]{1,0:T(8,128)(2,1)S(1)}, bf16[256,128]{1,0:T(8,128)(2,1)S(1)}, u32[]{:S(2)}, u32[]{:S(2)}) collective-permute-start(bf16[256,128]{1,0:T(8,128)(2,1)S(1)} %get-tuple-element.49), channel_id=1, source_target_pairs={{0,16},{16,0},{1,17},{17,1},{2,18},{18,2},{3,19},{19,3},{4,20},{20... | collective-permute-start | bytes 196616 | tf_op jit(solution)/shard_map/ppermute | solution.py:165
  121.4 2.1 %collective-permute-start.14 = (bf16[256,128]{1,0:T(8,128)(2,1)S(1)}, bf16[256,128]{1,0:T(8,128)(2,1)S(1)}, u32[]{:S(2)}, u32[]{:S(2)}) collective-permute-start(bf16[256,128]{1,0:T(8,128)(2,1)S(1)} %get-tuple-element.49), channel_id=1, source_target_pairs={{0,80},{16,64},{64,16},{80,0},{1,81},{17,65},{65,17},{81,1},{2,82}... | collective-permute-start | bytes 196616 | tf_op jit(solution)/shard_map/ppermute | solution.py:226
  123.5 0.6 collective-permute-start.13
  124.2 1.4 collective-permute-done.12.refs_0_
  125.5 5.1 %collective-permute-done.13.refs_1_ = bf16[256,128]{1,0:T(8,128)(2,1)S(1)} collective-permute-done((bf16[256,128]{1,0:T(8,128)(2,1)S(1)}, bf16[256,128]{1,0:T(8,128)(2,1)S(1)}, u32[]{:S(2)}, u32[]{:S(2)}) %collective-permute-start.13) | collective-permute-done | bytes 65568 | tf_op jit(solution)/shard_map/ppermute | solution.py:165
  130.7 33.0 %all_to_all.15.second_ref = bf16[16,64,1024]{2,1,0:T(8,128)(2,1)S(1)} all-to-all(bf16[16,64,1024]{2,1,0:T(8,128)(2,1)} %bitcast.19), channel_id=1, replica_groups=mesh['yh'=2,'core'=2,'yl'=2,'z'=4,'x'=4] {'yh','yl','x'}, dimensions={0} | all-to-all | bytes 4194304 | tf_op jit(solution)/shard_map/all_to_all | solution.py:209
  163.7 2.0 %finish.1 = (bf16[64,4096]{1,0:T(8,128)(2,1)}, bf16[64,4096]{1,0:T(8,128)(2,1)}, f32[256,128]{1,0:T(8,128)}, f32[256,128]{1,0:T(8,128)}) custom-call(s32[3]{0:T(128)S(1)} %pad_add_fusion.at_ref, bf16[16,64,1024]{2,1,0:T(8,128)(2,1)S(1)} %all-to-all-done.1.first_ref, bf16[16,64,1024]{2,1,0:T(8,128)(2,1)S(1)} %all_to_all.15.second_ref, ...), custom_call_target="tpu_custom_call" | custom-call | tf_op jit(solution)/shard_map/finish/pallas_call | solution.py:114
  (27 shorter events, 0.2 us)
Async XLA Ops:
  0.6 0.8 copy-start
  1.4 5.5 %copy-start.3 = (bf16[64,8192]{1,0:T(8,128)(2,1)S(1)}, bf16[64,8192]{1,0:T(8,128)(2,1)}, u32[]{:S(2)}) copy-start(bf16[64,8192]{1,0:T(8,128)(2,1)} %float_ref.1) | copy-start | bytes 3145732
  1.4 5.5 %copy-start.4 = (bf16[64,8192]{1,0:T(8,128)(2,1)S(1)}, bf16[64,8192]{1,0:T(8,128)(2,1)}, u32[]{:S(2)}) copy-start(bf16[64,8192]{1,0:T(8,128)(2,1)} %quant_ref.1) | copy-start | bytes 3145732
  3.1 9.4 %collective-permute-start = (bf16[256,1024]{1,0:T(8,128)(2,1)S(1)}, bf16[256,1024]{1,0:T(8,128)(2,1)}, u32[]{:S(2)}, u32[]{:S(2)}) collective-permute-start(bf16[256,1024]{1,0:T(8,128)(2,1)S(1)} %fusion.2), channel_id=1, source_target_pairs={{0,16},{16,0},{32,112},{48,96},{64,80},{80,64},{96,48},{112,32},{1... | collective-permute-start | bytes 1572872 | tf_op jit(solution)/shard_map/ppermute | solution.py:194
  7.2 2.1 %copy-start.1 = (bf16[16,64,2176]{2,1,0:T(8,128)(2,1)}, bf16[16,64,2176]{2,1,0:T(8,128)(2,1)S(1)}, u32[]{:S(2)}) copy-start(bf16[16,64,2176]{2,1,0:T(8,128)(2,1)S(1)} %pack.1) | copy-start | bytes 13369348
  13.6 74.0 %all-to-all-start = ((bf16[16,64,2176]{2,1,0:T(8,128)(2,1)}), bf16[16,64,2176]{2,1,0:T(8,128)(2,1)}, u32[]{:S(2)}, u32[]{:S(2)}) async-start(bf16[16,64,2176]{2,1,0:T(8,128)(2,1)} %copy-done.1), calls=%async_computation | async-start | bytes 8912896 | tf_op jit(solution)/shard_map/all_to_all | solution.py:203
  20.8 48.6 %collective-permute-start.1 = (bf16[512,1024]{1,0:T(8,128)(2,1)S(1)}, bf16[512,1024]{1,0:T(8,128)(2,1)}, u32[]{:S(2)}, u32[]{:S(2)}) collective-permute-start(bf16[512,1024]{1,0:T(8,128)(2,1)S(1)} %pad_maximum_fusion.refs_0_), channel_id=1, source_target_pairs={{4,0},{8,4},{12,8},{0,12},{5,1},{9,5},{13,9},{1,13},{6,2},{10,6},{... | collective-permute-start | bytes 3145736 | tf_op jit(solution)/shard_map/ppermute | solution.py:169
  24.9 44.5 %collective-permute-start.2 = (bf16[512,1024]{1,0:T(8,128)(2,1)S(1)}, bf16[512,1024]{1,0:T(8,128)(2,1)}, u32[]{:S(2)}, u32[]{:S(2)}) collective-permute-start(bf16[512,1024]{1,0:T(8,128)(2,1)S(1)} %pad_maximum_fusion.refs_0_), channel_id=1, source_target_pairs={{8,0},{12,4},{0,8},{4,12},{9,1},{13,5},{1,9},{5,13},{10,2},{14,6},... | collective-permute-start | bytes 3145736 | tf_op jit(solution)/shard_map/ppermute | solution.py:169
  24.9 48.0 %collective-permute-start.3 = (bf16[512,1024]{1,0:T(8,128)(2,1)S(1)}, bf16[512,1024]{1,0:T(8,128)(2,1)}, u32[]{:S(2)}, u32[]{:S(2)}) collective-permute-start(bf16[512,1024]{1,0:T(8,128)(2,1)S(1)} %pad_maximum_fusion.refs_0_), channel_id=1, source_target_pairs={{12,0},{0,4},{4,8},{8,12},{13,1},{1,5},{5,9},{9,13},{14,2},{2,6},{... | collective-permute-start | bytes 3145736 | tf_op jit(solution)/shard_map/ppermute | solution.py:169
  72.9 35.2 %collective-permute-start.4 = (bf16[512,1024]{1,0:T(8,128)(2,1)S(1)}, bf16[512,1024]{1,0:T(8,128)(2,1)}, u32[]{:S(2)}, u32[]{:S(2)}) collective-permute-start(bf16[512,1024]{1,0:T(8,128)(2,1)S(1)} %pad_maximum_fusion.refs_0_), channel_id=1, source_target_pairs={{0,32},{32,0},{1,33},{33,1},{2,34},{34,2},{3,35},{35,3},{4,36},{36... | collective-permute-start | bytes 3145736 | tf_op jit(solution)/shard_map/ppermute | solution.py:165
  72.9 35.2 %collective-permute-start.5 = (bf16[512,1024]{1,0:T(8,128)(2,1)}, bf16[512,1024]{1,0:T(8,128)(2,1)}, u32[]{:S(2)}, u32[]{:S(2)}) collective-permute-start(bf16[512,1024]{1,0:T(8,128)(2,1)} %collective-permute-done.1.refs_1_), channel_id=1, source_target_pairs={{0,32},{32,0},{1,33},{33,1},{2,34},{34,2},{3,35},{35,3},{4,36},{36... | collective-permute-start | bytes 3145736 | tf_op jit(solution)/shard_map/ppermute | solution.py:165
  73.4 36.6 %collective-permute-start.6 = (bf16[512,1024]{1,0:T(8,128)(2,1)}, bf16[512,1024]{1,0:T(8,128)(2,1)}, u32[]{:S(2)}, u32[]{:S(2)}) collective-permute-start(bf16[512,1024]{1,0:T(8,128)(2,1)} %collective-permute-done.2.refs_2_), channel_id=1, source_target_pairs={{0,32},{32,0},{1,33},{33,1},{2,34},{34,2},{3,35},{35,3},{4,36},{36... | collective-permute-start | bytes 3145736 | tf_op jit(solution)/shard_map/ppermute | solution.py:165
  73.4 36.6 %collective-permute-start.7 = (bf16[512,1024]{1,0:T(8,128)(2,1)}, bf16[512,1024]{1,0:T(8,128)(2,1)}, u32[]{:S(2)}, u32[]{:S(2)}) collective-permute-start(bf16[512,1024]{1,0:T(8,128)(2,1)} %collective-permute-done.3.refs_3_), channel_id=1, source_target_pairs={{0,32},{32,0},{1,33},{33,1},{2,34},{34,2},{3,35},{35,3},{4,36},{36... | collective-permute-start | bytes 3145736 | tf_op jit(solution)/shard_map/ppermute | solution.py:165
  95.8 34.8 %all-to-all-start.1 = ((bf16[16,64,1024]{2,1,0:T(8,128)(2,1)}), bf16[16,64,1024]{2,1,0:T(8,128)(2,1)S(1)}, u32[]{:S(2)}, u32[]{:S(2)}) async-start(bf16[16,64,1024]{2,1,0:T(8,128)(2,1)} %bitcast.7), calls=%async_computation.1 | async-start | bytes 4194304 | tf_op jit(solution)/shard_map/all_to_all | solution.py:209
  104.0 13.6 %collective-permute-start.10 = (bf16[512,128]{1,0:T(8,128)(2,1)S(1)}, bf16[512,128]{1,0:T(8,128)(2,1)S(1)}, u32[]{:S(2)}, u32[]{:S(2)}) collective-permute-start(bf16[512,128]{1,0:T(8,128)(2,1)S(1)} %get-tuple-element.35), channel_id=1, source_target_pairs={{4,0},{8,4},{12,8},{0,12},{5,1},{9,5},{13,9},{1,13},{6,2},{10,6},{... | collective-permute-start | bytes 393224 | tf_op jit(solution)/shard_map/ppermute | solution.py:169
  108.1 9.5 %collective-permute-start.8 = (bf16[512,128]{1,0:T(8,128)(2,1)S(1)}, bf16[512,128]{1,0:T(8,128)(2,1)S(1)}, u32[]{:S(2)}, u32[]{:S(2)}) collective-permute-start(bf16[512,128]{1,0:T(8,128)(2,1)S(1)} %get-tuple-element.33), channel_id=1, source_target_pairs={{12,0},{0,4},{4,8},{8,12},{13,1},{1,5},{5,9},{9,13},{14,2},{2,6},{... | collective-permute-start | bytes 393224 | tf_op jit(solution)/shard_map/ppermute | solution.py:169
  108.1 9.5 %collective-permute-start.9 = (bf16[512,128]{1,0:T(8,128)(2,1)S(1)}, bf16[512,128]{1,0:T(8,128)(2,1)S(1)}, u32[]{:S(2)}, u32[]{:S(2)}) collective-permute-start(bf16[512,128]{1,0:T(8,128)(2,1)S(1)} %get-tuple-element.34), channel_id=1, source_target_pairs={{8,0},{12,4},{0,8},{4,12},{9,1},{13,5},{1,9},{5,13},{10,2},{14,6},... | collective-permute-start | bytes 393224 | tf_op jit(solution)/shard_map/ppermute | solution.py:169
  117.6 13.0 %copy-start.2 = (bf16[1024,1024]{1,0:T(8,128)(2,1)}, bf16[1024,1024]{1,0:T(8,128)(2,1)S(1)}, u32[]{:S(2)}) copy-start(bf16[1024,1024]{1,0:T(8,128)(2,1)S(1)} %project.3) | copy-start | bytes 6291460
  117.7 1.6 collective-permute-start.11
  119.4 6.2 %collective-permute-start.12 = (bf16[256,128]{1,0:T(8,128)(2,1)S(1)}, bf16[256,128]{1,0:T(8,128)(2,1)S(1)}, u32[]{:S(2)}, u32[]{:S(2)}) collective-permute-start(bf16[256,128]{1,0:T(8,128)(2,1)S(1)} %get-tuple-element.49), channel_id=1, source_target_pairs={{0,16},{16,0},{1,17},{17,1},{2,18},{18,2},{3,19},{19,3},{4,20},{20... | collective-permute-start | bytes 196616 | tf_op jit(solution)/shard_map/ppermute | solution.py:165
  121.4 9.2 %collective-permute-start.14 = (bf16[256,128]{1,0:T(8,128)(2,1)S(1)}, bf16[256,128]{1,0:T(8,128)(2,1)S(1)}, u32[]{:S(2)}, u32[]{:S(2)}) collective-permute-start(bf16[256,128]{1,0:T(8,128)(2,1)S(1)} %get-tuple-element.49), channel_id=1, source_target_pairs={{0,80},{16,64},{64,16},{80,0},{1,81},{17,65},{65,17},{81,1},{2,82}... | collective-permute-start | bytes 196616 | tf_op jit(solution)/shard_map/ppermute | solution.py:226
  123.5 7.2 %collective-permute-start.13 = (bf16[256,128]{1,0:T(8,128)(2,1)S(1)}, bf16[256,128]{1,0:T(8,128)(2,1)S(1)}, u32[]{:S(2)}, u32[]{:S(2)}) collective-permute-start(bf16[256,128]{1,0:T(8,128)(2,1)S(1)} %get-tuple-element.48), channel_id=1, source_target_pairs={{0,64},{64,0},{1,65},{65,1},{2,66},{66,2},{3,67},{67,3},{4,68},{68... | collective-permute-start | bytes 196616 | tf_op jit(solution)/shard_map/ppermute | solution.py:165

commit v26 on v25

--- a/solution.py
+++ b/solution.py
@@ -19,7 +19,7 @@
 
 
 def params():
-    return pltpu.CompilerParams(vmem_limit_bytes=12 << 20)
+    return pltpu.CompilerParams(vmem_limit_bytes=16 << 20)
 
 
 def pack_kernel(z_ref, float_ref, quant_ref, out_ref):
@@ -71,7 +71,7 @@
 
 def project(acts, weights, after):
     rows, cols = acts.shape[0], weights[0].shape[1]
-    step = 256
+    step = 512
     return pl.pallas_call(
         project_kernel,
         out_shape=jax.ShapeDtypeStruct((rows, cols), BF16),

time: 166 us -> 166 us (level)
  no operation moved by 1% of the time
where the time goes in v26:
time: 166 us
  waiting for transfers between devices  71.6 us (43%)
  blocking collectives  33 us (20%)
  starting transfers between devices  30.6 us (18%)
  Pallas kernels  21.7 us (13%)
  other arithmetic  4.93 us (3%)
  local copies, waits for them, and re-layouts  2.91 us (2%)
    ppermute x6, waiting for transfers between devices, ahead(): return lax.ppermute(a, axis, [((i + j) % 4, i) for i in range(4)])  46.8 us
    all_to_all x1, blocking collectives, output(): lax.all_to_all(p.reshape(16, tokens, quarter), PLANE, 0, 0, tiled=True)  33 us
    pallas_call x2, Pallas kernels, project(): pl.pallas_call(project_kernel, out_shape=jax.ShapeDtypeStruct((rows, cols...  15.8 us
    all_to_all x1, waiting for transfers between devices, shards(): lax.all_to_all(payload, PLANE, 0, 0, tiled=True).reshape(16 * tokens, -1)  13.7 us
    ppermute x6, starting transfers between devices, ahead(): return lax.ppermute(a, axis, [((i + j) % 4, i) for i in range(4)])  11.3 us
    ppermute x7, waiting for transfers between devices, swap(): return lax.ppermute(a, axis, [(0, 1), (1, 0)])  8.02 us
    all_to_all x1, starting transfers between devices, shards(): lax.all_to_all(payload, PLANE, 0, 0, tiled=True).reshape(16 * tokens, -1)  7.17 us
    all_to_all x1, starting transfers between devices, output(): lax.all_to_all(p.reshape(16, tokens, quarter), PLANE, 0, 0, tiled=True)  4.61 us
  transfers between devices with their start and end apart: 17, of which 7 were waited for; matrix products, arithmetic and copies ran while one was open for 1% of the time, Pallas kernels for 12%

profile of v26, /device:TPU:0, one launch (start us, length us, event | category | flops | bytes accessed | tf_op | source)
XLA Modules:
  0.0 165.6 jit_solution(15242051852652663739)
XLA Ops:
  0.7 0.7 copy-done
  1.4 1.7 %fusion.2 = bf16[256,1024]{1,0:T(8,128)(2,1)S(1)} fusion(s32[256,4096]{1,0:T(8,128)} %param.8, s32[]{:T(128)S(6)} %select_n.26, f32[2,1024]{1,0:T(2,128)S(1)} %constant_dynamic-slice_fusion.1, bf16[256,4096]{1,0:T(8,128)(2,1)} %param.7, pred[]{:T(512)S(6)} %eq.7), kind=kLoop, calls=%fused_computation.5 | loop fusion | flops 1310720 | bytes 2105349 | tf_op jit(solution)/shard_map/jit(_where)/select_n | solution.py:186
  3.1 1.7 %collective-permute-start = (bf16[256,1024]{1,0:T(8,128)(2,1)S(1)}, bf16[256,1024]{1,0:T(8,128)(2,1)}, u32[]{:S(2)}, u32[]{:S(2)}) collective-permute-start(bf16[256,1024]{1,0:T(8,128)(2,1)S(1)} %fusion.2), channel_id=1, source_target_pairs={{0,16},{16,0},{32,112},{48,96},{64,80},{80,64},{96,48},{112,32},{1... | collective-permute-start | bytes 1572872 | tf_op jit(solution)/shard_map/ppermute | solution.py:194
  4.9 0.1 constant_dynamic-slice_fusion
  4.9 1.9 %fusion.3 = bf16[256,1024]{1,0:T(8,128)(2,1)S(1)} fusion(s32[256,4096]{1,0:T(8,128)} %param.8, s32[]{:T(128)S(6)} %select_n.28, f32[2,1024]{1,0:T(2,128)S(1)} %constant_dynamic-slice_fusion, bf16[256,4096]{1,0:T(8,128)(2,1)} %param.7, pred[]{:T(512)S(6)} %eq.6), kind=kLoop, calls=%fused_computation.6 | loop fusion | flops 1310720 | bytes 2105349 | tf_op jit(solution)/shard_map/jit(_where)/select_n | solution.py:186
  6.9 0.3 pack.1
  7.2 2.1 %copy-done.1 = bf16[16,64,2176]{2,1,0:T(8,128)(2,1)} copy-done((bf16[16,64,2176]{2,1,0:T(8,128)(2,1)}, bf16[16,64,2176]{2,1,0:T(8,128)(2,1)S(1)}, u32[]{:S(2)}) %copy-start.1) | copy-done | bytes 4456472
  9.3 3.2 %collective-permute-done = bf16[256,1024]{1,0:T(8,128)(2,1)} collective-permute-done((bf16[256,1024]{1,0:T(8,128)(2,1)S(1)}, bf16[256,1024]{1,0:T(8,128)(2,1)}, u32[]{:S(2)}, u32[]{:S(2)}) %collective-permute-start) | collective-permute-done | bytes 524320 | tf_op jit(solution)/shard_map/ppermute | solution.py:194
  12.5 1.1 pad_maximum_fusion.refs_0_
  13.6 7.2 %all-to-all-start = ((bf16[16,64,2176]{2,1,0:T(8,128)(2,1)}), bf16[16,64,2176]{2,1,0:T(8,128)(2,1)}, u32[]{:S(2)}, u32[]{:S(2)}) async-start(bf16[16,64,2176]{2,1,0:T(8,128)(2,1)} %copy-done.1), calls=%async_computation | async-start | bytes 8912896 | tf_op jit(solution)/shard_map/all_to_all | solution.py:203
  20.8 4.1 %collective-permute-start.1 = (bf16[512,1024]{1,0:T(8,128)(2,1)S(1)}, bf16[512,1024]{1,0:T(8,128)(2,1)}, u32[]{:S(2)}, u32[]{:S(2)}) collective-permute-start(bf16[512,1024]{1,0:T(8,128)(2,1)S(1)} %pad_maximum_fusion.refs_0_), channel_id=1, source_target_pairs={{4,0},{8,4},{12,8},{0,12},{5,1},{9,5},{13,9},{1,13},{6,2},{10,6},{... | collective-permute-start | bytes 3145736 | tf_op jit(solution)/shard_map/ppermute | solution.py:169
  24.9 1.3 collective-permute-start.3
  26.1 43.2 %collective-permute-done.1.refs_1_ = bf16[512,1024]{1,0:T(8,128)(2,1)} collective-permute-done((bf16[512,1024]{1,0:T(8,128)(2,1)S(1)}, bf16[512,1024]{1,0:T(8,128)(2,1)}, u32[]{:S(2)}, u32[]{:S(2)}) %collective-permute-start.1) | collective-permute-done | bytes 1048608 | tf_op jit(solution)/shard_map/ppermute | solution.py:169
  69.4 3.5 %collective-permute-done.3.refs_3_ = bf16[512,1024]{1,0:T(8,128)(2,1)} collective-permute-done((bf16[512,1024]{1,0:T(8,128)(2,1)S(1)}, bf16[512,1024]{1,0:T(8,128)(2,1)}, u32[]{:S(2)}, u32[]{:S(2)}) %collective-permute-start.3) | collective-permute-done | bytes 1048608 | tf_op jit(solution)/shard_map/ppermute | solution.py:169
  72.9 0.5 collective-permute-start.5
  73.4 0.5 collective-permute-start.7
  73.9 13.7 %all-to-all-done = bf16[16,64,2176]{2,1,0:T(8,128)(2,1)} async-done(((bf16[16,64,2176]{2,1,0:T(8,128)(2,1)}), bf16[16,64,2176]{2,1,0:T(8,128)(2,1)}, u32[]{:S(2)}, u32[]{:S(2)}) %all-to-all-start) | async-done | bytes 4456480 | tf_op jit(solution)/shard_map/all_to_all | solution.py:203
  87.6 8.2 %project.2.after_ref = bf16[1024,1024]{1,0:T(8,128)(2,1)} custom-call(bf16[1024,2176]{1,0:T(8,128)(2,1)} %bitcast.6.acts_ref, bf16[512,1024]{1,0:T(8,128)(2,1)S(1)} %pad_maximum_fusion.refs_0_, bf16[512,1024]{1,0:T(8,128)(2,1)} %collective-permute-done.1.refs_1_, bf16[512,1024]{1,0:T(8,128)(2,1)} %collective-permute-done.2.refs_2_, ...), custom_call_target="tpu_custom_call" | custom-call | flops 4294967296 | bytes 12582912 | tf_op jit(solution)/shard_map/project/pallas_call | solution.py:75
  95.8 4.6 %all-to-all-start.1 = ((bf16[16,64,1024]{2,1,0:T(8,128)(2,1)}), bf16[16,64,1024]{2,1,0:T(8,128)(2,1)S(1)}, u32[]{:S(2)}, u32[]{:S(2)}) async-start(bf16[16,64,1024]{2,1,0:T(8,128)(2,1)} %bitcast.7), calls=%async_computation.1 | async-start | bytes 4194304 | tf_op jit(solution)/shard_map/all_to_all | solution.py:209
  100.4 3.6 %stats.1 = (f32[512,128]{1,0:T(8,128)S(1)}, bf16[512,128]{1,0:T(8,128)(2,1)S(1)}, bf16[512,128]{1,0:T(8,128)(2,1)S(1)}, bf16[512,128]{1,0:T(8,128)(2,1)S(1)}) custom-call(bf16[1024,2176]{1,0:T(8,128)(2,1)} %bitcast.6.acts_ref, bf16[1024,1024]{1,0:T(8,128)(2,1)} %project.2.after_ref), custom_call_target="tpu_custom_call" | custom-call | tf_op jit(solution)/shard_map/stats/pallas_call | solution.py:138
  104.0 4.1 %collective-permute-start.10 = (bf16[512,128]{1,0:T(8,128)(2,1)S(1)}, bf16[512,128]{1,0:T(8,128)(2,1)S(1)}, u32[]{:S(2)}, u32[]{:S(2)}) collective-permute-start(bf16[512,128]{1,0:T(8,128)(2,1)S(1)} %get-tuple-element.35), channel_id=1, source_target_pairs={{4,0},{8,4},{12,8},{0,12},{5,1},{9,5},{13,9},{1,13},{6,2},{10,6},{... | collective-permute-start | bytes 393224 | tf_op jit(solution)/shard_map/ppermute | solution.py:169
  108.1 1.9 %collective-permute-start.9 = (bf16[512,128]{1,0:T(8,128)(2,1)S(1)}, bf16[512,128]{1,0:T(8,128)(2,1)S(1)}, u32[]{:S(2)}, u32[]{:S(2)}) collective-permute-start(bf16[512,128]{1,0:T(8,128)(2,1)S(1)} %get-tuple-element.34), channel_id=1, source_target_pairs={{8,0},{12,4},{0,8},{4,12},{9,1},{13,5},{1,9},{5,13},{10,2},{14,6},... | collective-permute-start | bytes 393224 | tf_op jit(solution)/shard_map/ppermute | solution.py:169
  110.0 7.5 %project.3 = bf16[1024,1024]{1,0:T(8,128)(2,1)S(1)} custom-call(bf16[1024,2176]{1,0:T(8,128)(2,1)} %bitcast.6.acts_ref, bf16[512,1024]{1,0:T(8,128)(2,1)} %collective-permute-done.4.refs_0_, bf16[512,1024]{1,0:T(8,128)(2,1)} %collective-permute-done.5.refs_1_, bf16[512,1024]{1,0:T(8,128)(2,1)} %collective-permute-done.6.refs_2_, ...), custom_call_target="tpu_custom_call" | custom-call | flops 4294967296 | bytes 12582912 | tf_op jit(solution)/shard_map/project/pallas_call | solution.py:75
  117.6 0.1 collective-permute-start.11
  117.7 1.5 collective-permute-done.11
  119.3 2.0 %collective-permute-start.12 = (bf16[256,128]{1,0:T(8,128)(2,1)S(1)}, bf16[256,128]{1,0:T(8,128)(2,1)S(1)}, u32[]{:S(2)}, u32[]{:S(2)}) collective-permute-start(bf16[256,128]{1,0:T(8,128)(2,1)S(1)} %get-tuple-element.49), channel_id=1, source_target_pairs={{0,16},{16,0},{1,17},{17,1},{2,18},{18,2},{3,19},{19,3},{4,20},{20... | collective-permute-start | bytes 196616 | tf_op jit(solution)/shard_map/ppermute | solution.py:165
  121.3 2.1 %collective-permute-start.14 = (bf16[256,128]{1,0:T(8,128)(2,1)S(1)}, bf16[256,128]{1,0:T(8,128)(2,1)S(1)}, u32[]{:S(2)}, u32[]{:S(2)}) collective-permute-start(bf16[256,128]{1,0:T(8,128)(2,1)S(1)} %get-tuple-element.49), channel_id=1, source_target_pairs={{0,80},{16,64},{64,16},{80,0},{1,81},{17,65},{65,17},{81,1},{2,82}... | collective-permute-start | bytes 196616 | tf_op jit(solution)/shard_map/ppermute | solution.py:226
  123.4 0.6 collective-permute-start.13
  124.0 1.4 collective-permute-done.12.refs_0_
  125.5 5.0 %collective-permute-done.13.refs_1_ = bf16[256,128]{1,0:T(8,128)(2,1)S(1)} collective-permute-done((bf16[256,128]{1,0:T(8,128)(2,1)S(1)}, bf16[256,128]{1,0:T(8,128)(2,1)S(1)}, u32[]{:S(2)}, u32[]{:S(2)}) %collective-permute-start.13) | collective-permute-done | bytes 65568 | tf_op jit(solution)/shard_map/ppermute | solution.py:165
  130.5 33.0 %all_to_all.15.second_ref = bf16[16,64,1024]{2,1,0:T(8,128)(2,1)S(1)} all-to-all(bf16[16,64,1024]{2,1,0:T(8,128)(2,1)} %bitcast.19), channel_id=1, replica_groups=mesh['yh'=2,'core'=2,'yl'=2,'z'=4,'x'=4] {'yh','yl','x'}, dimensions={0} | all-to-all | bytes 4194304 | tf_op jit(solution)/shard_map/all_to_all | solution.py:209
  163.6 2.0 %finish.1 = (bf16[64,4096]{1,0:T(8,128)(2,1)}, bf16[64,4096]{1,0:T(8,128)(2,1)}, f32[256,128]{1,0:T(8,128)}, f32[256,128]{1,0:T(8,128)}) custom-call(s32[3]{0:T(128)S(1)} %pad_add_fusion.at_ref, bf16[16,64,1024]{2,1,0:T(8,128)(2,1)S(1)} %all-to-all-done.1.first_ref, bf16[16,64,1024]{2,1,0:T(8,128)(2,1)S(1)} %all_to_all.15.second_ref, ...), custom_call_target="tpu_custom_call" | custom-call | tf_op jit(solution)/shard_map/finish/pallas_call | solution.py:114
  (27 shorter events, 0.2 us)
Async XLA Ops:
  0.6 0.8 copy-start
  1.4 5.5 %copy-start.3 = (bf16[64,8192]{1,0:T(8,128)(2,1)S(1)}, bf16[64,8192]{1,0:T(8,128)(2,1)}, u32[]{:S(2)}) copy-start(bf16[64,8192]{1,0:T(8,128)(2,1)} %float_ref.1) | copy-start | bytes 3145732
  1.4 5.5 %copy-start.4 = (bf16[64,8192]{1,0:T(8,128)(2,1)S(1)}, bf16[64,8192]{1,0:T(8,128)(2,1)}, u32[]{:S(2)}) copy-start(bf16[64,8192]{1,0:T(8,128)(2,1)} %quant_ref.1) | copy-start | bytes 3145732
  3.1 9.4 %collective-permute-start = (bf16[256,1024]{1,0:T(8,128)(2,1)S(1)}, bf16[256,1024]{1,0:T(8,128)(2,1)}, u32[]{:S(2)}, u32[]{:S(2)}) collective-permute-start(bf16[256,1024]{1,0:T(8,128)(2,1)S(1)} %fusion.2), channel_id=1, source_target_pairs={{0,16},{16,0},{32,112},{48,96},{64,80},{80,64},{96,48},{112,32},{1... | collective-permute-start | bytes 1572872 | tf_op jit(solution)/shard_map/ppermute | solution.py:194
  7.2 2.1 %copy-start.1 = (bf16[16,64,2176]{2,1,0:T(8,128)(2,1)}, bf16[16,64,2176]{2,1,0:T(8,128)(2,1)S(1)}, u32[]{:S(2)}) copy-start(bf16[16,64,2176]{2,1,0:T(8,128)(2,1)S(1)} %pack.1) | copy-start | bytes 13369348
  13.6 74.0 %all-to-all-start = ((bf16[16,64,2176]{2,1,0:T(8,128)(2,1)}), bf16[16,64,2176]{2,1,0:T(8,128)(2,1)}, u32[]{:S(2)}, u32[]{:S(2)}) async-start(bf16[16,64,2176]{2,1,0:T(8,128)(2,1)} %copy-done.1), calls=%async_computation | async-start | bytes 8912896 | tf_op jit(solution)/shard_map/all_to_all | solution.py:203
  20.8 48.6 %collective-permute-start.1 = (bf16[512,1024]{1,0:T(8,128)(2,1)S(1)}, bf16[512,1024]{1,0:T(8,128)(2,1)}, u32[]{:S(2)}, u32[]{:S(2)}) collective-permute-start(bf16[512,1024]{1,0:T(8,128)(2,1)S(1)} %pad_maximum_fusion.refs_0_), channel_id=1, source_target_pairs={{4,0},{8,4},{12,8},{0,12},{5,1},{9,5},{13,9},{1,13},{6,2},{10,6},{... | collective-permute-start | bytes 3145736 | tf_op jit(solution)/shard_map/ppermute | solution.py:169
  24.9 44.5 %collective-permute-start.2 = (bf16[512,1024]{1,0:T(8,128)(2,1)S(1)}, bf16[512,1024]{1,0:T(8,128)(2,1)}, u32[]{:S(2)}, u32[]{:S(2)}) collective-permute-start(bf16[512,1024]{1,0:T(8,128)(2,1)S(1)} %pad_maximum_fusion.refs_0_), channel_id=1, source_target_pairs={{8,0},{12,4},{0,8},{4,12},{9,1},{13,5},{1,9},{5,13},{10,2},{14,6},... | collective-permute-start | bytes 3145736 | tf_op jit(solution)/shard_map/ppermute | solution.py:169
  24.9 48.0 %collective-permute-start.3 = (bf16[512,1024]{1,0:T(8,128)(2,1)S(1)}, bf16[512,1024]{1,0:T(8,128)(2,1)}, u32[]{:S(2)}, u32[]{:S(2)}) collective-permute-start(bf16[512,1024]{1,0:T(8,128)(2,1)S(1)} %pad_maximum_fusion.refs_0_), channel_id=1, source_target_pairs={{12,0},{0,4},{4,8},{8,12},{13,1},{1,5},{5,9},{9,13},{14,2},{2,6},{... | collective-permute-start | bytes 3145736 | tf_op jit(solution)/shard_map/ppermute | solution.py:169
  72.9 35.2 %collective-permute-start.4 = (bf16[512,1024]{1,0:T(8,128)(2,1)S(1)}, bf16[512,1024]{1,0:T(8,128)(2,1)}, u32[]{:S(2)}, u32[]{:S(2)}) collective-permute-start(bf16[512,1024]{1,0:T(8,128)(2,1)S(1)} %pad_maximum_fusion.refs_0_), channel_id=1, source_target_pairs={{0,32},{32,0},{1,33},{33,1},{2,34},{34,2},{3,35},{35,3},{4,36},{36... | collective-permute-start | bytes 3145736 | tf_op jit(solution)/shard_map/ppermute | solution.py:165
  72.9 35.2 %collective-permute-start.5 = (bf16[512,1024]{1,0:T(8,128)(2,1)}, bf16[512,1024]{1,0:T(8,128)(2,1)}, u32[]{:S(2)}, u32[]{:S(2)}) collective-permute-start(bf16[512,1024]{1,0:T(8,128)(2,1)} %collective-permute-done.1.refs_1_), channel_id=1, source_target_pairs={{0,32},{32,0},{1,33},{33,1},{2,34},{34,2},{3,35},{35,3},{4,36},{36... | collective-permute-start | bytes 3145736 | tf_op jit(solution)/shard_map/ppermute | solution.py:165
  73.4 36.5 %collective-permute-start.6 = (bf16[512,1024]{1,0:T(8,128)(2,1)}, bf16[512,1024]{1,0:T(8,128)(2,1)}, u32[]{:S(2)}, u32[]{:S(2)}) collective-permute-start(bf16[512,1024]{1,0:T(8,128)(2,1)} %collective-permute-done.2.refs_2_), channel_id=1, source_target_pairs={{0,32},{32,0},{1,33},{33,1},{2,34},{34,2},{3,35},{35,3},{4,36},{36... | collective-permute-start | bytes 3145736 | tf_op jit(solution)/shard_map/ppermute | solution.py:165
  73.4 36.5 %collective-permute-start.7 = (bf16[512,1024]{1,0:T(8,128)(2,1)}, bf16[512,1024]{1,0:T(8,128)(2,1)}, u32[]{:S(2)}, u32[]{:S(2)}) collective-permute-start(bf16[512,1024]{1,0:T(8,128)(2,1)} %collective-permute-done.3.refs_3_), channel_id=1, source_target_pairs={{0,32},{32,0},{1,33},{33,1},{2,34},{34,2},{3,35},{35,3},{4,36},{36... | collective-permute-start | bytes 3145736 | tf_op jit(solution)/shard_map/ppermute | solution.py:165
  95.8 34.8 %all-to-all-start.1 = ((bf16[16,64,1024]{2,1,0:T(8,128)(2,1)}), bf16[16,64,1024]{2,1,0:T(8,128)(2,1)S(1)}, u32[]{:S(2)}, u32[]{:S(2)}) async-start(bf16[16,64,1024]{2,1,0:T(8,128)(2,1)} %bitcast.7), calls=%async_computation.1 | async-start | bytes 4194304 | tf_op jit(solution)/shard_map/all_to_all | solution.py:209
  104.0 13.6 %collective-permute-start.10 = (bf16[512,128]{1,0:T(8,128)(2,1)S(1)}, bf16[512,128]{1,0:T(8,128)(2,1)S(1)}, u32[]{:S(2)}, u32[]{:S(2)}) collective-permute-start(bf16[512,128]{1,0:T(8,128)(2,1)S(1)} %get-tuple-element.35), channel_id=1, source_target_pairs={{4,0},{8,4},{12,8},{0,12},{5,1},{9,5},{13,9},{1,13},{6,2},{10,6},{... | collective-permute-start | bytes 393224 | tf_op jit(solution)/shard_map/ppermute | solution.py:169
  108.1 9.5 %collective-permute-start.8 = (bf16[512,128]{1,0:T(8,128)(2,1)S(1)}, bf16[512,128]{1,0:T(8,128)(2,1)S(1)}, u32[]{:S(2)}, u32[]{:S(2)}) collective-permute-start(bf16[512,128]{1,0:T(8,128)(2,1)S(1)} %get-tuple-element.33), channel_id=1, source_target_pairs={{12,0},{0,4},{4,8},{8,12},{13,1},{1,5},{5,9},{9,13},{14,2},{2,6},{... | collective-permute-start | bytes 393224 | tf_op jit(solution)/shard_map/ppermute | solution.py:169
  108.1 9.5 %collective-permute-start.9 = (bf16[512,128]{1,0:T(8,128)(2,1)S(1)}, bf16[512,128]{1,0:T(8,128)(2,1)S(1)}, u32[]{:S(2)}, u32[]{:S(2)}) collective-permute-start(bf16[512,128]{1,0:T(8,128)(2,1)S(1)} %get-tuple-element.34), channel_id=1, source_target_pairs={{8,0},{12,4},{0,8},{4,12},{9,1},{13,5},{1,9},{5,13},{10,2},{14,6},... | collective-permute-start | bytes 393224 | tf_op jit(solution)/shard_map/ppermute | solution.py:169
  117.5 13.0 %copy-start.2 = (bf16[1024,1024]{1,0:T(8,128)(2,1)}, bf16[1024,1024]{1,0:T(8,128)(2,1)S(1)}, u32[]{:S(2)}) copy-start(bf16[1024,1024]{1,0:T(8,128)(2,1)S(1)} %project.3) | copy-start | bytes 6291460
  117.6 1.6 collective-permute-start.11
  119.3 6.2 %collective-permute-start.12 = (bf16[256,128]{1,0:T(8,128)(2,1)S(1)}, bf16[256,128]{1,0:T(8,128)(2,1)S(1)}, u32[]{:S(2)}, u32[]{:S(2)}) collective-permute-start(bf16[256,128]{1,0:T(8,128)(2,1)S(1)} %get-tuple-element.49), channel_id=1, source_target_pairs={{0,16},{16,0},{1,17},{17,1},{2,18},{18,2},{3,19},{19,3},{4,20},{20... | collective-permute-start | bytes 196616 | tf_op jit(solution)/shard_map/ppermute | solution.py:165
  121.3 9.2 %collective-permute-start.14 = (bf16[256,128]{1,0:T(8,128)(2,1)S(1)}, bf16[256,128]{1,0:T(8,128)(2,1)S(1)}, u32[]{:S(2)}, u32[]{:S(2)}) collective-permute-start(bf16[256,128]{1,0:T(8,128)(2,1)S(1)} %get-tuple-element.49), channel_id=1, source_target_pairs={{0,80},{16,64},{64,16},{80,0},{1,81},{17,65},{65,17},{81,1},{2,82}... | collective-permute-start | bytes 196616 | tf_op jit(solution)/shard_map/ppermute | solution.py:226
  123.4 7.2 %collective-permute-start.13 = (bf16[256,128]{1,0:T(8,128)(2,1)S(1)}, bf16[256,128]{1,0:T(8,128)(2,1)S(1)}, u32[]{:S(2)}, u32[]{:S(2)}) collective-permute-start(bf16[256,128]{1,0:T(8,128)(2,1)S(1)} %get-tuple-element.48), channel_id=1, source_target_pairs={{0,64},{64,0},{1,65},{65,1},{2,66},{66,2},{3,67},{67,3},{4,68},{68... | collective-permute-start | bytes 196616 | tf_op jit(solution)/shard_map/ppermute | solution.py:165
